TPU v7x, 32 devices: a whole 2x2x4 slice. The times are simulated.
32 devices in a mesh: groups: 2 (over x), ctx: 8 (over z, y), exp: 2 (over core).
Axes of the slice: x: 2, y: 2, z: 4, core: 2. Of those that a mesh axis runs over, the one named last changes fastest.
Arguments:
- queries: bfloat16 [2048, 1536], P(('groups', 'ctx'), 'exp'), parts along dimension 0, may hold values from -8 to 8
- latent: bfloat16 [2048, 576], P(('groups', 'ctx')), parts along dimension 0, may hold values from -8 to 8
- residual: bfloat16 [2048, 2048], P(('groups', 'ctx')), parts along dimension 0, may hold values from -12 to 12
- seg_lengths: int32 [32], P('groups'), parts along dimension 0, may hold values from 1 to 256, 1024 in all
- span_order: int32 [32], P('groups'), parts along dimension 0, may hold values from 0 to 15, each once
- expert_ids: int32 [2048, 6], P(('groups', 'ctx')), parts along dimension 0, may hold values from 0 to 63, all different within a row; in each aligned block of 128 rows (0 to 127, 128 to 255, ...) at most 14 rows name the same one
- route_weights: float32 [2048, 6], P(('groups', 'ctx')), parts along dimension 0, may hold values from 0.1 to 1
- kv_up: bfloat16 [512, 2048], P(None, 'exp'), may hold values from -0.25 to 0.25
- out_proj: bfloat16 [1024, 2048], P('exp'), may hold values from -0.75 to 0.75
- norm_gain: bfloat16 [2048], replicated, may hold values from 0.099609375 to 1.8984375
- w_gate: bfloat16 [64, 2048, 1408], P('ctx', None, 'exp'), may hold values from -0.125 to 0.125
- w_up: bfloat16 [64, 2048, 1408], P('ctx', None, 'exp'), may hold values from -0.125 to 0.125
- w_down: bfloat16 [64, 1408, 2048], P('ctx', 'exp'), may hold values from -0.15625 to 0.15625
Outputs:
- layer_out: bfloat16 [2048, 2048], P(('groups', 'ctx'), 'exp'), parts along dimension 0
There are 2 independent parts, one for each index of `groups`. A program takes and returns all parts, laid end to end along the dimension named above; an argument that names none is the same for every part. Nothing has to cross between parts.
Inputs may be any that keep to these rules, and one draw needn't show every extreme that they name: `seg_lengths`: the 16 lengths sum to 1024 and the longest is exactly 256. `span_order`: each block number appears once. `expert_ids`: each row names 6 different experts; within the rows of one index of ctx (aligned blocks of 128 rows) no expert is named by more than 14 rows, a bound that some block reaches.
All inputs are finite; a program needn't handle non-finite values.
Results may differ from a plain program's by a relative error of at most 0.018.
Values may be sent and summed in bfloat16 or wider, within the bound.
No kernel may reach another device: no remote copies, remote signals or barrier semaphores. Data moves between devices by JAX's collectives and lax.ppermute only.
A program may use at most 192 MiB of HBM per device.

v0:
```python
import math

import jax
import jax.numpy as jnp
from jax import lax
from jax.sharding import PartitionSpec as P

NOPE = 128
ROPE = 64
VHEAD = 128
LAT = 512
EXPERTS = 64
TOP = 6
MOST = 14


def lookup(values_table, wanted):
    hits = wanted[:, None] == jnp.arange(values_table.shape[0], dtype=jnp.int32)[None, :]
    return jnp.sum(jnp.where(hits, values_table[None, :], 0), axis=1)


def placed(row_ids, span_order, seg_ends, span):
    position = lookup(span_order, row_ids // span) * span + row_ids % span
    segment = jnp.sum((position[:, None] >= seg_ends[None, :]).astype(jnp.int32), axis=1)
    return (position, segment)


def attend_block(carry, query_nope, query_rope, key_nope, key_rope, values, visible, scale):
    best, weight_sum, accum = carry
    scores = jnp.einsum("rhn,khn->hrk", query_nope, key_nope, preferred_element_type=jnp.float32)
    scores = scores + jnp.einsum(
        "rhn,kn->hrk", query_rope, key_rope, preferred_element_type=jnp.float32
    )
    scores = jnp.where(visible[None], scores * scale, -1e30)
    fresh = jnp.maximum(best, jnp.max(scores, axis=2))
    weights = jnp.where(visible[None], jnp.exp(scores - fresh[:, :, None]), 0.0)
    shrink = jnp.exp(best - fresh)
    weight_sum = weight_sum * shrink + jnp.sum(weights, axis=2)
    mixed = jnp.einsum(
        "hrk,khv->hrv", weights.astype(jnp.bfloat16), values, preferred_element_type=jnp.float32
    )
    accum = accum * shrink[:, :, None] + mixed
    return (fresh, weight_sum, accum)


def body(
    queries,
    latent,
    residual,
    seg_lengths,
    span_order,
    expert_ids,
    route_weights,
    kv_up,
    out_proj,
    norm_gain,
    w_gate,
    w_up,
    w_down,
):
    local_rows = queries.shape[0]
    span = local_rows // 2
    heads_here = kv_up.shape[1] // (NOPE + VHEAD)
    side = lax.axis_index("exp")
    seg_ends = jnp.cumsum(seg_lengths)
    query_rows = lax.axis_index("ctx") * local_rows + jnp.arange(local_rows, dtype=jnp.int32)
    query_pos, query_seg = placed(query_rows, span_order, seg_ends, span)
    shaped = queries.reshape(local_rows, heads_here, NOPE + ROPE)
    query_nope = shaped[:, :, :NOPE]
    query_rope = shaped[:, :, NOPE:]
    scale = 1.0 / math.sqrt(NOPE + ROPE)
    initial = (
        jnp.full((heads_here, local_rows), -1e30, jnp.float32),
        jnp.zeros((heads_here, local_rows), jnp.float32),
        jnp.zeros((heads_here, local_rows, VHEAD), jnp.float32),
    )

    def unpack_latent(block):
        keyval = jnp.dot(block[:, :LAT], kv_up, preferred_element_type=jnp.float32).astype(
            jnp.bfloat16
        )
        return (keyval.reshape(block.shape[0], heads_here, NOPE + VHEAD), block[:, LAT:])

    piece = lax.all_gather(latent, "ctx", axis=0, tiled=True)
    count = piece.shape[0]
    step_rows = math.gcd(count, 512)
    blocks = piece.reshape(count // step_rows, step_rows, piece.shape[1])
    offsets = jnp.arange(count // step_rows, dtype=jnp.int32) * step_rows

    def visit(state, pair):
        offset, block = pair
        key_pos, key_seg = placed(
            offset + jnp.arange(step_rows, dtype=jnp.int32), span_order, seg_ends, span
        )
        visible = (key_seg[None, :] == query_seg[:, None]) & (
            key_pos[None, :] <= query_pos[:, None]
        )

        def compute(inner):
            keyval, key_rope = unpack_latent(block)
            return attend_block(
                inner,
                query_nope,
                query_rope,
                keyval[:, :, :NOPE],
                key_rope,
                keyval[:, :, NOPE:],
                visible,
                scale,
            )

        return (lax.cond(jnp.any(visible), compute, lambda inner: inner, state), None)

    state, _ = lax.scan(visit, initial, (offsets, blocks))
    best, weight_sum, accum = state
    attended = (accum / weight_sum[:, :, None]).astype(jnp.bfloat16)
    partial_attn = jnp.einsum(
        "hrv,hvd->rd",
        attended,
        out_proj.reshape(heads_here, VHEAD, out_proj.shape[1]),
        preferred_element_type=jnp.float32,
    )
    attention_out = lax.psum(partial_attn.astype(jnp.bfloat16), "exp").astype(jnp.float32)
    middle = (residual.astype(jnp.float32) + attention_out).astype(jnp.bfloat16)
    middle_f = middle.astype(jnp.float32)
    inverse = lax.rsqrt(jnp.mean(middle_f * middle_f, axis=1, keepdims=True) + 1e-06)
    normed = (middle_f * inverse * norm_gain.astype(jnp.float32)[None, :]).astype(jnp.bfloat16)
    pair_count = local_rows * TOP
    flat_experts = expert_ids.reshape(pair_count)
    onehot = (flat_experts[:, None] == jnp.arange(EXPERTS, dtype=jnp.int32)[None, :]).astype(
        jnp.bfloat16
    )
    pair_range = jnp.arange(pair_count, dtype=jnp.int32)
    earlier_mask = (pair_range[:, None] > pair_range[None, :]).astype(jnp.bfloat16)
    earlier = jnp.dot(earlier_mask, onehot, preferred_element_type=jnp.float32)
    slots = jnp.sum(earlier * onehot.astype(jnp.float32), axis=1).astype(jnp.int32)
    slot_total = EXPERTS * MOST
    slot_ids = flat_experts * MOST + slots
    slot_range = jnp.arange(slot_total, dtype=jnp.int32)
    select = jnp.sum(
        (slot_ids.reshape(1, local_rows, TOP) == slot_range[:, None, None]).astype(jnp.int32),
        axis=2,
    ).astype(jnp.bfloat16)
    combine = jnp.sum(
        jnp.where(
            slot_ids.reshape(local_rows, TOP, 1) == slot_range[None, None, :],
            route_weights[:, :, None],
            0.0,
        ),
        axis=1,
    )
    owners = lax.axis_size("ctx")
    per_owner = EXPERTS // owners
    width_half = normed.shape[1] // 2
    buffer = jnp.dot(select, normed, preferred_element_type=jnp.float32).astype(jnp.bfloat16)
    arrived = lax.all_to_all(
        buffer.reshape(owners, per_owner, MOST, normed.shape[1]),
        "ctx",
        split_axis=0,
        concat_axis=0,
        tiled=True,
    )
    gate = jnp.einsum("cesd,edf->cesf", arrived, w_gate, preferred_element_type=jnp.float32)
    upper = jnp.einsum("cesd,edf->cesf", arrived, w_up, preferred_element_type=jnp.float32)
    hidden = (jax.nn.silu(gate) * upper).astype(jnp.bfloat16)
    summed = lax.psum(
        jnp.einsum("cesf,efd->cesd", hidden, w_down, preferred_element_type=jnp.float32).astype(
            jnp.bfloat16
        ),
        "exp",
    )
    back = lax.all_to_all(summed, "ctx", split_axis=0, concat_axis=0, tiled=True)
    returned = lax.dynamic_slice_in_dim(
        back.reshape(slot_total, normed.shape[1]), side * width_half, width_half, 1
    )
    mixture = jnp.dot(combine, returned.astype(jnp.float32), precision=lax.Precision.HIGHEST)
    middle_half = lax.dynamic_slice_in_dim(middle_f, side * width_half, width_half, 1)
    return (middle_half + mixture).astype(jnp.bfloat16)


def solution(mesh):
    in_specs = (
        P(("groups", "ctx"), "exp"),
        P(("groups", "ctx"), None),
        P(("groups", "ctx"), None),
        P("groups"),
        P("groups"),
        P(("groups", "ctx"), None),
        P(("groups", "ctx"), None),
        P(None, "exp"),
        P("exp", None),
        P(),
        P("ctx", None, "exp"),
        P("ctx", None, "exp"),
        P("ctx", "exp", None),
    )
    out_specs = P(("groups", "ctx"), "exp")
    return jax.shard_map(body, mesh=mesh, in_specs=in_specs, out_specs=out_specs, check_vma=False)
```

profile of v0, /device:TPU:0, one launch (start us, length us, event | category | flops | bytes accessed | tf_op | source)
XLA Modules:
  0.0 391.8 jit_solution(8225226103502392121)
XLA Ops:
  6.5 0.7 all-gather.2.cloned.1.call-update
  7.3 1.1 copy.74
  8.4 0.7 copy.73
  9.3 0.8 copy.76
  10.7 0.7 select_reduce_fusion.2
  11.9 1.2 convert_reduce_fusion.2
  13.1 40.0 %all-gather.2.cloned.1.call-done = bf16[1024,576]{0,1:T(8,128)(2,1)} async-done(((bf16[128,576]{0,1:T(8,128)(2,1)}), bf16[1024,576]{0,1:T(8,128)(2,1)}) %all-gather.2.cloned.1.call-update) | async-done | bytes 1179664 | tf_op jit(solution)/shard_map/all_gather | solution.py:84
  53.1 2.4 copy.104
  55.5 31.7 %while.16 = (s32[]{:T(128)}, f32[4,128]{1,0:T(4,128)S(1)}, f32[4,128]{1,0:T(4,128)S(1)}, f32[4,128,128]{2,1,0:T(8,128)S(1)}, s32[2]{0:T(128)}, /*index=5*/s32[16...) while((s32[]{:T(128)}, f32[4,128]{1,0:T(4,128)S(1)}, ...), condition=%wide.region_11.12_spmd, body=%wide.region_3.11_spmd.sunk | while | flops 708246528 | bytes 17747392 | solution.py:114
  55.5 1.3 dynamic_slice.32
  57.4 0.7 select_reduce_fusion.4
  58.2 0.6 fusion.73
  58.9 1.5 fusion.74
  61.0 10.3 %conditional.2 = ((f32[4,128]{1,0:T(4,128)S(1)}, f32[4,128]{1,0:T(4,128)S(1)}, f32[4,128,128]{2,1,0:T(8,128)S(1)})) conditional(s32[]{:T(128)} %convert_element_type.162, (f32[4,128]{1,0:T(4,128)S(1)}, f32[4,128]{1,0:T(4,128)S(1)}, f32[4,128,128]{2,1,0:T(8,128)S(1)}) %tuple.49, (pred[128,512]{0,1:T(8,128)(4,1)S(1)}, bf16[2,512,576]{1,2,0:T(8,128)(2,1)}, ...), branch_computations={%region_7.7_spmd, %region_8.10_spmd} | conditional | flops 707920896 | bytes 17662016 | solution.py:112
  61.0 1.1 dynamic-slice_bitcast_fusion
  62.2 0.8 copy-done.2
  63.0 3.0 convolution_convert_fusion
  66.0 1.9 reshape.156
  68.2 1.2 convolution_bitcast_fusion.1
  69.4 1.2 fusion.65
  71.4 1.3 dynamic_slice.32
  73.3 0.7 select_reduce_fusion.4
  74.0 0.6 fusion.73
  74.8 1.5 fusion.74
  76.9 10.3 %conditional.2 = ((f32[4,128]{1,0:T(4,128)S(1)}, f32[4,128]{1,0:T(4,128)S(1)}, f32[4,128,128]{2,1,0:T(8,128)S(1)})) conditional(s32[]{:T(128)} %convert_element_type.162, (f32[4,128]{1,0:T(4,128)S(1)}, f32[4,128]{1,0:T(4,128)S(1)}, f32[4,128,128]{2,1,0:T(8,128)S(1)}) %tuple.49, (pred[128,512]{0,1:T(8,128)(4,1)S(1)}, bf16[2,512,576]{1,2,0:T(8,128)(2,1)}, ...), branch_computations={%region_7.7_spmd, %region_8.10_spmd} | conditional | flops 707920896 | bytes 17662016 | solution.py:112
  76.9 1.1 dynamic-slice_bitcast_fusion
  78.0 0.8 copy-done.2
  78.8 3.0 convolution_convert_fusion
  81.8 1.9 reshape.156
  84.0 1.2 convolution_bitcast_fusion.1
  85.3 1.2 fusion.65
  87.2 1.3 fusion.39
  89.8 16.1 %all-reduce.3.cloned.1.call-done = bf16[128,2048]{1,0:T(8,128)(2,1)} async-done(((bf16[128,2048]{1,0:T(8,128)(2,1)}), bf16[128,2048]{1,0:T(8,128)(2,1)}) %all-reduce.3.cloned.1.call-update) | async-done | bytes 524304 | tf_op jit(solution)/shard_map/psum | solution.py:123
  106.0 1.5 fusion.52
  107.5 4.0 %convolution_convert_fusion.1 = bf16[896,2048]{1,0:T(8,128)(2,1)} fusion(f32[2048]{0:T(1024)S(1)} %convert_element_type.99, f32[128]{0:T(128)S(1)} %add_rsqrt_fusion, s32[896,128]{1,0:T(8,128)S(1)} %convert_reduce_fusion.1, bf16[128,2048]{1,0:T(8,128)(2,1)} %all-reduce.3.cloned.1.call-done, bf16[128,2048]{1,0:T(8,128)(2,1)S(1)} %copy-done.3), kind=kOutput, calls=%fused_computation.45 | convolution fusion | flops 473808896 | bytes 5186048 | tf_op jit(solution)/shard_map/dot_general | solution.py:155
  111.5 6.0 %reshape.169 = bf16[8,8,14,2048]{3,2,1,0:T(8,128)(2,1)} reshape(bf16[896,2048]{1,0:T(8,128)(2,1)} %convolution_convert_fusion.1) | data formatting | bytes 7340032 | tf_op jit(solution)/shard_map/reshape | solution.py:157
  117.5 4.3 %copy.79 = bf16[8,8,14,2048]{3,1,2,0:T(8,128)(2,1)S(1)} copy(bf16[8,8,14,2048]{3,2,1,0:T(8,128)(2,1)} %reshape.169) | data formatting | bytes 7340032 | tf_op jit(solution)/shard_map/reshape | solution.py:157
  121.8 88.0 %all_to_all.10 = bf16[8,8,14,2048]{3,1,2,0:T(8,128)(2,1)} all-to-all(bf16[8,8,14,2048]{3,1,2,0:T(8,128)(2,1)S(1)} %copy.79), channel_id=1, replica_groups=mesh['groups'=2,'ctx'=8,'exp'=2] {'ctx'}, dimensions={0} | all-to-all | bytes 7340032 | tf_op jit(solution)/shard_map/all_to_all | solution.py:156
  209.8 15.4 %fusion.19 = f32[8,8,14,704]{3,2,1,0:T(8,128)} fusion(bf16[8,2048,704]{1,2,0:T(8,128)(2,1)} %param.28, bf16[8,8,14,2048]{3,1,2,0:T(8,128)(2,1)} %all_to_all.10), kind=kOutput, calls=%fused_computation.38 | convolution fusion | flops 2583691264 | bytes 29261824 | tf_op jit(solution)/shard_map/cesd,edf->cesf/dot_general | solution.py:164
  225.3 21.7 %convert_bitcast_fusion = bf16[8,8,14,2048]{3,2,0,1:T(8,128)(2,1)} fusion(bf16[8,704,2048]{2,1,0:T(8,128)(2,1)} %param.29, f32[8,8,14,704]{3,2,1,0:T(8,128)} %fusion.19, bf16[8,2048,704]{1,2,0:T(8,128)(2,1)} %param.27, bf16[8,8,14,2048]{3,1,2,0:T(8,128)(2,1)} %all_to_all.10), kind=kOutput, calls=%fused_computation.42 | convolution fusion | flops 5173002240 | bytes 56000512 | tf_op jit(solution)/shard_map/cesf,efd->cesd/dot_general | solution.py:167
  247.0 27.6 %all-reduce.5.cloned.1.call-done = bf16[8,8,14,2048]{3,2,0,1:T(8,128)(2,1)} async-done(((bf16[8,8,14,2048]{3,2,0,1:T(8,128)(2,1)}), bf16[8,8,14,2048]{3,2,0,1:T(8,128)(2,1)}) %all-reduce.5.cloned.1.call-update) | async-done | bytes 3670032 | tf_op jit(solution)/shard_map/psum | solution.py:166
  274.6 6.3 %copy.82 = bf16[8,8,14,2048]{3,1,2,0:T(8,128)(2,1)} copy(bf16[8,8,14,2048]{3,2,0,1:T(8,128)(2,1)} %all-reduce.5.cloned.1.call-done) | data formatting | bytes 7340032 | tf_op jit(solution)/shard_map/psum | solution.py:166
  280.9 5.9 %all-to-all-start.1 = ((bf16[8,8,14,2048]{3,1,2,0:T(8,128)(2,1)}), bf16[8,8,14,2048]{3,1,2,0:T(8,128)(2,1)}, u32[]{:S(2)}, u32[]{:S(2)}) async-start(bf16[8,8,14,2048]{3,1,2,0:T(8,128)(2,1)} %copy.82), calls=%async_computation.1 | async-start | bytes 7340032 | tf_op jit(solution)/shard_map/all_to_all | solution.py:172
  286.9 1.1 select_reduce_fusion.1
  288.0 81.4 %all-to-all-done.1 = bf16[8,8,14,2048]{3,1,2,0:T(8,128)(2,1)} async-done(((bf16[8,8,14,2048]{3,1,2,0:T(8,128)(2,1)}), bf16[8,8,14,2048]{3,1,2,0:T(8,128)(2,1)}, u32[]{:S(2)}, u32[]{:S(2)}) %all-to-all-start.1) | async-done | bytes 3670048 | tf_op jit(solution)/shard_map/all_to_all | solution.py:172
  369.4 6.6 %copy.83 = bf16[8,8,14,2048]{3,2,1,0:T(8,128)(2,1)} copy(bf16[8,8,14,2048]{3,1,2,0:T(8,128)(2,1)} %all-to-all-done.1) | data formatting | bytes 7340032 | tf_op jit(solution)/shard_map/all_to_all | solution.py:172
  375.9 6.0 %reshape.170 = bf16[896,2048]{1,0:T(8,128)(2,1)} reshape(bf16[8,8,14,2048]{3,2,1,0:T(8,128)(2,1)} %copy.83) | data formatting | bytes 7340032 | tf_op jit(solution)/shard_map/reshape | solution.py:174
  381.9 3.4 fusion.47
  (55 shorter events, 6.2 us)
Async XLA Ops:
  6.5 80.7 %copy-start = (bf16[512,2048]{1,0:T(8,128)(2,1)S(1)}, bf16[512,2048]{1,0:T(8,128)(2,1)}, u32[]{:S(2)}) copy-start(bf16[512,2048]{1,0:T(8,128)(2,1)} %param.25) | copy-start | bytes 6291460
  6.5 46.5 %all-gather.2.cloned.1.call-start = ((), (), s32[]{:S(2)}) async-start(), calls=%async_computation.2 | async-start | bytes 1327104 | tf_op jit(solution)/shard_map/all_gather | solution.py:84
  7.3 98.7 %all-reduce.3.cloned.1.call-start = ((), (), s32[]{:S(2)}) async-start(), calls=%async_computation.3 | async-start | bytes 1048576 | tf_op jit(solution)/shard_map/psum | solution.py:123
  55.5 33.1 %copy-start.4 = (s32[128,6]{0,1:T(8,128)S(1)}, s32[128,6]{0,1:T(8,128)}, u32[]{:S(2)}) copy-start(s32[128,6]{0,1:T(8,128)} %param.22) | copy-start | bytes 9220
  62.2 0.8 copy-start.2
  78.0 0.8 copy-start.2
  87.2 2.3 copy-start.6
  88.5 18.9 %copy-start.3 = (bf16[128,2048]{1,0:T(8,128)(2,1)S(1)}, bf16[128,2048]{1,0:T(8,128)(2,1)}, u32[]{:S(2)}) copy-start(bf16[128,2048]{1,0:T(8,128)(2,1)} %param.19) | copy-start | bytes 1572868
  88.6 186.1 %all-reduce.5.cloned.1.call-start = ((), (), s32[]{:S(2)}) async-start(), calls=%async_computation.4 | async-start | bytes 8388608 | tf_op jit(solution)/shard_map/psum | solution.py:166
  280.9 5.9 %copy-start.5 = (f32[128,6]{0,1:T(8,128)S(1)}, f32[128,6]{0,1:T(8,128)}, u32[]{:S(2)}) copy-start(f32[128,6]{0,1:T(8,128)} %param.23) | copy-start | bytes 9220
  280.9 88.4 %all-to-all-start.1 = ((bf16[8,8,14,2048]{3,1,2,0:T(8,128)(2,1)}), bf16[8,8,14,2048]{3,1,2,0:T(8,128)(2,1)}, u32[]{:S(2)}, u32[]{:S(2)}) async-start(bf16[8,8,14,2048]{3,1,2,0:T(8,128)(2,1)} %copy.82), calls=%async_computation.1 | async-start | bytes 7340032 | tf_op jit(solution)/shard_map/all_to_all | solution.py:172
  369.4 15.9 %copy-start.1 = (bf16[512,2048]{1,0:T(8,128)(2,1)S(1)}, bf16[512,2048]{1,0:T(8,128)(2,1)}, u32[]{:S(2)}) copy-start(bf16[512,2048]{1,0:T(8,128)(2,1)} %param.25) | copy-start | bytes 6291460
Sparse Core Ops, SparseCore 0:
  9.4 43.6 all-gather.1
  88.7 17.2 all-reduce.2
  247.2 27.4 all-reduce.4
where the time goes:
time: 393 us; the launch traced here: 392 us
  waiting for transfers between devices  166 us (42%)
  blocking collectives  88 us (22%)
  matrix products  58 us (15%)
  local copies, waits for them, and re-layouts  45.4 us (12%)
  other arithmetic  13.7 us (3%)
  between operations  13.3 us (3%)
  starting transfers between devices  5.99 us (2%)
    all_to_all x1, blocking collectives, body(): lax.all_to_all(buffer.reshape(owners, per_owner, MOST, normed.shape[1]),...  88 us
    all_to_all x1, waiting for transfers between devices, body(): lax.all_to_all(summed, 'ctx', split_axis=0, concat_axis=0, tiled=True)  81.4 us
    all_gather x1, waiting for transfers between devices, body(): piece = lax.all_gather(latent, 'ctx', axis=0, tiled=True)  40 us
    psum x1, waiting for transfers between devices, body(): lax.psum(jnp.einsum('cesf,efd->cesd', hidden, w_down, preferred_element_t...  27.6 us
    dot_general x1, matrix products, body(): jnp.einsum('cesf,efd->cesd', hidden, w_down, preferred_element_type=jnp.f...  21.7 us
    psum x1, waiting for transfers between devices, body(): lax.psum(partial_attn.astype(jnp.bfloat16), 'exp').astype(jnp.float32)  16.1 us
    dot_general x1, matrix products, body(): jnp.einsum('cesd,edf->cesf', arrived, w_up, preferred_element_type=jnp.fl...  15.4 us
    reshape x2, local copies, waits for them, and re-layouts, body(): buffer.reshape(owners, per_owner, MOST, normed.shape[1])  10.3 us
  transfers between devices with their start and end apart: 4, of which 4 were waited for; matrix products, arithmetic and copies ran while one was open for 2% of the time, Pallas kernels for 0%

commit v1 on v0

v1 whole, which is shorter than its diff:
```python
import functools
import math

import jax
import jax.numpy as jnp
from jax import lax
from jax.experimental import pallas as pl
from jax.experimental.pallas import tpu as pltpu
from jax.sharding import PartitionSpec as P

NOPE = 128
ROPE = 64
VHEAD = 128
LAT = 512
EXPERTS = 64
TOP = 6
SLOTS = 16
WIDE = 640
VMEM_LIMIT = 56 * 1024 * 1024
SWAP = [(0, 1), (1, 0)]
FEW = 8


def grid_of(count):
    fast = 2 ** (int(math.log2(count)) // 2)
    return (count // fast, fast)


def shift_slow(value, step, count):
    slow, fast = grid_of(count)
    perm = [(i, (i // fast + step) % slow * fast + i % fast) for i in range(count)]
    return lax.ppermute(value, "ctx", perm)


def shift_fast(value, step, count):
    fast = grid_of(count)[1]
    perm = [(i, i // fast * fast + (i % fast + step) % fast) for i in range(count)]
    return lax.ppermute(value, "ctx", perm)


def swap(value):
    return lax.ppermute(value, "exp", SWAP)


def each(send, pieces, count):
    if count <= FEW:
        return [send(piece) for piece in pieces]
    return list(send(jnp.stack(pieces)))


def spread(block, count):
    slow, fast = grid_of(count)
    line = [block] + [shift_slow(block, s, count) for s in range(1, slow)]
    found = list(line)
    for r in range(1, fast):
        found += each(lambda piece: shift_fast(piece, r, count), line, count)
    return found


def collect(parts, count):
    slow, fast = grid_of(count)
    sums = [part.astype(jnp.float32) for part in parts[:slow]]
    for r in range(1, fast):
        arrived = each(lambda piece: shift_fast(piece, -r, count), parts[r * slow : (r + 1) * slow], count)
        sums = [total + piece.astype(jnp.float32) for total, piece in zip(sums, arrived)]
    arrived = [shift_slow(sums[s].astype(jnp.bfloat16), -s, count) for s in range(1, slow)]
    total = sums[0]
    for piece in arrived:
        total = total + piece.astype(jnp.float32)
    return total


def owner_of(place, me, count):
    slow, fast = grid_of(count)
    r, s = place // slow, place % slow
    return (me // fast + slow - s) % slow * fast + (me % fast + fast - r) % fast


def attend_kernel(count, blocks, info, q_ref, mine_ref, other_ref, up_ref, proj_ref, out_ref, m_ref, l_ref, acc_ref):
    step = pl.program_id(0)
    me, side = info[0], info[1]
    segs = 16
    span = mine_ref.shape[1]
    heads, rows, _ = q_ref.shape

    @pl.when(step == 0)
    def _():
        m_ref[...] = jnp.full_like(m_ref, -1e30)
        l_ref[...] = jnp.zeros_like(l_ref)
        acc_ref[...] = jnp.zeros_like(acc_ref)

    row = lax.broadcasted_iota(jnp.int32, (rows, 1), 0)
    first = info[2 + segs + 2 * me] * span
    second = info[2 + segs + 2 * me + 1] * span
    qpos = jnp.where(row < span, first + row, second + row - span)
    low = jnp.zeros((rows, 1), jnp.int32)
    start = jnp.int32(0)
    for m in range(segs):
        low = jnp.where(qpos >= start, start, low)
        start = start + info[2 + m]
    keys = blocks * span
    lane = lax.broadcasted_iota(jnp.int32, (1, keys), 1)
    within, which = lane % span, lane // span
    kpos_parts = []
    for half in (side, 1 - side):
        base = jnp.zeros((1, keys), jnp.int32)
        for j in range(blocks):
            src = owner_of(step * blocks + j, me, count)
            base = jnp.where(which == j, info[2 + segs + 2 * src + half] * span, base)
        kpos_parts.append(base + within)
    kpos = jnp.concatenate(kpos_parts, axis=1)
    visible = (kpos >= low) & (kpos <= qpos)

    lat = jnp.concatenate([mine_ref[...].reshape(keys, WIDE), other_ref[...].reshape(keys, WIDE)], axis=0)
    keyval = jnp.dot(lat[:, :LAT], up_ref[...], preferred_element_type=jnp.float32).astype(jnp.bfloat16)
    rope = lat[:, LAT : LAT + ROPE]
    scale = 1.0 / math.sqrt(NOPE + ROPE)
    for h in range(heads):
        base = h * (NOPE + VHEAD)
        key = jnp.concatenate([keyval[:, base : base + NOPE], rope], axis=1)
        scores = lax.dot_general(q_ref[h], key, (((1,), (1,)), ((), ())), preferred_element_type=jnp.float32)
        scores = jnp.where(visible, scores * scale, -1e30)
        best = m_ref[h]
        fresh = jnp.maximum(best, jnp.max(scores, axis=1, keepdims=True))
        weights = jnp.where(visible, jnp.exp(scores - fresh), 0.0)
        shrink = jnp.exp(best - fresh)
        m_ref[h] = fresh
        l_ref[h] = l_ref[h] * shrink + jnp.sum(weights, axis=1, keepdims=True)
        mixed = jnp.dot(
            weights.astype(jnp.bfloat16), keyval[:, base + NOPE : base + NOPE + VHEAD], preferred_element_type=jnp.float32
        )
        acc_ref[h] = acc_ref[h] * shrink + mixed

    @pl.when(step == pl.num_programs(0) - 1)
    def _():
        attended = [(acc_ref[h] / l_ref[h]).astype(jnp.bfloat16) for h in range(heads)]
        out = jnp.dot(jnp.concatenate(attended, axis=1), proj_ref[...], preferred_element_type=jnp.float32)
        out_ref[...] = out.astype(jnp.bfloat16)


def attend(info, q, mine, other, kv_up, out_proj, count):
    heads, rows, depth = q.shape
    blocks = math.gcd(count, 8)
    span = mine.shape[1]
    whole2 = lambda i, *_: (0, 0)
    whole3 = lambda i, *_: (0, 0, 0)
    lat_spec = pl.BlockSpec((blocks, span, WIDE), lambda i, *_: (i, 0, 0))
    return pl.pallas_call(
        functools.partial(attend_kernel, count, blocks),
        grid_spec=pltpu.PrefetchScalarGridSpec(
            num_scalar_prefetch=1,
            grid=(count // blocks,),
            in_specs=[
                pl.BlockSpec(q.shape, whole3),
                lat_spec,
                lat_spec,
                pl.BlockSpec(kv_up.shape, whole2),
                pl.BlockSpec(out_proj.shape, whole2),
            ],
            out_specs=pl.BlockSpec((rows, out_proj.shape[1]), whole2),
            scratch_shapes=[
                pltpu.VMEM((heads, rows, 1), jnp.float32),
                pltpu.VMEM((heads, rows, 1), jnp.float32),
                pltpu.VMEM((heads, rows, VHEAD), jnp.float32),
            ],
        ),
        out_shape=jax.ShapeDtypeStruct((rows, out_proj.shape[1]), jnp.bfloat16),
        compiler_params=pltpu.CompilerParams(vmem_limit_bytes=VMEM_LIMIT),
        name="attend",
    )(info, q, mine, other, kv_up, out_proj)


def norm_kernel(info, residual_ref, here_ref, there_ref, gain_ref, middle_ref, normed_ref):
    side = info[1]
    half = middle_ref.shape[1]
    total = here_ref[...].astype(jnp.float32) + there_ref[...].astype(jnp.float32)
    middle = (residual_ref[...].astype(jnp.float32) + total).astype(jnp.bfloat16)
    wide = middle.astype(jnp.float32)
    inverse = lax.rsqrt(jnp.mean(wide * wide, axis=1, keepdims=True) + 1e-06)
    normed = wide * inverse * gain_ref[...].astype(jnp.float32)
    middle_ref[...] = jnp.where(side == 0, wide[:, :half], wide[:, half:]).astype(jnp.bfloat16)
    normed_ref[...] = jnp.where(side == 0, normed[:, :half], normed[:, half:]).astype(jnp.bfloat16)


def norm(info, residual, here, there, gain):
    rows, width = residual.shape
    half = jax.ShapeDtypeStruct((rows, width // 2), jnp.bfloat16)
    full = pl.BlockSpec((rows, width), lambda i, *_: (0, 0))
    part = pl.BlockSpec((rows, width // 2), lambda i, *_: (0, 0))
    return pl.pallas_call(
        norm_kernel,
        grid_spec=pltpu.PrefetchScalarGridSpec(
            num_scalar_prefetch=1,
            grid=(1,),
            in_specs=[full, full, full, pl.BlockSpec((1, width), lambda i, *_: (0, 0))],
            out_specs=[part, part],
        ),
        out_shape=[half, half],
        compiler_params=pltpu.CompilerParams(vmem_limit_bytes=VMEM_LIMIT),
        name="norm",
    )(info, residual, here, there, gain.reshape(1, width))


def up_kernel(info, mine_ref, other_ref, gm_ref, go_ref, um_ref, uo_ref, scale_ref, out_ref):
    rows = out_ref.shape[1]
    mine = mine_ref[...].reshape(rows, mine_ref.shape[3])
    other = other_ref[...].reshape(rows, other_ref.shape[3])
    gate = jnp.dot(mine, gm_ref[0], preferred_element_type=jnp.float32)
    gate = gate + jnp.dot(other, go_ref[0], preferred_element_type=jnp.float32)
    upper = jnp.dot(mine, um_ref[0], preferred_element_type=jnp.float32)
    upper = upper + jnp.dot(other, uo_ref[0], preferred_element_type=jnp.float32)
    hidden = gate / (1.0 + jnp.exp(-gate)) * upper * scale_ref[0]
    out_ref[0] = hidden.astype(jnp.bfloat16)


def up(info, mine, other, w_gate, w_up, scale):
    count, here, slots, half = mine.shape
    hidden = w_gate.shape[2]
    rows = count * slots
    rows_spec = pl.BlockSpec((count, 1, slots, half), lambda e, info: (0, e, 0, 0))
    mine_spec = pl.BlockSpec((1, half, hidden), lambda e, info: (e, info[1], 0))
    other_spec = pl.BlockSpec((1, half, hidden), lambda e, info: (e, 1 - info[1], 0))
    return pl.pallas_call(
        up_kernel,
        grid_spec=pltpu.PrefetchScalarGridSpec(
            num_scalar_prefetch=1,
            grid=(here,),
            in_specs=[
                rows_spec,
                rows_spec,
                mine_spec,
                other_spec,
                mine_spec,
                other_spec,
                pl.BlockSpec((1, rows, 1), lambda e, info: (e, 0, 0)),
            ],
            out_specs=pl.BlockSpec((1, rows, hidden), lambda e, info: (e, 0, 0)),
        ),
        out_shape=jax.ShapeDtypeStruct((here, rows, hidden), jnp.bfloat16),
        compiler_params=pltpu.CompilerParams(vmem_limit_bytes=VMEM_LIMIT),
        name="expert_up",
    )(info, mine, other, w_gate, w_gate, w_up, w_up, scale)


def down_kernel(info, hidden_ref, w_ref, combine_ref, out_ref, held):
    expert = pl.program_id(0)
    count, here, slots, half = held.shape
    result = jnp.dot(hidden_ref[0], w_ref[0], preferred_element_type=jnp.float32).astype(jnp.bfloat16)
    held[:, pl.ds(expert, 1)] = result.reshape(count, 1, slots, half)

    @pl.when(expert == pl.num_programs(0) - 1)
    def _():
        def place(c, _):
            rows = held[c].reshape(here * slots, half)
            out_ref[c] = jnp.dot(combine_ref[c], rows, preferred_element_type=jnp.float32).astype(jnp.bfloat16)
            return 0

        lax.fori_loop(0, count, place, 0)


def down(info, hidden, w_down, combine, flip):
    here, rows, units = hidden.shape
    count, local, _ = combine.shape
    half = w_down.shape[2] // 2
    return pl.pallas_call(
        down_kernel,
        grid_spec=pltpu.PrefetchScalarGridSpec(
            num_scalar_prefetch=1,
            grid=(here,),
            in_specs=[
                pl.BlockSpec((1, rows, units), lambda e, info: (e, 0, 0)),
                pl.BlockSpec((1, units, half), lambda e, info: (e, 0, 1 - info[1] if flip else info[1])),
                pl.BlockSpec(combine.shape, lambda e, info: (0, 0, 0)),
            ],
            out_specs=pl.BlockSpec((count, local, half), lambda e, info: (0, 0, 0)),
            scratch_shapes=[pltpu.VMEM((count, here, rows // count, half), jnp.bfloat16)],
        ),
        out_shape=jax.ShapeDtypeStruct((count, local, half), jnp.bfloat16),
        compiler_params=pltpu.CompilerParams(vmem_limit_bytes=VMEM_LIMIT),
        name="expert_down",
    )(info, hidden, w_down, combine)


def body(
    queries,
    latent,
    residual,
    seg_lengths,
    span_order,
    expert_ids,
    route_weights,
    kv_up,
    out_proj,
    norm_gain,
    w_gate,
    w_up,
    w_down,
):
    local_rows, width = residual.shape
    span = local_rows // 2
    heads = kv_up.shape[1] // (NOPE + VHEAD)
    count = lax.axis_size("ctx")
    here = EXPERTS // count
    me, side = lax.axis_index("ctx"), lax.axis_index("exp")
    info = jnp.concatenate([jnp.stack([me, side]).astype(jnp.int32), seg_lengths, span_order])

    high = route_weights.astype(jnp.bfloat16)
    lower = (route_weights - high.astype(jnp.float32)).astype(jnp.bfloat16)
    base = latent.shape[1]
    packed = jnp.concatenate(
        [
            latent,
            expert_ids.astype(jnp.bfloat16),
            high,
            lower,
            jnp.zeros((local_rows, WIDE - base - 3 * TOP), jnp.bfloat16),
        ],
        axis=1,
    )
    found = spread(lax.dynamic_slice_in_dim(packed, side * span, span, 0), count)
    mine = jnp.stack(found)
    other = jnp.stack(each(swap, found, count))

    q = queries.reshape(local_rows, heads, NOPE + ROPE).transpose(1, 0, 2)
    partial = attend(info, q, mine, other, kv_up, out_proj, count)
    middle, normed = norm(info, residual, partial, swap(partial), norm_gain)

    facts_mine, facts_other = mine[:, :, base : base + 3 * TOP], other[:, :, base : base + 3 * TOP]
    facts = jnp.concatenate(
        [jnp.where(side == 0, facts_mine, facts_other), jnp.where(side == 0, facts_other, facts_mine)], axis=1
    ).astype(jnp.float32)
    ids, share = facts[:, :, :TOP], facts[:, :, TOP : 2 * TOP] + facts[:, :, 2 * TOP :]
    own = (me * here + jnp.arange(here, dtype=jnp.int32)).astype(jnp.float32)
    hit = ids[:, :, :, None] == own
    hot = jnp.any(hit, axis=2)
    share = jnp.sum(jnp.where(hit, share[:, :, :, None], 0.0), axis=2)
    token = jnp.arange(local_rows, dtype=jnp.int32)
    before = (token[:, None] > token[None, :]).astype(jnp.bfloat16)
    rank = jnp.einsum("tu,cue->cte", before, hot.astype(jnp.bfloat16), preferred_element_type=jnp.float32)
    rank = jnp.where(hot, rank, -1.0)
    slot = jnp.arange(SLOTS, dtype=jnp.int32).astype(jnp.float32)
    combine = rank[:, :, :, None] == slot
    scale = jnp.sum(jnp.where(combine, share[:, :, :, None], 0.0), axis=1)
    scale = scale.transpose(1, 0, 2).reshape(here, count * SLOTS, 1)
    combine = combine.astype(jnp.bfloat16).reshape(count, local_rows, here * SLOTS)

    got = spread(normed, count)
    got_other = jnp.stack(each(swap, got, count))
    got = jnp.stack(got)

    def pick(rows):
        picked = jnp.einsum("cts,ctd->csd", combine, rows, preferred_element_type=jnp.float32)
        return picked.astype(jnp.bfloat16).reshape(count, here, SLOTS, rows.shape[2])

    hidden = up(info, pick(got), pick(got_other), w_gate, w_up, scale)
    away = down(info, hidden, w_down, combine, True)
    away = swap(away)
    kept = down(info, hidden, w_down, combine, False)
    sums = (kept.astype(jnp.float32) + away.astype(jnp.float32)).astype(jnp.bfloat16)
    mixture = collect([sums[c] for c in range(count)], count)
    return (middle.astype(jnp.float32) + mixture).astype(jnp.bfloat16)


def solution(mesh):
    in_specs = (
        P(("groups", "ctx"), "exp"),
        P(("groups", "ctx"), None),
        P(("groups", "ctx"), None),
        P("groups"),
        P("groups"),
        P(("groups", "ctx"), None),
        P(("groups", "ctx"), None),
        P(None, "exp"),
        P("exp", None),
        P(),
        P("ctx", None, "exp"),
        P("ctx", None, "exp"),
        P("ctx", "exp", None),
    )
    out_specs = P(("groups", "ctx"), "exp")
    return jax.shard_map(body, mesh=mesh, in_specs=in_specs, out_specs=out_specs, check_vma=False)
```

time: 393 us -> 250 us (0.64)
  blocking collectives: 88 us -> 0 us
  waiting for transfers between devices: 166 us -> 79 us
  Pallas kernels: 0 us -> 55.3 us
  matrix products: 58 us -> 4.35 us
  local copies, waits for them, and re-layouts: 45.4 us -> 70.5 us
  starting transfers between devices: 5.99 us -> 30.6 us
  between operations: 13.3 us -> 0.49 us
  other arithmetic: 13.7 us -> 7.48 us
    all_to_all x1 -> x0, blocking collectives: 88 us -> none  [body(): lax.all_to_all(buffer.reshape(owners, per_owner, MOST, normed.shape[1]),...]
    all_to_all x1 -> x0, waiting for transfers between devices: 81.4 us -> none  [body(): lax.all_to_all(summed, 'ctx', split_axis=0, concat_axis=0, tiled=True)]
    ppermute x0 -> x39, waiting for transfers between devices: none -> 79 us  [the longest x9 41.1 us: shift_slow(): return lax.ppermute(value, 'ctx', perm)]
    unnamed x14 -> x44, local copies, waits for them, and re-layouts: 1.23 us -> 65.9 us
    pallas_call x0 -> x5, Pallas kernels: none -> 55.3 us  [the longest x2 24.1 us: down(): pl.pallas_call(down_kernel, grid_spec=pltpu.PrefetchScalarGridSpec(num_sc...]
    dot_general x14 -> x3, matrix products: 58 us -> 4.35 us  [the longest x2 4.21 us: pick(): jnp.einsum('cts,ctd->csd', combine, rows, preferred_element_type=jnp.floa...]
    psum x2 -> x0, waiting for transfers between devices: 43.7 us -> none  [the longest x1 27.6 us: body(): lax.psum(jnp.einsum('cesf,efd->cesd', hidden, w_down, preferred_element_t...]
    all_gather x1 -> x0, waiting for transfers between devices: 40 us -> none  [body(): piece = lax.all_gather(latent, 'ctx', axis=0, tiled=True)]
  transfers between devices with their start and end apart: 4 -> 39, of which waited for: 4 -> 15; matrix products, arithmetic and copies ran while one was open for 2% -> 29% of each run, Pallas kernels for 0% -> 5%
where the time goes in v1:
time: 250 us; the launch traced here: 248 us
  waiting for transfers between devices  79 us (32%)
  local copies, waits for them, and re-layouts  70.5 us (28%)
  Pallas kernels  55.3 us (22%)
  starting transfers between devices  30.6 us (12%)
  other arithmetic  7.48 us (3%)
  matrix products  4.35 us (2%)
    unnamed x44, local copies, waits for them, and re-layouts  65.9 us
    ppermute x9, waiting for transfers between devices, shift_slow(): return lax.ppermute(value, 'ctx', perm)  41.1 us
    ppermute x12, waiting for transfers between devices, shift_fast(): return lax.ppermute(value, 'ctx', perm)  34.6 us
    pallas_call x2, Pallas kernels, down(): pl.pallas_call(down_kernel, grid_spec=pltpu.PrefetchScalarGridSpec(num_sc...  24.1 us
    pallas_call x1, Pallas kernels, up(): pl.pallas_call(up_kernel, grid_spec=pltpu.PrefetchScalarGridSpec(num_scal...  20.2 us
    ppermute x12, starting transfers between devices, shift_fast(): return lax.ppermute(value, 'ctx', perm)  14.3 us
    ppermute x9, starting transfers between devices, shift_slow(): return lax.ppermute(value, 'ctx', perm)  12.8 us
    pallas_call x1, Pallas kernels, attend(): pl.pallas_call(functools.partial(attend_kernel, count, blocks), grid_spec...  7.87 us
  transfers between devices with their start and end apart: 39, of which 15 were waited for; matrix products, arithmetic and copies ran while one was open for 29% of the time, Pallas kernels for 5%

profile of v1, /device:TPU:0, one launch (start us, length us, event | category | flops | bytes accessed | tf_op | source)
XLA Modules:
  0.0 247.8 jit_solution(1609897575240507259)
XLA Ops:
  1.9 1.1 copy.60
  3.1 3.0 %collective-permute-start.3 = (bf16[64,640]{1,0:T(8,128)(2,1)S(1)}, bf16[64,640]{1,0:T(8,128)(2,1)S(1)}, u32[]{:S(2)}, u32[]{:S(2)}) collective-permute-start(bf16[64,640]{1,0:T(8,128)(2,1)S(1)} %get-tuple-element.12), channel_id=1, source_target_pairs={{0,2},{2,0},{4,6},{6,4},{8,10},{10,8},{12,14},{14,12},{1,3},{3,1},... | collective-permute-start | bytes 245768 | tf_op jit(solution)/shard_map/ppermute | solution.py:38
  6.1 3.6 %collective-permute-start.2 = (bf16[64,640]{1,0:T(8,128)(2,1)S(1)}, bf16[64,640]{1,0:T(8,128)(2,1)S(1)}, u32[]{:S(2)}, u32[]{:S(2)}) collective-permute-start(bf16[64,640]{1,0:T(8,128)(2,1)S(1)} %get-tuple-element.12), channel_id=1, source_target_pairs={{0,12},{2,14},{4,0},{6,2},{8,4},{10,6},{12,8},{14,10},{1,13},{3,15... | collective-permute-start | bytes 245768 | tf_op jit(solution)/shard_map/ppermute | solution.py:32
  9.8 1.0 collective-permute-start
  10.9 1.3 reshape.42.gain_ref
  12.1 1.1 copy.58
  13.2 0.9 copy.59
  14.1 30.1 %copy.72.gm_ref.go_ref = bf16[8,2048,704]{2,1,0:T(8,128)(2,1)} copy(bf16[8,2048,704]{1,2,0:T(8,128)(2,1)} %param.23) | data formatting | bytes 46137344 | tf_op args[10]
  44.2 31.1 %copy.74.um_ref.uo_ref = bf16[8,2048,704]{2,1,0:T(8,128)(2,1)} copy(bf16[8,2048,704]{1,2,0:T(8,128)(2,1)} %param.24) | data formatting | bytes 46137344 | tf_op args[11]
  77.5 1.6 collective-permute-start.4
  79.1 3.5 %collective-permute-done.4 = bf16[64,640]{1,0:T(8,128)(2,1)S(1)} collective-permute-done((bf16[64,640]{1,0:T(8,128)(2,1)S(1)}, bf16[64,640]{1,0:T(8,128)(2,1)S(1)}, u32[]{:S(2)}, u32[]{:S(2)}) %collective-permute-start.4) | collective-permute-done | bytes 81952 | tf_op jit(solution)/shard_map/ppermute | solution.py:38
  82.6 0.9 collective-permute-start.5
  83.7 3.4 %collective-permute-done.5 = bf16[64,640]{1,0:T(8,128)(2,1)S(1)} collective-permute-done((bf16[64,640]{1,0:T(8,128)(2,1)S(1)}, bf16[64,640]{1,0:T(8,128)(2,1)S(1)}, u32[]{:S(2)}, u32[]{:S(2)}) %collective-permute-start.5) | collective-permute-done | bytes 81952 | tf_op jit(solution)/shard_map/ppermute | solution.py:38
  87.9 1.2 collective-permute-done.12
  90.0 7.9 %attend.1.here_ref = bf16[128,2048]{1,0:T(8,128)(2,1)} custom-call(s32[34]{0:T(128)} %pad_add_fusion.info, bf16[4,128,192]{2,1,0:T(8,128)(2,1)} %bitcast.115, bf16[8,64,640]{2,1,0:T(8,128)(2,1)} %copy-done.1, bf16[8,64,640]{2,1,0:T(8,128)(2,1)} %copy-done, bf16[512,1024]{1,0:T(8,128)(2,1)} %up_ref.1, bf16[512,2048]{1,0:T(8,128)(2,1)} %proj_ref.1), custom_call_target="tpu_custom_call" | custom-call | tf_op jit(solution)/shard_map/attend/pallas_call | solution.py:148
  100.0 0.8 copy-done.2
  100.8 3.2 %norm.1 = (bf16[128,1024]{1,0:T(8,128)(2,1)}, bf16[128,1024]{1,0:T(8,128)(2,1)}) custom-call(s32[34]{0:T(128)} %pad_add_fusion.info, bf16[128,2048]{1,0:T(8,128)(2,1)} %residual_ref.1, bf16[128,2048]{1,0:T(8,128)(2,1)} %attend.1.here_ref, bf16[128,2048]{1,0:T(8,128)(2,1)} %copy-done.2, bf16[1,2048]{1,0:T(2,128)(2,1)} %reshape.42.gain_ref), custom_call_target="tpu_custom_call" | custom-call | tf_op jit(solution)/shard_map/norm/pallas_call | solution.py:190
  104.2 1.0 collective-permute-start.19
  105.1 2.8 %collective-permute-start.18 = (bf16[128,1024]{1,0:T(8,128)(2,1)}, bf16[128,1024]{1,0:T(8,128)(2,1)S(1)}, u32[]{:S(2)}, u32[]{:S(2)}) collective-permute-start(bf16[128,1024]{1,0:T(8,128)(2,1)} %get-tuple-element.8), channel_id=1, source_target_pairs={{0,12},{2,14},{4,0},{6,2},{8,4},{10,6},{12,8},{14,10},{1,13},{3,15... | collective-permute-start | bytes 786440 | tf_op jit(solution)/shard_map/ppermute | solution.py:32
  107.9 1.1 collective-permute-start.17
  109.4 1.2 reshape.51.scale_ref
  110.5 1.0 bitcast_dynamic-update-slice_fusion.15
  111.5 3.5 %collective-permute-done.18 = bf16[128,1024]{1,0:T(8,128)(2,1)S(1)} collective-permute-done((bf16[128,1024]{1,0:T(8,128)(2,1)}, bf16[128,1024]{1,0:T(8,128)(2,1)S(1)}, u32[]{:S(2)}, u32[]{:S(2)}) %collective-permute-start.18) | collective-permute-done | bytes 262176 | tf_op jit(solution)/shard_map/ppermute | solution.py:32
  115.0 1.1 collective-permute-start.22
  116.3 16.0 %collective-permute-done.17 = bf16[128,1024]{1,0:T(8,128)(2,1)S(1)} collective-permute-done((bf16[128,1024]{1,0:T(8,128)(2,1)}, bf16[128,1024]{1,0:T(8,128)(2,1)S(1)}, u32[]{:S(2)}, u32[]{:S(2)}) %collective-permute-start.17) | collective-permute-done | bytes 262176 | tf_op jit(solution)/shard_map/ppermute | solution.py:32
  132.4 1.1 collective-permute-start.21
  133.4 0.9 collective-permute-start.20
  134.5 10.9 %collective-permute-done.20 = bf16[128,1024]{1,0:T(8,128)(2,1)S(1)} collective-permute-done((bf16[128,1024]{1,0:T(8,128)(2,1)S(1)}, bf16[128,1024]{1,0:T(8,128)(2,1)S(1)}, u32[]{:S(2)}, u32[]{:S(2)}) %collective-permute-start.20) | collective-permute-done | bytes 262176 | tf_op jit(solution)/shard_map/ppermute | solution.py:38
  146.1 2.1 convolution_convert_fusion.1
  148.9 1.6 collective-permute-done.28
  150.6 2.1 convolution_convert_fusion
  152.7 20.2 %expert_up.1.hidden_ref = bf16[8,128,704]{2,1,0:T(8,128)(2,1)} custom-call(s32[34]{0:T(128)} %pad_add_fusion.info, bf16[8,8,16,1024]{3,2,1,0:T(8,128)(2,1)} %bitcast.112, bf16[8,8,16,1024]{3,2,1,0:T(8,128)(2,1)} %bitcast.113, bf16[8,2048,704]{2,1,0:T(8,128)(2,1)} %copy.72.gm_ref.go_ref, bf16[8,2048,704]{2,1,0:T(8,128)(2,1)} %copy.72.gm_ref.go_ref, ...), custom_call_target="tpu_custom_call" | custom-call | tf_op jit(solution)/shard_map/expert_up/pallas_call | solution.py:223
  172.9 12.0 %expert_down.3 = bf16[8,128,1024]{2,1,0:T(8,128)(2,1)} custom-call(s32[34]{0:T(128)} %pad_add_fusion.info, bf16[8,128,704]{2,1,0:T(8,128)(2,1)} %expert_up.1.hidden_ref, bf16[8,704,2048]{2,1,0:T(8,128)(2,1)} %w_ref.3, bf16[8,128,128]{2,1,0:T(8,128)(2,1)} %get-tuple-element.9.combine_ref), custom_call_target="tpu_custom_call" | custom-call | tf_op jit(solution)/shard_map/expert_down/pallas_call | solution.py:265
  185.1 12.0 %expert_down.2 = bf16[8,128,1024]{2,1,0:T(8,128)(2,1)} custom-call(s32[34]{0:T(128)} %pad_add_fusion.info, bf16[8,128,704]{2,1,0:T(8,128)(2,1)} %expert_up.1.hidden_ref, bf16[8,704,2048]{2,1,0:T(8,128)(2,1)} %w_ref.3, bf16[8,128,128]{2,1,0:T(8,128)(2,1)} %get-tuple-element.9.combine_ref), custom_call_target="tpu_custom_call" | custom-call | tf_op jit(solution)/shard_map/expert_down/pallas_call | solution.py:265
  197.1 2.6 %add_convert_fusion = bf16[8,128,1024]{2,1,0:T(8,128)(2,1)S(1)} fusion(bf16[8,128,1024]{2,1,0:T(8,128)(2,1)S(1)} %collective-permute-done.31, bf16[8,128,1024]{2,1,0:T(8,128)(2,1)} %expert_down.2), kind=kLoop, calls=%fused_computation | loop fusion | flops 4194304 | bytes 6291456 | tf_op jit(solution)/shard_map/convert_element_type | solution.py:359
  199.8 1.2 collective-permute-start.37
  201.0 0.9 collective-permute-start.35
  201.9 1.1 collective-permute-start.33
  203.0 0.9 collective-permute-start.32
  203.9 5.1 %collective-permute-done.37 = bf16[128,1024]{1,0:T(8,128)(2,1)S(1)} collective-permute-done((bf16[128,1024]{1,0:T(8,128)(2,1)S(1)}, bf16[128,1024]{1,0:T(8,128)(2,1)S(1)}, u32[]{:S(2)}, u32[]{:S(2)}) %collective-permute-start.37) | collective-permute-done | bytes 262176 | tf_op jit(solution)/shard_map/ppermute | solution.py:38
  209.0 5.6 %collective-permute-done.35 = bf16[128,1024]{1,0:T(8,128)(2,1)S(1)} collective-permute-done((bf16[128,1024]{1,0:T(8,128)(2,1)S(1)}, bf16[128,1024]{1,0:T(8,128)(2,1)S(1)}, u32[]{:S(2)}, u32[]{:S(2)}) %collective-permute-start.35) | collective-permute-done | bytes 262176 | tf_op jit(solution)/shard_map/ppermute | solution.py:38
  214.6 5.6 %collective-permute-done.33 = bf16[128,1024]{1,0:T(8,128)(2,1)S(1)} collective-permute-done((bf16[128,1024]{1,0:T(8,128)(2,1)S(1)}, bf16[128,1024]{1,0:T(8,128)(2,1)S(1)}, u32[]{:S(2)}, u32[]{:S(2)}) %collective-permute-start.33) | collective-permute-done | bytes 262176 | tf_op jit(solution)/shard_map/ppermute | solution.py:38
  220.6 2.8 %collective-permute-start.38 = (bf16[128,1024]{1,0:T(8,128)(2,1)S(1)}, bf16[128,1024]{1,0:T(8,128)(2,1)S(1)}, u32[]{:S(2)}, u32[]{:S(2)}) collective-permute-start(bf16[128,1024]{1,0:T(8,128)(2,1)S(1)} %get-tuple-element.20), channel_id=1, source_target_pairs={{0,4},{2,6},{4,8},{6,10},{8,12},{10,14},{12,0},{14,2},{1,5},{3,7},... | collective-permute-start | bytes 786440 | tf_op jit(solution)/shard_map/ppermute | solution.py:32
  223.4 1.4 collective-permute-start.36
  225.3 8.0 %collective-permute-done.34 = bf16[128,1024]{1,0:T(8,128)(2,1)S(1)} collective-permute-done((bf16[128,1024]{1,0:T(8,128)(2,1)S(1)}, bf16[128,1024]{1,0:T(8,128)(2,1)S(1)}, u32[]{:S(2)}, u32[]{:S(2)}) %collective-permute-start.34) | collective-permute-done | bytes 262176 | tf_op jit(solution)/shard_map/ppermute | solution.py:32
  233.3 3.6 %collective-permute-done.38 = bf16[128,1024]{1,0:T(8,128)(2,1)S(1)} collective-permute-done((bf16[128,1024]{1,0:T(8,128)(2,1)S(1)}, bf16[128,1024]{1,0:T(8,128)(2,1)S(1)}, u32[]{:S(2)}, u32[]{:S(2)}) %collective-permute-start.38) | collective-permute-done | bytes 262176 | tf_op jit(solution)/shard_map/ppermute | solution.py:32
  236.8 10.0 %collective-permute-done.36 = bf16[128,1024]{1,0:T(8,128)(2,1)S(1)} collective-permute-done((bf16[128,1024]{1,0:T(8,128)(2,1)S(1)}, bf16[128,1024]{1,0:T(8,128)(2,1)S(1)}, u32[]{:S(2)}, u32[]{:S(2)}) %collective-permute-start.36) | collective-permute-done | bytes 262176 | tf_op jit(solution)/shard_map/ppermute | solution.py:32
  246.8 1.0 fusion.8
  (119 shorter events, 11.4 us)
Async XLA Ops:
  3.1 73.3 %collective-permute-start.3 = (bf16[64,640]{1,0:T(8,128)(2,1)S(1)}, bf16[64,640]{1,0:T(8,128)(2,1)S(1)}, u32[]{:S(2)}, u32[]{:S(2)}) collective-permute-start(bf16[64,640]{1,0:T(8,128)(2,1)S(1)} %get-tuple-element.12), channel_id=1, source_target_pairs={{0,2},{2,0},{4,6},{6,4},{8,10},{10,8},{12,14},{14,12},{1,3},{3,1},... | collective-permute-start | bytes 245768 | tf_op jit(solution)/shard_map/ppermute | solution.py:38
  6.1 69.8 %collective-permute-start.2 = (bf16[64,640]{1,0:T(8,128)(2,1)S(1)}, bf16[64,640]{1,0:T(8,128)(2,1)S(1)}, u32[]{:S(2)}, u32[]{:S(2)}) collective-permute-start(bf16[64,640]{1,0:T(8,128)(2,1)S(1)} %get-tuple-element.12), channel_id=1, source_target_pairs={{0,12},{2,14},{4,0},{6,2},{8,4},{10,6},{12,8},{14,10},{1,13},{3,15... | collective-permute-start | bytes 245768 | tf_op jit(solution)/shard_map/ppermute | solution.py:32
  9.8 67.2 %collective-permute-start.1 = (bf16[64,640]{1,0:T(8,128)(2,1)S(1)}, bf16[64,640]{1,0:T(8,128)(2,1)S(1)}, u32[]{:S(2)}, u32[]{:S(2)}) collective-permute-start(bf16[64,640]{1,0:T(8,128)(2,1)S(1)} %get-tuple-element.12), channel_id=1, source_target_pairs={{0,8},{2,10},{4,12},{6,14},{8,0},{10,2},{12,4},{14,6},{1,9},{3,11}... | collective-permute-start | bytes 245768 | tf_op jit(solution)/shard_map/ppermute | solution.py:32
  9.8 67.2 %collective-permute-start = (bf16[64,640]{1,0:T(8,128)(2,1)S(1)}, bf16[64,640]{1,0:T(8,128)(2,1)S(1)}, u32[]{:S(2)}, u32[]{:S(2)}) collective-permute-start(bf16[64,640]{1,0:T(8,128)(2,1)S(1)} %get-tuple-element.12), channel_id=1, source_target_pairs={{0,4},{2,6},{4,8},{6,10},{8,12},{10,14},{12,0},{14,2},{1,5},{3,7},... | collective-permute-start | bytes 245768 | tf_op jit(solution)/shard_map/ppermute | solution.py:32
  10.8 66.8 %collective-permute-start.7 = (bf16[64,640]{1,0:T(8,128)(2,1)S(1)}, bf16[64,640]{1,0:T(8,128)(2,1)S(1)}, u32[]{:S(2)}, u32[]{:S(2)}) collective-permute-start(bf16[64,640]{1,0:T(8,128)(2,1)S(1)} %get-tuple-element.12), channel_id=1, source_target_pairs={{0,1},{1,0},{2,3},{3,2},{4,5},{5,4},{6,7},{7,6},{8,9},{9,8},{10,11... | collective-permute-start | bytes 245768 | tf_op jit(solution)/shard_map/ppermute | solution.py:42
  44.2 31.1 %copy-start.4 = (s32[16]{0:T(128)S(1)}, s32[16]{0:T(128)}, u32[]{:S(2)}) copy-start(s32[16]{0:T(128)} %param.17) | copy-start | bytes 196
  44.2 31.1 %copy-start.5 = (s32[16]{0:T(128)S(1)}, s32[16]{0:T(128)}, u32[]{:S(2)}) copy-start(s32[16]{0:T(128)} %param.16) | copy-start | bytes 196
  75.9 11.9 %collective-permute-start.10 = (bf16[64,640]{1,0:T(8,128)(2,1)S(1)}, bf16[64,640]{1,0:T(8,128)(2,1)S(1)}, u32[]{:S(2)}, u32[]{:S(2)}) collective-permute-start(bf16[64,640]{1,0:T(8,128)(2,1)S(1)} %collective-permute-done.2), channel_id=1, source_target_pairs={{0,1},{1,0},{2,3},{3,2},{4,5},{5,4},{6,7},{7,6},{8,9},{9,8},{10,11... | collective-permute-start | bytes 245768 | tf_op jit(solution)/shard_map/ppermute | solution.py:42
  76.4 7.2 %collective-permute-start.6 = (bf16[64,640]{1,0:T(8,128)(2,1)S(1)}, bf16[64,640]{1,0:T(8,128)(2,1)S(1)}, u32[]{:S(2)}, u32[]{:S(2)}) collective-permute-start(bf16[64,640]{1,0:T(8,128)(2,1)S(1)} %collective-permute-done.2), channel_id=1, source_target_pairs={{0,2},{2,0},{4,6},{6,4},{8,10},{10,8},{12,14},{14,12},{1,3},{3,1},... | collective-permute-start | bytes 245768 | tf_op jit(solution)/shard_map/ppermute | solution.py:38
  76.9 10.9 %collective-permute-start.11 = (bf16[64,640]{1,0:T(8,128)(2,1)S(1)}, bf16[64,640]{1,0:T(8,128)(2,1)S(1)}, u32[]{:S(2)}, u32[]{:S(2)}) collective-permute-start(bf16[64,640]{1,0:T(8,128)(2,1)S(1)} %collective-permute-done.3), channel_id=1, source_target_pairs={{0,1},{1,0},{2,3},{3,2},{4,5},{5,4},{6,7},{7,6},{8,9},{9,8},{10,11... | collective-permute-start | bytes 245768 | tf_op jit(solution)/shard_map/ppermute | solution.py:42
  77.0 10.8 %collective-permute-start.9 = (bf16[64,640]{1,0:T(8,128)(2,1)S(1)}, bf16[64,640]{1,0:T(8,128)(2,1)S(1)}, u32[]{:S(2)}, u32[]{:S(2)}) collective-permute-start(bf16[64,640]{1,0:T(8,128)(2,1)S(1)} %collective-permute-done.1), channel_id=1, source_target_pairs={{0,1},{1,0},{2,3},{3,2},{4,5},{5,4},{6,7},{7,6},{8,9},{9,8},{10,11... | collective-permute-start | bytes 245768 | tf_op jit(solution)/shard_map/ppermute | solution.py:42
  77.5 5.1 %collective-permute-start.4 = (bf16[64,640]{1,0:T(8,128)(2,1)S(1)}, bf16[64,640]{1,0:T(8,128)(2,1)S(1)}, u32[]{:S(2)}, u32[]{:S(2)}) collective-permute-start(bf16[64,640]{1,0:T(8,128)(2,1)S(1)} %collective-permute-done), channel_id=1, source_target_pairs={{0,2},{2,0},{4,6},{6,4},{8,10},{10,8},{12,14},{14,12},{1,3},{3,1},... | collective-permute-start | bytes 245768 | tf_op jit(solution)/shard_map/ppermute | solution.py:38
  82.6 4.4 %collective-permute-start.5 = (bf16[64,640]{1,0:T(8,128)(2,1)S(1)}, bf16[64,640]{1,0:T(8,128)(2,1)S(1)}, u32[]{:S(2)}, u32[]{:S(2)}) collective-permute-start(bf16[64,640]{1,0:T(8,128)(2,1)S(1)} %collective-permute-done.1), channel_id=1, source_target_pairs={{0,2},{2,0},{4,6},{6,4},{8,10},{10,8},{12,14},{14,12},{1,3},{3,1},... | collective-permute-start | bytes 245768 | tf_op jit(solution)/shard_map/ppermute | solution.py:38
  83.6 3.5 %collective-permute-start.8 = (bf16[64,640]{1,0:T(8,128)(2,1)S(1)}, bf16[64,640]{1,0:T(8,128)(2,1)S(1)}, u32[]{:S(2)}, u32[]{:S(2)}) collective-permute-start(bf16[64,640]{1,0:T(8,128)(2,1)S(1)} %collective-permute-done), channel_id=1, source_target_pairs={{0,1},{1,0},{2,3},{3,2},{4,5},{5,4},{6,7},{7,6},{8,9},{9,8},{10,11... | collective-permute-start | bytes 245768 | tf_op jit(solution)/shard_map/ppermute | solution.py:42
  87.1 2.0 collective-permute-start.14
  87.1 2.6 %copy-start.1 = (bf16[8,64,640]{2,1,0:T(8,128)(2,1)}, bf16[8,64,640]{2,1,0:T(8,128)(2,1)S(1)}, u32[]{:S(2)}) copy-start(bf16[8,64,640]{2,1,0:T(8,128)(2,1)S(1)} %bitcast_dynamic-update-slice_fusion.24.mine_ref) | copy-start | bytes 1966084
  87.1 2.0 collective-permute-start.13
  87.7 1.3 collective-permute-start.12
  89.2 0.9 copy-start
  97.9 2.1 collective-permute-start.15
  100.0 0.8 copy-start.2
  104.0 11.0 %collective-permute-start.23 = (bf16[128,1024]{1,0:T(8,128)(2,1)}, bf16[128,1024]{1,0:T(8,128)(2,1)S(1)}, u32[]{:S(2)}, u32[]{:S(2)}) collective-permute-start(bf16[128,1024]{1,0:T(8,128)(2,1)} %get-tuple-element.8), channel_id=1, source_target_pairs={{0,1},{1,0},{2,3},{3,2},{4,5},{5,4},{6,7},{7,6},{8,9},{9,8},{10,11... | collective-permute-start | bytes 786440 | tf_op jit(solution)/shard_map/ppermute | solution.py:42
  104.2 12.0 %collective-permute-start.19 = (bf16[128,1024]{1,0:T(8,128)(2,1)}, bf16[128,1024]{1,0:T(8,128)(2,1)S(1)}, u32[]{:S(2)}, u32[]{:S(2)}) collective-permute-start(bf16[128,1024]{1,0:T(8,128)(2,1)} %get-tuple-element.8), channel_id=1, source_target_pairs={{0,2},{2,0},{4,6},{6,4},{8,10},{10,8},{12,14},{14,12},{1,3},{3,1},... | collective-permute-start | bytes 786440 | tf_op jit(solution)/shard_map/ppermute | solution.py:38
  105.1 9.9 %collective-permute-start.18 = (bf16[128,1024]{1,0:T(8,128)(2,1)}, bf16[128,1024]{1,0:T(8,128)(2,1)S(1)}, u32[]{:S(2)}, u32[]{:S(2)}) collective-permute-start(bf16[128,1024]{1,0:T(8,128)(2,1)} %get-tuple-element.8), channel_id=1, source_target_pairs={{0,12},{2,14},{4,0},{6,2},{8,4},{10,6},{12,8},{14,10},{1,13},{3,15... | collective-permute-start | bytes 786440 | tf_op jit(solution)/shard_map/ppermute | solution.py:32
  107.9 24.4 %collective-permute-start.17 = (bf16[128,1024]{1,0:T(8,128)(2,1)}, bf16[128,1024]{1,0:T(8,128)(2,1)S(1)}, u32[]{:S(2)}, u32[]{:S(2)}) collective-permute-start(bf16[128,1024]{1,0:T(8,128)(2,1)} %get-tuple-element.8), channel_id=1, source_target_pairs={{0,8},{2,10},{4,12},{6,14},{8,0},{10,2},{12,4},{14,6},{1,9},{3,11}... | collective-permute-start | bytes 786440 | tf_op jit(solution)/shard_map/ppermute | solution.py:32
  109.0 24.4 %collective-permute-start.16 = (bf16[128,1024]{1,0:T(8,128)(2,1)}, bf16[128,1024]{1,0:T(8,128)(2,1)S(1)}, u32[]{:S(2)}, u32[]{:S(2)}) collective-permute-start(bf16[128,1024]{1,0:T(8,128)(2,1)} %get-tuple-element.8), channel_id=1, source_target_pairs={{0,4},{2,6},{4,8},{6,10},{8,12},{10,14},{12,0},{14,2},{1,5},{3,7},... | collective-permute-start | bytes 786440 | tf_op jit(solution)/shard_map/ppermute | solution.py:32
  115.0 33.8 %collective-permute-start.26 = (bf16[128,1024]{1,0:T(8,128)(2,1)S(1)}, bf16[128,1024]{1,0:T(8,128)(2,1)S(1)}, u32[]{:S(2)}, u32[]{:S(2)}) collective-permute-start(bf16[128,1024]{1,0:T(8,128)(2,1)S(1)} %collective-permute-done.18), channel_id=1, source_target_pairs={{0,1},{1,0},{2,3},{3,2},{4,5},{5,4},{6,7},{7,6},{8,9},{9,8},{10,11... | collective-permute-start | bytes 786440 | tf_op jit(solution)/shard_map/ppermute | solution.py:42
  115.0 31.0 %collective-permute-start.22 = (bf16[128,1024]{1,0:T(8,128)(2,1)S(1)}, bf16[128,1024]{1,0:T(8,128)(2,1)S(1)}, u32[]{:S(2)}, u32[]{:S(2)}) collective-permute-start(bf16[128,1024]{1,0:T(8,128)(2,1)S(1)} %collective-permute-done.18), channel_id=1, source_target_pairs={{0,2},{2,0},{4,6},{6,4},{8,10},{10,8},{12,14},{14,12},{1,3},{3,1},... | collective-permute-start | bytes 786440 | tf_op jit(solution)/shard_map/ppermute | solution.py:38
  116.1 32.8 %collective-permute-start.27 = (bf16[128,1024]{1,0:T(8,128)(2,1)S(1)}, bf16[128,1024]{1,0:T(8,128)(2,1)S(1)}, u32[]{:S(2)}, u32[]{:S(2)}) collective-permute-start(bf16[128,1024]{1,0:T(8,128)(2,1)S(1)} %collective-permute-done.19), channel_id=1, source_target_pairs={{0,1},{1,0},{2,3},{3,2},{4,5},{5,4},{6,7},{7,6},{8,9},{9,8},{10,11... | collective-permute-start | bytes 786440 | tf_op jit(solution)/shard_map/ppermute | solution.py:42
  132.4 13.1 %collective-permute-start.21 = (bf16[128,1024]{1,0:T(8,128)(2,1)S(1)}, bf16[128,1024]{1,0:T(8,128)(2,1)S(1)}, u32[]{:S(2)}, u32[]{:S(2)}) collective-permute-start(bf16[128,1024]{1,0:T(8,128)(2,1)S(1)} %collective-permute-done.17), channel_id=1, source_target_pairs={{0,2},{2,0},{4,6},{6,4},{8,10},{10,8},{12,14},{14,12},{1,3},{3,1},... | collective-permute-start | bytes 786440 | tf_op jit(solution)/shard_map/ppermute | solution.py:38
  133.4 12.0 %collective-permute-start.20 = (bf16[128,1024]{1,0:T(8,128)(2,1)S(1)}, bf16[128,1024]{1,0:T(8,128)(2,1)S(1)}, u32[]{:S(2)}, u32[]{:S(2)}) collective-permute-start(bf16[128,1024]{1,0:T(8,128)(2,1)S(1)} %collective-permute-done.16), channel_id=1, source_target_pairs={{0,2},{2,0},{4,6},{6,4},{8,10},{10,8},{12,14},{14,12},{1,3},{3,1},... | collective-permute-start | bytes 786440 | tf_op jit(solution)/shard_map/ppermute | solution.py:38
  145.4 3.3 %collective-permute-start.25 = (bf16[128,1024]{1,0:T(8,128)(2,1)S(1)}, bf16[128,1024]{1,0:T(8,128)(2,1)S(1)}, u32[]{:S(2)}, u32[]{:S(2)}) collective-permute-start(bf16[128,1024]{1,0:T(8,128)(2,1)S(1)} %collective-permute-done.17), channel_id=1, source_target_pairs={{0,1},{1,0},{2,3},{3,2},{4,5},{5,4},{6,7},{7,6},{8,9},{9,8},{10,11... | collective-permute-start | bytes 786440 | tf_op jit(solution)/shard_map/ppermute | solution.py:42
  145.4 2.8 %collective-permute-start.24 = (bf16[128,1024]{1,0:T(8,128)(2,1)S(1)}, bf16[128,1024]{1,0:T(8,128)(2,1)S(1)}, u32[]{:S(2)}, u32[]{:S(2)}) collective-permute-start(bf16[128,1024]{1,0:T(8,128)(2,1)S(1)} %collective-permute-done.16), channel_id=1, source_target_pairs={{0,1},{1,0},{2,3},{3,2},{4,5},{5,4},{6,7},{7,6},{8,9},{9,8},{10,11... | collective-permute-start | bytes 786440 | tf_op jit(solution)/shard_map/ppermute | solution.py:42
  148.2 2.3 collective-permute-start.30
  148.2 2.3 collective-permute-start.29
  148.7 1.7 collective-permute-start.28
  184.9 12.2 %collective-permute-start.31 = (bf16[8,128,1024]{2,1,0:T(8,128)(2,1)}, bf16[8,128,1024]{2,1,0:T(8,128)(2,1)S(1)}, u32[]{:S(2)}, u32[]{:S(2)}) collective-permute-start(bf16[8,128,1024]{2,1,0:T(8,128)(2,1)} %expert_down.3), channel_id=1, source_target_pairs={{0,1},{1,0},{2,3},{3,2},{4,5},{5,4},{6,7},{7,6},{8,9},{9,8},{10,11... | collective-permute-start | bytes 6291464 | tf_op jit(solution)/shard_map/ppermute | solution.py:42
  199.7 47.1 %copy-start.3 = (bf16[128,1024]{1,0:T(8,128)(2,1)S(1)}, bf16[128,1024]{1,0:T(8,128)(2,1)}, u32[]{:S(2)}) copy-start(bf16[128,1024]{1,0:T(8,128)(2,1)} %get-tuple-element.7) | copy-start | bytes 786436
  199.8 9.2 %collective-permute-start.37 = (bf16[128,1024]{1,0:T(8,128)(2,1)S(1)}, bf16[128,1024]{1,0:T(8,128)(2,1)S(1)}, u32[]{:S(2)}, u32[]{:S(2)}) collective-permute-start(bf16[128,1024]{1,0:T(8,128)(2,1)S(1)} %get-tuple-element.16), channel_id=1, source_target_pairs={{0,2},{2,0},{4,6},{6,4},{8,10},{10,8},{12,14},{14,12},{1,3},{3,1},... | collective-permute-start | bytes 786440 | tf_op jit(solution)/shard_map/ppermute | solution.py:38
  201.0 13.7 %collective-permute-start.35 = (bf16[128,1024]{1,0:T(8,128)(2,1)S(1)}, bf16[128,1024]{1,0:T(8,128)(2,1)S(1)}, u32[]{:S(2)}, u32[]{:S(2)}) collective-permute-start(bf16[128,1024]{1,0:T(8,128)(2,1)S(1)} %get-tuple-element.17), channel_id=1, source_target_pairs={{0,2},{2,0},{4,6},{6,4},{8,10},{10,8},{12,14},{14,12},{1,3},{3,1},... | collective-permute-start | bytes 786440 | tf_op jit(solution)/shard_map/ppermute | solution.py:38
  201.9 18.3 %collective-permute-start.33 = (bf16[128,1024]{1,0:T(8,128)(2,1)S(1)}, bf16[128,1024]{1,0:T(8,128)(2,1)S(1)}, u32[]{:S(2)}, u32[]{:S(2)}) collective-permute-start(bf16[128,1024]{1,0:T(8,128)(2,1)S(1)} %get-tuple-element.18), channel_id=1, source_target_pairs={{0,2},{2,0},{4,6},{6,4},{8,10},{10,8},{12,14},{14,12},{1,3},{3,1},... | collective-permute-start | bytes 786440 | tf_op jit(solution)/shard_map/ppermute | solution.py:38
  203.0 22.3 %collective-permute-start.32 = (bf16[128,1024]{1,0:T(8,128)(2,1)S(1)}, bf16[128,1024]{1,0:T(8,128)(2,1)S(1)}, u32[]{:S(2)}, u32[]{:S(2)}) collective-permute-start(bf16[128,1024]{1,0:T(8,128)(2,1)S(1)} %get-tuple-element.15), channel_id=1, source_target_pairs={{0,2},{2,0},{4,6},{6,4},{8,10},{10,8},{12,14},{14,12},{1,3},{3,1},... | collective-permute-start | bytes 786440 | tf_op jit(solution)/shard_map/ppermute | solution.py:38
  220.5 12.7 %collective-permute-start.34 = (bf16[128,1024]{1,0:T(8,128)(2,1)S(1)}, bf16[128,1024]{1,0:T(8,128)(2,1)S(1)}, u32[]{:S(2)}, u32[]{:S(2)}) collective-permute-start(bf16[128,1024]{1,0:T(8,128)(2,1)S(1)} %get-tuple-element.19), channel_id=1, source_target_pairs={{0,12},{2,14},{4,0},{6,2},{8,4},{10,6},{12,8},{14,10},{1,13},{3,15... | collective-permute-start | bytes 786440 | tf_op jit(solution)/shard_map/ppermute | solution.py:32
  220.6 16.2 %collective-permute-start.38 = (bf16[128,1024]{1,0:T(8,128)(2,1)S(1)}, bf16[128,1024]{1,0:T(8,128)(2,1)S(1)}, u32[]{:S(2)}, u32[]{:S(2)}) collective-permute-start(bf16[128,1024]{1,0:T(8,128)(2,1)S(1)} %get-tuple-element.20), channel_id=1, source_target_pairs={{0,4},{2,6},{4,8},{6,10},{8,12},{10,14},{12,0},{14,2},{1,5},{3,7},... | collective-permute-start | bytes 786440 | tf_op jit(solution)/shard_map/ppermute | solution.py:32
  223.4 23.4 %collective-permute-start.36 = (bf16[128,1024]{1,0:T(8,128)(2,1)S(1)}, bf16[128,1024]{1,0:T(8,128)(2,1)S(1)}, u32[]{:S(2)}, u32[]{:S(2)}) collective-permute-start(bf16[128,1024]{1,0:T(8,128)(2,1)S(1)} %get-tuple-element.21), channel_id=1, source_target_pairs={{0,8},{2,10},{4,12},{6,14},{8,0},{10,2},{12,4},{14,6},{1,9},{3,11}... | collective-permute-start | bytes 786440 | tf_op jit(solution)/shard_map/ppermute | solution.py:32

commit v2 on v1

--- a/solution.py
+++ b/solution.py
@@ -45,29 +45,38 @@
 def each(send, pieces, count):
     if count <= FEW:
         return [send(piece) for piece in pieces]
-    return list(send(jnp.stack(pieces)))
+    return list(send(jnp.stack(list(pieces))))
 
 
 def spread(block, count):
     slow, fast = grid_of(count)
-    line = [block] + [shift_slow(block, s, count) for s in range(1, slow)]
+    line = [block]
+    for _ in range(1, slow):
+        line.append(shift_slow(line[-1], 1, count))
     found = list(line)
     for r in range(1, fast):
         found += each(lambda piece: shift_fast(piece, r, count), line, count)
     return found
 
 
-def collect(parts, count):
-    slow, fast = grid_of(count)
-    sums = [part.astype(jnp.float32) for part in parts[:slow]]
-    for r in range(1, fast):
-        arrived = each(lambda piece: shift_fast(piece, -r, count), parts[r * slow : (r + 1) * slow], count)
-        sums = [total + piece.astype(jnp.float32) for total, piece in zip(sums, arrived)]
-    arrived = [shift_slow(sums[s].astype(jnp.bfloat16), -s, count) for s in range(1, slow)]
-    total = sums[0]
-    for piece in arrived:
+def summed(pieces):
+    total = pieces[0].astype(jnp.float32)
+    for piece in pieces[1:]:
         total = total + piece.astype(jnp.float32)
     return total
+
+
+def collect(kept, away, count):
+    slow, fast = grid_of(count)
+    terms = [[kept[s], away[s]] for s in range(slow)]
+    for r in range(1, fast):
+        here = range(r * slow, (r + 1) * slow)
+        parts = [summed([kept[c], away[c]]).astype(jnp.bfloat16) for c in here]
+        for s, piece in enumerate(each(lambda piece: shift_fast(piece, -r, count), parts, count)):
+            terms[s].append(piece)
+    sums = [summed(pieces) for pieces in terms]
+    arrived = [shift_slow(sums[s].astype(jnp.bfloat16), -s, count) for s in range(1, slow)]
+    return summed([sums[0]] + arrived)
 
 
 def owner_of(place, me, count):
@@ -201,84 +210,127 @@
     )(info, residual, here, there, gain.reshape(1, width))
 
 
-def up_kernel(info, mine_ref, other_ref, gm_ref, go_ref, um_ref, uo_ref, scale_ref, out_ref):
-    rows = out_ref.shape[1]
-    mine = mine_ref[...].reshape(rows, mine_ref.shape[3])
-    other = other_ref[...].reshape(rows, other_ref.shape[3])
-    gate = jnp.dot(mine, gm_ref[0], preferred_element_type=jnp.float32)
-    gate = gate + jnp.dot(other, go_ref[0], preferred_element_type=jnp.float32)
-    upper = jnp.dot(mine, um_ref[0], preferred_element_type=jnp.float32)
-    upper = upper + jnp.dot(other, uo_ref[0], preferred_element_type=jnp.float32)
-    hidden = gate / (1.0 + jnp.exp(-gate)) * upper * scale_ref[0]
-    out_ref[0] = hidden.astype(jnp.bfloat16)
-
-
-def up(info, mine, other, w_gate, w_up, scale):
-    count, here, slots, half = mine.shape
-    hidden = w_gate.shape[2]
-    rows = count * slots
-    rows_spec = pl.BlockSpec((count, 1, slots, half), lambda e, info: (0, e, 0, 0))
-    mine_spec = pl.BlockSpec((1, half, hidden), lambda e, info: (e, info[1], 0))
-    other_spec = pl.BlockSpec((1, half, hidden), lambda e, info: (e, 1 - info[1], 0))
+def pack_kernel(info, latent_ref, facts_ref, out_ref):
+    rows = jnp.concatenate([latent_ref[...].astype(jnp.float32), facts_ref[...]], axis=0)
+    span = out_ref.shape[0]
+    tokens = rows.T.astype(jnp.bfloat16)
+    out_ref[...] = jnp.where(info[1] == 0, tokens[:span], tokens[span:])
+
+
+def pack(info, latent, expert_ids, route_weights):
+    local_rows, base = latent.shape
+    weights = route_weights.T
+    high = lax.reduce_precision(weights, 8, 7)
+    pad = jnp.zeros((WIDE - base - 3 * TOP, local_rows), jnp.float32)
+    facts = jnp.concatenate([expert_ids.T.astype(jnp.float32), high, weights - high, pad], axis=0)
     return pl.pallas_call(
-        up_kernel,
+        pack_kernel,
+        grid_spec=pltpu.PrefetchScalarGridSpec(
+            num_scalar_prefetch=1,
+            grid=(1,),
+            in_specs=[
+                pl.BlockSpec((base, local_rows), lambda i, *_: (0, 0)),
+                pl.BlockSpec(facts.shape, lambda i, *_: (0, 0)),
+            ],
+            out_specs=pl.BlockSpec((local_rows // 2, WIDE), lambda i, *_: (0, 0)),
+        ),
+        out_shape=jax.ShapeDtypeStruct((local_rows // 2, WIDE), jnp.bfloat16),
+        compiler_params=pltpu.CompilerParams(vmem_limit_bytes=VMEM_LIMIT),
+        name="pack",
+    )(info, latent.T, facts)
+
+
+def expert_rows(rows, gate_ref, up_ref, down_ref, scale_ref):
+    by_columns = (((1,), (1,)), ((), ()))
+    gate = lax.dot_general(rows, gate_ref[0], by_columns, preferred_element_type=jnp.float32)
+    upper = lax.dot_general(rows, up_ref[0], by_columns, preferred_element_type=jnp.float32)
+    hidden = (gate / (1.0 + jnp.exp(-gate)) * upper * scale_ref[0]).astype(jnp.bfloat16)
+    return jnp.dot(hidden, down_ref[0], preferred_element_type=jnp.float32).astype(jnp.bfloat16)
+
+
+def plain_kernel(info, rows_ref, gate_ref, up_ref, down_ref, scale_ref, out_ref):
+    out_ref[0] = expert_rows(rows_ref[0], gate_ref, up_ref, down_ref, scale_ref)
+
+
+def fused_kernel(count, info, *refs):
+    mine, other = refs[:count], refs[count : 2 * count]
+    pick_ref, combine_ref, gate_ref, up_ref, down_ref, scale_ref = refs[2 * count : 2 * count + 6]
+    kept, away = refs[2 * count + 6 : 3 * count + 6], refs[3 * count + 6 : 4 * count + 6]
+    picked, held = refs[4 * count + 6 :]
+    expert = pl.program_id(0)
+    here = picked.shape[0]
+    half = picked.shape[2] // 2
+    side = info[1]
+    near = pl.ds(pl.multiple_of(side * half, half), half)
+    far = pl.ds(pl.multiple_of((1 - side) * half, half), half)
+
+    @pl.when(expert == 0)
+    def _():
+        for c in range(count):
+            for columns, block in ((near, mine[c]), (far, other[c])):
+                rows = jnp.dot(pick_ref[c], block[...], preferred_element_type=jnp.float32).astype(jnp.bfloat16)
+                for e in range(here):
+                    picked[e, c * SLOTS : (c + 1) * SLOTS, columns] = rows[e * SLOTS : (e + 1) * SLOTS]
+
+    result = expert_rows(picked[expert], gate_ref, up_ref, down_ref, scale_ref)
+    place = pl.ds(pl.multiple_of(expert * SLOTS, SLOTS), SLOTS)
+    for c in range(count):
+        held[c, place, :] = result[c * SLOTS : (c + 1) * SLOTS]
+
+    @pl.when(expert == here - 1)
+    def _():
+        for c in range(count):
+            for columns, out in ((far, away[c]), (near, kept[c])):
+                total = jnp.dot(combine_ref[c], held[c, :, columns], preferred_element_type=jnp.float32)
+                out[...] = total.astype(jnp.bfloat16)
+
+
+def expert_specs(w_gate, rows):
+    hidden, width = w_gate.shape[1:]
+    weight = pl.BlockSpec((1, hidden, width), lambda e, info: (e, 0, 0))
+    return [weight, weight, weight, pl.BlockSpec((1, rows, 1), lambda e, info: (e, 0, 0))]
+
+
+def experts_plain(info, picked, w_gate, w_up, w_down, scale):
+    here, rows, width = picked.shape
+    rows_spec = pl.BlockSpec((1, rows, width), lambda e, info: (e, 0, 0))
+    return pl.pallas_call(
+        plain_kernel,
         grid_spec=pltpu.PrefetchScalarGridSpec(
             num_scalar_prefetch=1,
             grid=(here,),
-            in_specs=[
-                rows_spec,
-                rows_spec,
-                mine_spec,
-                other_spec,
-                mine_spec,
-                other_spec,
-                pl.BlockSpec((1, rows, 1), lambda e, info: (e, 0, 0)),
-            ],
-            out_specs=pl.BlockSpec((1, rows, hidden), lambda e, info: (e, 0, 0)),
+            in_specs=[rows_spec] + expert_specs(w_gate, rows),
+            out_specs=rows_spec,
         ),
-        out_shape=jax.ShapeDtypeStruct((here, rows, hidden), jnp.bfloat16),
+        out_shape=jax.ShapeDtypeStruct(picked.shape, jnp.bfloat16),
         compiler_params=pltpu.CompilerParams(vmem_limit_bytes=VMEM_LIMIT),
-        name="expert_up",
-    )(info, mine, other, w_gate, w_gate, w_up, w_up, scale)
-
-
-def down_kernel(info, hidden_ref, w_ref, combine_ref, out_ref, held):
-    expert = pl.program_id(0)
-    count, here, slots, half = held.shape
-    result = jnp.dot(hidden_ref[0], w_ref[0], preferred_element_type=jnp.float32).astype(jnp.bfloat16)
-    held[:, pl.ds(expert, 1)] = result.reshape(count, 1, slots, half)
-
-    @pl.when(expert == pl.num_programs(0) - 1)
-    def _():
-        def place(c, _):
-            rows = held[c].reshape(here * slots, half)
-            out_ref[c] = jnp.dot(combine_ref[c], rows, preferred_element_type=jnp.float32).astype(jnp.bfloat16)
-            return 0
-
-        lax.fori_loop(0, count, place, 0)
-
-
-def down(info, hidden, w_down, combine, flip):
-    here, rows, units = hidden.shape
-    count, local, _ = combine.shape
-    half = w_down.shape[2] // 2
-    return pl.pallas_call(
-        down_kernel,
+        name="experts",
+    )(info, picked, w_gate, w_up, w_down, scale)
+
+
+def experts_fused(info, mine, other, pick, combine, w_gate, w_up, w_down, scale):
+    count, (local, half) = len(mine), mine[0].shape
+    here, rows, _ = scale.shape
+    whole = pl.BlockSpec((local, half), lambda e, info: (0, 0))
+    outs = pl.pallas_call(
+        functools.partial(fused_kernel, count),
         grid_spec=pltpu.PrefetchScalarGridSpec(
             num_scalar_prefetch=1,
             grid=(here,),
-            in_specs=[
-                pl.BlockSpec((1, rows, units), lambda e, info: (e, 0, 0)),
-                pl.BlockSpec((1, units, half), lambda e, info: (e, 0, 1 - info[1] if flip else info[1])),
-                pl.BlockSpec(combine.shape, lambda e, info: (0, 0, 0)),
+            in_specs=[whole] * (2 * count)
+            + [pl.BlockSpec(pick.shape, lambda e, info: (0, 0, 0)), pl.BlockSpec(combine.shape, lambda e, info: (0, 0, 0))]
+            + expert_specs(w_gate, rows),
+            out_specs=[whole] * (2 * count),
+            scratch_shapes=[
+                pltpu.VMEM((here, rows, 2 * half), jnp.bfloat16),
+                pltpu.VMEM((count, here * SLOTS, 2 * half), jnp.bfloat16),
             ],
-            out_specs=pl.BlockSpec((count, local, half), lambda e, info: (0, 0, 0)),
-            scratch_shapes=[pltpu.VMEM((count, here, rows // count, half), jnp.bfloat16)],
         ),
-        out_shape=jax.ShapeDtypeStruct((count, local, half), jnp.bfloat16),
+        out_shape=[jax.ShapeDtypeStruct((local, half), jnp.bfloat16)] * (2 * count),
         compiler_params=pltpu.CompilerParams(vmem_limit_bytes=VMEM_LIMIT),
-        name="expert_down",
-    )(info, hidden, w_down, combine)
+        name="experts",
+    )(info, *mine, *other, pick, combine, w_gate, w_up, w_down, scale)
+    return outs[:count], outs[count:]
 
 
 def body(
@@ -304,20 +356,8 @@
     me, side = lax.axis_index("ctx"), lax.axis_index("exp")
     info = jnp.concatenate([jnp.stack([me, side]).astype(jnp.int32), seg_lengths, span_order])
 
-    high = route_weights.astype(jnp.bfloat16)
-    lower = (route_weights - high.astype(jnp.float32)).astype(jnp.bfloat16)
     base = latent.shape[1]
-    packed = jnp.concatenate(
-        [
-            latent,
-            expert_ids.astype(jnp.bfloat16),
-            high,
-            lower,
-            jnp.zeros((local_rows, WIDE - base - 3 * TOP), jnp.bfloat16),
-        ],
-        axis=1,
-    )
-    found = spread(lax.dynamic_slice_in_dim(packed, side * span, span, 0), count)
+    found = spread(pack(info, latent, expert_ids, route_weights), count)
     mine = jnp.stack(found)
     other = jnp.stack(each(swap, found, count))
 
@@ -343,21 +383,25 @@
     scale = jnp.sum(jnp.where(combine, share[:, :, :, None], 0.0), axis=1)
     scale = scale.transpose(1, 0, 2).reshape(here, count * SLOTS, 1)
     combine = combine.astype(jnp.bfloat16).reshape(count, local_rows, here * SLOTS)
+    pick = combine.transpose(0, 2, 1)
 
     got = spread(normed, count)
-    got_other = jnp.stack(each(swap, got, count))
-    got = jnp.stack(got)
-
-    def pick(rows):
-        picked = jnp.einsum("cts,ctd->csd", combine, rows, preferred_element_type=jnp.float32)
-        return picked.astype(jnp.bfloat16).reshape(count, here, SLOTS, rows.shape[2])
-
-    hidden = up(info, pick(got), pick(got_other), w_gate, w_up, scale)
-    away = down(info, hidden, w_down, combine, True)
-    away = swap(away)
-    kept = down(info, hidden, w_down, combine, False)
-    sums = (kept.astype(jnp.float32) + away.astype(jnp.float32)).astype(jnp.bfloat16)
-    mixture = collect([sums[c] for c in range(count)], count)
+    got_other = each(swap, got, count)
+    w_gate, w_up = w_gate.transpose(0, 2, 1), w_up.transpose(0, 2, 1)
+    if count <= FEW:
+        kept, away = experts_fused(info, got, got_other, pick, combine, w_gate, w_up, w_down, scale)
+    else:
+        near, far = jnp.stack(got), jnp.stack(got_other)
+        full = jnp.concatenate([jnp.where(side == 0, near, far), jnp.where(side == 0, far, near)], axis=2)
+        picked = jnp.einsum("cst,ctd->csd", pick, full, preferred_element_type=jnp.float32).astype(jnp.bfloat16)
+        picked = picked.reshape(count, here, SLOTS, width).transpose(1, 0, 2, 3).reshape(here, count * SLOTS, width)
+        result = experts_plain(info, picked, w_gate, w_up, w_down, scale)
+        result = result.reshape(here, count, SLOTS, width).transpose(1, 0, 2, 3).reshape(count, here * SLOTS, width)
+        total = jnp.einsum("cts,csd->ctd", combine, result, preferred_element_type=jnp.float32).astype(jnp.bfloat16)
+        left, right = jnp.split(total, 2, axis=2)
+        kept, away = jnp.where(side == 0, left, right), jnp.where(side == 0, right, left)
+    away = each(swap, away, count)
+    mixture = collect(kept, away, count)
     return (middle.astype(jnp.float32) + mixture).astype(jnp.bfloat16)
 
 

time: 250 us -> 176 us (0.70)
  local copies, waits for them, and re-layouts: 70.5 us -> 9.28 us
  starting transfers between devices: 30.6 us -> 22.5 us
  Pallas kernels: 55.3 us -> 47.6 us
  other arithmetic: 7.48 us -> 15 us
  matrix products: 4.35 us -> 0.14 us
    unnamed x44 -> x43, local copies, waits for them, and re-layouts: 65.9 us -> 4.44 us
    pallas_call x3 -> x2, Pallas kernels: 44.3 us -> 36.6 us  [the longest x1 34.2 us: experts_fused(): pl.pallas_call(functools.partial(fused_kernel, count), grid_spec=pltpu.Pr...]
    ppermute x9, starting transfers between devices: 12.8 us -> 5.58 us  [shift_slow(): return lax.ppermute(value, 'ctx', perm)]
    ppermute x9, waiting for transfers between devices: 41.1 us -> 48.1 us  [shift_slow(): return lax.ppermute(value, 'ctx', perm)]
    ppermute x12, waiting for transfers between devices: 34.6 us -> 29.4 us  [shift_fast(): return lax.ppermute(value, 'ctx', perm)]
    dot_general x2 -> x0, matrix products: 4.21 us -> none  [pick(): jnp.einsum('cts,ctd->csd', combine, rows, preferred_element_type=jnp.floa...]
    convert_element_type x1 -> x3, other arithmetic: 0.3 us -> 3.21 us  [collect(): sums[s].astype(jnp.bfloat16)]
  transfers between devices with their start and end apart: 39 -> 46, of which waited for: 15 -> 18; matrix products, arithmetic and copies ran while one was open for 29% -> 10% of each run, Pallas kernels for 5% -> 0%
where the time goes in v2:
time: 176 us; the launch traced here: 175 us
  waiting for transfers between devices  79.7 us (45%)
  Pallas kernels  47.6 us (27%)
  starting transfers between devices  22.5 us (13%)
  other arithmetic  15 us (9%)
  local copies, waits for them, and re-layouts  9.28 us (5%)
    ppermute x9, waiting for transfers between devices, shift_slow(): return lax.ppermute(value, 'ctx', perm)  48.1 us
    pallas_call x1, Pallas kernels, experts_fused(): pl.pallas_call(functools.partial(fused_kernel, count), grid_spec=pltpu.Pr...  34.2 us
    ppermute x12, waiting for transfers between devices, shift_fast(): return lax.ppermute(value, 'ctx', perm)  29.4 us
    ppermute x12, starting transfers between devices, shift_fast(): return lax.ppermute(value, 'ctx', perm)  12.5 us
    pallas_call x1, Pallas kernels, attend(): pl.pallas_call(functools.partial(attend_kernel, count, blocks), grid_spec...  7.86 us
    ppermute x9, starting transfers between devices, shift_slow(): return lax.ppermute(value, 'ctx', perm)  5.58 us
    unnamed x43, local copies, waits for them, and re-layouts  4.44 us
    ppermute x25, starting transfers between devices, swap(): return lax.ppermute(value, 'exp', SWAP)  4.33 us
  transfers between devices with their start and end apart: 46, of which 18 were waited for; matrix products, arithmetic and copies ran while one was open for 10% of the time, Pallas kernels for 0%

profile of v2, /device:TPU:0, one launch (start us, length us, event | category | flops | bytes accessed | tf_op | source)
XLA Modules:
  0.0 174.8 jit_solution(2596821609604058635)
XLA Ops:
  0.0 0.7 convert_bitcast_fusion
  0.7 0.7 bitcast_reduce-precision_fusion
  1.5 1.2 pad_add_fusion.info
  2.7 0.7 maximum_maximum_fusion.facts_ref
  3.4 2.4 %pack.1 = bf16[64,640]{1,0:T(8,128)(2,1)} custom-call(s32[34]{0:T(128)} %pad_add_fusion.info, bf16[576,128]{1,0:T(8,128)(2,1)} %bitcast.63, f32[64,128]{1,0:T(8,128)} %maximum_maximum_fusion.facts_ref), custom_call_target="tpu_custom_call" | custom-call | tf_op jit(solution)/shard_map/pack/pallas_call | solution.py:226
  6.2 2.5 %collective-permute-start.3 = (bf16[64,640]{1,0:T(8,128)(2,1)}, bf16[64,640]{1,0:T(8,128)(2,1)S(1)}, u32[]{:S(2)}, u32[]{:S(2)}) collective-permute-start(bf16[64,640]{1,0:T(8,128)(2,1)} %pack.1), channel_id=1, source_target_pairs={{0,2},{2,0},{4,6},{6,4},{8,10},{10,8},{12,14},{14,12},{1,3},{3,1},... | collective-permute-start | bytes 245768 | tf_op jit(solution)/shard_map/ppermute | solution.py:38
  8.7 1.6 collective-permute-start
  10.3 0.9 bitcast_dynamic-update-slice_fusion.15
  11.2 1.1 copy.31
  12.3 0.9 copy.32
  13.2 2.2 %collective-permute-done = bf16[64,640]{1,0:T(8,128)(2,1)S(1)} collective-permute-done((bf16[64,640]{1,0:T(8,128)(2,1)}, bf16[64,640]{1,0:T(8,128)(2,1)S(1)}, u32[]{:S(2)}, u32[]{:S(2)}) %collective-permute-start) | collective-permute-done | bytes 81952 | tf_op jit(solution)/shard_map/ppermute | solution.py:32
  16.2 6.1 %collective-permute-done.1 = bf16[64,640]{1,0:T(8,128)(2,1)S(1)} collective-permute-done((bf16[64,640]{1,0:T(8,128)(2,1)S(1)}, bf16[64,640]{1,0:T(8,128)(2,1)S(1)}, u32[]{:S(2)}, u32[]{:S(2)}) %collective-permute-start.1) | collective-permute-done | bytes 81952 | tf_op jit(solution)/shard_map/ppermute | solution.py:32
  22.3 1.5 collective-permute-start.5
  24.2 2.9 %collective-permute-done.5 = bf16[64,640]{1,0:T(8,128)(2,1)S(1)} collective-permute-done((bf16[64,640]{1,0:T(8,128)(2,1)S(1)}, bf16[64,640]{1,0:T(8,128)(2,1)S(1)}, u32[]{:S(2)}, u32[]{:S(2)}) %collective-permute-start.5) | collective-permute-done | bytes 81952 | tf_op jit(solution)/shard_map/ppermute | solution.py:38
  27.1 3.1 %collective-permute-done.2 = bf16[64,640]{1,0:T(8,128)(2,1)S(1)} collective-permute-done((bf16[64,640]{1,0:T(8,128)(2,1)S(1)}, bf16[64,640]{1,0:T(8,128)(2,1)S(1)}, u32[]{:S(2)}, u32[]{:S(2)}) %collective-permute-start.2) | collective-permute-done | bytes 81952 | tf_op jit(solution)/shard_map/ppermute | solution.py:32
  30.9 4.3 %collective-permute-done.6 = bf16[64,640]{1,0:T(8,128)(2,1)S(1)} collective-permute-done((bf16[64,640]{1,0:T(8,128)(2,1)S(1)}, bf16[64,640]{1,0:T(8,128)(2,1)S(1)}, u32[]{:S(2)}, u32[]{:S(2)}) %collective-permute-start.6) | collective-permute-done | bytes 81952 | tf_op jit(solution)/shard_map/ppermute | solution.py:38
  35.4 1.1 collective-permute-done.14
  36.6 0.8 copy-done
  37.4 7.9 %attend.1.here_ref = bf16[128,2048]{1,0:T(8,128)(2,1)} custom-call(s32[34]{0:T(128)} %pad_add_fusion.info, bf16[4,128,192]{2,1,0:T(8,128)(2,1)} %bitcast.61, bf16[8,64,640]{2,1,0:T(8,128)(2,1)} %copy-done.1, bf16[8,64,640]{2,1,0:T(8,128)(2,1)} %copy-done, bf16[512,1024]{1,0:T(8,128)(2,1)} %up_ref.1, bf16[512,2048]{1,0:T(8,128)(2,1)} %proj_ref.1), custom_call_target="tpu_custom_call" | custom-call | tf_op jit(solution)/shard_map/attend/pallas_call | solution.py:157
  45.4 1.3 reshape.26.gain_ref
  47.4 0.8 copy-done.2
  48.2 3.2 %norm.1 = (bf16[128,1024]{1,0:T(8,128)(2,1)}, bf16[128,1024]{1,0:T(8,128)(2,1)}) custom-call(s32[34]{0:T(128)} %pad_add_fusion.info, bf16[128,2048]{1,0:T(8,128)(2,1)} %residual_ref.1, bf16[128,2048]{1,0:T(8,128)(2,1)} %attend.1.here_ref, bf16[128,2048]{1,0:T(8,128)(2,1)} %copy-done.2, bf16[1,2048]{1,0:T(2,128)(2,1)} %reshape.26.gain_ref), custom_call_target="tpu_custom_call" | custom-call | tf_op jit(solution)/shard_map/norm/pallas_call | solution.py:199
  51.5 1.1 broadcast_select_fusion.1
  52.9 8.9 %collective-permute-done.16.refs_1_ = bf16[128,1024]{1,0:T(8,128)(2,1)S(1)} collective-permute-done((bf16[128,1024]{1,0:T(8,128)(2,1)}, bf16[128,1024]{1,0:T(8,128)(2,1)S(1)}, u32[]{:S(2)}, u32[]{:S(2)}) %collective-permute-start.16) | collective-permute-done | bytes 262176 | tf_op jit(solution)/shard_map/ppermute | solution.py:32
  62.5 8.6 %collective-permute-done.17.refs_2_ = bf16[128,1024]{1,0:T(8,128)(2,1)S(1)} collective-permute-done((bf16[128,1024]{1,0:T(8,128)(2,1)S(1)}, bf16[128,1024]{1,0:T(8,128)(2,1)S(1)}, u32[]{:S(2)}, u32[]{:S(2)}) %collective-permute-start.17) | collective-permute-done | bytes 262176 | tf_op jit(solution)/shard_map/ppermute | solution.py:32
  72.1 1.5 collective-permute-start.21
  73.6 5.9 %collective-permute-done.18.refs_3_ = bf16[128,1024]{1,0:T(8,128)(2,1)S(1)} collective-permute-done((bf16[128,1024]{1,0:T(8,128)(2,1)S(1)}, bf16[128,1024]{1,0:T(8,128)(2,1)S(1)}, u32[]{:S(2)}, u32[]{:S(2)}) %collective-permute-start.18) | collective-permute-done | bytes 262176 | tf_op jit(solution)/shard_map/ppermute | solution.py:32
  81.1 5.0 %collective-permute-done.21.refs_6_ = bf16[128,1024]{1,0:T(8,128)(2,1)S(1)} collective-permute-done((bf16[128,1024]{1,0:T(8,128)(2,1)S(1)}, bf16[128,1024]{1,0:T(8,128)(2,1)S(1)}, u32[]{:S(2)}, u32[]{:S(2)}) %collective-permute-start.21) | collective-permute-done | bytes 262176 | tf_op jit(solution)/shard_map/ppermute | solution.py:38
  86.1 5.3 %collective-permute-done.22.refs_7_ = bf16[128,1024]{1,0:T(8,128)(2,1)} collective-permute-done((bf16[128,1024]{1,0:T(8,128)(2,1)S(1)}, bf16[128,1024]{1,0:T(8,128)(2,1)}, u32[]{:S(2)}, u32[]{:S(2)}) %collective-permute-start.22) | collective-permute-done | bytes 262176 | tf_op jit(solution)/shard_map/ppermute | solution.py:38
  91.7 1.1 reshape.29.refs_21_
  92.8 0.9 copy.39.refs_16_
  93.7 0.8 compare_convert_fusion.refs_17_
  95.1 34.2 %experts.1 = (bf16[128,1024]{1,0:T(8,128)(2,1)}, bf16[128,1024]{1,0:T(8,128)(2,1)}, bf16[128,1024]{1,0:T(8,128)(2,1)}, bf16[128,1024]{1,0:T(8,128)(2,1)}, bf16[1...) custom-call(s32[34]{0:T(128)} %pad_add_fusion.info, ...), custom_call_target="tpu_custom_call" | custom-call | tf_op jit(solution)/shard_map/experts/pallas_call | solution.py:315
  131.7 1.0 add_convert_fusion.7
  132.9 1.0 add_convert_fusion.6
  134.5 1.0 add_convert_fusion.4
  135.6 1.6 collective-permute-start.40
  137.2 1.0 add_convert_fusion.2
  138.3 4.9 %collective-permute-done.36 = bf16[128,1024]{1,0:T(8,128)(2,1)S(1)} collective-permute-done((bf16[128,1024]{1,0:T(8,128)(2,1)S(1)}, bf16[128,1024]{1,0:T(8,128)(2,1)S(1)}, u32[]{:S(2)}, u32[]{:S(2)}) %collective-permute-start.36) | collective-permute-done | bytes 262176 | tf_op jit(solution)/shard_map/ppermute | solution.py:38
  143.7 1.1 add_convert_fusion.5
  144.8 1.6 collective-permute-start.33
  146.4 2.4 %collective-permute-done.40 = bf16[128,1024]{1,0:T(8,128)(2,1)S(1)} collective-permute-done((bf16[128,1024]{1,0:T(8,128)(2,1)S(1)}, bf16[128,1024]{1,0:T(8,128)(2,1)S(1)}, u32[]{:S(2)}, u32[]{:S(2)}) %collective-permute-start.40) | collective-permute-done | bytes 262176 | tf_op jit(solution)/shard_map/ppermute | solution.py:38
  148.8 3.8 %collective-permute-start.37 = (bf16[128,1024]{1,0:T(8,128)(2,1)S(1)}, bf16[128,1024]{1,0:T(8,128)(2,1)S(1)}, u32[]{:S(2)}, u32[]{:S(2)}) collective-permute-start(bf16[128,1024]{1,0:T(8,128)(2,1)S(1)} %add_convert_fusion.5), channel_id=1, source_target_pairs={{0,12},{2,14},{4,0},{6,2},{8,4},{10,6},{12,8},{14,10},{1,13},{3,15... | collective-permute-start | bytes 786440 | tf_op jit(solution)/shard_map/ppermute | solution.py:32
  152.6 1.1 add_convert_fusion.3
  154.4 1.1 add_convert_fusion.1
  155.6 3.9 %collective-permute-done.33 = bf16[128,1024]{1,0:T(8,128)(2,1)S(1)} collective-permute-done((bf16[128,1024]{1,0:T(8,128)(2,1)S(1)}, bf16[128,1024]{1,0:T(8,128)(2,1)S(1)}, u32[]{:S(2)}, u32[]{:S(2)}) %collective-permute-start.33) | collective-permute-done | bytes 262176 | tf_op jit(solution)/shard_map/ppermute | solution.py:38
  159.5 13.3 %collective-permute-done.41 = bf16[128,1024]{1,0:T(8,128)(2,1)S(1)} collective-permute-done((bf16[128,1024]{1,0:T(8,128)(2,1)S(1)}, bf16[128,1024]{1,0:T(8,128)(2,1)S(1)}, u32[]{:S(2)}, u32[]{:S(2)}) %collective-permute-start.41) | collective-permute-done | bytes 262176 | tf_op jit(solution)/shard_map/ppermute | solution.py:32
  172.8 2.0 %add_convert_fusion = bf16[128,1024]{1,0:T(8,128)(2,1)} fusion(bf16[128,1024]{1,0:T(8,128)(2,1)S(1)} %collective-permute-done.45, bf16[128,1024]{1,0:T(8,128)(2,1)S(1)} %collective-permute-done.41, bf16[128,1024]{1,0:T(8,128)(2,1)S(1)} %collective-permute-done.37, bf16[128,1024]{1,0:T(8,128)(2,1)S(1)} %collective-permute-done.33, ...), kind=kLoop, calls=%fused_computation.2 | loop fusion | flops 1835008 | bytes 2097152 | tf_op jit(solution)/shard_map/convert_element_type | solution.py:405
  (131 shorter events, 12.4 us)
Async XLA Ops:
  5.7 10.4 %collective-permute-start.7 = (bf16[64,640]{1,0:T(8,128)(2,1)}, bf16[64,640]{1,0:T(8,128)(2,1)S(1)}, u32[]{:S(2)}, u32[]{:S(2)}) collective-permute-start(bf16[64,640]{1,0:T(8,128)(2,1)} %pack.1), channel_id=1, source_target_pairs={{0,1},{1,0},{2,3},{3,2},{4,5},{5,4},{6,7},{7,6},{8,9},{9,8},{10,11... | collective-permute-start | bytes 245768 | tf_op jit(solution)/shard_map/ppermute | solution.py:42
  6.2 9.7 %collective-permute-start.3 = (bf16[64,640]{1,0:T(8,128)(2,1)}, bf16[64,640]{1,0:T(8,128)(2,1)S(1)}, u32[]{:S(2)}, u32[]{:S(2)}) collective-permute-start(bf16[64,640]{1,0:T(8,128)(2,1)} %pack.1), channel_id=1, source_target_pairs={{0,2},{2,0},{4,6},{6,4},{8,10},{10,8},{12,14},{14,12},{1,3},{3,1},... | collective-permute-start | bytes 245768 | tf_op jit(solution)/shard_map/ppermute | solution.py:38
  8.7 6.7 %collective-permute-start = (bf16[64,640]{1,0:T(8,128)(2,1)}, bf16[64,640]{1,0:T(8,128)(2,1)S(1)}, u32[]{:S(2)}, u32[]{:S(2)}) collective-permute-start(bf16[64,640]{1,0:T(8,128)(2,1)} %pack.1), channel_id=1, source_target_pairs={{0,4},{2,6},{4,8},{6,10},{8,12},{10,14},{12,0},{14,2},{1,5},{3,7},... | collective-permute-start | bytes 245768 | tf_op jit(solution)/shard_map/ppermute | solution.py:32
  15.4 8.4 %collective-permute-start.8 = (bf16[64,640]{1,0:T(8,128)(2,1)S(1)}, bf16[64,640]{1,0:T(8,128)(2,1)S(1)}, u32[]{:S(2)}, u32[]{:S(2)}) collective-permute-start(bf16[64,640]{1,0:T(8,128)(2,1)S(1)} %collective-permute-done), channel_id=1, source_target_pairs={{0,1},{1,0},{2,3},{3,2},{4,5},{5,4},{6,7},{7,6},{8,9},{9,8},{10,11... | collective-permute-start | bytes 245768 | tf_op jit(solution)/shard_map/ppermute | solution.py:42
  15.4 8.5 %collective-permute-start.4 = (bf16[64,640]{1,0:T(8,128)(2,1)S(1)}, bf16[64,640]{1,0:T(8,128)(2,1)S(1)}, u32[]{:S(2)}, u32[]{:S(2)}) collective-permute-start(bf16[64,640]{1,0:T(8,128)(2,1)S(1)} %collective-permute-done), channel_id=1, source_target_pairs={{0,2},{2,0},{4,6},{6,4},{8,10},{10,8},{12,14},{14,12},{1,3},{3,1},... | collective-permute-start | bytes 245768 | tf_op jit(solution)/shard_map/ppermute | solution.py:38
  15.9 6.4 %collective-permute-start.1 = (bf16[64,640]{1,0:T(8,128)(2,1)S(1)}, bf16[64,640]{1,0:T(8,128)(2,1)S(1)}, u32[]{:S(2)}, u32[]{:S(2)}) collective-permute-start(bf16[64,640]{1,0:T(8,128)(2,1)S(1)} %collective-permute-done), channel_id=1, source_target_pairs={{0,4},{2,6},{4,8},{6,10},{8,12},{10,14},{12,0},{14,2},{1,5},{3,7},... | collective-permute-start | bytes 245768 | tf_op jit(solution)/shard_map/ppermute | solution.py:32
  15.9 19.4 %collective-permute-start.11 = (bf16[64,640]{1,0:T(8,128)(2,1)S(1)}, bf16[64,640]{1,0:T(8,128)(2,1)S(1)}, u32[]{:S(2)}, u32[]{:S(2)}) collective-permute-start(bf16[64,640]{1,0:T(8,128)(2,1)S(1)} %collective-permute-done.3), channel_id=1, source_target_pairs={{0,1},{1,0},{2,3},{3,2},{4,5},{5,4},{6,7},{7,6},{8,9},{9,8},{10,11... | collective-permute-start | bytes 245768 | tf_op jit(solution)/shard_map/ppermute | solution.py:42
  22.3 8.1 %collective-permute-start.9 = (bf16[64,640]{1,0:T(8,128)(2,1)S(1)}, bf16[64,640]{1,0:T(8,128)(2,1)S(1)}, u32[]{:S(2)}, u32[]{:S(2)}) collective-permute-start(bf16[64,640]{1,0:T(8,128)(2,1)S(1)} %collective-permute-done.1), channel_id=1, source_target_pairs={{0,1},{1,0},{2,3},{3,2},{4,5},{5,4},{6,7},{7,6},{8,9},{9,8},{10,11... | collective-permute-start | bytes 245768 | tf_op jit(solution)/shard_map/ppermute | solution.py:42
  22.3 4.9 %collective-permute-start.5 = (bf16[64,640]{1,0:T(8,128)(2,1)S(1)}, bf16[64,640]{1,0:T(8,128)(2,1)S(1)}, u32[]{:S(2)}, u32[]{:S(2)}) collective-permute-start(bf16[64,640]{1,0:T(8,128)(2,1)S(1)} %collective-permute-done.1), channel_id=1, source_target_pairs={{0,2},{2,0},{4,6},{6,4},{8,10},{10,8},{12,14},{14,12},{1,3},{3,1},... | collective-permute-start | bytes 245768 | tf_op jit(solution)/shard_map/ppermute | solution.py:38
  23.8 6.4 %collective-permute-start.2 = (bf16[64,640]{1,0:T(8,128)(2,1)S(1)}, bf16[64,640]{1,0:T(8,128)(2,1)S(1)}, u32[]{:S(2)}, u32[]{:S(2)}) collective-permute-start(bf16[64,640]{1,0:T(8,128)(2,1)S(1)} %collective-permute-done.1), channel_id=1, source_target_pairs={{0,4},{2,6},{4,8},{6,10},{8,12},{10,14},{12,0},{14,2},{1,5},{3,7},... | collective-permute-start | bytes 245768 | tf_op jit(solution)/shard_map/ppermute | solution.py:32
  23.9 11.5 %collective-permute-start.12 = (bf16[64,640]{1,0:T(8,128)(2,1)S(1)}, bf16[64,640]{1,0:T(8,128)(2,1)S(1)}, u32[]{:S(2)}, u32[]{:S(2)}) collective-permute-start(bf16[64,640]{1,0:T(8,128)(2,1)S(1)} %collective-permute-done.4), channel_id=1, source_target_pairs={{0,1},{1,0},{2,3},{3,2},{4,5},{5,4},{6,7},{7,6},{8,9},{9,8},{10,11... | collective-permute-start | bytes 245768 | tf_op jit(solution)/shard_map/ppermute | solution.py:42
  27.1 8.3 %collective-permute-start.13 = (bf16[64,640]{1,0:T(8,128)(2,1)S(1)}, bf16[64,640]{1,0:T(8,128)(2,1)S(1)}, u32[]{:S(2)}, u32[]{:S(2)}) collective-permute-start(bf16[64,640]{1,0:T(8,128)(2,1)S(1)} %collective-permute-done.5), channel_id=1, source_target_pairs={{0,1},{1,0},{2,3},{3,2},{4,5},{5,4},{6,7},{7,6},{8,9},{9,8},{10,11... | collective-permute-start | bytes 245768 | tf_op jit(solution)/shard_map/ppermute | solution.py:42
  30.3 5.0 %collective-permute-start.10 = (bf16[64,640]{1,0:T(8,128)(2,1)S(1)}, bf16[64,640]{1,0:T(8,128)(2,1)S(1)}, u32[]{:S(2)}, u32[]{:S(2)}) collective-permute-start(bf16[64,640]{1,0:T(8,128)(2,1)S(1)} %collective-permute-done.2), channel_id=1, source_target_pairs={{0,1},{1,0},{2,3},{3,2},{4,5},{5,4},{6,7},{7,6},{8,9},{9,8},{10,11... | collective-permute-start | bytes 245768 | tf_op jit(solution)/shard_map/ppermute | solution.py:42
  30.3 4.9 %collective-permute-start.6 = (bf16[64,640]{1,0:T(8,128)(2,1)S(1)}, bf16[64,640]{1,0:T(8,128)(2,1)S(1)}, u32[]{:S(2)}, u32[]{:S(2)}) collective-permute-start(bf16[64,640]{1,0:T(8,128)(2,1)S(1)} %collective-permute-done.2), channel_id=1, source_target_pairs={{0,2},{2,0},{4,6},{6,4},{8,10},{10,8},{12,14},{14,12},{1,3},{3,1},... | collective-permute-start | bytes 245768 | tf_op jit(solution)/shard_map/ppermute | solution.py:38
  35.3 1.3 collective-permute-start.14
  45.3 2.1 %collective-permute-start.15 = (bf16[128,2048]{1,0:T(8,128)(2,1)}, bf16[128,2048]{1,0:T(8,128)(2,1)S(1)}, u32[]{:S(2)}, u32[]{:S(2)}) collective-permute-start(bf16[128,2048]{1,0:T(8,128)(2,1)} %attend.1.here_ref), channel_id=1, source_target_pairs={{0,1},{1,0},{2,3},{3,2},{4,5},{5,4},{6,7},{7,6},{8,9},{9,8},{10,11... | collective-permute-start | bytes 1572872 | tf_op jit(solution)/shard_map/ppermute | solution.py:42
  51.4 10.4 %collective-permute-start.16 = (bf16[128,1024]{1,0:T(8,128)(2,1)}, bf16[128,1024]{1,0:T(8,128)(2,1)S(1)}, u32[]{:S(2)}, u32[]{:S(2)}) collective-permute-start(bf16[128,1024]{1,0:T(8,128)(2,1)} %get-tuple-element.24.refs_0_), channel_id=1, source_target_pairs={{0,4},{2,6},{4,8},{6,10},{8,12},{10,14},{12,0},{14,2},{1,5},{3,7},... | collective-permute-start | bytes 786440 | tf_op jit(solution)/shard_map/ppermute | solution.py:32
  61.7 32.8 %copy-start.3 = (bf16[128,1024]{1,0:T(8,128)(2,1)}, bf16[128,1024]{1,0:T(8,128)(2,1)S(1)}, u32[]{:S(2)}) copy-start(bf16[128,1024]{1,0:T(8,128)(2,1)S(1)} %collective-permute-done.16.refs_1_) | copy-start | bytes 786436
  61.7 9.3 %collective-permute-start.17 = (bf16[128,1024]{1,0:T(8,128)(2,1)S(1)}, bf16[128,1024]{1,0:T(8,128)(2,1)S(1)}, u32[]{:S(2)}, u32[]{:S(2)}) collective-permute-start(bf16[128,1024]{1,0:T(8,128)(2,1)S(1)} %collective-permute-done.16.refs_1_), channel_id=1, source_target_pairs={{0,4},{2,6},{4,8},{6,10},{8,12},{10,14},{12,0},{14,2},{1,5},{3,7},... | collective-permute-start | bytes 786440 | tf_op jit(solution)/shard_map/ppermute | solution.py:32
  61.9 10.2 %collective-permute-start.23 = (bf16[128,1024]{1,0:T(8,128)(2,1)}, bf16[128,1024]{1,0:T(8,128)(2,1)S(1)}, u32[]{:S(2)}, u32[]{:S(2)}) collective-permute-start(bf16[128,1024]{1,0:T(8,128)(2,1)} %get-tuple-element.24.refs_0_), channel_id=1, source_target_pairs={{0,1},{1,0},{2,3},{3,2},{4,5},{5,4},{6,7},{7,6},{8,9},{9,8},{10,11... | collective-permute-start | bytes 786440 | tf_op jit(solution)/shard_map/ppermute | solution.py:42
  61.9 10.0 %collective-permute-start.19 = (bf16[128,1024]{1,0:T(8,128)(2,1)}, bf16[128,1024]{1,0:T(8,128)(2,1)S(1)}, u32[]{:S(2)}, u32[]{:S(2)}) collective-permute-start(bf16[128,1024]{1,0:T(8,128)(2,1)} %get-tuple-element.24.refs_0_), channel_id=1, source_target_pairs={{0,2},{2,0},{4,6},{6,4},{8,10},{10,8},{12,14},{14,12},{1,3},{3,1},... | collective-permute-start | bytes 786440 | tf_op jit(solution)/shard_map/ppermute | solution.py:38
  71.1 8.4 %collective-permute-start.18 = (bf16[128,1024]{1,0:T(8,128)(2,1)S(1)}, bf16[128,1024]{1,0:T(8,128)(2,1)S(1)}, u32[]{:S(2)}, u32[]{:S(2)}) collective-permute-start(bf16[128,1024]{1,0:T(8,128)(2,1)S(1)} %collective-permute-done.17.refs_2_), channel_id=1, source_target_pairs={{0,4},{2,6},{4,8},{6,10},{8,12},{10,14},{12,0},{14,2},{1,5},{3,7},... | collective-permute-start | bytes 786440 | tf_op jit(solution)/shard_map/ppermute | solution.py:32
  71.3 9.7 %collective-permute-start.24 = (bf16[128,1024]{1,0:T(8,128)(2,1)S(1)}, bf16[128,1024]{1,0:T(8,128)(2,1)S(1)}, u32[]{:S(2)}, u32[]{:S(2)}) collective-permute-start(bf16[128,1024]{1,0:T(8,128)(2,1)S(1)} %collective-permute-done.16.refs_1_), channel_id=1, source_target_pairs={{0,1},{1,0},{2,3},{3,2},{4,5},{5,4},{6,7},{7,6},{8,9},{9,8},{10,11... | collective-permute-start | bytes 786440 | tf_op jit(solution)/shard_map/ppermute | solution.py:42
  71.3 9.2 %collective-permute-start.20 = (bf16[128,1024]{1,0:T(8,128)(2,1)S(1)}, bf16[128,1024]{1,0:T(8,128)(2,1)S(1)}, u32[]{:S(2)}, u32[]{:S(2)}) collective-permute-start(bf16[128,1024]{1,0:T(8,128)(2,1)S(1)} %collective-permute-done.16.refs_1_), channel_id=1, source_target_pairs={{0,2},{2,0},{4,6},{6,4},{8,10},{10,8},{12,14},{14,12},{1,3},{3,1},... | collective-permute-start | bytes 786440 | tf_op jit(solution)/shard_map/ppermute | solution.py:38
  71.9 8.5 %collective-permute-start.27 = (bf16[128,1024]{1,0:T(8,128)(2,1)S(1)}, bf16[128,1024]{1,0:T(8,128)(2,1)S(1)}, u32[]{:S(2)}, u32[]{:S(2)}) collective-permute-start(bf16[128,1024]{1,0:T(8,128)(2,1)S(1)} %collective-permute-done.19.refs_4_), channel_id=1, source_target_pairs={{0,1},{1,0},{2,3},{3,2},{4,5},{5,4},{6,7},{7,6},{8,9},{9,8},{10,11... | collective-permute-start | bytes 786440 | tf_op jit(solution)/shard_map/ppermute | solution.py:42
  72.1 14.0 %collective-permute-start.21 = (bf16[128,1024]{1,0:T(8,128)(2,1)S(1)}, bf16[128,1024]{1,0:T(8,128)(2,1)S(1)}, u32[]{:S(2)}, u32[]{:S(2)}) collective-permute-start(bf16[128,1024]{1,0:T(8,128)(2,1)S(1)} %collective-permute-done.17.refs_2_), channel_id=1, source_target_pairs={{0,2},{2,0},{4,6},{6,4},{8,10},{10,8},{12,14},{14,12},{1,3},{3,1},... | collective-permute-start | bytes 786440 | tf_op jit(solution)/shard_map/ppermute | solution.py:38
  79.5 11.9 %collective-permute-start.22 = (bf16[128,1024]{1,0:T(8,128)(2,1)S(1)}, bf16[128,1024]{1,0:T(8,128)(2,1)}, u32[]{:S(2)}, u32[]{:S(2)}) collective-permute-start(bf16[128,1024]{1,0:T(8,128)(2,1)S(1)} %collective-permute-done.18.refs_3_), channel_id=1, source_target_pairs={{0,2},{2,0},{4,6},{6,4},{8,10},{10,8},{12,14},{14,12},{1,3},{3,1},... | collective-permute-start | bytes 786440 | tf_op jit(solution)/shard_map/ppermute | solution.py:38
  80.4 14.0 %collective-permute-start.25 = (bf16[128,1024]{1,0:T(8,128)(2,1)S(1)}, bf16[128,1024]{1,0:T(8,128)(2,1)S(1)}, u32[]{:S(2)}, u32[]{:S(2)}) collective-permute-start(bf16[128,1024]{1,0:T(8,128)(2,1)S(1)} %collective-permute-done.17.refs_2_), channel_id=1, source_target_pairs={{0,1},{1,0},{2,3},{3,2},{4,5},{5,4},{6,7},{7,6},{8,9},{9,8},{10,11... | collective-permute-start | bytes 786440 | tf_op jit(solution)/shard_map/ppermute | solution.py:42
  80.5 13.9 %collective-permute-start.28 = (bf16[128,1024]{1,0:T(8,128)(2,1)S(1)}, bf16[128,1024]{1,0:T(8,128)(2,1)}, u32[]{:S(2)}, u32[]{:S(2)}) collective-permute-start(bf16[128,1024]{1,0:T(8,128)(2,1)S(1)} %collective-permute-done.20.refs_5_), channel_id=1, source_target_pairs={{0,1},{1,0},{2,3},{3,2},{4,5},{5,4},{6,7},{7,6},{8,9},{9,8},{10,11... | collective-permute-start | bytes 786440 | tf_op jit(solution)/shard_map/ppermute | solution.py:42
  81.0 13.4 %collective-permute-start.26 = (bf16[128,1024]{1,0:T(8,128)(2,1)S(1)}, bf16[128,1024]{1,0:T(8,128)(2,1)}, u32[]{:S(2)}, u32[]{:S(2)}) collective-permute-start(bf16[128,1024]{1,0:T(8,128)(2,1)S(1)} %collective-permute-done.18.refs_3_), channel_id=1, source_target_pairs={{0,1},{1,0},{2,3},{3,2},{4,5},{5,4},{6,7},{7,6},{8,9},{9,8},{10,11... | collective-permute-start | bytes 786440 | tf_op jit(solution)/shard_map/ppermute | solution.py:42
  86.1 8.4 %collective-permute-start.29 = (bf16[128,1024]{1,0:T(8,128)(2,1)S(1)}, bf16[128,1024]{1,0:T(8,128)(2,1)}, u32[]{:S(2)}, u32[]{:S(2)}) collective-permute-start(bf16[128,1024]{1,0:T(8,128)(2,1)S(1)} %collective-permute-done.21.refs_6_), channel_id=1, source_target_pairs={{0,1},{1,0},{2,3},{3,2},{4,5},{5,4},{6,7},{7,6},{8,9},{9,8},{10,11... | collective-permute-start | bytes 786440 | tf_op jit(solution)/shard_map/ppermute | solution.py:42
  91.4 3.1 %collective-permute-start.30 = (bf16[128,1024]{1,0:T(8,128)(2,1)}, bf16[128,1024]{1,0:T(8,128)(2,1)}, u32[]{:S(2)}, u32[]{:S(2)}) collective-permute-start(bf16[128,1024]{1,0:T(8,128)(2,1)} %collective-permute-done.22.refs_7_), channel_id=1, source_target_pairs={{0,1},{1,0},{2,3},{3,2},{4,5},{5,4},{6,7},{7,6},{8,9},{9,8},{10,11... | collective-permute-start | bytes 786440 | tf_op jit(solution)/shard_map/ppermute | solution.py:42
  95.1 77.7 %copy-start.13 = (bf16[128,1024]{1,0:T(8,128)(2,1)S(1)}, bf16[128,1024]{1,0:T(8,128)(2,1)}, u32[]{:S(2)}) copy-start(bf16[128,1024]{1,0:T(8,128)(2,1)} %get-tuple-element.23) | copy-start | bytes 786436
  129.4 2.0 %collective-permute-start.32 = (bf16[128,1024]{1,0:T(8,128)(2,1)}, bf16[128,1024]{1,0:T(8,128)(2,1)S(1)}, u32[]{:S(2)}, u32[]{:S(2)}) collective-permute-start(bf16[128,1024]{1,0:T(8,128)(2,1)} %get-tuple-element.28), channel_id=1, source_target_pairs={{0,1},{1,0},{2,3},{3,2},{4,5},{5,4},{6,7},{7,6},{8,9},{9,8},{10,11... | collective-permute-start | bytes 786440 | tf_op jit(solution)/shard_map/ppermute | solution.py:42
  129.9 2.8 %collective-permute-start.35 = (bf16[128,1024]{1,0:T(8,128)(2,1)}, bf16[128,1024]{1,0:T(8,128)(2,1)S(1)}, u32[]{:S(2)}, u32[]{:S(2)}) collective-permute-start(bf16[128,1024]{1,0:T(8,128)(2,1)} %get-tuple-element.32), channel_id=1, source_target_pairs={{0,1},{1,0},{2,3},{3,2},{4,5},{5,4},{6,7},{7,6},{8,9},{9,8},{10,11... | collective-permute-start | bytes 786440 | tf_op jit(solution)/shard_map/ppermute | solution.py:42
  130.0 25.5 %collective-permute-start.31 = (bf16[128,1024]{1,0:T(8,128)(2,1)}, bf16[128,1024]{1,0:T(8,128)(2,1)S(1)}, u32[]{:S(2)}, u32[]{:S(2)}) collective-permute-start(bf16[128,1024]{1,0:T(8,128)(2,1)} %get-tuple-element.26), channel_id=1, source_target_pairs={{0,1},{1,0},{2,3},{3,2},{4,5},{5,4},{6,7},{7,6},{8,9},{9,8},{10,11... | collective-permute-start | bytes 786440 | tf_op jit(solution)/shard_map/ppermute | solution.py:42
  130.5 7.7 %collective-permute-start.34 = (bf16[128,1024]{1,0:T(8,128)(2,1)}, bf16[128,1024]{1,0:T(8,128)(2,1)S(1)}, u32[]{:S(2)}, u32[]{:S(2)}) collective-permute-start(bf16[128,1024]{1,0:T(8,128)(2,1)} %get-tuple-element.30), channel_id=1, source_target_pairs={{0,1},{1,0},{2,3},{3,2},{4,5},{5,4},{6,7},{7,6},{8,9},{9,8},{10,11... | collective-permute-start | bytes 786440 | tf_op jit(solution)/shard_map/ppermute | solution.py:42
  130.5 14.2 %collective-permute-start.38 = (bf16[128,1024]{1,0:T(8,128)(2,1)}, bf16[128,1024]{1,0:T(8,128)(2,1)S(1)}, u32[]{:S(2)}, u32[]{:S(2)}) collective-permute-start(bf16[128,1024]{1,0:T(8,128)(2,1)} %get-tuple-element.34), channel_id=1, source_target_pairs={{0,1},{1,0},{2,3},{3,2},{4,5},{5,4},{6,7},{7,6},{8,9},{9,8},{10,11... | collective-permute-start | bytes 786440 | tf_op jit(solution)/shard_map/ppermute | solution.py:42
  131.3 2.6 %collective-permute-start.39 = (bf16[128,1024]{1,0:T(8,128)(2,1)}, bf16[128,1024]{1,0:T(8,128)(2,1)S(1)}, u32[]{:S(2)}, u32[]{:S(2)}) collective-permute-start(bf16[128,1024]{1,0:T(8,128)(2,1)} %get-tuple-element.36), channel_id=1, source_target_pairs={{0,1},{1,0},{2,3},{3,2},{4,5},{5,4},{6,7},{7,6},{8,9},{9,8},{10,11... | collective-permute-start | bytes 786440 | tf_op jit(solution)/shard_map/ppermute | solution.py:42
  132.7 2.8 %collective-permute-start.43 = (bf16[128,1024]{1,0:T(8,128)(2,1)}, bf16[128,1024]{1,0:T(8,128)(2,1)S(1)}, u32[]{:S(2)}, u32[]{:S(2)}) collective-permute-start(bf16[128,1024]{1,0:T(8,128)(2,1)} %get-tuple-element.40), channel_id=1, source_target_pairs={{0,1},{1,0},{2,3},{3,2},{4,5},{5,4},{6,7},{7,6},{8,9},{9,8},{10,11... | collective-permute-start | bytes 786440 | tf_op jit(solution)/shard_map/ppermute | solution.py:42
  134.0 9.2 %collective-permute-start.36 = (bf16[128,1024]{1,0:T(8,128)(2,1)S(1)}, bf16[128,1024]{1,0:T(8,128)(2,1)S(1)}, u32[]{:S(2)}, u32[]{:S(2)}) collective-permute-start(bf16[128,1024]{1,0:T(8,128)(2,1)S(1)} %add_convert_fusion.6), channel_id=1, source_target_pairs={{0,2},{2,0},{4,6},{6,4},{8,10},{10,8},{12,14},{14,12},{1,3},{3,1},... | collective-permute-start | bytes 786440 | tf_op jit(solution)/shard_map/ppermute | solution.py:38
  135.6 13.2 %collective-permute-start.40 = (bf16[128,1024]{1,0:T(8,128)(2,1)S(1)}, bf16[128,1024]{1,0:T(8,128)(2,1)S(1)}, u32[]{:S(2)}, u32[]{:S(2)}) collective-permute-start(bf16[128,1024]{1,0:T(8,128)(2,1)S(1)} %add_convert_fusion.4), channel_id=1, source_target_pairs={{0,2},{2,0},{4,6},{6,4},{8,10},{10,8},{12,14},{14,12},{1,3},{3,1},... | collective-permute-start | bytes 786440 | tf_op jit(solution)/shard_map/ppermute | solution.py:38
  138.2 15.5 %collective-permute-start.42 = (bf16[128,1024]{1,0:T(8,128)(2,1)}, bf16[128,1024]{1,0:T(8,128)(2,1)S(1)}, u32[]{:S(2)}, u32[]{:S(2)}) collective-permute-start(bf16[128,1024]{1,0:T(8,128)(2,1)} %get-tuple-element.38), channel_id=1, source_target_pairs={{0,1},{1,0},{2,3},{3,2},{4,5},{5,4},{6,7},{7,6},{8,9},{9,8},{10,11... | collective-permute-start | bytes 786440 | tf_op jit(solution)/shard_map/ppermute | solution.py:42
  143.2 11.2 %collective-permute-start.44 = (bf16[128,1024]{1,0:T(8,128)(2,1)S(1)}, bf16[128,1024]{1,0:T(8,128)(2,1)S(1)}, u32[]{:S(2)}, u32[]{:S(2)}) collective-permute-start(bf16[128,1024]{1,0:T(8,128)(2,1)S(1)} %add_convert_fusion.2), channel_id=1, source_target_pairs={{0,2},{2,0},{4,6},{6,4},{8,10},{10,8},{12,14},{14,12},{1,3},{3,1},... | collective-permute-start | bytes 786440 | tf_op jit(solution)/shard_map/ppermute | solution.py:38
  144.8 14.7 %collective-permute-start.33 = (bf16[128,1024]{1,0:T(8,128)(2,1)S(1)}, bf16[128,1024]{1,0:T(8,128)(2,1)S(1)}, u32[]{:S(2)}, u32[]{:S(2)}) collective-permute-start(bf16[128,1024]{1,0:T(8,128)(2,1)S(1)} %add_convert_fusion.7), channel_id=1, source_target_pairs={{0,2},{2,0},{4,6},{6,4},{8,10},{10,8},{12,14},{14,12},{1,3},{3,1},... | collective-permute-start | bytes 786440 | tf_op jit(solution)/shard_map/ppermute | solution.py:38
  148.8 10.7 %collective-permute-start.37 = (bf16[128,1024]{1,0:T(8,128)(2,1)S(1)}, bf16[128,1024]{1,0:T(8,128)(2,1)S(1)}, u32[]{:S(2)}, u32[]{:S(2)}) collective-permute-start(bf16[128,1024]{1,0:T(8,128)(2,1)S(1)} %add_convert_fusion.5), channel_id=1, source_target_pairs={{0,12},{2,14},{4,0},{6,2},{8,4},{10,6},{12,8},{14,10},{1,13},{3,15... | collective-permute-start | bytes 786440 | tf_op jit(solution)/shard_map/ppermute | solution.py:32
  153.7 19.1 %collective-permute-start.41 = (bf16[128,1024]{1,0:T(8,128)(2,1)S(1)}, bf16[128,1024]{1,0:T(8,128)(2,1)S(1)}, u32[]{:S(2)}, u32[]{:S(2)}) collective-permute-start(bf16[128,1024]{1,0:T(8,128)(2,1)S(1)} %add_convert_fusion.3), channel_id=1, source_target_pairs={{0,8},{2,10},{4,12},{6,14},{8,0},{10,2},{12,4},{14,6},{1,9},{3,11}... | collective-permute-start | bytes 786440 | tf_op jit(solution)/shard_map/ppermute | solution.py:32
  155.5 17.3 %collective-permute-start.45 = (bf16[128,1024]{1,0:T(8,128)(2,1)S(1)}, bf16[128,1024]{1,0:T(8,128)(2,1)S(1)}, u32[]{:S(2)}, u32[]{:S(2)}) collective-permute-start(bf16[128,1024]{1,0:T(8,128)(2,1)S(1)} %add_convert_fusion.1), channel_id=1, source_target_pairs={{0,4},{2,6},{4,8},{6,10},{8,12},{10,14},{12,0},{14,2},{1,5},{3,7},... | collective-permute-start | bytes 786440 | tf_op jit(solution)/shard_map/ppermute | solution.py:32
  (12 other events, 137.3 us)

commit v3 on v2

v3 whole, which is shorter than its diff:
```python
import functools
import math

import jax
import jax.numpy as jnp
from jax import lax
from jax.experimental import pallas as pl
from jax.experimental.pallas import tpu as pltpu
from jax.sharding import PartitionSpec as P

NOPE = 128
ROPE = 64
VHEAD = 128
LAT = 512
EXPERTS = 64
TOP = 6
SLOTS = 16
WIDE = 640
VMEM_LIMIT = 56 * 1024 * 1024
SWAP = [(0, 1), (1, 0)]
FEW = 8


def grid_of(count):
    fast = 2 ** (int(math.log2(count)) // 2)
    return (count // fast, fast)


def shift_slow(value, step, count):
    slow, fast = grid_of(count)
    perm = [(i, (i // fast + step) % slow * fast + i % fast) for i in range(count)]
    return lax.ppermute(value, "ctx", perm)


def shift_fast(value, step, count):
    fast = grid_of(count)[1]
    perm = [(i, i // fast * fast + (i % fast + step) % fast) for i in range(count)]
    return lax.ppermute(value, "ctx", perm)


def swap(value):
    return lax.ppermute(value, "exp", SWAP)


def each(send, pieces, count):
    if count <= FEW:
        return [send(piece) for piece in pieces]
    return list(send(jnp.stack(list(pieces))))


def ring(block, count):
    line = [block]
    for _ in range(1, grid_of(count)[0]):
        line.append(shift_slow(line[-1], 1, count))
    return line


def direct(block, count):
    return [block] + [shift_slow(block, s, count) for s in range(1, grid_of(count)[0])]


def across(line, count):
    found = list(line)
    for r in range(1, grid_of(count)[1]):
        found += each(lambda piece: shift_fast(piece, r, count), line, count)
    return found


def summed(pieces):
    total = pieces[0].astype(jnp.float32)
    for piece in pieces[1:]:
        total = total + piece.astype(jnp.float32)
    return total


def collect(near, swapped, combine, count):
    slow, fast = grid_of(count)

    def part(c):
        rows = (near[c].astype(jnp.float32) + swapped[c].astype(jnp.float32)).astype(jnp.bfloat16)
        return jnp.dot(combine[c], rows, preferred_element_type=jnp.float32)

    terms = [[] for _ in range(slow)]
    for r in range(1, fast):
        parts = [part(r * slow + s).astype(jnp.bfloat16) for s in reversed(range(slow))]
        arrived = each(lambda piece: shift_fast(piece, -r, count), parts, count)
        for s, piece in zip(reversed(range(slow)), arrived):
            terms[s].append(piece)
    sums = [summed([part(s)] + terms[s]) for s in range(slow)]
    arrived = [shift_slow(sums[s].astype(jnp.bfloat16), -s, count) for s in range(1, slow)]
    return summed([sums[0]] + arrived)


def owner_of(place, me, count):
    slow, fast = grid_of(count)
    r, s = place // slow, place % slow
    return (me // fast + slow - s) % slow * fast + (me % fast + fast - r) % fast


def attend_kernel(count, blocks, where, lengths, order, q_ref, mine_ref, other_ref, up_ref, proj_ref, out_ref, m_ref, l_ref, acc_ref):
    step = pl.program_id(0)
    me, side = where[0], where[1]
    segs = lengths.shape[0]
    span = mine_ref.shape[1]
    heads, rows, _ = q_ref.shape

    @pl.when(step == 0)
    def _():
        m_ref[...] = jnp.full_like(m_ref, -1e30)
        l_ref[...] = jnp.zeros_like(l_ref)
        acc_ref[...] = jnp.zeros_like(acc_ref)

    row = lax.broadcasted_iota(jnp.int32, (rows, 1), 0)
    first = order[2 * me] * span
    second = order[2 * me + 1] * span
    qpos = jnp.where(row < span, first + row, second + row - span)
    low = jnp.zeros((rows, 1), jnp.int32)
    start = jnp.int32(0)
    for m in range(segs):
        low = jnp.where(qpos >= start, start, low)
        start = start + lengths[m]
    keys = blocks * span
    lane = lax.broadcasted_iota(jnp.int32, (1, keys), 1)
    within, which = lane % span, lane // span
    kpos_parts = []
    for half in (side, 1 - side):
        base = jnp.zeros((1, keys), jnp.int32)
        for j in range(blocks):
            src = owner_of(step * blocks + j, me, count)
            base = jnp.where(which == j, order[2 * src + half] * span, base)
        kpos_parts.append(base + within)
    kpos = jnp.concatenate(kpos_parts, axis=1)
    visible = (kpos >= low) & (kpos <= qpos)

    lat = jnp.concatenate([mine_ref[...].reshape(keys, WIDE), other_ref[...].reshape(keys, WIDE)], axis=0)
    keyval = jnp.dot(lat[:, :LAT], up_ref[...], preferred_element_type=jnp.float32).astype(jnp.bfloat16)
    rope = lat[:, LAT : LAT + ROPE]
    scale = 1.0 / math.sqrt(NOPE + ROPE)
    for h in range(heads):
        base = h * (NOPE + VHEAD)
        key = jnp.concatenate([keyval[:, base : base + NOPE], rope], axis=1)
        scores = lax.dot_general(q_ref[h], key, (((1,), (1,)), ((), ())), preferred_element_type=jnp.float32)
        scores = jnp.where(visible, scores * scale, -1e30)
        best = m_ref[h]
        fresh = jnp.maximum(best, jnp.max(scores, axis=1, keepdims=True))
        weights = jnp.where(visible, jnp.exp(scores - fresh), 0.0)
        shrink = jnp.exp(best - fresh)
        m_ref[h] = fresh
        l_ref[h] = l_ref[h] * shrink + jnp.sum(weights, axis=1, keepdims=True)
        mixed = jnp.dot(
            weights.astype(jnp.bfloat16), keyval[:, base + NOPE : base + NOPE + VHEAD], preferred_element_type=jnp.float32
        )
        acc_ref[h] = acc_ref[h] * shrink + mixed

    @pl.when(step == pl.num_programs(0) - 1)
    def _():
        attended = [(acc_ref[h] / l_ref[h]).astype(jnp.bfloat16) for h in range(heads)]
        out = jnp.dot(jnp.concatenate(attended, axis=1), proj_ref[...], preferred_element_type=jnp.float32)
        out_ref[...] = out.astype(jnp.bfloat16)


def attend(where, lengths, order, q, mine, other, kv_up, out_proj, count):
    heads, rows, depth = q.shape
    blocks = math.gcd(count, 8)
    span = mine.shape[1]
    whole2 = lambda i, *_: (0, 0)
    whole3 = lambda i, *_: (0, 0, 0)
    lat_spec = pl.BlockSpec((blocks, span, WIDE), lambda i, *_: (i, 0, 0))
    return pl.pallas_call(
        functools.partial(attend_kernel, count, blocks),
        grid_spec=pltpu.PrefetchScalarGridSpec(
            num_scalar_prefetch=3,
            grid=(count // blocks,),
            in_specs=[
                pl.BlockSpec(q.shape, whole3),
                lat_spec,
                lat_spec,
                pl.BlockSpec(kv_up.shape, whole2),
                pl.BlockSpec(out_proj.shape, whole2),
            ],
            out_specs=pl.BlockSpec((rows, out_proj.shape[1]), whole2),
            scratch_shapes=[
                pltpu.VMEM((heads, rows, 1), jnp.float32),
                pltpu.VMEM((heads, rows, 1), jnp.float32),
                pltpu.VMEM((heads, rows, VHEAD), jnp.float32),
            ],
        ),
        out_shape=jax.ShapeDtypeStruct((rows, out_proj.shape[1]), jnp.bfloat16),
        compiler_params=pltpu.CompilerParams(vmem_limit_bytes=VMEM_LIMIT),
        name="attend",
    )(where, lengths, order, q, mine, other, kv_up, out_proj)


def norm_kernel(where, residual_ref, here_ref, there_ref, gain_ref, middle_ref, upper_ref, lower_ref):
    side = where[1]
    half = middle_ref.shape[1]
    total = here_ref[...].astype(jnp.float32) + there_ref[...].astype(jnp.float32)
    middle = (residual_ref[...].astype(jnp.float32) + total).astype(jnp.bfloat16)
    wide = middle.astype(jnp.float32)
    inverse = lax.rsqrt(jnp.mean(wide * wide, axis=1, keepdims=True) + 1e-06)
    normed = wide * inverse * gain_ref[...].astype(jnp.float32)
    middle_ref[...] = jnp.where(side == 0, wide[:, :half], wide[:, half:]).astype(jnp.bfloat16)
    normed = jnp.where(side == 0, normed[:, :half], normed[:, half:]).astype(jnp.bfloat16)
    span = upper_ref.shape[0]
    upper_ref[...] = normed[:span]
    lower_ref[...] = normed[span:]


def norm(where, residual, here, there, gain):
    rows, width = residual.shape
    half = lambda size: jax.ShapeDtypeStruct((size, width // 2), jnp.bfloat16)
    full = pl.BlockSpec((rows, width), lambda i, *_: (0, 0))
    part = lambda size: pl.BlockSpec((size, width // 2), lambda i, *_: (0, 0))
    return pl.pallas_call(
        norm_kernel,
        grid_spec=pltpu.PrefetchScalarGridSpec(
            num_scalar_prefetch=1,
            grid=(1,),
            in_specs=[full, full, full, pl.BlockSpec((1, width), lambda i, *_: (0, 0))],
            out_specs=[part(rows), part(rows // 2), part(rows // 2)],
        ),
        out_shape=[half(rows), half(rows // 2), half(rows // 2)],
        compiler_params=pltpu.CompilerParams(vmem_limit_bytes=VMEM_LIMIT),
        name="norm",
    )(where, residual, here, there, gain.reshape(1, width))


def pack_kernel(where, latent_ref, ids_ref, weights_ref, out_ref, rows):
    base, tokens = latent_ref.shape
    span = out_ref.shape[0]
    weights = weights_ref[...]
    high = weights.astype(jnp.bfloat16).astype(jnp.float32)
    rows[...] = jnp.zeros_like(rows)
    rows[0:TOP] = ids_ref[...].astype(jnp.float32)
    rows[TOP : 2 * TOP] = high
    rows[2 * TOP : 3 * TOP] = weights - high
    row = lax.broadcasted_iota(jnp.int32, (span, tokens), 0) + where[1] * span
    chosen = (row == lax.broadcasted_iota(jnp.int32, (span, tokens), 1)).astype(jnp.float32).astype(jnp.bfloat16)
    turn = lambda value: lax.dot_general(
        chosen, value, (((1,), (1,)), ((), ())), preferred_element_type=jnp.float32
    ).astype(jnp.bfloat16)
    every = jnp.concatenate([latent_ref[...], rows[...].astype(jnp.bfloat16)], axis=0)
    out_ref[...] = turn(every)


def pack(where, latent, expert_ids, route_weights):
    local_rows, base = latent.shape
    whole = lambda i, *_: (0, 0)
    return pl.pallas_call(
        pack_kernel,
        grid_spec=pltpu.PrefetchScalarGridSpec(
            num_scalar_prefetch=1,
            grid=(1,),
            in_specs=[
                pl.BlockSpec((base, local_rows), whole),
                pl.BlockSpec((TOP, local_rows), whole),
                pl.BlockSpec((TOP, local_rows), whole),
            ],
            out_specs=pl.BlockSpec((local_rows // 2, WIDE), whole),
            scratch_shapes=[pltpu.VMEM((WIDE - base, local_rows), jnp.float32)],
        ),
        out_shape=jax.ShapeDtypeStruct((local_rows // 2, WIDE), jnp.bfloat16),
        compiler_params=pltpu.CompilerParams(vmem_limit_bytes=VMEM_LIMIT),
        name="pack",
    )(where, latent.T, expert_ids.T, route_weights.T)


def expert_rows(rows, gate_ref, up_ref, down_ref, scale_ref):
    by_columns = (((1,), (1,)), ((), ()))
    gate = lax.dot_general(rows, gate_ref[0], by_columns, preferred_element_type=jnp.float32)
    upper = lax.dot_general(rows, up_ref[0], by_columns, preferred_element_type=jnp.float32)
    hidden = (gate / (1.0 + jnp.exp(-gate)) * upper * scale_ref[0]).astype(jnp.bfloat16)
    return jnp.dot(hidden, down_ref[0], preferred_element_type=jnp.float32).astype(jnp.bfloat16)


def plain_kernel(where, rows_ref, gate_ref, up_ref, down_ref, scale_ref, out_ref):
    out_ref[0] = expert_rows(rows_ref[0], gate_ref, up_ref, down_ref, scale_ref)


def fused_kernel(count, where, *refs):
    mine, other = refs[:count], refs[count : 2 * count]
    gate_ref, up_ref, down_ref, scale_ref = refs[2 * count : 2 * count + 4]
    kept, away = refs[2 * count + 4 : 3 * count + 4], refs[3 * count + 4 : 4 * count + 4]
    rows, result = refs[4 * count + 4 :]
    half = mine[0].shape[1]
    side = where[1]
    near = pl.ds(pl.multiple_of(side * half, half), half)
    far = pl.ds(pl.multiple_of((1 - side) * half, half), half)
    place = pl.ds(pl.multiple_of(pl.program_id(0) * SLOTS, SLOTS), SLOTS)
    for c in range(count):
        rows[c * SLOTS : (c + 1) * SLOTS, near] = mine[c][place, :]
        rows[c * SLOTS : (c + 1) * SLOTS, far] = other[c][place, :]
    result[...] = expert_rows(rows[...], gate_ref, up_ref, down_ref, scale_ref)
    for c in range(count):
        kept[c][place, :] = result[c * SLOTS : (c + 1) * SLOTS, near]
        away[c][place, :] = result[c * SLOTS : (c + 1) * SLOTS, far]


def expert_specs(w_gate, rows):
    hidden, width = w_gate.shape[1:]
    weight = pl.BlockSpec((1, hidden, width), lambda e, where: (e, 0, 0))
    return [weight, weight, weight, pl.BlockSpec((1, rows, 1), lambda e, where: (e, 0, 0))]


def experts_plain(where, picked, w_gate, w_up, w_down, scale):
    here, rows, width = picked.shape
    rows_spec = pl.BlockSpec((1, rows, width), lambda e, where: (e, 0, 0))
    return pl.pallas_call(
        plain_kernel,
        grid_spec=pltpu.PrefetchScalarGridSpec(
            num_scalar_prefetch=1,
            grid=(here,),
            in_specs=[rows_spec] + expert_specs(w_gate, rows),
            out_specs=rows_spec,
        ),
        out_shape=jax.ShapeDtypeStruct(picked.shape, jnp.bfloat16),
        compiler_params=pltpu.CompilerParams(vmem_limit_bytes=VMEM_LIMIT),
        name="experts",
    )(where, picked, w_gate, w_up, w_down, scale)


def experts_fused(where, mine, other, w_gate, w_up, w_down, scale):
    count, (slots, half) = len(mine), mine[0].shape
    here, rows, _ = scale.shape
    whole = pl.BlockSpec((slots, half), lambda e, where: (0, 0))
    outs = pl.pallas_call(
        functools.partial(fused_kernel, count),
        grid_spec=pltpu.PrefetchScalarGridSpec(
            num_scalar_prefetch=1,
            grid=(here,),
            in_specs=[whole] * (2 * count) + expert_specs(w_gate, rows),
            out_specs=[whole] * (2 * count),
            scratch_shapes=[pltpu.VMEM((rows, 2 * half), jnp.bfloat16)] * 2,
        ),
        out_shape=[jax.ShapeDtypeStruct((slots, half), jnp.bfloat16)] * (2 * count),
        compiler_params=pltpu.CompilerParams(vmem_limit_bytes=VMEM_LIMIT),
        name="experts",
    )(where, *mine, *other, w_gate, w_up, w_down, scale)
    return outs[:count], outs[count:]


def body(
    queries,
    latent,
    residual,
    seg_lengths,
    span_order,
    expert_ids,
    route_weights,
    kv_up,
    out_proj,
    norm_gain,
    w_gate,
    w_up,
    w_down,
):
    local_rows, width = residual.shape
    span = local_rows // 2
    heads = kv_up.shape[1] // (NOPE + VHEAD)
    count = lax.axis_size("ctx")
    here = EXPERTS // count
    me, side = lax.axis_index("ctx"), lax.axis_index("exp")
    where = jnp.stack([me, side]).astype(jnp.int32)

    base = latent.shape[1]
    found = across(direct(pack(where, latent, expert_ids, route_weights), count), count)
    mine = jnp.stack(found)
    other = jnp.stack(each(swap, found, count))

    q = queries.reshape(local_rows, heads, NOPE + ROPE).transpose(1, 0, 2)
    partial = attend(where, seg_lengths, span_order, q, mine, other, kv_up, out_proj, count)
    middle, upper, lower = norm(where, residual, partial, swap(partial), norm_gain)

    facts_mine, facts_other = mine[:, :, base : base + 3 * TOP], other[:, :, base : base + 3 * TOP]
    facts = jnp.concatenate(
        [jnp.where(side == 0, facts_mine, facts_other), jnp.where(side == 0, facts_other, facts_mine)], axis=1
    ).astype(jnp.float32)
    ids, share = facts[:, :, :TOP], facts[:, :, TOP : 2 * TOP] + facts[:, :, 2 * TOP :]
    own = (me * here + jnp.arange(here, dtype=jnp.int32)).astype(jnp.float32)
    hit = ids[:, :, :, None] == own
    hot = jnp.any(hit, axis=2)
    share = jnp.sum(jnp.where(hit, share[:, :, :, None], 0.0), axis=2)
    token = jnp.arange(local_rows, dtype=jnp.int32)
    before = (token[:, None] > token[None, :]).astype(jnp.bfloat16)
    rank = jnp.einsum("tu,cue->cte", before, hot.astype(jnp.bfloat16), preferred_element_type=jnp.float32)
    rank = jnp.where(hot, rank, -1.0)
    slot = jnp.arange(SLOTS, dtype=jnp.int32).astype(jnp.float32)
    combine = rank[:, :, :, None] == slot
    scale = jnp.sum(jnp.where(combine, share[:, :, :, None], 0.0), axis=1)
    scale = scale.transpose(1, 0, 2).reshape(here, count * SLOTS, 1)
    combine = combine.astype(jnp.bfloat16).reshape(count, local_rows, here * SLOTS)
    pick = combine.transpose(0, 2, 1)

    lines = [ring(upper, count), ring(lower, count)]
    lines[0][1], pick, combine, scale = lax.optimization_barrier((lines[0][1], pick, combine, scale))
    halves = [across(line, count) for line in lines]
    got = [jnp.concatenate(pair, axis=0) for pair in zip(*halves)]
    got_other = each(swap, got, count)
    w_gate, w_up = w_gate.transpose(0, 2, 1), w_up.transpose(0, 2, 1)
    if count <= FEW:
        choose = lambda c, rows: jnp.dot(pick[c], rows, preferred_element_type=jnp.float32).astype(jnp.bfloat16)
        mine = [choose(c, got[c]) for c in range(count)]
        other = [choose(c, got_other[c]) for c in range(count)]
        kept, away = experts_fused(where, mine, other, w_gate, w_up, w_down, scale)
    else:
        near, far = jnp.stack(got), jnp.stack(got_other)
        full = jnp.concatenate([jnp.where(side == 0, near, far), jnp.where(side == 0, far, near)], axis=2)
        picked = jnp.einsum("cst,ctd->csd", pick, full, preferred_element_type=jnp.float32).astype(jnp.bfloat16)
        picked = picked.reshape(count, here, SLOTS, width).transpose(1, 0, 2, 3).reshape(here, count * SLOTS, width)
        result = experts_plain(where, picked, w_gate, w_up, w_down, scale)
        result = result.reshape(here, count, SLOTS, width).transpose(1, 0, 2, 3).reshape(count, here * SLOTS, width)
        left, right = jnp.split(result, 2, axis=2)
        kept, away = jnp.where(side == 0, left, right), jnp.where(side == 0, right, left)
    mixture = collect(kept, each(swap, away, count), combine, count)
    return (middle.astype(jnp.float32) + mixture).astype(jnp.bfloat16)


def solution(mesh):
    in_specs = (
        P(("groups", "ctx"), "exp"),
        P(("groups", "ctx"), None),
        P(("groups", "ctx"), None),
        P("groups"),
        P("groups"),
        P(("groups", "ctx"), None),
        P(("groups", "ctx"), None),
        P(None, "exp"),
        P("exp", None),
        P(),
        P("ctx", None, "exp"),
        P("ctx", None, "exp"),
        P("ctx", "exp", None),
    )
    out_specs = P(("groups", "ctx"), "exp")
    return jax.shard_map(body, mesh=mesh, in_specs=in_specs, out_specs=out_specs, check_vma=False)
```

time: 176 us -> 177 us (level)
  matrix products: 0.14 us -> 25.4 us
  other arithmetic: 15 us -> 1.44 us
  waiting for transfers between devices: 79.7 us -> 67.1 us
  starting transfers between devices: 22.5 us -> 28.3 us
  Pallas kernels: 47.6 us -> 45.2 us
    dot_general x0 -> x24, matrix products: none -> 25.2 us  [the longest x16 14.8 us: body(): jnp.dot(pick[c], rows, preferred_element_type=jnp.float32)]
    ppermute x9 -> x12, waiting for transfers between devices: 48.1 us -> 30.7 us  [shift_slow(): return lax.ppermute(value, 'ctx', perm)]
    convert_element_type x9 -> x0, other arithmetic: 9.92 us -> none  [the longest x4 4.07 us: collect(): parts = [summed([kept[c], away[c]]).astype(jnp.bfloat16) for c in here]]
    ppermute x12 -> x16, waiting for transfers between devices: 29.4 us -> 33.7 us  [shift_fast(): return lax.ppermute(value, 'ctx', perm)]
    ppermute x12 -> x16, starting transfers between devices: 12.5 us -> 16.6 us  [shift_fast(): return lax.ppermute(value, 'ctx', perm)]
    pallas_call x1, Pallas kernels: 34.2 us -> 31.7 us  [experts_fused(): pl.pallas_call(functools.partial(fused_kernel, count), grid_spec=pltpu.Pr...]
    ppermute x9 -> x12, starting transfers between devices: 5.58 us -> 7.9 us  [shift_slow(): return lax.ppermute(value, 'ctx', perm)]
    concatenate x2 -> x0, other arithmetic: 1.94 us -> none  [the longest x1 1.25 us: body(): jnp.concatenate([jnp.stack([me, side]).astype(jnp.int32), seg_lengths, sp...]
  transfers between devices with their start and end apart: 46 -> 53, of which waited for: 18 -> 21; matrix products, arithmetic and copies ran while one was open for 10% -> 17% of each run, Pallas kernels for 0% -> 0%
where the time goes in v3:
time: 177 us
  waiting for transfers between devices  67.1 us (38%)
  Pallas kernels  45.2 us (26%)
  starting transfers between devices  28.3 us (16%)
  matrix products  25.4 us (14%)
  local copies, waits for them, and re-layouts  8.88 us (5%)
    ppermute x16, waiting for transfers between devices, shift_fast(): return lax.ppermute(value, 'ctx', perm)  33.7 us
    pallas_call x1, Pallas kernels, experts_fused(): pl.pallas_call(functools.partial(fused_kernel, count), grid_spec=pltpu.Pr...  31.7 us
    ppermute x12, waiting for transfers between devices, shift_slow(): return lax.ppermute(value, 'ctx', perm)  30.7 us
    ppermute x16, starting transfers between devices, shift_fast(): return lax.ppermute(value, 'ctx', perm)  16.6 us
    dot_general x16, matrix products, body(): jnp.dot(pick[c], rows, preferred_element_type=jnp.float32)  14.8 us
    dot_general x8, matrix products, part(): return jnp.dot(combine[c], rows, preferred_element_type=jnp.float32)  10.4 us
    ppermute x12, starting transfers between devices, shift_slow(): return lax.ppermute(value, 'ctx', perm)  7.9 us
    pallas_call x1, Pallas kernels, attend(): pl.pallas_call(functools.partial(attend_kernel, count, blocks), grid_spec...  7.87 us
  transfers between devices with their start and end apart: 53, of which 21 were waited for; matrix products, arithmetic and copies ran while one was open for 17% of the time, Pallas kernels for 0%

profile of v3, /device:TPU:0, one launch (start us, length us, event | category | flops | bytes accessed | tf_op | source)
XLA Modules:
  0.0 176.8 jit_solution(10165003800627100896)
XLA Ops:
  0.6 2.4 %pack.1 = bf16[64,640]{1,0:T(8,128)(2,1)} custom-call(s32[2]{0:T(128)} %pad_add_fusion.where, bf16[576,128]{1,0:T(8,128)(2,1)} %bitcast.155, s32[6,128]{1,0:T(8,128)} %bitcast.157, f32[6,128]{1,0:T(8,128)} %bitcast.158), custom_call_target="tpu_custom_call" | custom-call | tf_op jit(solution)/shard_map/pack/pallas_call | solution.py:249
  3.5 2.5 %collective-permute-start.3 = (bf16[64,640]{1,0:T(8,128)(2,1)}, bf16[64,640]{1,0:T(8,128)(2,1)S(1)}, u32[]{:S(2)}, u32[]{:S(2)}) collective-permute-start(bf16[64,640]{1,0:T(8,128)(2,1)} %pack.1), channel_id=1, source_target_pairs={{0,2},{2,0},{4,6},{6,4},{8,10},{10,8},{12,14},{14,12},{1,3},{3,1},... | collective-permute-start | bytes 245768 | tf_op jit(solution)/shard_map/ppermute | solution.py:38
  6.0 3.6 %collective-permute-start.2 = (bf16[64,640]{1,0:T(8,128)(2,1)}, bf16[64,640]{1,0:T(8,128)(2,1)S(1)}, u32[]{:S(2)}, u32[]{:S(2)}) collective-permute-start(bf16[64,640]{1,0:T(8,128)(2,1)} %pack.1), channel_id=1, source_target_pairs={{0,12},{2,14},{4,0},{6,2},{8,4},{10,6},{12,8},{14,10},{1,13},{3,15... | collective-permute-start | bytes 245768 | tf_op jit(solution)/shard_map/ppermute | solution.py:32
  9.6 1.0 collective-permute-start
  11.6 1.3 reshape.26.gain_ref
  12.9 1.1 copy.26
  15.6 2.3 %collective-permute-done.1 = bf16[64,640]{1,0:T(8,128)(2,1)S(1)} collective-permute-done((bf16[64,640]{1,0:T(8,128)(2,1)}, bf16[64,640]{1,0:T(8,128)(2,1)S(1)}, u32[]{:S(2)}, u32[]{:S(2)}) %collective-permute-start.1) | collective-permute-done | bytes 81952 | tf_op jit(solution)/shard_map/ppermute | solution.py:32
  18.5 4.3 %collective-permute-done.4 = bf16[64,640]{1,0:T(8,128)(2,1)S(1)} collective-permute-done((bf16[64,640]{1,0:T(8,128)(2,1)S(1)}, bf16[64,640]{1,0:T(8,128)(2,1)S(1)}, u32[]{:S(2)}, u32[]{:S(2)}) %collective-permute-start.4) | collective-permute-done | bytes 81952 | tf_op jit(solution)/shard_map/ppermute | solution.py:38
  23.4 3.8 %collective-permute-done.5 = bf16[64,640]{1,0:T(8,128)(2,1)S(1)} collective-permute-done((bf16[64,640]{1,0:T(8,128)(2,1)S(1)}, bf16[64,640]{1,0:T(8,128)(2,1)S(1)}, u32[]{:S(2)}, u32[]{:S(2)}) %collective-permute-start.5) | collective-permute-done | bytes 81952 | tf_op jit(solution)/shard_map/ppermute | solution.py:38
  28.0 1.2 collective-permute-done.12
  30.1 7.9 %attend.1.here_ref = bf16[128,2048]{1,0:T(8,128)(2,1)} custom-call(s32[2]{0:T(128)} %pad_add_fusion.where, s32[16]{0:T(128)} %lengths.1, s32[16]{0:T(128)} %order.1, bf16[4,128,192]{2,1,0:T(8,128)(2,1)} %bitcast.153, bf16[8,64,640]{2,1,0:T(8,128)(2,1)} %copy-done, bf16[8,64,640]{2,1,0:T(8,128)(2,1)} %copy-done.1, bf16[512,1024]{1,0:T(8,128)(2,1)} %up_ref.1, ...), custom_call_target="tpu_custom_call" | custom-call | tf_op jit(solution)/shard_map/attend/pallas_call | solution.py:169
  39.0 1.1 collective-permute-done.15.there_ref
  40.9 3.2 %norm.1 = (bf16[128,1024]{1,0:T(8,128)(2,1)}, bf16[64,1024]{1,0:T(8,128)(2,1)}, bf16[64,1024]{1,0:T(8,128)(2,1)}) custom-call(s32[2]{0:T(128)} %pad_add_fusion.where, bf16[128,2048]{1,0:T(8,128)(2,1)} %residual_ref.1, bf16[128,2048]{1,0:T(8,128)(2,1)} %attend.1.here_ref, bf16[128,2048]{1,0:T(8,128)(2,1)} %copy-done.2, bf16[1,2048]{1,0:T(2,128)(2,1)} %reshape.26.gain_ref), custom_call_target="tpu_custom_call" | custom-call | tf_op jit(solution)/shard_map/norm/pallas_call | solution.py:214
  44.6 1.2 collective-permute-start.16
  45.8 1.5 collective-permute-start.23
  50.1 2.5 %collective-permute-done.16 = bf16[64,1024]{1,0:T(8,128)(2,1)S(1)} collective-permute-done((bf16[64,1024]{1,0:T(8,128)(2,1)}, bf16[64,1024]{1,0:T(8,128)(2,1)S(1)}, u32[]{:S(2)}, u32[]{:S(2)}) %collective-permute-start.16) | collective-permute-done | bytes 131104 | tf_op jit(solution)/shard_map/ppermute | solution.py:32
  52.6 1.9 %collective-permute-start.24 = (bf16[64,1024]{1,0:T(8,128)(2,1)S(1)}, bf16[64,1024]{1,0:T(8,128)(2,1)S(1)}, u32[]{:S(2)}, u32[]{:S(2)}) collective-permute-start(bf16[64,1024]{1,0:T(8,128)(2,1)S(1)} %collective-permute-done.16), channel_id=1, source_target_pairs={{0,2},{2,0},{4,6},{6,4},{8,10},{10,8},{12,14},{14,12},{1,3},{3,1},... | collective-permute-start | bytes 393224 | tf_op jit(solution)/shard_map/ppermute | solution.py:38
  54.5 0.9 convolution_convert_fusion.19.refs_0_
  57.7 1.0 copy.33.refs_19_
  58.7 5.8 %collective-permute-done.18 = bf16[64,1024]{1,0:T(8,128)(2,1)S(1)} collective-permute-done((bf16[64,1024]{1,0:T(8,128)(2,1)S(1)}, bf16[64,1024]{1,0:T(8,128)(2,1)S(1)}, u32[]{:S(2)}, u32[]{:S(2)}) %collective-permute-start.18) | collective-permute-done | bytes 131104 | tf_op jit(solution)/shard_map/ppermute | solution.py:32
  64.5 2.4 %collective-permute-done.19 = bf16[64,1024]{1,0:T(8,128)(2,1)S(1)} collective-permute-done((bf16[64,1024]{1,0:T(8,128)(2,1)S(1)}, bf16[64,1024]{1,0:T(8,128)(2,1)S(1)}, u32[]{:S(2)}, u32[]{:S(2)}) %collective-permute-start.19) | collective-permute-done | bytes 131104 | tf_op jit(solution)/shard_map/ppermute | solution.py:32
  68.7 3.4 %collective-permute-done.25 = bf16[64,1024]{1,0:T(8,128)(2,1)S(1)} collective-permute-done((bf16[64,1024]{1,0:T(8,128)(2,1)S(1)}, bf16[64,1024]{1,0:T(8,128)(2,1)S(1)}, u32[]{:S(2)}, u32[]{:S(2)}) %collective-permute-start.25) | collective-permute-done | bytes 131104 | tf_op jit(solution)/shard_map/ppermute | solution.py:38
  74.0 5.6 %collective-permute-done.20 = bf16[64,1024]{1,0:T(8,128)(2,1)S(1)} collective-permute-done((bf16[64,1024]{1,0:T(8,128)(2,1)S(1)}, bf16[64,1024]{1,0:T(8,128)(2,1)S(1)}, u32[]{:S(2)}, u32[]{:S(2)}) %collective-permute-start.20) | collective-permute-done | bytes 131104 | tf_op jit(solution)/shard_map/ppermute | solution.py:32
  82.7 1.9 %collective-permute-done.26 = bf16[64,1024]{1,0:T(8,128)(2,1)S(1)} collective-permute-done((bf16[64,1024]{1,0:T(8,128)(2,1)S(1)}, bf16[64,1024]{1,0:T(8,128)(2,1)S(1)}, u32[]{:S(2)}, u32[]{:S(2)}) %collective-permute-start.26) | collective-permute-done | bytes 131104 | tf_op jit(solution)/shard_map/ppermute | solution.py:38
  84.6 1.4 collective-permute-done.27
  86.0 0.9 convolution_convert_fusion.13.refs_6_
  88.6 1.3 collective-permute-start.29
  89.9 0.9 convolution_convert_fusion.7.refs_12_
  90.8 2.4 %collective-permute-done.28 = bf16[64,1024]{1,0:T(8,128)(2,1)S(1)} collective-permute-done((bf16[64,1024]{1,0:T(8,128)(2,1)S(1)}, bf16[64,1024]{1,0:T(8,128)(2,1)S(1)}, u32[]{:S(2)}, u32[]{:S(2)}) %collective-permute-start.28) | collective-permute-done | bytes 131104 | tf_op jit(solution)/shard_map/ppermute | solution.py:38
  93.2 2.4 %collective-permute-done.29 = bf16[64,1024]{1,0:T(8,128)(2,1)S(1)} collective-permute-done((bf16[64,1024]{1,0:T(8,128)(2,1)S(1)}, bf16[64,1024]{1,0:T(8,128)(2,1)S(1)}, u32[]{:S(2)}, u32[]{:S(2)}) %collective-permute-start.29) | collective-permute-done | bytes 131104 | tf_op jit(solution)/shard_map/ppermute | solution.py:38
  97.5 0.9 convolution_convert_fusion.6.refs_13_
  99.4 0.9 convolution_convert_fusion.5.refs_14_
  101.2 31.7 %experts.1 = (bf16[128,1024]{1,0:T(8,128)(2,1)}, bf16[128,1024]{1,0:T(8,128)(2,1)}, bf16[128,1024]{1,0:T(8,128)(2,1)}, bf16[128,1024]{1,0:T(8,128)(2,1)}, bf16[1...) custom-call(s32[2]{0:T(128)} %pad_add_fusion.where, ...), custom_call_target="tpu_custom_call" | custom-call | tf_op jit(solution)/shard_map/experts/pallas_call | solution.py:326
  135.3 1.2 convolution_convert_fusion.3
  136.7 1.2 convolution_convert_fusion.2
  138.7 1.2 convolution_convert_fusion.1
  140.0 1.4 collective-permute-start.47
  141.3 1.2 convolution_convert_fusion
  142.6 4.5 %collective-permute-done.43 = bf16[128,1024]{1,0:T(8,128)(2,1)S(1)} collective-permute-done((bf16[128,1024]{1,0:T(8,128)(2,1)S(1)}, bf16[128,1024]{1,0:T(8,128)(2,1)S(1)}, u32[]{:S(2)}, u32[]{:S(2)}) %collective-permute-start.43) | collective-permute-done | bytes 262176 | tf_op jit(solution)/shard_map/ppermute | solution.py:38
  147.9 1.2 fusion.3
  149.1 1.4 collective-permute-start.40
  150.4 2.3 %collective-permute-done.47 = bf16[128,1024]{1,0:T(8,128)(2,1)S(1)} collective-permute-done((bf16[128,1024]{1,0:T(8,128)(2,1)S(1)}, bf16[128,1024]{1,0:T(8,128)(2,1)S(1)}, u32[]{:S(2)}, u32[]{:S(2)}) %collective-permute-start.47) | collective-permute-done | bytes 262176 | tf_op jit(solution)/shard_map/ppermute | solution.py:38
  153.6 1.2 fusion.4
  154.9 3.5 %collective-permute-done.51 = bf16[128,1024]{1,0:T(8,128)(2,1)S(1)} collective-permute-done((bf16[128,1024]{1,0:T(8,128)(2,1)S(1)}, bf16[128,1024]{1,0:T(8,128)(2,1)S(1)}, u32[]{:S(2)}, u32[]{:S(2)}) %collective-permute-start.51) | collective-permute-done | bytes 262176 | tf_op jit(solution)/shard_map/ppermute | solution.py:38
  158.4 1.2 fusion.5
  159.6 3.8 %collective-permute-done.40 = bf16[128,1024]{1,0:T(8,128)(2,1)S(1)} collective-permute-done((bf16[128,1024]{1,0:T(8,128)(2,1)S(1)}, bf16[128,1024]{1,0:T(8,128)(2,1)S(1)}, u32[]{:S(2)}, u32[]{:S(2)}) %collective-permute-start.40) | collective-permute-done | bytes 262176 | tf_op jit(solution)/shard_map/ppermute | solution.py:38
  163.4 11.4 %collective-permute-done.48 = bf16[128,1024]{1,0:T(8,128)(2,1)S(1)} collective-permute-done((bf16[128,1024]{1,0:T(8,128)(2,1)S(1)}, bf16[128,1024]{1,0:T(8,128)(2,1)S(1)}, u32[]{:S(2)}, u32[]{:S(2)}) %collective-permute-start.48) | collective-permute-done | bytes 262176 | tf_op jit(solution)/shard_map/ppermute | solution.py:32
  174.8 2.0 %add_convert_fusion = bf16[128,1024]{1,0:T(8,128)(2,1)} fusion(bf16[128,1024]{1,0:T(8,128)(2,1)S(1)} %copy-done.3, bf16[128,1024]{1,0:T(8,128)(2,1)S(1)} %collective-permute-done.52, bf16[128,1024]{1,0:T(8,128)(2,1)S(1)} %collective-permute-done.48, bf16[128,1024]{1,0:T(8,128)(2,1)S(1)} %collective-permute-done.44, ...), kind=kOutput, calls=%fused_computation.33 | convolution fusion | flops 35520512 | bytes 2129920 | tf_op jit(solution)/shard_map/dot_general | solution.py:81
  (149 shorter events, 30.8 us)
Async XLA Ops:
  3.0 11.9 %collective-permute-start.7 = (bf16[64,640]{1,0:T(8,128)(2,1)}, bf16[64,640]{1,0:T(8,128)(2,1)S(1)}, u32[]{:S(2)}, u32[]{:S(2)}) collective-permute-start(bf16[64,640]{1,0:T(8,128)(2,1)} %pack.1), channel_id=1, source_target_pairs={{0,1},{1,0},{2,3},{3,2},{4,5},{5,4},{6,7},{7,6},{8,9},{9,8},{10,11... | collective-permute-start | bytes 245768 | tf_op jit(solution)/shard_map/ppermute | solution.py:42
  3.5 12.0 %collective-permute-start.3 = (bf16[64,640]{1,0:T(8,128)(2,1)}, bf16[64,640]{1,0:T(8,128)(2,1)S(1)}, u32[]{:S(2)}, u32[]{:S(2)}) collective-permute-start(bf16[64,640]{1,0:T(8,128)(2,1)} %pack.1), channel_id=1, source_target_pairs={{0,2},{2,0},{4,6},{6,4},{8,10},{10,8},{12,14},{14,12},{1,3},{3,1},... | collective-permute-start | bytes 245768 | tf_op jit(solution)/shard_map/ppermute | solution.py:38
  6.0 8.9 %collective-permute-start.2 = (bf16[64,640]{1,0:T(8,128)(2,1)}, bf16[64,640]{1,0:T(8,128)(2,1)S(1)}, u32[]{:S(2)}, u32[]{:S(2)}) collective-permute-start(bf16[64,640]{1,0:T(8,128)(2,1)} %pack.1), channel_id=1, source_target_pairs={{0,12},{2,14},{4,0},{6,2},{8,4},{10,6},{12,8},{14,10},{1,13},{3,15... | collective-permute-start | bytes 245768 | tf_op jit(solution)/shard_map/ppermute | solution.py:32
  9.6 8.3 %collective-permute-start.1 = (bf16[64,640]{1,0:T(8,128)(2,1)}, bf16[64,640]{1,0:T(8,128)(2,1)S(1)}, u32[]{:S(2)}, u32[]{:S(2)}) collective-permute-start(bf16[64,640]{1,0:T(8,128)(2,1)} %pack.1), channel_id=1, source_target_pairs={{0,8},{2,10},{4,12},{6,14},{8,0},{10,2},{12,4},{14,6},{1,9},{3,11}... | collective-permute-start | bytes 245768 | tf_op jit(solution)/shard_map/ppermute | solution.py:32
  9.6 8.3 %collective-permute-start = (bf16[64,640]{1,0:T(8,128)(2,1)}, bf16[64,640]{1,0:T(8,128)(2,1)S(1)}, u32[]{:S(2)}, u32[]{:S(2)}) collective-permute-start(bf16[64,640]{1,0:T(8,128)(2,1)} %pack.1), channel_id=1, source_target_pairs={{0,4},{2,6},{4,8},{6,10},{8,12},{10,14},{12,0},{14,2},{1,5},{3,7},... | collective-permute-start | bytes 245768 | tf_op jit(solution)/shard_map/ppermute | solution.py:32
  14.8 13.1 %collective-permute-start.10 = (bf16[64,640]{1,0:T(8,128)(2,1)S(1)}, bf16[64,640]{1,0:T(8,128)(2,1)S(1)}, u32[]{:S(2)}, u32[]{:S(2)}) collective-permute-start(bf16[64,640]{1,0:T(8,128)(2,1)S(1)} %collective-permute-done.2), channel_id=1, source_target_pairs={{0,1},{1,0},{2,3},{3,2},{4,5},{5,4},{6,7},{7,6},{8,9},{9,8},{10,11... | collective-permute-start | bytes 245768 | tf_op jit(solution)/shard_map/ppermute | solution.py:42
  14.9 8.4 %collective-permute-start.6 = (bf16[64,640]{1,0:T(8,128)(2,1)S(1)}, bf16[64,640]{1,0:T(8,128)(2,1)S(1)}, u32[]{:S(2)}, u32[]{:S(2)}) collective-permute-start(bf16[64,640]{1,0:T(8,128)(2,1)S(1)} %collective-permute-done.2), channel_id=1, source_target_pairs={{0,2},{2,0},{4,6},{6,4},{8,10},{10,8},{12,14},{14,12},{1,3},{3,1},... | collective-permute-start | bytes 245768 | tf_op jit(solution)/shard_map/ppermute | solution.py:38
  15.4 12.6 %collective-permute-start.11 = (bf16[64,640]{1,0:T(8,128)(2,1)S(1)}, bf16[64,640]{1,0:T(8,128)(2,1)S(1)}, u32[]{:S(2)}, u32[]{:S(2)}) collective-permute-start(bf16[64,640]{1,0:T(8,128)(2,1)S(1)} %collective-permute-done.3), channel_id=1, source_target_pairs={{0,1},{1,0},{2,3},{3,2},{4,5},{5,4},{6,7},{7,6},{8,9},{9,8},{10,11... | collective-permute-start | bytes 245768 | tf_op jit(solution)/shard_map/ppermute | solution.py:42
  17.9 10.0 %collective-permute-start.9 = (bf16[64,640]{1,0:T(8,128)(2,1)S(1)}, bf16[64,640]{1,0:T(8,128)(2,1)S(1)}, u32[]{:S(2)}, u32[]{:S(2)}) collective-permute-start(bf16[64,640]{1,0:T(8,128)(2,1)S(1)} %collective-permute-done.1), channel_id=1, source_target_pairs={{0,1},{1,0},{2,3},{3,2},{4,5},{5,4},{6,7},{7,6},{8,9},{9,8},{10,11... | collective-permute-start | bytes 245768 | tf_op jit(solution)/shard_map/ppermute | solution.py:42
  17.9 4.9 %collective-permute-start.4 = (bf16[64,640]{1,0:T(8,128)(2,1)S(1)}, bf16[64,640]{1,0:T(8,128)(2,1)S(1)}, u32[]{:S(2)}, u32[]{:S(2)}) collective-permute-start(bf16[64,640]{1,0:T(8,128)(2,1)S(1)} %collective-permute-done), channel_id=1, source_target_pairs={{0,2},{2,0},{4,6},{6,4},{8,10},{10,8},{12,14},{14,12},{1,3},{3,1},... | collective-permute-start | bytes 245768 | tf_op jit(solution)/shard_map/ppermute | solution.py:38
  22.8 4.4 %collective-permute-start.5 = (bf16[64,640]{1,0:T(8,128)(2,1)S(1)}, bf16[64,640]{1,0:T(8,128)(2,1)S(1)}, u32[]{:S(2)}, u32[]{:S(2)}) collective-permute-start(bf16[64,640]{1,0:T(8,128)(2,1)S(1)} %collective-permute-done.1), channel_id=1, source_target_pairs={{0,2},{2,0},{4,6},{6,4},{8,10},{10,8},{12,14},{14,12},{1,3},{3,1},... | collective-permute-start | bytes 245768 | tf_op jit(solution)/shard_map/ppermute | solution.py:38
  23.3 4.0 %collective-permute-start.8 = (bf16[64,640]{1,0:T(8,128)(2,1)S(1)}, bf16[64,640]{1,0:T(8,128)(2,1)S(1)}, u32[]{:S(2)}, u32[]{:S(2)}) collective-permute-start(bf16[64,640]{1,0:T(8,128)(2,1)S(1)} %collective-permute-done), channel_id=1, source_target_pairs={{0,1},{1,0},{2,3},{3,2},{4,5},{5,4},{6,7},{7,6},{8,9},{9,8},{10,11... | collective-permute-start | bytes 245768 | tf_op jit(solution)/shard_map/ppermute | solution.py:42
  44.1 12.3 %collective-permute-start.22 = (bf16[64,1024]{1,0:T(8,128)(2,1)}, bf16[64,1024]{1,0:T(8,128)(2,1)S(1)}, u32[]{:S(2)}, u32[]{:S(2)}) collective-permute-start(bf16[64,1024]{1,0:T(8,128)(2,1)} %get-tuple-element.29), channel_id=1, source_target_pairs={{0,2},{2,0},{4,6},{6,4},{8,10},{10,8},{12,14},{14,12},{1,3},{3,1},... | collective-permute-start | bytes 393224 | tf_op jit(solution)/shard_map/ppermute | solution.py:38
  44.6 8.0 %collective-permute-start.16 = (bf16[64,1024]{1,0:T(8,128)(2,1)}, bf16[64,1024]{1,0:T(8,128)(2,1)S(1)}, u32[]{:S(2)}, u32[]{:S(2)}) collective-permute-start(bf16[64,1024]{1,0:T(8,128)(2,1)} %get-tuple-element.29), channel_id=1, source_target_pairs={{0,4},{2,6},{4,8},{6,10},{8,12},{10,14},{12,0},{14,2},{1,5},{3,7},... | collective-permute-start | bytes 393224 | tf_op jit(solution)/shard_map/ppermute | solution.py:32
  45.8 10.7 %collective-permute-start.23 = (bf16[64,1024]{1,0:T(8,128)(2,1)}, bf16[64,1024]{1,0:T(8,128)(2,1)S(1)}, u32[]{:S(2)}, u32[]{:S(2)}) collective-permute-start(bf16[64,1024]{1,0:T(8,128)(2,1)} %get-tuple-element.32), channel_id=1, source_target_pairs={{0,2},{2,0},{4,6},{6,4},{8,10},{10,8},{12,14},{14,12},{1,3},{3,1},... | collective-permute-start | bytes 393224 | tf_op jit(solution)/shard_map/ppermute | solution.py:38
  47.3 8.2 %collective-permute-start.17 = (bf16[64,1024]{1,0:T(8,128)(2,1)}, bf16[64,1024]{1,0:T(8,128)(2,1)S(1)}, u32[]{:S(2)}, u32[]{:S(2)}) collective-permute-start(bf16[64,1024]{1,0:T(8,128)(2,1)} %get-tuple-element.32), channel_id=1, source_target_pairs={{0,4},{2,6},{4,8},{6,10},{8,12},{10,14},{12,0},{14,2},{1,5},{3,7},... | collective-permute-start | bytes 393224 | tf_op jit(solution)/shard_map/ppermute | solution.py:32
  50.0 23.1 %collective-permute-start.30 = (bf16[128,1024]{1,0:T(8,128)(2,1)S(1)}, bf16[128,1024]{1,0:T(8,128)(2,1)S(1)}, u32[]{:S(2)}, u32[]{:S(2)}) collective-permute-start(bf16[128,1024]{1,0:T(8,128)(2,1)S(1)} %constant_dynamic-update-slice_fusion), channel_id=1, source_target_pairs={{0,1},{1,0},{2,3},{3,2},{4,5},{5,4},{6,7},{7,6},{8,9},{9,8},{10,11... | collective-permute-start | bytes 786440 | tf_op jit(solution)/shard_map/ppermute | solution.py:42
  52.6 16.1 %collective-permute-start.24 = (bf16[64,1024]{1,0:T(8,128)(2,1)S(1)}, bf16[64,1024]{1,0:T(8,128)(2,1)S(1)}, u32[]{:S(2)}, u32[]{:S(2)}) collective-permute-start(bf16[64,1024]{1,0:T(8,128)(2,1)S(1)} %collective-permute-done.16), channel_id=1, source_target_pairs={{0,2},{2,0},{4,6},{6,4},{8,10},{10,8},{12,14},{14,12},{1,3},{3,1},... | collective-permute-start | bytes 393224 | tf_op jit(solution)/shard_map/ppermute | solution.py:38
  56.4 30.5 %collective-permute-start.31 = (bf16[128,1024]{1,0:T(8,128)(2,1)S(1)}, bf16[128,1024]{1,0:T(8,128)(2,1)S(1)}, u32[]{:S(2)}, u32[]{:S(2)}) collective-permute-start(bf16[128,1024]{1,0:T(8,128)(2,1)S(1)} %constant_dynamic-update-slice_fusion.2), channel_id=1, source_target_pairs={{0,1},{1,0},{2,3},{3,2},{4,5},{5,4},{6,7},{7,6},{8,9},{9,8},{10,11... | collective-permute-start | bytes 786440 | tf_op jit(solution)/shard_map/ppermute | solution.py:42
  56.4 8.1 %collective-permute-start.18 = (bf16[64,1024]{1,0:T(8,128)(2,1)S(1)}, bf16[64,1024]{1,0:T(8,128)(2,1)S(1)}, u32[]{:S(2)}, u32[]{:S(2)}) collective-permute-start(bf16[64,1024]{1,0:T(8,128)(2,1)S(1)} %collective-permute-done.16), channel_id=1, source_target_pairs={{0,4},{2,6},{4,8},{6,10},{8,12},{10,14},{12,0},{14,2},{1,5},{3,7},... | collective-permute-start | bytes 393224 | tf_op jit(solution)/shard_map/ppermute | solution.py:32
  56.5 10.5 %collective-permute-start.19 = (bf16[64,1024]{1,0:T(8,128)(2,1)S(1)}, bf16[64,1024]{1,0:T(8,128)(2,1)S(1)}, u32[]{:S(2)}, u32[]{:S(2)}) collective-permute-start(bf16[64,1024]{1,0:T(8,128)(2,1)S(1)} %collective-permute-done.17), channel_id=1, source_target_pairs={{0,4},{2,6},{4,8},{6,10},{8,12},{10,14},{12,0},{14,2},{1,5},{3,7},... | collective-permute-start | bytes 393224 | tf_op jit(solution)/shard_map/ppermute | solution.py:32
  64.5 24.0 %collective-permute-start.34 = (bf16[128,1024]{1,0:T(8,128)(2,1)S(1)}, bf16[128,1024]{1,0:T(8,128)(2,1)S(1)}, u32[]{:S(2)}, u32[]{:S(2)}) collective-permute-start(bf16[128,1024]{1,0:T(8,128)(2,1)S(1)} %constant_dynamic-update-slice_fusion.8), channel_id=1, source_target_pairs={{0,1},{1,0},{2,3},{3,2},{4,5},{5,4},{6,7},{7,6},{8,9},{9,8},{10,11... | collective-permute-start | bytes 786440 | tf_op jit(solution)/shard_map/ppermute | solution.py:42
  67.0 5.1 %collective-permute-start.25 = (bf16[64,1024]{1,0:T(8,128)(2,1)S(1)}, bf16[64,1024]{1,0:T(8,128)(2,1)S(1)}, u32[]{:S(2)}, u32[]{:S(2)}) collective-permute-start(bf16[64,1024]{1,0:T(8,128)(2,1)S(1)} %collective-permute-done.17), channel_id=1, source_target_pairs={{0,2},{2,0},{4,6},{6,4},{8,10},{10,8},{12,14},{14,12},{1,3},{3,1},... | collective-permute-start | bytes 393224 | tf_op jit(solution)/shard_map/ppermute | solution.py:38
  68.6 27.9 %collective-permute-start.32 = (bf16[128,1024]{1,0:T(8,128)(2,1)S(1)}, bf16[128,1024]{1,0:T(8,128)(2,1)S(1)}, u32[]{:S(2)}, u32[]{:S(2)}) collective-permute-start(bf16[128,1024]{1,0:T(8,128)(2,1)S(1)} %constant_dynamic-update-slice_fusion.4), channel_id=1, source_target_pairs={{0,1},{1,0},{2,3},{3,2},{4,5},{5,4},{6,7},{7,6},{8,9},{9,8},{10,11... | collective-permute-start | bytes 786440 | tf_op jit(solution)/shard_map/ppermute | solution.py:42
  72.1 7.5 %collective-permute-start.20 = (bf16[64,1024]{1,0:T(8,128)(2,1)S(1)}, bf16[64,1024]{1,0:T(8,128)(2,1)S(1)}, u32[]{:S(2)}, u32[]{:S(2)}) collective-permute-start(bf16[64,1024]{1,0:T(8,128)(2,1)S(1)} %collective-permute-done.18), channel_id=1, source_target_pairs={{0,4},{2,6},{4,8},{6,10},{8,12},{10,14},{12,0},{14,2},{1,5},{3,7},... | collective-permute-start | bytes 393224 | tf_op jit(solution)/shard_map/ppermute | solution.py:32
  73.0 7.9 %collective-permute-start.21 = (bf16[64,1024]{1,0:T(8,128)(2,1)S(1)}, bf16[64,1024]{1,0:T(8,128)(2,1)S(1)}, u32[]{:S(2)}, u32[]{:S(2)}) collective-permute-start(bf16[64,1024]{1,0:T(8,128)(2,1)S(1)} %collective-permute-done.19), channel_id=1, source_target_pairs={{0,4},{2,6},{4,8},{6,10},{8,12},{10,14},{12,0},{14,2},{1,5},{3,7},... | collective-permute-start | bytes 393224 | tf_op jit(solution)/shard_map/ppermute | solution.py:32
  79.6 5.0 %collective-permute-start.26 = (bf16[64,1024]{1,0:T(8,128)(2,1)S(1)}, bf16[64,1024]{1,0:T(8,128)(2,1)S(1)}, u32[]{:S(2)}, u32[]{:S(2)}) collective-permute-start(bf16[64,1024]{1,0:T(8,128)(2,1)S(1)} %collective-permute-done.18), channel_id=1, source_target_pairs={{0,2},{2,0},{4,6},{6,4},{8,10},{10,8},{12,14},{14,12},{1,3},{3,1},... | collective-permute-start | bytes 393224 | tf_op jit(solution)/shard_map/ppermute | solution.py:38
  81.0 5.0 %collective-permute-start.27 = (bf16[64,1024]{1,0:T(8,128)(2,1)S(1)}, bf16[64,1024]{1,0:T(8,128)(2,1)S(1)}, u32[]{:S(2)}, u32[]{:S(2)}) collective-permute-start(bf16[64,1024]{1,0:T(8,128)(2,1)S(1)} %collective-permute-done.19), channel_id=1, source_target_pairs={{0,2},{2,0},{4,6},{6,4},{8,10},{10,8},{12,14},{14,12},{1,3},{3,1},... | collective-permute-start | bytes 393224 | tf_op jit(solution)/shard_map/ppermute | solution.py:38
  84.5 13.0 %collective-permute-start.35 = (bf16[128,1024]{1,0:T(8,128)(2,1)S(1)}, bf16[128,1024]{1,0:T(8,128)(2,1)S(1)}, u32[]{:S(2)}, u32[]{:S(2)}) collective-permute-start(bf16[128,1024]{1,0:T(8,128)(2,1)S(1)} %constant_dynamic-update-slice_fusion.10), channel_id=1, source_target_pairs={{0,1},{1,0},{2,3},{3,2},{4,5},{5,4},{6,7},{7,6},{8,9},{9,8},{10,11... | collective-permute-start | bytes 786440 | tf_op jit(solution)/shard_map/ppermute | solution.py:42
  85.9 12.5 %collective-permute-start.33 = (bf16[128,1024]{1,0:T(8,128)(2,1)S(1)}, bf16[128,1024]{1,0:T(8,128)(2,1)S(1)}, u32[]{:S(2)}, u32[]{:S(2)}) collective-permute-start(bf16[128,1024]{1,0:T(8,128)(2,1)S(1)} %constant_dynamic-update-slice_fusion.6), channel_id=1, source_target_pairs={{0,1},{1,0},{2,3},{3,2},{4,5},{5,4},{6,7},{7,6},{8,9},{9,8},{10,11... | collective-permute-start | bytes 786440 | tf_op jit(solution)/shard_map/ppermute | solution.py:42
  86.9 6.3 %collective-permute-start.28 = (bf16[64,1024]{1,0:T(8,128)(2,1)S(1)}, bf16[64,1024]{1,0:T(8,128)(2,1)S(1)}, u32[]{:S(2)}, u32[]{:S(2)}) collective-permute-start(bf16[64,1024]{1,0:T(8,128)(2,1)S(1)} %collective-permute-done.20), channel_id=1, source_target_pairs={{0,2},{2,0},{4,6},{6,4},{8,10},{10,8},{12,14},{14,12},{1,3},{3,1},... | collective-permute-start | bytes 393224 | tf_op jit(solution)/shard_map/ppermute | solution.py:38
  88.6 7.1 %collective-permute-start.29 = (bf16[64,1024]{1,0:T(8,128)(2,1)S(1)}, bf16[64,1024]{1,0:T(8,128)(2,1)S(1)}, u32[]{:S(2)}, u32[]{:S(2)}) collective-permute-start(bf16[64,1024]{1,0:T(8,128)(2,1)S(1)} %collective-permute-done.21), channel_id=1, source_target_pairs={{0,2},{2,0},{4,6},{6,4},{8,10},{10,8},{12,14},{14,12},{1,3},{3,1},... | collective-permute-start | bytes 393224 | tf_op jit(solution)/shard_map/ppermute | solution.py:38
  93.2 6.2 %collective-permute-start.36 = (bf16[128,1024]{1,0:T(8,128)(2,1)S(1)}, bf16[128,1024]{1,0:T(8,128)(2,1)S(1)}, u32[]{:S(2)}, u32[]{:S(2)}) collective-permute-start(bf16[128,1024]{1,0:T(8,128)(2,1)S(1)} %constant_dynamic-update-slice_fusion.12), channel_id=1, source_target_pairs={{0,1},{1,0},{2,3},{3,2},{4,5},{5,4},{6,7},{7,6},{8,9},{9,8},{10,11... | collective-permute-start | bytes 786440 | tf_op jit(solution)/shard_map/ppermute | solution.py:42
  96.6 3.7 %collective-permute-start.37 = (bf16[128,1024]{1,0:T(8,128)(2,1)S(1)}, bf16[128,1024]{1,0:T(8,128)(2,1)S(1)}, u32[]{:S(2)}, u32[]{:S(2)}) collective-permute-start(bf16[128,1024]{1,0:T(8,128)(2,1)S(1)} %constant_dynamic-update-slice_fusion.14), channel_id=1, source_target_pairs={{0,1},{1,0},{2,3},{3,2},{4,5},{5,4},{6,7},{7,6},{8,9},{9,8},{10,11... | collective-permute-start | bytes 786440 | tf_op jit(solution)/shard_map/ppermute | solution.py:42
  133.5 3.0 %collective-permute-start.42 = (bf16[128,1024]{1,0:T(8,128)(2,1)}, bf16[128,1024]{1,0:T(8,128)(2,1)S(1)}, u32[]{:S(2)}, u32[]{:S(2)}) collective-permute-start(bf16[128,1024]{1,0:T(8,128)(2,1)} %get-tuple-element.42), channel_id=1, source_target_pairs={{0,1},{1,0},{2,3},{3,2},{4,5},{5,4},{6,7},{7,6},{8,9},{9,8},{10,11... | collective-permute-start | bytes 786440 | tf_op jit(solution)/shard_map/ppermute | solution.py:42
  133.6 26.0 %collective-permute-start.38 = (bf16[128,1024]{1,0:T(8,128)(2,1)}, bf16[128,1024]{1,0:T(8,128)(2,1)S(1)}, u32[]{:S(2)}, u32[]{:S(2)}) collective-permute-start(bf16[128,1024]{1,0:T(8,128)(2,1)} %get-tuple-element.36), channel_id=1, source_target_pairs={{0,1},{1,0},{2,3},{3,2},{4,5},{5,4},{6,7},{7,6},{8,9},{9,8},{10,11... | collective-permute-start | bytes 786440 | tf_op jit(solution)/shard_map/ppermute | solution.py:42
  134.0 8.5 %collective-permute-start.41 = (bf16[128,1024]{1,0:T(8,128)(2,1)}, bf16[128,1024]{1,0:T(8,128)(2,1)S(1)}, u32[]{:S(2)}, u32[]{:S(2)}) collective-permute-start(bf16[128,1024]{1,0:T(8,128)(2,1)} %get-tuple-element.40), channel_id=1, source_target_pairs={{0,1},{1,0},{2,3},{3,2},{4,5},{5,4},{6,7},{7,6},{8,9},{9,8},{10,11... | collective-permute-start | bytes 786440 | tf_op jit(solution)/shard_map/ppermute | solution.py:42
  134.1 14.9 %collective-permute-start.45 = (bf16[128,1024]{1,0:T(8,128)(2,1)}, bf16[128,1024]{1,0:T(8,128)(2,1)S(1)}, u32[]{:S(2)}, u32[]{:S(2)}) collective-permute-start(bf16[128,1024]{1,0:T(8,128)(2,1)} %get-tuple-element.44), channel_id=1, source_target_pairs={{0,1},{1,0},{2,3},{3,2},{4,5},{5,4},{6,7},{7,6},{8,9},{9,8},{10,11... | collective-permute-start | bytes 786440 | tf_op jit(solution)/shard_map/ppermute | solution.py:42
  134.9 3.0 %collective-permute-start.46 = (bf16[128,1024]{1,0:T(8,128)(2,1)}, bf16[128,1024]{1,0:T(8,128)(2,1)S(1)}, u32[]{:S(2)}, u32[]{:S(2)}) collective-permute-start(bf16[128,1024]{1,0:T(8,128)(2,1)} %get-tuple-element.46), channel_id=1, source_target_pairs={{0,1},{1,0},{2,3},{3,2},{4,5},{5,4},{6,7},{7,6},{8,9},{9,8},{10,11... | collective-permute-start | bytes 786440 | tf_op jit(solution)/shard_map/ppermute | solution.py:42
  136.5 3.4 %collective-permute-start.50 = (bf16[128,1024]{1,0:T(8,128)(2,1)}, bf16[128,1024]{1,0:T(8,128)(2,1)S(1)}, u32[]{:S(2)}, u32[]{:S(2)}) collective-permute-start(bf16[128,1024]{1,0:T(8,128)(2,1)} %get-tuple-element.50), channel_id=1, source_target_pairs={{0,1},{1,0},{2,3},{3,2},{4,5},{5,4},{6,7},{7,6},{8,9},{9,8},{10,11... | collective-permute-start | bytes 786440 | tf_op jit(solution)/shard_map/ppermute | solution.py:42
  137.9 9.2 %collective-permute-start.43 = (bf16[128,1024]{1,0:T(8,128)(2,1)S(1)}, bf16[128,1024]{1,0:T(8,128)(2,1)S(1)}, u32[]{:S(2)}, u32[]{:S(2)}) collective-permute-start(bf16[128,1024]{1,0:T(8,128)(2,1)S(1)} %convolution_convert_fusion.2), channel_id=1, source_target_pairs={{0,2},{2,0},{4,6},{6,4},{8,10},{10,8},{12,14},{14,12},{1,3},{3,1},... | collective-permute-start | bytes 786440 | tf_op jit(solution)/shard_map/ppermute | solution.py:38
  140.0 12.8 %collective-permute-start.47 = (bf16[128,1024]{1,0:T(8,128)(2,1)S(1)}, bf16[128,1024]{1,0:T(8,128)(2,1)S(1)}, u32[]{:S(2)}, u32[]{:S(2)}) collective-permute-start(bf16[128,1024]{1,0:T(8,128)(2,1)S(1)} %convolution_convert_fusion.1), channel_id=1, source_target_pairs={{0,2},{2,0},{4,6},{6,4},{8,10},{10,8},{12,14},{14,12},{1,3},{3,1},... | collective-permute-start | bytes 786440 | tf_op jit(solution)/shard_map/ppermute | solution.py:38
  142.5 12.3 %collective-permute-start.49 = (bf16[128,1024]{1,0:T(8,128)(2,1)}, bf16[128,1024]{1,0:T(8,128)(2,1)S(1)}, u32[]{:S(2)}, u32[]{:S(2)}) collective-permute-start(bf16[128,1024]{1,0:T(8,128)(2,1)} %get-tuple-element.48), channel_id=1, source_target_pairs={{0,1},{1,0},{2,3},{3,2},{4,5},{5,4},{6,7},{7,6},{8,9},{9,8},{10,11... | collective-permute-start | bytes 786440 | tf_op jit(solution)/shard_map/ppermute | solution.py:42
  147.1 11.2 %collective-permute-start.51 = (bf16[128,1024]{1,0:T(8,128)(2,1)S(1)}, bf16[128,1024]{1,0:T(8,128)(2,1)S(1)}, u32[]{:S(2)}, u32[]{:S(2)}) collective-permute-start(bf16[128,1024]{1,0:T(8,128)(2,1)S(1)} %convolution_convert_fusion), channel_id=1, source_target_pairs={{0,2},{2,0},{4,6},{6,4},{8,10},{10,8},{12,14},{14,12},{1,3},{3,1},... | collective-permute-start | bytes 786440 | tf_op jit(solution)/shard_map/ppermute | solution.py:38
  149.1 14.3 %collective-permute-start.40 = (bf16[128,1024]{1,0:T(8,128)(2,1)S(1)}, bf16[128,1024]{1,0:T(8,128)(2,1)S(1)}, u32[]{:S(2)}, u32[]{:S(2)}) collective-permute-start(bf16[128,1024]{1,0:T(8,128)(2,1)S(1)} %convolution_convert_fusion.3), channel_id=1, source_target_pairs={{0,2},{2,0},{4,6},{6,4},{8,10},{10,8},{12,14},{14,12},{1,3},{3,1},... | collective-permute-start | bytes 786440 | tf_op jit(solution)/shard_map/ppermute | solution.py:38
  152.7 10.7 %collective-permute-start.44 = (bf16[128,1024]{1,0:T(8,128)(2,1)S(1)}, bf16[128,1024]{1,0:T(8,128)(2,1)S(1)}, u32[]{:S(2)}, u32[]{:S(2)}) collective-permute-start(bf16[128,1024]{1,0:T(8,128)(2,1)S(1)} %fusion.3), channel_id=1, source_target_pairs={{0,12},{2,14},{4,0},{6,2},{8,4},{10,6},{12,8},{14,10},{1,13},{3,15... | collective-permute-start | bytes 786440 | tf_op jit(solution)/shard_map/ppermute | solution.py:32
  154.8 20.0 %collective-permute-start.48 = (bf16[128,1024]{1,0:T(8,128)(2,1)S(1)}, bf16[128,1024]{1,0:T(8,128)(2,1)S(1)}, u32[]{:S(2)}, u32[]{:S(2)}) collective-permute-start(bf16[128,1024]{1,0:T(8,128)(2,1)S(1)} %fusion.4), channel_id=1, source_target_pairs={{0,8},{2,10},{4,12},{6,14},{8,0},{10,2},{12,4},{14,6},{1,9},{3,11}... | collective-permute-start | bytes 786440 | tf_op jit(solution)/shard_map/ppermute | solution.py:32
  159.6 15.2 %collective-permute-start.52 = (bf16[128,1024]{1,0:T(8,128)(2,1)S(1)}, bf16[128,1024]{1,0:T(8,128)(2,1)S(1)}, u32[]{:S(2)}, u32[]{:S(2)}) collective-permute-start(bf16[128,1024]{1,0:T(8,128)(2,1)S(1)} %fusion.5), channel_id=1, source_target_pairs={{0,4},{2,6},{4,8},{6,10},{8,12},{10,14},{12,0},{14,2},{1,5},{3,7},... | collective-permute-start | bytes 786440 | tf_op jit(solution)/shard_map/ppermute | solution.py:32
  (9 other events, 87.2 us)

commit v4 on v3

--- a/solution.py
+++ b/solution.py
@@ -3,6 +3,7 @@
 
 import jax
 import jax.numpy as jnp
+import numpy as np
 from jax import lax
 from jax.experimental import pallas as pl
 from jax.experimental.pallas import tpu as pltpu
@@ -21,49 +22,23 @@
 FEW = 8
 
 
-def grid_of(count):
+def cycle_of(count):
     fast = 2 ** (int(math.log2(count)) // 2)
-    return (count // fast, fast)
-
-
-def shift_slow(value, step, count):
-    slow, fast = grid_of(count)
-    perm = [(i, (i // fast + step) % slow * fast + i % fast) for i in range(count)]
-    return lax.ppermute(value, "ctx", perm)
-
-
-def shift_fast(value, step, count):
-    fast = grid_of(count)[1]
-    perm = [(i, i // fast * fast + (i % fast + step) % fast) for i in range(count)]
-    return lax.ppermute(value, "ctx", perm)
+    slow = count // fast
+    cycle = [0]
+    for i in range(slow):
+        columns = range(1, fast)
+        cycle += [i * fast + j for j in (columns if i % 2 == 0 else reversed(columns))]
+    return cycle + [i * fast for i in reversed(range(1, slow))]
+
+
+def step(value, ahead, count):
+    cycle = cycle_of(count)
+    return lax.ppermute(value, "ctx", [(cycle[p], cycle[(p + ahead) % count]) for p in range(count)])
 
 
 def swap(value):
     return lax.ppermute(value, "exp", SWAP)
-
-
-def each(send, pieces, count):
-    if count <= FEW:
-        return [send(piece) for piece in pieces]
-    return list(send(jnp.stack(list(pieces))))
-
-
-def ring(block, count):
-    line = [block]
-    for _ in range(1, grid_of(count)[0]):
-        line.append(shift_slow(line[-1], 1, count))
-    return line
-
-
-def direct(block, count):
-    return [block] + [shift_slow(block, s, count) for s in range(1, grid_of(count)[0])]
-
-
-def across(line, count):
-    found = list(line)
-    for r in range(1, grid_of(count)[1]):
-        found += each(lambda piece: shift_fast(piece, r, count), line, count)
-    return found
 
 
 def summed(pieces):
@@ -73,38 +48,54 @@
     return total
 
 
-def collect(near, swapped, combine, count):
-    slow, fast = grid_of(count)
-
-    def part(c):
-        rows = (near[c].astype(jnp.float32) + swapped[c].astype(jnp.float32)).astype(jnp.bfloat16)
-        return jnp.dot(combine[c], rows, preferred_element_type=jnp.float32)
-
-    terms = [[] for _ in range(slow)]
-    for r in range(1, fast):
-        parts = [part(r * slow + s).astype(jnp.bfloat16) for s in reversed(range(slow))]
-        arrived = each(lambda piece: shift_fast(piece, -r, count), parts, count)
-        for s, piece in zip(reversed(range(slow)), arrived):
-            terms[s].append(piece)
-    sums = [summed([part(s)] + terms[s]) for s in range(slow)]
-    arrived = [shift_slow(sums[s].astype(jnp.bfloat16), -s, count) for s in range(1, slow)]
-    return summed([sums[0]] + arrived)
-
-
-def owner_of(place, me, count):
-    slow, fast = grid_of(count)
-    r, s = place // slow, place % slow
-    return (me // fast + slow - s) % slow * fast + (me % fast + fast - r) % fast
-
-
-def attend_kernel(count, blocks, where, lengths, order, q_ref, mine_ref, other_ref, up_ref, proj_ref, out_ref, m_ref, l_ref, acc_ref):
-    step = pl.program_id(0)
+def sources_of(me, count):
+    if count > FEW:
+        return jnp.arange(count, dtype=jnp.int32)
+    cycle = cycle_of(count)
+    table = np.zeros((count, count), np.int32)
+    for p in range(count):
+        table[cycle[p]] = [cycle[p - d] for d in range(count)]
+    return lax.dynamic_index_in_dim(jnp.asarray(table), me, keepdims=False)
+
+
+def gather(block, count):
+    if count > FEW:
+        return list(lax.all_gather(block, "ctx"))
+    middle = count // 2
+    found = [None] * count
+    found[0] = block
+    for d in range(1, middle):
+        found[d] = step(found[d - 1], 1, count)
+        found[-d] = step(found[(1 - d) % count], -1, count)
+    half = block.shape[0] // 2
+    ahead, back = step(found[middle - 1][:half], 1, count), step(found[middle + 1][half:], -1, count)
+    found[middle] = jnp.concatenate([ahead, back], axis=0)
+    return found
+
+
+def reduce(parts, count):
+    if count > FEW:
+        return lax.psum_scatter(jnp.stack([part() for part in parts]).astype(jnp.bfloat16), "ctx").astype(jnp.float32)
+    middle = count // 2
+    first = parts[middle]().astype(jnp.bfloat16)
+    half = first.shape[0] // 2
+    zero = jnp.zeros((half, first.shape[1]), jnp.bfloat16)
+    ahead = jnp.concatenate([step(first[:half], 1, count), zero], axis=0)
+    back = jnp.concatenate([zero, step(first[half:], -1, count)], axis=0)
+    for d in range(middle - 1, 0, -1):
+        ahead = step((parts[count - d]() + ahead.astype(jnp.float32)).astype(jnp.bfloat16), 1, count)
+        back = step((parts[d]() + back.astype(jnp.float32)).astype(jnp.bfloat16), -1, count)
+    return parts[0]() + ahead.astype(jnp.float32) + back.astype(jnp.float32)
+
+
+def attend_kernel(blocks, where, sources, lengths, order, q_ref, mine_ref, other_ref, up_ref, proj_ref, out_ref, m_ref, l_ref, acc_ref):
+    chunk = pl.program_id(0)
     me, side = where[0], where[1]
     segs = lengths.shape[0]
     span = mine_ref.shape[1]
     heads, rows, _ = q_ref.shape
 
-    @pl.when(step == 0)
+    @pl.when(chunk == 0)
     def _():
         m_ref[...] = jnp.full_like(m_ref, -1e30)
         l_ref[...] = jnp.zeros_like(l_ref)
@@ -126,7 +117,7 @@
     for half in (side, 1 - side):
         base = jnp.zeros((1, keys), jnp.int32)
         for j in range(blocks):
-            src = owner_of(step * blocks + j, me, count)
+            src = sources[chunk * blocks + j]
             base = jnp.where(which == j, order[2 * src + half] * span, base)
         kpos_parts.append(base + within)
     kpos = jnp.concatenate(kpos_parts, axis=1)
@@ -152,14 +143,14 @@
         )
         acc_ref[h] = acc_ref[h] * shrink + mixed
 
-    @pl.when(step == pl.num_programs(0) - 1)
+    @pl.when(chunk == pl.num_programs(0) - 1)
     def _():
         attended = [(acc_ref[h] / l_ref[h]).astype(jnp.bfloat16) for h in range(heads)]
         out = jnp.dot(jnp.concatenate(attended, axis=1), proj_ref[...], preferred_element_type=jnp.float32)
         out_ref[...] = out.astype(jnp.bfloat16)
 
 
-def attend(where, lengths, order, q, mine, other, kv_up, out_proj, count):
+def attend(where, sources, lengths, order, q, mine, other, kv_up, out_proj, count):
     heads, rows, depth = q.shape
     blocks = math.gcd(count, 8)
     span = mine.shape[1]
@@ -167,9 +158,9 @@
     whole3 = lambda i, *_: (0, 0, 0)
     lat_spec = pl.BlockSpec((blocks, span, WIDE), lambda i, *_: (i, 0, 0))
     return pl.pallas_call(
-        functools.partial(attend_kernel, count, blocks),
+        functools.partial(attend_kernel, blocks),
         grid_spec=pltpu.PrefetchScalarGridSpec(
-            num_scalar_prefetch=3,
+            num_scalar_prefetch=4,
             grid=(count // blocks,),
             in_specs=[
                 pl.BlockSpec(q.shape, whole3),
@@ -188,10 +179,10 @@
         out_shape=jax.ShapeDtypeStruct((rows, out_proj.shape[1]), jnp.bfloat16),
         compiler_params=pltpu.CompilerParams(vmem_limit_bytes=VMEM_LIMIT),
         name="attend",
-    )(where, lengths, order, q, mine, other, kv_up, out_proj)
-
-
-def norm_kernel(where, residual_ref, here_ref, there_ref, gain_ref, middle_ref, upper_ref, lower_ref):
+    )(where, sources, lengths, order, q, mine, other, kv_up, out_proj)
+
+
+def norm_kernel(where, residual_ref, here_ref, there_ref, gain_ref, middle_ref, normed_ref):
     side = where[1]
     half = middle_ref.shape[1]
     total = here_ref[...].astype(jnp.float32) + there_ref[...].astype(jnp.float32)
@@ -200,26 +191,23 @@
     inverse = lax.rsqrt(jnp.mean(wide * wide, axis=1, keepdims=True) + 1e-06)
     normed = wide * inverse * gain_ref[...].astype(jnp.float32)
     middle_ref[...] = jnp.where(side == 0, wide[:, :half], wide[:, half:]).astype(jnp.bfloat16)
-    normed = jnp.where(side == 0, normed[:, :half], normed[:, half:]).astype(jnp.bfloat16)
-    span = upper_ref.shape[0]
-    upper_ref[...] = normed[:span]
-    lower_ref[...] = normed[span:]
+    normed_ref[...] = jnp.where(side == 0, normed[:, :half], normed[:, half:]).astype(jnp.bfloat16)
 
 
 def norm(where, residual, here, there, gain):
     rows, width = residual.shape
-    half = lambda size: jax.ShapeDtypeStruct((size, width // 2), jnp.bfloat16)
+    half = jax.ShapeDtypeStruct((rows, width // 2), jnp.bfloat16)
     full = pl.BlockSpec((rows, width), lambda i, *_: (0, 0))
-    part = lambda size: pl.BlockSpec((size, width // 2), lambda i, *_: (0, 0))
+    part = pl.BlockSpec((rows, width // 2), lambda i, *_: (0, 0))
     return pl.pallas_call(
         norm_kernel,
         grid_spec=pltpu.PrefetchScalarGridSpec(
             num_scalar_prefetch=1,
             grid=(1,),
             in_specs=[full, full, full, pl.BlockSpec((1, width), lambda i, *_: (0, 0))],
-            out_specs=[part(rows), part(rows // 2), part(rows // 2)],
+            out_specs=[part, part],
         ),
-        out_shape=[half(rows), half(rows // 2), half(rows // 2)],
+        out_shape=[half, half],
         compiler_params=pltpu.CompilerParams(vmem_limit_bytes=VMEM_LIMIT),
         name="norm",
     )(where, residual, here, there, gain.reshape(1, width))
@@ -267,10 +255,11 @@
 
 def expert_rows(rows, gate_ref, up_ref, down_ref, scale_ref):
     by_columns = (((1,), (1,)), ((), ()))
-    gate = lax.dot_general(rows, gate_ref[0], by_columns, preferred_element_type=jnp.float32)
-    upper = lax.dot_general(rows, up_ref[0], by_columns, preferred_element_type=jnp.float32)
+    gate = lax.dot_general(gate_ref[0], rows, by_columns, preferred_element_type=jnp.float32)
+    upper = lax.dot_general(up_ref[0], rows, by_columns, preferred_element_type=jnp.float32)
     hidden = (gate / (1.0 + jnp.exp(-gate)) * upper * scale_ref[0]).astype(jnp.bfloat16)
-    return jnp.dot(hidden, down_ref[0], preferred_element_type=jnp.float32).astype(jnp.bfloat16)
+    by_rows = (((0,), (0,)), ((), ()))
+    return lax.dot_general(hidden, down_ref[0], by_rows, preferred_element_type=jnp.float32).astype(jnp.bfloat16)
 
 
 def plain_kernel(where, rows_ref, gate_ref, up_ref, down_ref, scale_ref, out_ref):
@@ -279,27 +268,41 @@
 
 def fused_kernel(count, where, *refs):
     mine, other = refs[:count], refs[count : 2 * count]
-    gate_ref, up_ref, down_ref, scale_ref = refs[2 * count : 2 * count + 4]
-    kept, away = refs[2 * count + 4 : 3 * count + 4], refs[3 * count + 4 : 4 * count + 4]
-    rows, result = refs[4 * count + 4 :]
-    half = mine[0].shape[1]
+    pick_ref, combine_ref, gate_ref, up_ref, down_ref, scale_ref = refs[2 * count : 2 * count + 6]
+    kept, away = refs[2 * count + 6 : 3 * count + 6], refs[3 * count + 6 : 4 * count + 6]
+    picked, held = refs[4 * count + 6 :]
+    expert = pl.program_id(0)
+    here = picked.shape[0]
+    half = picked.shape[2] // 2
     side = where[1]
     near = pl.ds(pl.multiple_of(side * half, half), half)
     far = pl.ds(pl.multiple_of((1 - side) * half, half), half)
-    place = pl.ds(pl.multiple_of(pl.program_id(0) * SLOTS, SLOTS), SLOTS)
+
+    @pl.when(expert == 0)
+    def _():
+        for c in range(count):
+            for columns, block in ((near, mine[c]), (far, other[c])):
+                rows = jnp.dot(pick_ref[c], block[...], preferred_element_type=jnp.float32).astype(jnp.bfloat16)
+                for e in range(here):
+                    picked[e, c * SLOTS : (c + 1) * SLOTS, columns] = rows[e * SLOTS : (e + 1) * SLOTS]
+
+    result = expert_rows(picked[expert], gate_ref, up_ref, down_ref, scale_ref)
+    place = pl.ds(pl.multiple_of(expert * SLOTS, SLOTS), SLOTS)
     for c in range(count):
-        rows[c * SLOTS : (c + 1) * SLOTS, near] = mine[c][place, :]
-        rows[c * SLOTS : (c + 1) * SLOTS, far] = other[c][place, :]
-    result[...] = expert_rows(rows[...], gate_ref, up_ref, down_ref, scale_ref)
-    for c in range(count):
-        kept[c][place, :] = result[c * SLOTS : (c + 1) * SLOTS, near]
-        away[c][place, :] = result[c * SLOTS : (c + 1) * SLOTS, far]
+        held[c, place, :] = result[c * SLOTS : (c + 1) * SLOTS]
+
+    @pl.when(expert == here - 1)
+    def _():
+        for c in range(count):
+            for columns, out in ((far, away[c]), (near, kept[c])):
+                total = jnp.dot(combine_ref[c], held[c, :, columns], preferred_element_type=jnp.float32)
+                out[...] = total.astype(jnp.bfloat16)
 
 
 def expert_specs(w_gate, rows):
     hidden, width = w_gate.shape[1:]
     weight = pl.BlockSpec((1, hidden, width), lambda e, where: (e, 0, 0))
-    return [weight, weight, weight, pl.BlockSpec((1, rows, 1), lambda e, where: (e, 0, 0))]
+    return [weight, weight, weight, pl.BlockSpec((1, 1, rows), lambda e, where: (e, 0, 0))]
 
 
 def experts_plain(where, picked, w_gate, w_up, w_down, scale):
@@ -319,23 +322,28 @@
     )(where, picked, w_gate, w_up, w_down, scale)
 
 
-def experts_fused(where, mine, other, w_gate, w_up, w_down, scale):
-    count, (slots, half) = len(mine), mine[0].shape
-    here, rows, _ = scale.shape
-    whole = pl.BlockSpec((slots, half), lambda e, where: (0, 0))
+def experts_fused(where, mine, other, pick, combine, w_gate, w_up, w_down, scale):
+    count, (local, half) = len(mine), mine[0].shape
+    here, _, rows = scale.shape
+    whole = pl.BlockSpec((local, half), lambda e, where: (0, 0))
     outs = pl.pallas_call(
         functools.partial(fused_kernel, count),
         grid_spec=pltpu.PrefetchScalarGridSpec(
             num_scalar_prefetch=1,
             grid=(here,),
-            in_specs=[whole] * (2 * count) + expert_specs(w_gate, rows),
+            in_specs=[whole] * (2 * count)
+            + [pl.BlockSpec(pick.shape, lambda e, where: (0, 0, 0)), pl.BlockSpec(combine.shape, lambda e, where: (0, 0, 0))]
+            + expert_specs(w_gate, rows),
             out_specs=[whole] * (2 * count),
-            scratch_shapes=[pltpu.VMEM((rows, 2 * half), jnp.bfloat16)] * 2,
+            scratch_shapes=[
+                pltpu.VMEM((here, rows, 2 * half), jnp.bfloat16),
+                pltpu.VMEM((count, here * SLOTS, 2 * half), jnp.bfloat16),
+            ],
         ),
-        out_shape=[jax.ShapeDtypeStruct((slots, half), jnp.bfloat16)] * (2 * count),
+        out_shape=[jax.ShapeDtypeStruct((local, half), jnp.bfloat16)] * (2 * count),
         compiler_params=pltpu.CompilerParams(vmem_limit_bytes=VMEM_LIMIT),
         name="experts",
-    )(where, *mine, *other, w_gate, w_up, w_down, scale)
+    )(where, *mine, *other, pick, combine, w_gate, w_up, w_down, scale)
     return outs[:count], outs[count:]
 
 
@@ -363,13 +371,15 @@
     where = jnp.stack([me, side]).astype(jnp.int32)
 
     base = latent.shape[1]
-    found = across(direct(pack(where, latent, expert_ids, route_weights), count), count)
+    sources = sources_of(me, count)
+    found = gather(pack(where, latent, expert_ids, route_weights), count)
+    swap_all = lambda pieces: [swap(piece) for piece in pieces] if count <= FEW else list(swap(jnp.stack(pieces)))
     mine = jnp.stack(found)
-    other = jnp.stack(each(swap, found, count))
+    other = jnp.stack(swap_all(found))
 
     q = queries.reshape(local_rows, heads, NOPE + ROPE).transpose(1, 0, 2)
-    partial = attend(where, seg_lengths, span_order, q, mine, other, kv_up, out_proj, count)
-    middle, upper, lower = norm(where, residual, partial, swap(partial), norm_gain)
+    partial = attend(where, sources, seg_lengths, span_order, q, mine, other, kv_up, out_proj, count)
+    middle, normed = norm(where, residual, partial, swap(partial), norm_gain)
 
     facts_mine, facts_other = mine[:, :, base : base + 3 * TOP], other[:, :, base : base + 3 * TOP]
     facts = jnp.concatenate(
@@ -387,21 +397,16 @@
     slot = jnp.arange(SLOTS, dtype=jnp.int32).astype(jnp.float32)
     combine = rank[:, :, :, None] == slot
     scale = jnp.sum(jnp.where(combine, share[:, :, :, None], 0.0), axis=1)
-    scale = scale.transpose(1, 0, 2).reshape(here, count * SLOTS, 1)
+    scale = scale.transpose(1, 0, 2).reshape(here, 1, count * SLOTS)
     combine = combine.astype(jnp.bfloat16).reshape(count, local_rows, here * SLOTS)
     pick = combine.transpose(0, 2, 1)
 
-    lines = [ring(upper, count), ring(lower, count)]
-    lines[0][1], pick, combine, scale = lax.optimization_barrier((lines[0][1], pick, combine, scale))
-    halves = [across(line, count) for line in lines]
-    got = [jnp.concatenate(pair, axis=0) for pair in zip(*halves)]
-    got_other = each(swap, got, count)
+    got = gather(normed, count)
+    got[1], pick, combine, scale = lax.optimization_barrier((got[1], pick, combine, scale))
+    got_other = swap_all(got)
     w_gate, w_up = w_gate.transpose(0, 2, 1), w_up.transpose(0, 2, 1)
     if count <= FEW:
-        choose = lambda c, rows: jnp.dot(pick[c], rows, preferred_element_type=jnp.float32).astype(jnp.bfloat16)
-        mine = [choose(c, got[c]) for c in range(count)]
-        other = [choose(c, got_other[c]) for c in range(count)]
-        kept, away = experts_fused(where, mine, other, w_gate, w_up, w_down, scale)
+        kept, away = experts_fused(where, got, got_other, pick, combine, w_gate, w_up, w_down, scale)
     else:
         near, far = jnp.stack(got), jnp.stack(got_other)
         full = jnp.concatenate([jnp.where(side == 0, near, far), jnp.where(side == 0, far, near)], axis=2)
@@ -409,10 +414,13 @@
         picked = picked.reshape(count, here, SLOTS, width).transpose(1, 0, 2, 3).reshape(here, count * SLOTS, width)
         result = experts_plain(where, picked, w_gate, w_up, w_down, scale)
         result = result.reshape(here, count, SLOTS, width).transpose(1, 0, 2, 3).reshape(count, here * SLOTS, width)
-        left, right = jnp.split(result, 2, axis=2)
+        total = jnp.einsum("cts,csd->ctd", combine, result, preferred_element_type=jnp.float32).astype(jnp.bfloat16)
+        left, right = jnp.split(total, 2, axis=2)
         kept, away = jnp.where(side == 0, left, right), jnp.where(side == 0, right, left)
-    mixture = collect(kept, each(swap, away, count), combine, count)
-    return (middle.astype(jnp.float32) + mixture).astype(jnp.bfloat16)
+    order = [(count // 2 + (d + 1) // 2 * (1 - d % 2 * 2)) % count for d in range(count)]
+    swapped = dict(zip(order, swap_all([away[c] for c in order])))
+    parts = [functools.partial(summed, [kept[c], swapped[c]]) for c in range(count)]
+    return (middle.astype(jnp.float32) + reduce(parts, count)).astype(jnp.bfloat16)
 
 
 def solution(mesh):

time: 177 us -> 152 us (0.86)
  matrix products: 25.4 us -> 0.14 us
  waiting for transfers between devices: 67.1 us -> 50.7 us
  other arithmetic: 1.44 us -> 12.4 us
  starting transfers between devices: 28.3 us -> 30.9 us
  Pallas kernels: 45.2 us -> 47 us
    dot_general x24 -> x0, matrix products: 25.2 us -> none  [the longest x16 14.8 us: body(): jnp.dot(pick[c], rows, preferred_element_type=jnp.float32)]
    ppermute x28 -> x24, waiting for transfers between devices: 64.4 us -> 47.8 us  [step(): lax.ppermute(value, 'ctx', [(cycle[p], cycle[(p + ahead) % count]) for p...]
    convert_element_type x0 -> x8, other arithmetic: none -> 9.25 us  [the longest x3 3.18 us: reduce(): (parts[d]() + back.astype(jnp.float32)).astype(jnp.bfloat16)]
    pallas_call x1, Pallas kernels: 31.7 us -> 33.6 us  [experts_fused(): pl.pallas_call(functools.partial(fused_kernel, count), grid_spec=pltpu.Pr...]
    ppermute x28 -> x24, starting transfers between devices: 24.5 us -> 25.6 us  [step(): lax.ppermute(value, 'ctx', [(cycle[p], cycle[(p + ahead) % count]) for p...]
    unnamed x31 -> x49, local copies, waits for them, and re-layouts: 4.22 us -> 3.93 us
  transfers between devices with their start and end apart: 53 -> 49, of which waited for: 21 -> 21; matrix products, arithmetic and copies ran while one was open for 17% -> 12% of each run, Pallas kernels for 0% -> 0%
where the time goes in v4:
time: 152 us; the launch traced here: 151 us
  waiting for transfers between devices  50.7 us (33%)
  Pallas kernels  47 us (31%)
  starting transfers between devices  30.9 us (20%)
  other arithmetic  12.4 us (8%)
  local copies, waits for them, and re-layouts  9.51 us (6%)
    ppermute x24, waiting for transfers between devices, step(): lax.ppermute(value, 'ctx', [(cycle[p], cycle[(p + ahead) % count]) for p...  47.8 us
    pallas_call x1, Pallas kernels, experts_fused(): pl.pallas_call(functools.partial(fused_kernel, count), grid_spec=pltpu.Pr...  33.6 us
    ppermute x24, starting transfers between devices, step(): lax.ppermute(value, 'ctx', [(cycle[p], cycle[(p + ahead) % count]) for p...  25.6 us
    pallas_call x1, Pallas kernels, attend(): pl.pallas_call(functools.partial(attend_kernel, blocks), grid_spec=pltpu....  7.89 us
    ppermute x25, starting transfers between devices, swap(): return lax.ppermute(value, 'exp', SWAP)  5.32 us
    unnamed x49, local copies, waits for them, and re-layouts  3.93 us
    convert_element_type x3, other arithmetic, reduce(): (parts[d]() + back.astype(jnp.float32)).astype(jnp.bfloat16)  3.18 us
    convert_element_type x3, other arithmetic, reduce(): (parts[count - d]() + ahead.astype(jnp.float32)).astype(jnp.bfloat16)  3.18 us
  transfers between devices with their start and end apart: 49, of which 21 were waited for; matrix products, arithmetic and copies ran while one was open for 12% of the time, Pallas kernels for 0%

profile of v4, /device:TPU:0, one launch (start us, length us, event | category | flops | bytes accessed | tf_op | source)
XLA Modules:
  0.0 151.1 jit_solution(11831227131550003143)
XLA Ops:
  0.6 2.4 %pack.1 = bf16[64,640]{1,0:T(8,128)(2,1)} custom-call(s32[2]{0:T(128)} %pad_add_fusion.where, bf16[576,128]{1,0:T(8,128)(2,1)} %bitcast.60, s32[6,128]{1,0:T(8,128)} %bitcast.62, f32[6,128]{1,0:T(8,128)} %bitcast.63), custom_call_target="tpu_custom_call" | custom-call | tf_op jit(solution)/shard_map/pack/pallas_call | solution.py:237
  3.5 2.6 %collective-permute-start.4 = (bf16[64,640]{1,0:T(8,128)(2,1)}, bf16[64,640]{1,0:T(8,128)(2,1)S(1)}, u32[]{:S(2)}, u32[]{:S(2)}) collective-permute-start(bf16[64,640]{1,0:T(8,128)(2,1)} %pack.1), channel_id=1, source_target_pairs={{0,4},{2,0},{6,2},{10,6},{14,10},{12,14},{8,12},{4,8},{1,5},{3,1},... | collective-permute-start | bytes 245768 | tf_op jit(solution)/shard_map/ppermute | solution.py:37
  6.1 1.0 bitcast_dynamic-update-slice_fusion.15
  7.0 1.1 copy.30
  8.1 0.9 copy.31
  9.0 1.2 dynamic-slice_bitcast_fusion.sources
  10.4 1.8 %collective-permute-start.5 = (bf16[64,640]{1,0:T(8,128)(2,1)S(1)}, bf16[64,640]{1,0:T(8,128)(2,1)S(1)}, u32[]{:S(2)}, u32[]{:S(2)}) collective-permute-start(bf16[64,640]{1,0:T(8,128)(2,1)S(1)} %collective-permute-done.4), channel_id=1, source_target_pairs={{0,4},{2,0},{6,2},{10,6},{14,10},{12,14},{8,12},{4,8},{1,5},{3,1},... | collective-permute-start | bytes 245768 | tf_op jit(solution)/shard_map/ppermute | solution.py:37
  12.6 2.6 %collective-permute-done.5 = bf16[64,640]{1,0:T(8,128)(2,1)S(1)} collective-permute-done((bf16[64,640]{1,0:T(8,128)(2,1)S(1)}, bf16[64,640]{1,0:T(8,128)(2,1)S(1)}, u32[]{:S(2)}, u32[]{:S(2)}) %collective-permute-start.5) | collective-permute-done | bytes 81952 | tf_op jit(solution)/shard_map/ppermute | solution.py:37
  15.2 1.8 %collective-permute-start.6 = (bf16[64,640]{1,0:T(8,128)(2,1)S(1)}, bf16[64,640]{1,0:T(8,128)(2,1)S(1)}, u32[]{:S(2)}, u32[]{:S(2)}) collective-permute-start(bf16[64,640]{1,0:T(8,128)(2,1)S(1)} %collective-permute-done.5), channel_id=1, source_target_pairs={{0,4},{2,0},{6,2},{10,6},{14,10},{12,14},{8,12},{4,8},{1,5},{3,1},... | collective-permute-start | bytes 245768 | tf_op jit(solution)/shard_map/ppermute | solution.py:37
  17.5 2.5 %collective-permute-done.6 = bf16[64,640]{1,0:T(8,128)(2,1)S(1)} collective-permute-done((bf16[64,640]{1,0:T(8,128)(2,1)S(1)}, bf16[64,640]{1,0:T(8,128)(2,1)S(1)}, u32[]{:S(2)}, u32[]{:S(2)}) %collective-permute-start.6) | collective-permute-done | bytes 81952 | tf_op jit(solution)/shard_map/ppermute | solution.py:37
  20.1 1.8 %collective-permute-start.7 = (bf16[32,640]{1,0:T(8,128)(2,1)S(1)}, bf16[32,640]{1,0:T(8,128)(2,1)S(1)}, u32[]{:S(2)}, u32[]{:S(2)}) collective-permute-start(bf16[32,640]{1,0:T(8,128)(2,1)S(1)} %slice.45), channel_id=1, source_target_pairs={{0,4},{2,0},{6,2},{10,6},{14,10},{12,14},{8,12},{4,8},{1,5},{3,1},... | collective-permute-start | bytes 122888 | tf_op jit(solution)/shard_map/ppermute | solution.py:37
  22.4 3.6 %collective-permute-done.3 = bf16[32,640]{1,0:T(8,128)(2,1)S(1)} collective-permute-done((bf16[32,640]{1,0:T(8,128)(2,1)S(1)}, bf16[32,640]{1,0:T(8,128)(2,1)S(1)}, u32[]{:S(2)}, u32[]{:S(2)}) %collective-permute-start.3) | collective-permute-done | bytes 40992 | tf_op jit(solution)/shard_map/ppermute | solution.py:37
  27.6 0.8 copy-done.1
  28.4 7.9 %attend.1.here_ref = bf16[128,2048]{1,0:T(8,128)(2,1)} custom-call(s32[2]{0:T(128)} %pad_add_fusion.where, s32[8]{0:T(128)} %dynamic-slice_bitcast_fusion.sources, s32[16]{0:T(128)} %lengths.1, s32[16]{0:T(128)} %order.1, bf16[4,128,192]{2,1,0:T(8,128)(2,1)} %bitcast.58, bf16[8,64,640]{2,1,0:T(8,128)(2,1)} %copy-done, bf16[8,64,640]{2,1,0:T(8,128)(2,1)} %copy-done.1, ...), custom_call_target="tpu_custom_call" | custom-call | tf_op jit(solution)/shard_map/attend/pallas_call | solution.py:160
  36.7 1.3 reshape.26.gain_ref
  38.0 1.1 broadcast_select_fusion.1
  40.4 3.1 %norm.1 = (bf16[128,1024]{1,0:T(8,128)(2,1)}, bf16[128,1024]{1,0:T(8,128)(2,1)}) custom-call(s32[2]{0:T(128)} %pad_add_fusion.where, bf16[128,2048]{1,0:T(8,128)(2,1)} %residual_ref.1, bf16[128,2048]{1,0:T(8,128)(2,1)} %attend.1.here_ref, bf16[128,2048]{1,0:T(8,128)(2,1)} %copy-done.5, bf16[1,2048]{1,0:T(2,128)(2,1)} %reshape.26.gain_ref), custom_call_target="tpu_custom_call" | custom-call | tf_op jit(solution)/shard_map/norm/pallas_call | solution.py:202
  43.5 1.6 %collective-permute-start.21 = (bf16[128,1024]{1,0:T(8,128)(2,1)}, bf16[128,1024]{1,0:T(8,128)(2,1)S(1)}, u32[]{:S(2)}, u32[]{:S(2)}) collective-permute-start(bf16[128,1024]{1,0:T(8,128)(2,1)} %get-tuple-element.28.refs_0_), channel_id=1, source_target_pairs={{0,4},{2,0},{6,2},{10,6},{14,10},{12,14},{8,12},{4,8},{1,5},{3,1},... | collective-permute-start | bytes 786440 | tf_op jit(solution)/shard_map/ppermute | solution.py:37
  45.7 6.4 %collective-permute-done.21.refs_7_ = bf16[128,1024]{1,0:T(8,128)(2,1)S(1)} collective-permute-done((bf16[128,1024]{1,0:T(8,128)(2,1)}, bf16[128,1024]{1,0:T(8,128)(2,1)S(1)}, u32[]{:S(2)}, u32[]{:S(2)}) %collective-permute-start.21) | collective-permute-done | bytes 262176 | tf_op jit(solution)/shard_map/ppermute | solution.py:37
  52.1 1.6 %collective-permute-start.22 = (bf16[128,1024]{1,0:T(8,128)(2,1)S(1)}, bf16[128,1024]{1,0:T(8,128)(2,1)S(1)}, u32[]{:S(2)}, u32[]{:S(2)}) collective-permute-start(bf16[128,1024]{1,0:T(8,128)(2,1)S(1)} %collective-permute-done.21.refs_7_), channel_id=1, source_target_pairs={{0,4},{2,0},{6,2},{10,6},{14,10},{12,14},{8,12},{4,8},{1,5},{3,1},... | collective-permute-start | bytes 786440 | tf_op jit(solution)/shard_map/ppermute | solution.py:37
  54.6 5.0 %collective-permute-done.22.refs_6_ = bf16[128,1024]{1,0:T(8,128)(2,1)S(1)} collective-permute-done((bf16[128,1024]{1,0:T(8,128)(2,1)S(1)}, bf16[128,1024]{1,0:T(8,128)(2,1)S(1)}, u32[]{:S(2)}, u32[]{:S(2)}) %collective-permute-start.22) | collective-permute-done | bytes 262176 | tf_op jit(solution)/shard_map/ppermute | solution.py:37
  59.6 1.6 %collective-permute-start.23 = (bf16[128,1024]{1,0:T(8,128)(2,1)S(1)}, bf16[128,1024]{1,0:T(8,128)(2,1)S(1)}, u32[]{:S(2)}, u32[]{:S(2)}) collective-permute-start(bf16[128,1024]{1,0:T(8,128)(2,1)S(1)} %collective-permute-done.22.refs_6_), channel_id=1, source_target_pairs={{0,4},{2,0},{6,2},{10,6},{14,10},{12,14},{8,12},{4,8},{1,5},{3,1},... | collective-permute-start | bytes 786440 | tf_op jit(solution)/shard_map/ppermute | solution.py:37
  62.5 5.1 %collective-permute-done.19.refs_3_ = bf16[128,1024]{1,0:T(8,128)(2,1)S(1)} collective-permute-done((bf16[128,1024]{1,0:T(8,128)(2,1)S(1)}, bf16[128,1024]{1,0:T(8,128)(2,1)S(1)}, u32[]{:S(2)}, u32[]{:S(2)}) %collective-permute-start.19) | collective-permute-done | bytes 262176 | tf_op jit(solution)/shard_map/ppermute | solution.py:37
  69.6 1.8 %collective-permute-start.24 = (bf16[64,1024]{1,0:T(8,128)(2,1)S(1)}, bf16[64,1024]{1,0:T(8,128)(2,1)S(1)}, u32[]{:S(2)}, u32[]{:S(2)}) collective-permute-start(bf16[64,1024]{1,0:T(8,128)(2,1)S(1)} %slice.52), channel_id=1, source_target_pairs={{0,4},{2,0},{6,2},{10,6},{14,10},{12,14},{8,12},{4,8},{1,5},{3,1},... | collective-permute-start | bytes 393224 | tf_op jit(solution)/shard_map/ppermute | solution.py:37
  71.4 1.2 collective-permute-done.20
  72.6 3.1 %collective-permute-done.24 = bf16[64,1024]{1,0:T(8,128)(2,1)S(1)} collective-permute-done((bf16[64,1024]{1,0:T(8,128)(2,1)S(1)}, bf16[64,1024]{1,0:T(8,128)(2,1)S(1)}, u32[]{:S(2)}, u32[]{:S(2)}) %collective-permute-start.24) | collective-permute-done | bytes 131104 | tf_op jit(solution)/shard_map/ppermute | solution.py:37
  76.9 0.9 copy.38.refs_16_
  78.7 33.6 %experts.1 = (bf16[128,1024]{1,0:T(8,128)(2,1)}, bf16[128,1024]{1,0:T(8,128)(2,1)}, bf16[128,1024]{1,0:T(8,128)(2,1)}, bf16[128,1024]{1,0:T(8,128)(2,1)}, bf16[1...) custom-call(s32[2]{0:T(128)} %pad_add_fusion.where, ...), custom_call_target="tpu_custom_call" | custom-call | tf_op jit(solution)/shard_map/experts/pallas_call | solution.py:329
  112.8 1.2 collective-permute-done.37
  114.1 1.0 add_convert_fusion.7
  116.0 1.7 %collective-permute-start.45 = (bf16[64,1024]{1,0:T(8,128)(2,1)S(1)}, bf16[64,1024]{1,0:T(8,128)(2,1)S(1)}, u32[]{:S(2)}, u32[]{:S(2)}) collective-permute-start(bf16[64,1024]{1,0:T(8,128)(2,1)S(1)} %get-tuple-element.52), channel_id=1, source_target_pairs={{0,4},{2,0},{6,2},{10,6},{14,10},{12,14},{8,12},{4,8},{1,5},{3,1},... | collective-permute-start | bytes 393224 | tf_op jit(solution)/shard_map/ppermute | solution.py:37
  117.7 3.1 %collective-permute-done.38 = bf16[64,1024]{1,0:T(8,128)(2,1)S(1)} collective-permute-done((bf16[64,1024]{1,0:T(8,128)(2,1)S(1)}, bf16[64,1024]{1,0:T(8,128)(2,1)S(1)}, u32[]{:S(2)}, u32[]{:S(2)}) %collective-permute-start.38) | collective-permute-done | bytes 131104 | tf_op jit(solution)/shard_map/ppermute | solution.py:37
  120.8 1.0 add_convert_fusion.6
  122.2 1.0 add_convert_fusion.3
  123.3 1.8 %collective-permute-start.46 = (bf16[128,1024]{1,0:T(8,128)(2,1)S(1)}, bf16[128,1024]{1,0:T(8,128)(2,1)S(1)}, u32[]{:S(2)}, u32[]{:S(2)}) collective-permute-start(bf16[128,1024]{1,0:T(8,128)(2,1)S(1)} %add_convert_fusion.3), channel_id=1, source_target_pairs={{0,4},{2,0},{6,2},{10,6},{14,10},{12,14},{8,12},{4,8},{1,5},{3,1},... | collective-permute-start | bytes 786440 | tf_op jit(solution)/shard_map/ppermute | solution.py:37
  125.6 4.0 %collective-permute-done.39 = bf16[128,1024]{1,0:T(8,128)(2,1)S(1)} collective-permute-done((bf16[128,1024]{1,0:T(8,128)(2,1)S(1)}, bf16[128,1024]{1,0:T(8,128)(2,1)S(1)}, u32[]{:S(2)}, u32[]{:S(2)}) %collective-permute-start.39) | collective-permute-done | bytes 262176 | tf_op jit(solution)/shard_map/ppermute | solution.py:37
  129.5 1.1 add_convert_fusion.5
  131.0 1.1 collective-permute-done.46
  132.0 1.1 add_convert_fusion.2
  133.1 1.8 %collective-permute-start.47 = (bf16[128,1024]{1,0:T(8,128)(2,1)S(1)}, bf16[128,1024]{1,0:T(8,128)(2,1)S(1)}, u32[]{:S(2)}, u32[]{:S(2)}) collective-permute-start(bf16[128,1024]{1,0:T(8,128)(2,1)S(1)} %add_convert_fusion.2), channel_id=1, source_target_pairs={{0,4},{2,0},{6,2},{10,6},{14,10},{12,14},{8,12},{4,8},{1,5},{3,1},... | collective-permute-start | bytes 786440 | tf_op jit(solution)/shard_map/ppermute | solution.py:37
  134.9 2.5 %collective-permute-done.40 = bf16[128,1024]{1,0:T(8,128)(2,1)S(1)} collective-permute-done((bf16[128,1024]{1,0:T(8,128)(2,1)S(1)}, bf16[128,1024]{1,0:T(8,128)(2,1)S(1)}, u32[]{:S(2)}, u32[]{:S(2)}) %collective-permute-start.40) | collective-permute-done | bytes 262176 | tf_op jit(solution)/shard_map/ppermute | solution.py:37
  137.4 1.1 add_convert_fusion.4
  138.8 2.3 %collective-permute-done.47 = bf16[128,1024]{1,0:T(8,128)(2,1)S(1)} collective-permute-done((bf16[128,1024]{1,0:T(8,128)(2,1)S(1)}, bf16[128,1024]{1,0:T(8,128)(2,1)S(1)}, u32[]{:S(2)}, u32[]{:S(2)}) %collective-permute-start.47) | collective-permute-done | bytes 262176 | tf_op jit(solution)/shard_map/ppermute | solution.py:37
  141.1 1.1 add_convert_fusion.1
  142.2 1.8 %collective-permute-start.48 = (bf16[128,1024]{1,0:T(8,128)(2,1)S(1)}, bf16[128,1024]{1,0:T(8,128)(2,1)S(1)}, u32[]{:S(2)}, u32[]{:S(2)}) collective-permute-start(bf16[128,1024]{1,0:T(8,128)(2,1)S(1)} %add_convert_fusion.1), channel_id=1, source_target_pairs={{0,4},{2,0},{6,2},{10,6},{14,10},{12,14},{8,12},{4,8},{1,5},{3,1},... | collective-permute-start | bytes 786440 | tf_op jit(solution)/shard_map/ppermute | solution.py:37
  144.0 0.9 collective-permute-done.41
  144.9 4.4 %collective-permute-done.48 = bf16[128,1024]{1,0:T(8,128)(2,1)S(1)} collective-permute-done((bf16[128,1024]{1,0:T(8,128)(2,1)S(1)}, bf16[128,1024]{1,0:T(8,128)(2,1)S(1)}, u32[]{:S(2)}, u32[]{:S(2)}) %collective-permute-start.48) | collective-permute-done | bytes 262176 | tf_op jit(solution)/shard_map/ppermute | solution.py:37
  149.3 1.9 %add_convert_fusion = bf16[128,1024]{1,0:T(8,128)(2,1)} fusion(bf16[128,1024]{1,0:T(8,128)(2,1)S(1)} %collective-permute-done.48, bf16[128,1024]{1,0:T(8,128)(2,1)S(1)} %collective-permute-done.41, bf16[128,1024]{1,0:T(8,128)(2,1)S(1)} %collective-permute-done.33, bf16[128,1024]{1,0:T(8,128)(2,1)} %get-tuple-element.33, bf16[128,1024]{1,0:T(8,128)(2,1)S(1)} %copy-done.15), kind=kLoop, calls=%fused_computation.2 | loop fusion | flops 1310720 | bytes 1572864 | tf_op jit(solution)/shard_map/convert_element_type | solution.py:423
  (146 shorter events, 15.7 us)
Async XLA Ops:
  3.0 9.6 %collective-permute-start.8 = (bf16[64,640]{1,0:T(8,128)(2,1)}, bf16[64,640]{1,0:T(8,128)(2,1)S(1)}, u32[]{:S(2)}, u32[]{:S(2)}) collective-permute-start(bf16[64,640]{1,0:T(8,128)(2,1)} %pack.1), channel_id=1, source_target_pairs={{0,1},{1,0},{2,3},{3,2},{4,5},{5,4},{6,7},{7,6},{8,9},{9,8},{10,11... | collective-permute-start | bytes 245768 | tf_op jit(solution)/shard_map/ppermute | solution.py:41
  3.5 6.7 %collective-permute-start.4 = (bf16[64,640]{1,0:T(8,128)(2,1)}, bf16[64,640]{1,0:T(8,128)(2,1)S(1)}, u32[]{:S(2)}, u32[]{:S(2)}) collective-permute-start(bf16[64,640]{1,0:T(8,128)(2,1)} %pack.1), channel_id=1, source_target_pairs={{0,4},{2,0},{6,2},{10,6},{14,10},{12,14},{8,12},{4,8},{1,5},{3,1},... | collective-permute-start | bytes 245768 | tf_op jit(solution)/shard_map/ppermute | solution.py:37
  6.1 6.1 %collective-permute-start = (bf16[64,640]{1,0:T(8,128)(2,1)}, bf16[64,640]{1,0:T(8,128)(2,1)S(1)}, u32[]{:S(2)}, u32[]{:S(2)}) collective-permute-start(bf16[64,640]{1,0:T(8,128)(2,1)} %pack.1), channel_id=1, source_target_pairs={{0,2},{2,6},{6,10},{10,14},{14,12},{12,8},{8,4},{4,0},{1,3},{3,7},... | collective-permute-start | bytes 245768 | tf_op jit(solution)/shard_map/ppermute | solution.py:37
  10.1 17.4 %collective-permute-start.15 = (bf16[64,640]{1,0:T(8,128)(2,1)S(1)}, bf16[64,640]{1,0:T(8,128)(2,1)S(1)}, u32[]{:S(2)}, u32[]{:S(2)}) collective-permute-start(bf16[64,640]{1,0:T(8,128)(2,1)S(1)} %collective-permute-done.4), channel_id=1, source_target_pairs={{0,1},{1,0},{2,3},{3,2},{4,5},{5,4},{6,7},{7,6},{8,9},{9,8},{10,11... | collective-permute-start | bytes 245768 | tf_op jit(solution)/shard_map/ppermute | solution.py:41
  10.4 4.8 %collective-permute-start.5 = (bf16[64,640]{1,0:T(8,128)(2,1)S(1)}, bf16[64,640]{1,0:T(8,128)(2,1)S(1)}, u32[]{:S(2)}, u32[]{:S(2)}) collective-permute-start(bf16[64,640]{1,0:T(8,128)(2,1)S(1)} %collective-permute-done.4), channel_id=1, source_target_pairs={{0,4},{2,0},{6,2},{10,6},{14,10},{12,14},{8,12},{4,8},{1,5},{3,1},... | collective-permute-start | bytes 245768 | tf_op jit(solution)/shard_map/ppermute | solution.py:37
  12.1 5.1 %collective-permute-start.9 = (bf16[64,640]{1,0:T(8,128)(2,1)S(1)}, bf16[64,640]{1,0:T(8,128)(2,1)S(1)}, u32[]{:S(2)}, u32[]{:S(2)}) collective-permute-start(bf16[64,640]{1,0:T(8,128)(2,1)S(1)} %collective-permute-done), channel_id=1, source_target_pairs={{0,1},{1,0},{2,3},{3,2},{4,5},{5,4},{6,7},{7,6},{8,9},{9,8},{10,11... | collective-permute-start | bytes 245768 | tf_op jit(solution)/shard_map/ppermute | solution.py:41
  12.4 4.6 %collective-permute-start.1 = (bf16[64,640]{1,0:T(8,128)(2,1)S(1)}, bf16[64,640]{1,0:T(8,128)(2,1)S(1)}, u32[]{:S(2)}, u32[]{:S(2)}) collective-permute-start(bf16[64,640]{1,0:T(8,128)(2,1)S(1)} %collective-permute-done), channel_id=1, source_target_pairs={{0,2},{2,6},{6,10},{10,14},{14,12},{12,8},{8,4},{4,0},{1,3},{3,7},... | collective-permute-start | bytes 245768 | tf_op jit(solution)/shard_map/ppermute | solution.py:37
  15.2 12.3 %collective-permute-start.14 = (bf16[64,640]{1,0:T(8,128)(2,1)S(1)}, bf16[64,640]{1,0:T(8,128)(2,1)S(1)}, u32[]{:S(2)}, u32[]{:S(2)}) collective-permute-start(bf16[64,640]{1,0:T(8,128)(2,1)S(1)} %collective-permute-done.5), channel_id=1, source_target_pairs={{0,1},{1,0},{2,3},{3,2},{4,5},{5,4},{6,7},{7,6},{8,9},{9,8},{10,11... | collective-permute-start | bytes 245768 | tf_op jit(solution)/shard_map/ppermute | solution.py:41
  15.2 4.9 %collective-permute-start.6 = (bf16[64,640]{1,0:T(8,128)(2,1)S(1)}, bf16[64,640]{1,0:T(8,128)(2,1)S(1)}, u32[]{:S(2)}, u32[]{:S(2)}) collective-permute-start(bf16[64,640]{1,0:T(8,128)(2,1)S(1)} %collective-permute-done.5), channel_id=1, source_target_pairs={{0,4},{2,0},{6,2},{10,6},{14,10},{12,14},{8,12},{4,8},{1,5},{3,1},... | collective-permute-start | bytes 245768 | tf_op jit(solution)/shard_map/ppermute | solution.py:37
  17.0 5.2 %collective-permute-start.10 = (bf16[64,640]{1,0:T(8,128)(2,1)S(1)}, bf16[64,640]{1,0:T(8,128)(2,1)S(1)}, u32[]{:S(2)}, u32[]{:S(2)}) collective-permute-start(bf16[64,640]{1,0:T(8,128)(2,1)S(1)} %collective-permute-done.1), channel_id=1, source_target_pairs={{0,1},{1,0},{2,3},{3,2},{4,5},{5,4},{6,7},{7,6},{8,9},{9,8},{10,11... | collective-permute-start | bytes 245768 | tf_op jit(solution)/shard_map/ppermute | solution.py:41
  17.3 4.7 %collective-permute-start.2 = (bf16[64,640]{1,0:T(8,128)(2,1)S(1)}, bf16[64,640]{1,0:T(8,128)(2,1)S(1)}, u32[]{:S(2)}, u32[]{:S(2)}) collective-permute-start(bf16[64,640]{1,0:T(8,128)(2,1)S(1)} %collective-permute-done.1), channel_id=1, source_target_pairs={{0,2},{2,6},{6,10},{10,14},{14,12},{12,8},{8,4},{4,0},{1,3},{3,7},... | collective-permute-start | bytes 245768 | tf_op jit(solution)/shard_map/ppermute | solution.py:37
  20.1 5.9 %collective-permute-start.7 = (bf16[32,640]{1,0:T(8,128)(2,1)S(1)}, bf16[32,640]{1,0:T(8,128)(2,1)S(1)}, u32[]{:S(2)}, u32[]{:S(2)}) collective-permute-start(bf16[32,640]{1,0:T(8,128)(2,1)S(1)} %slice.45), channel_id=1, source_target_pairs={{0,4},{2,0},{6,2},{10,6},{14,10},{12,14},{8,12},{4,8},{1,5},{3,1},... | collective-permute-start | bytes 122888 | tf_op jit(solution)/shard_map/ppermute | solution.py:37
  21.9 4.0 %collective-permute-start.3 = (bf16[32,640]{1,0:T(8,128)(2,1)S(1)}, bf16[32,640]{1,0:T(8,128)(2,1)S(1)}, u32[]{:S(2)}, u32[]{:S(2)}) collective-permute-start(bf16[32,640]{1,0:T(8,128)(2,1)S(1)} %slice.44), channel_id=1, source_target_pairs={{0,2},{2,6},{6,10},{10,14},{14,12},{12,8},{8,4},{4,0},{1,3},{3,7},... | collective-permute-start | bytes 122888 | tf_op jit(solution)/shard_map/ppermute | solution.py:37
  22.3 5.2 %collective-permute-start.13 = (bf16[64,640]{1,0:T(8,128)(2,1)S(1)}, bf16[64,640]{1,0:T(8,128)(2,1)S(1)}, u32[]{:S(2)}, u32[]{:S(2)}) collective-permute-start(bf16[64,640]{1,0:T(8,128)(2,1)S(1)} %collective-permute-done.6), channel_id=1, source_target_pairs={{0,1},{1,0},{2,3},{3,2},{4,5},{5,4},{6,7},{7,6},{8,9},{9,8},{10,11... | collective-permute-start | bytes 245768 | tf_op jit(solution)/shard_map/ppermute | solution.py:41
  26.0 1.5 collective-permute-start.12
  36.3 3.2 %collective-permute-start.16 = (bf16[128,2048]{1,0:T(8,128)(2,1)}, bf16[128,2048]{1,0:T(8,128)(2,1)S(1)}, u32[]{:S(2)}, u32[]{:S(2)}) collective-permute-start(bf16[128,2048]{1,0:T(8,128)(2,1)} %attend.1.here_ref), channel_id=1, source_target_pairs={{0,1},{1,0},{2,3},{3,2},{4,5},{5,4},{6,7},{7,6},{8,9},{9,8},{10,11... | collective-permute-start | bytes 1572872 | tf_op jit(solution)/shard_map/ppermute | solution.py:41
  43.5 8.6 %collective-permute-start.21 = (bf16[128,1024]{1,0:T(8,128)(2,1)}, bf16[128,1024]{1,0:T(8,128)(2,1)S(1)}, u32[]{:S(2)}, u32[]{:S(2)}) collective-permute-start(bf16[128,1024]{1,0:T(8,128)(2,1)} %get-tuple-element.28.refs_0_), channel_id=1, source_target_pairs={{0,4},{2,0},{6,2},{10,6},{14,10},{12,14},{8,12},{4,8},{1,5},{3,1},... | collective-permute-start | bytes 786440 | tf_op jit(solution)/shard_map/ppermute | solution.py:37
  45.1 8.6 %collective-permute-start.17 = (bf16[128,1024]{1,0:T(8,128)(2,1)}, bf16[128,1024]{1,0:T(8,128)(2,1)S(1)}, u32[]{:S(2)}, u32[]{:S(2)}) collective-permute-start(bf16[128,1024]{1,0:T(8,128)(2,1)} %get-tuple-element.28.refs_0_), channel_id=1, source_target_pairs={{0,2},{2,6},{6,10},{10,14},{14,12},{12,8},{8,4},{4,0},{1,3},{3,7},... | collective-permute-start | bytes 786440 | tf_op jit(solution)/shard_map/ppermute | solution.py:37
  52.1 7.5 %collective-permute-start.22 = (bf16[128,1024]{1,0:T(8,128)(2,1)S(1)}, bf16[128,1024]{1,0:T(8,128)(2,1)S(1)}, u32[]{:S(2)}, u32[]{:S(2)}) collective-permute-start(bf16[128,1024]{1,0:T(8,128)(2,1)S(1)} %collective-permute-done.21.refs_7_), channel_id=1, source_target_pairs={{0,4},{2,0},{6,2},{10,6},{14,10},{12,14},{8,12},{4,8},{1,5},{3,1},... | collective-permute-start | bytes 786440 | tf_op jit(solution)/shard_map/ppermute | solution.py:37
  53.7 7.5 %collective-permute-start.18 = (bf16[128,1024]{1,0:T(8,128)(2,1)S(1)}, bf16[128,1024]{1,0:T(8,128)(2,1)S(1)}, u32[]{:S(2)}, u32[]{:S(2)}) collective-permute-start(bf16[128,1024]{1,0:T(8,128)(2,1)S(1)} %collective-permute-done.17.refs_1_), channel_id=1, source_target_pairs={{0,2},{2,6},{6,10},{10,14},{14,12},{12,8},{8,4},{4,0},{1,3},{3,7},... | collective-permute-start | bytes 786440 | tf_op jit(solution)/shard_map/ppermute | solution.py:37
  59.6 10.0 %collective-permute-start.23 = (bf16[128,1024]{1,0:T(8,128)(2,1)S(1)}, bf16[128,1024]{1,0:T(8,128)(2,1)S(1)}, u32[]{:S(2)}, u32[]{:S(2)}) collective-permute-start(bf16[128,1024]{1,0:T(8,128)(2,1)S(1)} %collective-permute-done.22.refs_6_), channel_id=1, source_target_pairs={{0,4},{2,0},{6,2},{10,6},{14,10},{12,14},{8,12},{4,8},{1,5},{3,1},... | collective-permute-start | bytes 786440 | tf_op jit(solution)/shard_map/ppermute | solution.py:37
  61.2 6.4 %collective-permute-start.19 = (bf16[128,1024]{1,0:T(8,128)(2,1)S(1)}, bf16[128,1024]{1,0:T(8,128)(2,1)S(1)}, u32[]{:S(2)}, u32[]{:S(2)}) collective-permute-start(bf16[128,1024]{1,0:T(8,128)(2,1)S(1)} %collective-permute-done.18.refs_2_), channel_id=1, source_target_pairs={{0,2},{2,6},{6,10},{10,14},{14,12},{12,8},{8,4},{4,0},{1,3},{3,7},... | collective-permute-start | bytes 786440 | tf_op jit(solution)/shard_map/ppermute | solution.py:37
  67.6 5.0 %collective-permute-start.20 = (bf16[64,1024]{1,0:T(8,128)(2,1)S(1)}, bf16[64,1024]{1,0:T(8,128)(2,1)S(1)}, u32[]{:S(2)}, u32[]{:S(2)}) collective-permute-start(bf16[64,1024]{1,0:T(8,128)(2,1)S(1)} %slice.51), channel_id=1, source_target_pairs={{0,2},{2,6},{6,10},{10,14},{14,12},{12,8},{8,4},{4,0},{1,3},{3,7},... | collective-permute-start | bytes 393224 | tf_op jit(solution)/shard_map/ppermute | solution.py:37
  69.1 6.7 %collective-permute-start.25 = (bf16[128,1024]{1,0:T(8,128)(2,1)}, bf16[128,1024]{1,0:T(8,128)(2,1)S(1)}, u32[]{:S(2)}, u32[]{:S(2)}) collective-permute-start(bf16[128,1024]{1,0:T(8,128)(2,1)} %get-tuple-element.28.refs_0_), channel_id=1, source_target_pairs={{0,1},{1,0},{2,3},{3,2},{4,5},{5,4},{6,7},{7,6},{8,9},{9,8},{10,11... | collective-permute-start | bytes 786440 | tf_op jit(solution)/shard_map/ppermute | solution.py:41
  69.1 7.3 %collective-permute-start.32 = (bf16[128,1024]{1,0:T(8,128)(2,1)S(1)}, bf16[128,1024]{1,0:T(8,128)(2,1)S(1)}, u32[]{:S(2)}, u32[]{:S(2)}) collective-permute-start(bf16[128,1024]{1,0:T(8,128)(2,1)S(1)} %collective-permute-done.21.refs_7_), channel_id=1, source_target_pairs={{0,1},{1,0},{2,3},{3,2},{4,5},{5,4},{6,7},{7,6},{8,9},{9,8},{10,11... | collective-permute-start | bytes 786440 | tf_op jit(solution)/shard_map/ppermute | solution.py:41
  69.6 6.9 %collective-permute-start.26 = (bf16[128,1024]{1,0:T(8,128)(2,1)S(1)}, bf16[128,1024]{1,0:T(8,128)(2,1)S(1)}, u32[]{:S(2)}, u32[]{:S(2)}) collective-permute-start(bf16[128,1024]{1,0:T(8,128)(2,1)S(1)} %collective-permute-done.17.refs_1_), channel_id=1, source_target_pairs={{0,1},{1,0},{2,3},{3,2},{4,5},{5,4},{6,7},{7,6},{8,9},{9,8},{10,11... | collective-permute-start | bytes 786440 | tf_op jit(solution)/shard_map/ppermute | solution.py:41
  69.6 6.1 %collective-permute-start.24 = (bf16[64,1024]{1,0:T(8,128)(2,1)S(1)}, bf16[64,1024]{1,0:T(8,128)(2,1)S(1)}, u32[]{:S(2)}, u32[]{:S(2)}) collective-permute-start(bf16[64,1024]{1,0:T(8,128)(2,1)S(1)} %slice.52), channel_id=1, source_target_pairs={{0,4},{2,0},{6,2},{10,6},{14,10},{12,14},{8,12},{4,8},{1,5},{3,1},... | collective-permute-start | bytes 393224 | tf_op jit(solution)/shard_map/ppermute | solution.py:37
  72.6 5.1 %collective-permute-start.31 = (bf16[128,1024]{1,0:T(8,128)(2,1)S(1)}, bf16[128,1024]{1,0:T(8,128)(2,1)S(1)}, u32[]{:S(2)}, u32[]{:S(2)}) collective-permute-start(bf16[128,1024]{1,0:T(8,128)(2,1)S(1)} %collective-permute-done.22.refs_6_), channel_id=1, source_target_pairs={{0,1},{1,0},{2,3},{3,2},{4,5},{5,4},{6,7},{7,6},{8,9},{9,8},{10,11... | collective-permute-start | bytes 786440 | tf_op jit(solution)/shard_map/ppermute | solution.py:41
  75.8 2.0 %collective-permute-start.27 = (bf16[128,1024]{1,0:T(8,128)(2,1)S(1)}, bf16[128,1024]{1,0:T(8,128)(2,1)S(1)}, u32[]{:S(2)}, u32[]{:S(2)}) collective-permute-start(bf16[128,1024]{1,0:T(8,128)(2,1)S(1)} %collective-permute-done.18.refs_2_), channel_id=1, source_target_pairs={{0,1},{1,0},{2,3},{3,2},{4,5},{5,4},{6,7},{7,6},{8,9},{9,8},{10,11... | collective-permute-start | bytes 786440 | tf_op jit(solution)/shard_map/ppermute | solution.py:41
  75.8 2.0 %collective-permute-start.30 = (bf16[128,1024]{1,0:T(8,128)(2,1)S(1)}, bf16[128,1024]{1,0:T(8,128)(2,1)}, u32[]{:S(2)}, u32[]{:S(2)}) collective-permute-start(bf16[128,1024]{1,0:T(8,128)(2,1)S(1)} %collective-permute-done.23.refs_5_), channel_id=1, source_target_pairs={{0,1},{1,0},{2,3},{3,2},{4,5},{5,4},{6,7},{7,6},{8,9},{9,8},{10,11... | collective-permute-start | bytes 786440 | tf_op jit(solution)/shard_map/ppermute | solution.py:41
  76.4 1.8 %collective-permute-start.28 = (bf16[128,1024]{1,0:T(8,128)(2,1)S(1)}, bf16[128,1024]{1,0:T(8,128)(2,1)}, u32[]{:S(2)}, u32[]{:S(2)}) collective-permute-start(bf16[128,1024]{1,0:T(8,128)(2,1)S(1)} %collective-permute-done.19.refs_3_), channel_id=1, source_target_pairs={{0,1},{1,0},{2,3},{3,2},{4,5},{5,4},{6,7},{7,6},{8,9},{9,8},{10,11... | collective-permute-start | bytes 786440 | tf_op jit(solution)/shard_map/ppermute | solution.py:41
  76.5 2.1 %collective-permute-start.29 = (bf16[128,1024]{1,0:T(8,128)(2,1)S(1)}, bf16[128,1024]{1,0:T(8,128)(2,1)}, u32[]{:S(2)}, u32[]{:S(2)}) collective-permute-start(bf16[128,1024]{1,0:T(8,128)(2,1)S(1)} %constant_dynamic-update-slice_fusion.2.refs_4_), channel_id=1, source_target_pairs={{0,1},{1,0},{2,3},{3,2},{4,5},{5,4},{6,7},{7,6},{8,9},{9,8},{10,11... | collective-permute-start | bytes 786440 | tf_op jit(solution)/shard_map/ppermute | solution.py:41
  112.3 1.8 %collective-permute-start.37 = (bf16[128,1024]{1,0:T(8,128)(2,1)}, bf16[128,1024]{1,0:T(8,128)(2,1)S(1)}, u32[]{:S(2)}, u32[]{:S(2)}) collective-permute-start(bf16[128,1024]{1,0:T(8,128)(2,1)} %get-tuple-element.42), channel_id=1, source_target_pairs={{0,1},{1,0},{2,3},{3,2},{4,5},{5,4},{6,7},{7,6},{8,9},{9,8},{10,11... | collective-permute-start | bytes 786440 | tf_op jit(solution)/shard_map/ppermute | solution.py:41
  112.6 5.1 %collective-permute-start.36 = (bf16[128,1024]{1,0:T(8,128)(2,1)}, bf16[128,1024]{1,0:T(8,128)(2,1)S(1)}, u32[]{:S(2)}, u32[]{:S(2)}) collective-permute-start(bf16[128,1024]{1,0:T(8,128)(2,1)} %get-tuple-element.40), channel_id=1, source_target_pairs={{0,1},{1,0},{2,3},{3,2},{4,5},{5,4},{6,7},{7,6},{8,9},{9,8},{10,11... | collective-permute-start | bytes 786440 | tf_op jit(solution)/shard_map/ppermute | solution.py:41
  115.1 5.7 %collective-permute-start.38 = (bf16[64,1024]{1,0:T(8,128)(2,1)S(1)}, bf16[64,1024]{1,0:T(8,128)(2,1)S(1)}, u32[]{:S(2)}, u32[]{:S(2)}) collective-permute-start(bf16[64,1024]{1,0:T(8,128)(2,1)S(1)} %get-tuple-element.51), channel_id=1, source_target_pairs={{0,2},{2,6},{6,10},{10,14},{14,12},{12,8},{8,4},{4,0},{1,3},{3,7},... | collective-permute-start | bytes 393224 | tf_op jit(solution)/shard_map/ppermute | solution.py:37
  115.5 6.7 %collective-permute-start.44 = (bf16[128,1024]{1,0:T(8,128)(2,1)}, bf16[128,1024]{1,0:T(8,128)(2,1)S(1)}, u32[]{:S(2)}, u32[]{:S(2)}) collective-permute-start(bf16[128,1024]{1,0:T(8,128)(2,1)} %get-tuple-element.48), channel_id=1, source_target_pairs={{0,1},{1,0},{2,3},{3,2},{4,5},{5,4},{6,7},{7,6},{8,9},{9,8},{10,11... | collective-permute-start | bytes 786440 | tf_op jit(solution)/shard_map/ppermute | solution.py:41
  115.5 9.8 %collective-permute-start.35 = (bf16[128,1024]{1,0:T(8,128)(2,1)}, bf16[128,1024]{1,0:T(8,128)(2,1)S(1)}, u32[]{:S(2)}, u32[]{:S(2)}) collective-permute-start(bf16[128,1024]{1,0:T(8,128)(2,1)} %get-tuple-element.38), channel_id=1, source_target_pairs={{0,1},{1,0},{2,3},{3,2},{4,5},{5,4},{6,7},{7,6},{8,9},{9,8},{10,11... | collective-permute-start | bytes 786440 | tf_op jit(solution)/shard_map/ppermute | solution.py:41
  116.0 6.2 %collective-permute-start.45 = (bf16[64,1024]{1,0:T(8,128)(2,1)S(1)}, bf16[64,1024]{1,0:T(8,128)(2,1)S(1)}, u32[]{:S(2)}, u32[]{:S(2)}) collective-permute-start(bf16[64,1024]{1,0:T(8,128)(2,1)S(1)} %get-tuple-element.52), channel_id=1, source_target_pairs={{0,4},{2,0},{6,2},{10,6},{14,10},{12,14},{8,12},{4,8},{1,5},{3,1},... | collective-permute-start | bytes 393224 | tf_op jit(solution)/shard_map/ppermute | solution.py:37
  121.9 7.7 %collective-permute-start.39 = (bf16[128,1024]{1,0:T(8,128)(2,1)S(1)}, bf16[128,1024]{1,0:T(8,128)(2,1)S(1)}, u32[]{:S(2)}, u32[]{:S(2)}) collective-permute-start(bf16[128,1024]{1,0:T(8,128)(2,1)S(1)} %add_convert_fusion.6), channel_id=1, source_target_pairs={{0,2},{2,6},{6,10},{10,14},{14,12},{12,8},{8,4},{4,0},{1,3},{3,7},... | collective-permute-start | bytes 786440 | tf_op jit(solution)/shard_map/ppermute | solution.py:37
  122.2 8.8 %collective-permute-start.43 = (bf16[128,1024]{1,0:T(8,128)(2,1)}, bf16[128,1024]{1,0:T(8,128)(2,1)S(1)}, u32[]{:S(2)}, u32[]{:S(2)}) collective-permute-start(bf16[128,1024]{1,0:T(8,128)(2,1)} %get-tuple-element.46), channel_id=1, source_target_pairs={{0,1},{1,0},{2,3},{3,2},{4,5},{5,4},{6,7},{7,6},{8,9},{9,8},{10,11... | collective-permute-start | bytes 786440 | tf_op jit(solution)/shard_map/ppermute | solution.py:41
  123.3 8.8 %collective-permute-start.46 = (bf16[128,1024]{1,0:T(8,128)(2,1)S(1)}, bf16[128,1024]{1,0:T(8,128)(2,1)S(1)}, u32[]{:S(2)}, u32[]{:S(2)}) collective-permute-start(bf16[128,1024]{1,0:T(8,128)(2,1)S(1)} %add_convert_fusion.3), channel_id=1, source_target_pairs={{0,4},{2,0},{6,2},{10,6},{14,10},{12,14},{8,12},{4,8},{1,5},{3,1},... | collective-permute-start | bytes 786440 | tf_op jit(solution)/shard_map/ppermute | solution.py:37
  125.0 9.9 %collective-permute-start.34 = (bf16[128,1024]{1,0:T(8,128)(2,1)}, bf16[128,1024]{1,0:T(8,128)(2,1)S(1)}, u32[]{:S(2)}, u32[]{:S(2)}) collective-permute-start(bf16[128,1024]{1,0:T(8,128)(2,1)} %get-tuple-element.36), channel_id=1, source_target_pairs={{0,1},{1,0},{2,3},{3,2},{4,5},{5,4},{6,7},{7,6},{8,9},{9,8},{10,11... | collective-permute-start | bytes 786440 | tf_op jit(solution)/shard_map/ppermute | solution.py:41
  125.3 13.5 %collective-permute-start.42 = (bf16[128,1024]{1,0:T(8,128)(2,1)}, bf16[128,1024]{1,0:T(8,128)(2,1)S(1)}, u32[]{:S(2)}, u32[]{:S(2)}) collective-permute-start(bf16[128,1024]{1,0:T(8,128)(2,1)} %get-tuple-element.44), channel_id=1, source_target_pairs={{0,1},{1,0},{2,3},{3,2},{4,5},{5,4},{6,7},{7,6},{8,9},{9,8},{10,11... | collective-permute-start | bytes 786440 | tf_op jit(solution)/shard_map/ppermute | solution.py:41
  130.6 6.8 %collective-permute-start.40 = (bf16[128,1024]{1,0:T(8,128)(2,1)S(1)}, bf16[128,1024]{1,0:T(8,128)(2,1)S(1)}, u32[]{:S(2)}, u32[]{:S(2)}) collective-permute-start(bf16[128,1024]{1,0:T(8,128)(2,1)S(1)} %add_convert_fusion.5), channel_id=1, source_target_pairs={{0,2},{2,6},{6,10},{10,14},{14,12},{12,8},{8,4},{4,0},{1,3},{3,7},... | collective-permute-start | bytes 786440 | tf_op jit(solution)/shard_map/ppermute | solution.py:37
  133.1 8.0 %collective-permute-start.47 = (bf16[128,1024]{1,0:T(8,128)(2,1)S(1)}, bf16[128,1024]{1,0:T(8,128)(2,1)S(1)}, u32[]{:S(2)}, u32[]{:S(2)}) collective-permute-start(bf16[128,1024]{1,0:T(8,128)(2,1)S(1)} %add_convert_fusion.2), channel_id=1, source_target_pairs={{0,4},{2,0},{6,2},{10,6},{14,10},{12,14},{8,12},{4,8},{1,5},{3,1},... | collective-permute-start | bytes 786440 | tf_op jit(solution)/shard_map/ppermute | solution.py:37
  134.9 9.1 %collective-permute-start.33 = (bf16[128,1024]{1,0:T(8,128)(2,1)}, bf16[128,1024]{1,0:T(8,128)(2,1)S(1)}, u32[]{:S(2)}, u32[]{:S(2)}) collective-permute-start(bf16[128,1024]{1,0:T(8,128)(2,1)} %get-tuple-element.34), channel_id=1, source_target_pairs={{0,1},{1,0},{2,3},{3,2},{4,5},{5,4},{6,7},{7,6},{8,9},{9,8},{10,11... | collective-permute-start | bytes 786440 | tf_op jit(solution)/shard_map/ppermute | solution.py:41
  138.5 6.4 %collective-permute-start.41 = (bf16[128,1024]{1,0:T(8,128)(2,1)S(1)}, bf16[128,1024]{1,0:T(8,128)(2,1)S(1)}, u32[]{:S(2)}, u32[]{:S(2)}) collective-permute-start(bf16[128,1024]{1,0:T(8,128)(2,1)S(1)} %add_convert_fusion.4), channel_id=1, source_target_pairs={{0,2},{2,6},{6,10},{10,14},{14,12},{12,8},{8,4},{4,0},{1,3},{3,7},... | collective-permute-start | bytes 786440 | tf_op jit(solution)/shard_map/ppermute | solution.py:37
  142.2 7.1 %collective-permute-start.48 = (bf16[128,1024]{1,0:T(8,128)(2,1)S(1)}, bf16[128,1024]{1,0:T(8,128)(2,1)S(1)}, u32[]{:S(2)}, u32[]{:S(2)}) collective-permute-start(bf16[128,1024]{1,0:T(8,128)(2,1)S(1)} %add_convert_fusion.1), channel_id=1, source_target_pairs={{0,4},{2,0},{6,2},{10,6},{14,10},{12,14},{8,12},{4,8},{1,5},{3,1},... | collective-permute-start | bytes 786440 | tf_op jit(solution)/shard_map/ppermute | solution.py:37
  (17 other events, 193.9 us)

commit v5 on v4

--- a/solution.py
+++ b/solution.py
@@ -17,7 +17,9 @@
 TOP = 6
 SLOTS = 16
 WIDE = 640
-VMEM_LIMIT = 56 * 1024 * 1024
+VMEM_LIMIT = 50 * 1024 * 1024
+DEPTH = 3
+PIECES = 2
 SWAP = [(0, 1), (1, 0)]
 FEW = 8
 
@@ -60,17 +62,22 @@
 
 def gather(block, count):
     if count > FEW:
-        return list(lax.all_gather(block, "ctx"))
+        found = lax.all_gather(block, "ctx")
+        return list(found), list(swap(found))
     middle = count // 2
-    found = [None] * count
+    found, other = [None] * count, [None] * count
     found[0] = block
+    other[0] = swap(block)
     for d in range(1, middle):
-        found[d] = step(found[d - 1], 1, count)
-        found[-d] = step(found[(1 - d) % count], -1, count)
+        for place, before, ahead in ((d, d - 1, 1), (count - d, (1 - d) % count, -1)):
+            arrived = step(found[before], ahead, count)
+            found[place], other[before] = lax.optimization_barrier((arrived, other[before]))
+            other[place] = swap(found[place])
     half = block.shape[0] // 2
     ahead, back = step(found[middle - 1][:half], 1, count), step(found[middle + 1][half:], -1, count)
     found[middle] = jnp.concatenate([ahead, back], axis=0)
-    return found
+    other[middle] = swap(found[middle])
+    return found, other
 
 
 def reduce(parts, count):
@@ -176,7 +183,7 @@
                 pltpu.VMEM((heads, rows, VHEAD), jnp.float32),
             ],
         ),
-        out_shape=jax.ShapeDtypeStruct((rows, out_proj.shape[1]), jnp.bfloat16),
+        out_shape=pltpu.VMEM((rows, out_proj.shape[1]), jnp.bfloat16),
         compiler_params=pltpu.CompilerParams(vmem_limit_bytes=VMEM_LIMIT),
         name="attend",
     )(where, sources, lengths, order, q, mine, other, kv_up, out_proj)
@@ -196,7 +203,7 @@
 
 def norm(where, residual, here, there, gain):
     rows, width = residual.shape
-    half = jax.ShapeDtypeStruct((rows, width // 2), jnp.bfloat16)
+    half = pltpu.VMEM((rows, width // 2), jnp.bfloat16)
     full = pl.BlockSpec((rows, width), lambda i, *_: (0, 0))
     part = pl.BlockSpec((rows, width // 2), lambda i, *_: (0, 0))
     return pl.pallas_call(
@@ -210,7 +217,7 @@
         out_shape=[half, half],
         compiler_params=pltpu.CompilerParams(vmem_limit_bytes=VMEM_LIMIT),
         name="norm",
-    )(where, residual, here, there, gain.reshape(1, width))
+    )(where, residual, here, there, gain)
 
 
 def pack_kernel(where, latent_ref, ids_ref, weights_ref, out_ref, rows):
@@ -268,35 +275,57 @@
 
 def fused_kernel(count, where, *refs):
     mine, other = refs[:count], refs[count : 2 * count]
-    pick_ref, combine_ref, gate_ref, up_ref, down_ref, scale_ref = refs[2 * count : 2 * count + 6]
+    pick_ref, combine_ref, scale_ref = refs[2 * count : 2 * count + 3]
+    weights = refs[2 * count + 3 : 2 * count + 6]
     kept, away = refs[2 * count + 6 : 3 * count + 6], refs[3 * count + 6 : 4 * count + 6]
-    picked, held = refs[4 * count + 6 :]
-    expert = pl.program_id(0)
+    picked, held = refs[4 * count + 6 : 4 * count + 8]
+    buffers, sems = refs[4 * count + 8 : 4 * count + 11], refs[4 * count + 11]
     here = picked.shape[0]
+    depth, units, _ = buffers[0].shape
     half = picked.shape[2] // 2
     side = where[1]
     near = pl.ds(pl.multiple_of(side * half, half), half)
     far = pl.ds(pl.multiple_of((1 - side) * half, half), half)
-
-    @pl.when(expert == 0)
-    def _():
+    piece = units // PIECES
+
+    def copies(expert, slot):
+        for w in range(3):
+            for i in range(PIECES):
+                rows = pl.ds(i * piece, piece)
+                yield pltpu.make_async_copy(weights[w].at[expert, rows], buffers[w].at[slot, rows], sems.at[slot, w, i])
+
+    for e in range(depth):
+        for copy in copies(e, e):
+            copy.start()
+
+    for c in range(count):
+        for columns, block in ((near, mine[c]), (far, other[c])):
+            rows = jnp.dot(pick_ref[c], block[...], preferred_element_type=jnp.float32).astype(jnp.bfloat16)
+            for e in range(here):
+                picked[e, c * SLOTS : (c + 1) * SLOTS, columns] = rows[e * SLOTS : (e + 1) * SLOTS]
+
+    def work(expert, _):
+        slot = lax.rem(expert, depth)
+        for copy in copies(expert, slot):
+            copy.wait()
+        one = pl.ds(slot, 1)
+        result = expert_rows(picked[expert], *(buffer.at[one] for buffer in buffers), scale_ref.at[pl.ds(expert, 1)])
+        place = pl.ds(pl.multiple_of(expert * SLOTS, SLOTS), SLOTS)
         for c in range(count):
-            for columns, block in ((near, mine[c]), (far, other[c])):
-                rows = jnp.dot(pick_ref[c], block[...], preferred_element_type=jnp.float32).astype(jnp.bfloat16)
-                for e in range(here):
-                    picked[e, c * SLOTS : (c + 1) * SLOTS, columns] = rows[e * SLOTS : (e + 1) * SLOTS]
-
-    result = expert_rows(picked[expert], gate_ref, up_ref, down_ref, scale_ref)
-    place = pl.ds(pl.multiple_of(expert * SLOTS, SLOTS), SLOTS)
+            held[c, place, :] = result[c * SLOTS : (c + 1) * SLOTS]
+
+        @pl.when(expert + depth < here)
+        def _():
+            for copy in copies(expert + depth, slot):
+                copy.start()
+
+        return 0
+
+    lax.fori_loop(0, here, work, 0)
     for c in range(count):
-        held[c, place, :] = result[c * SLOTS : (c + 1) * SLOTS]
-
-    @pl.when(expert == here - 1)
-    def _():
-        for c in range(count):
-            for columns, out in ((far, away[c]), (near, kept[c])):
-                total = jnp.dot(combine_ref[c], held[c, :, columns], preferred_element_type=jnp.float32)
-                out[...] = total.astype(jnp.bfloat16)
+        for columns, out in ((far, away[c]), (near, kept[c])):
+            total = jnp.dot(combine_ref[c], held[c, :, columns], preferred_element_type=jnp.float32)
+            out[...] = total.astype(jnp.bfloat16)
 
 
 def expert_specs(w_gate, rows):
@@ -325,25 +354,25 @@
 def experts_fused(where, mine, other, pick, combine, w_gate, w_up, w_down, scale):
     count, (local, half) = len(mine), mine[0].shape
     here, _, rows = scale.shape
-    whole = pl.BlockSpec((local, half), lambda e, where: (0, 0))
+    units = w_gate.shape[1]
+    depth = min(DEPTH, here)
+    whole = pl.BlockSpec(memory_space=pltpu.VMEM)
     outs = pl.pallas_call(
         functools.partial(fused_kernel, count),
-        grid_spec=pltpu.PrefetchScalarGridSpec(
-            num_scalar_prefetch=1,
-            grid=(here,),
-            in_specs=[whole] * (2 * count)
-            + [pl.BlockSpec(pick.shape, lambda e, where: (0, 0, 0)), pl.BlockSpec(combine.shape, lambda e, where: (0, 0, 0))]
-            + expert_specs(w_gate, rows),
-            out_specs=[whole] * (2 * count),
-            scratch_shapes=[
-                pltpu.VMEM((here, rows, 2 * half), jnp.bfloat16),
-                pltpu.VMEM((count, here * SLOTS, 2 * half), jnp.bfloat16),
-            ],
-        ),
-        out_shape=[jax.ShapeDtypeStruct((local, half), jnp.bfloat16)] * (2 * count),
+        in_specs=[pl.BlockSpec(memory_space=pltpu.SMEM)]
+        + [whole] * (2 * count + 3)
+        + [pl.BlockSpec(memory_space=pl.ANY)] * 3,
+        out_specs=[whole] * (2 * count),
+        scratch_shapes=[
+            pltpu.VMEM((here, rows, 2 * half), jnp.bfloat16),
+            pltpu.VMEM((count, here * SLOTS, 2 * half), jnp.bfloat16),
+        ]
+        + [pltpu.VMEM((depth, units, 2 * half), jnp.bfloat16)] * 3
+        + [pltpu.SemaphoreType.DMA((depth, 3, PIECES))],
+        out_shape=[pltpu.VMEM((local, half), jnp.bfloat16)] * (2 * count),
         compiler_params=pltpu.CompilerParams(vmem_limit_bytes=VMEM_LIMIT),
         name="experts",
-    )(where, *mine, *other, pick, combine, w_gate, w_up, w_down, scale)
+    )(where, *mine, *other, pick, combine, scale, w_gate, w_up, w_down)
     return outs[:count], outs[count:]
 
 
@@ -372,14 +401,14 @@
 
     base = latent.shape[1]
     sources = sources_of(me, count)
-    found = gather(pack(where, latent, expert_ids, route_weights), count)
-    swap_all = lambda pieces: [swap(piece) for piece in pieces] if count <= FEW else list(swap(jnp.stack(pieces)))
-    mine = jnp.stack(found)
-    other = jnp.stack(swap_all(found))
+    found, found_other = gather(pack(where, latent, expert_ids, route_weights), count)
+    gain = norm_gain.reshape(1, width)
+    found[1], gain = lax.optimization_barrier((found[1], gain))
+    mine, other = jnp.stack(found), jnp.stack(found_other)
 
     q = queries.reshape(local_rows, heads, NOPE + ROPE).transpose(1, 0, 2)
     partial = attend(where, sources, seg_lengths, span_order, q, mine, other, kv_up, out_proj, count)
-    middle, normed = norm(where, residual, partial, swap(partial), norm_gain)
+    middle, normed = norm(where, residual, partial, swap(partial), gain)
 
     facts_mine, facts_other = mine[:, :, base : base + 3 * TOP], other[:, :, base : base + 3 * TOP]
     facts = jnp.concatenate(
@@ -401,9 +430,8 @@
     combine = combine.astype(jnp.bfloat16).reshape(count, local_rows, here * SLOTS)
     pick = combine.transpose(0, 2, 1)
 
-    got = gather(normed, count)
+    got, got_other = gather(normed, count)
     got[1], pick, combine, scale = lax.optimization_barrier((got[1], pick, combine, scale))
-    got_other = swap_all(got)
     w_gate, w_up = w_gate.transpose(0, 2, 1), w_up.transpose(0, 2, 1)
     if count <= FEW:
         kept, away = experts_fused(where, got, got_other, pick, combine, w_gate, w_up, w_down, scale)
@@ -417,6 +445,7 @@
         total = jnp.einsum("cts,csd->ctd", combine, result, preferred_element_type=jnp.float32).astype(jnp.bfloat16)
         left, right = jnp.split(total, 2, axis=2)
         kept, away = jnp.where(side == 0, left, right), jnp.where(side == 0, right, left)
+    swap_all = lambda pieces: [swap(piece) for piece in pieces] if count <= FEW else list(swap(jnp.stack(pieces)))
     order = [(count // 2 + (d + 1) // 2 * (1 - d % 2 * 2)) % count for d in range(count)]
     swapped = dict(zip(order, swap_all([away[c] for c in order])))
     parts = [functools.partial(summed, [kept[c], swapped[c]]) for c in range(count)]

time: 152 us -> 139 us (0.914)
  Pallas kernels: 47 us -> 34.7 us
  other arithmetic: 12.4 us -> 3.27 us
  waiting for transfers between devices: 50.7 us -> 57.9 us
  local copies, waits for them, and re-layouts: 9.51 us -> 12.2 us
    pallas_call x1, Pallas kernels: 33.6 us -> 26.9 us  [experts_fused(): pl.pallas_call(functools.partial(fused_kernel, count), in_specs=[pl.Block...]
    ppermute x24, waiting for transfers between devices: 47.8 us -> 53.8 us  [step(): lax.ppermute(value, 'ctx', [(cycle[p], cycle[(p + ahead) % count]) for p...]
    unnamed x49 -> x53, local copies, waits for them, and re-layouts: 3.93 us -> 8.41 us
    convert_element_type x3, other arithmetic: 3.18 us -> 0.33 us  [reduce(): (parts[d]() + back.astype(jnp.float32)).astype(jnp.bfloat16)]
    convert_element_type x3, other arithmetic: 3.18 us -> 0.33 us  [reduce(): (parts[count - d]() + ahead.astype(jnp.float32)).astype(jnp.bfloat16)]
    pallas_call x1, Pallas kernels: 3.15 us -> 0.97 us  [norm(): pl.pallas_call(norm_kernel, grid_spec=pltpu.PrefetchScalarGridSpec(num_sc...]
    pallas_call x1, Pallas kernels: 7.89 us -> 6.14 us  [attend(): pl.pallas_call(functools.partial(attend_kernel, blocks), grid_spec=pltpu....]
    pallas_call x1, Pallas kernels: 2.42 us -> 0.73 us  [pack(): pl.pallas_call(pack_kernel, grid_spec=pltpu.PrefetchScalarGridSpec(num_sc...]
  transfers between devices with their start and end apart: 49 -> 49, of which waited for: 21 -> 23; matrix products, arithmetic and copies ran while one was open for 12% -> 5% of each run, Pallas kernels for 0% -> 0%
where the time goes in v5:
time: 139 us
  waiting for transfers between devices  57.9 us (42%)
  Pallas kernels  34.7 us (25%)
  starting transfers between devices  30 us (22%)
  local copies, waits for them, and re-layouts  12.2 us (9%)
  other arithmetic  3.27 us (2%)
    ppermute x24, waiting for transfers between devices, step(): lax.ppermute(value, 'ctx', [(cycle[p], cycle[(p + ahead) % count]) for p...  53.8 us
    pallas_call x1, Pallas kernels, experts_fused(): pl.pallas_call(functools.partial(fused_kernel, count), in_specs=[pl.Block...  26.9 us
    ppermute x24, starting transfers between devices, step(): lax.ppermute(value, 'ctx', [(cycle[p], cycle[(p + ahead) % count]) for p...  26.1 us
    unnamed x53, local copies, waits for them, and re-layouts  8.41 us
    pallas_call x1, Pallas kernels, attend(): pl.pallas_call(functools.partial(attend_kernel, blocks), grid_spec=pltpu....  6.14 us
    ppermute x25, waiting for transfers between devices, swap(): return lax.ppermute(value, 'exp', SWAP)  4.06 us
    ppermute x25, starting transfers between devices, swap(): return lax.ppermute(value, 'exp', SWAP)  3.81 us
  transfers between devices with their start and end apart: 49, of which 23 were waited for; matrix products, arithmetic and copies ran while one was open for 5% of the time, Pallas kernels for 0%

profile of v5, /device:TPU:0, one launch (start us, length us, event | category | flops | bytes accessed | tf_op | source)
XLA Modules:
  0.0 138.7 jit_solution(6212917664975675244)
XLA Ops:
  0.1 0.9 copy-done.3
  1.0 0.7 copy-done.5
  1.7 0.7 copy-done.6
  2.4 0.7 pack.1
  3.1 3.1 %collective-permute-start.7 = (bf16[64,640]{1,0:T(8,128)(2,1)S(1)}, bf16[64,640]{1,0:T(8,128)(2,1)S(1)}, u32[]{:S(2)}, u32[]{:S(2)}) collective-permute-start(bf16[64,640]{1,0:T(8,128)(2,1)S(1)} %pack.1), channel_id=1, source_target_pairs={{0,4},{2,0},{6,2},{10,6},{14,10},{12,14},{8,12},{4,8},{1,5},{3,1},... | collective-permute-start | bytes 245768 | tf_op jit(solution)/shard_map/ppermute | solution.py:39
  6.3 0.7 reshape.26.gain_ref
  6.9 1.1 copy.30
  8.2 0.7 dynamic-slice_bitcast_fusion.sources
  8.9 2.1 %collective-permute-done = bf16[64,640]{1,0:T(8,128)(2,1)S(1)} collective-permute-done((bf16[64,640]{1,0:T(8,128)(2,1)S(1)}, bf16[64,640]{1,0:T(8,128)(2,1)S(1)}, u32[]{:S(2)}, u32[]{:S(2)}) %collective-permute-start) | collective-permute-done | bytes 81952 | tf_op jit(solution)/shard_map/ppermute | solution.py:39
  11.0 1.6 %collective-permute-start.8 = (bf16[64,640]{1,0:T(8,128)(2,1)S(1)}, bf16[64,640]{1,0:T(8,128)(2,1)S(1)}, u32[]{:S(2)}, u32[]{:S(2)}) collective-permute-start(bf16[64,640]{1,0:T(8,128)(2,1)S(1)} %collective-permute-done.7), channel_id=1, source_target_pairs={{0,4},{2,0},{6,2},{10,6},{14,10},{12,14},{8,12},{4,8},{1,5},{3,1},... | collective-permute-start | bytes 245768 | tf_op jit(solution)/shard_map/ppermute | solution.py:39
  13.3 2.6 %collective-permute-done.8 = bf16[64,640]{1,0:T(8,128)(2,1)S(1)} collective-permute-done((bf16[64,640]{1,0:T(8,128)(2,1)S(1)}, bf16[64,640]{1,0:T(8,128)(2,1)S(1)}, u32[]{:S(2)}, u32[]{:S(2)}) %collective-permute-start.8) | collective-permute-done | bytes 81952 | tf_op jit(solution)/shard_map/ppermute | solution.py:39
  15.9 1.6 %collective-permute-start.10 = (bf16[64,640]{1,0:T(8,128)(2,1)S(1)}, bf16[64,640]{1,0:T(8,128)(2,1)S(1)}, u32[]{:S(2)}, u32[]{:S(2)}) collective-permute-start(bf16[64,640]{1,0:T(8,128)(2,1)S(1)} %collective-permute-done.8), channel_id=1, source_target_pairs={{0,4},{2,0},{6,2},{10,6},{14,10},{12,14},{8,12},{4,8},{1,5},{3,1},... | collective-permute-start | bytes 245768 | tf_op jit(solution)/shard_map/ppermute | solution.py:39
  18.2 2.5 %collective-permute-done.10 = bf16[64,640]{1,0:T(8,128)(2,1)S(1)} collective-permute-done((bf16[64,640]{1,0:T(8,128)(2,1)S(1)}, bf16[64,640]{1,0:T(8,128)(2,1)S(1)}, u32[]{:S(2)}, u32[]{:S(2)}) %collective-permute-start.10) | collective-permute-done | bytes 81952 | tf_op jit(solution)/shard_map/ppermute | solution.py:39
  20.8 1.6 %collective-permute-done.4 = bf16[64,640]{1,0:T(8,128)(2,1)S(1)} collective-permute-done((bf16[64,640]{1,0:T(8,128)(2,1)S(1)}, bf16[64,640]{1,0:T(8,128)(2,1)S(1)}, u32[]{:S(2)}, u32[]{:S(2)}) %collective-permute-start.4) | collective-permute-done | bytes 81952 | tf_op jit(solution)/shard_map/ppermute | solution.py:39
  22.3 1.6 %collective-permute-start.12 = (bf16[32,640]{1,0:T(8,128)(2,1)S(1)}, bf16[32,640]{1,0:T(8,128)(2,1)S(1)}, u32[]{:S(2)}, u32[]{:S(2)}) collective-permute-start(bf16[32,640]{1,0:T(8,128)(2,1)S(1)} %slice.34), channel_id=1, source_target_pairs={{0,4},{2,0},{6,2},{10,6},{14,10},{12,14},{8,12},{4,8},{1,5},{3,1},... | collective-permute-start | bytes 122888 | tf_op jit(solution)/shard_map/ppermute | solution.py:39
  24.5 3.5 %collective-permute-done.6 = bf16[32,640]{1,0:T(8,128)(2,1)S(1)} collective-permute-done((bf16[32,640]{1,0:T(8,128)(2,1)S(1)}, bf16[32,640]{1,0:T(8,128)(2,1)S(1)}, u32[]{:S(2)}, u32[]{:S(2)}) %collective-permute-start.6) | collective-permute-done | bytes 40992 | tf_op jit(solution)/shard_map/ppermute | solution.py:39
  28.2 1.2 collective-permute-done.14
  29.4 1.2 copy-done
  32.0 6.1 %attend.1.here_ref = bf16[128,2048]{1,0:T(8,128)(2,1)S(1)} custom-call(s32[2]{0:T(128)S(1)} %pad_add_fusion.where, s32[8]{0:T(128)S(1)} %dynamic-slice_bitcast_fusion.sources, s32[16]{0:T(128)S(1)} %copy-done.7, s32[16]{0:T(128)S(1)} %copy-done.8, bf16[4,128,192]{2,1,0:T(8,128)(2,1)S(1)} %bitcast.55, bf16[8,64,640]{2,1,0:T(8,128)(2,1)S(1)} %get-tuple-element.108.mine_ref, ...), custom_call_target="tpu_custom_call" | custom-call | tf_op jit(solution)/shard_map/attend/pallas_call | solution.py:167
  38.4 1.8 %collective-permute-done.16.there_ref = bf16[128,2048]{1,0:T(8,128)(2,1)S(1)} collective-permute-done((bf16[128,2048]{1,0:T(8,128)(2,1)S(1)}, bf16[128,2048]{1,0:T(8,128)(2,1)S(1)}, u32[]{:S(2)}, u32[]{:S(2)}) %collective-permute-start.16) | collective-permute-done | bytes 524320 | tf_op jit(solution)/shard_map/ppermute | solution.py:43
  40.1 1.0 copy-done.1
  41.1 1.0 norm.1
  42.9 1.6 %collective-permute-start.24 = (bf16[128,1024]{1,0:T(8,128)(2,1)S(1)}, bf16[128,1024]{1,0:T(8,128)(2,1)S(1)}, u32[]{:S(2)}, u32[]{:S(2)}) collective-permute-start(bf16[128,1024]{1,0:T(8,128)(2,1)S(1)} %get-tuple-element.68.refs_0_), channel_id=1, source_target_pairs={{0,4},{2,0},{6,2},{10,6},{14,10},{12,14},{8,12},{4,8},{1,5},{3,1},... | collective-permute-start | bytes 786440 | tf_op jit(solution)/shard_map/ppermute | solution.py:39
  44.9 6.0 %collective-permute-done.17.refs_1_ = bf16[128,1024]{1,0:T(8,128)(2,1)S(1)} collective-permute-done((bf16[128,1024]{1,0:T(8,128)(2,1)S(1)}, bf16[128,1024]{1,0:T(8,128)(2,1)S(1)}, u32[]{:S(2)}, u32[]{:S(2)}) %collective-permute-start.17) | collective-permute-done | bytes 262176 | tf_op jit(solution)/shard_map/ppermute | solution.py:39
  51.8 1.6 %collective-permute-start.25 = (bf16[128,1024]{1,0:T(8,128)(2,1)S(1)}, bf16[128,1024]{1,0:T(8,128)(2,1)}, u32[]{:S(2)}, u32[]{:S(2)}) collective-permute-start(bf16[128,1024]{1,0:T(8,128)(2,1)S(1)} %collective-permute-done.24.refs_7_), channel_id=1, source_target_pairs={{0,4},{2,0},{6,2},{10,6},{14,10},{12,14},{8,12},{4,8},{1,5},{3,1},... | collective-permute-start | bytes 786440 | tf_op jit(solution)/shard_map/ppermute | solution.py:39
  53.4 6.4 %collective-permute-done.19.refs_2_ = bf16[128,1024]{1,0:T(8,128)(2,1)} collective-permute-done((bf16[128,1024]{1,0:T(8,128)(2,1)S(1)}, bf16[128,1024]{1,0:T(8,128)(2,1)}, u32[]{:S(2)}, u32[]{:S(2)}) %collective-permute-start.19) | collective-permute-done | bytes 262176 | tf_op jit(solution)/shard_map/ppermute | solution.py:39
  61.2 1.6 %collective-permute-start.27 = (bf16[128,1024]{1,0:T(8,128)(2,1)}, bf16[128,1024]{1,0:T(8,128)(2,1)S(1)}, u32[]{:S(2)}, u32[]{:S(2)}) collective-permute-start(bf16[128,1024]{1,0:T(8,128)(2,1)} %collective-permute-done.25.refs_6_), channel_id=1, source_target_pairs={{0,4},{2,0},{6,2},{10,6},{14,10},{12,14},{8,12},{4,8},{1,5},{3,1},... | collective-permute-start | bytes 786440 | tf_op jit(solution)/shard_map/ppermute | solution.py:39
  63.2 5.4 %collective-permute-done.21.refs_3_ = bf16[128,1024]{1,0:T(8,128)(2,1)S(1)} collective-permute-done((bf16[128,1024]{1,0:T(8,128)(2,1)}, bf16[128,1024]{1,0:T(8,128)(2,1)S(1)}, u32[]{:S(2)}, u32[]{:S(2)}) %collective-permute-start.21) | collective-permute-done | bytes 262176 | tf_op jit(solution)/shard_map/ppermute | solution.py:39
  70.0 1.8 %collective-permute-start.29 = (bf16[64,1024]{1,0:T(8,128)(2,1)S(1)}, bf16[64,1024]{1,0:T(8,128)(2,1)S(1)}, u32[]{:S(2)}, u32[]{:S(2)}) collective-permute-start(bf16[64,1024]{1,0:T(8,128)(2,1)S(1)} %slice.41), channel_id=1, source_target_pairs={{0,4},{2,0},{6,2},{10,6},{14,10},{12,14},{8,12},{4,8},{1,5},{3,1},... | collective-permute-start | bytes 393224 | tf_op jit(solution)/shard_map/ppermute | solution.py:39
  72.4 1.4 %collective-permute-done.23 = bf16[64,1024]{1,0:T(8,128)(2,1)S(1)} collective-permute-done((bf16[64,1024]{1,0:T(8,128)(2,1)S(1)}, bf16[64,1024]{1,0:T(8,128)(2,1)S(1)}, u32[]{:S(2)}, u32[]{:S(2)}) %collective-permute-start.23) | collective-permute-done | bytes 131104 | tf_op jit(solution)/shard_map/ppermute | solution.py:39
  73.9 1.3 collective-permute-done.29
  75.6 0.7 reshape.27.refs_18_
  76.2 0.8 compare_convert_fusion.refs_17_
  77.0 0.9 copy.38.refs_16_
  78.6 26.9 %experts.1 = (bf16[128,1024]{1,0:T(8,128)(2,1)S(1)}, bf16[128,1024]{1,0:T(8,128)(2,1)S(1)}, bf16[128,1024]{1,0:T(8,128)(2,1)S(1)}, bf16[128,1024]{1,0:T(8,128)(2...) custom-call(s32[2]{0:T(128)} %copy-done.4, ...), custom_call_target="tpu_custom_call" | custom-call | tf_op jit(solution)/shard_map/experts/pallas_call | solution.py:360
  106.1 1.1 collective-permute-done.37
  108.3 1.6 %collective-permute-start.45 = (bf16[64,1024]{1,0:T(8,128)(2,1)S(1)}, bf16[64,1024]{1,0:T(8,128)(2,1)S(1)}, u32[]{:S(2)}, u32[]{:S(2)}) collective-permute-start(bf16[64,1024]{1,0:T(8,128)(2,1)S(1)} %get-tuple-element.104), channel_id=1, source_target_pairs={{0,4},{2,0},{6,2},{10,6},{14,10},{12,14},{8,12},{4,8},{1,5},{3,1},... | collective-permute-start | bytes 393224 | tf_op jit(solution)/shard_map/ppermute | solution.py:39
  109.9 3.2 %collective-permute-done.38 = bf16[64,1024]{1,0:T(8,128)(2,1)S(1)} collective-permute-done((bf16[64,1024]{1,0:T(8,128)(2,1)S(1)}, bf16[64,1024]{1,0:T(8,128)(2,1)S(1)}, u32[]{:S(2)}, u32[]{:S(2)}) %collective-permute-start.38) | collective-permute-done | bytes 131104 | tf_op jit(solution)/shard_map/ppermute | solution.py:39
  113.9 1.6 %collective-permute-start.46 = (bf16[128,1024]{1,0:T(8,128)(2,1)S(1)}, bf16[128,1024]{1,0:T(8,128)(2,1)S(1)}, u32[]{:S(2)}, u32[]{:S(2)}) collective-permute-start(bf16[128,1024]{1,0:T(8,128)(2,1)S(1)} %add_convert_fusion.3), channel_id=1, source_target_pairs={{0,4},{2,0},{6,2},{10,6},{14,10},{12,14},{8,12},{4,8},{1,5},{3,1},... | collective-permute-start | bytes 786440 | tf_op jit(solution)/shard_map/ppermute | solution.py:39
  116.0 5.0 %collective-permute-done.39 = bf16[128,1024]{1,0:T(8,128)(2,1)S(1)} collective-permute-done((bf16[128,1024]{1,0:T(8,128)(2,1)S(1)}, bf16[128,1024]{1,0:T(8,128)(2,1)S(1)}, u32[]{:S(2)}, u32[]{:S(2)}) %collective-permute-start.39) | collective-permute-done | bytes 262176 | tf_op jit(solution)/shard_map/ppermute | solution.py:39
  121.7 0.9 collective-permute-done.46
  122.7 1.6 %collective-permute-start.47 = (bf16[128,1024]{1,0:T(8,128)(2,1)S(1)}, bf16[128,1024]{1,0:T(8,128)(2,1)S(1)}, u32[]{:S(2)}, u32[]{:S(2)}) collective-permute-start(bf16[128,1024]{1,0:T(8,128)(2,1)S(1)} %add_convert_fusion.2), channel_id=1, source_target_pairs={{0,4},{2,0},{6,2},{10,6},{14,10},{12,14},{8,12},{4,8},{1,5},{3,1},... | collective-permute-start | bytes 786440 | tf_op jit(solution)/shard_map/ppermute | solution.py:39
  124.4 3.7 %collective-permute-done.40 = bf16[128,1024]{1,0:T(8,128)(2,1)S(1)} collective-permute-done((bf16[128,1024]{1,0:T(8,128)(2,1)S(1)}, bf16[128,1024]{1,0:T(8,128)(2,1)S(1)}, u32[]{:S(2)}, u32[]{:S(2)}) %collective-permute-start.40) | collective-permute-done | bytes 262176 | tf_op jit(solution)/shard_map/ppermute | solution.py:39
  128.7 2.0 %collective-permute-done.47 = bf16[128,1024]{1,0:T(8,128)(2,1)S(1)} collective-permute-done((bf16[128,1024]{1,0:T(8,128)(2,1)S(1)}, bf16[128,1024]{1,0:T(8,128)(2,1)S(1)}, u32[]{:S(2)}, u32[]{:S(2)}) %collective-permute-start.47) | collective-permute-done | bytes 262176 | tf_op jit(solution)/shard_map/ppermute | solution.py:39
  130.8 1.6 %collective-permute-start.48 = (bf16[128,1024]{1,0:T(8,128)(2,1)S(1)}, bf16[128,1024]{1,0:T(8,128)(2,1)S(1)}, u32[]{:S(2)}, u32[]{:S(2)}) collective-permute-start(bf16[128,1024]{1,0:T(8,128)(2,1)S(1)} %add_convert_fusion.1), channel_id=1, source_target_pairs={{0,4},{2,0},{6,2},{10,6},{14,10},{12,14},{8,12},{4,8},{1,5},{3,1},... | collective-permute-start | bytes 786440 | tf_op jit(solution)/shard_map/ppermute | solution.py:39
  132.4 2.2 %collective-permute-done.41 = bf16[128,1024]{1,0:T(8,128)(2,1)S(1)} collective-permute-done((bf16[128,1024]{1,0:T(8,128)(2,1)S(1)}, bf16[128,1024]{1,0:T(8,128)(2,1)S(1)}, u32[]{:S(2)}, u32[]{:S(2)}) %collective-permute-start.41) | collective-permute-done | bytes 262176 | tf_op jit(solution)/shard_map/ppermute | solution.py:39
  134.6 3.2 %collective-permute-done.48 = bf16[128,1024]{1,0:T(8,128)(2,1)S(1)} collective-permute-done((bf16[128,1024]{1,0:T(8,128)(2,1)S(1)}, bf16[128,1024]{1,0:T(8,128)(2,1)S(1)}, u32[]{:S(2)}, u32[]{:S(2)}) %collective-permute-start.48) | collective-permute-done | bytes 262176 | tf_op jit(solution)/shard_map/ppermute | solution.py:39
  137.8 0.9 add_convert_fusion
  (149 shorter events, 15.4 us)
Async XLA Ops:
  3.1 7.9 %collective-permute-start.7 = (bf16[64,640]{1,0:T(8,128)(2,1)S(1)}, bf16[64,640]{1,0:T(8,128)(2,1)S(1)}, u32[]{:S(2)}, u32[]{:S(2)}) collective-permute-start(bf16[64,640]{1,0:T(8,128)(2,1)S(1)} %pack.1), channel_id=1, source_target_pairs={{0,4},{2,0},{6,2},{10,6},{14,10},{12,14},{8,12},{4,8},{1,5},{3,1},... | collective-permute-start | bytes 245768 | tf_op jit(solution)/shard_map/ppermute | solution.py:39
  6.2 2.7 %collective-permute-start.1 = (bf16[64,640]{1,0:T(8,128)(2,1)S(1)}, bf16[64,640]{1,0:T(8,128)(2,1)S(1)}, u32[]{:S(2)}, u32[]{:S(2)}) collective-permute-start(bf16[64,640]{1,0:T(8,128)(2,1)S(1)} %pack.1), channel_id=1, source_target_pairs={{0,1},{1,0},{2,3},{3,2},{4,5},{5,4},{6,7},{7,6},{8,9},{9,8},{10,11... | collective-permute-start | bytes 245768 | tf_op jit(solution)/shard_map/ppermute | solution.py:43
  6.2 4.9 %collective-permute-start = (bf16[64,640]{1,0:T(8,128)(2,1)S(1)}, bf16[64,640]{1,0:T(8,128)(2,1)S(1)}, u32[]{:S(2)}, u32[]{:S(2)}) collective-permute-start(bf16[64,640]{1,0:T(8,128)(2,1)S(1)} %pack.1), channel_id=1, source_target_pairs={{0,2},{2,6},{6,10},{10,14},{14,12},{12,8},{8,4},{4,0},{1,3},{3,7},... | collective-permute-start | bytes 245768 | tf_op jit(solution)/shard_map/ppermute | solution.py:39
  11.0 2.3 %collective-permute-start.9 = (bf16[64,640]{1,0:T(8,128)(2,1)S(1)}, bf16[64,640]{1,0:T(8,128)(2,1)S(1)}, u32[]{:S(2)}, u32[]{:S(2)}) collective-permute-start(bf16[64,640]{1,0:T(8,128)(2,1)S(1)} %collective-permute-done.7), channel_id=1, source_target_pairs={{0,1},{1,0},{2,3},{3,2},{4,5},{5,4},{6,7},{7,6},{8,9},{9,8},{10,11... | collective-permute-start | bytes 245768 | tf_op jit(solution)/shard_map/ppermute | solution.py:43
  11.0 4.9 %collective-permute-start.8 = (bf16[64,640]{1,0:T(8,128)(2,1)S(1)}, bf16[64,640]{1,0:T(8,128)(2,1)S(1)}, u32[]{:S(2)}, u32[]{:S(2)}) collective-permute-start(bf16[64,640]{1,0:T(8,128)(2,1)S(1)} %collective-permute-done.7), channel_id=1, source_target_pairs={{0,4},{2,0},{6,2},{10,6},{14,10},{12,14},{8,12},{4,8},{1,5},{3,1},... | collective-permute-start | bytes 245768 | tf_op jit(solution)/shard_map/ppermute | solution.py:39
  12.6 4.9 %collective-permute-start.3 = (bf16[64,640]{1,0:T(8,128)(2,1)S(1)}, bf16[64,640]{1,0:T(8,128)(2,1)S(1)}, u32[]{:S(2)}, u32[]{:S(2)}) collective-permute-start(bf16[64,640]{1,0:T(8,128)(2,1)S(1)} %collective-permute-done), channel_id=1, source_target_pairs={{0,1},{1,0},{2,3},{3,2},{4,5},{5,4},{6,7},{7,6},{8,9},{9,8},{10,11... | collective-permute-start | bytes 245768 | tf_op jit(solution)/shard_map/ppermute | solution.py:43
  12.8 4.6 %collective-permute-start.2 = (bf16[64,640]{1,0:T(8,128)(2,1)S(1)}, bf16[64,640]{1,0:T(8,128)(2,1)S(1)}, u32[]{:S(2)}, u32[]{:S(2)}) collective-permute-start(bf16[64,640]{1,0:T(8,128)(2,1)S(1)} %collective-permute-done), channel_id=1, source_target_pairs={{0,2},{2,6},{6,10},{10,14},{14,12},{12,8},{8,4},{4,0},{1,3},{3,7},... | collective-permute-start | bytes 245768 | tf_op jit(solution)/shard_map/ppermute | solution.py:39
  15.9 2.3 %collective-permute-start.11 = (bf16[64,640]{1,0:T(8,128)(2,1)S(1)}, bf16[64,640]{1,0:T(8,128)(2,1)S(1)}, u32[]{:S(2)}, u32[]{:S(2)}) collective-permute-start(bf16[64,640]{1,0:T(8,128)(2,1)S(1)} %collective-permute-done.8), channel_id=1, source_target_pairs={{0,1},{1,0},{2,3},{3,2},{4,5},{5,4},{6,7},{7,6},{8,9},{9,8},{10,11... | collective-permute-start | bytes 245768 | tf_op jit(solution)/shard_map/ppermute | solution.py:43
  15.9 4.9 %collective-permute-start.10 = (bf16[64,640]{1,0:T(8,128)(2,1)S(1)}, bf16[64,640]{1,0:T(8,128)(2,1)S(1)}, u32[]{:S(2)}, u32[]{:S(2)}) collective-permute-start(bf16[64,640]{1,0:T(8,128)(2,1)S(1)} %collective-permute-done.8), channel_id=1, source_target_pairs={{0,4},{2,0},{6,2},{10,6},{14,10},{12,14},{8,12},{4,8},{1,5},{3,1},... | collective-permute-start | bytes 245768 | tf_op jit(solution)/shard_map/ppermute | solution.py:39
  17.5 3.3 %collective-permute-start.5 = (bf16[64,640]{1,0:T(8,128)(2,1)S(1)}, bf16[64,640]{1,0:T(8,128)(2,1)S(1)}, u32[]{:S(2)}, u32[]{:S(2)}) collective-permute-start(bf16[64,640]{1,0:T(8,128)(2,1)S(1)} %collective-permute-done.2), channel_id=1, source_target_pairs={{0,1},{1,0},{2,3},{3,2},{4,5},{5,4},{6,7},{7,6},{8,9},{9,8},{10,11... | collective-permute-start | bytes 245768 | tf_op jit(solution)/shard_map/ppermute | solution.py:43
  17.7 4.6 %collective-permute-start.4 = (bf16[64,640]{1,0:T(8,128)(2,1)S(1)}, bf16[64,640]{1,0:T(8,128)(2,1)S(1)}, u32[]{:S(2)}, u32[]{:S(2)}) collective-permute-start(bf16[64,640]{1,0:T(8,128)(2,1)S(1)} %collective-permute-done.2), channel_id=1, source_target_pairs={{0,2},{2,6},{6,10},{10,14},{14,12},{12,8},{8,4},{4,0},{1,3},{3,7},... | collective-permute-start | bytes 245768 | tf_op jit(solution)/shard_map/ppermute | solution.py:39
  20.7 8.6 %collective-permute-start.15 = (bf16[64,640]{1,0:T(8,128)(2,1)S(1)}, bf16[64,640]{1,0:T(8,128)(2,1)S(1)}, u32[]{:S(2)}, u32[]{:S(2)}) collective-permute-start(bf16[64,640]{1,0:T(8,128)(2,1)S(1)} %collective-permute-done.10), channel_id=1, source_target_pairs={{0,1},{1,0},{2,3},{3,2},{4,5},{5,4},{6,7},{7,6},{8,9},{9,8},{10,11... | collective-permute-start | bytes 245768 | tf_op jit(solution)/shard_map/ppermute | solution.py:43
  22.3 5.8 %collective-permute-start.13 = (bf16[64,640]{1,0:T(8,128)(2,1)S(1)}, bf16[64,640]{1,0:T(8,128)(2,1)S(1)}, u32[]{:S(2)}, u32[]{:S(2)}) collective-permute-start(bf16[64,640]{1,0:T(8,128)(2,1)S(1)} %collective-permute-done.4), channel_id=1, source_target_pairs={{0,1},{1,0},{2,3},{3,2},{4,5},{5,4},{6,7},{7,6},{8,9},{9,8},{10,11... | collective-permute-start | bytes 245768 | tf_op jit(solution)/shard_map/ppermute | solution.py:43
  22.3 5.6 %collective-permute-start.12 = (bf16[32,640]{1,0:T(8,128)(2,1)S(1)}, bf16[32,640]{1,0:T(8,128)(2,1)S(1)}, u32[]{:S(2)}, u32[]{:S(2)}) collective-permute-start(bf16[32,640]{1,0:T(8,128)(2,1)S(1)} %slice.34), channel_id=1, source_target_pairs={{0,4},{2,0},{6,2},{10,6},{14,10},{12,14},{8,12},{4,8},{1,5},{3,1},... | collective-permute-start | bytes 122888 | tf_op jit(solution)/shard_map/ppermute | solution.py:39
  24.0 4.0 %collective-permute-start.6 = (bf16[32,640]{1,0:T(8,128)(2,1)S(1)}, bf16[32,640]{1,0:T(8,128)(2,1)S(1)}, u32[]{:S(2)}, u32[]{:S(2)}) collective-permute-start(bf16[32,640]{1,0:T(8,128)(2,1)S(1)} %slice.33), channel_id=1, source_target_pairs={{0,2},{2,6},{6,10},{10,14},{14,12},{12,8},{8,4},{4,0},{1,3},{3,7},... | collective-permute-start | bytes 122888 | tf_op jit(solution)/shard_map/ppermute | solution.py:39
  38.1 2.0 %collective-permute-start.16 = (bf16[128,2048]{1,0:T(8,128)(2,1)S(1)}, bf16[128,2048]{1,0:T(8,128)(2,1)S(1)}, u32[]{:S(2)}, u32[]{:S(2)}) collective-permute-start(bf16[128,2048]{1,0:T(8,128)(2,1)S(1)} %attend.1.here_ref), channel_id=1, source_target_pairs={{0,1},{1,0},{2,3},{3,2},{4,5},{5,4},{6,7},{7,6},{8,9},{9,8},{10,11... | collective-permute-start | bytes 1572872 | tf_op jit(solution)/shard_map/ppermute | solution.py:43
  42.1 2.8 %collective-permute-start.18 = (bf16[128,1024]{1,0:T(8,128)(2,1)S(1)}, bf16[128,1024]{1,0:T(8,128)(2,1)S(1)}, u32[]{:S(2)}, u32[]{:S(2)}) collective-permute-start(bf16[128,1024]{1,0:T(8,128)(2,1)S(1)} %get-tuple-element.68.refs_0_), channel_id=1, source_target_pairs={{0,1},{1,0},{2,3},{3,2},{4,5},{5,4},{6,7},{7,6},{8,9},{9,8},{10,11... | collective-permute-start | bytes 786440 | tf_op jit(solution)/shard_map/ppermute | solution.py:43
  42.4 8.6 %collective-permute-start.17 = (bf16[128,1024]{1,0:T(8,128)(2,1)S(1)}, bf16[128,1024]{1,0:T(8,128)(2,1)S(1)}, u32[]{:S(2)}, u32[]{:S(2)}) collective-permute-start(bf16[128,1024]{1,0:T(8,128)(2,1)S(1)} %get-tuple-element.68.refs_0_), channel_id=1, source_target_pairs={{0,2},{2,6},{6,10},{10,14},{14,12},{12,8},{8,4},{4,0},{1,3},{3,7},... | collective-permute-start | bytes 786440 | tf_op jit(solution)/shard_map/ppermute | solution.py:39
  42.9 8.6 %collective-permute-start.24 = (bf16[128,1024]{1,0:T(8,128)(2,1)S(1)}, bf16[128,1024]{1,0:T(8,128)(2,1)S(1)}, u32[]{:S(2)}, u32[]{:S(2)}) collective-permute-start(bf16[128,1024]{1,0:T(8,128)(2,1)S(1)} %get-tuple-element.68.refs_0_), channel_id=1, source_target_pairs={{0,4},{2,0},{6,2},{10,6},{14,10},{12,14},{8,12},{4,8},{1,5},{3,1},... | collective-permute-start | bytes 786440 | tf_op jit(solution)/shard_map/ppermute | solution.py:39
  50.9 2.5 %collective-permute-start.20 = (bf16[128,1024]{1,0:T(8,128)(2,1)S(1)}, bf16[128,1024]{1,0:T(8,128)(2,1)S(1)}, u32[]{:S(2)}, u32[]{:S(2)}) collective-permute-start(bf16[128,1024]{1,0:T(8,128)(2,1)S(1)} %collective-permute-done.17.refs_1_), channel_id=1, source_target_pairs={{0,1},{1,0},{2,3},{3,2},{4,5},{5,4},{6,7},{7,6},{8,9},{9,8},{10,11... | collective-permute-start | bytes 786440 | tf_op jit(solution)/shard_map/ppermute | solution.py:43
  50.9 8.8 %collective-permute-start.19 = (bf16[128,1024]{1,0:T(8,128)(2,1)S(1)}, bf16[128,1024]{1,0:T(8,128)(2,1)}, u32[]{:S(2)}, u32[]{:S(2)}) collective-permute-start(bf16[128,1024]{1,0:T(8,128)(2,1)S(1)} %collective-permute-done.17.refs_1_), channel_id=1, source_target_pairs={{0,2},{2,6},{6,10},{10,14},{14,12},{12,8},{8,4},{4,0},{1,3},{3,7},... | collective-permute-start | bytes 786440 | tf_op jit(solution)/shard_map/ppermute | solution.py:39
  51.5 8.8 %collective-permute-start.26 = (bf16[128,1024]{1,0:T(8,128)(2,1)S(1)}, bf16[128,1024]{1,0:T(8,128)(2,1)S(1)}, u32[]{:S(2)}, u32[]{:S(2)}) collective-permute-start(bf16[128,1024]{1,0:T(8,128)(2,1)S(1)} %collective-permute-done.24.refs_7_), channel_id=1, source_target_pairs={{0,1},{1,0},{2,3},{3,2},{4,5},{5,4},{6,7},{7,6},{8,9},{9,8},{10,11... | collective-permute-start | bytes 786440 | tf_op jit(solution)/shard_map/ppermute | solution.py:43
  51.8 8.6 %collective-permute-start.25 = (bf16[128,1024]{1,0:T(8,128)(2,1)S(1)}, bf16[128,1024]{1,0:T(8,128)(2,1)}, u32[]{:S(2)}, u32[]{:S(2)}) collective-permute-start(bf16[128,1024]{1,0:T(8,128)(2,1)S(1)} %collective-permute-done.24.refs_7_), channel_id=1, source_target_pairs={{0,4},{2,0},{6,2},{10,6},{14,10},{12,14},{8,12},{4,8},{1,5},{3,1},... | collective-permute-start | bytes 786440 | tf_op jit(solution)/shard_map/ppermute | solution.py:39
  59.7 3.5 %collective-permute-start.22 = (bf16[128,1024]{1,0:T(8,128)(2,1)}, bf16[128,1024]{1,0:T(8,128)(2,1)}, u32[]{:S(2)}, u32[]{:S(2)}) collective-permute-start(bf16[128,1024]{1,0:T(8,128)(2,1)} %collective-permute-done.19.refs_2_), channel_id=1, source_target_pairs={{0,1},{1,0},{2,3},{3,2},{4,5},{5,4},{6,7},{7,6},{8,9},{9,8},{10,11... | collective-permute-start | bytes 786440 | tf_op jit(solution)/shard_map/ppermute | solution.py:43
  59.8 8.9 %collective-permute-start.21 = (bf16[128,1024]{1,0:T(8,128)(2,1)}, bf16[128,1024]{1,0:T(8,128)(2,1)S(1)}, u32[]{:S(2)}, u32[]{:S(2)}) collective-permute-start(bf16[128,1024]{1,0:T(8,128)(2,1)} %collective-permute-done.19.refs_2_), channel_id=1, source_target_pairs={{0,2},{2,6},{6,10},{10,14},{14,12},{12,8},{8,4},{4,0},{1,3},{3,7},... | collective-permute-start | bytes 786440 | tf_op jit(solution)/shard_map/ppermute | solution.py:39
  61.0 8.3 %collective-permute-start.28 = (bf16[128,1024]{1,0:T(8,128)(2,1)}, bf16[128,1024]{1,0:T(8,128)(2,1)}, u32[]{:S(2)}, u32[]{:S(2)}) collective-permute-start(bf16[128,1024]{1,0:T(8,128)(2,1)} %collective-permute-done.25.refs_6_), channel_id=1, source_target_pairs={{0,1},{1,0},{2,3},{3,2},{4,5},{5,4},{6,7},{7,6},{8,9},{9,8},{10,11... | collective-permute-start | bytes 786440 | tf_op jit(solution)/shard_map/ppermute | solution.py:43
  61.2 8.7 %collective-permute-start.27 = (bf16[128,1024]{1,0:T(8,128)(2,1)}, bf16[128,1024]{1,0:T(8,128)(2,1)S(1)}, u32[]{:S(2)}, u32[]{:S(2)}) collective-permute-start(bf16[128,1024]{1,0:T(8,128)(2,1)} %collective-permute-done.25.refs_6_), channel_id=1, source_target_pairs={{0,4},{2,0},{6,2},{10,6},{14,10},{12,14},{8,12},{4,8},{1,5},{3,1},... | collective-permute-start | bytes 786440 | tf_op jit(solution)/shard_map/ppermute | solution.py:39
  68.7 5.2 %collective-permute-start.23 = (bf16[64,1024]{1,0:T(8,128)(2,1)S(1)}, bf16[64,1024]{1,0:T(8,128)(2,1)S(1)}, u32[]{:S(2)}, u32[]{:S(2)}) collective-permute-start(bf16[64,1024]{1,0:T(8,128)(2,1)S(1)} %slice.40), channel_id=1, source_target_pairs={{0,2},{2,6},{6,10},{10,14},{14,12},{12,8},{8,4},{4,0},{1,3},{3,7},... | collective-permute-start | bytes 393224 | tf_op jit(solution)/shard_map/ppermute | solution.py:39
  70.0 5.2 %collective-permute-start.29 = (bf16[64,1024]{1,0:T(8,128)(2,1)S(1)}, bf16[64,1024]{1,0:T(8,128)(2,1)S(1)}, u32[]{:S(2)}, u32[]{:S(2)}) collective-permute-start(bf16[64,1024]{1,0:T(8,128)(2,1)S(1)} %slice.41), channel_id=1, source_target_pairs={{0,4},{2,0},{6,2},{10,6},{14,10},{12,14},{8,12},{4,8},{1,5},{3,1},... | collective-permute-start | bytes 393224 | tf_op jit(solution)/shard_map/ppermute | solution.py:39
  71.9 6.0 %collective-permute-start.32 = (bf16[128,1024]{1,0:T(8,128)(2,1)S(1)}, bf16[128,1024]{1,0:T(8,128)(2,1)S(1)}, u32[]{:S(2)}, u32[]{:S(2)}) collective-permute-start(bf16[128,1024]{1,0:T(8,128)(2,1)S(1)} %collective-permute-done.27.refs_5_), channel_id=1, source_target_pairs={{0,1},{1,0},{2,3},{3,2},{4,5},{5,4},{6,7},{7,6},{8,9},{9,8},{10,11... | collective-permute-start | bytes 786440 | tf_op jit(solution)/shard_map/ppermute | solution.py:43
  71.9 5.9 %collective-permute-start.30 = (bf16[128,1024]{1,0:T(8,128)(2,1)S(1)}, bf16[128,1024]{1,0:T(8,128)(2,1)}, u32[]{:S(2)}, u32[]{:S(2)}) collective-permute-start(bf16[128,1024]{1,0:T(8,128)(2,1)S(1)} %collective-permute-done.21.refs_3_), channel_id=1, source_target_pairs={{0,1},{1,0},{2,3},{3,2},{4,5},{5,4},{6,7},{7,6},{8,9},{9,8},{10,11... | collective-permute-start | bytes 786440 | tf_op jit(solution)/shard_map/ppermute | solution.py:43
  75.2 2.7 %collective-permute-start.31 = (bf16[128,1024]{1,0:T(8,128)(2,1)S(1)}, bf16[128,1024]{1,0:T(8,128)(2,1)}, u32[]{:S(2)}, u32[]{:S(2)}) collective-permute-start(bf16[128,1024]{1,0:T(8,128)(2,1)S(1)} %constant_dynamic-update-slice_fusion.2.refs_4_), channel_id=1, source_target_pairs={{0,1},{1,0},{2,3},{3,2},{4,5},{5,4},{6,7},{7,6},{8,9},{9,8},{10,11... | collective-permute-start | bytes 786440 | tf_op jit(solution)/shard_map/ppermute | solution.py:43
  105.5 1.7 %collective-permute-start.37 = (bf16[128,1024]{1,0:T(8,128)(2,1)S(1)}, bf16[128,1024]{1,0:T(8,128)(2,1)S(1)}, u32[]{:S(2)}, u32[]{:S(2)}) collective-permute-start(bf16[128,1024]{1,0:T(8,128)(2,1)S(1)} %get-tuple-element.94), channel_id=1, source_target_pairs={{0,1},{1,0},{2,3},{3,2},{4,5},{5,4},{6,7},{7,6},{8,9},{9,8},{10,11... | collective-permute-start | bytes 786440 | tf_op jit(solution)/shard_map/ppermute | solution.py:43
  106.0 3.9 %collective-permute-start.36 = (bf16[128,1024]{1,0:T(8,128)(2,1)S(1)}, bf16[128,1024]{1,0:T(8,128)(2,1)S(1)}, u32[]{:S(2)}, u32[]{:S(2)}) collective-permute-start(bf16[128,1024]{1,0:T(8,128)(2,1)S(1)} %get-tuple-element.92), channel_id=1, source_target_pairs={{0,1},{1,0},{2,3},{3,2},{4,5},{5,4},{6,7},{7,6},{8,9},{9,8},{10,11... | collective-permute-start | bytes 786440 | tf_op jit(solution)/shard_map/ppermute | solution.py:43
  107.3 5.8 %collective-permute-start.38 = (bf16[64,1024]{1,0:T(8,128)(2,1)S(1)}, bf16[64,1024]{1,0:T(8,128)(2,1)S(1)}, u32[]{:S(2)}, u32[]{:S(2)}) collective-permute-start(bf16[64,1024]{1,0:T(8,128)(2,1)S(1)} %get-tuple-element.103), channel_id=1, source_target_pairs={{0,2},{2,6},{6,10},{10,14},{14,12},{12,8},{8,4},{4,0},{1,3},{3,7},... | collective-permute-start | bytes 393224 | tf_op jit(solution)/shard_map/ppermute | solution.py:39
  107.8 5.9 %collective-permute-start.44 = (bf16[128,1024]{1,0:T(8,128)(2,1)S(1)}, bf16[128,1024]{1,0:T(8,128)(2,1)S(1)}, u32[]{:S(2)}, u32[]{:S(2)}) collective-permute-start(bf16[128,1024]{1,0:T(8,128)(2,1)S(1)} %get-tuple-element.100), channel_id=1, source_target_pairs={{0,1},{1,0},{2,3},{3,2},{4,5},{5,4},{6,7},{7,6},{8,9},{9,8},{10,11... | collective-permute-start | bytes 786440 | tf_op jit(solution)/shard_map/ppermute | solution.py:43
  107.9 7.8 %collective-permute-start.35 = (bf16[128,1024]{1,0:T(8,128)(2,1)S(1)}, bf16[128,1024]{1,0:T(8,128)(2,1)S(1)}, u32[]{:S(2)}, u32[]{:S(2)}) collective-permute-start(bf16[128,1024]{1,0:T(8,128)(2,1)S(1)} %get-tuple-element.90), channel_id=1, source_target_pairs={{0,1},{1,0},{2,3},{3,2},{4,5},{5,4},{6,7},{7,6},{8,9},{9,8},{10,11... | collective-permute-start | bytes 786440 | tf_op jit(solution)/shard_map/ppermute | solution.py:43
  108.3 5.5 %collective-permute-start.45 = (bf16[64,1024]{1,0:T(8,128)(2,1)S(1)}, bf16[64,1024]{1,0:T(8,128)(2,1)S(1)}, u32[]{:S(2)}, u32[]{:S(2)}) collective-permute-start(bf16[64,1024]{1,0:T(8,128)(2,1)S(1)} %get-tuple-element.104), channel_id=1, source_target_pairs={{0,4},{2,0},{6,2},{10,6},{14,10},{12,14},{8,12},{4,8},{1,5},{3,1},... | collective-permute-start | bytes 393224 | tf_op jit(solution)/shard_map/ppermute | solution.py:39
  113.2 7.8 %collective-permute-start.39 = (bf16[128,1024]{1,0:T(8,128)(2,1)S(1)}, bf16[128,1024]{1,0:T(8,128)(2,1)S(1)}, u32[]{:S(2)}, u32[]{:S(2)}) collective-permute-start(bf16[128,1024]{1,0:T(8,128)(2,1)S(1)} %add_convert_fusion.6), channel_id=1, source_target_pairs={{0,2},{2,6},{6,10},{10,14},{14,12},{12,8},{8,4},{4,0},{1,3},{3,7},... | collective-permute-start | bytes 786440 | tf_op jit(solution)/shard_map/ppermute | solution.py:39
  113.7 8.0 %collective-permute-start.43 = (bf16[128,1024]{1,0:T(8,128)(2,1)S(1)}, bf16[128,1024]{1,0:T(8,128)(2,1)S(1)}, u32[]{:S(2)}, u32[]{:S(2)}) collective-permute-start(bf16[128,1024]{1,0:T(8,128)(2,1)S(1)} %get-tuple-element.98), channel_id=1, source_target_pairs={{0,1},{1,0},{2,3},{3,2},{4,5},{5,4},{6,7},{7,6},{8,9},{9,8},{10,11... | collective-permute-start | bytes 786440 | tf_op jit(solution)/shard_map/ppermute | solution.py:43
  113.9 8.7 %collective-permute-start.46 = (bf16[128,1024]{1,0:T(8,128)(2,1)S(1)}, bf16[128,1024]{1,0:T(8,128)(2,1)S(1)}, u32[]{:S(2)}, u32[]{:S(2)}) collective-permute-start(bf16[128,1024]{1,0:T(8,128)(2,1)S(1)} %add_convert_fusion.3), channel_id=1, source_target_pairs={{0,4},{2,0},{6,2},{10,6},{14,10},{12,14},{8,12},{4,8},{1,5},{3,1},... | collective-permute-start | bytes 786440 | tf_op jit(solution)/shard_map/ppermute | solution.py:39
  115.5 8.8 %collective-permute-start.34 = (bf16[128,1024]{1,0:T(8,128)(2,1)S(1)}, bf16[128,1024]{1,0:T(8,128)(2,1)S(1)}, u32[]{:S(2)}, u32[]{:S(2)}) collective-permute-start(bf16[128,1024]{1,0:T(8,128)(2,1)S(1)} %get-tuple-element.88), channel_id=1, source_target_pairs={{0,1},{1,0},{2,3},{3,2},{4,5},{5,4},{6,7},{7,6},{8,9},{9,8},{10,11... | collective-permute-start | bytes 786440 | tf_op jit(solution)/shard_map/ppermute | solution.py:43
  115.7 13.0 %collective-permute-start.42 = (bf16[128,1024]{1,0:T(8,128)(2,1)S(1)}, bf16[128,1024]{1,0:T(8,128)(2,1)S(1)}, u32[]{:S(2)}, u32[]{:S(2)}) collective-permute-start(bf16[128,1024]{1,0:T(8,128)(2,1)S(1)} %get-tuple-element.96), channel_id=1, source_target_pairs={{0,1},{1,0},{2,3},{3,2},{4,5},{5,4},{6,7},{7,6},{8,9},{9,8},{10,11... | collective-permute-start | bytes 786440 | tf_op jit(solution)/shard_map/ppermute | solution.py:43
  121.2 6.9 %collective-permute-start.40 = (bf16[128,1024]{1,0:T(8,128)(2,1)S(1)}, bf16[128,1024]{1,0:T(8,128)(2,1)S(1)}, u32[]{:S(2)}, u32[]{:S(2)}) collective-permute-start(bf16[128,1024]{1,0:T(8,128)(2,1)S(1)} %add_convert_fusion.5), channel_id=1, source_target_pairs={{0,2},{2,6},{6,10},{10,14},{14,12},{12,8},{8,4},{4,0},{1,3},{3,7},... | collective-permute-start | bytes 786440 | tf_op jit(solution)/shard_map/ppermute | solution.py:39
  122.7 7.9 %collective-permute-start.47 = (bf16[128,1024]{1,0:T(8,128)(2,1)S(1)}, bf16[128,1024]{1,0:T(8,128)(2,1)S(1)}, u32[]{:S(2)}, u32[]{:S(2)}) collective-permute-start(bf16[128,1024]{1,0:T(8,128)(2,1)S(1)} %add_convert_fusion.2), channel_id=1, source_target_pairs={{0,4},{2,0},{6,2},{10,6},{14,10},{12,14},{8,12},{4,8},{1,5},{3,1},... | collective-permute-start | bytes 786440 | tf_op jit(solution)/shard_map/ppermute | solution.py:39
  124.4 8.1 %collective-permute-start.33 = (bf16[128,1024]{1,0:T(8,128)(2,1)S(1)}, bf16[128,1024]{1,0:T(8,128)(2,1)S(1)}, u32[]{:S(2)}, u32[]{:S(2)}) collective-permute-start(bf16[128,1024]{1,0:T(8,128)(2,1)S(1)} %get-tuple-element.86), channel_id=1, source_target_pairs={{0,1},{1,0},{2,3},{3,2},{4,5},{5,4},{6,7},{7,6},{8,9},{9,8},{10,11... | collective-permute-start | bytes 786440 | tf_op jit(solution)/shard_map/ppermute | solution.py:43
  128.2 6.4 %collective-permute-start.41 = (bf16[128,1024]{1,0:T(8,128)(2,1)S(1)}, bf16[128,1024]{1,0:T(8,128)(2,1)S(1)}, u32[]{:S(2)}, u32[]{:S(2)}) collective-permute-start(bf16[128,1024]{1,0:T(8,128)(2,1)S(1)} %add_convert_fusion.4), channel_id=1, source_target_pairs={{0,2},{2,6},{6,10},{10,14},{14,12},{12,8},{8,4},{4,0},{1,3},{3,7},... | collective-permute-start | bytes 786440 | tf_op jit(solution)/shard_map/ppermute | solution.py:39
  130.8 7.0 %collective-permute-start.48 = (bf16[128,1024]{1,0:T(8,128)(2,1)S(1)}, bf16[128,1024]{1,0:T(8,128)(2,1)S(1)}, u32[]{:S(2)}, u32[]{:S(2)}) collective-permute-start(bf16[128,1024]{1,0:T(8,128)(2,1)S(1)} %add_convert_fusion.1), channel_id=1, source_target_pairs={{0,4},{2,0},{6,2},{10,6},{14,10},{12,14},{8,12},{4,8},{1,5},{3,1},... | collective-permute-start | bytes 786440 | tf_op jit(solution)/shard_map/ppermute | solution.py:39
  (19 other events, 253.5 us)

commit v6 on v5

--- a/solution.py
+++ b/solution.py
@@ -17,8 +17,10 @@
 TOP = 6
 SLOTS = 16
 WIDE = 640
-VMEM_LIMIT = 50 * 1024 * 1024
-DEPTH = 3
+MIB = 1024 * 1024
+VMEM_LIMIT = 50 * MIB
+STAGED = 2
+DEPTH = 2
 PIECES = 2
 SWAP = [(0, 1), (1, 0)]
 FEW = 8
@@ -60,24 +62,27 @@
     return lax.dynamic_index_in_dim(jnp.asarray(table), me, keepdims=False)
 
 
-def gather(block, count):
+def gather(block, count, beside=()):
     if count > FEW:
         found = lax.all_gather(block, "ctx")
-        return list(found), list(swap(found))
+        return list(found), list(swap(found)), list(beside)
     middle = count // 2
-    found, other = [None] * count, [None] * count
+    found, other, made = [None] * count, [None] * count, []
     found[0] = block
     other[0] = swap(block)
     for d in range(1, middle):
         for place, before, ahead in ((d, d - 1, 1), (count - d, (1 - d) % count, -1)):
             arrived = step(found[before], ahead, count)
-            found[place], other[before] = lax.optimization_barrier((arrived, other[before]))
+            extra = beside[d - 1] if ahead == 1 and len(beside) >= d else ()
+            found[place], other[before], extra = lax.optimization_barrier((arrived, other[before], extra))
+            if ahead == 1:
+                made.append(extra)
             other[place] = swap(found[place])
     half = block.shape[0] // 2
     ahead, back = step(found[middle - 1][:half], 1, count), step(found[middle + 1][half:], -1, count)
     found[middle] = jnp.concatenate([ahead, back], axis=0)
     other[middle] = swap(found[middle])
-    return found, other
+    return found, other, made[: len(beside)]
 
 
 def reduce(parts, count):
@@ -95,10 +100,12 @@
     return parts[0]() + ahead.astype(jnp.float32) + back.astype(jnp.float32)
 
 
-def attend_kernel(blocks, where, sources, lengths, order, q_ref, mine_ref, other_ref, up_ref, proj_ref, out_ref, m_ref, l_ref, acc_ref):
+def attend_kernel(count, blocks, info, q_ref, mine_ref, other_ref, up_ref, proj_ref, out_ref, m_ref, l_ref, acc_ref):
     chunk = pl.program_id(0)
-    me, side = where[0], where[1]
-    segs = lengths.shape[0]
+    side = info[1]
+    sources = lambda c: info[2 + c]
+    order = lambda j: info[2 + count + j]
+    segs = info.shape[0] - 2 - 3 * count
     span = mine_ref.shape[1]
     heads, rows, _ = q_ref.shape
 
@@ -109,14 +116,14 @@
         acc_ref[...] = jnp.zeros_like(acc_ref)
 
     row = lax.broadcasted_iota(jnp.int32, (rows, 1), 0)
-    first = order[2 * me] * span
-    second = order[2 * me + 1] * span
+    first = order(2 * sources(0)) * span
+    second = order(2 * sources(0) + 1) * span
     qpos = jnp.where(row < span, first + row, second + row - span)
     low = jnp.zeros((rows, 1), jnp.int32)
     start = jnp.int32(0)
     for m in range(segs):
         low = jnp.where(qpos >= start, start, low)
-        start = start + lengths[m]
+        start = start + info[2 + 3 * count + m]
     keys = blocks * span
     lane = lax.broadcasted_iota(jnp.int32, (1, keys), 1)
     within, which = lane % span, lane // span
@@ -124,8 +131,8 @@
     for half in (side, 1 - side):
         base = jnp.zeros((1, keys), jnp.int32)
         for j in range(blocks):
-            src = sources[chunk * blocks + j]
-            base = jnp.where(which == j, order[2 * src + half] * span, base)
+            src = sources(chunk * blocks + j)
+            base = jnp.where(which == j, order(2 * src + half) * span, base)
         kpos_parts.append(base + within)
     kpos = jnp.concatenate(kpos_parts, axis=1)
     visible = (kpos >= low) & (kpos <= qpos)
@@ -157,26 +164,19 @@
         out_ref[...] = out.astype(jnp.bfloat16)
 
 
-def attend(where, sources, lengths, order, q, mine, other, kv_up, out_proj, count):
+def attend(info, q, mine, other, kv_up, out_proj, count):
     heads, rows, depth = q.shape
     blocks = math.gcd(count, 8)
     span = mine.shape[1]
-    whole2 = lambda i, *_: (0, 0)
-    whole3 = lambda i, *_: (0, 0, 0)
-    lat_spec = pl.BlockSpec((blocks, span, WIDE), lambda i, *_: (i, 0, 0))
+    whole = pl.BlockSpec(memory_space=pltpu.VMEM)
+    lat_spec = whole if blocks == count else pl.BlockSpec((blocks, span, WIDE), lambda i, *_: (i, 0, 0))
     return pl.pallas_call(
-        functools.partial(attend_kernel, blocks),
+        functools.partial(attend_kernel, count, blocks),
         grid_spec=pltpu.PrefetchScalarGridSpec(
-            num_scalar_prefetch=4,
+            num_scalar_prefetch=1,
             grid=(count // blocks,),
-            in_specs=[
-                pl.BlockSpec(q.shape, whole3),
-                lat_spec,
-                lat_spec,
-                pl.BlockSpec(kv_up.shape, whole2),
-                pl.BlockSpec(out_proj.shape, whole2),
-            ],
-            out_specs=pl.BlockSpec((rows, out_proj.shape[1]), whole2),
+            in_specs=[whole, lat_spec, lat_spec, whole, whole],
+            out_specs=whole,
             scratch_shapes=[
                 pltpu.VMEM((heads, rows, 1), jnp.float32),
                 pltpu.VMEM((heads, rows, 1), jnp.float32),
@@ -184,9 +184,38 @@
             ],
         ),
         out_shape=pltpu.VMEM((rows, out_proj.shape[1]), jnp.bfloat16),
-        compiler_params=pltpu.CompilerParams(vmem_limit_bytes=VMEM_LIMIT),
+        compiler_params=pltpu.CompilerParams(vmem_limit_bytes=28 * MIB),
         name="attend",
-    )(where, sources, lengths, order, q, mine, other, kv_up, out_proj)
+    )(info, q, mine, other, kv_up, out_proj)
+
+
+def stage_kernel(picks, *refs):
+    here = len(picks)
+    sems = refs[2 * here]
+    copies = []
+    for i, pick in enumerate(picks):
+        source = refs[i] if pick is None else refs[i].at[pick]
+        piece = source.shape[0] // PIECES
+        for p in range(PIECES):
+            rows = pl.ds(p * piece, piece)
+            copies.append(pltpu.make_async_copy(source.at[rows], refs[here + i].at[rows], sems.at[i, p]))
+    for copy in copies:
+        copy.start()
+    for copy in copies:
+        copy.wait()
+
+
+def stage(arrays, picks):
+    shapes = [x.shape if pick is None else x.shape[1:] for x, pick in zip(arrays, picks)]
+    return pl.pallas_call(
+        functools.partial(stage_kernel, picks),
+        in_specs=[pl.BlockSpec(memory_space=pltpu.HBM)] * len(arrays),
+        out_specs=[pl.BlockSpec(memory_space=pltpu.VMEM)] * len(arrays),
+        scratch_shapes=[pltpu.SemaphoreType.DMA((len(arrays), PIECES))],
+        out_shape=[pltpu.VMEM(shape, x.dtype) for shape, x in zip(shapes, arrays)],
+        compiler_params=pltpu.CompilerParams(vmem_limit_bytes=2 * MIB),
+        name="stage",
+    )(*(pltpu.with_memory_space_constraint(x, pltpu.HBM) for x in arrays))
 
 
 def norm_kernel(where, residual_ref, here_ref, there_ref, gain_ref, middle_ref, normed_ref):
@@ -204,23 +233,24 @@
 def norm(where, residual, here, there, gain):
     rows, width = residual.shape
     half = pltpu.VMEM((rows, width // 2), jnp.bfloat16)
-    full = pl.BlockSpec((rows, width), lambda i, *_: (0, 0))
-    part = pl.BlockSpec((rows, width // 2), lambda i, *_: (0, 0))
+    whole = pl.BlockSpec(memory_space=pltpu.VMEM)
     return pl.pallas_call(
         norm_kernel,
-        grid_spec=pltpu.PrefetchScalarGridSpec(
-            num_scalar_prefetch=1,
-            grid=(1,),
-            in_specs=[full, full, full, pl.BlockSpec((1, width), lambda i, *_: (0, 0))],
-            out_specs=[part, part],
-        ),
+        in_specs=[pl.BlockSpec(memory_space=pltpu.SMEM)] + [whole] * 4,
+        out_specs=[whole, whole],
         out_shape=[half, half],
-        compiler_params=pltpu.CompilerParams(vmem_limit_bytes=VMEM_LIMIT),
+        compiler_params=pltpu.CompilerParams(vmem_limit_bytes=12 * MIB),
         name="norm",
     )(where, residual, here, there, gain)
 
 
-def pack_kernel(where, latent_ref, ids_ref, weights_ref, out_ref, rows):
+def pack_kernel(where, *refs):
+    copies = [pltpu.make_async_copy(refs[i], refs[4 + i], refs[8].at[i]) for i in range(3)]
+    for copy in copies:
+        copy.start()
+    for copy in copies:
+        copy.wait()
+    out_ref, (latent_ref, ids_ref, weights_ref, rows) = refs[3], refs[4:8]
     base, tokens = latent_ref.shape
     span = out_ref.shape[0]
     weights = weights_ref[...]
@@ -240,46 +270,40 @@
 
 def pack(where, latent, expert_ids, route_weights):
     local_rows, base = latent.shape
-    whole = lambda i, *_: (0, 0)
+    arrays = (latent.T, expert_ids.T, route_weights.T)
     return pl.pallas_call(
         pack_kernel,
-        grid_spec=pltpu.PrefetchScalarGridSpec(
-            num_scalar_prefetch=1,
-            grid=(1,),
-            in_specs=[
-                pl.BlockSpec((base, local_rows), whole),
-                pl.BlockSpec((TOP, local_rows), whole),
-                pl.BlockSpec((TOP, local_rows), whole),
-            ],
-            out_specs=pl.BlockSpec((local_rows // 2, WIDE), whole),
-            scratch_shapes=[pltpu.VMEM((WIDE - base, local_rows), jnp.float32)],
-        ),
-        out_shape=jax.ShapeDtypeStruct((local_rows // 2, WIDE), jnp.bfloat16),
-        compiler_params=pltpu.CompilerParams(vmem_limit_bytes=VMEM_LIMIT),
+        in_specs=[pl.BlockSpec(memory_space=pltpu.SMEM)] + [pl.BlockSpec(memory_space=pltpu.HBM)] * 3,
+        out_specs=pl.BlockSpec(memory_space=pltpu.VMEM),
+        scratch_shapes=[pltpu.VMEM(x.shape, x.dtype) for x in arrays]
+        + [pltpu.VMEM((WIDE - base, local_rows), jnp.float32), pltpu.SemaphoreType.DMA((3,))],
+        out_shape=pltpu.VMEM((local_rows // 2, WIDE), jnp.bfloat16),
+        compiler_params=pltpu.CompilerParams(vmem_limit_bytes=4 * MIB),
         name="pack",
-    )(where, latent.T, expert_ids.T, route_weights.T)
-
-
-def expert_rows(rows, gate_ref, up_ref, down_ref, scale_ref):
+    )(where, *(pltpu.with_memory_space_constraint(x, pltpu.HBM) for x in arrays))
+
+
+def expert_rows(rows, gate_ref, up_ref, down_ref, scale):
     by_columns = (((1,), (1,)), ((), ()))
-    gate = lax.dot_general(gate_ref[0], rows, by_columns, preferred_element_type=jnp.float32)
-    upper = lax.dot_general(up_ref[0], rows, by_columns, preferred_element_type=jnp.float32)
-    hidden = (gate / (1.0 + jnp.exp(-gate)) * upper * scale_ref[0]).astype(jnp.bfloat16)
+    gate = lax.dot_general(gate_ref[...], rows, by_columns, preferred_element_type=jnp.float32)
+    upper = lax.dot_general(up_ref[...], rows, by_columns, preferred_element_type=jnp.float32)
+    hidden = (gate / (1.0 + jnp.exp(-gate)) * upper * scale).astype(jnp.bfloat16)
     by_rows = (((0,), (0,)), ((), ()))
-    return lax.dot_general(hidden, down_ref[0], by_rows, preferred_element_type=jnp.float32).astype(jnp.bfloat16)
+    return lax.dot_general(hidden, down_ref[...], by_rows, preferred_element_type=jnp.float32).astype(jnp.bfloat16)
 
 
 def plain_kernel(where, rows_ref, gate_ref, up_ref, down_ref, scale_ref, out_ref):
-    out_ref[0] = expert_rows(rows_ref[0], gate_ref, up_ref, down_ref, scale_ref)
-
-
-def fused_kernel(count, where, *refs):
+    out_ref[0] = expert_rows(rows_ref[0], gate_ref.at[0], up_ref.at[0], down_ref.at[0], scale_ref[0])
+
+
+def fused_kernel(count, staged, where, *refs):
     mine, other = refs[:count], refs[count : 2 * count]
     pick_ref, combine_ref, scale_ref = refs[2 * count : 2 * count + 3]
-    weights = refs[2 * count + 3 : 2 * count + 6]
-    kept, away = refs[2 * count + 6 : 3 * count + 6], refs[3 * count + 6 : 4 * count + 6]
-    picked, held = refs[4 * count + 6 : 4 * count + 8]
-    buffers, sems = refs[4 * count + 8 : 4 * count + 11], refs[4 * count + 11]
+    at = 2 * count + 3
+    early, at = [refs[at + 3 * i : at + 3 * i + 3] for i in range(staged)], at + 3 * staged
+    weights, at = refs[at : at + 3], at + 3
+    kept, away, at = refs[at : at + count], refs[at + count : at + 2 * count], at + 2 * count
+    picked, buffers, sems = refs[at], refs[at + 1 : at + 4], refs[at + 4]
     here = picked.shape[0]
     depth, units, _ = buffers[0].shape
     half = picked.shape[2] // 2
@@ -294,8 +318,8 @@
                 rows = pl.ds(i * piece, piece)
                 yield pltpu.make_async_copy(weights[w].at[expert, rows], buffers[w].at[slot, rows], sems.at[slot, w, i])
 
-    for e in range(depth):
-        for copy in copies(e, e):
+    for i in range(min(depth, here - staged)):
+        for copy in copies(staged + i, i):
             copy.start()
 
     for c in range(count):
@@ -304,15 +328,15 @@
             for e in range(here):
                 picked[e, c * SLOTS : (c + 1) * SLOTS, columns] = rows[e * SLOTS : (e + 1) * SLOTS]
 
-    def work(expert, _):
-        slot = lax.rem(expert, depth)
+    for e in range(staged):
+        picked[e] = expert_rows(picked[e], *early[e], scale_ref[e])
+
+    def work(i, _):
+        slot = lax.rem(i, depth)
+        expert = staged + i
         for copy in copies(expert, slot):
             copy.wait()
-        one = pl.ds(slot, 1)
-        result = expert_rows(picked[expert], *(buffer.at[one] for buffer in buffers), scale_ref.at[pl.ds(expert, 1)])
-        place = pl.ds(pl.multiple_of(expert * SLOTS, SLOTS), SLOTS)
-        for c in range(count):
-            held[c, place, :] = result[c * SLOTS : (c + 1) * SLOTS]
+        picked[expert] = expert_rows(picked[expert], *(buffer.at[slot] for buffer in buffers), scale_ref[expert])
 
         @pl.when(expert + depth < here)
         def _():
@@ -321,10 +345,11 @@
 
         return 0
 
-    lax.fori_loop(0, here, work, 0)
+    lax.fori_loop(0, here - staged, work, 0)
     for c in range(count):
         for columns, out in ((far, away[c]), (near, kept[c])):
-            total = jnp.dot(combine_ref[c], held[c, :, columns], preferred_element_type=jnp.float32)
+            rows = [picked[e, c * SLOTS : (c + 1) * SLOTS, columns] for e in range(here)]
+            total = jnp.dot(combine_ref[c], jnp.concatenate(rows, axis=0), preferred_element_type=jnp.float32)
             out[...] = total.astype(jnp.bfloat16)
 
 
@@ -351,28 +376,26 @@
     )(where, picked, w_gate, w_up, w_down, scale)
 
 
-def experts_fused(where, mine, other, pick, combine, w_gate, w_up, w_down, scale):
+def experts_fused(where, mine, other, pick, combine, scale, early, w_gate, w_up, w_down):
     count, (local, half) = len(mine), mine[0].shape
     here, _, rows = scale.shape
     units = w_gate.shape[1]
     depth = min(DEPTH, here)
     whole = pl.BlockSpec(memory_space=pltpu.VMEM)
     outs = pl.pallas_call(
-        functools.partial(fused_kernel, count),
+        functools.partial(fused_kernel, count, len(early)),
         in_specs=[pl.BlockSpec(memory_space=pltpu.SMEM)]
-        + [whole] * (2 * count + 3)
-        + [pl.BlockSpec(memory_space=pl.ANY)] * 3,
+        + [whole] * (2 * count + 3 + 3 * len(early))
+        + [pl.BlockSpec(memory_space=pltpu.HBM)] * 3,
         out_specs=[whole] * (2 * count),
-        scratch_shapes=[
-            pltpu.VMEM((here, rows, 2 * half), jnp.bfloat16),
-            pltpu.VMEM((count, here * SLOTS, 2 * half), jnp.bfloat16),
-        ]
+        scratch_shapes=[pltpu.VMEM((here, rows, 2 * half), jnp.bfloat16)]
         + [pltpu.VMEM((depth, units, 2 * half), jnp.bfloat16)] * 3
         + [pltpu.SemaphoreType.DMA((depth, 3, PIECES))],
         out_shape=[pltpu.VMEM((local, half), jnp.bfloat16)] * (2 * count),
-        compiler_params=pltpu.CompilerParams(vmem_limit_bytes=VMEM_LIMIT),
+        compiler_params=pltpu.CompilerParams(vmem_limit_bytes=28 * MIB),
         name="experts",
-    )(where, *mine, *other, pick, combine, scale, w_gate, w_up, w_down)
+    )(where, *mine, *other, pick, combine, scale, *sum(early, []),
+      *(pltpu.with_memory_space_constraint(w, pltpu.HBM) for w in (w_gate, w_up, w_down)))
     return outs[:count], outs[count:]
 
 
@@ -400,15 +423,19 @@
     where = jnp.stack([me, side]).astype(jnp.int32)
 
     base = latent.shape[1]
-    sources = sources_of(me, count)
-    found, found_other = gather(pack(where, latent, expert_ids, route_weights), count)
+    w_gate, w_up = w_gate.transpose(0, 2, 1), w_up.transpose(0, 2, 1)
+    packed = pack(where, latent, expert_ids, route_weights)
+    info = jnp.concatenate([where, sources_of(me, count), span_order, seg_lengths])
+    q = queries.reshape(local_rows, heads, NOPE + ROPE).transpose(1, 0, 2)
     gain = norm_gain.reshape(1, width)
-    found[1], gain = lax.optimization_barrier((found[1], gain))
+    ready = stage((kv_up, out_proj, residual), (None, None, None)) if count <= FEW else (kv_up, out_proj, residual)
+    found, found_other, made = gather(packed, count, [(info, q, gain), tuple(ready)])
+    (info, q, gain), (kv_up, out_proj, residual) = made
     mine, other = jnp.stack(found), jnp.stack(found_other)
-
-    q = queries.reshape(local_rows, heads, NOPE + ROPE).transpose(1, 0, 2)
-    partial = attend(where, sources, seg_lengths, span_order, q, mine, other, kv_up, out_proj, count)
-    middle, normed = norm(where, residual, partial, swap(partial), gain)
+    partial = attend(info, q, mine, other, kv_up, out_proj, count)
+    there = swap(partial)
+    mine, other, partial = lax.optimization_barrier((mine, other, partial))
+    middle, normed = norm(where, residual, partial, there, gain)
 
     facts_mine, facts_other = mine[:, :, base : base + 3 * TOP], other[:, :, base : base + 3 * TOP]
     facts = jnp.concatenate(
@@ -430,11 +457,11 @@
     combine = combine.astype(jnp.bfloat16).reshape(count, local_rows, here * SLOTS)
     pick = combine.transpose(0, 2, 1)
 
-    got, got_other = gather(normed, count)
-    got[1], pick, combine, scale = lax.optimization_barrier((got[1], pick, combine, scale))
-    w_gate, w_up = w_gate.transpose(0, 2, 1), w_up.transpose(0, 2, 1)
+    early = [()] * STAGED if count > FEW else [stage((w_gate, w_up, w_down), (e, e, e)) for e in range(STAGED)]
+    got, got_other, made = gather(normed, count, [(pick, combine, scale)] + [tuple(x) for x in early])
+    (pick, combine, scale), early = made[0], [list(x) for x in made[1:]]
     if count <= FEW:
-        kept, away = experts_fused(where, got, got_other, pick, combine, w_gate, w_up, w_down, scale)
+        kept, away = experts_fused(where, got, got_other, pick, combine, scale, early, w_gate, w_up, w_down)
     else:
         near, far = jnp.stack(got), jnp.stack(got_other)
         full = jnp.concatenate([jnp.where(side == 0, near, far), jnp.where(side == 0, far, near)], axis=2)

time: 139 us -> 152 us (1.094)
  local copies, waits for them, and re-layouts: 12.2 us -> 35.8 us
  waiting for transfers between devices: 57.9 us -> 41 us
  Pallas kernels: 34.7 us -> 40.3 us
    unnamed x53 -> x77, local copies, waits for them, and re-layouts: 8.41 us -> 28.9 us
    ppermute x24, waiting for transfers between devices: 53.8 us -> 38 us  [step(): lax.ppermute(value, 'ctx', [(cycle[p], cycle[(p + ahead) % count]) for p...]
    pallas_call x4 -> x7, Pallas kernels: 34.7 us -> 40.3 us  [the longest x1 23.9 us: experts_fused(): pl.pallas_call(functools.partial(fused_kernel, count, len(early)), in_spe...]
  transfers between devices with their start and end apart: 49 -> 49, of which waited for: 23 -> 19; matrix products, arithmetic and copies ran while one was open for 5% -> 7% of each run, Pallas kernels for 0% -> 6%
where the time goes in v6:
time: 152 us; the launch traced here: 151 us
  waiting for transfers between devices  41 us (27%)
  Pallas kernels  40.3 us (27%)
  local copies, waits for them, and re-layouts  35.8 us (24%)
  starting transfers between devices  30.1 us (20%)
  other arithmetic  3.28 us (2%)
    ppermute x24, waiting for transfers between devices, step(): lax.ppermute(value, 'ctx', [(cycle[p], cycle[(p + ahead) % count]) for p...  38 us
    unnamed x77, local copies, waits for them, and re-layouts  28.9 us
    ppermute x24, starting transfers between devices, step(): lax.ppermute(value, 'ctx', [(cycle[p], cycle[(p + ahead) % count]) for p...  26.3 us
    pallas_call x1, Pallas kernels, experts_fused(): pl.pallas_call(functools.partial(fused_kernel, count, len(early)), in_spe...  23.9 us
    pallas_call x3, Pallas kernels, stage(): pl.pallas_call(functools.partial(stage_kernel, picks), in_specs=[pl.Block...  9.19 us
    pallas_call x1, Pallas kernels, attend(): pl.pallas_call(functools.partial(attend_kernel, count, blocks), grid_spec...  4.57 us
    ppermute x25, starting transfers between devices, swap(): return lax.ppermute(value, 'exp', SWAP)  3.8 us
  transfers between devices with their start and end apart: 49, of which 19 were waited for; matrix products, arithmetic and copies ran while one was open for 7% of the time, Pallas kernels for 6%

profile of v6, /device:TPU:0, one launch (start us, length us, event | category | flops | bytes accessed | tf_op | source)
XLA Modules:
  0.0 151.2 jit_solution(95873761924222832)
XLA Ops:
  0.1 1.7 %pack.1 = bf16[64,640]{1,0:T(8,128)(2,1)S(1)} custom-call(s32[2]{0:T(128)S(1)} %pad_add_fusion.where, bf16[576,128]{1,0:T(8,128)(2,1)} %bitcast.64, s32[6,128]{1,0:T(8,128)} %bitcast.66, f32[6,128]{1,0:T(8,128)} %bitcast.67), custom_call_target="tpu_custom_call" | custom-call | tf_op jit(solution)/shard_map/pack/pallas_call | solution.py:274
  1.8 3.1 %collective-permute-start.7 = (bf16[64,640]{1,0:T(8,128)(2,1)S(1)}, bf16[64,640]{1,0:T(8,128)(2,1)S(1)}, u32[]{:S(2)}, u32[]{:S(2)}) collective-permute-start(bf16[64,640]{1,0:T(8,128)(2,1)S(1)} %pack.1), channel_id=1, source_target_pairs={{0,4},{2,0},{6,2},{10,6},{14,10},{12,14},{8,12},{4,8},{1,5},{3,1},... | collective-permute-start | bytes 245768 | tf_op jit(solution)/shard_map/ppermute | solution.py:41
  5.7 1.1 copy.30
  8.4 2.0 %stage.3 = (bf16[512,1024]{1,0:T(8,128)(2,1)S(1)}, bf16[512,2048]{1,0:T(8,128)(2,1)S(1)}, bf16[128,2048]{1,0:T(8,128)(2,1)S(1)}) custom-call(bf16[512,1024]{1,0:T(8,128)(2,1)} %refs_0_.1, bf16[512,2048]{1,0:T(8,128)(2,1)} %refs_1_.1, bf16[128,2048]{1,0:T(8,128)(2,1)} %refs_2_.3), custom_call_target="tpu_custom_call" | custom-call | tf_op jit(solution)/shard_map/stage/pallas_call | solution.py:210
  11.0 1.7 %collective-permute-start.8 = (bf16[64,640]{1,0:T(8,128)(2,1)S(1)}, bf16[64,640]{1,0:T(8,128)(2,1)S(1)}, u32[]{:S(2)}, u32[]{:S(2)}) collective-permute-start(bf16[64,640]{1,0:T(8,128)(2,1)S(1)} %collective-permute-done.7), channel_id=1, source_target_pairs={{0,4},{2,0},{6,2},{10,6},{14,10},{12,14},{8,12},{4,8},{1,5},{3,1},... | collective-permute-start | bytes 245768 | tf_op jit(solution)/shard_map/ppermute | solution.py:41
  13.1 2.5 %collective-permute-done.8 = bf16[64,640]{1,0:T(8,128)(2,1)S(1)} collective-permute-done((bf16[64,640]{1,0:T(8,128)(2,1)S(1)}, bf16[64,640]{1,0:T(8,128)(2,1)S(1)}, u32[]{:S(2)}, u32[]{:S(2)}) %collective-permute-start.8) | collective-permute-done | bytes 81952 | tf_op jit(solution)/shard_map/ppermute | solution.py:41
  15.6 1.8 %collective-permute-start.10 = (bf16[64,640]{1,0:T(8,128)(2,1)S(1)}, bf16[64,640]{1,0:T(8,128)(2,1)S(1)}, u32[]{:S(2)}, u32[]{:S(2)}) collective-permute-start(bf16[64,640]{1,0:T(8,128)(2,1)S(1)} %collective-permute-done.8), channel_id=1, source_target_pairs={{0,4},{2,0},{6,2},{10,6},{14,10},{12,14},{8,12},{4,8},{1,5},{3,1},... | collective-permute-start | bytes 245768 | tf_op jit(solution)/shard_map/ppermute | solution.py:41
  17.9 2.5 %collective-permute-done.10 = bf16[64,640]{1,0:T(8,128)(2,1)S(1)} collective-permute-done((bf16[64,640]{1,0:T(8,128)(2,1)S(1)}, bf16[64,640]{1,0:T(8,128)(2,1)S(1)}, u32[]{:S(2)}, u32[]{:S(2)}) %collective-permute-start.10) | collective-permute-done | bytes 81952 | tf_op jit(solution)/shard_map/ppermute | solution.py:41
  20.4 2.0 %collective-permute-done.4 = bf16[64,640]{1,0:T(8,128)(2,1)S(1)} collective-permute-done((bf16[64,640]{1,0:T(8,128)(2,1)S(1)}, bf16[64,640]{1,0:T(8,128)(2,1)S(1)}, u32[]{:S(2)}, u32[]{:S(2)}) %collective-permute-start.4) | collective-permute-done | bytes 81952 | tf_op jit(solution)/shard_map/ppermute | solution.py:41
  22.5 1.6 %collective-permute-start.12 = (bf16[32,640]{1,0:T(8,128)(2,1)S(1)}, bf16[32,640]{1,0:T(8,128)(2,1)S(1)}, u32[]{:S(2)}, u32[]{:S(2)}) collective-permute-start(bf16[32,640]{1,0:T(8,128)(2,1)S(1)} %slice.34), channel_id=1, source_target_pairs={{0,4},{2,0},{6,2},{10,6},{14,10},{12,14},{8,12},{4,8},{1,5},{3,1},... | collective-permute-start | bytes 122888 | tf_op jit(solution)/shard_map/ppermute | solution.py:41
  24.6 3.5 %collective-permute-done.6 = bf16[32,640]{1,0:T(8,128)(2,1)S(1)} collective-permute-done((bf16[32,640]{1,0:T(8,128)(2,1)S(1)}, bf16[32,640]{1,0:T(8,128)(2,1)S(1)}, u32[]{:S(2)}, u32[]{:S(2)}) %collective-permute-start.6) | collective-permute-done | bytes 40992 | tf_op jit(solution)/shard_map/ppermute | solution.py:41
  28.4 1.2 collective-permute-done.14
  29.6 4.6 %attend.1.here_ref = bf16[128,2048]{1,0:T(8,128)(2,1)S(1)} custom-call(s32[42]{0:T(128)S(1)} %concatenate.19.info, bf16[4,128,192]{2,1,0:T(8,128)(2,1)S(1)} %bitcast.55, bf16[8,64,640]{2,1,0:T(8,128)(2,1)S(1)} %bitcast_dynamic-update-slice_fusion.8.mine_ref, bf16[8,64,640]{2,1,0:T(8,128)(2,1)S(1)} %bitcast_dynamic-update-slice_fusion.other_ref, ...), custom_call_target="tpu_custom_call" | custom-call | tf_op jit(solution)/shard_map/attend/pallas_call | solution.py:173
  36.4 1.0 norm.1
  39.3 1.6 %collective-permute-start.24 = (bf16[128,1024]{1,0:T(8,128)(2,1)S(1)}, bf16[128,1024]{1,0:T(8,128)(2,1)S(1)}, u32[]{:S(2)}, u32[]{:S(2)}) collective-permute-start(bf16[128,1024]{1,0:T(8,128)(2,1)S(1)} %get-tuple-element.97.refs_0_), channel_id=1, source_target_pairs={{0,4},{2,0},{6,2},{10,6},{14,10},{12,14},{8,12},{4,8},{1,5},{3,1},... | collective-permute-start | bytes 786440 | tf_op jit(solution)/shard_map/ppermute | solution.py:41
  41.7 5.2 %collective-permute-done.17.refs_1_ = bf16[128,1024]{1,0:T(8,128)(2,1)} collective-permute-done((bf16[128,1024]{1,0:T(8,128)(2,1)S(1)}, bf16[128,1024]{1,0:T(8,128)(2,1)}, u32[]{:S(2)}, u32[]{:S(2)}) %collective-permute-start.17) | collective-permute-done | bytes 262176 | tf_op jit(solution)/shard_map/ppermute | solution.py:41
  47.6 1.6 %collective-permute-start.25 = (bf16[128,1024]{1,0:T(8,128)(2,1)S(1)}, bf16[128,1024]{1,0:T(8,128)(2,1)S(1)}, u32[]{:S(2)}, u32[]{:S(2)}) collective-permute-start(bf16[128,1024]{1,0:T(8,128)(2,1)S(1)} %collective-permute-done.24.refs_7_), channel_id=1, source_target_pairs={{0,4},{2,0},{6,2},{10,6},{14,10},{12,14},{8,12},{4,8},{1,5},{3,1},... | collective-permute-start | bytes 786440 | tf_op jit(solution)/shard_map/ppermute | solution.py:41
  49.2 3.6 %stage.4 = (bf16[704,2048]{1,0:T(8,128)(2,1)S(1)}, bf16[704,2048]{1,0:T(8,128)(2,1)S(1)}, bf16[704,2048]{1,0:T(8,128)(2,1)S(1)}) custom-call(bf16[8,704,2048]{2,1,0:T(8,128)(2,1)} %bitcast.56, bf16[8,704,2048]{2,1,0:T(8,128)(2,1)} %bitcast.59, bf16[8,704,2048]{2,1,0:T(8,128)(2,1)} %refs_27_.1), custom_call_target="tpu_custom_call" | custom-call | tf_op jit(solution)/shard_map/stage/pallas_call | solution.py:210
  52.8 1.5 %copy-done = bf16[704,2048]{1,0:T(8,128)(2,1)} copy-done((bf16[704,2048]{1,0:T(8,128)(2,1)}, bf16[704,2048]{1,0:T(8,128)(2,1)S(1)}, u32[]{:S(2)}) %copy-start) | copy-done | bytes 2883608
  54.3 1.6 %copy-done.2 = bf16[704,2048]{1,0:T(8,128)(2,1)} copy-done((bf16[704,2048]{1,0:T(8,128)(2,1)}, bf16[704,2048]{1,0:T(8,128)(2,1)S(1)}, u32[]{:S(2)}) %copy-start.2) | copy-done | bytes 2883608
  56.7 1.6 %collective-permute-start.27 = (bf16[128,1024]{1,0:T(8,128)(2,1)S(1)}, bf16[128,1024]{1,0:T(8,128)(2,1)}, u32[]{:S(2)}, u32[]{:S(2)}) collective-permute-start(bf16[128,1024]{1,0:T(8,128)(2,1)S(1)} %collective-permute-done.25.refs_6_), channel_id=1, source_target_pairs={{0,4},{2,0},{6,2},{10,6},{14,10},{12,14},{8,12},{4,8},{1,5},{3,1},... | collective-permute-start | bytes 786440 | tf_op jit(solution)/shard_map/ppermute | solution.py:41
  58.3 3.6 %stage.5 = (bf16[704,2048]{1,0:T(8,128)(2,1)S(1)}, bf16[704,2048]{1,0:T(8,128)(2,1)S(1)}, bf16[704,2048]{1,0:T(8,128)(2,1)S(1)}) custom-call(bf16[8,704,2048]{2,1,0:T(8,128)(2,1)} %bitcast.57, bf16[8,704,2048]{2,1,0:T(8,128)(2,1)} %bitcast.60, bf16[8,704,2048]{2,1,0:T(8,128)(2,1)} %refs_27_.1), custom_call_target="tpu_custom_call" | custom-call | tf_op jit(solution)/shard_map/stage/pallas_call | solution.py:210
  62.0 1.6 %copy-done.4 = bf16[704,2048]{1,0:T(8,128)(2,1)} copy-done((bf16[704,2048]{1,0:T(8,128)(2,1)}, bf16[704,2048]{1,0:T(8,128)(2,1)S(1)}, u32[]{:S(2)}) %copy-start.4) | copy-done | bytes 2883608
  63.6 1.6 %copy-done.6 = bf16[704,2048]{1,0:T(8,128)(2,1)} copy-done((bf16[704,2048]{1,0:T(8,128)(2,1)}, bf16[704,2048]{1,0:T(8,128)(2,1)S(1)}, u32[]{:S(2)}) %copy-start.6) | copy-done | bytes 2883608
  65.2 1.6 %copy-done.8 = bf16[704,2048]{1,0:T(8,128)(2,1)} copy-done((bf16[704,2048]{1,0:T(8,128)(2,1)}, bf16[704,2048]{1,0:T(8,128)(2,1)S(1)}, u32[]{:S(2)}) %copy-start.8) | copy-done | bytes 2883608
  66.8 1.0 slice.40
  68.3 1.0 slice.41
  69.3 1.8 %collective-permute-start.29 = (bf16[64,1024]{1,0:T(8,128)(2,1)S(1)}, bf16[64,1024]{1,0:T(8,128)(2,1)S(1)}, u32[]{:S(2)}, u32[]{:S(2)}) collective-permute-start(bf16[64,1024]{1,0:T(8,128)(2,1)S(1)} %slice.41), channel_id=1, source_target_pairs={{0,4},{2,0},{6,2},{10,6},{14,10},{12,14},{8,12},{4,8},{1,5},{3,1},... | collective-permute-start | bytes 393224 | tf_op jit(solution)/shard_map/ppermute | solution.py:41
  71.6 1.7 %collective-permute-done.23 = bf16[64,1024]{1,0:T(8,128)(2,1)S(1)} collective-permute-done((bf16[64,1024]{1,0:T(8,128)(2,1)S(1)}, bf16[64,1024]{1,0:T(8,128)(2,1)S(1)}, u32[]{:S(2)}, u32[]{:S(2)}) %collective-permute-start.23) | collective-permute-done | bytes 131104 | tf_op jit(solution)/shard_map/ppermute | solution.py:41
  75.4 1.1 copy.38.refs_16_
  77.3 1.8 %copy-done.1 = bf16[704,2048]{1,0:T(8,128)(2,1)S(1)} copy-done((bf16[704,2048]{1,0:T(8,128)(2,1)S(1)}, bf16[704,2048]{1,0:T(8,128)(2,1)}, u32[]{:S(2)}) %copy-start.1) | copy-done | bytes 2883608
  79.1 1.8 %copy-done.3 = bf16[704,2048]{1,0:T(8,128)(2,1)S(1)} copy-done((bf16[704,2048]{1,0:T(8,128)(2,1)S(1)}, bf16[704,2048]{1,0:T(8,128)(2,1)}, u32[]{:S(2)}) %copy-start.3) | copy-done | bytes 2883608
  80.9 1.8 %copy-done.5 = bf16[704,2048]{1,0:T(8,128)(2,1)S(1)} copy-done((bf16[704,2048]{1,0:T(8,128)(2,1)S(1)}, bf16[704,2048]{1,0:T(8,128)(2,1)}, u32[]{:S(2)}) %copy-start.5) | copy-done | bytes 2883608
  82.7 1.8 %copy-done.7 = bf16[704,2048]{1,0:T(8,128)(2,1)S(1)} copy-done((bf16[704,2048]{1,0:T(8,128)(2,1)S(1)}, bf16[704,2048]{1,0:T(8,128)(2,1)}, u32[]{:S(2)}) %copy-start.7) | copy-done | bytes 2883608
  84.5 1.8 %copy-done.9 = bf16[704,2048]{1,0:T(8,128)(2,1)S(1)} copy-done((bf16[704,2048]{1,0:T(8,128)(2,1)S(1)}, bf16[704,2048]{1,0:T(8,128)(2,1)}, u32[]{:S(2)}) %copy-start.9) | copy-done | bytes 2883608
  94.9 23.9 %experts.1 = (bf16[128,1024]{1,0:T(8,128)(2,1)S(1)}, bf16[128,1024]{1,0:T(8,128)(2,1)S(1)}, bf16[128,1024]{1,0:T(8,128)(2,1)S(1)}, bf16[128,1024]{1,0:T(8,128)(2...) custom-call(s32[2]{0:T(128)S(1)} %pad_add_fusion.where, ...), custom_call_target="tpu_custom_call" | custom-call | tf_op jit(solution)/shard_map/experts/pallas_call | solution.py:385
  119.3 1.0 collective-permute-done.37
  121.4 1.7 %collective-permute-start.45 = (bf16[64,1024]{1,0:T(8,128)(2,1)S(1)}, bf16[64,1024]{1,0:T(8,128)(2,1)S(1)}, u32[]{:S(2)}, u32[]{:S(2)}) collective-permute-start(bf16[64,1024]{1,0:T(8,128)(2,1)S(1)} %get-tuple-element.146), channel_id=1, source_target_pairs={{0,4},{2,0},{6,2},{10,6},{14,10},{12,14},{8,12},{4,8},{1,5},{3,1},... | collective-permute-start | bytes 393224 | tf_op jit(solution)/shard_map/ppermute | solution.py:41
  123.1 3.0 %collective-permute-done.38 = bf16[64,1024]{1,0:T(8,128)(2,1)S(1)} collective-permute-done((bf16[64,1024]{1,0:T(8,128)(2,1)S(1)}, bf16[64,1024]{1,0:T(8,128)(2,1)S(1)}, u32[]{:S(2)}, u32[]{:S(2)}) %collective-permute-start.38) | collective-permute-done | bytes 131104 | tf_op jit(solution)/shard_map/ppermute | solution.py:41
  126.9 1.7 %collective-permute-start.46 = (bf16[128,1024]{1,0:T(8,128)(2,1)S(1)}, bf16[128,1024]{1,0:T(8,128)(2,1)S(1)}, u32[]{:S(2)}, u32[]{:S(2)}) collective-permute-start(bf16[128,1024]{1,0:T(8,128)(2,1)S(1)} %add_convert_fusion.3), channel_id=1, source_target_pairs={{0,4},{2,0},{6,2},{10,6},{14,10},{12,14},{8,12},{4,8},{1,5},{3,1},... | collective-permute-start | bytes 786440 | tf_op jit(solution)/shard_map/ppermute | solution.py:41
  129.1 4.6 %collective-permute-done.39 = bf16[128,1024]{1,0:T(8,128)(2,1)S(1)} collective-permute-done((bf16[128,1024]{1,0:T(8,128)(2,1)S(1)}, bf16[128,1024]{1,0:T(8,128)(2,1)S(1)}, u32[]{:S(2)}, u32[]{:S(2)}) %collective-permute-start.39) | collective-permute-done | bytes 262176 | tf_op jit(solution)/shard_map/ppermute | solution.py:41
  134.3 1.2 collective-permute-done.46
  135.6 1.7 %collective-permute-start.47 = (bf16[128,1024]{1,0:T(8,128)(2,1)S(1)}, bf16[128,1024]{1,0:T(8,128)(2,1)S(1)}, u32[]{:S(2)}, u32[]{:S(2)}) collective-permute-start(bf16[128,1024]{1,0:T(8,128)(2,1)S(1)} %add_convert_fusion.2), channel_id=1, source_target_pairs={{0,4},{2,0},{6,2},{10,6},{14,10},{12,14},{8,12},{4,8},{1,5},{3,1},... | collective-permute-start | bytes 786440 | tf_op jit(solution)/shard_map/ppermute | solution.py:41
  137.3 3.2 %collective-permute-done.40 = bf16[128,1024]{1,0:T(8,128)(2,1)S(1)} collective-permute-done((bf16[128,1024]{1,0:T(8,128)(2,1)S(1)}, bf16[128,1024]{1,0:T(8,128)(2,1)S(1)}, u32[]{:S(2)}, u32[]{:S(2)}) %collective-permute-start.40) | collective-permute-done | bytes 262176 | tf_op jit(solution)/shard_map/ppermute | solution.py:41
  141.0 2.3 %collective-permute-done.47 = bf16[128,1024]{1,0:T(8,128)(2,1)S(1)} collective-permute-done((bf16[128,1024]{1,0:T(8,128)(2,1)S(1)}, bf16[128,1024]{1,0:T(8,128)(2,1)S(1)}, u32[]{:S(2)}, u32[]{:S(2)}) %collective-permute-start.47) | collective-permute-done | bytes 262176 | tf_op jit(solution)/shard_map/ppermute | solution.py:41
  143.4 1.7 %collective-permute-start.48 = (bf16[128,1024]{1,0:T(8,128)(2,1)S(1)}, bf16[128,1024]{1,0:T(8,128)(2,1)S(1)}, u32[]{:S(2)}, u32[]{:S(2)}) collective-permute-start(bf16[128,1024]{1,0:T(8,128)(2,1)S(1)} %add_convert_fusion.1), channel_id=1, source_target_pairs={{0,4},{2,0},{6,2},{10,6},{14,10},{12,14},{8,12},{4,8},{1,5},{3,1},... | collective-permute-start | bytes 786440 | tf_op jit(solution)/shard_map/ppermute | solution.py:41
  145.2 1.9 %collective-permute-done.41 = bf16[128,1024]{1,0:T(8,128)(2,1)S(1)} collective-permute-done((bf16[128,1024]{1,0:T(8,128)(2,1)S(1)}, bf16[128,1024]{1,0:T(8,128)(2,1)S(1)}, u32[]{:S(2)}, u32[]{:S(2)}) %collective-permute-start.41) | collective-permute-done | bytes 262176 | tf_op jit(solution)/shard_map/ppermute | solution.py:41
  147.1 3.2 %collective-permute-done.48 = bf16[128,1024]{1,0:T(8,128)(2,1)S(1)} collective-permute-done((bf16[128,1024]{1,0:T(8,128)(2,1)S(1)}, bf16[128,1024]{1,0:T(8,128)(2,1)S(1)}, u32[]{:S(2)}, u32[]{:S(2)}) %collective-permute-start.48) | collective-permute-done | bytes 262176 | tf_op jit(solution)/shard_map/ppermute | solution.py:41
  (178 shorter events, 28.5 us)
Async XLA Ops:
  1.8 8.7 %collective-permute-start.7 = (bf16[64,640]{1,0:T(8,128)(2,1)S(1)}, bf16[64,640]{1,0:T(8,128)(2,1)S(1)}, u32[]{:S(2)}, u32[]{:S(2)}) collective-permute-start(bf16[64,640]{1,0:T(8,128)(2,1)S(1)} %pack.1), channel_id=1, source_target_pairs={{0,4},{2,0},{6,2},{10,6},{14,10},{12,14},{8,12},{4,8},{1,5},{3,1},... | collective-permute-start | bytes 245768 | tf_op jit(solution)/shard_map/ppermute | solution.py:41
  4.8 5.6 %collective-permute-start.1 = (bf16[64,640]{1,0:T(8,128)(2,1)S(1)}, bf16[64,640]{1,0:T(8,128)(2,1)S(1)}, u32[]{:S(2)}, u32[]{:S(2)}) collective-permute-start(bf16[64,640]{1,0:T(8,128)(2,1)S(1)} %pack.1), channel_id=1, source_target_pairs={{0,1},{1,0},{2,3},{3,2},{4,5},{5,4},{6,7},{7,6},{8,9},{9,8},{10,11... | collective-permute-start | bytes 245768 | tf_op jit(solution)/shard_map/ppermute | solution.py:45
  4.8 5.6 %collective-permute-start = (bf16[64,640]{1,0:T(8,128)(2,1)S(1)}, bf16[64,640]{1,0:T(8,128)(2,1)S(1)}, u32[]{:S(2)}, u32[]{:S(2)}) collective-permute-start(bf16[64,640]{1,0:T(8,128)(2,1)S(1)} %pack.1), channel_id=1, source_target_pairs={{0,2},{2,6},{6,10},{10,14},{14,12},{12,8},{8,4},{4,0},{1,3},{3,7},... | collective-permute-start | bytes 245768 | tf_op jit(solution)/shard_map/ppermute | solution.py:41
  10.5 2.6 %collective-permute-start.9 = (bf16[64,640]{1,0:T(8,128)(2,1)S(1)}, bf16[64,640]{1,0:T(8,128)(2,1)S(1)}, u32[]{:S(2)}, u32[]{:S(2)}) collective-permute-start(bf16[64,640]{1,0:T(8,128)(2,1)S(1)} %collective-permute-done.7), channel_id=1, source_target_pairs={{0,1},{1,0},{2,3},{3,2},{4,5},{5,4},{6,7},{7,6},{8,9},{9,8},{10,11... | collective-permute-start | bytes 245768 | tf_op jit(solution)/shard_map/ppermute | solution.py:45
  11.0 4.6 %collective-permute-start.8 = (bf16[64,640]{1,0:T(8,128)(2,1)S(1)}, bf16[64,640]{1,0:T(8,128)(2,1)S(1)}, u32[]{:S(2)}, u32[]{:S(2)}) collective-permute-start(bf16[64,640]{1,0:T(8,128)(2,1)S(1)} %collective-permute-done.7), channel_id=1, source_target_pairs={{0,4},{2,0},{6,2},{10,6},{14,10},{12,14},{8,12},{4,8},{1,5},{3,1},... | collective-permute-start | bytes 245768 | tf_op jit(solution)/shard_map/ppermute | solution.py:41
  12.7 4.6 %collective-permute-start.3 = (bf16[64,640]{1,0:T(8,128)(2,1)S(1)}, bf16[64,640]{1,0:T(8,128)(2,1)S(1)}, u32[]{:S(2)}, u32[]{:S(2)}) collective-permute-start(bf16[64,640]{1,0:T(8,128)(2,1)S(1)} %collective-permute-done), channel_id=1, source_target_pairs={{0,1},{1,0},{2,3},{3,2},{4,5},{5,4},{6,7},{7,6},{8,9},{9,8},{10,11... | collective-permute-start | bytes 245768 | tf_op jit(solution)/shard_map/ppermute | solution.py:45
  12.7 4.9 %collective-permute-start.2 = (bf16[64,640]{1,0:T(8,128)(2,1)S(1)}, bf16[64,640]{1,0:T(8,128)(2,1)S(1)}, u32[]{:S(2)}, u32[]{:S(2)}) collective-permute-start(bf16[64,640]{1,0:T(8,128)(2,1)S(1)} %collective-permute-done), channel_id=1, source_target_pairs={{0,2},{2,6},{6,10},{10,14},{14,12},{12,8},{8,4},{4,0},{1,3},{3,7},... | collective-permute-start | bytes 245768 | tf_op jit(solution)/shard_map/ppermute | solution.py:41
  15.6 2.4 %collective-permute-start.11 = (bf16[64,640]{1,0:T(8,128)(2,1)S(1)}, bf16[64,640]{1,0:T(8,128)(2,1)S(1)}, u32[]{:S(2)}, u32[]{:S(2)}) collective-permute-start(bf16[64,640]{1,0:T(8,128)(2,1)S(1)} %collective-permute-done.8), channel_id=1, source_target_pairs={{0,1},{1,0},{2,3},{3,2},{4,5},{5,4},{6,7},{7,6},{8,9},{9,8},{10,11... | collective-permute-start | bytes 245768 | tf_op jit(solution)/shard_map/ppermute | solution.py:45
  15.6 4.9 %collective-permute-start.10 = (bf16[64,640]{1,0:T(8,128)(2,1)S(1)}, bf16[64,640]{1,0:T(8,128)(2,1)S(1)}, u32[]{:S(2)}, u32[]{:S(2)}) collective-permute-start(bf16[64,640]{1,0:T(8,128)(2,1)S(1)} %collective-permute-done.8), channel_id=1, source_target_pairs={{0,4},{2,0},{6,2},{10,6},{14,10},{12,14},{8,12},{4,8},{1,5},{3,1},... | collective-permute-start | bytes 245768 | tf_op jit(solution)/shard_map/ppermute | solution.py:41
  17.6 2.8 %collective-permute-start.5 = (bf16[64,640]{1,0:T(8,128)(2,1)S(1)}, bf16[64,640]{1,0:T(8,128)(2,1)S(1)}, u32[]{:S(2)}, u32[]{:S(2)}) collective-permute-start(bf16[64,640]{1,0:T(8,128)(2,1)S(1)} %collective-permute-done.2), channel_id=1, source_target_pairs={{0,1},{1,0},{2,3},{3,2},{4,5},{5,4},{6,7},{7,6},{8,9},{9,8},{10,11... | collective-permute-start | bytes 245768 | tf_op jit(solution)/shard_map/ppermute | solution.py:45
  17.6 4.8 %collective-permute-start.4 = (bf16[64,640]{1,0:T(8,128)(2,1)S(1)}, bf16[64,640]{1,0:T(8,128)(2,1)S(1)}, u32[]{:S(2)}, u32[]{:S(2)}) collective-permute-start(bf16[64,640]{1,0:T(8,128)(2,1)S(1)} %collective-permute-done.2), channel_id=1, source_target_pairs={{0,2},{2,6},{6,10},{10,14},{14,12},{12,8},{8,4},{4,0},{1,3},{3,7},... | collective-permute-start | bytes 245768 | tf_op jit(solution)/shard_map/ppermute | solution.py:41
  20.4 9.1 %collective-permute-start.15 = (bf16[64,640]{1,0:T(8,128)(2,1)S(1)}, bf16[64,640]{1,0:T(8,128)(2,1)S(1)}, u32[]{:S(2)}, u32[]{:S(2)}) collective-permute-start(bf16[64,640]{1,0:T(8,128)(2,1)S(1)} %collective-permute-done.10), channel_id=1, source_target_pairs={{0,1},{1,0},{2,3},{3,2},{4,5},{5,4},{6,7},{7,6},{8,9},{9,8},{10,11... | collective-permute-start | bytes 245768 | tf_op jit(solution)/shard_map/ppermute | solution.py:45
  22.5 5.9 %collective-permute-start.13 = (bf16[64,640]{1,0:T(8,128)(2,1)S(1)}, bf16[64,640]{1,0:T(8,128)(2,1)S(1)}, u32[]{:S(2)}, u32[]{:S(2)}) collective-permute-start(bf16[64,640]{1,0:T(8,128)(2,1)S(1)} %collective-permute-done.4), channel_id=1, source_target_pairs={{0,1},{1,0},{2,3},{3,2},{4,5},{5,4},{6,7},{7,6},{8,9},{9,8},{10,11... | collective-permute-start | bytes 245768 | tf_op jit(solution)/shard_map/ppermute | solution.py:45
  22.5 5.7 %collective-permute-start.12 = (bf16[32,640]{1,0:T(8,128)(2,1)S(1)}, bf16[32,640]{1,0:T(8,128)(2,1)S(1)}, u32[]{:S(2)}, u32[]{:S(2)}) collective-permute-start(bf16[32,640]{1,0:T(8,128)(2,1)S(1)} %slice.34), channel_id=1, source_target_pairs={{0,4},{2,0},{6,2},{10,6},{14,10},{12,14},{8,12},{4,8},{1,5},{3,1},... | collective-permute-start | bytes 122888 | tf_op jit(solution)/shard_map/ppermute | solution.py:41
  24.1 4.1 %collective-permute-start.6 = (bf16[32,640]{1,0:T(8,128)(2,1)S(1)}, bf16[32,640]{1,0:T(8,128)(2,1)S(1)}, u32[]{:S(2)}, u32[]{:S(2)}) collective-permute-start(bf16[32,640]{1,0:T(8,128)(2,1)S(1)} %slice.33), channel_id=1, source_target_pairs={{0,2},{2,6},{6,10},{10,14},{14,12},{12,8},{8,4},{4,0},{1,3},{3,7},... | collective-permute-start | bytes 122888 | tf_op jit(solution)/shard_map/ppermute | solution.py:41
  34.2 2.2 %collective-permute-start.16 = (bf16[128,2048]{1,0:T(8,128)(2,1)S(1)}, bf16[128,2048]{1,0:T(8,128)(2,1)S(1)}, u32[]{:S(2)}, u32[]{:S(2)}) collective-permute-start(bf16[128,2048]{1,0:T(8,128)(2,1)S(1)} %attend.1.here_ref), channel_id=1, source_target_pairs={{0,1},{1,0},{2,3},{3,2},{4,5},{5,4},{6,7},{7,6},{8,9},{9,8},{10,11... | collective-permute-start | bytes 1572872 | tf_op jit(solution)/shard_map/ppermute | solution.py:45
  38.1 2.9 %collective-permute-start.18 = (bf16[128,1024]{1,0:T(8,128)(2,1)S(1)}, bf16[128,1024]{1,0:T(8,128)(2,1)S(1)}, u32[]{:S(2)}, u32[]{:S(2)}) collective-permute-start(bf16[128,1024]{1,0:T(8,128)(2,1)S(1)} %get-tuple-element.97.refs_0_), channel_id=1, source_target_pairs={{0,1},{1,0},{2,3},{3,2},{4,5},{5,4},{6,7},{7,6},{8,9},{9,8},{10,11... | collective-permute-start | bytes 786440 | tf_op jit(solution)/shard_map/ppermute | solution.py:45
  38.4 8.5 %collective-permute-start.17 = (bf16[128,1024]{1,0:T(8,128)(2,1)S(1)}, bf16[128,1024]{1,0:T(8,128)(2,1)}, u32[]{:S(2)}, u32[]{:S(2)}) collective-permute-start(bf16[128,1024]{1,0:T(8,128)(2,1)S(1)} %get-tuple-element.97.refs_0_), channel_id=1, source_target_pairs={{0,2},{2,6},{6,10},{10,14},{14,12},{12,8},{8,4},{4,0},{1,3},{3,7},... | collective-permute-start | bytes 786440 | tf_op jit(solution)/shard_map/ppermute | solution.py:41
  39.3 8.1 %collective-permute-start.24 = (bf16[128,1024]{1,0:T(8,128)(2,1)S(1)}, bf16[128,1024]{1,0:T(8,128)(2,1)S(1)}, u32[]{:S(2)}, u32[]{:S(2)}) collective-permute-start(bf16[128,1024]{1,0:T(8,128)(2,1)S(1)} %get-tuple-element.97.refs_0_), channel_id=1, source_target_pairs={{0,4},{2,0},{6,2},{10,6},{14,10},{12,14},{8,12},{4,8},{1,5},{3,1},... | collective-permute-start | bytes 786440 | tf_op jit(solution)/shard_map/ppermute | solution.py:41
  46.9 9.0 %collective-permute-start.20 = (bf16[128,1024]{1,0:T(8,128)(2,1)}, bf16[128,1024]{1,0:T(8,128)(2,1)S(1)}, u32[]{:S(2)}, u32[]{:S(2)}) collective-permute-start(bf16[128,1024]{1,0:T(8,128)(2,1)} %collective-permute-done.17.refs_1_), channel_id=1, source_target_pairs={{0,1},{1,0},{2,3},{3,2},{4,5},{5,4},{6,7},{7,6},{8,9},{9,8},{10,11... | collective-permute-start | bytes 786440 | tf_op jit(solution)/shard_map/ppermute | solution.py:45
  46.9 9.0 %collective-permute-start.19 = (bf16[128,1024]{1,0:T(8,128)(2,1)}, bf16[128,1024]{1,0:T(8,128)(2,1)S(1)}, u32[]{:S(2)}, u32[]{:S(2)}) collective-permute-start(bf16[128,1024]{1,0:T(8,128)(2,1)} %collective-permute-done.17.refs_1_), channel_id=1, source_target_pairs={{0,2},{2,6},{6,10},{10,14},{14,12},{12,8},{8,4},{4,0},{1,3},{3,7},... | collective-permute-start | bytes 786440 | tf_op jit(solution)/shard_map/ppermute | solution.py:41
  47.4 9.1 %collective-permute-start.26 = (bf16[128,1024]{1,0:T(8,128)(2,1)S(1)}, bf16[128,1024]{1,0:T(8,128)(2,1)S(1)}, u32[]{:S(2)}, u32[]{:S(2)}) collective-permute-start(bf16[128,1024]{1,0:T(8,128)(2,1)S(1)} %collective-permute-done.24.refs_7_), channel_id=1, source_target_pairs={{0,1},{1,0},{2,3},{3,2},{4,5},{5,4},{6,7},{7,6},{8,9},{9,8},{10,11... | collective-permute-start | bytes 786440 | tf_op jit(solution)/shard_map/ppermute | solution.py:45
  47.6 8.9 %collective-permute-start.25 = (bf16[128,1024]{1,0:T(8,128)(2,1)S(1)}, bf16[128,1024]{1,0:T(8,128)(2,1)S(1)}, u32[]{:S(2)}, u32[]{:S(2)}) collective-permute-start(bf16[128,1024]{1,0:T(8,128)(2,1)S(1)} %collective-permute-done.24.refs_7_), channel_id=1, source_target_pairs={{0,4},{2,0},{6,2},{10,6},{14,10},{12,14},{8,12},{4,8},{1,5},{3,1},... | collective-permute-start | bytes 786440 | tf_op jit(solution)/shard_map/ppermute | solution.py:41
  55.9 10.8 %collective-permute-start.22 = (bf16[128,1024]{1,0:T(8,128)(2,1)S(1)}, bf16[128,1024]{1,0:T(8,128)(2,1)S(1)}, u32[]{:S(2)}, u32[]{:S(2)}) collective-permute-start(bf16[128,1024]{1,0:T(8,128)(2,1)S(1)} %collective-permute-done.19.refs_2_), channel_id=1, source_target_pairs={{0,1},{1,0},{2,3},{3,2},{4,5},{5,4},{6,7},{7,6},{8,9},{9,8},{10,11... | collective-permute-start | bytes 786440 | tf_op jit(solution)/shard_map/ppermute | solution.py:45
  56.0 10.8 %collective-permute-start.21 = (bf16[128,1024]{1,0:T(8,128)(2,1)S(1)}, bf16[128,1024]{1,0:T(8,128)(2,1)}, u32[]{:S(2)}, u32[]{:S(2)}) collective-permute-start(bf16[128,1024]{1,0:T(8,128)(2,1)S(1)} %collective-permute-done.19.refs_2_), channel_id=1, source_target_pairs={{0,2},{2,6},{6,10},{10,14},{14,12},{12,8},{8,4},{4,0},{1,3},{3,7},... | collective-permute-start | bytes 786440 | tf_op jit(solution)/shard_map/ppermute | solution.py:41
  56.5 11.8 %collective-permute-start.28 = (bf16[128,1024]{1,0:T(8,128)(2,1)S(1)}, bf16[128,1024]{1,0:T(8,128)(2,1)S(1)}, u32[]{:S(2)}, u32[]{:S(2)}) collective-permute-start(bf16[128,1024]{1,0:T(8,128)(2,1)S(1)} %collective-permute-done.25.refs_6_), channel_id=1, source_target_pairs={{0,1},{1,0},{2,3},{3,2},{4,5},{5,4},{6,7},{7,6},{8,9},{9,8},{10,11... | collective-permute-start | bytes 786440 | tf_op jit(solution)/shard_map/ppermute | solution.py:45
  56.7 11.5 %collective-permute-start.27 = (bf16[128,1024]{1,0:T(8,128)(2,1)S(1)}, bf16[128,1024]{1,0:T(8,128)(2,1)}, u32[]{:S(2)}, u32[]{:S(2)}) collective-permute-start(bf16[128,1024]{1,0:T(8,128)(2,1)S(1)} %collective-permute-done.25.refs_6_), channel_id=1, source_target_pairs={{0,4},{2,0},{6,2},{10,6},{14,10},{12,14},{8,12},{4,8},{1,5},{3,1},... | collective-permute-start | bytes 786440 | tf_op jit(solution)/shard_map/ppermute | solution.py:41
  67.8 5.5 %collective-permute-start.23 = (bf16[64,1024]{1,0:T(8,128)(2,1)S(1)}, bf16[64,1024]{1,0:T(8,128)(2,1)S(1)}, u32[]{:S(2)}, u32[]{:S(2)}) collective-permute-start(bf16[64,1024]{1,0:T(8,128)(2,1)S(1)} %slice.40), channel_id=1, source_target_pairs={{0,2},{2,6},{6,10},{10,14},{14,12},{12,8},{8,4},{4,0},{1,3},{3,7},... | collective-permute-start | bytes 393224 | tf_op jit(solution)/shard_map/ppermute | solution.py:41
  69.3 5.4 %collective-permute-start.29 = (bf16[64,1024]{1,0:T(8,128)(2,1)S(1)}, bf16[64,1024]{1,0:T(8,128)(2,1)S(1)}, u32[]{:S(2)}, u32[]{:S(2)}) collective-permute-start(bf16[64,1024]{1,0:T(8,128)(2,1)S(1)} %slice.41), channel_id=1, source_target_pairs={{0,4},{2,0},{6,2},{10,6},{14,10},{12,14},{8,12},{4,8},{1,5},{3,1},... | collective-permute-start | bytes 393224 | tf_op jit(solution)/shard_map/ppermute | solution.py:41
  71.1 5.4 %collective-permute-start.32 = (bf16[128,1024]{1,0:T(8,128)(2,1)}, bf16[128,1024]{1,0:T(8,128)(2,1)}, u32[]{:S(2)}, u32[]{:S(2)}) collective-permute-start(bf16[128,1024]{1,0:T(8,128)(2,1)} %collective-permute-done.27.refs_5_), channel_id=1, source_target_pairs={{0,1},{1,0},{2,3},{3,2},{4,5},{5,4},{6,7},{7,6},{8,9},{9,8},{10,11... | collective-permute-start | bytes 786440 | tf_op jit(solution)/shard_map/ppermute | solution.py:45
  71.1 5.4 %collective-permute-start.30 = (bf16[128,1024]{1,0:T(8,128)(2,1)}, bf16[128,1024]{1,0:T(8,128)(2,1)}, u32[]{:S(2)}, u32[]{:S(2)}) collective-permute-start(bf16[128,1024]{1,0:T(8,128)(2,1)} %collective-permute-done.21.refs_3_), channel_id=1, source_target_pairs={{0,1},{1,0},{2,3},{3,2},{4,5},{5,4},{6,7},{7,6},{8,9},{9,8},{10,11... | collective-permute-start | bytes 786440 | tf_op jit(solution)/shard_map/ppermute | solution.py:45
  75.4 1.9 %collective-permute-start.31 = (bf16[128,1024]{1,0:T(8,128)(2,1)}, bf16[128,1024]{1,0:T(8,128)(2,1)}, u32[]{:S(2)}, u32[]{:S(2)}) collective-permute-start(bf16[128,1024]{1,0:T(8,128)(2,1)} %constant_dynamic-update-slice_fusion.2.refs_4_), channel_id=1, source_target_pairs={{0,1},{1,0},{2,3},{3,2},{4,5},{5,4},{6,7},{7,6},{8,9},{9,8},{10,11... | collective-permute-start | bytes 786440 | tf_op jit(solution)/shard_map/ppermute | solution.py:45
  118.8 1.6 %collective-permute-start.37 = (bf16[128,1024]{1,0:T(8,128)(2,1)S(1)}, bf16[128,1024]{1,0:T(8,128)(2,1)S(1)}, u32[]{:S(2)}, u32[]{:S(2)}) collective-permute-start(bf16[128,1024]{1,0:T(8,128)(2,1)S(1)} %get-tuple-element.136), channel_id=1, source_target_pairs={{0,1},{1,0},{2,3},{3,2},{4,5},{5,4},{6,7},{7,6},{8,9},{9,8},{10,11... | collective-permute-start | bytes 786440 | tf_op jit(solution)/shard_map/ppermute | solution.py:45
  119.0 4.1 %collective-permute-start.36 = (bf16[128,1024]{1,0:T(8,128)(2,1)S(1)}, bf16[128,1024]{1,0:T(8,128)(2,1)S(1)}, u32[]{:S(2)}, u32[]{:S(2)}) collective-permute-start(bf16[128,1024]{1,0:T(8,128)(2,1)S(1)} %get-tuple-element.134), channel_id=1, source_target_pairs={{0,1},{1,0},{2,3},{3,2},{4,5},{5,4},{6,7},{7,6},{8,9},{9,8},{10,11... | collective-permute-start | bytes 786440 | tf_op jit(solution)/shard_map/ppermute | solution.py:45
  120.5 5.6 %collective-permute-start.38 = (bf16[64,1024]{1,0:T(8,128)(2,1)S(1)}, bf16[64,1024]{1,0:T(8,128)(2,1)S(1)}, u32[]{:S(2)}, u32[]{:S(2)}) collective-permute-start(bf16[64,1024]{1,0:T(8,128)(2,1)S(1)} %get-tuple-element.145), channel_id=1, source_target_pairs={{0,2},{2,6},{6,10},{10,14},{14,12},{12,8},{8,4},{4,0},{1,3},{3,7},... | collective-permute-start | bytes 393224 | tf_op jit(solution)/shard_map/ppermute | solution.py:41
  120.9 5.7 %collective-permute-start.44 = (bf16[128,1024]{1,0:T(8,128)(2,1)S(1)}, bf16[128,1024]{1,0:T(8,128)(2,1)S(1)}, u32[]{:S(2)}, u32[]{:S(2)}) collective-permute-start(bf16[128,1024]{1,0:T(8,128)(2,1)S(1)} %get-tuple-element.142), channel_id=1, source_target_pairs={{0,1},{1,0},{2,3},{3,2},{4,5},{5,4},{6,7},{7,6},{8,9},{9,8},{10,11... | collective-permute-start | bytes 786440 | tf_op jit(solution)/shard_map/ppermute | solution.py:45
  120.9 7.8 %collective-permute-start.35 = (bf16[128,1024]{1,0:T(8,128)(2,1)S(1)}, bf16[128,1024]{1,0:T(8,128)(2,1)S(1)}, u32[]{:S(2)}, u32[]{:S(2)}) collective-permute-start(bf16[128,1024]{1,0:T(8,128)(2,1)S(1)} %get-tuple-element.132), channel_id=1, source_target_pairs={{0,1},{1,0},{2,3},{3,2},{4,5},{5,4},{6,7},{7,6},{8,9},{9,8},{10,11... | collective-permute-start | bytes 786440 | tf_op jit(solution)/shard_map/ppermute | solution.py:45
  121.4 5.4 %collective-permute-start.45 = (bf16[64,1024]{1,0:T(8,128)(2,1)S(1)}, bf16[64,1024]{1,0:T(8,128)(2,1)S(1)}, u32[]{:S(2)}, u32[]{:S(2)}) collective-permute-start(bf16[64,1024]{1,0:T(8,128)(2,1)S(1)} %get-tuple-element.146), channel_id=1, source_target_pairs={{0,4},{2,0},{6,2},{10,6},{14,10},{12,14},{8,12},{4,8},{1,5},{3,1},... | collective-permute-start | bytes 393224 | tf_op jit(solution)/shard_map/ppermute | solution.py:41
  126.2 7.6 %collective-permute-start.39 = (bf16[128,1024]{1,0:T(8,128)(2,1)S(1)}, bf16[128,1024]{1,0:T(8,128)(2,1)S(1)}, u32[]{:S(2)}, u32[]{:S(2)}) collective-permute-start(bf16[128,1024]{1,0:T(8,128)(2,1)S(1)} %add_convert_fusion.6), channel_id=1, source_target_pairs={{0,2},{2,6},{6,10},{10,14},{14,12},{12,8},{8,4},{4,0},{1,3},{3,7},... | collective-permute-start | bytes 786440 | tf_op jit(solution)/shard_map/ppermute | solution.py:41
  126.6 7.7 %collective-permute-start.43 = (bf16[128,1024]{1,0:T(8,128)(2,1)S(1)}, bf16[128,1024]{1,0:T(8,128)(2,1)S(1)}, u32[]{:S(2)}, u32[]{:S(2)}) collective-permute-start(bf16[128,1024]{1,0:T(8,128)(2,1)S(1)} %get-tuple-element.140), channel_id=1, source_target_pairs={{0,1},{1,0},{2,3},{3,2},{4,5},{5,4},{6,7},{7,6},{8,9},{9,8},{10,11... | collective-permute-start | bytes 786440 | tf_op jit(solution)/shard_map/ppermute | solution.py:45
  126.9 8.6 %collective-permute-start.46 = (bf16[128,1024]{1,0:T(8,128)(2,1)S(1)}, bf16[128,1024]{1,0:T(8,128)(2,1)S(1)}, u32[]{:S(2)}, u32[]{:S(2)}) collective-permute-start(bf16[128,1024]{1,0:T(8,128)(2,1)S(1)} %add_convert_fusion.3), channel_id=1, source_target_pairs={{0,4},{2,0},{6,2},{10,6},{14,10},{12,14},{8,12},{4,8},{1,5},{3,1},... | collective-permute-start | bytes 786440 | tf_op jit(solution)/shard_map/ppermute | solution.py:41
  128.6 8.7 %collective-permute-start.34 = (bf16[128,1024]{1,0:T(8,128)(2,1)S(1)}, bf16[128,1024]{1,0:T(8,128)(2,1)S(1)}, u32[]{:S(2)}, u32[]{:S(2)}) collective-permute-start(bf16[128,1024]{1,0:T(8,128)(2,1)S(1)} %get-tuple-element.130), channel_id=1, source_target_pairs={{0,1},{1,0},{2,3},{3,2},{4,5},{5,4},{6,7},{7,6},{8,9},{9,8},{10,11... | collective-permute-start | bytes 786440 | tf_op jit(solution)/shard_map/ppermute | solution.py:45
  128.6 12.4 %collective-permute-start.42 = (bf16[128,1024]{1,0:T(8,128)(2,1)S(1)}, bf16[128,1024]{1,0:T(8,128)(2,1)S(1)}, u32[]{:S(2)}, u32[]{:S(2)}) collective-permute-start(bf16[128,1024]{1,0:T(8,128)(2,1)S(1)} %get-tuple-element.138), channel_id=1, source_target_pairs={{0,1},{1,0},{2,3},{3,2},{4,5},{5,4},{6,7},{7,6},{8,9},{9,8},{10,11... | collective-permute-start | bytes 786440 | tf_op jit(solution)/shard_map/ppermute | solution.py:45
  133.9 6.7 %collective-permute-start.40 = (bf16[128,1024]{1,0:T(8,128)(2,1)S(1)}, bf16[128,1024]{1,0:T(8,128)(2,1)S(1)}, u32[]{:S(2)}, u32[]{:S(2)}) collective-permute-start(bf16[128,1024]{1,0:T(8,128)(2,1)S(1)} %add_convert_fusion.5), channel_id=1, source_target_pairs={{0,2},{2,6},{6,10},{10,14},{14,12},{12,8},{8,4},{4,0},{1,3},{3,7},... | collective-permute-start | bytes 786440 | tf_op jit(solution)/shard_map/ppermute | solution.py:41
  135.6 7.7 %collective-permute-start.47 = (bf16[128,1024]{1,0:T(8,128)(2,1)S(1)}, bf16[128,1024]{1,0:T(8,128)(2,1)S(1)}, u32[]{:S(2)}, u32[]{:S(2)}) collective-permute-start(bf16[128,1024]{1,0:T(8,128)(2,1)S(1)} %add_convert_fusion.2), channel_id=1, source_target_pairs={{0,4},{2,0},{6,2},{10,6},{14,10},{12,14},{8,12},{4,8},{1,5},{3,1},... | collective-permute-start | bytes 786440 | tf_op jit(solution)/shard_map/ppermute | solution.py:41
  137.3 7.9 %collective-permute-start.33 = (bf16[128,1024]{1,0:T(8,128)(2,1)S(1)}, bf16[128,1024]{1,0:T(8,128)(2,1)S(1)}, u32[]{:S(2)}, u32[]{:S(2)}) collective-permute-start(bf16[128,1024]{1,0:T(8,128)(2,1)S(1)} %get-tuple-element.128), channel_id=1, source_target_pairs={{0,1},{1,0},{2,3},{3,2},{4,5},{5,4},{6,7},{7,6},{8,9},{9,8},{10,11... | collective-permute-start | bytes 786440 | tf_op jit(solution)/shard_map/ppermute | solution.py:45
  140.6 6.4 %collective-permute-start.41 = (bf16[128,1024]{1,0:T(8,128)(2,1)S(1)}, bf16[128,1024]{1,0:T(8,128)(2,1)S(1)}, u32[]{:S(2)}, u32[]{:S(2)}) collective-permute-start(bf16[128,1024]{1,0:T(8,128)(2,1)S(1)} %add_convert_fusion.4), channel_id=1, source_target_pairs={{0,2},{2,6},{6,10},{10,14},{14,12},{12,8},{8,4},{4,0},{1,3},{3,7},... | collective-permute-start | bytes 786440 | tf_op jit(solution)/shard_map/ppermute | solution.py:41
  143.4 6.8 %collective-permute-start.48 = (bf16[128,1024]{1,0:T(8,128)(2,1)S(1)}, bf16[128,1024]{1,0:T(8,128)(2,1)S(1)}, u32[]{:S(2)}, u32[]{:S(2)}) collective-permute-start(bf16[128,1024]{1,0:T(8,128)(2,1)S(1)} %add_convert_fusion.1), channel_id=1, source_target_pairs={{0,4},{2,0},{6,2},{10,6},{14,10},{12,14},{8,12},{4,8},{1,5},{3,1},... | collective-permute-start | bytes 786440 | tf_op jit(solution)/shard_map/ppermute | solution.py:41
  (31 other events, 107.7 us)

commit v7 on v6

--- a/solution.py
+++ b/solution.py
@@ -19,8 +19,8 @@
 WIDE = 640
 MIB = 1024 * 1024
 VMEM_LIMIT = 50 * MIB
-STAGED = 2
-DEPTH = 2
+STREAMS = 2
+DEPTH = 3
 PIECES = 2
 SWAP = [(0, 1), (1, 0)]
 FEW = 8
@@ -65,7 +65,7 @@
 def gather(block, count, beside=()):
     if count > FEW:
         found = lax.all_gather(block, "ctx")
-        return list(found), list(swap(found)), list(beside)
+        return list(found), list(swap(found)), [run(*arguments) for run, arguments in beside]
     middle = count // 2
     found, other, made = [None] * count, [None] * count, []
     found[0] = block
@@ -73,7 +73,10 @@
     for d in range(1, middle):
         for place, before, ahead in ((d, d - 1, 1), (count - d, (1 - d) % count, -1)):
             arrived = step(found[before], ahead, count)
-            extra = beside[d - 1] if ahead == 1 and len(beside) >= d else ()
+            extra = ()
+            if ahead == 1 and len(beside) >= d:
+                run, arguments = beside[d - 1]
+                extra = run(*lax.optimization_barrier((found[before], arguments))[1])
             found[place], other[before], extra = lax.optimization_barrier((arrived, other[before], extra))
             if ahead == 1:
                 made.append(extra)
@@ -218,7 +221,7 @@
     )(*(pltpu.with_memory_space_constraint(x, pltpu.HBM) for x in arrays))
 
 
-def norm_kernel(where, residual_ref, here_ref, there_ref, gain_ref, middle_ref, normed_ref):
+def norm_kernel(where, residual_ref, here_ref, there_ref, gain_ref, middle_ref, *normed_refs):
     side = where[1]
     half = middle_ref.shape[1]
     total = here_ref[...].astype(jnp.float32) + there_ref[...].astype(jnp.float32)
@@ -227,18 +230,22 @@
     inverse = lax.rsqrt(jnp.mean(wide * wide, axis=1, keepdims=True) + 1e-06)
     normed = wide * inverse * gain_ref[...].astype(jnp.float32)
     middle_ref[...] = jnp.where(side == 0, wide[:, :half], wide[:, half:]).astype(jnp.bfloat16)
-    normed_ref[...] = jnp.where(side == 0, normed[:, :half], normed[:, half:]).astype(jnp.bfloat16)
+    normed = jnp.where(side == 0, normed[:, :half], normed[:, half:]).astype(jnp.bfloat16)
+    part = half // len(normed_refs)
+    for h, ref in enumerate(normed_refs):
+        ref[...] = normed[:, h * part : (h + 1) * part]
 
 
 def norm(where, residual, here, there, gain):
     rows, width = residual.shape
-    half = pltpu.VMEM((rows, width // 2), jnp.bfloat16)
+    half = width // 2
+    shapes = [(rows, half)] + [(rows, half // STREAMS)] * STREAMS
     whole = pl.BlockSpec(memory_space=pltpu.VMEM)
     return pl.pallas_call(
         norm_kernel,
         in_specs=[pl.BlockSpec(memory_space=pltpu.SMEM)] + [whole] * 4,
-        out_specs=[whole, whole],
-        out_shape=[half, half],
+        out_specs=[whole] * len(shapes),
+        out_shape=[pltpu.VMEM(shape, jnp.bfloat16) for shape in shapes],
         compiler_params=pltpu.CompilerParams(vmem_limit_bytes=12 * MIB),
         name="norm",
     )(where, residual, here, there, gain)
@@ -296,21 +303,23 @@
     out_ref[0] = expert_rows(rows_ref[0], gate_ref.at[0], up_ref.at[0], down_ref.at[0], scale_ref[0])
 
 
-def fused_kernel(count, staged, where, *refs):
-    mine, other = refs[:count], refs[count : 2 * count]
-    pick_ref, combine_ref, scale_ref = refs[2 * count : 2 * count + 3]
-    at = 2 * count + 3
-    early, at = [refs[at + 3 * i : at + 3 * i + 3] for i in range(staged)], at + 3 * staged
-    weights, at = refs[at : at + 3], at + 3
-    kept, away, at = refs[at : at + count], refs[at + count : at + 2 * count], at + 2 * count
-    picked, buffers, sems = refs[at], refs[at + 1 : at + 4], refs[at + 4]
+def fused_kernel(count, where, *refs):
+    blocks = STREAMS * count
+    mine, other = refs[:blocks], refs[blocks : 2 * blocks]
+    combine_ref, scale_ref = refs[2 * blocks : 2 * blocks + 2]
+    weights = refs[2 * blocks + 2 : 2 * blocks + 5]
+    kept, away = refs[2 * blocks + 5 : 3 * blocks + 5], refs[3 * blocks + 5 : 4 * blocks + 5]
+    picked, buffers, sems = refs[4 * blocks + 5], refs[4 * blocks + 6 : 4 * blocks + 9], refs[4 * blocks + 9]
     here = picked.shape[0]
     depth, units, _ = buffers[0].shape
-    half = picked.shape[2] // 2
+    part = mine[0].shape[1]
+    half = part * STREAMS
     side = where[1]
-    near = pl.ds(pl.multiple_of(side * half, half), half)
-    far = pl.ds(pl.multiple_of((1 - side) * half, half), half)
     piece = units // PIECES
+    by_rows = (((0,), (0,)), ((), ()))
+
+    def columns(side, h):
+        return pl.ds(pl.multiple_of(side * half + h * part, part), part)
 
     def copies(expert, slot):
         for w in range(3):
@@ -318,22 +327,21 @@
                 rows = pl.ds(i * piece, piece)
                 yield pltpu.make_async_copy(weights[w].at[expert, rows], buffers[w].at[slot, rows], sems.at[slot, w, i])
 
-    for i in range(min(depth, here - staged)):
-        for copy in copies(staged + i, i):
+    for e in range(depth):
+        for copy in copies(e, e):
             copy.start()
 
     for c in range(count):
-        for columns, block in ((near, mine[c]), (far, other[c])):
-            rows = jnp.dot(pick_ref[c], block[...], preferred_element_type=jnp.float32).astype(jnp.bfloat16)
-            for e in range(here):
-                picked[e, c * SLOTS : (c + 1) * SLOTS, columns] = rows[e * SLOTS : (e + 1) * SLOTS]
-
-    for e in range(staged):
-        picked[e] = expert_rows(picked[e], *early[e], scale_ref[e])
-
-    def work(i, _):
-        slot = lax.rem(i, depth)
-        expert = staged + i
+        for h in range(STREAMS):
+            for place, block in ((columns(side, h), mine), (columns(1 - side, h), other)):
+                rows = lax.dot_general(
+                    combine_ref[c], block[h * count + c][...], by_rows, preferred_element_type=jnp.float32
+                ).astype(jnp.bfloat16)
+                for e in range(here):
+                    picked[e, c * SLOTS : (c + 1) * SLOTS, place] = rows[e * SLOTS : (e + 1) * SLOTS]
+
+    def work(expert, _):
+        slot = lax.rem(expert, depth)
         for copy in copies(expert, slot):
             copy.wait()
         picked[expert] = expert_rows(picked[expert], *(buffer.at[slot] for buffer in buffers), scale_ref[expert])
@@ -345,12 +353,13 @@
 
         return 0
 
-    lax.fori_loop(0, here - staged, work, 0)
+    lax.fori_loop(0, here, work, 0)
     for c in range(count):
-        for columns, out in ((far, away[c]), (near, kept[c])):
-            rows = [picked[e, c * SLOTS : (c + 1) * SLOTS, columns] for e in range(here)]
-            total = jnp.dot(combine_ref[c], jnp.concatenate(rows, axis=0), preferred_element_type=jnp.float32)
-            out[...] = total.astype(jnp.bfloat16)
+        for h in range(STREAMS):
+            for place, out in ((columns(1 - side, h), away), (columns(side, h), kept)):
+                rows = [picked[e, c * SLOTS : (c + 1) * SLOTS, place] for e in range(here)]
+                total = jnp.dot(combine_ref[c], jnp.concatenate(rows, axis=0), preferred_element_type=jnp.float32)
+                out[h * count + c][...] = total.astype(jnp.bfloat16)
 
 
 def expert_specs(w_gate, rows):
@@ -376,27 +385,29 @@
     )(where, picked, w_gate, w_up, w_down, scale)
 
 
-def experts_fused(where, mine, other, pick, combine, scale, early, w_gate, w_up, w_down):
-    count, (local, half) = len(mine), mine[0].shape
+def experts_fused(where, mine, other, combine, scale, w_gate, w_up, w_down):
+    count, (local, part) = len(mine[0]), mine[0][0].shape
     here, _, rows = scale.shape
     units = w_gate.shape[1]
     depth = min(DEPTH, here)
+    blocks = STREAMS * count
     whole = pl.BlockSpec(memory_space=pltpu.VMEM)
     outs = pl.pallas_call(
-        functools.partial(fused_kernel, count, len(early)),
+        functools.partial(fused_kernel, count),
         in_specs=[pl.BlockSpec(memory_space=pltpu.SMEM)]
-        + [whole] * (2 * count + 3 + 3 * len(early))
+        + [whole] * (2 * blocks + 2)
         + [pl.BlockSpec(memory_space=pltpu.HBM)] * 3,
-        out_specs=[whole] * (2 * count),
-        scratch_shapes=[pltpu.VMEM((here, rows, 2 * half), jnp.bfloat16)]
-        + [pltpu.VMEM((depth, units, 2 * half), jnp.bfloat16)] * 3
+        out_specs=[whole] * (2 * blocks),
+        scratch_shapes=[pltpu.VMEM((here, rows, w_gate.shape[2]), jnp.bfloat16)]
+        + [pltpu.VMEM((depth, units, w_gate.shape[2]), jnp.bfloat16)] * 3
         + [pltpu.SemaphoreType.DMA((depth, 3, PIECES))],
-        out_shape=[pltpu.VMEM((local, half), jnp.bfloat16)] * (2 * count),
-        compiler_params=pltpu.CompilerParams(vmem_limit_bytes=28 * MIB),
+        out_shape=[pltpu.VMEM((local, part), jnp.bfloat16)] * (2 * blocks),
+        compiler_params=pltpu.CompilerParams(vmem_limit_bytes=38 * MIB),
         name="experts",
-    )(where, *mine, *other, pick, combine, scale, *sum(early, []),
+    )(where, *sum(mine, []), *sum(other, []), combine, scale,
       *(pltpu.with_memory_space_constraint(w, pltpu.HBM) for w in (w_gate, w_up, w_down)))
-    return outs[:count], outs[count:]
+    lists = [outs[i * count : (i + 1) * count] for i in range(2 * STREAMS)]
+    return lists[:STREAMS], lists[STREAMS:]
 
 
 def body(
@@ -425,17 +436,22 @@
     base = latent.shape[1]
     w_gate, w_up = w_gate.transpose(0, 2, 1), w_up.transpose(0, 2, 1)
     packed = pack(where, latent, expert_ids, route_weights)
-    info = jnp.concatenate([where, sources_of(me, count), span_order, seg_lengths])
-    q = queries.reshape(local_rows, heads, NOPE + ROPE).transpose(1, 0, 2)
-    gain = norm_gain.reshape(1, width)
-    ready = stage((kv_up, out_proj, residual), (None, None, None)) if count <= FEW else (kv_up, out_proj, residual)
-    found, found_other, made = gather(packed, count, [(info, q, gain), tuple(ready)])
-    (info, q, gain), (kv_up, out_proj, residual) = made
+    few = count <= FEW
+    bring = lambda *arrays: stage(arrays, (None,) * len(arrays)) if few else arrays
+    arrange = lambda x: x.reshape(local_rows, heads, NOPE + ROPE).transpose(1, 0, 2)
+    scalars = lambda *arrays: jnp.concatenate([where, sources_of(me, count), *arrays])
+    beside = [
+        (arrange, (queries,)),
+        (bring, (kv_up, out_proj, residual)),
+        (lambda gain, *arrays: (gain.reshape(1, width), scalars(*arrays)), (norm_gain, span_order, seg_lengths)),
+    ]
+    found, found_other, made = gather(packed, count, beside)
+    q, (kv_up, out_proj, residual), (gain, info) = made
     mine, other = jnp.stack(found), jnp.stack(found_other)
     partial = attend(info, q, mine, other, kv_up, out_proj, count)
     there = swap(partial)
     mine, other, partial = lax.optimization_barrier((mine, other, partial))
-    middle, normed = norm(where, residual, partial, there, gain)
+    middle, *normed = norm(where, residual, partial, there, gain)
 
     facts_mine, facts_other = mine[:, :, base : base + 3 * TOP], other[:, :, base : base + 3 * TOP]
     facts = jnp.concatenate(
@@ -455,28 +471,37 @@
     scale = jnp.sum(jnp.where(combine, share[:, :, :, None], 0.0), axis=1)
     scale = scale.transpose(1, 0, 2).reshape(here, 1, count * SLOTS)
     combine = combine.astype(jnp.bfloat16).reshape(count, local_rows, here * SLOTS)
-    pick = combine.transpose(0, 2, 1)
-
-    early = [()] * STAGED if count > FEW else [stage((w_gate, w_up, w_down), (e, e, e)) for e in range(STAGED)]
-    got, got_other, made = gather(normed, count, [(pick, combine, scale)] + [tuple(x) for x in early])
-    (pick, combine, scale), early = made[0], [list(x) for x in made[1:]]
-    if count <= FEW:
-        kept, away = experts_fused(where, got, got_other, pick, combine, scale, early, w_gate, w_up, w_down)
+
+    facts = [(lambda *x: x, (combine, scale))]
+    streams = [gather(x, count, facts if h == 0 else ()) for h, x in enumerate(normed)]
+    combine, scale = streams[0][2][0]
+    near, far = [x[0] for x in streams], [x[1] for x in streams]
+    if few:
+        kept, away = experts_fused(where, near, far, combine, scale, w_gate, w_up, w_down)
     else:
-        near, far = jnp.stack(got), jnp.stack(got_other)
+        near, far = (jnp.concatenate([jnp.stack(x) for x in xs], axis=2) for xs in (near, far))
         full = jnp.concatenate([jnp.where(side == 0, near, far), jnp.where(side == 0, far, near)], axis=2)
-        picked = jnp.einsum("cst,ctd->csd", pick, full, preferred_element_type=jnp.float32).astype(jnp.bfloat16)
+        picked = jnp.einsum("cts,ctd->csd", combine, full, preferred_element_type=jnp.float32).astype(jnp.bfloat16)
         picked = picked.reshape(count, here, SLOTS, width).transpose(1, 0, 2, 3).reshape(here, count * SLOTS, width)
         result = experts_plain(where, picked, w_gate, w_up, w_down, scale)
         result = result.reshape(here, count, SLOTS, width).transpose(1, 0, 2, 3).reshape(count, here * SLOTS, width)
         total = jnp.einsum("cts,csd->ctd", combine, result, preferred_element_type=jnp.float32).astype(jnp.bfloat16)
         left, right = jnp.split(total, 2, axis=2)
         kept, away = jnp.where(side == 0, left, right), jnp.where(side == 0, right, left)
-    swap_all = lambda pieces: [swap(piece) for piece in pieces] if count <= FEW else list(swap(jnp.stack(pieces)))
+        kept, away = ([list(part) for part in jnp.split(x, STREAMS, axis=2)] for x in (kept, away))
     order = [(count // 2 + (d + 1) // 2 * (1 - d % 2 * 2)) % count for d in range(count)]
-    swapped = dict(zip(order, swap_all([away[c] for c in order])))
-    parts = [functools.partial(summed, [kept[c], swapped[c]]) for c in range(count)]
-    return (middle.astype(jnp.float32) + reduce(parts, count)).astype(jnp.bfloat16)
+    swapped = [{} for _ in range(STREAMS)]
+    if few:
+        for c in order:
+            for h in range(STREAMS):
+                swapped[h][c] = swap(away[h][c])
+    else:
+        swapped = [dict(enumerate(swap(jnp.stack(part)))) for part in away]
+    sums = [
+        reduce([functools.partial(summed, [kept[h][c], swapped[h][c]]) for c in range(count)], count)
+        for h in range(STREAMS)
+    ]
+    return (middle.astype(jnp.float32) + jnp.concatenate(sums, axis=1)).astype(jnp.bfloat16)
 
 
 def solution(mesh):

time: 152 us -> 186 us (1.22)
  waiting for transfers between devices: 41 us -> 72.3 us
  starting transfers between devices: 30.1 us -> 46 us
  local copies, waits for them, and re-layouts: 35.8 us -> 23.2 us
  Pallas kernels: 40.3 us -> 35.9 us
  other arithmetic: 3.28 us -> 6.47 us
    ppermute x24 -> x40, waiting for transfers between devices: 38 us -> 70.3 us  [step(): lax.ppermute(value, 'ctx', [(cycle[p], cycle[(p + ahead) % count]) for p...]
    unnamed x77 -> x29, local copies, waits for them, and re-layouts: 28.9 us -> 14 us
    ppermute x24 -> x40, starting transfers between devices: 26.3 us -> 40.1 us  [step(): lax.ppermute(value, 'ctx', [(cycle[p], cycle[(p + ahead) % count]) for p...]
    pallas_call x3 -> x1, Pallas kernels: 9.19 us -> 2.03 us  [stage(): pl.pallas_call(functools.partial(stage_kernel, picks), in_specs=[pl.Block...]
    another operation x2, local copies, waits for them, and re-layouts: 0.03 us -> 2.43 us  [body(): mine, other = (jnp.stack(found), jnp.stack(found_other))]
    ppermute x25 -> x41, starting transfers between devices: 3.8 us -> 5.93 us  [swap(): return lax.ppermute(value, 'exp', SWAP)]
  transfers between devices with their start and end apart: 49 -> 81, of which waited for: 19 -> 33; matrix products, arithmetic and copies ran while one was open for 7% -> 12% of each run, Pallas kernels for 6% -> 1%
where the time goes in v7:
time: 186 us; the launch traced here: 185 us
  waiting for transfers between devices  72.3 us (39%)
  starting transfers between devices  46 us (25%)
  Pallas kernels  35.9 us (19%)
  local copies, waits for them, and re-layouts  23.2 us (12%)
  other arithmetic  6.47 us (3%)
    ppermute x40, waiting for transfers between devices, step(): lax.ppermute(value, 'ctx', [(cycle[p], cycle[(p + ahead) % count]) for p...  70.3 us
    ppermute x40, starting transfers between devices, step(): lax.ppermute(value, 'ctx', [(cycle[p], cycle[(p + ahead) % count]) for p...  40.1 us
    pallas_call x1, Pallas kernels, experts_fused(): pl.pallas_call(functools.partial(fused_kernel, count), in_specs=[pl.Block...  25.6 us
    unnamed x29, local copies, waits for them, and re-layouts  14 us
    ppermute x41, starting transfers between devices, swap(): return lax.ppermute(value, 'exp', SWAP)  5.93 us
    pallas_call x1, Pallas kernels, attend(): pl.pallas_call(functools.partial(attend_kernel, count, blocks), grid_spec...  5.65 us
  transfers between devices with their start and end apart: 81, of which 33 were waited for; matrix products, arithmetic and copies ran while one was open for 12% of the time, Pallas kernels for 1%

profile of v7, /device:TPU:0, one launch (start us, length us, event | category | flops | bytes accessed | tf_op | source)
XLA Modules:
  0.0 184.6 jit_solution(17798244568568530446)
XLA Ops:
  0.1 1.7 pack.1
  1.8 3.1 %collective-permute-start.7 = (bf16[64,640]{1,0:T(8,128)(2,1)S(1)}, bf16[64,640]{1,0:T(8,128)(2,1)}, u32[]{:S(2)}, u32[]{:S(2)}) collective-permute-start(bf16[64,640]{1,0:T(8,128)(2,1)S(1)} %pack.1), channel_id=1, source_target_pairs={{0,4},{2,0},{6,2},{10,6},{14,10},{12,14},{8,12},{4,8},{1,5},{3,1},... | collective-permute-start | bytes 245768 | tf_op jit(solution)/shard_map/ppermute | solution.py:41
  7.4 1.2 dynamic-slice_bitcast_fusion
  8.6 1.2 collective-permute-done
  9.8 1.6 collective-permute-start.8
  13.6 2.0 %stage.1 = (bf16[512,1024]{1,0:T(8,128)(2,1)S(1)}, bf16[512,2048]{1,0:T(8,128)(2,1)S(1)}, bf16[128,2048]{1,0:T(8,128)(2,1)S(1)}) custom-call(bf16[512,1024]{1,0:T(8,128)(2,1)} %refs_0_, bf16[512,2048]{1,0:T(8,128)(2,1)} %refs_1_, bf16[128,2048]{1,0:T(8,128)(2,1)} %refs_2_), custom_call_target="tpu_custom_call" | custom-call | tf_op jit(solution)/shard_map/stage/pallas_call | solution.py:213
  16.7 1.6 collective-permute-start.10
  24.3 1.6 collective-permute-start.12
  27.3 1.5 bitcast_dynamic-update-slice_fusion.5
  28.8 2.0 %collective-permute-done.6 = bf16[32,640]{1,0:T(8,128)(2,1)S(1)} collective-permute-done((bf16[32,640]{1,0:T(8,128)(2,1)S(1)}, bf16[32,640]{1,0:T(8,128)(2,1)S(1)}, u32[]{:S(2)}, u32[]{:S(2)}) %collective-permute-start.6) | collective-permute-done | bytes 40992 | tf_op jit(solution)/shard_map/ppermute | solution.py:41
  35.6 1.5 bitcast_dynamic-update-slice_fusion.1
  37.1 1.5 bitcast_dynamic-update-slice_fusion.other_ref
  38.6 1.2 copy-done.1
  39.9 5.6 %attend.1.here_ref = bf16[128,2048]{1,0:T(8,128)(2,1)S(1)} custom-call(s32[42]{0:T(128)S(1)} %concatenate.31.info, bf16[4,128,192]{2,1,0:T(8,128)(2,1)S(1)} %bitcast.53, bf16[8,64,640]{2,1,0:T(8,128)(2,1)S(1)} %bitcast_dynamic-update-slice_fusion.8.mine_ref, bf16[8,64,640]{2,1,0:T(8,128)(2,1)} %bitcast_dynamic-update-slice_fusion.other_ref, ...), custom_call_target="tpu_custom_call" | custom-call | tf_op jit(solution)/shard_map/attend/pallas_call | solution.py:176
  50.8 1.6 collective-permute-start.37
  53.5 1.6 collective-permute-start.24
  55.6 2.7 %collective-permute-done.30.refs_9_ = bf16[128,512]{1,0:T(8,128)(2,1)S(1)} collective-permute-done((bf16[128,512]{1,0:T(8,128)(2,1)S(1)}, bf16[128,512]{1,0:T(8,128)(2,1)S(1)}, u32[]{:S(2)}, u32[]{:S(2)}) %collective-permute-start.30) | collective-permute-done | bytes 131104 | tf_op jit(solution)/shard_map/ppermute | solution.py:41
  59.0 1.4 collective-permute-start.38
  62.5 1.4 collective-permute-start.25
  63.8 1.2 collective-permute-done.38.refs_14_
  65.5 1.9 %collective-permute-done.32.refs_10_ = bf16[128,512]{1,0:T(8,128)(2,1)S(1)} collective-permute-done((bf16[128,512]{1,0:T(8,128)(2,1)S(1)}, bf16[128,512]{1,0:T(8,128)(2,1)S(1)}, u32[]{:S(2)}, u32[]{:S(2)}) %collective-permute-start.32) | collective-permute-done | bytes 131104 | tf_op jit(solution)/shard_map/ppermute | solution.py:41
  68.9 1.5 collective-permute-start.40
  71.2 1.3 collective-permute-start.27
  74.8 2.2 %collective-permute-done.27.refs_5_ = bf16[128,512]{1,0:T(8,128)(2,1)S(1)} collective-permute-done((bf16[128,512]{1,0:T(8,128)(2,1)S(1)}, bf16[128,512]{1,0:T(8,128)(2,1)S(1)}, u32[]{:S(2)}, u32[]{:S(2)}) %collective-permute-start.27) | collective-permute-done | bytes 131104 | tf_op jit(solution)/shard_map/ppermute | solution.py:41
  77.7 1.5 collective-permute-done.21.refs_3_
  80.5 3.6 %collective-permute-done.23 = bf16[64,512]{1,0:T(8,128)(2,1)S(1)} collective-permute-done((bf16[64,512]{1,0:T(8,128)(2,1)S(1)}, bf16[64,512]{1,0:T(8,128)(2,1)S(1)}, u32[]{:S(2)}, u32[]{:S(2)}) %collective-permute-start.23) | collective-permute-done | bytes 65568 | tf_op jit(solution)/shard_map/ppermute | solution.py:41
  85.2 3.1 %collective-permute-done.42 = bf16[64,512]{1,0:T(8,128)(2,1)S(1)} collective-permute-done((bf16[64,512]{1,0:T(8,128)(2,1)S(1)}, bf16[64,512]{1,0:T(8,128)(2,1)S(1)}, u32[]{:S(2)}, u32[]{:S(2)}) %collective-permute-start.42) | collective-permute-done | bytes 65568 | tf_op jit(solution)/shard_map/ppermute | solution.py:41
  89.5 3.1 %collective-permute-done.29 = bf16[64,512]{1,0:T(8,128)(2,1)S(1)} collective-permute-done((bf16[64,512]{1,0:T(8,128)(2,1)S(1)}, bf16[64,512]{1,0:T(8,128)(2,1)S(1)}, u32[]{:S(2)}, u32[]{:S(2)}) %collective-permute-start.29) | collective-permute-done | bytes 65568 | tf_op jit(solution)/shard_map/ppermute | solution.py:41
  94.2 25.6 %experts.1 = (bf16[128,512]{1,0:T(8,128)(2,1)S(1)}, bf16[128,512]{1,0:T(8,128)(2,1)S(1)}, bf16[128,512]{1,0:T(8,128)(2,1)S(1)}, bf16[128,512]{1,0:T(8,128)(2,1)S...) custom-call(s32[2]{0:T(128)S(1)} %pad_add_fusion.where, ...), custom_call_target="tpu_custom_call" | custom-call | tf_op jit(solution)/shard_map/experts/pallas_call | solution.py:395
  123.4 3.5 %collective-permute-done.54 = bf16[64,512]{1,0:T(8,128)(2,1)S(1)} collective-permute-done((bf16[64,512]{1,0:T(8,128)(2,1)S(1)}, bf16[64,512]{1,0:T(8,128)(2,1)S(1)}, u32[]{:S(2)}, u32[]{:S(2)}) %collective-permute-start.54) | collective-permute-done | bytes 65568 | tf_op jit(solution)/shard_map/ppermute | solution.py:41
  126.9 1.1 collective-permute-start.61
  128.1 3.0 %collective-permute-done.61 = bf16[64,512]{1,0:T(8,128)(2,1)S(1)} collective-permute-done((bf16[64,512]{1,0:T(8,128)(2,1)S(1)}, bf16[64,512]{1,0:T(8,128)(2,1)S(1)}, u32[]{:S(2)}, u32[]{:S(2)}) %collective-permute-start.61) | collective-permute-done | bytes 65568 | tf_op jit(solution)/shard_map/ppermute | solution.py:41
  132.0 3.4 %collective-permute-done.70 = bf16[64,512]{1,0:T(8,128)(2,1)S(1)} collective-permute-done((bf16[64,512]{1,0:T(8,128)(2,1)S(1)}, bf16[64,512]{1,0:T(8,128)(2,1)S(1)}, u32[]{:S(2)}, u32[]{:S(2)}) %collective-permute-start.70) | collective-permute-done | bytes 65568 | tf_op jit(solution)/shard_map/ppermute | solution.py:41
  135.4 1.1 collective-permute-start.77
  136.7 3.0 %collective-permute-done.77 = bf16[64,512]{1,0:T(8,128)(2,1)S(1)} collective-permute-done((bf16[64,512]{1,0:T(8,128)(2,1)S(1)}, bf16[64,512]{1,0:T(8,128)(2,1)S(1)}, u32[]{:S(2)}, u32[]{:S(2)}) %collective-permute-start.77) | collective-permute-done | bytes 65568 | tf_op jit(solution)/shard_map/ppermute | solution.py:41
  140.5 4.1 %collective-permute-done.55 = bf16[128,512]{1,0:T(8,128)(2,1)S(1)} collective-permute-done((bf16[128,512]{1,0:T(8,128)(2,1)S(1)}, bf16[128,512]{1,0:T(8,128)(2,1)S(1)}, u32[]{:S(2)}, u32[]{:S(2)}) %collective-permute-start.55) | collective-permute-done | bytes 131104 | tf_op jit(solution)/shard_map/ppermute | solution.py:41
  144.7 1.1 collective-permute-start.62
  145.9 3.7 %collective-permute-done.62 = bf16[128,512]{1,0:T(8,128)(2,1)S(1)} collective-permute-done((bf16[128,512]{1,0:T(8,128)(2,1)S(1)}, bf16[128,512]{1,0:T(8,128)(2,1)S(1)}, u32[]{:S(2)}, u32[]{:S(2)}) %collective-permute-start.62) | collective-permute-done | bytes 131104 | tf_op jit(solution)/shard_map/ppermute | solution.py:41
  150.5 4.1 %collective-permute-done.71 = bf16[128,512]{1,0:T(8,128)(2,1)S(1)} collective-permute-done((bf16[128,512]{1,0:T(8,128)(2,1)S(1)}, bf16[128,512]{1,0:T(8,128)(2,1)S(1)}, u32[]{:S(2)}, u32[]{:S(2)}) %collective-permute-start.71) | collective-permute-done | bytes 131104 | tf_op jit(solution)/shard_map/ppermute | solution.py:41
  154.6 1.1 collective-permute-start.78
  155.9 3.7 %collective-permute-done.78 = bf16[128,512]{1,0:T(8,128)(2,1)S(1)} collective-permute-done((bf16[128,512]{1,0:T(8,128)(2,1)S(1)}, bf16[128,512]{1,0:T(8,128)(2,1)S(1)}, u32[]{:S(2)}, u32[]{:S(2)}) %collective-permute-start.78) | collective-permute-done | bytes 131104 | tf_op jit(solution)/shard_map/ppermute | solution.py:41
  160.4 4.1 %collective-permute-done.56 = bf16[128,512]{1,0:T(8,128)(2,1)S(1)} collective-permute-done((bf16[128,512]{1,0:T(8,128)(2,1)S(1)}, bf16[128,512]{1,0:T(8,128)(2,1)S(1)}, u32[]{:S(2)}, u32[]{:S(2)}) %collective-permute-start.56) | collective-permute-done | bytes 131104 | tf_op jit(solution)/shard_map/ppermute | solution.py:41
  165.8 3.7 %collective-permute-done.63 = bf16[128,512]{1,0:T(8,128)(2,1)S(1)} collective-permute-done((bf16[128,512]{1,0:T(8,128)(2,1)S(1)}, bf16[128,512]{1,0:T(8,128)(2,1)S(1)}, u32[]{:S(2)}, u32[]{:S(2)}) %collective-permute-start.63) | collective-permute-done | bytes 131104 | tf_op jit(solution)/shard_map/ppermute | solution.py:41
  170.2 1.4 collective-permute-start.79
  171.6 4.1 %collective-permute-done.72 = bf16[128,512]{1,0:T(8,128)(2,1)S(1)} collective-permute-done((bf16[128,512]{1,0:T(8,128)(2,1)S(1)}, bf16[128,512]{1,0:T(8,128)(2,1)S(1)}, u32[]{:S(2)}, u32[]{:S(2)}) %collective-permute-start.72) | collective-permute-done | bytes 131104 | tf_op jit(solution)/shard_map/ppermute | solution.py:41
  176.6 1.3 collective-permute-start.64
  178.8 1.3 collective-permute-start.80
  181.7 1.2 collective-permute-done.73
  (204 shorter events, 52.7 us)
Async XLA Ops:
  1.8 8.0 %collective-permute-start.7 = (bf16[64,640]{1,0:T(8,128)(2,1)S(1)}, bf16[64,640]{1,0:T(8,128)(2,1)}, u32[]{:S(2)}, u32[]{:S(2)}) collective-permute-start(bf16[64,640]{1,0:T(8,128)(2,1)S(1)} %pack.1), channel_id=1, source_target_pairs={{0,4},{2,0},{6,2},{10,6},{14,10},{12,14},{8,12},{4,8},{1,5},{3,1},... | collective-permute-start | bytes 245768 | tf_op jit(solution)/shard_map/ppermute | solution.py:41
  9.8 6.8 %collective-permute-start.9 = (bf16[64,640]{1,0:T(8,128)(2,1)}, bf16[64,640]{1,0:T(8,128)(2,1)S(1)}, u32[]{:S(2)}, u32[]{:S(2)}) collective-permute-start(bf16[64,640]{1,0:T(8,128)(2,1)} %collective-permute-done.7), channel_id=1, source_target_pairs={{0,1},{1,0},{2,3},{3,2},{4,5},{5,4},{6,7},{7,6},{8,9},{9,8},{10,11... | collective-permute-start | bytes 245768 | tf_op jit(solution)/shard_map/ppermute | solution.py:45
  9.8 6.8 %collective-permute-start.8 = (bf16[64,640]{1,0:T(8,128)(2,1)}, bf16[64,640]{1,0:T(8,128)(2,1)}, u32[]{:S(2)}, u32[]{:S(2)}) collective-permute-start(bf16[64,640]{1,0:T(8,128)(2,1)} %collective-permute-done.7), channel_id=1, source_target_pairs={{0,4},{2,0},{6,2},{10,6},{14,10},{12,14},{8,12},{4,8},{1,5},{3,1},... | collective-permute-start | bytes 245768 | tf_op jit(solution)/shard_map/ppermute | solution.py:41
  11.4 7.0 %collective-permute-start.3 = (bf16[64,640]{1,0:T(8,128)(2,1)}, bf16[64,640]{1,0:T(8,128)(2,1)S(1)}, u32[]{:S(2)}, u32[]{:S(2)}) collective-permute-start(bf16[64,640]{1,0:T(8,128)(2,1)} %collective-permute-done), channel_id=1, source_target_pairs={{0,1},{1,0},{2,3},{3,2},{4,5},{5,4},{6,7},{7,6},{8,9},{9,8},{10,11... | collective-permute-start | bytes 245768 | tf_op jit(solution)/shard_map/ppermute | solution.py:45
  11.6 6.7 %collective-permute-start.2 = (bf16[64,640]{1,0:T(8,128)(2,1)}, bf16[64,640]{1,0:T(8,128)(2,1)}, u32[]{:S(2)}, u32[]{:S(2)}) collective-permute-start(bf16[64,640]{1,0:T(8,128)(2,1)} %collective-permute-done), channel_id=1, source_target_pairs={{0,2},{2,6},{6,10},{10,14},{14,12},{12,8},{8,4},{4,0},{1,3},{3,7},... | collective-permute-start | bytes 245768 | tf_op jit(solution)/shard_map/ppermute | solution.py:41
  16.6 5.4 %collective-permute-start.11 = (bf16[64,640]{1,0:T(8,128)(2,1)}, bf16[64,640]{1,0:T(8,128)(2,1)}, u32[]{:S(2)}, u32[]{:S(2)}) collective-permute-start(bf16[64,640]{1,0:T(8,128)(2,1)} %collective-permute-done.8), channel_id=1, source_target_pairs={{0,1},{1,0},{2,3},{3,2},{4,5},{5,4},{6,7},{7,6},{8,9},{9,8},{10,11... | collective-permute-start | bytes 245768 | tf_op jit(solution)/shard_map/ppermute | solution.py:45
  16.7 5.3 %collective-permute-start.10 = (bf16[64,640]{1,0:T(8,128)(2,1)}, bf16[64,640]{1,0:T(8,128)(2,1)}, u32[]{:S(2)}, u32[]{:S(2)}) collective-permute-start(bf16[64,640]{1,0:T(8,128)(2,1)} %collective-permute-done.8), channel_id=1, source_target_pairs={{0,4},{2,0},{6,2},{10,6},{14,10},{12,14},{8,12},{4,8},{1,5},{3,1},... | collective-permute-start | bytes 245768 | tf_op jit(solution)/shard_map/ppermute | solution.py:41
  18.5 5.0 %collective-permute-start.4 = (bf16[64,640]{1,0:T(8,128)(2,1)}, bf16[64,640]{1,0:T(8,128)(2,1)}, u32[]{:S(2)}, u32[]{:S(2)}) collective-permute-start(bf16[64,640]{1,0:T(8,128)(2,1)} %collective-permute-done.2), channel_id=1, source_target_pairs={{0,2},{2,6},{6,10},{10,14},{14,12},{12,8},{8,4},{4,0},{1,3},{3,7},... | collective-permute-start | bytes 245768 | tf_op jit(solution)/shard_map/ppermute | solution.py:41
  22.8 12.2 %collective-permute-start.15 = (bf16[64,640]{1,0:T(8,128)(2,1)}, bf16[64,640]{1,0:T(8,128)(2,1)S(1)}, u32[]{:S(2)}, u32[]{:S(2)}) collective-permute-start(bf16[64,640]{1,0:T(8,128)(2,1)} %collective-permute-done.10), channel_id=1, source_target_pairs={{0,1},{1,0},{2,3},{3,2},{4,5},{5,4},{6,7},{7,6},{8,9},{9,8},{10,11... | collective-permute-start | bytes 245768 | tf_op jit(solution)/shard_map/ppermute | solution.py:45
  24.3 9.4 %collective-permute-start.13 = (bf16[64,640]{1,0:T(8,128)(2,1)}, bf16[64,640]{1,0:T(8,128)(2,1)S(1)}, u32[]{:S(2)}, u32[]{:S(2)}) collective-permute-start(bf16[64,640]{1,0:T(8,128)(2,1)} %collective-permute-done.4), channel_id=1, source_target_pairs={{0,1},{1,0},{2,3},{3,2},{4,5},{5,4},{6,7},{7,6},{8,9},{9,8},{10,11... | collective-permute-start | bytes 245768 | tf_op jit(solution)/shard_map/ppermute | solution.py:45
  24.3 6.5 %collective-permute-start.12 = (bf16[32,640]{1,0:T(8,128)(2,1)S(1)}, bf16[32,640]{1,0:T(8,128)(2,1)S(1)}, u32[]{:S(2)}, u32[]{:S(2)}) collective-permute-start(bf16[32,640]{1,0:T(8,128)(2,1)S(1)} %slice.46), channel_id=1, source_target_pairs={{0,4},{2,0},{6,2},{10,6},{14,10},{12,14},{8,12},{4,8},{1,5},{3,1},... | collective-permute-start | bytes 122888 | tf_op jit(solution)/shard_map/ppermute | solution.py:41
  50.8 7.5 %collective-permute-start.37 = (bf16[128,512]{1,0:T(8,128)(2,1)S(1)}, bf16[128,512]{1,0:T(8,128)(2,1)S(1)}, u32[]{:S(2)}, u32[]{:S(2)}) collective-permute-start(bf16[128,512]{1,0:T(8,128)(2,1)S(1)} %get-tuple-element.141.refs_8_), channel_id=1, source_target_pairs={{0,4},{2,0},{6,2},{10,6},{14,10},{12,14},{8,12},{4,8},{1,5},{3,1},... | collective-permute-start | bytes 393224 | tf_op jit(solution)/shard_map/ppermute | solution.py:41
  52.4 5.9 %collective-permute-start.30 = (bf16[128,512]{1,0:T(8,128)(2,1)S(1)}, bf16[128,512]{1,0:T(8,128)(2,1)S(1)}, u32[]{:S(2)}, u32[]{:S(2)}) collective-permute-start(bf16[128,512]{1,0:T(8,128)(2,1)S(1)} %get-tuple-element.141.refs_8_), channel_id=1, source_target_pairs={{0,2},{2,6},{6,10},{10,14},{14,12},{12,8},{8,4},{4,0},{1,3},{3,7},... | collective-permute-start | bytes 393224 | tf_op jit(solution)/shard_map/ppermute | solution.py:41
  53.5 8.9 %collective-permute-start.24 = (bf16[128,512]{1,0:T(8,128)(2,1)S(1)}, bf16[128,512]{1,0:T(8,128)(2,1)S(1)}, u32[]{:S(2)}, u32[]{:S(2)}) collective-permute-start(bf16[128,512]{1,0:T(8,128)(2,1)S(1)} %get-tuple-element.129.refs_0_), channel_id=1, source_target_pairs={{0,4},{2,0},{6,2},{10,6},{14,10},{12,14},{8,12},{4,8},{1,5},{3,1},... | collective-permute-start | bytes 393224 | tf_op jit(solution)/shard_map/ppermute | solution.py:41
  55.1 6.4 %collective-permute-start.18 = (bf16[128,512]{1,0:T(8,128)(2,1)S(1)}, bf16[128,512]{1,0:T(8,128)(2,1)S(1)}, u32[]{:S(2)}, u32[]{:S(2)}) collective-permute-start(bf16[128,512]{1,0:T(8,128)(2,1)S(1)} %get-tuple-element.129.refs_0_), channel_id=1, source_target_pairs={{0,1},{1,0},{2,3},{3,2},{4,5},{5,4},{6,7},{7,6},{8,9},{9,8},{10,11... | collective-permute-start | bytes 393224 | tf_op jit(solution)/shard_map/ppermute | solution.py:45
  55.1 6.7 %collective-permute-start.17 = (bf16[128,512]{1,0:T(8,128)(2,1)S(1)}, bf16[128,512]{1,0:T(8,128)(2,1)S(1)}, u32[]{:S(2)}, u32[]{:S(2)}) collective-permute-start(bf16[128,512]{1,0:T(8,128)(2,1)S(1)} %get-tuple-element.129.refs_0_), channel_id=1, source_target_pairs={{0,2},{2,6},{6,10},{10,14},{14,12},{12,8},{8,4},{4,0},{1,3},{3,7},... | collective-permute-start | bytes 393224 | tf_op jit(solution)/shard_map/ppermute | solution.py:41
  59.0 6.0 %collective-permute-start.38 = (bf16[128,512]{1,0:T(8,128)(2,1)S(1)}, bf16[128,512]{1,0:T(8,128)(2,1)S(1)}, u32[]{:S(2)}, u32[]{:S(2)}) collective-permute-start(bf16[128,512]{1,0:T(8,128)(2,1)S(1)} %collective-permute-done.37.refs_15_), channel_id=1, source_target_pairs={{0,4},{2,0},{6,2},{10,6},{14,10},{12,14},{8,12},{4,8},{1,5},{3,1},... | collective-permute-start | bytes 393224 | tf_op jit(solution)/shard_map/ppermute | solution.py:41
  61.8 5.7 %collective-permute-start.32 = (bf16[128,512]{1,0:T(8,128)(2,1)S(1)}, bf16[128,512]{1,0:T(8,128)(2,1)S(1)}, u32[]{:S(2)}, u32[]{:S(2)}) collective-permute-start(bf16[128,512]{1,0:T(8,128)(2,1)S(1)} %collective-permute-done.30.refs_9_), channel_id=1, source_target_pairs={{0,2},{2,6},{6,10},{10,14},{14,12},{12,8},{8,4},{4,0},{1,3},{3,7},... | collective-permute-start | bytes 393224 | tf_op jit(solution)/shard_map/ppermute | solution.py:41
  62.4 5.0 %collective-permute-start.26 = (bf16[128,512]{1,0:T(8,128)(2,1)S(1)}, bf16[128,512]{1,0:T(8,128)(2,1)S(1)}, u32[]{:S(2)}, u32[]{:S(2)}) collective-permute-start(bf16[128,512]{1,0:T(8,128)(2,1)S(1)} %collective-permute-done.24.refs_7_), channel_id=1, source_target_pairs={{0,1},{1,0},{2,3},{3,2},{4,5},{5,4},{6,7},{7,6},{8,9},{9,8},{10,11... | collective-permute-start | bytes 393224 | tf_op jit(solution)/shard_map/ppermute | solution.py:45
  62.5 5.9 %collective-permute-start.25 = (bf16[128,512]{1,0:T(8,128)(2,1)S(1)}, bf16[128,512]{1,0:T(8,128)(2,1)S(1)}, u32[]{:S(2)}, u32[]{:S(2)}) collective-permute-start(bf16[128,512]{1,0:T(8,128)(2,1)S(1)} %collective-permute-done.24.refs_7_), channel_id=1, source_target_pairs={{0,4},{2,0},{6,2},{10,6},{14,10},{12,14},{8,12},{4,8},{1,5},{3,1},... | collective-permute-start | bytes 393224 | tf_op jit(solution)/shard_map/ppermute | solution.py:41
  65.0 6.1 %collective-permute-start.19 = (bf16[128,512]{1,0:T(8,128)(2,1)S(1)}, bf16[128,512]{1,0:T(8,128)(2,1)S(1)}, u32[]{:S(2)}, u32[]{:S(2)}) collective-permute-start(bf16[128,512]{1,0:T(8,128)(2,1)S(1)} %collective-permute-done.17.refs_1_), channel_id=1, source_target_pairs={{0,2},{2,6},{6,10},{10,14},{14,12},{12,8},{8,4},{4,0},{1,3},{3,7},... | collective-permute-start | bytes 393224 | tf_op jit(solution)/shard_map/ppermute | solution.py:41
  67.4 5.1 %collective-permute-start.35 = (bf16[128,512]{1,0:T(8,128)(2,1)S(1)}, bf16[128,512]{1,0:T(8,128)(2,1)S(1)}, u32[]{:S(2)}, u32[]{:S(2)}) collective-permute-start(bf16[128,512]{1,0:T(8,128)(2,1)S(1)} %collective-permute-done.32.refs_10_), channel_id=1, source_target_pairs={{0,1},{1,0},{2,3},{3,2},{4,5},{5,4},{6,7},{7,6},{8,9},{9,8},{10,11... | collective-permute-start | bytes 393224 | tf_op jit(solution)/shard_map/ppermute | solution.py:45
  68.4 5.4 %collective-permute-start.34 = (bf16[128,512]{1,0:T(8,128)(2,1)S(1)}, bf16[128,512]{1,0:T(8,128)(2,1)S(1)}, u32[]{:S(2)}, u32[]{:S(2)}) collective-permute-start(bf16[128,512]{1,0:T(8,128)(2,1)S(1)} %collective-permute-done.32.refs_10_), channel_id=1, source_target_pairs={{0,2},{2,6},{6,10},{10,14},{14,12},{12,8},{8,4},{4,0},{1,3},{3,7},... | collective-permute-start | bytes 393224 | tf_op jit(solution)/shard_map/ppermute | solution.py:41
  68.9 5.4 %collective-permute-start.40 = (bf16[128,512]{1,0:T(8,128)(2,1)S(1)}, bf16[128,512]{1,0:T(8,128)(2,1)S(1)}, u32[]{:S(2)}, u32[]{:S(2)}) collective-permute-start(bf16[128,512]{1,0:T(8,128)(2,1)S(1)} %collective-permute-done.38.refs_14_), channel_id=1, source_target_pairs={{0,4},{2,0},{6,2},{10,6},{14,10},{12,14},{8,12},{4,8},{1,5},{3,1},... | collective-permute-start | bytes 393224 | tf_op jit(solution)/shard_map/ppermute | solution.py:41
  71.2 5.9 %collective-permute-start.27 = (bf16[128,512]{1,0:T(8,128)(2,1)S(1)}, bf16[128,512]{1,0:T(8,128)(2,1)S(1)}, u32[]{:S(2)}, u32[]{:S(2)}) collective-permute-start(bf16[128,512]{1,0:T(8,128)(2,1)S(1)} %collective-permute-done.25.refs_6_), channel_id=1, source_target_pairs={{0,4},{2,0},{6,2},{10,6},{14,10},{12,14},{8,12},{4,8},{1,5},{3,1},... | collective-permute-start | bytes 393224 | tf_op jit(solution)/shard_map/ppermute | solution.py:41
  73.7 5.4 %collective-permute-start.21 = (bf16[128,512]{1,0:T(8,128)(2,1)S(1)}, bf16[128,512]{1,0:T(8,128)(2,1)S(1)}, u32[]{:S(2)}, u32[]{:S(2)}) collective-permute-start(bf16[128,512]{1,0:T(8,128)(2,1)S(1)} %collective-permute-done.19.refs_2_), channel_id=1, source_target_pairs={{0,2},{2,6},{6,10},{10,14},{14,12},{12,8},{8,4},{4,0},{1,3},{3,7},... | collective-permute-start | bytes 393224 | tf_op jit(solution)/shard_map/ppermute | solution.py:41
  74.2 5.6 %collective-permute-start.36 = (bf16[64,512]{1,0:T(8,128)(2,1)S(1)}, bf16[64,512]{1,0:T(8,128)(2,1)S(1)}, u32[]{:S(2)}, u32[]{:S(2)}) collective-permute-start(bf16[64,512]{1,0:T(8,128)(2,1)S(1)} %slice.54), channel_id=1, source_target_pairs={{0,2},{2,6},{6,10},{10,14},{14,12},{12,8},{8,4},{4,0},{1,3},{3,7},... | collective-permute-start | bytes 196616 | tf_op jit(solution)/shard_map/ppermute | solution.py:41
  74.8 17.9 %collective-permute-start.48 = (bf16[128,512]{1,0:T(8,128)(2,1)S(1)}, bf16[128,512]{1,0:T(8,128)(2,1)S(1)}, u32[]{:S(2)}, u32[]{:S(2)}) collective-permute-start(bf16[128,512]{1,0:T(8,128)(2,1)S(1)} %collective-permute-done.40.refs_13_), channel_id=1, source_target_pairs={{0,1},{1,0},{2,3},{3,2},{4,5},{5,4},{6,7},{7,6},{8,9},{9,8},{10,11... | collective-permute-start | bytes 393224 | tf_op jit(solution)/shard_map/ppermute | solution.py:45
  77.1 16.1 %collective-permute-start.46 = (bf16[128,512]{1,0:T(8,128)(2,1)S(1)}, bf16[128,512]{1,0:T(8,128)(2,1)S(1)}, u32[]{:S(2)}, u32[]{:S(2)}) collective-permute-start(bf16[128,512]{1,0:T(8,128)(2,1)S(1)} %collective-permute-done.34.refs_11_), channel_id=1, source_target_pairs={{0,1},{1,0},{2,3},{3,2},{4,5},{5,4},{6,7},{7,6},{8,9},{9,8},{10,11... | collective-permute-start | bytes 393224 | tf_op jit(solution)/shard_map/ppermute | solution.py:45
  77.1 16.1 %collective-permute-start.45 = (bf16[128,512]{1,0:T(8,128)(2,1)S(1)}, bf16[128,512]{1,0:T(8,128)(2,1)S(1)}, u32[]{:S(2)}, u32[]{:S(2)}) collective-permute-start(bf16[128,512]{1,0:T(8,128)(2,1)S(1)} %collective-permute-done.27.refs_5_), channel_id=1, source_target_pairs={{0,1},{1,0},{2,3},{3,2},{4,5},{5,4},{6,7},{7,6},{8,9},{9,8},{10,11... | collective-permute-start | bytes 393224 | tf_op jit(solution)/shard_map/ppermute | solution.py:45
  79.1 14.1 %collective-permute-start.43 = (bf16[128,512]{1,0:T(8,128)(2,1)S(1)}, bf16[128,512]{1,0:T(8,128)(2,1)S(1)}, u32[]{:S(2)}, u32[]{:S(2)}) collective-permute-start(bf16[128,512]{1,0:T(8,128)(2,1)S(1)} %collective-permute-done.21.refs_3_), channel_id=1, source_target_pairs={{0,1},{1,0},{2,3},{3,2},{4,5},{5,4},{6,7},{7,6},{8,9},{9,8},{10,11... | collective-permute-start | bytes 393224 | tf_op jit(solution)/shard_map/ppermute | solution.py:45
  120.2 58.6 %collective-permute-start.49 = (bf16[128,512]{1,0:T(8,128)(2,1)S(1)}, bf16[128,512]{1,0:T(8,128)(2,1)S(1)}, u32[]{:S(2)}, u32[]{:S(2)}) collective-permute-start(bf16[128,512]{1,0:T(8,128)(2,1)S(1)} %get-tuple-element.162), channel_id=1, source_target_pairs={{0,1},{1,0},{2,3},{3,2},{4,5},{5,4},{6,7},{7,6},{8,9},{9,8},{10,11... | collective-permute-start | bytes 393224 | tf_op jit(solution)/shard_map/ppermute | solution.py:45
  120.4 40.0 %collective-permute-start.50 = (bf16[128,512]{1,0:T(8,128)(2,1)S(1)}, bf16[128,512]{1,0:T(8,128)(2,1)S(1)}, u32[]{:S(2)}, u32[]{:S(2)}) collective-permute-start(bf16[128,512]{1,0:T(8,128)(2,1)S(1)} %get-tuple-element.164), channel_id=1, source_target_pairs={{0,1},{1,0},{2,3},{3,2},{4,5},{5,4},{6,7},{7,6},{8,9},{9,8},{10,11... | collective-permute-start | bytes 393224 | tf_op jit(solution)/shard_map/ppermute | solution.py:45
  120.7 19.7 %collective-permute-start.51 = (bf16[128,512]{1,0:T(8,128)(2,1)S(1)}, bf16[128,512]{1,0:T(8,128)(2,1)S(1)}, u32[]{:S(2)}, u32[]{:S(2)}) collective-permute-start(bf16[128,512]{1,0:T(8,128)(2,1)S(1)} %get-tuple-element.166), channel_id=1, source_target_pairs={{0,1},{1,0},{2,3},{3,2},{4,5},{5,4},{6,7},{7,6},{8,9},{9,8},{10,11... | collective-permute-start | bytes 393224 | tf_op jit(solution)/shard_map/ppermute | solution.py:45
  136.6 29.1 %collective-permute-start.58 = (bf16[128,512]{1,0:T(8,128)(2,1)S(1)}, bf16[128,512]{1,0:T(8,128)(2,1)S(1)}, u32[]{:S(2)}, u32[]{:S(2)}) collective-permute-start(bf16[128,512]{1,0:T(8,128)(2,1)S(1)} %get-tuple-element.172), channel_id=1, source_target_pairs={{0,1},{1,0},{2,3},{3,2},{4,5},{5,4},{6,7},{7,6},{8,9},{9,8},{10,11... | collective-permute-start | bytes 393224 | tf_op jit(solution)/shard_map/ppermute | solution.py:45
  140.4 5.4 %collective-permute-start.59 = (bf16[128,512]{1,0:T(8,128)(2,1)S(1)}, bf16[128,512]{1,0:T(8,128)(2,1)S(1)}, u32[]{:S(2)}, u32[]{:S(2)}) collective-permute-start(bf16[128,512]{1,0:T(8,128)(2,1)S(1)} %get-tuple-element.174), channel_id=1, source_target_pairs={{0,1},{1,0},{2,3},{3,2},{4,5},{5,4},{6,7},{7,6},{8,9},{9,8},{10,11... | collective-permute-start | bytes 393224 | tf_op jit(solution)/shard_map/ppermute | solution.py:45
  150.4 5.4 %collective-permute-start.75 = (bf16[128,512]{1,0:T(8,128)(2,1)S(1)}, bf16[128,512]{1,0:T(8,128)(2,1)S(1)}, u32[]{:S(2)}, u32[]{:S(2)}) collective-permute-start(bf16[128,512]{1,0:T(8,128)(2,1)S(1)} %get-tuple-element.190), channel_id=1, source_target_pairs={{0,1},{1,0},{2,3},{3,2},{4,5},{5,4},{6,7},{7,6},{8,9},{9,8},{10,11... | collective-permute-start | bytes 393224 | tf_op jit(solution)/shard_map/ppermute | solution.py:45
  155.8 25.9 %collective-permute-start.65 = (bf16[128,512]{1,0:T(8,128)(2,1)S(1)}, bf16[128,512]{1,0:T(8,128)(2,1)S(1)}, u32[]{:S(2)}, u32[]{:S(2)}) collective-permute-start(bf16[128,512]{1,0:T(8,128)(2,1)S(1)} %get-tuple-element.178), channel_id=1, source_target_pairs={{0,1},{1,0},{2,3},{3,2},{4,5},{5,4},{6,7},{7,6},{8,9},{9,8},{10,11... | collective-permute-start | bytes 393224 | tf_op jit(solution)/shard_map/ppermute | solution.py:45
  159.6 5.0 %collective-permute-start.56 = (bf16[128,512]{1,0:T(8,128)(2,1)S(1)}, bf16[128,512]{1,0:T(8,128)(2,1)S(1)}, u32[]{:S(2)}, u32[]{:S(2)}) collective-permute-start(bf16[128,512]{1,0:T(8,128)(2,1)S(1)} %add_convert_fusion.11), channel_id=1, source_target_pairs={{0,2},{2,6},{6,10},{10,14},{14,12},{12,8},{8,4},{4,0},{1,3},{3,7},... | collective-permute-start | bytes 393224 | tf_op jit(solution)/shard_map/ppermute | solution.py:41
  160.3 9.9 %collective-permute-start.66 = (bf16[128,512]{1,0:T(8,128)(2,1)S(1)}, bf16[128,512]{1,0:T(8,128)(2,1)S(1)}, u32[]{:S(2)}, u32[]{:S(2)}) collective-permute-start(bf16[128,512]{1,0:T(8,128)(2,1)S(1)} %get-tuple-element.180), channel_id=1, source_target_pairs={{0,1},{1,0},{2,3},{3,2},{4,5},{5,4},{6,7},{7,6},{8,9},{9,8},{10,11... | collective-permute-start | bytes 393224 | tf_op jit(solution)/shard_map/ppermute | solution.py:45
  164.5 5.0 %collective-permute-start.63 = (bf16[128,512]{1,0:T(8,128)(2,1)S(1)}, bf16[128,512]{1,0:T(8,128)(2,1)S(1)}, u32[]{:S(2)}, u32[]{:S(2)}) collective-permute-start(bf16[128,512]{1,0:T(8,128)(2,1)S(1)} %add_convert_fusion.8), channel_id=1, source_target_pairs={{0,4},{2,0},{6,2},{10,6},{14,10},{12,14},{8,12},{4,8},{1,5},{3,1},... | collective-permute-start | bytes 393224 | tf_op jit(solution)/shard_map/ppermute | solution.py:41
  165.7 10.9 %collective-permute-start.74 = (bf16[128,512]{1,0:T(8,128)(2,1)S(1)}, bf16[128,512]{1,0:T(8,128)(2,1)S(1)}, u32[]{:S(2)}, u32[]{:S(2)}) collective-permute-start(bf16[128,512]{1,0:T(8,128)(2,1)S(1)} %get-tuple-element.188), channel_id=1, source_target_pairs={{0,1},{1,0},{2,3},{3,2},{4,5},{5,4},{6,7},{7,6},{8,9},{9,8},{10,11... | collective-permute-start | bytes 393224 | tf_op jit(solution)/shard_map/ppermute | solution.py:45
  169.5 6.3 %collective-permute-start.72 = (bf16[128,512]{1,0:T(8,128)(2,1)S(1)}, bf16[128,512]{1,0:T(8,128)(2,1)S(1)}, u32[]{:S(2)}, u32[]{:S(2)}) collective-permute-start(bf16[128,512]{1,0:T(8,128)(2,1)S(1)} %add_convert_fusion.4), channel_id=1, source_target_pairs={{0,2},{2,6},{6,10},{10,14},{14,12},{12,8},{8,4},{4,0},{1,3},{3,7},... | collective-permute-start | bytes 393224 | tf_op jit(solution)/shard_map/ppermute | solution.py:41
  170.2 7.7 %collective-permute-start.79 = (bf16[128,512]{1,0:T(8,128)(2,1)S(1)}, bf16[128,512]{1,0:T(8,128)(2,1)S(1)}, u32[]{:S(2)}, u32[]{:S(2)}) collective-permute-start(bf16[128,512]{1,0:T(8,128)(2,1)S(1)} %add_convert_fusion.1), channel_id=1, source_target_pairs={{0,4},{2,0},{6,2},{10,6},{14,10},{12,14},{8,12},{4,8},{1,5},{3,1},... | collective-permute-start | bytes 393224 | tf_op jit(solution)/shard_map/ppermute | solution.py:41
  175.8 5.0 %collective-permute-start.57 = (bf16[128,512]{1,0:T(8,128)(2,1)S(1)}, bf16[128,512]{1,0:T(8,128)(2,1)S(1)}, u32[]{:S(2)}, u32[]{:S(2)}) collective-permute-start(bf16[128,512]{1,0:T(8,128)(2,1)S(1)} %add_convert_fusion.10), channel_id=1, source_target_pairs={{0,2},{2,6},{6,10},{10,14},{14,12},{12,8},{8,4},{4,0},{1,3},{3,7},... | collective-permute-start | bytes 393224 | tf_op jit(solution)/shard_map/ppermute | solution.py:41
  176.6 5.0 %collective-permute-start.64 = (bf16[128,512]{1,0:T(8,128)(2,1)S(1)}, bf16[128,512]{1,0:T(8,128)(2,1)S(1)}, u32[]{:S(2)}, u32[]{:S(2)}) collective-permute-start(bf16[128,512]{1,0:T(8,128)(2,1)S(1)} %add_convert_fusion.7), channel_id=1, source_target_pairs={{0,4},{2,0},{6,2},{10,6},{14,10},{12,14},{8,12},{4,8},{1,5},{3,1},... | collective-permute-start | bytes 393224 | tf_op jit(solution)/shard_map/ppermute | solution.py:41
  177.9 5.0 %collective-permute-start.73 = (bf16[128,512]{1,0:T(8,128)(2,1)S(1)}, bf16[128,512]{1,0:T(8,128)(2,1)S(1)}, u32[]{:S(2)}, u32[]{:S(2)}) collective-permute-start(bf16[128,512]{1,0:T(8,128)(2,1)S(1)} %add_convert_fusion.3), channel_id=1, source_target_pairs={{0,2},{2,6},{6,10},{10,14},{14,12},{12,8},{8,4},{4,0},{1,3},{3,7},... | collective-permute-start | bytes 393224 | tf_op jit(solution)/shard_map/ppermute | solution.py:41
  178.8 5.0 %collective-permute-start.80 = (bf16[128,512]{1,0:T(8,128)(2,1)S(1)}, bf16[128,512]{1,0:T(8,128)(2,1)S(1)}, u32[]{:S(2)}, u32[]{:S(2)}) collective-permute-start(bf16[128,512]{1,0:T(8,128)(2,1)S(1)} %add_convert_fusion), channel_id=1, source_target_pairs={{0,4},{2,0},{6,2},{10,6},{14,10},{12,14},{8,12},{4,8},{1,5},{3,1},... | collective-permute-start | bytes 393224 | tf_op jit(solution)/shard_map/ppermute | solution.py:41
  (39 other events, 155.9 us)

commit v8 on v7

--- a/solution.py
+++ b/solution.py
@@ -19,7 +19,7 @@
 WIDE = 640
 MIB = 1024 * 1024
 VMEM_LIMIT = 50 * MIB
-STREAMS = 2
+STREAMS = 1
 DEPTH = 3
 PIECES = 2
 SWAP = [(0, 1), (1, 0)]
@@ -103,14 +103,16 @@
     return parts[0]() + ahead.astype(jnp.float32) + back.astype(jnp.float32)
 
 
-def attend_kernel(count, blocks, info, q_ref, mine_ref, other_ref, up_ref, proj_ref, out_ref, m_ref, l_ref, acc_ref):
+def attend_kernel(count, blocks, info, q_ref, *refs):
+    up_ref, proj_ref, out_ref, m_ref, l_ref, acc_ref = refs[-6:]
+    latents = refs[:-6]
     chunk = pl.program_id(0)
     side = info[1]
     sources = lambda c: info[2 + c]
     order = lambda j: info[2 + count + j]
     segs = info.shape[0] - 2 - 3 * count
-    span = mine_ref.shape[1]
     heads, rows, _ = q_ref.shape
+    span = rows // 2
 
     @pl.when(chunk == 0)
     def _():
@@ -140,7 +142,7 @@
     kpos = jnp.concatenate(kpos_parts, axis=1)
     visible = (kpos >= low) & (kpos <= qpos)
 
-    lat = jnp.concatenate([mine_ref[...].reshape(keys, WIDE), other_ref[...].reshape(keys, WIDE)], axis=0)
+    lat = jnp.concatenate([ref[...].reshape(-1, WIDE) for ref in latents], axis=0)
     keyval = jnp.dot(lat[:, :LAT], up_ref[...], preferred_element_type=jnp.float32).astype(jnp.bfloat16)
     rope = lat[:, LAT : LAT + ROPE]
     scale = 1.0 / math.sqrt(NOPE + ROPE)
@@ -170,15 +172,18 @@
 def attend(info, q, mine, other, kv_up, out_proj, count):
     heads, rows, depth = q.shape
     blocks = math.gcd(count, 8)
-    span = mine.shape[1]
     whole = pl.BlockSpec(memory_space=pltpu.VMEM)
-    lat_spec = whole if blocks == count else pl.BlockSpec((blocks, span, WIDE), lambda i, *_: (i, 0, 0))
+    if blocks == count:
+        latents, lat_spec = [*mine, *other], whole
+    else:
+        latents = [jnp.stack(mine), jnp.stack(other)]
+        lat_spec = pl.BlockSpec((blocks, rows // 2, WIDE), lambda i, *_: (i, 0, 0))
     return pl.pallas_call(
         functools.partial(attend_kernel, count, blocks),
         grid_spec=pltpu.PrefetchScalarGridSpec(
             num_scalar_prefetch=1,
             grid=(count // blocks,),
-            in_specs=[whole, lat_spec, lat_spec, whole, whole],
+            in_specs=[whole] + [lat_spec] * len(latents) + [whole, whole],
             out_specs=whole,
             scratch_shapes=[
                 pltpu.VMEM((heads, rows, 1), jnp.float32),
@@ -189,7 +194,43 @@
         out_shape=pltpu.VMEM((rows, out_proj.shape[1]), jnp.bfloat16),
         compiler_params=pltpu.CompilerParams(vmem_limit_bytes=28 * MIB),
         name="attend",
-    )(info, q, mine, other, kv_up, out_proj)
+    )(info, q, *latents, kv_up, out_proj)
+
+
+def route_kernel(count, where, *refs):
+    mine, other, out_ref = refs[:count], refs[count : 2 * count], refs[2 * count]
+    _, rows, width = out_ref.shape
+    side, here = where[1], width // SLOTS
+    base = LAT + ROPE
+    lane = lax.broadcasted_iota(jnp.int32, (rows, width), 1)
+    own = (where[0] * here + lane // SLOTS).astype(jnp.float32)
+    slot = (lane % SLOTS).astype(jnp.float32)
+    first = lax.broadcasted_iota(jnp.int32, (rows, rows), 0)
+    before = (first > lax.broadcasted_iota(jnp.int32, (rows, rows), 1)).astype(jnp.float32).astype(jnp.bfloat16)
+    for c in range(count):
+        near, far = mine[c][:, LAT:].astype(jnp.float32), other[c][:, LAT:].astype(jnp.float32)
+        left, right = jnp.where(side == 0, near, far), jnp.where(side == 0, far, near)
+        facts = jnp.concatenate([left, right], axis=0)
+        hot, share = jnp.zeros((rows, width), jnp.float32), jnp.zeros((rows, width), jnp.float32)
+        for k in range(TOP):
+            hit = facts[:, ROPE + k : ROPE + k + 1] == own
+            hot = jnp.where(hit, 1.0, hot)
+            share = jnp.where(hit, facts[:, ROPE + TOP + k : ROPE + TOP + k + 1], share)
+        rank = jnp.dot(before, hot.astype(jnp.bfloat16), preferred_element_type=jnp.float32)
+        out_ref[c] = jnp.where(rank == slot, share, 0.0).astype(jnp.bfloat16)
+
+
+def route(where, mine, other, here):
+    count, (span, _) = len(mine), mine[0].shape
+    whole = pl.BlockSpec(memory_space=pltpu.VMEM)
+    return pl.pallas_call(
+        functools.partial(route_kernel, count),
+        in_specs=[pl.BlockSpec(memory_space=pltpu.SMEM)] + [whole] * (2 * count),
+        out_specs=whole,
+        out_shape=pltpu.VMEM((count, 2 * span, here * SLOTS), jnp.bfloat16),
+        compiler_params=pltpu.CompilerParams(vmem_limit_bytes=8 * MIB),
+        name="route",
+    )(where, *mine, *other)
 
 
 def stage_kernel(picks, *refs):
@@ -260,12 +301,9 @@
     out_ref, (latent_ref, ids_ref, weights_ref, rows) = refs[3], refs[4:8]
     base, tokens = latent_ref.shape
     span = out_ref.shape[0]
-    weights = weights_ref[...]
-    high = weights.astype(jnp.bfloat16).astype(jnp.float32)
     rows[...] = jnp.zeros_like(rows)
     rows[0:TOP] = ids_ref[...].astype(jnp.float32)
-    rows[TOP : 2 * TOP] = high
-    rows[2 * TOP : 3 * TOP] = weights - high
+    rows[TOP : 2 * TOP] = weights_ref[...]
     row = lax.broadcasted_iota(jnp.int32, (span, tokens), 0) + where[1] * span
     chosen = (row == lax.broadcasted_iota(jnp.int32, (span, tokens), 1)).astype(jnp.float32).astype(jnp.bfloat16)
     turn = lambda value: lax.dot_general(
@@ -290,26 +328,26 @@
     )(where, *(pltpu.with_memory_space_constraint(x, pltpu.HBM) for x in arrays))
 
 
-def expert_rows(rows, gate_ref, up_ref, down_ref, scale):
+def expert_rows(rows, gate_ref, up_ref, down_ref):
     by_columns = (((1,), (1,)), ((), ()))
     gate = lax.dot_general(gate_ref[...], rows, by_columns, preferred_element_type=jnp.float32)
     upper = lax.dot_general(up_ref[...], rows, by_columns, preferred_element_type=jnp.float32)
-    hidden = (gate / (1.0 + jnp.exp(-gate)) * upper * scale).astype(jnp.bfloat16)
+    hidden = (gate / (1.0 + jnp.exp(-gate)) * upper).astype(jnp.bfloat16)
     by_rows = (((0,), (0,)), ((), ()))
     return lax.dot_general(hidden, down_ref[...], by_rows, preferred_element_type=jnp.float32).astype(jnp.bfloat16)
 
 
-def plain_kernel(where, rows_ref, gate_ref, up_ref, down_ref, scale_ref, out_ref):
-    out_ref[0] = expert_rows(rows_ref[0], gate_ref.at[0], up_ref.at[0], down_ref.at[0], scale_ref[0])
+def plain_kernel(where, rows_ref, gate_ref, up_ref, down_ref, out_ref):
+    out_ref[0] = expert_rows(rows_ref[0], gate_ref.at[0], up_ref.at[0], down_ref.at[0])
 
 
 def fused_kernel(count, where, *refs):
     blocks = STREAMS * count
     mine, other = refs[:blocks], refs[blocks : 2 * blocks]
-    combine_ref, scale_ref = refs[2 * blocks : 2 * blocks + 2]
-    weights = refs[2 * blocks + 2 : 2 * blocks + 5]
-    kept, away = refs[2 * blocks + 5 : 3 * blocks + 5], refs[3 * blocks + 5 : 4 * blocks + 5]
-    picked, buffers, sems = refs[4 * blocks + 5], refs[4 * blocks + 6 : 4 * blocks + 9], refs[4 * blocks + 9]
+    combine_ref = refs[2 * blocks]
+    weights = refs[2 * blocks + 1 : 2 * blocks + 4]
+    kept, away = refs[2 * blocks + 4 : 3 * blocks + 4], refs[3 * blocks + 4 : 4 * blocks + 4]
+    picked, buffers, sems = refs[4 * blocks + 4], refs[4 * blocks + 5 : 4 * blocks + 8], refs[4 * blocks + 8]
     here = picked.shape[0]
     depth, units, _ = buffers[0].shape
     part = mine[0].shape[1]
@@ -332,10 +370,11 @@
             copy.start()
 
     for c in range(count):
+        pick = (combine_ref[c].astype(jnp.float32) > 0).astype(jnp.float32).astype(jnp.bfloat16)
         for h in range(STREAMS):
             for place, block in ((columns(side, h), mine), (columns(1 - side, h), other)):
                 rows = lax.dot_general(
-                    combine_ref[c], block[h * count + c][...], by_rows, preferred_element_type=jnp.float32
+                    pick, block[h * count + c][...], by_rows, preferred_element_type=jnp.float32
                 ).astype(jnp.bfloat16)
                 for e in range(here):
                     picked[e, c * SLOTS : (c + 1) * SLOTS, place] = rows[e * SLOTS : (e + 1) * SLOTS]
@@ -344,7 +383,7 @@
         slot = lax.rem(expert, depth)
         for copy in copies(expert, slot):
             copy.wait()
-        picked[expert] = expert_rows(picked[expert], *(buffer.at[slot] for buffer in buffers), scale_ref[expert])
+        picked[expert] = expert_rows(picked[expert], *(buffer.at[slot] for buffer in buffers))
 
         @pl.when(expert + depth < here)
         def _():
@@ -362,13 +401,12 @@
                 out[h * count + c][...] = total.astype(jnp.bfloat16)
 
 
-def expert_specs(w_gate, rows):
+def expert_specs(w_gate):
     hidden, width = w_gate.shape[1:]
-    weight = pl.BlockSpec((1, hidden, width), lambda e, where: (e, 0, 0))
-    return [weight, weight, weight, pl.BlockSpec((1, 1, rows), lambda e, where: (e, 0, 0))]
-
-
-def experts_plain(where, picked, w_gate, w_up, w_down, scale):
+    return [pl.BlockSpec((1, hidden, width), lambda e, where: (e, 0, 0))] * 3
+
+
+def experts_plain(where, picked, w_gate, w_up, w_down):
     here, rows, width = picked.shape
     rows_spec = pl.BlockSpec((1, rows, width), lambda e, where: (e, 0, 0))
     return pl.pallas_call(
@@ -376,35 +414,35 @@
         grid_spec=pltpu.PrefetchScalarGridSpec(
             num_scalar_prefetch=1,
             grid=(here,),
-            in_specs=[rows_spec] + expert_specs(w_gate, rows),
+            in_specs=[rows_spec] + expert_specs(w_gate),
             out_specs=rows_spec,
         ),
         out_shape=jax.ShapeDtypeStruct(picked.shape, jnp.bfloat16),
         compiler_params=pltpu.CompilerParams(vmem_limit_bytes=VMEM_LIMIT),
         name="experts",
-    )(where, picked, w_gate, w_up, w_down, scale)
-
-
-def experts_fused(where, mine, other, combine, scale, w_gate, w_up, w_down):
+    )(where, picked, w_gate, w_up, w_down)
+
+
+def experts_fused(where, mine, other, combine, w_gate, w_up, w_down):
     count, (local, part) = len(mine[0]), mine[0][0].shape
-    here, _, rows = scale.shape
-    units = w_gate.shape[1]
+    here, units, _ = w_gate.shape
+    rows = count * SLOTS
     depth = min(DEPTH, here)
     blocks = STREAMS * count
     whole = pl.BlockSpec(memory_space=pltpu.VMEM)
     outs = pl.pallas_call(
         functools.partial(fused_kernel, count),
         in_specs=[pl.BlockSpec(memory_space=pltpu.SMEM)]
-        + [whole] * (2 * blocks + 2)
+        + [whole] * (2 * blocks + 1)
         + [pl.BlockSpec(memory_space=pltpu.HBM)] * 3,
         out_specs=[whole] * (2 * blocks),
         scratch_shapes=[pltpu.VMEM((here, rows, w_gate.shape[2]), jnp.bfloat16)]
         + [pltpu.VMEM((depth, units, w_gate.shape[2]), jnp.bfloat16)] * 3
         + [pltpu.SemaphoreType.DMA((depth, 3, PIECES))],
         out_shape=[pltpu.VMEM((local, part), jnp.bfloat16)] * (2 * blocks),
-        compiler_params=pltpu.CompilerParams(vmem_limit_bytes=38 * MIB),
+        compiler_params=pltpu.CompilerParams(vmem_limit_bytes=36 * MIB),
         name="experts",
-    )(where, *sum(mine, []), *sum(other, []), combine, scale,
+    )(where, *sum(mine, []), *sum(other, []), combine,
       *(pltpu.with_memory_space_constraint(w, pltpu.HBM) for w in (w_gate, w_up, w_down)))
     lists = [outs[i * count : (i + 1) * count] for i in range(2 * STREAMS)]
     return lists[:STREAMS], lists[STREAMS:]
@@ -447,43 +485,40 @@
     ]
     found, found_other, made = gather(packed, count, beside)
     q, (kv_up, out_proj, residual), (gain, info) = made
-    mine, other = jnp.stack(found), jnp.stack(found_other)
-    partial = attend(info, q, mine, other, kv_up, out_proj, count)
-    there = swap(partial)
-    mine, other, partial = lax.optimization_barrier((mine, other, partial))
-    middle, *normed = norm(where, residual, partial, there, gain)
-
-    facts_mine, facts_other = mine[:, :, base : base + 3 * TOP], other[:, :, base : base + 3 * TOP]
-    facts = jnp.concatenate(
-        [jnp.where(side == 0, facts_mine, facts_other), jnp.where(side == 0, facts_other, facts_mine)], axis=1
-    ).astype(jnp.float32)
-    ids, share = facts[:, :, :TOP], facts[:, :, TOP : 2 * TOP] + facts[:, :, 2 * TOP :]
-    own = (me * here + jnp.arange(here, dtype=jnp.int32)).astype(jnp.float32)
-    hit = ids[:, :, :, None] == own
-    hot = jnp.any(hit, axis=2)
-    share = jnp.sum(jnp.where(hit, share[:, :, :, None], 0.0), axis=2)
-    token = jnp.arange(local_rows, dtype=jnp.int32)
-    before = (token[:, None] > token[None, :]).astype(jnp.bfloat16)
-    rank = jnp.einsum("tu,cue->cte", before, hot.astype(jnp.bfloat16), preferred_element_type=jnp.float32)
-    rank = jnp.where(hot, rank, -1.0)
-    slot = jnp.arange(SLOTS, dtype=jnp.int32).astype(jnp.float32)
-    combine = rank[:, :, :, None] == slot
-    scale = jnp.sum(jnp.where(combine, share[:, :, :, None], 0.0), axis=1)
-    scale = scale.transpose(1, 0, 2).reshape(here, 1, count * SLOTS)
-    combine = combine.astype(jnp.bfloat16).reshape(count, local_rows, here * SLOTS)
-
-    facts = [(lambda *x: x, (combine, scale))]
-    streams = [gather(x, count, facts if h == 0 else ()) for h, x in enumerate(normed)]
-    combine, scale = streams[0][2][0]
+    partial = attend(info, q, found, found_other, kv_up, out_proj, count)
+    middle, *normed = norm(where, residual, partial, swap(partial), gain)
+
+    def place_rows(*blocks):
+        if few:
+            return route(where, blocks[:count], blocks[count:], here)
+        near, far = (jnp.stack(x)[:, :, base : base + 2 * TOP] for x in (blocks[:count], blocks[count:]))
+        facts = jnp.concatenate([jnp.where(side == 0, near, far), jnp.where(side == 0, far, near)], axis=1)
+        facts = facts.astype(jnp.float32)
+        own = (me * here + jnp.arange(here, dtype=jnp.int32)).astype(jnp.float32)
+        hit = facts[:, :, :TOP, None] == own
+        hot = jnp.any(hit, axis=2)
+        share = jnp.sum(jnp.where(hit, facts[:, :, TOP:, None], 0.0), axis=2)
+        token = jnp.arange(local_rows, dtype=jnp.int32)
+        before = (token[:, None] > token[None, :]).astype(jnp.bfloat16)
+        rank = jnp.einsum("tu,cue->cte", before, hot.astype(jnp.bfloat16), preferred_element_type=jnp.float32)
+        slot = jnp.arange(SLOTS, dtype=jnp.int32).astype(jnp.float32)
+        combine = jnp.where(rank[:, :, :, None] == slot, share[:, :, :, None], 0.0)
+        return combine.astype(jnp.bfloat16).reshape(count, local_rows, here * SLOTS)
+
+    streams = [
+        gather(x, count, [(place_rows, (*found, *found_other))] if h == 0 else ()) for h, x in enumerate(normed)
+    ]
+    combine = streams[0][2][0]
     near, far = [x[0] for x in streams], [x[1] for x in streams]
     if few:
-        kept, away = experts_fused(where, near, far, combine, scale, w_gate, w_up, w_down)
+        kept, away = experts_fused(where, near, far, combine, w_gate, w_up, w_down)
     else:
         near, far = (jnp.concatenate([jnp.stack(x) for x in xs], axis=2) for xs in (near, far))
         full = jnp.concatenate([jnp.where(side == 0, near, far), jnp.where(side == 0, far, near)], axis=2)
-        picked = jnp.einsum("cts,ctd->csd", combine, full, preferred_element_type=jnp.float32).astype(jnp.bfloat16)
+        pick = (combine > 0).astype(jnp.bfloat16)
+        picked = jnp.einsum("cts,ctd->csd", pick, full, preferred_element_type=jnp.float32).astype(jnp.bfloat16)
         picked = picked.reshape(count, here, SLOTS, width).transpose(1, 0, 2, 3).reshape(here, count * SLOTS, width)
-        result = experts_plain(where, picked, w_gate, w_up, w_down, scale)
+        result = experts_plain(where, picked, w_gate, w_up, w_down)
         result = result.reshape(here, count, SLOTS, width).transpose(1, 0, 2, 3).reshape(count, here * SLOTS, width)
         total = jnp.einsum("cts,csd->ctd", combine, result, preferred_element_type=jnp.float32).astype(jnp.bfloat16)
         left, right = jnp.split(total, 2, axis=2)

time: 186 us -> 134 us (0.72)
  waiting for transfers between devices: 72.3 us -> 54.7 us
  starting transfers between devices: 46 us -> 30.2 us
  local copies, waits for them, and re-layouts: 23.2 us -> 8.36 us
  other arithmetic: 6.47 us -> 1.73 us
  Pallas kernels: 35.9 us -> 38.6 us
    ppermute x40 -> x24, waiting for transfers between devices: 70.3 us -> 49.1 us  [step(): lax.ppermute(value, 'ctx', [(cycle[p], cycle[(p + ahead) % count]) for p...]
    ppermute x40 -> x24, starting transfers between devices: 40.1 us -> 25.6 us  [step(): lax.ppermute(value, 'ctx', [(cycle[p], cycle[(p + ahead) % count]) for p...]
    unnamed x29 -> x10, local copies, waits for them, and re-layouts: 14 us -> 3.38 us
    ppermute x41 -> x25, waiting for transfers between devices: 2.04 us -> 5.59 us  [swap(): return lax.ppermute(value, 'exp', SWAP)]
    pallas_call x0 -> x1, Pallas kernels: none -> 2.53 us  [route(): pl.pallas_call(functools.partial(route_kernel, count), in_specs=[pl.Block...]
    another operation x2 -> x0, local copies, waits for them, and re-layouts: 2.43 us -> none  [body(): mine, other = (jnp.stack(found), jnp.stack(found_other))]
    ppermute x41 -> x25, starting transfers between devices: 5.93 us -> 4.6 us  [swap(): return lax.ppermute(value, 'exp', SWAP)]
  transfers between devices with their start and end apart: 81 -> 49, of which waited for: 33 -> 23; matrix products, arithmetic and copies ran while one was open for 12% -> 4% of each run, Pallas kernels for 1% -> 3%
where the time goes in v8:
time: 134 us
  waiting for transfers between devices  54.7 us (41%)
  Pallas kernels  38.6 us (29%)
  starting transfers between devices  30.2 us (23%)
  local copies, waits for them, and re-layouts  8.36 us (6%)
  other arithmetic  1.73 us (1%)
    ppermute x24, waiting for transfers between devices, step(): lax.ppermute(value, 'ctx', [(cycle[p], cycle[(p + ahead) % count]) for p...  49.1 us
    pallas_call x1, Pallas kernels, experts_fused(): pl.pallas_call(functools.partial(fused_kernel, count), in_specs=[pl.Block...  25.7 us
    ppermute x24, starting transfers between devices, step(): lax.ppermute(value, 'ctx', [(cycle[p], cycle[(p + ahead) % count]) for p...  25.6 us
    pallas_call x1, Pallas kernels, attend(): pl.pallas_call(functools.partial(attend_kernel, count, blocks), grid_spec...  5.76 us
    ppermute x25, waiting for transfers between devices, swap(): return lax.ppermute(value, 'exp', SWAP)  5.59 us
    ppermute x25, starting transfers between devices, swap(): return lax.ppermute(value, 'exp', SWAP)  4.6 us
    unnamed x10, local copies, waits for them, and re-layouts  3.38 us
  transfers between devices with their start and end apart: 49, of which 23 were waited for; matrix products, arithmetic and copies ran while one was open for 4% of the time, Pallas kernels for 3%

profile of v8, /device:TPU:0, one launch (start us, length us, event | category | flops | bytes accessed | tf_op | source)
XLA Modules:
  0.0 133.9 jit_solution(13557206681075380848)
XLA Ops:
  0.1 1.7 %pack.1.refs_0_ = bf16[64,640]{1,0:T(8,128)(2,1)S(1)} custom-call(s32[2]{0:T(128)S(1)} %pad_add_fusion.where, bf16[576,128]{1,0:T(8,128)(2,1)} %bitcast.15, s32[6,128]{1,0:T(8,128)} %bitcast.16, f32[6,128]{1,0:T(8,128)} %bitcast.17), custom_call_target="tpu_custom_call" | custom-call | tf_op jit(solution)/shard_map/pack/pallas_call | solution.py:319
  2.3 2.6 %collective-permute-start = (bf16[64,640]{1,0:T(8,128)(2,1)S(1)}, bf16[64,640]{1,0:T(8,128)(2,1)}, u32[]{:S(2)}, u32[]{:S(2)}) collective-permute-start(bf16[64,640]{1,0:T(8,128)(2,1)S(1)} %pack.1.refs_0_), channel_id=1, source_target_pairs={{0,2},{2,6},{6,10},{10,14},{14,12},{12,8},{8,4},{4,0},{1,3},{3,7},... | collective-permute-start | bytes 245768 | tf_op jit(solution)/shard_map/ppermute | solution.py:41
  5.0 1.1 copy.15
  6.9 1.2 collective-permute-done.refs_1_
  8.1 1.4 %collective-permute-done.7.refs_7_ = bf16[64,640]{1,0:T(8,128)(2,1)} collective-permute-done((bf16[64,640]{1,0:T(8,128)(2,1)S(1)}, bf16[64,640]{1,0:T(8,128)(2,1)}, u32[]{:S(2)}, u32[]{:S(2)}) %collective-permute-start.7) | collective-permute-done | bytes 81952 | tf_op jit(solution)/shard_map/ppermute | solution.py:41
  10.0 1.7 %collective-permute-start.2 = (bf16[64,640]{1,0:T(8,128)(2,1)}, bf16[64,640]{1,0:T(8,128)(2,1)}, u32[]{:S(2)}, u32[]{:S(2)}) collective-permute-start(bf16[64,640]{1,0:T(8,128)(2,1)} %collective-permute-done.refs_1_), channel_id=1, source_target_pairs={{0,2},{2,6},{6,10},{10,14},{14,12},{12,8},{8,4},{4,0},{1,3},{3,7},... | collective-permute-start | bytes 245768 | tf_op jit(solution)/shard_map/ppermute | solution.py:41
  11.7 2.0 %stage.1 = (bf16[512,1024]{1,0:T(8,128)(2,1)S(1)}, bf16[512,2048]{1,0:T(8,128)(2,1)S(1)}, bf16[128,2048]{1,0:T(8,128)(2,1)S(1)}) custom-call(bf16[512,1024]{1,0:T(8,128)(2,1)} %refs_0_, bf16[512,2048]{1,0:T(8,128)(2,1)} %refs_1_, bf16[128,2048]{1,0:T(8,128)(2,1)} %refs_2_), custom_call_target="tpu_custom_call" | custom-call | tf_op jit(solution)/shard_map/stage/pallas_call | solution.py:254
  13.8 0.8 copy-done
  15.3 1.7 %collective-permute-start.4 = (bf16[64,640]{1,0:T(8,128)(2,1)}, bf16[64,640]{1,0:T(8,128)(2,1)}, u32[]{:S(2)}, u32[]{:S(2)}) collective-permute-start(bf16[64,640]{1,0:T(8,128)(2,1)} %collective-permute-done.2.refs_2_), channel_id=1, source_target_pairs={{0,2},{2,6},{6,10},{10,14},{14,12},{12,8},{8,4},{4,0},{1,3},{3,7},... | collective-permute-start | bytes 245768 | tf_op jit(solution)/shard_map/ppermute | solution.py:41
  16.9 0.7 dynamic-slice_bitcast_fusion
  17.6 0.7 reshape.7.gain_ref
  18.3 0.7 concatenate.16.info
  19.1 1.1 collective-permute-done.4.refs_3_
  20.2 0.8 slice.18
  21.0 1.7 %collective-permute-start.6 = (bf16[32,640]{1,0:T(8,128)(2,1)S(1)}, bf16[32,640]{1,0:T(8,128)(2,1)S(1)}, u32[]{:S(2)}, u32[]{:S(2)}) collective-permute-start(bf16[32,640]{1,0:T(8,128)(2,1)S(1)} %slice.18), channel_id=1, source_target_pairs={{0,2},{2,6},{6,10},{10,14},{14,12},{12,8},{8,4},{4,0},{1,3},{3,7},... | collective-permute-start | bytes 122888 | tf_op jit(solution)/shard_map/ppermute | solution.py:41
  22.7 0.8 slice.19
  25.0 3.0 %collective-permute-done.12 = bf16[32,640]{1,0:T(8,128)(2,1)S(1)} collective-permute-done((bf16[32,640]{1,0:T(8,128)(2,1)S(1)}, bf16[32,640]{1,0:T(8,128)(2,1)S(1)}, u32[]{:S(2)}, u32[]{:S(2)}) %collective-permute-start.12) | collective-permute-done | bytes 40992 | tf_op jit(solution)/shard_map/ppermute | solution.py:41
  28.0 1.3 collective-permute-done.14.refs_12_
  29.2 0.9 copy-done.3
  30.1 5.8 %attend.1.here_ref = bf16[128,2048]{1,0:T(8,128)(2,1)S(1)} custom-call(s32[42]{0:T(128)S(1)} %concatenate.16.info, bf16[4,128,192]{2,1,0:T(8,128)(2,1)S(1)} %bitcast.11, bf16[64,640]{1,0:T(8,128)(2,1)S(1)} %pack.1.refs_0_, bf16[64,640]{1,0:T(8,128)(2,1)} %collective-permute-done.refs_1_, bf16[64,640]{1,0:T(8,128)(2,1)} %collective-permute-done.2.refs_2_, ...), custom_call_target="tpu_custom_call" | custom-call | tf_op jit(solution)/shard_map/attend/pallas_call | solution.py:181
  36.1 1.8 %collective-permute-done.16.there_ref = bf16[128,2048]{1,0:T(8,128)(2,1)S(1)} collective-permute-done((bf16[128,2048]{1,0:T(8,128)(2,1)S(1)}, bf16[128,2048]{1,0:T(8,128)(2,1)S(1)}, u32[]{:S(2)}, u32[]{:S(2)}) %collective-permute-start.16) | collective-permute-done | bytes 524320 | tf_op jit(solution)/shard_map/ppermute | solution.py:45
  37.9 1.0 copy-done.1
  38.9 1.0 norm.1
  40.1 1.6 %collective-permute-start.17 = (bf16[128,1024]{1,0:T(8,128)(2,1)S(1)}, bf16[128,1024]{1,0:T(8,128)(2,1)S(1)}, u32[]{:S(2)}, u32[]{:S(2)}) collective-permute-start(bf16[128,1024]{1,0:T(8,128)(2,1)S(1)} %get-tuple-element.109.refs_0_), channel_id=1, source_target_pairs={{0,2},{2,6},{6,10},{10,14},{14,12},{12,8},{8,4},{4,0},{1,3},{3,7},... | collective-permute-start | bytes 786440 | tf_op jit(solution)/shard_map/ppermute | solution.py:41
  42.1 2.5 %route.1.refs_16_ = bf16[8,128,128]{2,1,0:T(8,128)(2,1)S(1)} custom-call(s32[2]{0:T(128)S(1)} %pad_add_fusion.where, bf16[64,640]{1,0:T(8,128)(2,1)S(1)} %pack.1.refs_0_, bf16[64,640]{1,0:T(8,128)(2,1)} %collective-permute-done.refs_1_, bf16[64,640]{1,0:T(8,128)(2,1)} %collective-permute-done.2.refs_2_, bf16[64,640]{1,0:T(8,128)(2,1)} %collective-permute-done.4.refs_3_, ...), custom_call_target="tpu_custom_call" | custom-call | tf_op jit(solution)/shard_map/route/pallas_call | solution.py:226
  44.7 4.0 %collective-permute-done.17.refs_1_ = bf16[128,1024]{1,0:T(8,128)(2,1)S(1)} collective-permute-done((bf16[128,1024]{1,0:T(8,128)(2,1)S(1)}, bf16[128,1024]{1,0:T(8,128)(2,1)S(1)}, u32[]{:S(2)}, u32[]{:S(2)}) %collective-permute-start.17) | collective-permute-done | bytes 262176 | tf_op jit(solution)/shard_map/ppermute | solution.py:41
  48.7 1.6 %collective-permute-start.19 = (bf16[128,1024]{1,0:T(8,128)(2,1)S(1)}, bf16[128,1024]{1,0:T(8,128)(2,1)S(1)}, u32[]{:S(2)}, u32[]{:S(2)}) collective-permute-start(bf16[128,1024]{1,0:T(8,128)(2,1)S(1)} %collective-permute-done.17.refs_1_), channel_id=1, source_target_pairs={{0,2},{2,6},{6,10},{10,14},{14,12},{12,8},{8,4},{4,0},{1,3},{3,7},... | collective-permute-start | bytes 786440 | tf_op jit(solution)/shard_map/ppermute | solution.py:41
  50.9 6.5 %collective-permute-done.19.refs_2_ = bf16[128,1024]{1,0:T(8,128)(2,1)S(1)} collective-permute-done((bf16[128,1024]{1,0:T(8,128)(2,1)S(1)}, bf16[128,1024]{1,0:T(8,128)(2,1)S(1)}, u32[]{:S(2)}, u32[]{:S(2)}) %collective-permute-start.19) | collective-permute-done | bytes 262176 | tf_op jit(solution)/shard_map/ppermute | solution.py:41
  57.4 1.6 %collective-permute-start.21 = (bf16[128,1024]{1,0:T(8,128)(2,1)S(1)}, bf16[128,1024]{1,0:T(8,128)(2,1)S(1)}, u32[]{:S(2)}, u32[]{:S(2)}) collective-permute-start(bf16[128,1024]{1,0:T(8,128)(2,1)S(1)} %collective-permute-done.19.refs_2_), channel_id=1, source_target_pairs={{0,2},{2,6},{6,10},{10,14},{14,12},{12,8},{8,4},{4,0},{1,3},{3,7},... | collective-permute-start | bytes 786440 | tf_op jit(solution)/shard_map/ppermute | solution.py:41
  59.7 6.5 %collective-permute-done.21.refs_3_ = bf16[128,1024]{1,0:T(8,128)(2,1)S(1)} collective-permute-done((bf16[128,1024]{1,0:T(8,128)(2,1)S(1)}, bf16[128,1024]{1,0:T(8,128)(2,1)S(1)}, u32[]{:S(2)}, u32[]{:S(2)}) %collective-permute-start.21) | collective-permute-done | bytes 262176 | tf_op jit(solution)/shard_map/ppermute | solution.py:41
  66.1 1.6 %collective-permute-start.23 = (bf16[64,1024]{1,0:T(8,128)(2,1)S(1)}, bf16[64,1024]{1,0:T(8,128)(2,1)S(1)}, u32[]{:S(2)}, u32[]{:S(2)}) collective-permute-start(bf16[64,1024]{1,0:T(8,128)(2,1)S(1)} %slice.20), channel_id=1, source_target_pairs={{0,2},{2,6},{6,10},{10,14},{14,12},{12,8},{8,4},{4,0},{1,3},{3,7},... | collective-permute-start | bytes 393224 | tf_op jit(solution)/shard_map/ppermute | solution.py:41
  69.0 2.3 %collective-permute-done.23 = bf16[64,1024]{1,0:T(8,128)(2,1)S(1)} collective-permute-done((bf16[64,1024]{1,0:T(8,128)(2,1)S(1)}, bf16[64,1024]{1,0:T(8,128)(2,1)S(1)}, u32[]{:S(2)}, u32[]{:S(2)}) %collective-permute-start.23) | collective-permute-done | bytes 131104 | tf_op jit(solution)/shard_map/ppermute | solution.py:41
  71.3 1.7 %collective-permute-done.29 = bf16[64,1024]{1,0:T(8,128)(2,1)S(1)} collective-permute-done((bf16[64,1024]{1,0:T(8,128)(2,1)S(1)}, bf16[64,1024]{1,0:T(8,128)(2,1)S(1)}, u32[]{:S(2)}, u32[]{:S(2)}) %collective-permute-start.29) | collective-permute-done | bytes 131104 | tf_op jit(solution)/shard_map/ppermute | solution.py:41
  73.1 1.5 %collective-permute-done.31.refs_12_ = bf16[128,1024]{1,0:T(8,128)(2,1)S(1)} collective-permute-done((bf16[128,1024]{1,0:T(8,128)(2,1)S(1)}, bf16[128,1024]{1,0:T(8,128)(2,1)S(1)}, u32[]{:S(2)}, u32[]{:S(2)}) %collective-permute-start.31) | collective-permute-done | bytes 262176 | tf_op jit(solution)/shard_map/ppermute | solution.py:45
  74.6 25.7 %experts.1 = (bf16[128,1024]{1,0:T(8,128)(2,1)S(1)}, bf16[128,1024]{1,0:T(8,128)(2,1)S(1)}, bf16[128,1024]{1,0:T(8,128)(2,1)S(1)}, bf16[128,1024]{1,0:T(8,128)(2...) custom-call(s32[2]{0:T(128)S(1)} %pad_add_fusion.where, ...), custom_call_target="tpu_custom_call" | custom-call | tf_op jit(solution)/shard_map/experts/pallas_call | solution.py:433
  100.9 1.0 collective-permute-done.37
  102.0 1.6 %collective-permute-start.38 = (bf16[64,1024]{1,0:T(8,128)(2,1)S(1)}, bf16[64,1024]{1,0:T(8,128)(2,1)S(1)}, u32[]{:S(2)}, u32[]{:S(2)}) collective-permute-start(bf16[64,1024]{1,0:T(8,128)(2,1)S(1)} %get-tuple-element.155), channel_id=1, source_target_pairs={{0,2},{2,6},{6,10},{10,14},{14,12},{12,8},{8,4},{4,0},{1,3},{3,7},... | collective-permute-start | bytes 393224 | tf_op jit(solution)/shard_map/ppermute | solution.py:41
  104.6 3.0 %collective-permute-done.38 = bf16[64,1024]{1,0:T(8,128)(2,1)S(1)} collective-permute-done((bf16[64,1024]{1,0:T(8,128)(2,1)S(1)}, bf16[64,1024]{1,0:T(8,128)(2,1)S(1)}, u32[]{:S(2)}, u32[]{:S(2)}) %collective-permute-start.38) | collective-permute-done | bytes 131104 | tf_op jit(solution)/shard_map/ppermute | solution.py:41
  107.7 1.6 %collective-permute-start.39 = (bf16[128,1024]{1,0:T(8,128)(2,1)S(1)}, bf16[128,1024]{1,0:T(8,128)(2,1)S(1)}, u32[]{:S(2)}, u32[]{:S(2)}) collective-permute-start(bf16[128,1024]{1,0:T(8,128)(2,1)S(1)} %add_convert_fusion.6), channel_id=1, source_target_pairs={{0,2},{2,6},{6,10},{10,14},{14,12},{12,8},{8,4},{4,0},{1,3},{3,7},... | collective-permute-start | bytes 786440 | tf_op jit(solution)/shard_map/ppermute | solution.py:41
  110.6 4.6 %collective-permute-done.39 = bf16[128,1024]{1,0:T(8,128)(2,1)S(1)} collective-permute-done((bf16[128,1024]{1,0:T(8,128)(2,1)S(1)}, bf16[128,1024]{1,0:T(8,128)(2,1)S(1)}, u32[]{:S(2)}, u32[]{:S(2)}) %collective-permute-start.39) | collective-permute-done | bytes 262176 | tf_op jit(solution)/shard_map/ppermute | solution.py:41
  115.4 1.6 %collective-permute-start.40 = (bf16[128,1024]{1,0:T(8,128)(2,1)S(1)}, bf16[128,1024]{1,0:T(8,128)(2,1)S(1)}, u32[]{:S(2)}, u32[]{:S(2)}) collective-permute-start(bf16[128,1024]{1,0:T(8,128)(2,1)S(1)} %add_convert_fusion.5), channel_id=1, source_target_pairs={{0,2},{2,6},{6,10},{10,14},{14,12},{12,8},{8,4},{4,0},{1,3},{3,7},... | collective-permute-start | bytes 786440 | tf_op jit(solution)/shard_map/ppermute | solution.py:41
  117.0 1.2 collective-permute-done.46
  118.8 3.2 %collective-permute-done.40 = bf16[128,1024]{1,0:T(8,128)(2,1)S(1)} collective-permute-done((bf16[128,1024]{1,0:T(8,128)(2,1)S(1)}, bf16[128,1024]{1,0:T(8,128)(2,1)S(1)}, u32[]{:S(2)}, u32[]{:S(2)}) %collective-permute-start.40) | collective-permute-done | bytes 262176 | tf_op jit(solution)/shard_map/ppermute | solution.py:41
  122.2 1.6 %collective-permute-start.41 = (bf16[128,1024]{1,0:T(8,128)(2,1)S(1)}, bf16[128,1024]{1,0:T(8,128)(2,1)S(1)}, u32[]{:S(2)}, u32[]{:S(2)}) collective-permute-start(bf16[128,1024]{1,0:T(8,128)(2,1)S(1)} %add_convert_fusion.4), channel_id=1, source_target_pairs={{0,2},{2,6},{6,10},{10,14},{14,12},{12,8},{8,4},{4,0},{1,3},{3,7},... | collective-permute-start | bytes 786440 | tf_op jit(solution)/shard_map/ppermute | solution.py:41
  123.8 2.3 %collective-permute-done.47 = bf16[128,1024]{1,0:T(8,128)(2,1)S(1)} collective-permute-done((bf16[128,1024]{1,0:T(8,128)(2,1)S(1)}, bf16[128,1024]{1,0:T(8,128)(2,1)S(1)}, u32[]{:S(2)}, u32[]{:S(2)}) %collective-permute-start.47) | collective-permute-done | bytes 262176 | tf_op jit(solution)/shard_map/ppermute | solution.py:41
  126.7 1.9 %collective-permute-done.41 = bf16[128,1024]{1,0:T(8,128)(2,1)S(1)} collective-permute-done((bf16[128,1024]{1,0:T(8,128)(2,1)S(1)}, bf16[128,1024]{1,0:T(8,128)(2,1)S(1)}, u32[]{:S(2)}, u32[]{:S(2)}) %collective-permute-start.41) | collective-permute-done | bytes 262176 | tf_op jit(solution)/shard_map/ppermute | solution.py:41
  128.6 4.4 %collective-permute-done.48 = bf16[128,1024]{1,0:T(8,128)(2,1)S(1)} collective-permute-done((bf16[128,1024]{1,0:T(8,128)(2,1)S(1)}, bf16[128,1024]{1,0:T(8,128)(2,1)S(1)}, u32[]{:S(2)}, u32[]{:S(2)}) %collective-permute-start.48) | collective-permute-done | bytes 262176 | tf_op jit(solution)/shard_map/ppermute | solution.py:41
  133.0 0.9 add_convert_fusion
  (87 shorter events, 12.4 us)
Async XLA Ops:
  1.8 4.5 %collective-permute-start.1 = (bf16[64,640]{1,0:T(8,128)(2,1)S(1)}, bf16[64,640]{1,0:T(8,128)(2,1)S(1)}, u32[]{:S(2)}, u32[]{:S(2)}) collective-permute-start(bf16[64,640]{1,0:T(8,128)(2,1)S(1)} %pack.1.refs_0_), channel_id=1, source_target_pairs={{0,1},{1,0},{2,3},{3,2},{4,5},{5,4},{6,7},{7,6},{8,9},{9,8},{10,11... | collective-permute-start | bytes 245768 | tf_op jit(solution)/shard_map/ppermute | solution.py:45
  2.3 5.8 %collective-permute-start = (bf16[64,640]{1,0:T(8,128)(2,1)S(1)}, bf16[64,640]{1,0:T(8,128)(2,1)}, u32[]{:S(2)}, u32[]{:S(2)}) collective-permute-start(bf16[64,640]{1,0:T(8,128)(2,1)S(1)} %pack.1.refs_0_), channel_id=1, source_target_pairs={{0,2},{2,6},{6,10},{10,14},{14,12},{12,8},{8,4},{4,0},{1,3},{3,7},... | collective-permute-start | bytes 245768 | tf_op jit(solution)/shard_map/ppermute | solution.py:41
  4.9 4.6 %collective-permute-start.7 = (bf16[64,640]{1,0:T(8,128)(2,1)S(1)}, bf16[64,640]{1,0:T(8,128)(2,1)}, u32[]{:S(2)}, u32[]{:S(2)}) collective-permute-start(bf16[64,640]{1,0:T(8,128)(2,1)S(1)} %pack.1.refs_0_), channel_id=1, source_target_pairs={{0,4},{2,0},{6,2},{10,6},{14,10},{12,14},{8,12},{4,8},{1,5},{3,1},... | collective-permute-start | bytes 245768 | tf_op jit(solution)/shard_map/ppermute | solution.py:41
  9.5 5.1 %collective-permute-start.9 = (bf16[64,640]{1,0:T(8,128)(2,1)}, bf16[64,640]{1,0:T(8,128)(2,1)}, u32[]{:S(2)}, u32[]{:S(2)}) collective-permute-start(bf16[64,640]{1,0:T(8,128)(2,1)} %collective-permute-done.7.refs_7_), channel_id=1, source_target_pairs={{0,1},{1,0},{2,3},{3,2},{4,5},{5,4},{6,7},{7,6},{8,9},{9,8},{10,11... | collective-permute-start | bytes 245768 | tf_op jit(solution)/shard_map/ppermute | solution.py:45
  9.5 5.2 %collective-permute-start.8 = (bf16[64,640]{1,0:T(8,128)(2,1)}, bf16[64,640]{1,0:T(8,128)(2,1)}, u32[]{:S(2)}, u32[]{:S(2)}) collective-permute-start(bf16[64,640]{1,0:T(8,128)(2,1)} %collective-permute-done.7.refs_7_), channel_id=1, source_target_pairs={{0,4},{2,0},{6,2},{10,6},{14,10},{12,14},{8,12},{4,8},{1,5},{3,1},... | collective-permute-start | bytes 245768 | tf_op jit(solution)/shard_map/ppermute | solution.py:41
  9.8 5.2 %collective-permute-start.3 = (bf16[64,640]{1,0:T(8,128)(2,1)}, bf16[64,640]{1,0:T(8,128)(2,1)}, u32[]{:S(2)}, u32[]{:S(2)}) collective-permute-start(bf16[64,640]{1,0:T(8,128)(2,1)} %collective-permute-done.refs_1_), channel_id=1, source_target_pairs={{0,1},{1,0},{2,3},{3,2},{4,5},{5,4},{6,7},{7,6},{8,9},{9,8},{10,11... | collective-permute-start | bytes 245768 | tf_op jit(solution)/shard_map/ppermute | solution.py:45
  10.0 5.0 %collective-permute-start.2 = (bf16[64,640]{1,0:T(8,128)(2,1)}, bf16[64,640]{1,0:T(8,128)(2,1)}, u32[]{:S(2)}, u32[]{:S(2)}) collective-permute-start(bf16[64,640]{1,0:T(8,128)(2,1)} %collective-permute-done.refs_1_), channel_id=1, source_target_pairs={{0,2},{2,6},{6,10},{10,14},{14,12},{12,8},{8,4},{4,0},{1,3},{3,7},... | collective-permute-start | bytes 245768 | tf_op jit(solution)/shard_map/ppermute | solution.py:41
  14.7 8.0 %collective-permute-start.11 = (bf16[64,640]{1,0:T(8,128)(2,1)}, bf16[64,640]{1,0:T(8,128)(2,1)}, u32[]{:S(2)}, u32[]{:S(2)}) collective-permute-start(bf16[64,640]{1,0:T(8,128)(2,1)} %collective-permute-done.8.refs_6_), channel_id=1, source_target_pairs={{0,1},{1,0},{2,3},{3,2},{4,5},{5,4},{6,7},{7,6},{8,9},{9,8},{10,11... | collective-permute-start | bytes 245768 | tf_op jit(solution)/shard_map/ppermute | solution.py:45
  14.7 8.0 %collective-permute-start.10 = (bf16[64,640]{1,0:T(8,128)(2,1)}, bf16[64,640]{1,0:T(8,128)(2,1)}, u32[]{:S(2)}, u32[]{:S(2)}) collective-permute-start(bf16[64,640]{1,0:T(8,128)(2,1)} %collective-permute-done.8.refs_6_), channel_id=1, source_target_pairs={{0,4},{2,0},{6,2},{10,6},{14,10},{12,14},{8,12},{4,8},{1,5},{3,1},... | collective-permute-start | bytes 245768 | tf_op jit(solution)/shard_map/ppermute | solution.py:41
  15.0 4.0 %collective-permute-start.5 = (bf16[64,640]{1,0:T(8,128)(2,1)}, bf16[64,640]{1,0:T(8,128)(2,1)}, u32[]{:S(2)}, u32[]{:S(2)}) collective-permute-start(bf16[64,640]{1,0:T(8,128)(2,1)} %collective-permute-done.2.refs_2_), channel_id=1, source_target_pairs={{0,1},{1,0},{2,3},{3,2},{4,5},{5,4},{6,7},{7,6},{8,9},{9,8},{10,11... | collective-permute-start | bytes 245768 | tf_op jit(solution)/shard_map/ppermute | solution.py:45
  15.3 4.9 %collective-permute-start.4 = (bf16[64,640]{1,0:T(8,128)(2,1)}, bf16[64,640]{1,0:T(8,128)(2,1)}, u32[]{:S(2)}, u32[]{:S(2)}) collective-permute-start(bf16[64,640]{1,0:T(8,128)(2,1)} %collective-permute-done.2.refs_2_), channel_id=1, source_target_pairs={{0,2},{2,6},{6,10},{10,14},{14,12},{12,8},{8,4},{4,0},{1,3},{3,7},... | collective-permute-start | bytes 245768 | tf_op jit(solution)/shard_map/ppermute | solution.py:41
  21.0 4.0 %collective-permute-start.6 = (bf16[32,640]{1,0:T(8,128)(2,1)S(1)}, bf16[32,640]{1,0:T(8,128)(2,1)S(1)}, u32[]{:S(2)}, u32[]{:S(2)}) collective-permute-start(bf16[32,640]{1,0:T(8,128)(2,1)S(1)} %slice.18), channel_id=1, source_target_pairs={{0,2},{2,6},{6,10},{10,14},{14,12},{12,8},{8,4},{4,0},{1,3},{3,7},... | collective-permute-start | bytes 122888 | tf_op jit(solution)/shard_map/ppermute | solution.py:41
  23.4 4.5 %collective-permute-start.15 = (bf16[64,640]{1,0:T(8,128)(2,1)}, bf16[64,640]{1,0:T(8,128)(2,1)S(1)}, u32[]{:S(2)}, u32[]{:S(2)}) collective-permute-start(bf16[64,640]{1,0:T(8,128)(2,1)} %collective-permute-done.10.refs_5_), channel_id=1, source_target_pairs={{0,1},{1,0},{2,3},{3,2},{4,5},{5,4},{6,7},{7,6},{8,9},{9,8},{10,11... | collective-permute-start | bytes 245768 | tf_op jit(solution)/shard_map/ppermute | solution.py:45
  23.4 4.5 %collective-permute-start.13 = (bf16[64,640]{1,0:T(8,128)(2,1)}, bf16[64,640]{1,0:T(8,128)(2,1)S(1)}, u32[]{:S(2)}, u32[]{:S(2)}) collective-permute-start(bf16[64,640]{1,0:T(8,128)(2,1)} %collective-permute-done.4.refs_3_), channel_id=1, source_target_pairs={{0,1},{1,0},{2,3},{3,2},{4,5},{5,4},{6,7},{7,6},{8,9},{9,8},{10,11... | collective-permute-start | bytes 245768 | tf_op jit(solution)/shard_map/ppermute | solution.py:45
  24.0 4.0 %collective-permute-start.12 = (bf16[32,640]{1,0:T(8,128)(2,1)S(1)}, bf16[32,640]{1,0:T(8,128)(2,1)S(1)}, u32[]{:S(2)}, u32[]{:S(2)}) collective-permute-start(bf16[32,640]{1,0:T(8,128)(2,1)S(1)} %slice.19), channel_id=1, source_target_pairs={{0,4},{2,0},{6,2},{10,6},{14,10},{12,14},{8,12},{4,8},{1,5},{3,1},... | collective-permute-start | bytes 122888 | tf_op jit(solution)/shard_map/ppermute | solution.py:41
  35.9 2.0 %collective-permute-start.16 = (bf16[128,2048]{1,0:T(8,128)(2,1)S(1)}, bf16[128,2048]{1,0:T(8,128)(2,1)S(1)}, u32[]{:S(2)}, u32[]{:S(2)}) collective-permute-start(bf16[128,2048]{1,0:T(8,128)(2,1)S(1)} %attend.1.here_ref), channel_id=1, source_target_pairs={{0,1},{1,0},{2,3},{3,2},{4,5},{5,4},{6,7},{7,6},{8,9},{9,8},{10,11... | collective-permute-start | bytes 1572872 | tf_op jit(solution)/shard_map/ppermute | solution.py:45
  39.9 4.8 %collective-permute-start.18 = (bf16[128,1024]{1,0:T(8,128)(2,1)S(1)}, bf16[128,1024]{1,0:T(8,128)(2,1)S(1)}, u32[]{:S(2)}, u32[]{:S(2)}) collective-permute-start(bf16[128,1024]{1,0:T(8,128)(2,1)S(1)} %get-tuple-element.109.refs_0_), channel_id=1, source_target_pairs={{0,1},{1,0},{2,3},{3,2},{4,5},{5,4},{6,7},{7,6},{8,9},{9,8},{10,11... | collective-permute-start | bytes 786440 | tf_op jit(solution)/shard_map/ppermute | solution.py:45
  40.1 8.6 %collective-permute-start.17 = (bf16[128,1024]{1,0:T(8,128)(2,1)S(1)}, bf16[128,1024]{1,0:T(8,128)(2,1)S(1)}, u32[]{:S(2)}, u32[]{:S(2)}) collective-permute-start(bf16[128,1024]{1,0:T(8,128)(2,1)S(1)} %get-tuple-element.109.refs_0_), channel_id=1, source_target_pairs={{0,2},{2,6},{6,10},{10,14},{14,12},{12,8},{8,4},{4,0},{1,3},{3,7},... | collective-permute-start | bytes 786440 | tf_op jit(solution)/shard_map/ppermute | solution.py:41
  41.7 8.6 %collective-permute-start.24 = (bf16[128,1024]{1,0:T(8,128)(2,1)S(1)}, bf16[128,1024]{1,0:T(8,128)(2,1)S(1)}, u32[]{:S(2)}, u32[]{:S(2)}) collective-permute-start(bf16[128,1024]{1,0:T(8,128)(2,1)S(1)} %get-tuple-element.109.refs_0_), channel_id=1, source_target_pairs={{0,4},{2,0},{6,2},{10,6},{14,10},{12,14},{8,12},{4,8},{1,5},{3,1},... | collective-permute-start | bytes 786440 | tf_op jit(solution)/shard_map/ppermute | solution.py:41
  48.7 2.3 %collective-permute-start.20 = (bf16[128,1024]{1,0:T(8,128)(2,1)S(1)}, bf16[128,1024]{1,0:T(8,128)(2,1)S(1)}, u32[]{:S(2)}, u32[]{:S(2)}) collective-permute-start(bf16[128,1024]{1,0:T(8,128)(2,1)S(1)} %collective-permute-done.17.refs_1_), channel_id=1, source_target_pairs={{0,1},{1,0},{2,3},{3,2},{4,5},{5,4},{6,7},{7,6},{8,9},{9,8},{10,11... | collective-permute-start | bytes 786440 | tf_op jit(solution)/shard_map/ppermute | solution.py:45
  48.7 8.7 %collective-permute-start.19 = (bf16[128,1024]{1,0:T(8,128)(2,1)S(1)}, bf16[128,1024]{1,0:T(8,128)(2,1)S(1)}, u32[]{:S(2)}, u32[]{:S(2)}) collective-permute-start(bf16[128,1024]{1,0:T(8,128)(2,1)S(1)} %collective-permute-done.17.refs_1_), channel_id=1, source_target_pairs={{0,2},{2,6},{6,10},{10,14},{14,12},{12,8},{8,4},{4,0},{1,3},{3,7},... | collective-permute-start | bytes 786440 | tf_op jit(solution)/shard_map/ppermute | solution.py:41
  50.3 8.7 %collective-permute-start.26 = (bf16[128,1024]{1,0:T(8,128)(2,1)S(1)}, bf16[128,1024]{1,0:T(8,128)(2,1)S(1)}, u32[]{:S(2)}, u32[]{:S(2)}) collective-permute-start(bf16[128,1024]{1,0:T(8,128)(2,1)S(1)} %collective-permute-done.24.refs_7_), channel_id=1, source_target_pairs={{0,1},{1,0},{2,3},{3,2},{4,5},{5,4},{6,7},{7,6},{8,9},{9,8},{10,11... | collective-permute-start | bytes 786440 | tf_op jit(solution)/shard_map/ppermute | solution.py:45
  50.5 8.5 %collective-permute-start.25 = (bf16[128,1024]{1,0:T(8,128)(2,1)S(1)}, bf16[128,1024]{1,0:T(8,128)(2,1)S(1)}, u32[]{:S(2)}, u32[]{:S(2)}) collective-permute-start(bf16[128,1024]{1,0:T(8,128)(2,1)S(1)} %collective-permute-done.24.refs_7_), channel_id=1, source_target_pairs={{0,4},{2,0},{6,2},{10,6},{14,10},{12,14},{8,12},{4,8},{1,5},{3,1},... | collective-permute-start | bytes 786440 | tf_op jit(solution)/shard_map/ppermute | solution.py:41
  57.4 2.3 %collective-permute-start.22 = (bf16[128,1024]{1,0:T(8,128)(2,1)S(1)}, bf16[128,1024]{1,0:T(8,128)(2,1)S(1)}, u32[]{:S(2)}, u32[]{:S(2)}) collective-permute-start(bf16[128,1024]{1,0:T(8,128)(2,1)S(1)} %collective-permute-done.19.refs_2_), channel_id=1, source_target_pairs={{0,1},{1,0},{2,3},{3,2},{4,5},{5,4},{6,7},{7,6},{8,9},{9,8},{10,11... | collective-permute-start | bytes 786440 | tf_op jit(solution)/shard_map/ppermute | solution.py:45
  57.4 8.7 %collective-permute-start.21 = (bf16[128,1024]{1,0:T(8,128)(2,1)S(1)}, bf16[128,1024]{1,0:T(8,128)(2,1)S(1)}, u32[]{:S(2)}, u32[]{:S(2)}) collective-permute-start(bf16[128,1024]{1,0:T(8,128)(2,1)S(1)} %collective-permute-done.19.refs_2_), channel_id=1, source_target_pairs={{0,2},{2,6},{6,10},{10,14},{14,12},{12,8},{8,4},{4,0},{1,3},{3,7},... | collective-permute-start | bytes 786440 | tf_op jit(solution)/shard_map/ppermute | solution.py:41
  59.0 8.8 %collective-permute-start.28 = (bf16[128,1024]{1,0:T(8,128)(2,1)S(1)}, bf16[128,1024]{1,0:T(8,128)(2,1)S(1)}, u32[]{:S(2)}, u32[]{:S(2)}) collective-permute-start(bf16[128,1024]{1,0:T(8,128)(2,1)S(1)} %collective-permute-done.25.refs_6_), channel_id=1, source_target_pairs={{0,1},{1,0},{2,3},{3,2},{4,5},{5,4},{6,7},{7,6},{8,9},{9,8},{10,11... | collective-permute-start | bytes 786440 | tf_op jit(solution)/shard_map/ppermute | solution.py:45
  59.2 8.6 %collective-permute-start.27 = (bf16[128,1024]{1,0:T(8,128)(2,1)S(1)}, bf16[128,1024]{1,0:T(8,128)(2,1)S(1)}, u32[]{:S(2)}, u32[]{:S(2)}) collective-permute-start(bf16[128,1024]{1,0:T(8,128)(2,1)S(1)} %collective-permute-done.25.refs_6_), channel_id=1, source_target_pairs={{0,4},{2,0},{6,2},{10,6},{14,10},{12,14},{8,12},{4,8},{1,5},{3,1},... | collective-permute-start | bytes 786440 | tf_op jit(solution)/shard_map/ppermute | solution.py:41
  66.1 5.2 %collective-permute-start.23 = (bf16[64,1024]{1,0:T(8,128)(2,1)S(1)}, bf16[64,1024]{1,0:T(8,128)(2,1)S(1)}, u32[]{:S(2)}, u32[]{:S(2)}) collective-permute-start(bf16[64,1024]{1,0:T(8,128)(2,1)S(1)} %slice.20), channel_id=1, source_target_pairs={{0,2},{2,6},{6,10},{10,14},{14,12},{12,8},{8,4},{4,0},{1,3},{3,7},... | collective-permute-start | bytes 393224 | tf_op jit(solution)/shard_map/ppermute | solution.py:41
  67.8 5.2 %collective-permute-start.29 = (bf16[64,1024]{1,0:T(8,128)(2,1)S(1)}, bf16[64,1024]{1,0:T(8,128)(2,1)S(1)}, u32[]{:S(2)}, u32[]{:S(2)}) collective-permute-start(bf16[64,1024]{1,0:T(8,128)(2,1)S(1)} %slice.21), channel_id=1, source_target_pairs={{0,4},{2,0},{6,2},{10,6},{14,10},{12,14},{8,12},{4,8},{1,5},{3,1},... | collective-permute-start | bytes 393224 | tf_op jit(solution)/shard_map/ppermute | solution.py:41
  68.5 4.6 %collective-permute-start.32 = (bf16[128,1024]{1,0:T(8,128)(2,1)S(1)}, bf16[128,1024]{1,0:T(8,128)(2,1)S(1)}, u32[]{:S(2)}, u32[]{:S(2)}) collective-permute-start(bf16[128,1024]{1,0:T(8,128)(2,1)S(1)} %collective-permute-done.27.refs_5_), channel_id=1, source_target_pairs={{0,1},{1,0},{2,3},{3,2},{4,5},{5,4},{6,7},{7,6},{8,9},{9,8},{10,11... | collective-permute-start | bytes 786440 | tf_op jit(solution)/shard_map/ppermute | solution.py:45
  68.5 4.6 %collective-permute-start.30 = (bf16[128,1024]{1,0:T(8,128)(2,1)S(1)}, bf16[128,1024]{1,0:T(8,128)(2,1)S(1)}, u32[]{:S(2)}, u32[]{:S(2)}) collective-permute-start(bf16[128,1024]{1,0:T(8,128)(2,1)S(1)} %collective-permute-done.21.refs_3_), channel_id=1, source_target_pairs={{0,1},{1,0},{2,3},{3,2},{4,5},{5,4},{6,7},{7,6},{8,9},{9,8},{10,11... | collective-permute-start | bytes 786440 | tf_op jit(solution)/shard_map/ppermute | solution.py:45
  73.0 1.6 %collective-permute-start.31 = (bf16[128,1024]{1,0:T(8,128)(2,1)S(1)}, bf16[128,1024]{1,0:T(8,128)(2,1)S(1)}, u32[]{:S(2)}, u32[]{:S(2)}) collective-permute-start(bf16[128,1024]{1,0:T(8,128)(2,1)S(1)} %constant_dynamic-update-slice_fusion.2.refs_4_), channel_id=1, source_target_pairs={{0,1},{1,0},{2,3},{3,2},{4,5},{5,4},{6,7},{7,6},{8,9},{9,8},{10,11... | collective-permute-start | bytes 786440 | tf_op jit(solution)/shard_map/ppermute | solution.py:45
  100.3 1.6 %collective-permute-start.37 = (bf16[128,1024]{1,0:T(8,128)(2,1)S(1)}, bf16[128,1024]{1,0:T(8,128)(2,1)S(1)}, u32[]{:S(2)}, u32[]{:S(2)}) collective-permute-start(bf16[128,1024]{1,0:T(8,128)(2,1)S(1)} %get-tuple-element.148), channel_id=1, source_target_pairs={{0,1},{1,0},{2,3},{3,2},{4,5},{5,4},{6,7},{7,6},{8,9},{9,8},{10,11... | collective-permute-start | bytes 786440 | tf_op jit(solution)/shard_map/ppermute | solution.py:45
  100.5 4.1 %collective-permute-start.36 = (bf16[128,1024]{1,0:T(8,128)(2,1)S(1)}, bf16[128,1024]{1,0:T(8,128)(2,1)S(1)}, u32[]{:S(2)}, u32[]{:S(2)}) collective-permute-start(bf16[128,1024]{1,0:T(8,128)(2,1)S(1)} %get-tuple-element.146), channel_id=1, source_target_pairs={{0,1},{1,0},{2,3},{3,2},{4,5},{5,4},{6,7},{7,6},{8,9},{9,8},{10,11... | collective-permute-start | bytes 786440 | tf_op jit(solution)/shard_map/ppermute | solution.py:45
  102.0 5.6 %collective-permute-start.38 = (bf16[64,1024]{1,0:T(8,128)(2,1)S(1)}, bf16[64,1024]{1,0:T(8,128)(2,1)S(1)}, u32[]{:S(2)}, u32[]{:S(2)}) collective-permute-start(bf16[64,1024]{1,0:T(8,128)(2,1)S(1)} %get-tuple-element.155), channel_id=1, source_target_pairs={{0,2},{2,6},{6,10},{10,14},{14,12},{12,8},{8,4},{4,0},{1,3},{3,7},... | collective-permute-start | bytes 393224 | tf_op jit(solution)/shard_map/ppermute | solution.py:41
  103.6 5.7 %collective-permute-start.44 = (bf16[128,1024]{1,0:T(8,128)(2,1)S(1)}, bf16[128,1024]{1,0:T(8,128)(2,1)S(1)}, u32[]{:S(2)}, u32[]{:S(2)}) collective-permute-start(bf16[128,1024]{1,0:T(8,128)(2,1)S(1)} %get-tuple-element.154), channel_id=1, source_target_pairs={{0,1},{1,0},{2,3},{3,2},{4,5},{5,4},{6,7},{7,6},{8,9},{9,8},{10,11... | collective-permute-start | bytes 786440 | tf_op jit(solution)/shard_map/ppermute | solution.py:45
  103.6 6.5 %collective-permute-start.35 = (bf16[128,1024]{1,0:T(8,128)(2,1)S(1)}, bf16[128,1024]{1,0:T(8,128)(2,1)S(1)}, u32[]{:S(2)}, u32[]{:S(2)}) collective-permute-start(bf16[128,1024]{1,0:T(8,128)(2,1)S(1)} %get-tuple-element.144), channel_id=1, source_target_pairs={{0,1},{1,0},{2,3},{3,2},{4,5},{5,4},{6,7},{7,6},{8,9},{9,8},{10,11... | collective-permute-start | bytes 786440 | tf_op jit(solution)/shard_map/ppermute | solution.py:45
  104.1 5.4 %collective-permute-start.45 = (bf16[64,1024]{1,0:T(8,128)(2,1)S(1)}, bf16[64,1024]{1,0:T(8,128)(2,1)S(1)}, u32[]{:S(2)}, u32[]{:S(2)}) collective-permute-start(bf16[64,1024]{1,0:T(8,128)(2,1)S(1)} %get-tuple-element.156), channel_id=1, source_target_pairs={{0,4},{2,0},{6,2},{10,6},{14,10},{12,14},{8,12},{4,8},{1,5},{3,1},... | collective-permute-start | bytes 393224 | tf_op jit(solution)/shard_map/ppermute | solution.py:41
  107.7 7.6 %collective-permute-start.39 = (bf16[128,1024]{1,0:T(8,128)(2,1)S(1)}, bf16[128,1024]{1,0:T(8,128)(2,1)S(1)}, u32[]{:S(2)}, u32[]{:S(2)}) collective-permute-start(bf16[128,1024]{1,0:T(8,128)(2,1)S(1)} %add_convert_fusion.6), channel_id=1, source_target_pairs={{0,2},{2,6},{6,10},{10,14},{14,12},{12,8},{8,4},{4,0},{1,3},{3,7},... | collective-permute-start | bytes 786440 | tf_op jit(solution)/shard_map/ppermute | solution.py:41
  109.3 7.7 %collective-permute-start.43 = (bf16[128,1024]{1,0:T(8,128)(2,1)S(1)}, bf16[128,1024]{1,0:T(8,128)(2,1)S(1)}, u32[]{:S(2)}, u32[]{:S(2)}) collective-permute-start(bf16[128,1024]{1,0:T(8,128)(2,1)S(1)} %get-tuple-element.152), channel_id=1, source_target_pairs={{0,1},{1,0},{2,3},{3,2},{4,5},{5,4},{6,7},{7,6},{8,9},{9,8},{10,11... | collective-permute-start | bytes 786440 | tf_op jit(solution)/shard_map/ppermute | solution.py:45
  109.6 8.6 %collective-permute-start.46 = (bf16[128,1024]{1,0:T(8,128)(2,1)S(1)}, bf16[128,1024]{1,0:T(8,128)(2,1)S(1)}, u32[]{:S(2)}, u32[]{:S(2)}) collective-permute-start(bf16[128,1024]{1,0:T(8,128)(2,1)S(1)} %add_convert_fusion.3), channel_id=1, source_target_pairs={{0,4},{2,0},{6,2},{10,6},{14,10},{12,14},{8,12},{4,8},{1,5},{3,1},... | collective-permute-start | bytes 786440 | tf_op jit(solution)/shard_map/ppermute | solution.py:41
  110.1 8.7 %collective-permute-start.34 = (bf16[128,1024]{1,0:T(8,128)(2,1)S(1)}, bf16[128,1024]{1,0:T(8,128)(2,1)S(1)}, u32[]{:S(2)}, u32[]{:S(2)}) collective-permute-start(bf16[128,1024]{1,0:T(8,128)(2,1)S(1)} %get-tuple-element.142), channel_id=1, source_target_pairs={{0,1},{1,0},{2,3},{3,2},{4,5},{5,4},{6,7},{7,6},{8,9},{9,8},{10,11... | collective-permute-start | bytes 786440 | tf_op jit(solution)/shard_map/ppermute | solution.py:45
  110.1 13.6 %collective-permute-start.42 = (bf16[128,1024]{1,0:T(8,128)(2,1)S(1)}, bf16[128,1024]{1,0:T(8,128)(2,1)S(1)}, u32[]{:S(2)}, u32[]{:S(2)}) collective-permute-start(bf16[128,1024]{1,0:T(8,128)(2,1)S(1)} %get-tuple-element.150), channel_id=1, source_target_pairs={{0,1},{1,0},{2,3},{3,2},{4,5},{5,4},{6,7},{7,6},{8,9},{9,8},{10,11... | collective-permute-start | bytes 786440 | tf_op jit(solution)/shard_map/ppermute | solution.py:45
  115.4 6.7 %collective-permute-start.40 = (bf16[128,1024]{1,0:T(8,128)(2,1)S(1)}, bf16[128,1024]{1,0:T(8,128)(2,1)S(1)}, u32[]{:S(2)}, u32[]{:S(2)}) collective-permute-start(bf16[128,1024]{1,0:T(8,128)(2,1)S(1)} %add_convert_fusion.5), channel_id=1, source_target_pairs={{0,2},{2,6},{6,10},{10,14},{14,12},{12,8},{8,4},{4,0},{1,3},{3,7},... | collective-permute-start | bytes 786440 | tf_op jit(solution)/shard_map/ppermute | solution.py:41
  118.3 7.7 %collective-permute-start.47 = (bf16[128,1024]{1,0:T(8,128)(2,1)S(1)}, bf16[128,1024]{1,0:T(8,128)(2,1)S(1)}, u32[]{:S(2)}, u32[]{:S(2)}) collective-permute-start(bf16[128,1024]{1,0:T(8,128)(2,1)S(1)} %add_convert_fusion.2), channel_id=1, source_target_pairs={{0,4},{2,0},{6,2},{10,6},{14,10},{12,14},{8,12},{4,8},{1,5},{3,1},... | collective-permute-start | bytes 786440 | tf_op jit(solution)/shard_map/ppermute | solution.py:41
  118.8 7.9 %collective-permute-start.33 = (bf16[128,1024]{1,0:T(8,128)(2,1)S(1)}, bf16[128,1024]{1,0:T(8,128)(2,1)S(1)}, u32[]{:S(2)}, u32[]{:S(2)}) collective-permute-start(bf16[128,1024]{1,0:T(8,128)(2,1)S(1)} %get-tuple-element.140), channel_id=1, source_target_pairs={{0,1},{1,0},{2,3},{3,2},{4,5},{5,4},{6,7},{7,6},{8,9},{9,8},{10,11... | collective-permute-start | bytes 786440 | tf_op jit(solution)/shard_map/ppermute | solution.py:45
  122.2 6.4 %collective-permute-start.41 = (bf16[128,1024]{1,0:T(8,128)(2,1)S(1)}, bf16[128,1024]{1,0:T(8,128)(2,1)S(1)}, u32[]{:S(2)}, u32[]{:S(2)}) collective-permute-start(bf16[128,1024]{1,0:T(8,128)(2,1)S(1)} %add_convert_fusion.4), channel_id=1, source_target_pairs={{0,2},{2,6},{6,10},{10,14},{14,12},{12,8},{8,4},{4,0},{1,3},{3,7},... | collective-permute-start | bytes 786440 | tf_op jit(solution)/shard_map/ppermute | solution.py:41
  126.2 6.8 %collective-permute-start.48 = (bf16[128,1024]{1,0:T(8,128)(2,1)S(1)}, bf16[128,1024]{1,0:T(8,128)(2,1)S(1)}, u32[]{:S(2)}, u32[]{:S(2)}) collective-permute-start(bf16[128,1024]{1,0:T(8,128)(2,1)S(1)} %add_convert_fusion.1), channel_id=1, source_target_pairs={{0,4},{2,0},{6,2},{10,6},{14,10},{12,14},{8,12},{4,8},{1,5},{3,1},... | collective-permute-start | bytes 786440 | tf_op jit(solution)/shard_map/ppermute | solution.py:41
  (5 other events, 4.7 us)

commit v9 on v8

v9 whole, which is shorter than its diff:
```python
import functools
import math

import jax
import jax.numpy as jnp
import numpy as np
from jax import lax
from jax.experimental import pallas as pl
from jax.experimental.pallas import tpu as pltpu
from jax.sharding import PartitionSpec as P

NOPE = 128
ROPE = 64
VHEAD = 128
LAT = 512
EXPERTS = 64
TOP = 6
SLOTS = 16
WIDE = 640
MIB = 1024 * 1024
VMEM_LIMIT = 50 * MIB
DEPTH = 3
PIECES = 2
SWAP = [(0, 1), (1, 0)]
FEW = 8


def cycle_of(count):
    fast = 2 ** (int(math.log2(count)) // 2)
    slow = count // fast
    cycle = [0]
    for i in range(slow):
        columns = range(1, fast)
        cycle += [i * fast + j for j in (columns if i % 2 == 0 else reversed(columns))]
    return cycle + [i * fast for i in reversed(range(1, slow))]


def swap(value):
    return lax.ppermute(value, "exp", SWAP)


def turn(value, count, cross=False):
    cycle = cycle_of(count)
    pairs = []
    for p in range(count):
        for core, ahead in ((0, 1), (1, -1)):
            pairs.append((cycle[p] * 2 + core, cycle[(p + ahead) % count] * 2 + (core ^ int(cross))))
    return lax.ppermute(value, ("ctx", "exp"), pairs)


def summed(pieces):
    total = pieces[0].astype(jnp.float32)
    for piece in pieces[1:]:
        total = total + piece.astype(jnp.float32)
    return total


def sources_of(me, side, count):
    if count > FEW:
        return jnp.arange(count, dtype=jnp.int32)
    cycle = cycle_of(count)
    middle = count // 2
    table = np.zeros((2 * count, count), np.int32)
    for p in range(count):
        for core, sign in ((0, 1), (1, -1)):
            ways = [sign * d for d in range(middle + 1)] + [-sign * d for d in range(1, middle)]
            table[cycle[p] * 2 + core] = [cycle[(p - way) % count] for way in ways]
    return lax.dynamic_index_in_dim(jnp.asarray(table), me * 2 + side, keepdims=False)


def gather(block, count, beside=()):
    if count > FEW:
        return list(lax.all_gather(block, "ctx")), [run(*arguments) for run, arguments in beside]
    middle = count // 2
    found, other, made = [block], [()], []
    for d in range(1, middle + 1):
        arrived, extra = turn(found[-1], count), ()
        if len(beside) >= d:
            run, arguments = beside[d - 1]
            extra = run(*lax.optimization_barrier((found[-1], arguments))[1])
        arrived, other[-1], extra = lax.optimization_barrier((arrived, other[-1], extra))
        made.append(extra)
        found.append(arrived)
        if d < middle:
            other.append(swap(arrived))
    return found + other[1:], made[: len(beside)]


def reduce(parts, opposite, own, side, count):
    middle = count // 2
    given = {d: swap(x) for d, x in [(middle, opposite[1])] + [(d, parts[d]) for d in range(middle - 1, 0, -1)]}
    first = turn(summed([opposite[0], given[middle]]).astype(jnp.bfloat16), count).astype(jnp.float32)
    nothing = jnp.zeros_like(first)
    running = jnp.concatenate([jnp.where(side == 0, first, nothing), jnp.where(side == 0, nothing, first)], axis=0)
    for d in range(middle - 1, 0, -1):
        total = summed([parts[middle + d], given[d]]) + running
        if d > 1:
            running = turn(total.astype(jnp.bfloat16), count).astype(jnp.float32)
    left, right = jnp.split(total.astype(jnp.bfloat16), 2, axis=1)
    near = turn(jnp.where(side == 0, left, right), count)
    far = turn(jnp.where(side == 0, right, left), count, cross=True)
    return summed([own[0], swap(own[1]), near, far])


def attend_kernel(count, blocks, info, q_ref, *refs):
    up_ref, proj_ref, out_ref, m_ref, l_ref, acc_ref = refs[-6:]
    latents = refs[:-6]
    chunk = pl.program_id(0)
    sources = lambda c: info[2 + c]
    order = lambda j: info[2 + count + j]
    segs = info.shape[0] - 2 - 3 * count
    heads, rows, _ = q_ref.shape
    span = rows // 2

    @pl.when(chunk == 0)
    def _():
        m_ref[...] = jnp.full_like(m_ref, -1e30)
        l_ref[...] = jnp.zeros_like(l_ref)
        acc_ref[...] = jnp.zeros_like(acc_ref)

    row = lax.broadcasted_iota(jnp.int32, (rows, 1), 0)
    first = order(2 * info[0]) * span
    second = order(2 * info[0] + 1) * span
    qpos = jnp.where(row < span, first + row, second + row - span)
    low = jnp.zeros((rows, 1), jnp.int32)
    start = jnp.int32(0)
    for m in range(segs):
        low = jnp.where(qpos >= start, start, low)
        start = start + info[2 + 3 * count + m]
    keys = blocks * rows
    lane = lax.broadcasted_iota(jnp.int32, (1, keys), 1)
    which = lane // span
    kpos = lane % span
    for j in range(blocks):
        source = sources(chunk * blocks + j)
        for i in range(2):
            kpos = jnp.where(which == 2 * j + i, order(2 * source + i) * span + lane % span, kpos)
    visible = (kpos >= low) & (kpos <= qpos)

    lat = jnp.concatenate([ref[...].reshape(-1, WIDE) for ref in latents], axis=0)
    keyval = jnp.dot(lat[:, :LAT], up_ref[...], preferred_element_type=jnp.float32).astype(jnp.bfloat16)
    rope = lat[:, LAT : LAT + ROPE]
    scale = 1.0 / math.sqrt(NOPE + ROPE)
    for h in range(heads):
        base = h * (NOPE + VHEAD)
        key = jnp.concatenate([keyval[:, base : base + NOPE], rope], axis=1)
        scores = lax.dot_general(q_ref[h], key, (((1,), (1,)), ((), ())), preferred_element_type=jnp.float32)
        scores = jnp.where(visible, scores * scale, -1e30)
        best = m_ref[h]
        fresh = jnp.maximum(best, jnp.max(scores, axis=1, keepdims=True))
        weights = jnp.where(visible, jnp.exp(scores - fresh), 0.0)
        shrink = jnp.exp(best - fresh)
        m_ref[h] = fresh
        l_ref[h] = l_ref[h] * shrink + jnp.sum(weights, axis=1, keepdims=True)
        mixed = jnp.dot(
            weights.astype(jnp.bfloat16), keyval[:, base + NOPE : base + NOPE + VHEAD], preferred_element_type=jnp.float32
        )
        acc_ref[h] = acc_ref[h] * shrink + mixed

    @pl.when(chunk == pl.num_programs(0) - 1)
    def _():
        attended = [(acc_ref[h] / l_ref[h]).astype(jnp.bfloat16) for h in range(heads)]
        out = jnp.dot(jnp.concatenate(attended, axis=1), proj_ref[...], preferred_element_type=jnp.float32)
        out_ref[...] = out.astype(jnp.bfloat16)


def attend(info, q, found, kv_up, out_proj, count):
    heads, rows, depth = q.shape
    blocks = math.gcd(count, 8)
    whole = pl.BlockSpec(memory_space=pltpu.VMEM)
    if blocks == count:
        latents, lat_spec = found, whole
    else:
        latents, lat_spec = [jnp.stack(found)], pl.BlockSpec((blocks, rows, WIDE), lambda i, *_: (i, 0, 0))
    return pl.pallas_call(
        functools.partial(attend_kernel, count, blocks),
        grid_spec=pltpu.PrefetchScalarGridSpec(
            num_scalar_prefetch=1,
            grid=(count // blocks,),
            in_specs=[whole] + [lat_spec] * len(latents) + [whole, whole],
            out_specs=whole,
            scratch_shapes=[
                pltpu.VMEM((heads, rows, 1), jnp.float32),
                pltpu.VMEM((heads, rows, 1), jnp.float32),
                pltpu.VMEM((heads, rows, VHEAD), jnp.float32),
            ],
        ),
        out_shape=pltpu.VMEM((rows, out_proj.shape[1]), jnp.bfloat16),
        compiler_params=pltpu.CompilerParams(vmem_limit_bytes=28 * MIB),
        name="attend",
    )(info, q, *latents, kv_up, out_proj)


def route_kernel(count, where, *refs):
    blocks, out_ref = refs[:count], refs[count]
    _, rows, width = out_ref.shape
    here = width // SLOTS
    lane = lax.broadcasted_iota(jnp.int32, (rows, width), 1)
    own = (where[0] * here + lane // SLOTS).astype(jnp.float32)
    slot = (lane % SLOTS).astype(jnp.float32)
    first = lax.broadcasted_iota(jnp.int32, (rows, rows), 0)
    before = (first > lax.broadcasted_iota(jnp.int32, (rows, rows), 1)).astype(jnp.float32).astype(jnp.bfloat16)
    for c in range(count):
        facts = blocks[c][:, LAT:].astype(jnp.float32)
        hot, share = jnp.zeros((rows, width), jnp.float32), jnp.zeros((rows, width), jnp.float32)
        for k in range(TOP):
            hit = facts[:, ROPE + k : ROPE + k + 1] == own
            hot = jnp.where(hit, 1.0, hot)
            share = jnp.where(hit, facts[:, ROPE + TOP + k : ROPE + TOP + k + 1], share)
        rank = jnp.dot(before, hot.astype(jnp.bfloat16), preferred_element_type=jnp.float32)
        out_ref[c] = jnp.where(rank == slot, share, 0.0).astype(jnp.bfloat16)


def route(where, found, here):
    count, (rows, _) = len(found), found[0].shape
    whole = pl.BlockSpec(memory_space=pltpu.VMEM)
    return pl.pallas_call(
        functools.partial(route_kernel, count),
        in_specs=[pl.BlockSpec(memory_space=pltpu.SMEM)] + [whole] * count,
        out_specs=whole,
        out_shape=pltpu.VMEM((count, rows, here * SLOTS), jnp.bfloat16),
        compiler_params=pltpu.CompilerParams(vmem_limit_bytes=8 * MIB),
        name="route",
    )(where, *found)


def stage_kernel(picks, *refs):
    here = len(picks)
    sems = refs[2 * here]
    copies = []
    for i, pick in enumerate(picks):
        source = refs[i] if pick is None else refs[i].at[pick]
        piece = source.shape[0] // PIECES
        for p in range(PIECES):
            rows = pl.ds(p * piece, piece)
            copies.append(pltpu.make_async_copy(source.at[rows], refs[here + i].at[rows], sems.at[i, p]))
    for copy in copies:
        copy.start()
    for copy in copies:
        copy.wait()


def stage(arrays, picks):
    shapes = [x.shape if pick is None else x.shape[1:] for x, pick in zip(arrays, picks)]
    return pl.pallas_call(
        functools.partial(stage_kernel, picks),
        in_specs=[pl.BlockSpec(memory_space=pltpu.HBM)] * len(arrays),
        out_specs=[pl.BlockSpec(memory_space=pltpu.VMEM)] * len(arrays),
        scratch_shapes=[pltpu.SemaphoreType.DMA((len(arrays), PIECES))],
        out_shape=[pltpu.VMEM(shape, x.dtype) for shape, x in zip(shapes, arrays)],
        compiler_params=pltpu.CompilerParams(vmem_limit_bytes=2 * MIB),
        name="stage",
    )(*(pltpu.with_memory_space_constraint(x, pltpu.HBM) for x in arrays))


def norm_kernel(where, residual_ref, here_ref, there_ref, gain_ref, middle_ref, normed_ref):
    half = middle_ref.shape[1]
    total = here_ref[...].astype(jnp.float32) + there_ref[...].astype(jnp.float32)
    middle = (residual_ref[...].astype(jnp.float32) + total).astype(jnp.bfloat16)
    wide = middle.astype(jnp.float32)
    inverse = lax.rsqrt(jnp.mean(wide * wide, axis=1, keepdims=True) + 1e-06)
    normed_ref[...] = (wide * inverse * gain_ref[...].astype(jnp.float32)).astype(jnp.bfloat16)
    middle_ref[...] = jnp.where(where[1] == 0, wide[:, :half], wide[:, half:]).astype(jnp.bfloat16)


def norm(where, residual, here, there, gain):
    rows, width = residual.shape
    whole = pl.BlockSpec(memory_space=pltpu.VMEM)
    return pl.pallas_call(
        norm_kernel,
        in_specs=[pl.BlockSpec(memory_space=pltpu.SMEM)] + [whole] * 4,
        out_specs=[whole] * 2,
        out_shape=[pltpu.VMEM(shape, jnp.bfloat16) for shape in ((rows, width // 2), (rows, width))],
        compiler_params=pltpu.CompilerParams(vmem_limit_bytes=12 * MIB),
        name="norm",
    )(where, residual, here, there, gain)


def pack_kernel(*refs):
    copies = [pltpu.make_async_copy(refs[i], refs[4 + i], refs[8].at[i]) for i in range(3)]
    for copy in copies:
        copy.start()
    for copy in copies:
        copy.wait()
    out_ref, (latent_ref, ids_ref, weights_ref, rows) = refs[3], refs[4:8]
    tokens = out_ref.shape[0]
    rows[...] = jnp.zeros_like(rows)
    rows[0:TOP] = ids_ref[...].astype(jnp.float32)
    rows[TOP : 2 * TOP] = weights_ref[...]
    row = lax.broadcasted_iota(jnp.int32, (tokens, tokens), 0)
    same = (row == lax.broadcasted_iota(jnp.int32, (tokens, tokens), 1)).astype(jnp.float32).astype(jnp.bfloat16)
    every = jnp.concatenate([latent_ref[...], rows[...].astype(jnp.bfloat16)], axis=0)
    turned = lax.dot_general(same, every, (((1,), (1,)), ((), ())), preferred_element_type=jnp.float32)
    out_ref[...] = turned.astype(jnp.bfloat16)


def pack(latent, expert_ids, route_weights):
    local_rows, base = latent.shape
    arrays = (latent.T, expert_ids.T, route_weights.T)
    return pl.pallas_call(
        pack_kernel,
        in_specs=[pl.BlockSpec(memory_space=pltpu.HBM)] * 3,
        out_specs=pl.BlockSpec(memory_space=pltpu.VMEM),
        scratch_shapes=[pltpu.VMEM(x.shape, x.dtype) for x in arrays]
        + [pltpu.VMEM((WIDE - base, local_rows), jnp.float32), pltpu.SemaphoreType.DMA((3,))],
        out_shape=pltpu.VMEM((local_rows, WIDE), jnp.bfloat16),
        compiler_params=pltpu.CompilerParams(vmem_limit_bytes=4 * MIB),
        name="pack",
    )(*(pltpu.with_memory_space_constraint(x, pltpu.HBM) for x in arrays))


def expert_rows(rows, gate_ref, up_ref, down_ref):
    by_columns = (((1,), (1,)), ((), ()))
    gate = lax.dot_general(gate_ref[...], rows, by_columns, preferred_element_type=jnp.float32)
    upper = lax.dot_general(up_ref[...], rows, by_columns, preferred_element_type=jnp.float32)
    hidden = (gate / (1.0 + jnp.exp(-gate)) * upper).astype(jnp.bfloat16)
    by_rows = (((0,), (0,)), ((), ()))
    return lax.dot_general(hidden, down_ref[...], by_rows, preferred_element_type=jnp.float32).astype(jnp.bfloat16)


def plain_kernel(where, rows_ref, gate_ref, up_ref, down_ref, out_ref):
    out_ref[0] = expert_rows(rows_ref[0], gate_ref.at[0], up_ref.at[0], down_ref.at[0])


def fused_kernel(count, where, *refs):
    blocks, combine_ref, weights = refs[:count], refs[count], refs[count + 1 : count + 4]
    outs, at = refs[count + 4 : 2 * count + 6], 2 * count + 6
    picked, buffers, sems = refs[at], refs[at + 1 : at + 4], refs[at + 4]
    here = picked.shape[0]
    depth, units, width = buffers[0].shape
    side = where[1]
    piece = units // PIECES
    middle = count // 2
    by_rows = (((0,), (0,)), ((), ()))

    def copies(expert, slot):
        for w in range(3):
            for i in range(PIECES):
                rows = pl.ds(i * piece, piece)
                yield pltpu.make_async_copy(weights[w].at[expert, rows], buffers[w].at[slot, rows], sems.at[slot, w, i])

    for e in range(depth):
        for copy in copies(e, e):
            copy.start()

    for c in range(count):
        pick = (combine_ref[c].astype(jnp.float32) > 0).astype(jnp.float32).astype(jnp.bfloat16)
        rows = lax.dot_general(pick, blocks[c][...], by_rows, preferred_element_type=jnp.float32).astype(jnp.bfloat16)
        for e in range(here):
            picked[e, c * SLOTS : (c + 1) * SLOTS] = rows[e * SLOTS : (e + 1) * SLOTS]

    def work(expert, _):
        slot = lax.rem(expert, depth)
        for copy in copies(expert, slot):
            copy.wait()
        picked[expert] = expert_rows(picked[expert], *(buffer.at[slot] for buffer in buffers))

        @pl.when(expert + depth < here)
        def _():
            for copy in copies(expert + depth, slot):
                copy.start()

        return 0

    lax.fori_loop(0, here, work, 0)

    def total(c):
        rows = jnp.concatenate([picked[e, c * SLOTS : (c + 1) * SLOTS] for e in range(here)], axis=0)
        return jnp.dot(combine_ref[c], rows, preferred_element_type=jnp.float32).astype(jnp.bfloat16)

    result = total(middle)
    half = result.shape[0] // 2
    upper, lower = result[:half], result[half:]
    outs[0][...] = jnp.where(side == 0, upper, lower)
    outs[1][...] = jnp.where(side == 0, lower, upper)
    result = total(0)
    left, right = result[:, : width // 2], result[:, width // 2 :]
    outs[2][...] = jnp.where(side == 0, left, right)
    outs[3][...] = jnp.where(side == 0, right, left)
    rest = [c for c in range(count) if c not in (0, middle)]
    for i, c in enumerate(rest):
        outs[4 + i][...] = total(c)


def expert_specs(w_gate):
    hidden, width = w_gate.shape[1:]
    return [pl.BlockSpec((1, hidden, width), lambda e, where: (e, 0, 0))] * 3


def experts_plain(where, picked, w_gate, w_up, w_down):
    here, rows, width = picked.shape
    rows_spec = pl.BlockSpec((1, rows, width), lambda e, where: (e, 0, 0))
    return pl.pallas_call(
        plain_kernel,
        grid_spec=pltpu.PrefetchScalarGridSpec(
            num_scalar_prefetch=1,
            grid=(here,),
            in_specs=[rows_spec] + expert_specs(w_gate),
            out_specs=rows_spec,
        ),
        out_shape=jax.ShapeDtypeStruct(picked.shape, jnp.bfloat16),
        compiler_params=pltpu.CompilerParams(vmem_limit_bytes=VMEM_LIMIT),
        name="experts",
    )(where, picked, w_gate, w_up, w_down)


def experts_fused(where, found, combine, w_gate, w_up, w_down):
    count, (local, width) = len(found), found[0].shape
    here, units, _ = w_gate.shape
    rows = count * SLOTS
    depth = min(DEPTH, here)
    middle = count // 2
    whole = pl.BlockSpec(memory_space=pltpu.VMEM)
    shapes = [(local // 2, width)] * 2 + [(local, width // 2)] * 2 + [(local, width)] * (count - 2)
    outs = pl.pallas_call(
        functools.partial(fused_kernel, count),
        in_specs=[pl.BlockSpec(memory_space=pltpu.SMEM)]
        + [whole] * (count + 1)
        + [pl.BlockSpec(memory_space=pltpu.HBM)] * 3,
        out_specs=[whole] * len(shapes),
        scratch_shapes=[pltpu.VMEM((here, rows, width), jnp.bfloat16)]
        + [pltpu.VMEM((depth, units, width), jnp.bfloat16)] * 3
        + [pltpu.SemaphoreType.DMA((depth, 3, PIECES))],
        out_shape=[pltpu.VMEM(shape, jnp.bfloat16) for shape in shapes],
        compiler_params=pltpu.CompilerParams(vmem_limit_bytes=36 * MIB),
        name="experts",
    )(where, *found, combine, *(pltpu.with_memory_space_constraint(w, pltpu.HBM) for w in (w_gate, w_up, w_down)))
    rest = [c for c in range(count) if c not in (0, middle)]
    return dict(zip(rest, outs[4:])), outs[:2], outs[2:4]


def body(
    queries,
    latent,
    residual,
    seg_lengths,
    span_order,
    expert_ids,
    route_weights,
    kv_up,
    out_proj,
    norm_gain,
    w_gate,
    w_up,
    w_down,
):
    local_rows, width = residual.shape
    span = local_rows // 2
    heads = kv_up.shape[1] // (NOPE + VHEAD)
    count = lax.axis_size("ctx")
    here = EXPERTS // count
    me, side = lax.axis_index("ctx"), lax.axis_index("exp")
    where = jnp.stack([me, side]).astype(jnp.int32)

    base = latent.shape[1]
    w_gate, w_up = w_gate.transpose(0, 2, 1), w_up.transpose(0, 2, 1)
    packed = pack(latent, expert_ids, route_weights)
    few = count <= FEW
    bring = lambda *arrays: stage(arrays, (None,) * len(arrays)) if few else arrays
    arrange = lambda x: x.reshape(local_rows, heads, NOPE + ROPE).transpose(1, 0, 2)
    scalars = lambda *arrays: jnp.concatenate([where, sources_of(me, side, count), *arrays])
    beside = [
        (arrange, (queries,)),
        (bring, (kv_up, out_proj, residual)),
        (lambda gain, *arrays: (gain.reshape(1, width), scalars(*arrays)), (norm_gain, span_order, seg_lengths)),
    ]
    found, made = gather(packed, count, beside)
    q, (kv_up, out_proj, residual), (gain, info) = made
    partial = attend(info, q, found, kv_up, out_proj, count)
    middle, normed = norm(where, residual, partial, swap(partial), gain)

    def place_rows(*blocks):
        if few:
            return route(where, blocks, here)
        facts = jnp.stack(blocks)[:, :, base : base + 2 * TOP].astype(jnp.float32)
        own = (me * here + jnp.arange(here, dtype=jnp.int32)).astype(jnp.float32)
        hit = facts[:, :, :TOP, None] == own
        hot = jnp.any(hit, axis=2)
        share = jnp.sum(jnp.where(hit, facts[:, :, TOP:, None], 0.0), axis=2)
        token = jnp.arange(local_rows, dtype=jnp.int32)
        before = (token[:, None] > token[None, :]).astype(jnp.bfloat16)
        rank = jnp.einsum("tu,cue->cte", before, hot.astype(jnp.bfloat16), preferred_element_type=jnp.float32)
        slot = jnp.arange(SLOTS, dtype=jnp.int32).astype(jnp.float32)
        combine = jnp.where(rank[:, :, :, None] == slot, share[:, :, :, None], 0.0)
        return combine.astype(jnp.bfloat16).reshape(count, local_rows, here * SLOTS)

    got, (combine,) = gather(normed, count, [(place_rows, tuple(found))])
    if few:
        parts, opposite, own = experts_fused(where, got, combine, w_gate, w_up, w_down)
        mixture = reduce(parts, opposite, own, side, count)
    else:
        pick = (combine > 0).astype(jnp.bfloat16)
        picked = jnp.einsum("cts,ctd->csd", pick, jnp.stack(got), preferred_element_type=jnp.float32).astype(jnp.bfloat16)
        picked = picked.reshape(count, here, SLOTS, width).transpose(1, 0, 2, 3).reshape(here, count * SLOTS, width)
        result = experts_plain(where, picked, w_gate, w_up, w_down)
        result = result.reshape(here, count, SLOTS, width).transpose(1, 0, 2, 3).reshape(count, here * SLOTS, width)
        total = jnp.einsum("cts,csd->ctd", combine, result, preferred_element_type=jnp.float32).astype(jnp.bfloat16)
        left, right = jnp.split(total, 2, axis=2)
        both = summed([jnp.where(side == 0, left, right), swap(jnp.where(side == 0, right, left))])
        mixture = lax.psum_scatter(both.astype(jnp.bfloat16), "ctx").astype(jnp.float32)
    return (middle.astype(jnp.float32) + mixture).astype(jnp.bfloat16)


def solution(mesh):
    in_specs = (
        P(("groups", "ctx"), "exp"),
        P(("groups", "ctx"), None),
        P(("groups", "ctx"), None),
        P("groups"),
        P("groups"),
        P(("groups", "ctx"), None),
        P(("groups", "ctx"), None),
        P(None, "exp"),
        P("exp", None),
        P(),
        P("ctx", None, "exp"),
        P("ctx", None, "exp"),
        P("ctx", "exp", None),
    )
    out_specs = P(("groups", "ctx"), "exp")
    return jax.shard_map(body, mesh=mesh, in_specs=in_specs, out_specs=out_specs, check_vma=False)
```

time: 134 us -> 139 us (1.037)
  waiting for transfers between devices: 54.7 us -> 64.5 us
  starting transfers between devices: 30.2 us -> 22.5 us
  other arithmetic: 1.73 us -> 3.84 us
    ppermute x24 -> x13, waiting for transfers between devices: 49.1 us -> 60.3 us  [turn(): return lax.ppermute(value, ('ctx', 'exp'), pairs)]
    ppermute x24 -> x13, starting transfers between devices: 25.6 us -> 21.5 us  [turn(): return lax.ppermute(value, ('ctx', 'exp'), pairs)]
    ppermute x25 -> x12, starting transfers between devices: 4.6 us -> 0.96 us  [swap(): return lax.ppermute(value, 'exp', SWAP)]
    slice x5 -> x0, local copies, waits for them, and re-layouts: 1.61 us -> none  [the longest x2 0.79 us: gather(): found[middle + 1][half:]]
    ppermute x25 -> x12, waiting for transfers between devices: 5.59 us -> 4.19 us  [swap(): return lax.ppermute(value, 'exp', SWAP)]
    unnamed x10 -> x14, local copies, waits for them, and re-layouts: 3.38 us -> 4.38 us
  transfers between devices with their start and end apart: 49 -> 25, of which waited for: 23 -> 17; matrix products, arithmetic and copies ran while one was open for 4% -> 5% of each run, Pallas kernels for 3% -> 3%
where the time goes in v9:
time: 139 us; the launch traced here: 138 us
  waiting for transfers between devices  64.5 us (46%)
  Pallas kernels  39 us (28%)
  starting transfers between devices  22.5 us (16%)
  local copies, waits for them, and re-layouts  8.45 us (6%)
  other arithmetic  3.84 us (3%)
    ppermute x13, waiting for transfers between devices, turn(): return lax.ppermute(value, ('ctx', 'exp'), pairs)  60.3 us
    pallas_call x1, Pallas kernels, experts_fused(): pl.pallas_call(functools.partial(fused_kernel, count), in_specs=[pl.Block...  26.9 us
    ppermute x13, starting transfers between devices, turn(): return lax.ppermute(value, ('ctx', 'exp'), pairs)  21.5 us
    pallas_call x1, Pallas kernels, attend(): pl.pallas_call(functools.partial(attend_kernel, count, blocks), grid_spec...  5.59 us
    unnamed x14, local copies, waits for them, and re-layouts  4.38 us
    ppermute x12, waiting for transfers between devices, swap(): return lax.ppermute(value, 'exp', SWAP)  4.19 us
  transfers between devices with their start and end apart: 25, of which 17 were waited for; matrix products, arithmetic and copies ran while one was open for 5% of the time, Pallas kernels for 3%

profile of v9, /device:TPU:0, one launch (start us, length us, event | category | flops | bytes accessed | tf_op | source)
XLA Modules:
  0.0 138.4 jit_solution(1433005397853352088)
XLA Ops:
  0.0 1.1 pack.1.refs_0_
  1.1 3.0 %collective-permute-start = (bf16[128,640]{1,0:T(8,128)(2,1)S(1)}, bf16[128,640]{1,0:T(8,128)(2,1)S(1)}, u32[]{:S(2)}, u32[]{:S(2)}) collective-permute-start(bf16[128,640]{1,0:T(8,128)(2,1)S(1)} %pack.1.refs_0_), channel_id=1, source_target_pairs={{0,2},{1,5},{2,6},{3,1},{6,10},{7,3},{10,14},{11,7},{14,12},{15,11... | collective-permute-start | bytes 491528 | tf_op jit(solution)/shard_map/ppermute | solution.py:48
  4.2 1.1 copy.15
  5.3 0.9 copy.16
  6.1 1.4 %collective-permute-done.refs_1_ = bf16[128,640]{1,0:T(8,128)(2,1)S(1)} collective-permute-done((bf16[128,640]{1,0:T(8,128)(2,1)S(1)}, bf16[128,640]{1,0:T(8,128)(2,1)S(1)}, u32[]{:S(2)}, u32[]{:S(2)}) %collective-permute-start) | collective-permute-done | bytes 163872 | tf_op jit(solution)/shard_map/ppermute | solution.py:48
  7.5 2.0 %collective-permute-start.1 = (bf16[128,640]{1,0:T(8,128)(2,1)S(1)}, bf16[128,640]{1,0:T(8,128)(2,1)}, u32[]{:S(2)}, u32[]{:S(2)}) collective-permute-start(bf16[128,640]{1,0:T(8,128)(2,1)S(1)} %collective-permute-done.refs_1_), channel_id=1, source_target_pairs={{0,2},{1,5},{2,6},{3,1},{6,10},{7,3},{10,14},{11,7},{14,12},{15,11... | collective-permute-start | bytes 491528 | tf_op jit(solution)/shard_map/ppermute | solution.py:48
  9.5 2.0 %stage.1 = (bf16[512,1024]{1,0:T(8,128)(2,1)S(1)}, bf16[512,2048]{1,0:T(8,128)(2,1)S(1)}, bf16[128,2048]{1,0:T(8,128)(2,1)S(1)}) custom-call(bf16[512,1024]{1,0:T(8,128)(2,1)} %refs_0_, bf16[512,2048]{1,0:T(8,128)(2,1)} %refs_1_, bf16[128,2048]{1,0:T(8,128)(2,1)} %refs_2_), custom_call_target="tpu_custom_call" | custom-call | tf_op jit(solution)/shard_map/stage/pallas_call | solution.py:245
  11.5 0.8 copy-done.3
  12.3 0.7 copy-done.1
  13.0 0.3 collective-permute-start.4
  13.3 1.6 %collective-permute-start.3 = (bf16[128,640]{1,0:T(8,128)(2,1)}, bf16[128,640]{1,0:T(8,128)(2,1)}, u32[]{:S(2)}, u32[]{:S(2)}) collective-permute-start(bf16[128,640]{1,0:T(8,128)(2,1)} %collective-permute-done.1.refs_2_), channel_id=1, source_target_pairs={{0,2},{1,5},{2,6},{3,1},{6,10},{7,3},{10,14},{11,7},{14,12},{15,11... | collective-permute-start | bytes 491528 | tf_op jit(solution)/shard_map/ppermute | solution.py:48
  14.9 0.7 dynamic-slice_bitcast_fusion
  15.6 0.7 reshape.7.gain_ref
  16.3 0.7 concatenate.7.info
  17.1 1.9 %collective-permute-done.3.refs_3_ = bf16[128,640]{1,0:T(8,128)(2,1)} collective-permute-done((bf16[128,640]{1,0:T(8,128)(2,1)}, bf16[128,640]{1,0:T(8,128)(2,1)}, u32[]{:S(2)}, u32[]{:S(2)}) %collective-permute-start.3) | collective-permute-done | bytes 163872 | tf_op jit(solution)/shard_map/ppermute | solution.py:48
  18.9 1.6 %collective-permute-start.5 = (bf16[128,640]{1,0:T(8,128)(2,1)}, bf16[128,640]{1,0:T(8,128)(2,1)S(1)}, u32[]{:S(2)}, u32[]{:S(2)}) collective-permute-start(bf16[128,640]{1,0:T(8,128)(2,1)} %collective-permute-done.3.refs_3_), channel_id=1, source_target_pairs={{0,2},{1,5},{2,6},{3,1},{6,10},{7,3},{10,14},{11,7},{14,12},{15,11... | collective-permute-start | bytes 491528 | tf_op jit(solution)/shard_map/ppermute | solution.py:48
  20.6 3.9 %collective-permute-done.5.refs_4_ = bf16[128,640]{1,0:T(8,128)(2,1)S(1)} collective-permute-done((bf16[128,640]{1,0:T(8,128)(2,1)}, bf16[128,640]{1,0:T(8,128)(2,1)S(1)}, u32[]{:S(2)}, u32[]{:S(2)}) %collective-permute-start.5) | collective-permute-done | bytes 163872 | tf_op jit(solution)/shard_map/ppermute | solution.py:48
  24.5 0.9 copy-done
  25.4 0.9 copy-done.2
  26.3 5.6 %attend.1.here_ref = bf16[128,2048]{1,0:T(8,128)(2,1)S(1)} custom-call(s32[42]{0:T(128)S(1)} %concatenate.7.info, bf16[4,128,192]{2,1,0:T(8,128)(2,1)S(1)} %bitcast.11, bf16[128,640]{1,0:T(8,128)(2,1)S(1)} %pack.1.refs_0_, bf16[128,640]{1,0:T(8,128)(2,1)S(1)} %collective-permute-done.refs_1_, bf16[128,640]{1,0:T(8,128)(2,1)} %collective-permute-done.1.refs_2_, ...), custom_call_target="tpu_custom_call" | custom-call | tf_op jit(solution)/shard_map/attend/pallas_call | solution.py:175
  32.1 1.8 %collective-permute-done.7.there_ref = bf16[128,2048]{1,0:T(8,128)(2,1)S(1)} collective-permute-done((bf16[128,2048]{1,0:T(8,128)(2,1)S(1)}, bf16[128,2048]{1,0:T(8,128)(2,1)S(1)}, u32[]{:S(2)}, u32[]{:S(2)}) %collective-permute-start.7) | collective-permute-done | bytes 524320 | tf_op jit(solution)/shard_map/ppermute | solution.py:39
  33.9 1.0 copy-done.4
  34.9 1.0 norm.1
  35.9 1.7 %collective-permute-start.8 = (bf16[128,2048]{1,0:T(8,128)(2,1)S(1)}, bf16[128,2048]{1,0:T(8,128)(2,1)S(1)}, u32[]{:S(2)}, u32[]{:S(2)}) collective-permute-start(bf16[128,2048]{1,0:T(8,128)(2,1)S(1)} %get-tuple-element.80.refs_0_), channel_id=1, source_target_pairs={{0,2},{1,5},{2,6},{3,1},{6,10},{7,3},{10,14},{11,7},{14,12},{15,11... | collective-permute-start | bytes 1572872 | tf_op jit(solution)/shard_map/ppermute | solution.py:48
  37.6 2.4 %route.1.refs_8_ = bf16[8,128,128]{2,1,0:T(8,128)(2,1)S(1)} custom-call(s32[2]{0:T(128)S(1)} %pad_add_fusion.where, bf16[128,640]{1,0:T(8,128)(2,1)S(1)} %pack.1.refs_0_, bf16[128,640]{1,0:T(8,128)(2,1)S(1)} %collective-permute-done.refs_1_, bf16[128,640]{1,0:T(8,128)(2,1)} %collective-permute-done.1.refs_2_, ...), custom_call_target="tpu_custom_call" | custom-call | tf_op jit(solution)/shard_map/route/pallas_call | solution.py:217
  40.0 5.2 %collective-permute-done.8.refs_1_ = bf16[128,2048]{1,0:T(8,128)(2,1)S(1)} collective-permute-done((bf16[128,2048]{1,0:T(8,128)(2,1)S(1)}, bf16[128,2048]{1,0:T(8,128)(2,1)S(1)}, u32[]{:S(2)}, u32[]{:S(2)}) %collective-permute-start.8) | collective-permute-done | bytes 524320 | tf_op jit(solution)/shard_map/ppermute | solution.py:48
  45.2 1.6 %collective-permute-start.9 = (bf16[128,2048]{1,0:T(8,128)(2,1)S(1)}, bf16[128,2048]{1,0:T(8,128)(2,1)S(1)}, u32[]{:S(2)}, u32[]{:S(2)}) collective-permute-start(bf16[128,2048]{1,0:T(8,128)(2,1)S(1)} %collective-permute-done.8.refs_1_), channel_id=1, source_target_pairs={{0,2},{1,5},{2,6},{3,1},{6,10},{7,3},{10,14},{11,7},{14,12},{15,11... | collective-permute-start | bytes 1572872 | tf_op jit(solution)/shard_map/ppermute | solution.py:48
  46.8 0.3 collective-permute-done.10.refs_5_
  47.1 7.3 %collective-permute-done.9.refs_2_ = bf16[128,2048]{1,0:T(8,128)(2,1)S(1)} collective-permute-done((bf16[128,2048]{1,0:T(8,128)(2,1)S(1)}, bf16[128,2048]{1,0:T(8,128)(2,1)S(1)}, u32[]{:S(2)}, u32[]{:S(2)}) %collective-permute-start.9) | collective-permute-done | bytes 524320 | tf_op jit(solution)/shard_map/ppermute | solution.py:48
  54.3 1.6 %collective-permute-start.11 = (bf16[128,2048]{1,0:T(8,128)(2,1)S(1)}, bf16[128,2048]{1,0:T(8,128)(2,1)S(1)}, u32[]{:S(2)}, u32[]{:S(2)}) collective-permute-start(bf16[128,2048]{1,0:T(8,128)(2,1)S(1)} %collective-permute-done.9.refs_2_), channel_id=1, source_target_pairs={{0,2},{1,5},{2,6},{3,1},{6,10},{7,3},{10,14},{11,7},{14,12},{15,11... | collective-permute-start | bytes 1572872 | tf_op jit(solution)/shard_map/ppermute | solution.py:48
  56.2 7.3 %collective-permute-done.11.refs_3_ = bf16[128,2048]{1,0:T(8,128)(2,1)S(1)} collective-permute-done((bf16[128,2048]{1,0:T(8,128)(2,1)S(1)}, bf16[128,2048]{1,0:T(8,128)(2,1)S(1)}, u32[]{:S(2)}, u32[]{:S(2)}) %collective-permute-start.11) | collective-permute-done | bytes 524320 | tf_op jit(solution)/shard_map/ppermute | solution.py:48
  63.5 1.6 %collective-permute-start.13 = (bf16[128,2048]{1,0:T(8,128)(2,1)S(1)}, bf16[128,2048]{1,0:T(8,128)(2,1)S(1)}, u32[]{:S(2)}, u32[]{:S(2)}) collective-permute-start(bf16[128,2048]{1,0:T(8,128)(2,1)S(1)} %collective-permute-done.11.refs_3_), channel_id=1, source_target_pairs={{0,2},{1,5},{2,6},{3,1},{6,10},{7,3},{10,14},{11,7},{14,12},{15,11... | collective-permute-start | bytes 1572872 | tf_op jit(solution)/shard_map/ppermute | solution.py:48
  65.4 7.3 %collective-permute-done.13.refs_4_ = bf16[128,2048]{1,0:T(8,128)(2,1)S(1)} collective-permute-done((bf16[128,2048]{1,0:T(8,128)(2,1)S(1)}, bf16[128,2048]{1,0:T(8,128)(2,1)S(1)}, u32[]{:S(2)}, u32[]{:S(2)}) %collective-permute-start.13) | collective-permute-done | bytes 524320 | tf_op jit(solution)/shard_map/ppermute | solution.py:48
  72.7 26.9 %experts.1 = (bf16[64,2048]{1,0:T(8,128)(2,1)S(1)}, bf16[64,2048]{1,0:T(8,128)(2,1)S(1)}, bf16[128,1024]{1,0:T(8,128)(2,1)S(1)}, bf16[128,1024]{1,0:T(8,128)(2,1...) custom-call(s32[2]{0:T(128)S(1)} %pad_add_fusion.where, ...), custom_call_target="tpu_custom_call" | custom-call | tf_op jit(solution)/shard_map/experts/pallas_call | solution.py:415
  99.7 1.5 %collective-permute-done.19 = bf16[64,2048]{1,0:T(8,128)(2,1)S(1)} collective-permute-done((bf16[64,2048]{1,0:T(8,128)(2,1)S(1)}, bf16[64,2048]{1,0:T(8,128)(2,1)S(1)}, u32[]{:S(2)}, u32[]{:S(2)}) %collective-permute-start.19) | collective-permute-done | bytes 262176 | tf_op jit(solution)/shard_map/ppermute | solution.py:39
  101.3 1.7 %collective-permute-start.20 = (bf16[64,2048]{1,0:T(8,128)(2,1)S(1)}, bf16[64,2048]{1,0:T(8,128)(2,1)}, u32[]{:S(2)}, u32[]{:S(2)}) collective-permute-start(bf16[64,2048]{1,0:T(8,128)(2,1)S(1)} %add_convert_fusion.3), channel_id=1, source_target_pairs={{0,2},{1,5},{2,6},{3,1},{6,10},{7,3},{10,14},{11,7},{14,12},{15,11... | collective-permute-start | bytes 786440 | tf_op jit(solution)/shard_map/ppermute | solution.py:48
  103.0 0.5 collective-permute-start.17
  103.5 4.3 %collective-permute-done.20 = bf16[64,2048]{1,0:T(8,128)(2,1)} collective-permute-done((bf16[64,2048]{1,0:T(8,128)(2,1)S(1)}, bf16[64,2048]{1,0:T(8,128)(2,1)}, u32[]{:S(2)}, u32[]{:S(2)}) %collective-permute-start.20) | collective-permute-done | bytes 262176 | tf_op jit(solution)/shard_map/ppermute | solution.py:48
  107.8 1.0 convert_select_fusion.1
  108.8 1.2 fusion
  110.1 1.7 %collective-permute-start.21 = (bf16[128,2048]{1,0:T(8,128)(2,1)S(1)}, bf16[128,2048]{1,0:T(8,128)(2,1)S(1)}, u32[]{:S(2)}, u32[]{:S(2)}) collective-permute-start(bf16[128,2048]{1,0:T(8,128)(2,1)S(1)} %fusion), channel_id=1, source_target_pairs={{0,2},{1,5},{2,6},{3,1},{6,10},{7,3},{10,14},{11,7},{14,12},{15,11... | collective-permute-start | bytes 1572872 | tf_op jit(solution)/shard_map/ppermute | solution.py:48
  111.8 7.5 %collective-permute-done.21 = bf16[128,2048]{1,0:T(8,128)(2,1)S(1)} collective-permute-done((bf16[128,2048]{1,0:T(8,128)(2,1)S(1)}, bf16[128,2048]{1,0:T(8,128)(2,1)S(1)}, u32[]{:S(2)}, u32[]{:S(2)}) %collective-permute-start.21) | collective-permute-done | bytes 524320 | tf_op jit(solution)/shard_map/ppermute | solution.py:48
  119.6 1.7 %collective-permute-start.22 = (bf16[128,2048]{1,0:T(8,128)(2,1)S(1)}, bf16[128,2048]{1,0:T(8,128)(2,1)S(1)}, u32[]{:S(2)}, u32[]{:S(2)}) collective-permute-start(bf16[128,2048]{1,0:T(8,128)(2,1)S(1)} %add_convert_fusion.1), channel_id=1, source_target_pairs={{0,2},{1,5},{2,6},{3,1},{6,10},{7,3},{10,14},{11,7},{14,12},{15,11... | collective-permute-start | bytes 1572872 | tf_op jit(solution)/shard_map/ppermute | solution.py:48
  121.2 7.5 %collective-permute-done.22 = bf16[128,2048]{1,0:T(8,128)(2,1)S(1)} collective-permute-done((bf16[128,2048]{1,0:T(8,128)(2,1)S(1)}, bf16[128,2048]{1,0:T(8,128)(2,1)S(1)}, u32[]{:S(2)}, u32[]{:S(2)}) %collective-permute-start.22) | collective-permute-done | bytes 524320 | tf_op jit(solution)/shard_map/ppermute | solution.py:48
  129.1 1.7 %collective-permute-start.23 = (bf16[128,1024]{1,0:T(8,128)(2,1)S(1)}, bf16[128,1024]{1,0:T(8,128)(2,1)S(1)}, u32[]{:S(2)}, u32[]{:S(2)}) collective-permute-start(bf16[128,1024]{1,0:T(8,128)(2,1)S(1)} %get-tuple-element.107), channel_id=1, source_target_pairs={{0,2},{1,5},{2,6},{3,1},{6,10},{7,3},{10,14},{11,7},{14,12},{15,11... | collective-permute-start | bytes 786440 | tf_op jit(solution)/shard_map/ppermute | solution.py:48
  130.8 4.7 %collective-permute-done.23 = bf16[128,1024]{1,0:T(8,128)(2,1)S(1)} collective-permute-done((bf16[128,1024]{1,0:T(8,128)(2,1)S(1)}, bf16[128,1024]{1,0:T(8,128)(2,1)S(1)}, u32[]{:S(2)}, u32[]{:S(2)}) %collective-permute-start.23) | collective-permute-done | bytes 262176 | tf_op jit(solution)/shard_map/ppermute | solution.py:48
  135.5 2.0 %collective-permute-done.24 = bf16[128,1024]{1,0:T(8,128)(2,1)S(1)} collective-permute-done((bf16[128,1024]{1,0:T(8,128)(2,1)S(1)}, bf16[128,1024]{1,0:T(8,128)(2,1)S(1)}, u32[]{:S(2)}, u32[]{:S(2)}) %collective-permute-start.24) | collective-permute-done | bytes 262176 | tf_op jit(solution)/shard_map/ppermute | solution.py:48
  137.5 0.9 add_convert_fusion.2
  (35 shorter events, 1.4 us)
Async XLA Ops:
  1.1 6.4 %collective-permute-start = (bf16[128,640]{1,0:T(8,128)(2,1)S(1)}, bf16[128,640]{1,0:T(8,128)(2,1)S(1)}, u32[]{:S(2)}, u32[]{:S(2)}) collective-permute-start(bf16[128,640]{1,0:T(8,128)(2,1)S(1)} %pack.1.refs_0_), channel_id=1, source_target_pairs={{0,2},{1,5},{2,6},{3,1},{6,10},{7,3},{10,14},{11,7},{14,12},{15,11... | collective-permute-start | bytes 491528 | tf_op jit(solution)/shard_map/ppermute | solution.py:48
  7.5 4.8 %collective-permute-start.2 = (bf16[128,640]{1,0:T(8,128)(2,1)S(1)}, bf16[128,640]{1,0:T(8,128)(2,1)S(1)}, u32[]{:S(2)}, u32[]{:S(2)}) collective-permute-start(bf16[128,640]{1,0:T(8,128)(2,1)S(1)} %collective-permute-done.refs_1_), channel_id=1, source_target_pairs={{0,1},{1,0},{2,3},{3,2},{4,5},{5,4},{6,7},{7,6},{8,9},{9,8},{10,11... | collective-permute-start | bytes 491528 | tf_op jit(solution)/shard_map/ppermute | solution.py:39
  7.5 5.5 %collective-permute-start.1 = (bf16[128,640]{1,0:T(8,128)(2,1)S(1)}, bf16[128,640]{1,0:T(8,128)(2,1)}, u32[]{:S(2)}, u32[]{:S(2)}) collective-permute-start(bf16[128,640]{1,0:T(8,128)(2,1)S(1)} %collective-permute-done.refs_1_), channel_id=1, source_target_pairs={{0,2},{1,5},{2,6},{3,1},{6,10},{7,3},{10,14},{11,7},{14,12},{15,11... | collective-permute-start | bytes 491528 | tf_op jit(solution)/shard_map/ppermute | solution.py:48
  11.5 0.8 copy-start.3
  12.3 0.7 copy-start.1
  13.0 4.0 %collective-permute-start.4 = (bf16[128,640]{1,0:T(8,128)(2,1)}, bf16[128,640]{1,0:T(8,128)(2,1)}, u32[]{:S(2)}, u32[]{:S(2)}) collective-permute-start(bf16[128,640]{1,0:T(8,128)(2,1)} %collective-permute-done.1.refs_2_), channel_id=1, source_target_pairs={{0,1},{1,0},{2,3},{3,2},{4,5},{5,4},{6,7},{7,6},{8,9},{9,8},{10,11... | collective-permute-start | bytes 491528 | tf_op jit(solution)/shard_map/ppermute | solution.py:39
  13.3 5.6 %collective-permute-start.3 = (bf16[128,640]{1,0:T(8,128)(2,1)}, bf16[128,640]{1,0:T(8,128)(2,1)}, u32[]{:S(2)}, u32[]{:S(2)}) collective-permute-start(bf16[128,640]{1,0:T(8,128)(2,1)} %collective-permute-done.1.refs_2_), channel_id=1, source_target_pairs={{0,2},{1,5},{2,6},{3,1},{6,10},{7,3},{10,14},{11,7},{14,12},{15,11... | collective-permute-start | bytes 491528 | tf_op jit(solution)/shard_map/ppermute | solution.py:48
  18.9 1.6 %collective-permute-start.6 = (bf16[128,640]{1,0:T(8,128)(2,1)}, bf16[128,640]{1,0:T(8,128)(2,1)S(1)}, u32[]{:S(2)}, u32[]{:S(2)}) collective-permute-start(bf16[128,640]{1,0:T(8,128)(2,1)} %collective-permute-done.3.refs_3_), channel_id=1, source_target_pairs={{0,1},{1,0},{2,3},{3,2},{4,5},{5,4},{6,7},{7,6},{8,9},{9,8},{10,11... | collective-permute-start | bytes 491528 | tf_op jit(solution)/shard_map/ppermute | solution.py:39
  18.9 5.5 %collective-permute-start.5 = (bf16[128,640]{1,0:T(8,128)(2,1)}, bf16[128,640]{1,0:T(8,128)(2,1)S(1)}, u32[]{:S(2)}, u32[]{:S(2)}) collective-permute-start(bf16[128,640]{1,0:T(8,128)(2,1)} %collective-permute-done.3.refs_3_), channel_id=1, source_target_pairs={{0,2},{1,5},{2,6},{3,1},{6,10},{7,3},{10,14},{11,7},{14,12},{15,11... | collective-permute-start | bytes 491528 | tf_op jit(solution)/shard_map/ppermute | solution.py:48
  24.5 1.0 copy-start
  25.4 0.9 copy-start.2
  31.9 2.0 %collective-permute-start.7 = (bf16[128,2048]{1,0:T(8,128)(2,1)S(1)}, bf16[128,2048]{1,0:T(8,128)(2,1)S(1)}, u32[]{:S(2)}, u32[]{:S(2)}) collective-permute-start(bf16[128,2048]{1,0:T(8,128)(2,1)S(1)} %attend.1.here_ref), channel_id=1, source_target_pairs={{0,1},{1,0},{2,3},{3,2},{4,5},{5,4},{6,7},{7,6},{8,9},{9,8},{10,11... | collective-permute-start | bytes 1572872 | tf_op jit(solution)/shard_map/ppermute | solution.py:39
  33.9 1.0 copy-start.4
  35.9 9.2 %collective-permute-start.8 = (bf16[128,2048]{1,0:T(8,128)(2,1)S(1)}, bf16[128,2048]{1,0:T(8,128)(2,1)S(1)}, u32[]{:S(2)}, u32[]{:S(2)}) collective-permute-start(bf16[128,2048]{1,0:T(8,128)(2,1)S(1)} %get-tuple-element.80.refs_0_), channel_id=1, source_target_pairs={{0,2},{1,5},{2,6},{3,1},{6,10},{7,3},{10,14},{11,7},{14,12},{15,11... | collective-permute-start | bytes 1572872 | tf_op jit(solution)/shard_map/ppermute | solution.py:48
  45.1 1.9 %collective-permute-start.10 = (bf16[128,2048]{1,0:T(8,128)(2,1)S(1)}, bf16[128,2048]{1,0:T(8,128)(2,1)S(1)}, u32[]{:S(2)}, u32[]{:S(2)}) collective-permute-start(bf16[128,2048]{1,0:T(8,128)(2,1)S(1)} %collective-permute-done.8.refs_1_), channel_id=1, source_target_pairs={{0,1},{1,0},{2,3},{3,2},{4,5},{5,4},{6,7},{7,6},{8,9},{9,8},{10,11... | collective-permute-start | bytes 1572872 | tf_op jit(solution)/shard_map/ppermute | solution.py:39
  45.2 9.2 %collective-permute-start.9 = (bf16[128,2048]{1,0:T(8,128)(2,1)S(1)}, bf16[128,2048]{1,0:T(8,128)(2,1)S(1)}, u32[]{:S(2)}, u32[]{:S(2)}) collective-permute-start(bf16[128,2048]{1,0:T(8,128)(2,1)S(1)} %collective-permute-done.8.refs_1_), channel_id=1, source_target_pairs={{0,2},{1,5},{2,6},{3,1},{6,10},{7,3},{10,14},{11,7},{14,12},{15,11... | collective-permute-start | bytes 1572872 | tf_op jit(solution)/shard_map/ppermute | solution.py:48
  54.3 1.9 %collective-permute-start.12 = (bf16[128,2048]{1,0:T(8,128)(2,1)S(1)}, bf16[128,2048]{1,0:T(8,128)(2,1)S(1)}, u32[]{:S(2)}, u32[]{:S(2)}) collective-permute-start(bf16[128,2048]{1,0:T(8,128)(2,1)S(1)} %collective-permute-done.9.refs_2_), channel_id=1, source_target_pairs={{0,1},{1,0},{2,3},{3,2},{4,5},{5,4},{6,7},{7,6},{8,9},{9,8},{10,11... | collective-permute-start | bytes 1572872 | tf_op jit(solution)/shard_map/ppermute | solution.py:39
  54.3 9.2 %collective-permute-start.11 = (bf16[128,2048]{1,0:T(8,128)(2,1)S(1)}, bf16[128,2048]{1,0:T(8,128)(2,1)S(1)}, u32[]{:S(2)}, u32[]{:S(2)}) collective-permute-start(bf16[128,2048]{1,0:T(8,128)(2,1)S(1)} %collective-permute-done.9.refs_2_), channel_id=1, source_target_pairs={{0,2},{1,5},{2,6},{3,1},{6,10},{7,3},{10,14},{11,7},{14,12},{15,11... | collective-permute-start | bytes 1572872 | tf_op jit(solution)/shard_map/ppermute | solution.py:48
  63.5 1.9 %collective-permute-start.14 = (bf16[128,2048]{1,0:T(8,128)(2,1)S(1)}, bf16[128,2048]{1,0:T(8,128)(2,1)S(1)}, u32[]{:S(2)}, u32[]{:S(2)}) collective-permute-start(bf16[128,2048]{1,0:T(8,128)(2,1)S(1)} %collective-permute-done.11.refs_3_), channel_id=1, source_target_pairs={{0,1},{1,0},{2,3},{3,2},{4,5},{5,4},{6,7},{7,6},{8,9},{9,8},{10,11... | collective-permute-start | bytes 1572872 | tf_op jit(solution)/shard_map/ppermute | solution.py:39
  63.5 9.2 %collective-permute-start.13 = (bf16[128,2048]{1,0:T(8,128)(2,1)S(1)}, bf16[128,2048]{1,0:T(8,128)(2,1)S(1)}, u32[]{:S(2)}, u32[]{:S(2)}) collective-permute-start(bf16[128,2048]{1,0:T(8,128)(2,1)S(1)} %collective-permute-done.11.refs_3_), channel_id=1, source_target_pairs={{0,2},{1,5},{2,6},{3,1},{6,10},{7,3},{10,14},{11,7},{14,12},{15,11... | collective-permute-start | bytes 1572872 | tf_op jit(solution)/shard_map/ppermute | solution.py:48
  99.6 1.7 %copy-start.5 = (bf16[128,2048]{1,0:T(8,128)(2,1)}, bf16[128,2048]{1,0:T(8,128)(2,1)S(1)}, u32[]{:S(2)}) copy-start(bf16[128,2048]{1,0:T(8,128)(2,1)S(1)} %get-tuple-element.102) | copy-start | bytes 1572868
  99.6 3.4 %copy-start.6 = (bf16[128,1024]{1,0:T(8,128)(2,1)}, bf16[128,1024]{1,0:T(8,128)(2,1)S(1)}, u32[]{:S(2)}) copy-start(bf16[128,1024]{1,0:T(8,128)(2,1)S(1)} %get-tuple-element.98) | copy-start | bytes 786436
  99.6 1.6 %collective-permute-start.19 = (bf16[64,2048]{1,0:T(8,128)(2,1)S(1)}, bf16[64,2048]{1,0:T(8,128)(2,1)S(1)}, u32[]{:S(2)}, u32[]{:S(2)}) collective-permute-start(bf16[64,2048]{1,0:T(8,128)(2,1)S(1)} %get-tuple-element.106), channel_id=1, source_target_pairs={{0,1},{1,0},{2,3},{3,2},{4,5},{5,4},{6,7},{7,6},{8,9},{9,8},{10,11... | collective-permute-start | bytes 786440 | tf_op jit(solution)/shard_map/ppermute | solution.py:39
  101.3 6.5 %collective-permute-start.20 = (bf16[64,2048]{1,0:T(8,128)(2,1)S(1)}, bf16[64,2048]{1,0:T(8,128)(2,1)}, u32[]{:S(2)}, u32[]{:S(2)}) collective-permute-start(bf16[64,2048]{1,0:T(8,128)(2,1)S(1)} %add_convert_fusion.3), channel_id=1, source_target_pairs={{0,2},{1,5},{2,6},{3,1},{6,10},{7,3},{10,14},{11,7},{14,12},{15,11... | collective-permute-start | bytes 786440 | tf_op jit(solution)/shard_map/ppermute | solution.py:48
  103.0 5.9 %collective-permute-start.18 = (bf16[128,2048]{1,0:T(8,128)(2,1)}, bf16[128,2048]{1,0:T(8,128)(2,1)}, u32[]{:S(2)}, u32[]{:S(2)}) collective-permute-start(bf16[128,2048]{1,0:T(8,128)(2,1)} %get-tuple-element.104), channel_id=1, source_target_pairs={{0,1},{1,0},{2,3},{3,2},{4,5},{5,4},{6,7},{7,6},{8,9},{9,8},{10,11... | collective-permute-start | bytes 1572872 | tf_op jit(solution)/shard_map/ppermute | solution.py:39
  103.0 8.8 %collective-permute-start.17 = (bf16[128,2048]{1,0:T(8,128)(2,1)}, bf16[128,2048]{1,0:T(8,128)(2,1)S(1)}, u32[]{:S(2)}, u32[]{:S(2)}) collective-permute-start(bf16[128,2048]{1,0:T(8,128)(2,1)} %copy-done.5), channel_id=1, source_target_pairs={{0,1},{1,0},{2,3},{3,2},{4,5},{5,4},{6,7},{7,6},{8,9},{9,8},{10,11... | collective-permute-start | bytes 1572872 | tf_op jit(solution)/shard_map/ppermute | solution.py:39
  110.1 9.2 %collective-permute-start.21 = (bf16[128,2048]{1,0:T(8,128)(2,1)S(1)}, bf16[128,2048]{1,0:T(8,128)(2,1)S(1)}, u32[]{:S(2)}, u32[]{:S(2)}) collective-permute-start(bf16[128,2048]{1,0:T(8,128)(2,1)S(1)} %fusion), channel_id=1, source_target_pairs={{0,2},{1,5},{2,6},{3,1},{6,10},{7,3},{10,14},{11,7},{14,12},{15,11... | collective-permute-start | bytes 1572872 | tf_op jit(solution)/shard_map/ppermute | solution.py:48
  111.8 9.5 %collective-permute-start.16 = (bf16[128,2048]{1,0:T(8,128)(2,1)S(1)}, bf16[128,2048]{1,0:T(8,128)(2,1)S(1)}, u32[]{:S(2)}, u32[]{:S(2)}) collective-permute-start(bf16[128,2048]{1,0:T(8,128)(2,1)S(1)} %get-tuple-element.100), channel_id=1, source_target_pairs={{0,1},{1,0},{2,3},{3,2},{4,5},{5,4},{6,7},{7,6},{8,9},{9,8},{10,11... | collective-permute-start | bytes 1572872 | tf_op jit(solution)/shard_map/ppermute | solution.py:39
  119.6 9.2 %collective-permute-start.22 = (bf16[128,2048]{1,0:T(8,128)(2,1)S(1)}, bf16[128,2048]{1,0:T(8,128)(2,1)S(1)}, u32[]{:S(2)}, u32[]{:S(2)}) collective-permute-start(bf16[128,2048]{1,0:T(8,128)(2,1)S(1)} %add_convert_fusion.1), channel_id=1, source_target_pairs={{0,2},{1,5},{2,6},{3,1},{6,10},{7,3},{10,14},{11,7},{14,12},{15,11... | collective-permute-start | bytes 1572872 | tf_op jit(solution)/shard_map/ppermute | solution.py:48
  121.2 9.5 %collective-permute-start.15 = (bf16[128,1024]{1,0:T(8,128)(2,1)}, bf16[128,1024]{1,0:T(8,128)(2,1)S(1)}, u32[]{:S(2)}, u32[]{:S(2)}) collective-permute-start(bf16[128,1024]{1,0:T(8,128)(2,1)} %copy-done.6), channel_id=1, source_target_pairs={{0,1},{1,0},{2,3},{3,2},{4,5},{5,4},{6,7},{7,6},{8,9},{9,8},{10,11... | collective-permute-start | bytes 786440 | tf_op jit(solution)/shard_map/ppermute | solution.py:39
  129.1 6.4 %collective-permute-start.23 = (bf16[128,1024]{1,0:T(8,128)(2,1)S(1)}, bf16[128,1024]{1,0:T(8,128)(2,1)S(1)}, u32[]{:S(2)}, u32[]{:S(2)}) collective-permute-start(bf16[128,1024]{1,0:T(8,128)(2,1)S(1)} %get-tuple-element.107), channel_id=1, source_target_pairs={{0,2},{1,5},{2,6},{3,1},{6,10},{7,3},{10,14},{11,7},{14,12},{15,11... | collective-permute-start | bytes 786440 | tf_op jit(solution)/shard_map/ppermute | solution.py:48
  130.8 6.7 %collective-permute-start.24 = (bf16[128,1024]{1,0:T(8,128)(2,1)S(1)}, bf16[128,1024]{1,0:T(8,128)(2,1)S(1)}, u32[]{:S(2)}, u32[]{:S(2)}) collective-permute-start(bf16[128,1024]{1,0:T(8,128)(2,1)S(1)} %get-tuple-element.108), channel_id=1, source_target_pairs={{0,3},{1,4},{2,7},{3,0},{6,11},{7,2},{10,15},{11,6},{14,13},{15,10... | collective-permute-start | bytes 786440 | tf_op jit(solution)/shard_map/ppermute | solution.py:48

commit v10 on v9

--- a/solution.py
+++ b/solution.py
@@ -22,6 +22,7 @@
 DEPTH = 3
 PIECES = 2
 SWAP = [(0, 1), (1, 0)]
+PARTS = 2
 FEW = 8
 
 
@@ -68,13 +69,14 @@
     return lax.dynamic_index_in_dim(jnp.asarray(table), me * 2 + side, keepdims=False)
 
 
-def gather(block, count, beside=()):
+def gather(arrays, count, beside=()):
     if count > FEW:
-        return list(lax.all_gather(block, "ctx")), [run(*arguments) for run, arguments in beside]
+        found = [lax.all_gather(block, "ctx") for block in arrays]
+        return list(zip(*found)), [run(*arguments) for run, arguments in beside]
     middle = count // 2
-    found, other, made = [block], [()], []
+    found, other, made = [tuple(arrays)], [()], []
     for d in range(1, middle + 1):
-        arrived, extra = turn(found[-1], count), ()
+        arrived, extra = tuple(turn(x, count) for x in found[-1]), ()
         if len(beside) >= d:
             run, arguments = beside[d - 1]
             extra = run(*lax.optimization_barrier((found[-1], arguments))[1])
@@ -82,35 +84,50 @@
         made.append(extra)
         found.append(arrived)
         if d < middle:
-            other.append(swap(arrived))
+            other.append(tuple(swap(x) for x in arrived))
     return found + other[1:], made[: len(beside)]
 
 
-def reduce(parts, opposite, own, side, count):
+def step(value, ahead, count):
+    cycle = cycle_of(count)
+    return lax.ppermute(value, "ctx", [(cycle[p], cycle[(p + ahead) % count]) for p in range(count)])
+
+
+def reduce(parts, count):
     middle = count // 2
-    given = {d: swap(x) for d, x in [(middle, opposite[1])] + [(d, parts[d]) for d in range(middle - 1, 0, -1)]}
-    first = turn(summed([opposite[0], given[middle]]).astype(jnp.bfloat16), count).astype(jnp.float32)
-    nothing = jnp.zeros_like(first)
-    running = jnp.concatenate([jnp.where(side == 0, first, nothing), jnp.where(side == 0, nothing, first)], axis=0)
+    first = parts[middle]().astype(jnp.bfloat16)
+    half = first.shape[0] // 2
+    zero = jnp.zeros((half, first.shape[1]), jnp.bfloat16)
+    ahead = jnp.concatenate([step(first[:half], 1, count), zero], axis=0)
+    back = jnp.concatenate([zero, step(first[half:], -1, count)], axis=0)
     for d in range(middle - 1, 0, -1):
-        total = summed([parts[middle + d], given[d]]) + running
-        if d > 1:
-            running = turn(total.astype(jnp.bfloat16), count).astype(jnp.float32)
-    left, right = jnp.split(total.astype(jnp.bfloat16), 2, axis=1)
-    near = turn(jnp.where(side == 0, left, right), count)
-    far = turn(jnp.where(side == 0, right, left), count, cross=True)
-    return summed([own[0], swap(own[1]), near, far])
-
-
-def attend_kernel(count, blocks, info, q_ref, *refs):
-    up_ref, proj_ref, out_ref, m_ref, l_ref, acc_ref = refs[-6:]
-    latents = refs[:-6]
+        ahead = step((parts[count - d]() + ahead.astype(jnp.float32)).astype(jnp.bfloat16), 1, count)
+        back = step((parts[d]() + back.astype(jnp.float32)).astype(jnp.bfloat16), -1, count)
+    return parts[0]() + ahead.astype(jnp.float32) + back.astype(jnp.float32)
+
+
+def order_of(count):
+    return [(count // 2 + (d + 1) // 2 * (1 - d % 2 * 2)) % count for d in range(count)]
+
+
+def attend_kernel(count, blocks, heads, info, *refs):
+    latents, refs = refs[: len(refs) - 14], refs[len(refs) - 14 :]
+    wanted, (out_ref, base_ref) = refs[:4], refs[4:6]
+    held, sems, (m_ref, l_ref, acc_ref) = refs[6:10], refs[10], refs[11:14]
+    q_ref, up_ref, proj_ref, residual_ref = held
+    copies = [pltpu.make_async_copy(wanted[i], held[i], sems.at[i]) for i in range(4)]
     chunk = pl.program_id(0)
     sources = lambda c: info[2 + c]
     order = lambda j: info[2 + count + j]
     segs = info.shape[0] - 2 - 3 * count
-    heads, rows, _ = q_ref.shape
+    rows = q_ref.shape[0]
     span = rows // 2
+    depth = q_ref.shape[1] // heads
+
+    @pl.when(chunk == 0)
+    def _():
+        for copy in copies:
+            copy.start()
 
     @pl.when(chunk == 0)
     def _():
@@ -138,13 +155,19 @@
     visible = (kpos >= low) & (kpos <= qpos)
 
     lat = jnp.concatenate([ref[...].reshape(-1, WIDE) for ref in latents], axis=0)
+
+    @pl.when(chunk == 0)
+    def _():
+        copies[0].wait()
+        copies[1].wait()
+
     keyval = jnp.dot(lat[:, :LAT], up_ref[...], preferred_element_type=jnp.float32).astype(jnp.bfloat16)
     rope = lat[:, LAT : LAT + ROPE]
     scale = 1.0 / math.sqrt(NOPE + ROPE)
     for h in range(heads):
         base = h * (NOPE + VHEAD)
         key = jnp.concatenate([keyval[:, base : base + NOPE], rope], axis=1)
-        scores = lax.dot_general(q_ref[h], key, (((1,), (1,)), ((), ())), preferred_element_type=jnp.float32)
+        scores = lax.dot_general(q_ref[:, h * depth : (h + 1) * depth], key, (((1,), (1,)), ((), ())), preferred_element_type=jnp.float32)
         scores = jnp.where(visible, scores * scale, -1e30)
         best = m_ref[h]
         fresh = jnp.maximum(best, jnp.max(scores, axis=1, keepdims=True))
@@ -160,35 +183,43 @@
     @pl.when(chunk == pl.num_programs(0) - 1)
     def _():
         attended = [(acc_ref[h] / l_ref[h]).astype(jnp.bfloat16) for h in range(heads)]
+        copies[2].wait()
+        copies[3].wait()
         out = jnp.dot(jnp.concatenate(attended, axis=1), proj_ref[...], preferred_element_type=jnp.float32)
-        out_ref[...] = out.astype(jnp.bfloat16)
-
-
-def attend(info, q, found, kv_up, out_proj, count):
-    heads, rows, depth = q.shape
+        out = out.astype(jnp.bfloat16)
+        out_ref[...] = out
+        base_ref[...] = residual_ref[...].astype(jnp.float32) + out.astype(jnp.float32)
+
+
+def attend(info, found, queries, kv_up, out_proj, residual, count):
+    rows, width = residual.shape
+    heads = kv_up.shape[1] // (NOPE + VHEAD)
     blocks = math.gcd(count, 8)
     whole = pl.BlockSpec(memory_space=pltpu.VMEM)
     if blocks == count:
         latents, lat_spec = found, whole
     else:
         latents, lat_spec = [jnp.stack(found)], pl.BlockSpec((blocks, rows, WIDE), lambda i, *_: (i, 0, 0))
+    wanted = (queries, kv_up, out_proj, residual)
     return pl.pallas_call(
-        functools.partial(attend_kernel, count, blocks),
+        functools.partial(attend_kernel, count, blocks, heads),
         grid_spec=pltpu.PrefetchScalarGridSpec(
             num_scalar_prefetch=1,
             grid=(count // blocks,),
-            in_specs=[whole] + [lat_spec] * len(latents) + [whole, whole],
-            out_specs=whole,
-            scratch_shapes=[
+            in_specs=[lat_spec] * len(latents) + [pl.BlockSpec(memory_space=pltpu.HBM)] * 4,
+            out_specs=[whole, whole],
+            scratch_shapes=[pltpu.VMEM(x.shape, x.dtype) for x in wanted]
+            + [
+                pltpu.SemaphoreType.DMA((4,)),
                 pltpu.VMEM((heads, rows, 1), jnp.float32),
                 pltpu.VMEM((heads, rows, 1), jnp.float32),
                 pltpu.VMEM((heads, rows, VHEAD), jnp.float32),
             ],
         ),
-        out_shape=pltpu.VMEM((rows, out_proj.shape[1]), jnp.bfloat16),
+        out_shape=[pltpu.VMEM((rows, width), jnp.bfloat16), pltpu.VMEM((rows, width), jnp.float32)],
         compiler_params=pltpu.CompilerParams(vmem_limit_bytes=28 * MIB),
         name="attend",
-    )(info, q, *latents, kv_up, out_proj)
+    )(info, *latents, *(pltpu.with_memory_space_constraint(x, pltpu.HBM) for x in wanted))
 
 
 def route_kernel(count, where, *refs):
@@ -224,56 +255,30 @@
     )(where, *found)
 
 
-def stage_kernel(picks, *refs):
-    here = len(picks)
-    sems = refs[2 * here]
-    copies = []
-    for i, pick in enumerate(picks):
-        source = refs[i] if pick is None else refs[i].at[pick]
-        piece = source.shape[0] // PIECES
-        for p in range(PIECES):
-            rows = pl.ds(p * piece, piece)
-            copies.append(pltpu.make_async_copy(source.at[rows], refs[here + i].at[rows], sems.at[i, p]))
-    for copy in copies:
-        copy.start()
-    for copy in copies:
-        copy.wait()
-
-
-def stage(arrays, picks):
-    shapes = [x.shape if pick is None else x.shape[1:] for x, pick in zip(arrays, picks)]
-    return pl.pallas_call(
-        functools.partial(stage_kernel, picks),
-        in_specs=[pl.BlockSpec(memory_space=pltpu.HBM)] * len(arrays),
-        out_specs=[pl.BlockSpec(memory_space=pltpu.VMEM)] * len(arrays),
-        scratch_shapes=[pltpu.SemaphoreType.DMA((len(arrays), PIECES))],
-        out_shape=[pltpu.VMEM(shape, x.dtype) for shape, x in zip(shapes, arrays)],
-        compiler_params=pltpu.CompilerParams(vmem_limit_bytes=2 * MIB),
-        name="stage",
-    )(*(pltpu.with_memory_space_constraint(x, pltpu.HBM) for x in arrays))
-
-
-def norm_kernel(where, residual_ref, here_ref, there_ref, gain_ref, middle_ref, normed_ref):
+def norm_kernel(where, base_ref, there_ref, gain_ref, middle_ref, *normed_refs):
     half = middle_ref.shape[1]
-    total = here_ref[...].astype(jnp.float32) + there_ref[...].astype(jnp.float32)
-    middle = (residual_ref[...].astype(jnp.float32) + total).astype(jnp.bfloat16)
+    middle = (base_ref[...] + there_ref[...].astype(jnp.float32)).astype(jnp.bfloat16)
     wide = middle.astype(jnp.float32)
     inverse = lax.rsqrt(jnp.mean(wide * wide, axis=1, keepdims=True) + 1e-06)
-    normed_ref[...] = (wide * inverse * gain_ref[...].astype(jnp.float32)).astype(jnp.bfloat16)
+    normed = (wide * inverse * gain_ref[...].astype(jnp.float32)).astype(jnp.bfloat16)
+    part = normed_refs[0].shape[1]
+    for h, ref in enumerate(normed_refs):
+        ref[...] = normed[:, h * part : (h + 1) * part]
     middle_ref[...] = jnp.where(where[1] == 0, wide[:, :half], wide[:, half:]).astype(jnp.bfloat16)
 
 
-def norm(where, residual, here, there, gain):
-    rows, width = residual.shape
+def norm(where, base, there, gain):
+    rows, width = base.shape
     whole = pl.BlockSpec(memory_space=pltpu.VMEM)
+    shapes = [(rows, width // 2)] + [(rows, width // PARTS)] * PARTS
     return pl.pallas_call(
         norm_kernel,
-        in_specs=[pl.BlockSpec(memory_space=pltpu.SMEM)] + [whole] * 4,
-        out_specs=[whole] * 2,
-        out_shape=[pltpu.VMEM(shape, jnp.bfloat16) for shape in ((rows, width // 2), (rows, width))],
+        in_specs=[pl.BlockSpec(memory_space=pltpu.SMEM)] + [whole] * 3,
+        out_specs=[whole] * len(shapes),
+        out_shape=[pltpu.VMEM(shape, jnp.bfloat16) for shape in shapes],
         compiler_params=pltpu.CompilerParams(vmem_limit_bytes=12 * MIB),
         name="norm",
-    )(where, residual, here, there, gain)
+    )(where, base, there, gain)
 
 
 def pack_kernel(*refs):
@@ -323,8 +328,10 @@
 
 
 def fused_kernel(count, where, *refs):
-    blocks, combine_ref, weights = refs[:count], refs[count], refs[count + 1 : count + 4]
-    outs, at = refs[count + 4 : 2 * count + 6], 2 * count + 6
+    at = PARTS * count
+    blocks, combine_ref, weights = refs[:at], refs[at], refs[at + 1 : at + 4]
+    kept, away = refs[at + 4 : at + 4 + count], refs[at + 4 + count : at + 4 + 2 * count]
+    at += 4 + 2 * count
     picked, buffers, sems = refs[at], refs[at + 1 : at + 4], refs[at + 4]
     here = picked.shape[0]
     depth, units, width = buffers[0].shape
@@ -345,9 +352,12 @@
 
     for c in range(count):
         pick = (combine_ref[c].astype(jnp.float32) > 0).astype(jnp.float32).astype(jnp.bfloat16)
-        rows = lax.dot_general(pick, blocks[c][...], by_rows, preferred_element_type=jnp.float32).astype(jnp.bfloat16)
-        for e in range(here):
-            picked[e, c * SLOTS : (c + 1) * SLOTS] = rows[e * SLOTS : (e + 1) * SLOTS]
+        for h in range(PARTS):
+            block = blocks[PARTS * c + h][...]
+            rows = lax.dot_general(pick, block, by_rows, preferred_element_type=jnp.float32).astype(jnp.bfloat16)
+            columns = pl.ds(h * block.shape[1], block.shape[1])
+            for e in range(here):
+                picked[e, c * SLOTS : (c + 1) * SLOTS, columns] = rows[e * SLOTS : (e + 1) * SLOTS]
 
     def work(expert, _):
         slot = lax.rem(expert, depth)
@@ -364,22 +374,16 @@
 
     lax.fori_loop(0, here, work, 0)
 
-    def total(c):
-        rows = jnp.concatenate([picked[e, c * SLOTS : (c + 1) * SLOTS] for e in range(here)], axis=0)
-        return jnp.dot(combine_ref[c], rows, preferred_element_type=jnp.float32).astype(jnp.bfloat16)
-
-    result = total(middle)
-    half = result.shape[0] // 2
-    upper, lower = result[:half], result[half:]
-    outs[0][...] = jnp.where(side == 0, upper, lower)
-    outs[1][...] = jnp.where(side == 0, lower, upper)
-    result = total(0)
-    left, right = result[:, : width // 2], result[:, width // 2 :]
-    outs[2][...] = jnp.where(side == 0, left, right)
-    outs[3][...] = jnp.where(side == 0, right, left)
-    rest = [c for c in range(count) if c not in (0, middle)]
-    for i, c in enumerate(rest):
-        outs[4 + i][...] = total(c)
+    half = width // 2
+    for d in order_of(count):
+        forward = d if d <= middle else middle + count - d
+        backward = forward if d in (0, middle) else (count - d if d > middle else middle + d)
+        c = forward if forward == backward else jnp.where(side == 0, forward, backward)
+        place = pl.ds(c * SLOTS if forward == backward else pl.multiple_of(c * SLOTS, SLOTS), SLOTS)
+        for turned, out in ((1 - side, away[d]), (side, kept[d])):
+            columns = pl.ds(pl.multiple_of(turned * half, half), half)
+            rows = jnp.concatenate([picked[e, place, columns] for e in range(here)], axis=0)
+            out[...] = jnp.dot(combine_ref[c], rows, preferred_element_type=jnp.float32).astype(jnp.bfloat16)
 
 
 def expert_specs(w_gate):
@@ -405,28 +409,26 @@
 
 
 def experts_fused(where, found, combine, w_gate, w_up, w_down):
-    count, (local, width) = len(found), found[0].shape
-    here, units, _ = w_gate.shape
+    count, local = len(found), found[0][0].shape[0]
+    here, units, width = w_gate.shape
     rows = count * SLOTS
     depth = min(DEPTH, here)
-    middle = count // 2
     whole = pl.BlockSpec(memory_space=pltpu.VMEM)
-    shapes = [(local // 2, width)] * 2 + [(local, width // 2)] * 2 + [(local, width)] * (count - 2)
     outs = pl.pallas_call(
         functools.partial(fused_kernel, count),
         in_specs=[pl.BlockSpec(memory_space=pltpu.SMEM)]
-        + [whole] * (count + 1)
+        + [whole] * (PARTS * count + 1)
         + [pl.BlockSpec(memory_space=pltpu.HBM)] * 3,
-        out_specs=[whole] * len(shapes),
+        out_specs=[whole] * (2 * count),
         scratch_shapes=[pltpu.VMEM((here, rows, width), jnp.bfloat16)]
         + [pltpu.VMEM((depth, units, width), jnp.bfloat16)] * 3
         + [pltpu.SemaphoreType.DMA((depth, 3, PIECES))],
-        out_shape=[pltpu.VMEM(shape, jnp.bfloat16) for shape in shapes],
+        out_shape=[pltpu.VMEM((local, width // 2), jnp.bfloat16)] * (2 * count),
         compiler_params=pltpu.CompilerParams(vmem_limit_bytes=36 * MIB),
         name="experts",
-    )(where, *found, combine, *(pltpu.with_memory_space_constraint(w, pltpu.HBM) for w in (w_gate, w_up, w_down)))
-    rest = [c for c in range(count) if c not in (0, middle)]
-    return dict(zip(rest, outs[4:])), outs[:2], outs[2:4]
+    )(where, *(x for block in found for x in block), combine,
+      *(pltpu.with_memory_space_constraint(w, pltpu.HBM) for w in (w_gate, w_up, w_down)))
+    return outs[:count], outs[count:]
 
 
 def body(
@@ -446,7 +448,6 @@
 ):
     local_rows, width = residual.shape
     span = local_rows // 2
-    heads = kv_up.shape[1] // (NOPE + VHEAD)
     count = lax.axis_size("ctx")
     here = EXPERTS // count
     me, side = lax.axis_index("ctx"), lax.axis_index("exp")
@@ -456,18 +457,12 @@
     w_gate, w_up = w_gate.transpose(0, 2, 1), w_up.transpose(0, 2, 1)
     packed = pack(latent, expert_ids, route_weights)
     few = count <= FEW
-    bring = lambda *arrays: stage(arrays, (None,) * len(arrays)) if few else arrays
-    arrange = lambda x: x.reshape(local_rows, heads, NOPE + ROPE).transpose(1, 0, 2)
     scalars = lambda *arrays: jnp.concatenate([where, sources_of(me, side, count), *arrays])
-    beside = [
-        (arrange, (queries,)),
-        (bring, (kv_up, out_proj, residual)),
-        (lambda gain, *arrays: (gain.reshape(1, width), scalars(*arrays)), (norm_gain, span_order, seg_lengths)),
-    ]
-    found, made = gather(packed, count, beside)
-    q, (kv_up, out_proj, residual), (gain, info) = made
-    partial = attend(info, q, found, kv_up, out_proj, count)
-    middle, normed = norm(where, residual, partial, swap(partial), gain)
+    beside = [(scalars, (span_order, seg_lengths)), (lambda gain: gain.reshape(1, width), (norm_gain,))]
+    found, (info, gain) = gather([packed], count, beside)
+    found = [block for block, in found]
+    partial, summand = attend(info, found, queries, kv_up, out_proj, residual, count)
+    middle, *normed = norm(where, summand, swap(partial), gain)
 
     def place_rows(*blocks):
         if few:
@@ -486,11 +481,14 @@
 
     got, (combine,) = gather(normed, count, [(place_rows, tuple(found))])
     if few:
-        parts, opposite, own = experts_fused(where, got, combine, w_gate, w_up, w_down)
-        mixture = reduce(parts, opposite, own, side, count)
+        kept, away = experts_fused(where, got, combine, w_gate, w_up, w_down)
+        swapped = {d: swap(away[d]) for d in order_of(count)}
+        parts = [functools.partial(summed, [kept[d], swapped[d]]) for d in range(count)]
+        mixture = reduce(parts, count)
     else:
         pick = (combine > 0).astype(jnp.bfloat16)
-        picked = jnp.einsum("cts,ctd->csd", pick, jnp.stack(got), preferred_element_type=jnp.float32).astype(jnp.bfloat16)
+        rows = jnp.stack([jnp.concatenate(block, axis=1) for block in got])
+        picked = jnp.einsum("cts,ctd->csd", pick, rows, preferred_element_type=jnp.float32).astype(jnp.bfloat16)
         picked = picked.reshape(count, here, SLOTS, width).transpose(1, 0, 2, 3).reshape(here, count * SLOTS, width)
         result = experts_plain(where, picked, w_gate, w_up, w_down)
         result = result.reshape(here, count, SLOTS, width).transpose(1, 0, 2, 3).reshape(count, here * SLOTS, width)

time: 139 us -> 129 us (0.928)
  starting transfers between devices: 22.5 us -> 32.5 us
  waiting for transfers between devices: 64.5 us -> 56.8 us
  local copies, waits for them, and re-layouts: 8.45 us -> 2.15 us
  Pallas kernels: 39 us -> 35.2 us
  other arithmetic: 3.84 us -> 1.73 us
    ppermute x13 -> x12, waiting for transfers between devices: 60.3 us -> 31.9 us  [turn(): return lax.ppermute(value, ('ctx', 'exp'), pairs)]
    ppermute x0 -> x8, waiting for transfers between devices: none -> 22 us  [step(): lax.ppermute(value, 'ctx', [(cycle[p], cycle[(p + ahead) % count]) for p...]
    ppermute x0 -> x8, starting transfers between devices: none -> 7.64 us  [step(): lax.ppermute(value, 'ctx', [(cycle[p], cycle[(p + ahead) % count]) for p...]
    unnamed x14 -> x0, local copies, waits for them, and re-layouts: 4.38 us -> none
    pallas_call x2 -> x1, Pallas kernels: 7.62 us -> 5.86 us  [attend(): pl.pallas_call(functools.partial(attend_kernel, count, blocks, heads), gr...]
    ppermute x12 -> x18, starting transfers between devices: 0.96 us -> 2.55 us  [swap(): return lax.ppermute(value, 'exp', SWAP)]
    ppermute x12 -> x18, waiting for transfers between devices: 4.19 us -> 2.89 us  [swap(): return lax.ppermute(value, 'exp', SWAP)]
    ppermute x13 -> x12, starting transfers between devices: 21.5 us -> 22.3 us  [turn(): return lax.ppermute(value, ('ctx', 'exp'), pairs)]
  transfers between devices with their start and end apart: 25 -> 38, of which waited for: 17 -> 22; matrix products, arithmetic and copies ran while one was open for 5% -> 2% of each run, Pallas kernels for 3% -> 1%
where the time goes in v10:
time: 129 us
  waiting for transfers between devices  56.8 us (44%)
  Pallas kernels  35.2 us (27%)
  starting transfers between devices  32.5 us (25%)
  local copies, waits for them, and re-layouts  2.15 us (2%)
  other arithmetic  1.73 us (1%)
    ppermute x12, waiting for transfers between devices, turn(): return lax.ppermute(value, ('ctx', 'exp'), pairs)  31.9 us
    pallas_call x1, Pallas kernels, experts_fused(): pl.pallas_call(functools.partial(fused_kernel, count), in_specs=[pl.Block...  25.5 us
    ppermute x12, starting transfers between devices, turn(): return lax.ppermute(value, ('ctx', 'exp'), pairs)  22.3 us
    ppermute x8, waiting for transfers between devices, step(): lax.ppermute(value, 'ctx', [(cycle[p], cycle[(p + ahead) % count]) for p...  22 us
    ppermute x8, starting transfers between devices, step(): lax.ppermute(value, 'ctx', [(cycle[p], cycle[(p + ahead) % count]) for p...  7.64 us
    pallas_call x1, Pallas kernels, attend(): pl.pallas_call(functools.partial(attend_kernel, count, blocks, heads), gr...  5.86 us
    ppermute x18, waiting for transfers between devices, swap(): return lax.ppermute(value, 'exp', SWAP)  2.89 us
  transfers between devices with their start and end apart: 38, of which 22 were waited for; matrix products, arithmetic and copies ran while one was open for 2% of the time, Pallas kernels for 1%

profile of v10, /device:TPU:0, one launch (start us, length us, event | category | flops | bytes accessed | tf_op | source)
XLA Modules:
  0.0 128.5 jit_solution(5903032529734493954)
XLA Ops:
  0.0 1.1 pack.1.refs_0_
  1.1 3.0 %collective-permute-start = (bf16[128,640]{1,0:T(8,128)(2,1)S(1)}, bf16[128,640]{1,0:T(8,128)(2,1)S(1)}, u32[]{:S(2)}, u32[]{:S(2)}) collective-permute-start(bf16[128,640]{1,0:T(8,128)(2,1)S(1)} %pack.1.refs_0_), channel_id=1, source_target_pairs={{0,2},{1,5},{2,6},{3,1},{6,10},{7,3},{10,14},{11,7},{14,12},{15,11... | collective-permute-start | bytes 491528 | tf_op jit(solution)/shard_map/ppermute | solution.py:49
  4.2 0.7 dynamic-slice_bitcast_fusion
  4.9 0.7 concatenate.10.info
  5.6 1.9 %collective-permute-done.refs_1_ = bf16[128,640]{1,0:T(8,128)(2,1)S(1)} collective-permute-done((bf16[128,640]{1,0:T(8,128)(2,1)S(1)}, bf16[128,640]{1,0:T(8,128)(2,1)S(1)}, u32[]{:S(2)}, u32[]{:S(2)}) %collective-permute-start) | collective-permute-done | bytes 163872 | tf_op jit(solution)/shard_map/ppermute | solution.py:49
  7.5 2.0 %collective-permute-start.1 = (bf16[128,640]{1,0:T(8,128)(2,1)S(1)}, bf16[128,640]{1,0:T(8,128)(2,1)S(1)}, u32[]{:S(2)}, u32[]{:S(2)}) collective-permute-start(bf16[128,640]{1,0:T(8,128)(2,1)S(1)} %collective-permute-done.refs_1_), channel_id=1, source_target_pairs={{0,2},{1,5},{2,6},{3,1},{6,10},{7,3},{10,14},{11,7},{14,12},{15,11... | collective-permute-start | bytes 491528 | tf_op jit(solution)/shard_map/ppermute | solution.py:49
  9.5 0.7 reshape.3.gain_ref
  10.2 2.7 %collective-permute-done.1.refs_2_ = bf16[128,640]{1,0:T(8,128)(2,1)S(1)} collective-permute-done((bf16[128,640]{1,0:T(8,128)(2,1)S(1)}, bf16[128,640]{1,0:T(8,128)(2,1)S(1)}, u32[]{:S(2)}, u32[]{:S(2)}) %collective-permute-start.1) | collective-permute-done | bytes 163872 | tf_op jit(solution)/shard_map/ppermute | solution.py:49
  12.9 2.0 %collective-permute-start.3 = (bf16[128,640]{1,0:T(8,128)(2,1)S(1)}, bf16[128,640]{1,0:T(8,128)(2,1)S(1)}, u32[]{:S(2)}, u32[]{:S(2)}) collective-permute-start(bf16[128,640]{1,0:T(8,128)(2,1)S(1)} %collective-permute-done.1.refs_2_), channel_id=1, source_target_pairs={{0,2},{1,5},{2,6},{3,1},{6,10},{7,3},{10,14},{11,7},{14,12},{15,11... | collective-permute-start | bytes 491528 | tf_op jit(solution)/shard_map/ppermute | solution.py:49
  14.8 3.4 %collective-permute-done.3.refs_3_ = bf16[128,640]{1,0:T(8,128)(2,1)S(1)} collective-permute-done((bf16[128,640]{1,0:T(8,128)(2,1)S(1)}, bf16[128,640]{1,0:T(8,128)(2,1)S(1)}, u32[]{:S(2)}, u32[]{:S(2)}) %collective-permute-start.3) | collective-permute-done | bytes 163872 | tf_op jit(solution)/shard_map/ppermute | solution.py:49
  18.2 2.0 %collective-permute-start.5 = (bf16[128,640]{1,0:T(8,128)(2,1)S(1)}, bf16[128,640]{1,0:T(8,128)(2,1)S(1)}, u32[]{:S(2)}, u32[]{:S(2)}) collective-permute-start(bf16[128,640]{1,0:T(8,128)(2,1)S(1)} %collective-permute-done.3.refs_3_), channel_id=1, source_target_pairs={{0,2},{1,5},{2,6},{3,1},{6,10},{7,3},{10,14},{11,7},{14,12},{15,11... | collective-permute-start | bytes 491528 | tf_op jit(solution)/shard_map/ppermute | solution.py:49
  20.1 3.4 %collective-permute-done.5.refs_4_ = bf16[128,640]{1,0:T(8,128)(2,1)S(1)} collective-permute-done((bf16[128,640]{1,0:T(8,128)(2,1)S(1)}, bf16[128,640]{1,0:T(8,128)(2,1)S(1)}, u32[]{:S(2)}, u32[]{:S(2)}) %collective-permute-start.5) | collective-permute-done | bytes 163872 | tf_op jit(solution)/shard_map/ppermute | solution.py:49
  23.5 5.9 %attend.1 = (bf16[128,2048]{1,0:T(8,128)(2,1)S(1)}, f32[128,2048]{1,0:T(8,128)S(1)}) custom-call(s32[42]{0:T(128)S(1)} %concatenate.10.info, bf16[128,640]{1,0:T(8,128)(2,1)S(1)} %pack.1.refs_0_, bf16[128,640]{1,0:T(8,128)(2,1)S(1)} %collective-permute-done.refs_1_, bf16[128,640]{1,0:T(8,128)(2,1)S(1)} %collective-permute-done.1.refs_2_, ...), custom_call_target="tpu_custom_call" | custom-call | tf_op jit(solution)/shard_map/attend/pallas_call | solution.py:204
  29.5 1.8 %collective-permute-done.7.there_ref = bf16[128,2048]{1,0:T(8,128)(2,1)S(1)} collective-permute-done((bf16[128,2048]{1,0:T(8,128)(2,1)S(1)}, bf16[128,2048]{1,0:T(8,128)(2,1)S(1)}, u32[]{:S(2)}, u32[]{:S(2)}) %collective-permute-start.7) | collective-permute-done | bytes 524320 | tf_op jit(solution)/shard_map/ppermute | solution.py:40
  31.3 0.9 norm.1
  32.2 2.0 %collective-permute-start.8 = (bf16[128,1024]{1,0:T(8,128)(2,1)S(1)}, bf16[128,1024]{1,0:T(8,128)(2,1)S(1)}, u32[]{:S(2)}, u32[]{:S(2)}) collective-permute-start(bf16[128,1024]{1,0:T(8,128)(2,1)S(1)} %get-tuple-element.76.refs_0_), channel_id=1, source_target_pairs={{0,2},{1,5},{2,6},{3,1},{6,10},{7,3},{10,14},{11,7},{14,12},{15,11... | collective-permute-start | bytes 786440 | tf_op jit(solution)/shard_map/ppermute | solution.py:49
  34.2 1.6 %collective-permute-start.9 = (bf16[128,1024]{1,0:T(8,128)(2,1)S(1)}, bf16[128,1024]{1,0:T(8,128)(2,1)S(1)}, u32[]{:S(2)}, u32[]{:S(2)}) collective-permute-start(bf16[128,1024]{1,0:T(8,128)(2,1)S(1)} %get-tuple-element.77.refs_1_), channel_id=1, source_target_pairs={{0,2},{1,5},{2,6},{3,1},{6,10},{7,3},{10,14},{11,7},{14,12},{15,11... | collective-permute-start | bytes 786440 | tf_op jit(solution)/shard_map/ppermute | solution.py:49
  35.8 1.8 %route.1.refs_16_ = bf16[8,128,128]{2,1,0:T(8,128)(2,1)S(1)} custom-call(s32[2]{0:T(128)S(1)} %pad_add_fusion.where, bf16[128,640]{1,0:T(8,128)(2,1)S(1)} %pack.1.refs_0_, bf16[128,640]{1,0:T(8,128)(2,1)S(1)} %collective-permute-done.refs_1_, bf16[128,640]{1,0:T(8,128)(2,1)S(1)} %collective-permute-done.1.refs_2_, ...), custom_call_target="tpu_custom_call" | custom-call | tf_op jit(solution)/shard_map/route/pallas_call | solution.py:248
  37.7 1.0 collective-permute-done.8.refs_2_
  38.6 2.8 %collective-permute-done.9.refs_3_ = bf16[128,1024]{1,0:T(8,128)(2,1)S(1)} collective-permute-done((bf16[128,1024]{1,0:T(8,128)(2,1)S(1)}, bf16[128,1024]{1,0:T(8,128)(2,1)S(1)}, u32[]{:S(2)}, u32[]{:S(2)}) %collective-permute-start.9) | collective-permute-done | bytes 262176 | tf_op jit(solution)/shard_map/ppermute | solution.py:49
  41.5 2.0 %collective-permute-start.10 = (bf16[128,1024]{1,0:T(8,128)(2,1)S(1)}, bf16[128,1024]{1,0:T(8,128)(2,1)S(1)}, u32[]{:S(2)}, u32[]{:S(2)}) collective-permute-start(bf16[128,1024]{1,0:T(8,128)(2,1)S(1)} %collective-permute-done.8.refs_2_), channel_id=1, source_target_pairs={{0,2},{1,5},{2,6},{3,1},{6,10},{7,3},{10,14},{11,7},{14,12},{15,11... | collective-permute-start | bytes 786440 | tf_op jit(solution)/shard_map/ppermute | solution.py:49
  43.7 1.3 %collective-permute-start.11 = (bf16[128,1024]{1,0:T(8,128)(2,1)S(1)}, bf16[128,1024]{1,0:T(8,128)(2,1)S(1)}, u32[]{:S(2)}, u32[]{:S(2)}) collective-permute-start(bf16[128,1024]{1,0:T(8,128)(2,1)S(1)} %collective-permute-done.9.refs_3_), channel_id=1, source_target_pairs={{0,2},{1,5},{2,6},{3,1},{6,10},{7,3},{10,14},{11,7},{14,12},{15,11... | collective-permute-start | bytes 786440 | tf_op jit(solution)/shard_map/ppermute | solution.py:49
  45.0 2.8 %collective-permute-done.10.refs_4_ = bf16[128,1024]{1,0:T(8,128)(2,1)S(1)} collective-permute-done((bf16[128,1024]{1,0:T(8,128)(2,1)S(1)}, bf16[128,1024]{1,0:T(8,128)(2,1)S(1)}, u32[]{:S(2)}, u32[]{:S(2)}) %collective-permute-start.10) | collective-permute-done | bytes 262176 | tf_op jit(solution)/shard_map/ppermute | solution.py:49
  47.8 2.8 %collective-permute-done.11.refs_5_ = bf16[128,1024]{1,0:T(8,128)(2,1)S(1)} collective-permute-done((bf16[128,1024]{1,0:T(8,128)(2,1)S(1)}, bf16[128,1024]{1,0:T(8,128)(2,1)S(1)}, u32[]{:S(2)}, u32[]{:S(2)}) %collective-permute-start.11) | collective-permute-done | bytes 262176 | tf_op jit(solution)/shard_map/ppermute | solution.py:49
  50.6 2.0 %collective-permute-start.14 = (bf16[128,1024]{1,0:T(8,128)(2,1)S(1)}, bf16[128,1024]{1,0:T(8,128)(2,1)S(1)}, u32[]{:S(2)}, u32[]{:S(2)}) collective-permute-start(bf16[128,1024]{1,0:T(8,128)(2,1)S(1)} %collective-permute-done.10.refs_4_), channel_id=1, source_target_pairs={{0,2},{1,5},{2,6},{3,1},{6,10},{7,3},{10,14},{11,7},{14,12},{15,11... | collective-permute-start | bytes 786440 | tf_op jit(solution)/shard_map/ppermute | solution.py:49
  52.9 1.3 %collective-permute-start.15 = (bf16[128,1024]{1,0:T(8,128)(2,1)S(1)}, bf16[128,1024]{1,0:T(8,128)(2,1)S(1)}, u32[]{:S(2)}, u32[]{:S(2)}) collective-permute-start(bf16[128,1024]{1,0:T(8,128)(2,1)S(1)} %collective-permute-done.11.refs_5_), channel_id=1, source_target_pairs={{0,2},{1,5},{2,6},{3,1},{6,10},{7,3},{10,14},{11,7},{14,12},{15,11... | collective-permute-start | bytes 786440 | tf_op jit(solution)/shard_map/ppermute | solution.py:49
  54.2 2.8 %collective-permute-done.14.refs_6_ = bf16[128,1024]{1,0:T(8,128)(2,1)S(1)} collective-permute-done((bf16[128,1024]{1,0:T(8,128)(2,1)S(1)}, bf16[128,1024]{1,0:T(8,128)(2,1)S(1)}, u32[]{:S(2)}, u32[]{:S(2)}) %collective-permute-start.14) | collective-permute-done | bytes 262176 | tf_op jit(solution)/shard_map/ppermute | solution.py:49
  57.0 2.8 %collective-permute-done.15.refs_7_ = bf16[128,1024]{1,0:T(8,128)(2,1)S(1)} collective-permute-done((bf16[128,1024]{1,0:T(8,128)(2,1)S(1)}, bf16[128,1024]{1,0:T(8,128)(2,1)S(1)}, u32[]{:S(2)}, u32[]{:S(2)}) %collective-permute-start.15) | collective-permute-done | bytes 262176 | tf_op jit(solution)/shard_map/ppermute | solution.py:49
  59.8 2.0 %collective-permute-start.18 = (bf16[128,1024]{1,0:T(8,128)(2,1)S(1)}, bf16[128,1024]{1,0:T(8,128)(2,1)S(1)}, u32[]{:S(2)}, u32[]{:S(2)}) collective-permute-start(bf16[128,1024]{1,0:T(8,128)(2,1)S(1)} %collective-permute-done.14.refs_6_), channel_id=1, source_target_pairs={{0,2},{1,5},{2,6},{3,1},{6,10},{7,3},{10,14},{11,7},{14,12},{15,11... | collective-permute-start | bytes 786440 | tf_op jit(solution)/shard_map/ppermute | solution.py:49
  62.1 1.3 %collective-permute-start.19 = (bf16[128,1024]{1,0:T(8,128)(2,1)S(1)}, bf16[128,1024]{1,0:T(8,128)(2,1)S(1)}, u32[]{:S(2)}, u32[]{:S(2)}) collective-permute-start(bf16[128,1024]{1,0:T(8,128)(2,1)S(1)} %collective-permute-done.15.refs_7_), channel_id=1, source_target_pairs={{0,2},{1,5},{2,6},{3,1},{6,10},{7,3},{10,14},{11,7},{14,12},{15,11... | collective-permute-start | bytes 786440 | tf_op jit(solution)/shard_map/ppermute | solution.py:49
  63.4 2.8 %collective-permute-done.18.refs_8_ = bf16[128,1024]{1,0:T(8,128)(2,1)S(1)} collective-permute-done((bf16[128,1024]{1,0:T(8,128)(2,1)S(1)}, bf16[128,1024]{1,0:T(8,128)(2,1)S(1)}, u32[]{:S(2)}, u32[]{:S(2)}) %collective-permute-start.18) | collective-permute-done | bytes 262176 | tf_op jit(solution)/shard_map/ppermute | solution.py:49
  66.2 2.8 %collective-permute-done.19.refs_9_ = bf16[128,1024]{1,0:T(8,128)(2,1)S(1)} collective-permute-done((bf16[128,1024]{1,0:T(8,128)(2,1)S(1)}, bf16[128,1024]{1,0:T(8,128)(2,1)S(1)}, u32[]{:S(2)}, u32[]{:S(2)}) %collective-permute-start.19) | collective-permute-done | bytes 262176 | tf_op jit(solution)/shard_map/ppermute | solution.py:49
  69.0 25.5 %experts.1 = (bf16[128,1024]{1,0:T(8,128)(2,1)S(1)}, bf16[128,1024]{1,0:T(8,128)(2,1)S(1)}, bf16[128,1024]{1,0:T(8,128)(2,1)S(1)}, bf16[128,1024]{1,0:T(8,128)(2...) custom-call(s32[2]{0:T(128)S(1)} %pad_add_fusion.where, ...), custom_call_target="tpu_custom_call" | custom-call | tf_op jit(solution)/shard_map/experts/pallas_call | solution.py:417
  94.6 0.5 collective-permute-start.25
  95.1 1.0 collective-permute-done.26
  96.2 2.0 %collective-permute-start.27 = (bf16[64,1024]{1,0:T(8,128)(2,1)S(1)}, bf16[64,1024]{1,0:T(8,128)(2,1)S(1)}, u32[]{:S(2)}, u32[]{:S(2)}) collective-permute-start(bf16[64,1024]{1,0:T(8,128)(2,1)S(1)} %get-tuple-element.117), channel_id=1, source_target_pairs={{0,2},{2,6},{6,10},{10,14},{14,12},{12,8},{8,4},{4,0},{1,3},{3,7},... | collective-permute-start | bytes 393224 | tf_op jit(solution)/shard_map/ppermute | solution.py:93
  98.2 0.5 collective-permute-start.24
  98.8 3.2 %collective-permute-done.27 = bf16[64,1024]{1,0:T(8,128)(2,1)S(1)} collective-permute-done((bf16[64,1024]{1,0:T(8,128)(2,1)S(1)}, bf16[64,1024]{1,0:T(8,128)(2,1)S(1)}, u32[]{:S(2)}, u32[]{:S(2)}) %collective-permute-start.27) | collective-permute-done | bytes 131104 | tf_op jit(solution)/shard_map/ppermute | solution.py:93
  102.1 1.7 %collective-permute-start.28 = (bf16[128,1024]{1,0:T(8,128)(2,1)S(1)}, bf16[128,1024]{1,0:T(8,128)(2,1)S(1)}, u32[]{:S(2)}, u32[]{:S(2)}) collective-permute-start(bf16[128,1024]{1,0:T(8,128)(2,1)S(1)} %add_convert_fusion.6), channel_id=1, source_target_pairs={{0,2},{2,6},{6,10},{10,14},{14,12},{12,8},{8,4},{4,0},{1,3},{3,7},... | collective-permute-start | bytes 786440 | tf_op jit(solution)/shard_map/ppermute | solution.py:93
  105.1 4.9 %collective-permute-done.28 = bf16[128,1024]{1,0:T(8,128)(2,1)S(1)} collective-permute-done((bf16[128,1024]{1,0:T(8,128)(2,1)S(1)}, bf16[128,1024]{1,0:T(8,128)(2,1)S(1)}, u32[]{:S(2)}, u32[]{:S(2)}) %collective-permute-start.28) | collective-permute-done | bytes 262176 | tf_op jit(solution)/shard_map/ppermute | solution.py:93
  110.1 1.4 %collective-permute-start.29 = (bf16[128,1024]{1,0:T(8,128)(2,1)S(1)}, bf16[128,1024]{1,0:T(8,128)(2,1)S(1)}, u32[]{:S(2)}, u32[]{:S(2)}) collective-permute-start(bf16[128,1024]{1,0:T(8,128)(2,1)S(1)} %add_convert_fusion.5), channel_id=1, source_target_pairs={{0,2},{2,6},{6,10},{10,14},{14,12},{12,8},{8,4},{4,0},{1,3},{3,7},... | collective-permute-start | bytes 786440 | tf_op jit(solution)/shard_map/ppermute | solution.py:93
  111.6 1.2 collective-permute-done.35
  113.3 3.8 %collective-permute-done.29 = bf16[128,1024]{1,0:T(8,128)(2,1)S(1)} collective-permute-done((bf16[128,1024]{1,0:T(8,128)(2,1)S(1)}, bf16[128,1024]{1,0:T(8,128)(2,1)S(1)}, u32[]{:S(2)}, u32[]{:S(2)}) %collective-permute-start.29) | collective-permute-done | bytes 262176 | tf_op jit(solution)/shard_map/ppermute | solution.py:93
  117.2 1.1 collective-permute-start.30
  118.4 2.3 %collective-permute-done.36 = bf16[128,1024]{1,0:T(8,128)(2,1)S(1)} collective-permute-done((bf16[128,1024]{1,0:T(8,128)(2,1)S(1)}, bf16[128,1024]{1,0:T(8,128)(2,1)S(1)}, u32[]{:S(2)}, u32[]{:S(2)}) %collective-permute-start.36) | collective-permute-done | bytes 262176 | tf_op jit(solution)/shard_map/ppermute | solution.py:93
  121.2 2.4 %collective-permute-done.30 = bf16[128,1024]{1,0:T(8,128)(2,1)S(1)} collective-permute-done((bf16[128,1024]{1,0:T(8,128)(2,1)S(1)}, bf16[128,1024]{1,0:T(8,128)(2,1)S(1)}, u32[]{:S(2)}, u32[]{:S(2)}) %collective-permute-start.30) | collective-permute-done | bytes 262176 | tf_op jit(solution)/shard_map/ppermute | solution.py:93
  123.6 3.9 %collective-permute-done.37 = bf16[128,1024]{1,0:T(8,128)(2,1)S(1)} collective-permute-done((bf16[128,1024]{1,0:T(8,128)(2,1)S(1)}, bf16[128,1024]{1,0:T(8,128)(2,1)S(1)}, u32[]{:S(2)}, u32[]{:S(2)}) %collective-permute-start.37) | collective-permute-done | bytes 262176 | tf_op jit(solution)/shard_map/ppermute | solution.py:93
  127.6 0.9 add_convert_fusion
  (46 shorter events, 3.9 us)
Async XLA Ops:
  1.1 6.4 %collective-permute-start = (bf16[128,640]{1,0:T(8,128)(2,1)S(1)}, bf16[128,640]{1,0:T(8,128)(2,1)S(1)}, u32[]{:S(2)}, u32[]{:S(2)}) collective-permute-start(bf16[128,640]{1,0:T(8,128)(2,1)S(1)} %pack.1.refs_0_), channel_id=1, source_target_pairs={{0,2},{1,5},{2,6},{3,1},{6,10},{7,3},{10,14},{11,7},{14,12},{15,11... | collective-permute-start | bytes 491528 | tf_op jit(solution)/shard_map/ppermute | solution.py:49
  7.5 2.7 %collective-permute-start.2 = (bf16[128,640]{1,0:T(8,128)(2,1)S(1)}, bf16[128,640]{1,0:T(8,128)(2,1)S(1)}, u32[]{:S(2)}, u32[]{:S(2)}) collective-permute-start(bf16[128,640]{1,0:T(8,128)(2,1)S(1)} %collective-permute-done.refs_1_), channel_id=1, source_target_pairs={{0,1},{1,0},{2,3},{3,2},{4,5},{5,4},{6,7},{7,6},{8,9},{9,8},{10,11... | collective-permute-start | bytes 491528 | tf_op jit(solution)/shard_map/ppermute | solution.py:40
  7.5 5.3 %collective-permute-start.1 = (bf16[128,640]{1,0:T(8,128)(2,1)S(1)}, bf16[128,640]{1,0:T(8,128)(2,1)S(1)}, u32[]{:S(2)}, u32[]{:S(2)}) collective-permute-start(bf16[128,640]{1,0:T(8,128)(2,1)S(1)} %collective-permute-done.refs_1_), channel_id=1, source_target_pairs={{0,2},{1,5},{2,6},{3,1},{6,10},{7,3},{10,14},{11,7},{14,12},{15,11... | collective-permute-start | bytes 491528 | tf_op jit(solution)/shard_map/ppermute | solution.py:49
  12.9 2.0 %collective-permute-start.4 = (bf16[128,640]{1,0:T(8,128)(2,1)S(1)}, bf16[128,640]{1,0:T(8,128)(2,1)S(1)}, u32[]{:S(2)}, u32[]{:S(2)}) collective-permute-start(bf16[128,640]{1,0:T(8,128)(2,1)S(1)} %collective-permute-done.1.refs_2_), channel_id=1, source_target_pairs={{0,1},{1,0},{2,3},{3,2},{4,5},{5,4},{6,7},{7,6},{8,9},{9,8},{10,11... | collective-permute-start | bytes 491528 | tf_op jit(solution)/shard_map/ppermute | solution.py:40
  12.9 5.3 %collective-permute-start.3 = (bf16[128,640]{1,0:T(8,128)(2,1)S(1)}, bf16[128,640]{1,0:T(8,128)(2,1)S(1)}, u32[]{:S(2)}, u32[]{:S(2)}) collective-permute-start(bf16[128,640]{1,0:T(8,128)(2,1)S(1)} %collective-permute-done.1.refs_2_), channel_id=1, source_target_pairs={{0,2},{1,5},{2,6},{3,1},{6,10},{7,3},{10,14},{11,7},{14,12},{15,11... | collective-permute-start | bytes 491528 | tf_op jit(solution)/shard_map/ppermute | solution.py:49
  18.2 2.0 %collective-permute-start.6 = (bf16[128,640]{1,0:T(8,128)(2,1)S(1)}, bf16[128,640]{1,0:T(8,128)(2,1)S(1)}, u32[]{:S(2)}, u32[]{:S(2)}) collective-permute-start(bf16[128,640]{1,0:T(8,128)(2,1)S(1)} %collective-permute-done.3.refs_3_), channel_id=1, source_target_pairs={{0,1},{1,0},{2,3},{3,2},{4,5},{5,4},{6,7},{7,6},{8,9},{9,8},{10,11... | collective-permute-start | bytes 491528 | tf_op jit(solution)/shard_map/ppermute | solution.py:40
  18.2 5.3 %collective-permute-start.5 = (bf16[128,640]{1,0:T(8,128)(2,1)S(1)}, bf16[128,640]{1,0:T(8,128)(2,1)S(1)}, u32[]{:S(2)}, u32[]{:S(2)}) collective-permute-start(bf16[128,640]{1,0:T(8,128)(2,1)S(1)} %collective-permute-done.3.refs_3_), channel_id=1, source_target_pairs={{0,2},{1,5},{2,6},{3,1},{6,10},{7,3},{10,14},{11,7},{14,12},{15,11... | collective-permute-start | bytes 491528 | tf_op jit(solution)/shard_map/ppermute | solution.py:49
  29.4 2.0 %collective-permute-start.7 = (bf16[128,2048]{1,0:T(8,128)(2,1)S(1)}, bf16[128,2048]{1,0:T(8,128)(2,1)S(1)}, u32[]{:S(2)}, u32[]{:S(2)}) collective-permute-start(bf16[128,2048]{1,0:T(8,128)(2,1)S(1)} %get-tuple-element.73), channel_id=1, source_target_pairs={{0,1},{1,0},{2,3},{3,2},{4,5},{5,4},{6,7},{7,6},{8,9},{9,8},{10,11... | collective-permute-start | bytes 1572872 | tf_op jit(solution)/shard_map/ppermute | solution.py:40
  32.2 6.4 %collective-permute-start.8 = (bf16[128,1024]{1,0:T(8,128)(2,1)S(1)}, bf16[128,1024]{1,0:T(8,128)(2,1)S(1)}, u32[]{:S(2)}, u32[]{:S(2)}) collective-permute-start(bf16[128,1024]{1,0:T(8,128)(2,1)S(1)} %get-tuple-element.76.refs_0_), channel_id=1, source_target_pairs={{0,2},{1,5},{2,6},{3,1},{6,10},{7,3},{10,14},{11,7},{14,12},{15,11... | collective-permute-start | bytes 786440 | tf_op jit(solution)/shard_map/ppermute | solution.py:49
  34.2 7.2 %collective-permute-start.9 = (bf16[128,1024]{1,0:T(8,128)(2,1)S(1)}, bf16[128,1024]{1,0:T(8,128)(2,1)S(1)}, u32[]{:S(2)}, u32[]{:S(2)}) collective-permute-start(bf16[128,1024]{1,0:T(8,128)(2,1)S(1)} %get-tuple-element.77.refs_1_), channel_id=1, source_target_pairs={{0,2},{1,5},{2,6},{3,1},{6,10},{7,3},{10,14},{11,7},{14,12},{15,11... | collective-permute-start | bytes 786440 | tf_op jit(solution)/shard_map/ppermute | solution.py:49
  41.5 3.6 %collective-permute-start.12 = (bf16[128,1024]{1,0:T(8,128)(2,1)S(1)}, bf16[128,1024]{1,0:T(8,128)(2,1)S(1)}, u32[]{:S(2)}, u32[]{:S(2)}) collective-permute-start(bf16[128,1024]{1,0:T(8,128)(2,1)S(1)} %collective-permute-done.8.refs_2_), channel_id=1, source_target_pairs={{0,1},{1,0},{2,3},{3,2},{4,5},{5,4},{6,7},{7,6},{8,9},{9,8},{10,11... | collective-permute-start | bytes 786440 | tf_op jit(solution)/shard_map/ppermute | solution.py:40
  41.5 6.4 %collective-permute-start.10 = (bf16[128,1024]{1,0:T(8,128)(2,1)S(1)}, bf16[128,1024]{1,0:T(8,128)(2,1)S(1)}, u32[]{:S(2)}, u32[]{:S(2)}) collective-permute-start(bf16[128,1024]{1,0:T(8,128)(2,1)S(1)} %collective-permute-done.8.refs_2_), channel_id=1, source_target_pairs={{0,2},{1,5},{2,6},{3,1},{6,10},{7,3},{10,14},{11,7},{14,12},{15,11... | collective-permute-start | bytes 786440 | tf_op jit(solution)/shard_map/ppermute | solution.py:49
  43.4 4.4 %collective-permute-start.13 = (bf16[128,1024]{1,0:T(8,128)(2,1)S(1)}, bf16[128,1024]{1,0:T(8,128)(2,1)S(1)}, u32[]{:S(2)}, u32[]{:S(2)}) collective-permute-start(bf16[128,1024]{1,0:T(8,128)(2,1)S(1)} %collective-permute-done.9.refs_3_), channel_id=1, source_target_pairs={{0,1},{1,0},{2,3},{3,2},{4,5},{5,4},{6,7},{7,6},{8,9},{9,8},{10,11... | collective-permute-start | bytes 786440 | tf_op jit(solution)/shard_map/ppermute | solution.py:40
  43.7 6.9 %collective-permute-start.11 = (bf16[128,1024]{1,0:T(8,128)(2,1)S(1)}, bf16[128,1024]{1,0:T(8,128)(2,1)S(1)}, u32[]{:S(2)}, u32[]{:S(2)}) collective-permute-start(bf16[128,1024]{1,0:T(8,128)(2,1)S(1)} %collective-permute-done.9.refs_3_), channel_id=1, source_target_pairs={{0,2},{1,5},{2,6},{3,1},{6,10},{7,3},{10,14},{11,7},{14,12},{15,11... | collective-permute-start | bytes 786440 | tf_op jit(solution)/shard_map/ppermute | solution.py:49
  50.6 3.6 %collective-permute-start.16 = (bf16[128,1024]{1,0:T(8,128)(2,1)S(1)}, bf16[128,1024]{1,0:T(8,128)(2,1)S(1)}, u32[]{:S(2)}, u32[]{:S(2)}) collective-permute-start(bf16[128,1024]{1,0:T(8,128)(2,1)S(1)} %collective-permute-done.10.refs_4_), channel_id=1, source_target_pairs={{0,1},{1,0},{2,3},{3,2},{4,5},{5,4},{6,7},{7,6},{8,9},{9,8},{10,11... | collective-permute-start | bytes 786440 | tf_op jit(solution)/shard_map/ppermute | solution.py:40
  50.6 6.4 %collective-permute-start.14 = (bf16[128,1024]{1,0:T(8,128)(2,1)S(1)}, bf16[128,1024]{1,0:T(8,128)(2,1)S(1)}, u32[]{:S(2)}, u32[]{:S(2)}) collective-permute-start(bf16[128,1024]{1,0:T(8,128)(2,1)S(1)} %collective-permute-done.10.refs_4_), channel_id=1, source_target_pairs={{0,2},{1,5},{2,6},{3,1},{6,10},{7,3},{10,14},{11,7},{14,12},{15,11... | collective-permute-start | bytes 786440 | tf_op jit(solution)/shard_map/ppermute | solution.py:49
  52.6 4.4 %collective-permute-start.17 = (bf16[128,1024]{1,0:T(8,128)(2,1)S(1)}, bf16[128,1024]{1,0:T(8,128)(2,1)S(1)}, u32[]{:S(2)}, u32[]{:S(2)}) collective-permute-start(bf16[128,1024]{1,0:T(8,128)(2,1)S(1)} %collective-permute-done.11.refs_5_), channel_id=1, source_target_pairs={{0,1},{1,0},{2,3},{3,2},{4,5},{5,4},{6,7},{7,6},{8,9},{9,8},{10,11... | collective-permute-start | bytes 786440 | tf_op jit(solution)/shard_map/ppermute | solution.py:40
  52.9 6.9 %collective-permute-start.15 = (bf16[128,1024]{1,0:T(8,128)(2,1)S(1)}, bf16[128,1024]{1,0:T(8,128)(2,1)S(1)}, u32[]{:S(2)}, u32[]{:S(2)}) collective-permute-start(bf16[128,1024]{1,0:T(8,128)(2,1)S(1)} %collective-permute-done.11.refs_5_), channel_id=1, source_target_pairs={{0,2},{1,5},{2,6},{3,1},{6,10},{7,3},{10,14},{11,7},{14,12},{15,11... | collective-permute-start | bytes 786440 | tf_op jit(solution)/shard_map/ppermute | solution.py:49
  59.8 3.6 %collective-permute-start.20 = (bf16[128,1024]{1,0:T(8,128)(2,1)S(1)}, bf16[128,1024]{1,0:T(8,128)(2,1)S(1)}, u32[]{:S(2)}, u32[]{:S(2)}) collective-permute-start(bf16[128,1024]{1,0:T(8,128)(2,1)S(1)} %collective-permute-done.14.refs_6_), channel_id=1, source_target_pairs={{0,1},{1,0},{2,3},{3,2},{4,5},{5,4},{6,7},{7,6},{8,9},{9,8},{10,11... | collective-permute-start | bytes 786440 | tf_op jit(solution)/shard_map/ppermute | solution.py:40
  59.8 6.4 %collective-permute-start.18 = (bf16[128,1024]{1,0:T(8,128)(2,1)S(1)}, bf16[128,1024]{1,0:T(8,128)(2,1)S(1)}, u32[]{:S(2)}, u32[]{:S(2)}) collective-permute-start(bf16[128,1024]{1,0:T(8,128)(2,1)S(1)} %collective-permute-done.14.refs_6_), channel_id=1, source_target_pairs={{0,2},{1,5},{2,6},{3,1},{6,10},{7,3},{10,14},{11,7},{14,12},{15,11... | collective-permute-start | bytes 786440 | tf_op jit(solution)/shard_map/ppermute | solution.py:49
  61.8 4.4 %collective-permute-start.21 = (bf16[128,1024]{1,0:T(8,128)(2,1)S(1)}, bf16[128,1024]{1,0:T(8,128)(2,1)S(1)}, u32[]{:S(2)}, u32[]{:S(2)}) collective-permute-start(bf16[128,1024]{1,0:T(8,128)(2,1)S(1)} %collective-permute-done.15.refs_7_), channel_id=1, source_target_pairs={{0,1},{1,0},{2,3},{3,2},{4,5},{5,4},{6,7},{7,6},{8,9},{9,8},{10,11... | collective-permute-start | bytes 786440 | tf_op jit(solution)/shard_map/ppermute | solution.py:40
  62.1 6.9 %collective-permute-start.19 = (bf16[128,1024]{1,0:T(8,128)(2,1)S(1)}, bf16[128,1024]{1,0:T(8,128)(2,1)S(1)}, u32[]{:S(2)}, u32[]{:S(2)}) collective-permute-start(bf16[128,1024]{1,0:T(8,128)(2,1)S(1)} %collective-permute-done.15.refs_7_), channel_id=1, source_target_pairs={{0,2},{1,5},{2,6},{3,1},{6,10},{7,3},{10,14},{11,7},{14,12},{15,11... | collective-permute-start | bytes 786440 | tf_op jit(solution)/shard_map/ppermute | solution.py:49
  94.5 1.6 %collective-permute-start.26 = (bf16[128,1024]{1,0:T(8,128)(2,1)S(1)}, bf16[128,1024]{1,0:T(8,128)(2,1)S(1)}, u32[]{:S(2)}, u32[]{:S(2)}) collective-permute-start(bf16[128,1024]{1,0:T(8,128)(2,1)S(1)} %get-tuple-element.110), channel_id=1, source_target_pairs={{0,1},{1,0},{2,3},{3,2},{4,5},{5,4},{6,7},{7,6},{8,9},{9,8},{10,11... | collective-permute-start | bytes 786440 | tf_op jit(solution)/shard_map/ppermute | solution.py:40
  94.6 4.3 %collective-permute-start.25 = (bf16[128,1024]{1,0:T(8,128)(2,1)S(1)}, bf16[128,1024]{1,0:T(8,128)(2,1)S(1)}, u32[]{:S(2)}, u32[]{:S(2)}) collective-permute-start(bf16[128,1024]{1,0:T(8,128)(2,1)S(1)} %get-tuple-element.108), channel_id=1, source_target_pairs={{0,1},{1,0},{2,3},{3,2},{4,5},{5,4},{6,7},{7,6},{8,9},{9,8},{10,11... | collective-permute-start | bytes 786440 | tf_op jit(solution)/shard_map/ppermute | solution.py:40
  96.2 5.8 %collective-permute-start.27 = (bf16[64,1024]{1,0:T(8,128)(2,1)S(1)}, bf16[64,1024]{1,0:T(8,128)(2,1)S(1)}, u32[]{:S(2)}, u32[]{:S(2)}) collective-permute-start(bf16[64,1024]{1,0:T(8,128)(2,1)S(1)} %get-tuple-element.117), channel_id=1, source_target_pairs={{0,2},{2,6},{6,10},{10,14},{14,12},{12,8},{8,4},{4,0},{1,3},{3,7},... | collective-permute-start | bytes 393224 | tf_op jit(solution)/shard_map/ppermute | solution.py:93
  98.2 5.7 %collective-permute-start.33 = (bf16[128,1024]{1,0:T(8,128)(2,1)S(1)}, bf16[128,1024]{1,0:T(8,128)(2,1)S(1)}, u32[]{:S(2)}, u32[]{:S(2)}) collective-permute-start(bf16[128,1024]{1,0:T(8,128)(2,1)S(1)} %get-tuple-element.116), channel_id=1, source_target_pairs={{0,1},{1,0},{2,3},{3,2},{4,5},{5,4},{6,7},{7,6},{8,9},{9,8},{10,11... | collective-permute-start | bytes 786440 | tf_op jit(solution)/shard_map/ppermute | solution.py:40
  98.2 6.4 %collective-permute-start.24 = (bf16[128,1024]{1,0:T(8,128)(2,1)S(1)}, bf16[128,1024]{1,0:T(8,128)(2,1)S(1)}, u32[]{:S(2)}, u32[]{:S(2)}) collective-permute-start(bf16[128,1024]{1,0:T(8,128)(2,1)S(1)} %get-tuple-element.106), channel_id=1, source_target_pairs={{0,1},{1,0},{2,3},{3,2},{4,5},{5,4},{6,7},{7,6},{8,9},{9,8},{10,11... | collective-permute-start | bytes 786440 | tf_op jit(solution)/shard_map/ppermute | solution.py:40
  98.7 5.4 %collective-permute-start.34 = (bf16[64,1024]{1,0:T(8,128)(2,1)S(1)}, bf16[64,1024]{1,0:T(8,128)(2,1)S(1)}, u32[]{:S(2)}, u32[]{:S(2)}) collective-permute-start(bf16[64,1024]{1,0:T(8,128)(2,1)S(1)} %get-tuple-element.118), channel_id=1, source_target_pairs={{0,4},{2,0},{6,2},{10,6},{14,10},{12,14},{8,12},{4,8},{1,5},{3,1},... | collective-permute-start | bytes 393224 | tf_op jit(solution)/shard_map/ppermute | solution.py:93
  102.1 7.9 %collective-permute-start.28 = (bf16[128,1024]{1,0:T(8,128)(2,1)S(1)}, bf16[128,1024]{1,0:T(8,128)(2,1)S(1)}, u32[]{:S(2)}, u32[]{:S(2)}) collective-permute-start(bf16[128,1024]{1,0:T(8,128)(2,1)S(1)} %add_convert_fusion.6), channel_id=1, source_target_pairs={{0,2},{2,6},{6,10},{10,14},{14,12},{12,8},{8,4},{4,0},{1,3},{3,7},... | collective-permute-start | bytes 786440 | tf_op jit(solution)/shard_map/ppermute | solution.py:93
  103.9 7.7 %collective-permute-start.32 = (bf16[128,1024]{1,0:T(8,128)(2,1)S(1)}, bf16[128,1024]{1,0:T(8,128)(2,1)S(1)}, u32[]{:S(2)}, u32[]{:S(2)}) collective-permute-start(bf16[128,1024]{1,0:T(8,128)(2,1)S(1)} %get-tuple-element.114), channel_id=1, source_target_pairs={{0,1},{1,0},{2,3},{3,2},{4,5},{5,4},{6,7},{7,6},{8,9},{9,8},{10,11... | collective-permute-start | bytes 786440 | tf_op jit(solution)/shard_map/ppermute | solution.py:40
  104.2 8.6 %collective-permute-start.35 = (bf16[128,1024]{1,0:T(8,128)(2,1)S(1)}, bf16[128,1024]{1,0:T(8,128)(2,1)S(1)}, u32[]{:S(2)}, u32[]{:S(2)}) collective-permute-start(bf16[128,1024]{1,0:T(8,128)(2,1)S(1)} %add_convert_fusion.3), channel_id=1, source_target_pairs={{0,4},{2,0},{6,2},{10,6},{14,10},{12,14},{8,12},{4,8},{1,5},{3,1},... | collective-permute-start | bytes 786440 | tf_op jit(solution)/shard_map/ppermute | solution.py:93
  104.5 8.7 %collective-permute-start.23 = (bf16[128,1024]{1,0:T(8,128)(2,1)S(1)}, bf16[128,1024]{1,0:T(8,128)(2,1)S(1)}, u32[]{:S(2)}, u32[]{:S(2)}) collective-permute-start(bf16[128,1024]{1,0:T(8,128)(2,1)S(1)} %get-tuple-element.104), channel_id=1, source_target_pairs={{0,1},{1,0},{2,3},{3,2},{4,5},{5,4},{6,7},{7,6},{8,9},{9,8},{10,11... | collective-permute-start | bytes 786440 | tf_op jit(solution)/shard_map/ppermute | solution.py:40
  104.6 13.7 %collective-permute-start.31 = (bf16[128,1024]{1,0:T(8,128)(2,1)S(1)}, bf16[128,1024]{1,0:T(8,128)(2,1)S(1)}, u32[]{:S(2)}, u32[]{:S(2)}) collective-permute-start(bf16[128,1024]{1,0:T(8,128)(2,1)S(1)} %get-tuple-element.112), channel_id=1, source_target_pairs={{0,1},{1,0},{2,3},{3,2},{4,5},{5,4},{6,7},{7,6},{8,9},{9,8},{10,11... | collective-permute-start | bytes 786440 | tf_op jit(solution)/shard_map/ppermute | solution.py:40
  110.1 7.0 %collective-permute-start.29 = (bf16[128,1024]{1,0:T(8,128)(2,1)S(1)}, bf16[128,1024]{1,0:T(8,128)(2,1)S(1)}, u32[]{:S(2)}, u32[]{:S(2)}) collective-permute-start(bf16[128,1024]{1,0:T(8,128)(2,1)S(1)} %add_convert_fusion.5), channel_id=1, source_target_pairs={{0,2},{2,6},{6,10},{10,14},{14,12},{12,8},{8,4},{4,0},{1,3},{3,7},... | collective-permute-start | bytes 786440 | tf_op jit(solution)/shard_map/ppermute | solution.py:93
  112.9 7.7 %collective-permute-start.36 = (bf16[128,1024]{1,0:T(8,128)(2,1)S(1)}, bf16[128,1024]{1,0:T(8,128)(2,1)S(1)}, u32[]{:S(2)}, u32[]{:S(2)}) collective-permute-start(bf16[128,1024]{1,0:T(8,128)(2,1)S(1)} %add_convert_fusion.2), channel_id=1, source_target_pairs={{0,4},{2,0},{6,2},{10,6},{14,10},{12,14},{8,12},{4,8},{1,5},{3,1},... | collective-permute-start | bytes 786440 | tf_op jit(solution)/shard_map/ppermute | solution.py:93
  113.3 7.9 %collective-permute-start.22 = (bf16[128,1024]{1,0:T(8,128)(2,1)S(1)}, bf16[128,1024]{1,0:T(8,128)(2,1)S(1)}, u32[]{:S(2)}, u32[]{:S(2)}) collective-permute-start(bf16[128,1024]{1,0:T(8,128)(2,1)S(1)} %get-tuple-element.102), channel_id=1, source_target_pairs={{0,1},{1,0},{2,3},{3,2},{4,5},{5,4},{6,7},{7,6},{8,9},{9,8},{10,11... | collective-permute-start | bytes 786440 | tf_op jit(solution)/shard_map/ppermute | solution.py:40
  117.2 6.4 %collective-permute-start.30 = (bf16[128,1024]{1,0:T(8,128)(2,1)S(1)}, bf16[128,1024]{1,0:T(8,128)(2,1)S(1)}, u32[]{:S(2)}, u32[]{:S(2)}) collective-permute-start(bf16[128,1024]{1,0:T(8,128)(2,1)S(1)} %add_convert_fusion.4), channel_id=1, source_target_pairs={{0,2},{2,6},{6,10},{10,14},{14,12},{12,8},{8,4},{4,0},{1,3},{3,7},... | collective-permute-start | bytes 786440 | tf_op jit(solution)/shard_map/ppermute | solution.py:93
  120.8 6.8 %collective-permute-start.37 = (bf16[128,1024]{1,0:T(8,128)(2,1)S(1)}, bf16[128,1024]{1,0:T(8,128)(2,1)S(1)}, u32[]{:S(2)}, u32[]{:S(2)}) collective-permute-start(bf16[128,1024]{1,0:T(8,128)(2,1)S(1)} %add_convert_fusion.1), channel_id=1, source_target_pairs={{0,4},{2,0},{6,2},{10,6},{14,10},{12,14},{8,12},{4,8},{1,5},{3,1},... | collective-permute-start | bytes 786440 | tf_op jit(solution)/shard_map/ppermute | solution.py:93

commit v11 on v10

--- a/solution.py
+++ b/solution.py
@@ -69,14 +69,13 @@
     return lax.dynamic_index_in_dim(jnp.asarray(table), me * 2 + side, keepdims=False)
 
 
-def gather(arrays, count, beside=()):
+def gather(block, count, beside=()):
     if count > FEW:
-        found = [lax.all_gather(block, "ctx") for block in arrays]
-        return list(zip(*found)), [run(*arguments) for run, arguments in beside]
+        return list(lax.all_gather(block, "ctx")), [run(*arguments) for run, arguments in beside]
     middle = count // 2
-    found, other, made = [tuple(arrays)], [()], []
+    found, other, made = [block], [()], []
     for d in range(1, middle + 1):
-        arrived, extra = tuple(turn(x, count) for x in found[-1]), ()
+        arrived, extra = turn(found[-1], count), ()
         if len(beside) >= d:
             run, arguments = beside[d - 1]
             extra = run(*lax.optimization_barrier((found[-1], arguments))[1])
@@ -84,30 +83,29 @@
         made.append(extra)
         found.append(arrived)
         if d < middle:
-            other.append(tuple(swap(x) for x in arrived))
+            other.append(swap(arrived))
     return found + other[1:], made[: len(beside)]
 
 
-def step(value, ahead, count):
-    cycle = cycle_of(count)
-    return lax.ppermute(value, "ctx", [(cycle[p], cycle[(p + ahead) % count]) for p in range(count)])
-
-
-def reduce(parts, count):
+def reduce(parts, side, count):
     middle = count // 2
-    first = parts[middle]().astype(jnp.bfloat16)
-    half = first.shape[0] // 2
-    zero = jnp.zeros((half, first.shape[1]), jnp.bfloat16)
-    ahead = jnp.concatenate([step(first[:half], 1, count), zero], axis=0)
-    back = jnp.concatenate([zero, step(first[half:], -1, count)], axis=0)
-    for d in range(middle - 1, 0, -1):
-        ahead = step((parts[count - d]() + ahead.astype(jnp.float32)).astype(jnp.bfloat16), 1, count)
-        back = step((parts[d]() + back.astype(jnp.float32)).astype(jnp.bfloat16), -1, count)
-    return parts[0]() + ahead.astype(jnp.float32) + back.astype(jnp.float32)
-
-
-def order_of(count):
-    return [(count // 2 + (d + 1) // 2 * (1 - d % 2 * 2)) % count for d in range(count)]
+    near, far = 0, 1
+    sums = [None, None]
+    given = {}
+    for d in range(middle, 0, -1):
+        for stream in (near, far):
+            mine = parts[1 - stream][d]
+            given[stream, d] = swap(mine[1] if d == middle else mine)
+    for stream in (near, far):
+        first = summed([parts[stream][middle][0], given[stream, middle]]).astype(jnp.bfloat16)
+        first = turn(first, count).astype(jnp.float32)
+        nothing = jnp.zeros_like(first)
+        running = jnp.concatenate([jnp.where(side == 0, first, nothing), jnp.where(side == 0, nothing, first)], axis=0)
+        for d in range(middle - 1, 0, -1):
+            total = (summed([parts[stream][middle + d], given[stream, d]]) + running).astype(jnp.bfloat16)
+            running = turn(total, count, cross=d == 1 and stream == far).astype(jnp.float32)
+        sums[stream] = running
+    return summed([parts[near][0], swap(parts[far][0])]) + sums[near] + sums[far]
 
 
 def attend_kernel(count, blocks, heads, info, *refs):
@@ -330,8 +328,8 @@
 def fused_kernel(count, where, *refs):
     at = PARTS * count
     blocks, combine_ref, weights = refs[:at], refs[at], refs[at + 1 : at + 4]
-    kept, away = refs[at + 4 : at + 4 + count], refs[at + 4 + count : at + 4 + 2 * count]
-    at += 4 + 2 * count
+    near, far = refs[at + 4 : at + 5 + count], refs[at + 5 + count : at + 6 + 2 * count]
+    at += 6 + 2 * count
     picked, buffers, sems = refs[at], refs[at + 1 : at + 4], refs[at + 4]
     here = picked.shape[0]
     depth, units, width = buffers[0].shape
@@ -375,15 +373,17 @@
     lax.fori_loop(0, here, work, 0)
 
     half = width // 2
-    for d in order_of(count):
-        forward = d if d <= middle else middle + count - d
-        backward = forward if d in (0, middle) else (count - d if d > middle else middle + d)
-        c = forward if forward == backward else jnp.where(side == 0, forward, backward)
-        place = pl.ds(c * SLOTS if forward == backward else pl.multiple_of(c * SLOTS, SLOTS), SLOTS)
-        for turned, out in ((1 - side, away[d]), (side, kept[d])):
+    for c in [middle] + list(range(middle)) + list(range(middle + 1, count)):
+        for turned, outs in ((1 - side, far), (side, near)):
             columns = pl.ds(pl.multiple_of(turned * half, half), half)
-            rows = jnp.concatenate([picked[e, place, columns] for e in range(here)], axis=0)
-            out[...] = jnp.dot(combine_ref[c], rows, preferred_element_type=jnp.float32).astype(jnp.bfloat16)
+            rows = jnp.concatenate([picked[e, c * SLOTS : (c + 1) * SLOTS, columns] for e in range(here)], axis=0)
+            total = jnp.dot(combine_ref[c], rows, preferred_element_type=jnp.float32).astype(jnp.bfloat16)
+            if c == middle:
+                upper, lower = total[: total.shape[0] // 2], total[total.shape[0] // 2 :]
+                outs[c][...] = jnp.where(side == 0, upper, lower)
+                outs[count][...] = jnp.where(side == 0, lower, upper)
+            else:
+                outs[c][...] = total
 
 
 def expert_specs(w_gate):
@@ -413,22 +413,25 @@
     here, units, width = w_gate.shape
     rows = count * SLOTS
     depth = min(DEPTH, here)
+    middle = count // 2
+    sizes = [local // 2 if c in (middle, count) else local for c in range(count + 1)]
     whole = pl.BlockSpec(memory_space=pltpu.VMEM)
     outs = pl.pallas_call(
         functools.partial(fused_kernel, count),
         in_specs=[pl.BlockSpec(memory_space=pltpu.SMEM)]
         + [whole] * (PARTS * count + 1)
         + [pl.BlockSpec(memory_space=pltpu.HBM)] * 3,
-        out_specs=[whole] * (2 * count),
+        out_specs=[whole] * (2 * count + 2),
         scratch_shapes=[pltpu.VMEM((here, rows, width), jnp.bfloat16)]
         + [pltpu.VMEM((depth, units, width), jnp.bfloat16)] * 3
         + [pltpu.SemaphoreType.DMA((depth, 3, PIECES))],
-        out_shape=[pltpu.VMEM((local, width // 2), jnp.bfloat16)] * (2 * count),
+        out_shape=[pltpu.VMEM((size, width // 2), jnp.bfloat16) for size in sizes] * 2,
         compiler_params=pltpu.CompilerParams(vmem_limit_bytes=36 * MIB),
         name="experts",
     )(where, *(x for block in found for x in block), combine,
       *(pltpu.with_memory_space_constraint(w, pltpu.HBM) for w in (w_gate, w_up, w_down)))
-    return outs[:count], outs[count:]
+    parts = [list(outs[: count + 1]), list(outs[count + 1 :])]
+    return [x[:middle] + [(x[middle], x[count])] + x[middle + 1 : count] for x in parts]
 
 
 def body(
@@ -459,8 +462,7 @@
     few = count <= FEW
     scalars = lambda *arrays: jnp.concatenate([where, sources_of(me, side, count), *arrays])
     beside = [(scalars, (span_order, seg_lengths)), (lambda gain: gain.reshape(1, width), (norm_gain,))]
-    found, (info, gain) = gather([packed], count, beside)
-    found = [block for block, in found]
+    found, (info, gain) = gather(packed, count, beside)
     partial, summand = attend(info, found, queries, kv_up, out_proj, residual, count)
     middle, *normed = norm(where, summand, swap(partial), gain)
 
@@ -479,12 +481,11 @@
         combine = jnp.where(rank[:, :, :, None] == slot, share[:, :, :, None], 0.0)
         return combine.astype(jnp.bfloat16).reshape(count, local_rows, here * SLOTS)
 
-    got, (combine,) = gather(normed, count, [(place_rows, tuple(found))])
+    streams = [gather(x, count, [(place_rows, tuple(found))] if h == 0 else ()) for h, x in enumerate(normed)]
+    combine = streams[0][1][0]
+    got = list(zip(*(blocks for blocks, _ in streams)))
     if few:
-        kept, away = experts_fused(where, got, combine, w_gate, w_up, w_down)
-        swapped = {d: swap(away[d]) for d in order_of(count)}
-        parts = [functools.partial(summed, [kept[d], swapped[d]]) for d in range(count)]
-        mixture = reduce(parts, count)
+        mixture = reduce(experts_fused(where, got, combine, w_gate, w_up, w_down), side, count)
     else:
         pick = (combine > 0).astype(jnp.bfloat16)
         rows = jnp.stack([jnp.concatenate(block, axis=1) for block in got])

time: 129 us -> 124 us (0.961)
  waiting for transfers between devices: 56.8 us -> 46.1 us
  local copies, waits for them, and re-layouts: 2.15 us -> 4.26 us
  starting transfers between devices: 32.5 us -> 34.6 us
    ppermute x8 -> x0, waiting for transfers between devices: 22 us -> none  [step(): lax.ppermute(value, 'ctx', [(cycle[p], cycle[(p + ahead) % count]) for p...]
    ppermute x12 -> x20, waiting for transfers between devices: 31.9 us -> 43.4 us  [turn(): return lax.ppermute(value, ('ctx', 'exp'), pairs)]
    ppermute x12 -> x20, starting transfers between devices: 22.3 us -> 32.5 us  [turn(): return lax.ppermute(value, ('ctx', 'exp'), pairs)]
    ppermute x8 -> x0, starting transfers between devices: 7.64 us -> none  [step(): lax.ppermute(value, 'ctx', [(cycle[p], cycle[(p + ahead) % count]) for p...]
    unnamed x0 -> x6, local copies, waits for them, and re-layouts: none -> 2.13 us
    ppermute x18 -> x19, waiting for transfers between devices: 2.89 us -> 2.68 us  [swap(): return lax.ppermute(value, 'exp', SWAP)]
  transfers between devices with their start and end apart: 38 -> 39, of which waited for: 22 -> 21; matrix products, arithmetic and copies ran while one was open for 2% -> 3% of each run, Pallas kernels for 1% -> 1%
where the time goes in v11:
time: 124 us
  waiting for transfers between devices  46.1 us (37%)
  Pallas kernels  35.7 us (29%)
  starting transfers between devices  34.6 us (28%)
  local copies, waits for them, and re-layouts  4.26 us (3%)
  other arithmetic  2.74 us (2%)
    ppermute x20, waiting for transfers between devices, turn(): return lax.ppermute(value, ('ctx', 'exp'), pairs)  43.4 us
    ppermute x20, starting transfers between devices, turn(): return lax.ppermute(value, ('ctx', 'exp'), pairs)  32.5 us
    pallas_call x1, Pallas kernels, experts_fused(): pl.pallas_call(functools.partial(fused_kernel, count), in_specs=[pl.Block...  26 us
    pallas_call x1, Pallas kernels, attend(): pl.pallas_call(functools.partial(attend_kernel, count, blocks, heads), gr...  5.86 us
    ppermute x19, waiting for transfers between devices, swap(): return lax.ppermute(value, 'exp', SWAP)  2.68 us
  transfers between devices with their start and end apart: 39, of which 21 were waited for; matrix products, arithmetic and copies ran while one was open for 3% of the time, Pallas kernels for 1%

profile of v11, /device:TPU:0, one launch (start us, length us, event | category | flops | bytes accessed | tf_op | source)
XLA Modules:
  0.0 123.6 jit_solution(11584502619764987863)
XLA Ops:
  0.0 1.1 pack.1.refs_0_
  1.1 3.0 %collective-permute-start = (bf16[128,640]{1,0:T(8,128)(2,1)S(1)}, bf16[128,640]{1,0:T(8,128)(2,1)S(1)}, u32[]{:S(2)}, u32[]{:S(2)}) collective-permute-start(bf16[128,640]{1,0:T(8,128)(2,1)S(1)} %pack.1.refs_0_), channel_id=1, source_target_pairs={{0,2},{1,5},{2,6},{3,1},{6,10},{7,3},{10,14},{11,7},{14,12},{15,11... | collective-permute-start | bytes 491528 | tf_op jit(solution)/shard_map/ppermute | solution.py:49
  4.9 0.7 concatenate.10.info
  5.6 1.9 %collective-permute-done.refs_1_ = bf16[128,640]{1,0:T(8,128)(2,1)S(1)} collective-permute-done((bf16[128,640]{1,0:T(8,128)(2,1)S(1)}, bf16[128,640]{1,0:T(8,128)(2,1)S(1)}, u32[]{:S(2)}, u32[]{:S(2)}) %collective-permute-start) | collective-permute-done | bytes 163872 | tf_op jit(solution)/shard_map/ppermute | solution.py:49
  7.5 2.0 %collective-permute-start.1 = (bf16[128,640]{1,0:T(8,128)(2,1)S(1)}, bf16[128,640]{1,0:T(8,128)(2,1)S(1)}, u32[]{:S(2)}, u32[]{:S(2)}) collective-permute-start(bf16[128,640]{1,0:T(8,128)(2,1)S(1)} %collective-permute-done.refs_1_), channel_id=1, source_target_pairs={{0,2},{1,5},{2,6},{3,1},{6,10},{7,3},{10,14},{11,7},{14,12},{15,11... | collective-permute-start | bytes 491528 | tf_op jit(solution)/shard_map/ppermute | solution.py:49
  10.2 2.7 %collective-permute-done.1.refs_2_ = bf16[128,640]{1,0:T(8,128)(2,1)S(1)} collective-permute-done((bf16[128,640]{1,0:T(8,128)(2,1)S(1)}, bf16[128,640]{1,0:T(8,128)(2,1)S(1)}, u32[]{:S(2)}, u32[]{:S(2)}) %collective-permute-start.1) | collective-permute-done | bytes 163872 | tf_op jit(solution)/shard_map/ppermute | solution.py:49
  12.9 2.0 %collective-permute-start.3 = (bf16[128,640]{1,0:T(8,128)(2,1)S(1)}, bf16[128,640]{1,0:T(8,128)(2,1)S(1)}, u32[]{:S(2)}, u32[]{:S(2)}) collective-permute-start(bf16[128,640]{1,0:T(8,128)(2,1)S(1)} %collective-permute-done.1.refs_2_), channel_id=1, source_target_pairs={{0,2},{1,5},{2,6},{3,1},{6,10},{7,3},{10,14},{11,7},{14,12},{15,11... | collective-permute-start | bytes 491528 | tf_op jit(solution)/shard_map/ppermute | solution.py:49
  14.8 3.4 %collective-permute-done.3.refs_3_ = bf16[128,640]{1,0:T(8,128)(2,1)S(1)} collective-permute-done((bf16[128,640]{1,0:T(8,128)(2,1)S(1)}, bf16[128,640]{1,0:T(8,128)(2,1)S(1)}, u32[]{:S(2)}, u32[]{:S(2)}) %collective-permute-start.3) | collective-permute-done | bytes 163872 | tf_op jit(solution)/shard_map/ppermute | solution.py:49
  18.2 2.0 %collective-permute-start.5 = (bf16[128,640]{1,0:T(8,128)(2,1)S(1)}, bf16[128,640]{1,0:T(8,128)(2,1)S(1)}, u32[]{:S(2)}, u32[]{:S(2)}) collective-permute-start(bf16[128,640]{1,0:T(8,128)(2,1)S(1)} %collective-permute-done.3.refs_3_), channel_id=1, source_target_pairs={{0,2},{1,5},{2,6},{3,1},{6,10},{7,3},{10,14},{11,7},{14,12},{15,11... | collective-permute-start | bytes 491528 | tf_op jit(solution)/shard_map/ppermute | solution.py:49
  20.1 3.4 %collective-permute-done.5.refs_4_ = bf16[128,640]{1,0:T(8,128)(2,1)S(1)} collective-permute-done((bf16[128,640]{1,0:T(8,128)(2,1)S(1)}, bf16[128,640]{1,0:T(8,128)(2,1)S(1)}, u32[]{:S(2)}, u32[]{:S(2)}) %collective-permute-start.5) | collective-permute-done | bytes 163872 | tf_op jit(solution)/shard_map/ppermute | solution.py:49
  23.5 5.9 %attend.1 = (bf16[128,2048]{1,0:T(8,128)(2,1)S(1)}, f32[128,2048]{1,0:T(8,128)S(1)}) custom-call(s32[42]{0:T(128)S(1)} %concatenate.10.info, bf16[128,640]{1,0:T(8,128)(2,1)S(1)} %pack.1.refs_0_, bf16[128,640]{1,0:T(8,128)(2,1)S(1)} %collective-permute-done.refs_1_, bf16[128,640]{1,0:T(8,128)(2,1)S(1)} %collective-permute-done.1.refs_2_, ...), custom_call_target="tpu_custom_call" | custom-call | tf_op jit(solution)/shard_map/attend/pallas_call | solution.py:202
  29.5 1.8 %collective-permute-done.7.there_ref = bf16[128,2048]{1,0:T(8,128)(2,1)S(1)} collective-permute-done((bf16[128,2048]{1,0:T(8,128)(2,1)S(1)}, bf16[128,2048]{1,0:T(8,128)(2,1)S(1)}, u32[]{:S(2)}, u32[]{:S(2)}) %collective-permute-start.7) | collective-permute-done | bytes 524320 | tf_op jit(solution)/shard_map/ppermute | solution.py:40
  31.3 0.9 norm.1
  32.2 2.0 %collective-permute-start.9 = (bf16[128,1024]{1,0:T(8,128)(2,1)S(1)}, bf16[128,1024]{1,0:T(8,128)(2,1)S(1)}, u32[]{:S(2)}, u32[]{:S(2)}) collective-permute-start(bf16[128,1024]{1,0:T(8,128)(2,1)S(1)} %get-tuple-element.78.refs_1_), channel_id=1, source_target_pairs={{0,2},{1,5},{2,6},{3,1},{6,10},{7,3},{10,14},{11,7},{14,12},{15,11... | collective-permute-start | bytes 786440 | tf_op jit(solution)/shard_map/ppermute | solution.py:49
  34.2 1.6 %collective-permute-start.8 = (bf16[128,1024]{1,0:T(8,128)(2,1)S(1)}, bf16[128,1024]{1,0:T(8,128)(2,1)S(1)}, u32[]{:S(2)}, u32[]{:S(2)}) collective-permute-start(bf16[128,1024]{1,0:T(8,128)(2,1)S(1)} %get-tuple-element.77.refs_0_), channel_id=1, source_target_pairs={{0,2},{1,5},{2,6},{3,1},{6,10},{7,3},{10,14},{11,7},{14,12},{15,11... | collective-permute-start | bytes 786440 | tf_op jit(solution)/shard_map/ppermute | solution.py:49
  35.8 2.8 %collective-permute-done.9.refs_3_ = bf16[128,1024]{1,0:T(8,128)(2,1)S(1)} collective-permute-done((bf16[128,1024]{1,0:T(8,128)(2,1)S(1)}, bf16[128,1024]{1,0:T(8,128)(2,1)S(1)}, u32[]{:S(2)}, u32[]{:S(2)}) %collective-permute-start.9) | collective-permute-done | bytes 262176 | tf_op jit(solution)/shard_map/ppermute | solution.py:49
  38.6 2.0 %collective-permute-start.12 = (bf16[128,1024]{1,0:T(8,128)(2,1)S(1)}, bf16[128,1024]{1,0:T(8,128)(2,1)S(1)}, u32[]{:S(2)}, u32[]{:S(2)}) collective-permute-start(bf16[128,1024]{1,0:T(8,128)(2,1)S(1)} %collective-permute-done.9.refs_3_), channel_id=1, source_target_pairs={{0,2},{1,5},{2,6},{3,1},{6,10},{7,3},{10,14},{11,7},{14,12},{15,11... | collective-permute-start | bytes 786440 | tf_op jit(solution)/shard_map/ppermute | solution.py:49
  40.6 1.8 %route.1.refs_16_ = bf16[8,128,128]{2,1,0:T(8,128)(2,1)S(1)} custom-call(s32[2]{0:T(128)S(1)} %pad_add_fusion.where, bf16[128,640]{1,0:T(8,128)(2,1)S(1)} %pack.1.refs_0_, bf16[128,640]{1,0:T(8,128)(2,1)S(1)} %collective-permute-done.refs_1_, bf16[128,640]{1,0:T(8,128)(2,1)S(1)} %collective-permute-done.1.refs_2_, ...), custom_call_target="tpu_custom_call" | custom-call | tf_op jit(solution)/shard_map/route/pallas_call | solution.py:246
  42.8 1.4 %collective-permute-start.10 = (bf16[128,1024]{1,0:T(8,128)(2,1)S(1)}, bf16[128,1024]{1,0:T(8,128)(2,1)S(1)}, u32[]{:S(2)}, u32[]{:S(2)}) collective-permute-start(bf16[128,1024]{1,0:T(8,128)(2,1)S(1)} %collective-permute-done.8.refs_2_), channel_id=1, source_target_pairs={{0,2},{1,5},{2,6},{3,1},{6,10},{7,3},{10,14},{11,7},{14,12},{15,11... | collective-permute-start | bytes 786440 | tf_op jit(solution)/shard_map/ppermute | solution.py:49
  44.2 0.8 collective-permute-done.12.refs_5_
  45.0 2.0 %collective-permute-start.16 = (bf16[128,1024]{1,0:T(8,128)(2,1)S(1)}, bf16[128,1024]{1,0:T(8,128)(2,1)S(1)}, u32[]{:S(2)}, u32[]{:S(2)}) collective-permute-start(bf16[128,1024]{1,0:T(8,128)(2,1)S(1)} %collective-permute-done.12.refs_5_), channel_id=1, source_target_pairs={{0,2},{1,5},{2,6},{3,1},{6,10},{7,3},{10,14},{11,7},{14,12},{15,11... | collective-permute-start | bytes 786440 | tf_op jit(solution)/shard_map/ppermute | solution.py:49
  47.0 2.2 %collective-permute-done.10.refs_4_ = bf16[128,1024]{1,0:T(8,128)(2,1)S(1)} collective-permute-done((bf16[128,1024]{1,0:T(8,128)(2,1)S(1)}, bf16[128,1024]{1,0:T(8,128)(2,1)S(1)}, u32[]{:S(2)}, u32[]{:S(2)}) %collective-permute-start.10) | collective-permute-done | bytes 262176 | tf_op jit(solution)/shard_map/ppermute | solution.py:49
  49.2 1.4 %collective-permute-start.14 = (bf16[128,1024]{1,0:T(8,128)(2,1)S(1)}, bf16[128,1024]{1,0:T(8,128)(2,1)S(1)}, u32[]{:S(2)}, u32[]{:S(2)}) collective-permute-start(bf16[128,1024]{1,0:T(8,128)(2,1)S(1)} %collective-permute-done.10.refs_4_), channel_id=1, source_target_pairs={{0,2},{1,5},{2,6},{3,1},{6,10},{7,3},{10,14},{11,7},{14,12},{15,11... | collective-permute-start | bytes 786440 | tf_op jit(solution)/shard_map/ppermute | solution.py:49
  50.6 1.4 %collective-permute-done.16.refs_7_ = bf16[128,1024]{1,0:T(8,128)(2,1)S(1)} collective-permute-done((bf16[128,1024]{1,0:T(8,128)(2,1)S(1)}, bf16[128,1024]{1,0:T(8,128)(2,1)S(1)}, u32[]{:S(2)}, u32[]{:S(2)}) %collective-permute-start.16) | collective-permute-done | bytes 262176 | tf_op jit(solution)/shard_map/ppermute | solution.py:49
  52.0 1.4 %collective-permute-start.20 = (bf16[128,1024]{1,0:T(8,128)(2,1)S(1)}, bf16[128,1024]{1,0:T(8,128)(2,1)S(1)}, u32[]{:S(2)}, u32[]{:S(2)}) collective-permute-start(bf16[128,1024]{1,0:T(8,128)(2,1)S(1)} %collective-permute-done.16.refs_7_), channel_id=1, source_target_pairs={{0,2},{1,5},{2,6},{3,1},{6,10},{7,3},{10,14},{11,7},{14,12},{15,11... | collective-permute-start | bytes 786440 | tf_op jit(solution)/shard_map/ppermute | solution.py:49
  53.4 2.2 %collective-permute-done.14.refs_6_ = bf16[128,1024]{1,0:T(8,128)(2,1)S(1)} collective-permute-done((bf16[128,1024]{1,0:T(8,128)(2,1)S(1)}, bf16[128,1024]{1,0:T(8,128)(2,1)S(1)}, u32[]{:S(2)}, u32[]{:S(2)}) %collective-permute-start.14) | collective-permute-done | bytes 262176 | tf_op jit(solution)/shard_map/ppermute | solution.py:49
  55.6 1.4 %collective-permute-start.18 = (bf16[128,1024]{1,0:T(8,128)(2,1)S(1)}, bf16[128,1024]{1,0:T(8,128)(2,1)S(1)}, u32[]{:S(2)}, u32[]{:S(2)}) collective-permute-start(bf16[128,1024]{1,0:T(8,128)(2,1)S(1)} %collective-permute-done.14.refs_6_), channel_id=1, source_target_pairs={{0,2},{1,5},{2,6},{3,1},{6,10},{7,3},{10,14},{11,7},{14,12},{15,11... | collective-permute-start | bytes 786440 | tf_op jit(solution)/shard_map/ppermute | solution.py:49
  56.9 1.4 %collective-permute-done.20.refs_9_ = bf16[128,1024]{1,0:T(8,128)(2,1)S(1)} collective-permute-done((bf16[128,1024]{1,0:T(8,128)(2,1)S(1)}, bf16[128,1024]{1,0:T(8,128)(2,1)S(1)}, u32[]{:S(2)}, u32[]{:S(2)}) %collective-permute-start.20) | collective-permute-done | bytes 262176 | tf_op jit(solution)/shard_map/ppermute | solution.py:49
  58.4 3.6 %collective-permute-done.18.refs_8_ = bf16[128,1024]{1,0:T(8,128)(2,1)S(1)} collective-permute-done((bf16[128,1024]{1,0:T(8,128)(2,1)S(1)}, bf16[128,1024]{1,0:T(8,128)(2,1)S(1)}, u32[]{:S(2)}, u32[]{:S(2)}) %collective-permute-start.18) | collective-permute-done | bytes 262176 | tf_op jit(solution)/shard_map/ppermute | solution.py:49
  61.9 26.0 %experts.1 = (bf16[128,1024]{1,0:T(8,128)(2,1)S(1)}, bf16[128,1024]{1,0:T(8,128)(2,1)S(1)}, bf16[128,1024]{1,0:T(8,128)(2,1)S(1)}, bf16[128,1024]{1,0:T(8,128)(2...) custom-call(s32[2]{0:T(128)S(1)} %pad_add_fusion.where, ...), custom_call_target="tpu_custom_call" | custom-call | tf_op jit(solution)/shard_map/experts/pallas_call | solution.py:419
  91.1 0.8 collective-permute-done.34
  92.0 0.9 add_convert_fusion.5
  93.0 1.4 %collective-permute-start.35 = (bf16[64,1024]{1,0:T(8,128)(2,1)S(1)}, bf16[64,1024]{1,0:T(8,128)(2,1)S(1)}, u32[]{:S(2)}, u32[]{:S(2)}) collective-permute-start(bf16[64,1024]{1,0:T(8,128)(2,1)S(1)} %add_convert_fusion.5), channel_id=1, source_target_pairs={{0,2},{1,5},{2,6},{3,1},{6,10},{7,3},{10,14},{11,7},{14,12},{15,11... | collective-permute-start | bytes 393224 | tf_op jit(solution)/shard_map/ppermute | solution.py:49
  94.4 3.6 %collective-permute-done.35 = bf16[64,1024]{1,0:T(8,128)(2,1)S(1)} collective-permute-done((bf16[64,1024]{1,0:T(8,128)(2,1)S(1)}, bf16[64,1024]{1,0:T(8,128)(2,1)S(1)}, u32[]{:S(2)}, u32[]{:S(2)}) %collective-permute-start.35) | collective-permute-done | bytes 131104 | tf_op jit(solution)/shard_map/ppermute | solution.py:49
  98.0 1.4 %collective-permute-start.27 = (bf16[64,1024]{1,0:T(8,128)(2,1)S(1)}, bf16[64,1024]{1,0:T(8,128)(2,1)S(1)}, u32[]{:S(2)}, u32[]{:S(2)}) collective-permute-start(bf16[64,1024]{1,0:T(8,128)(2,1)S(1)} %add_convert_fusion.6), channel_id=1, source_target_pairs={{0,2},{1,5},{2,6},{3,1},{6,10},{7,3},{10,14},{11,7},{14,12},{15,11... | collective-permute-start | bytes 393224 | tf_op jit(solution)/shard_map/ppermute | solution.py:49
  99.5 1.6 %collective-permute-start.36 = (bf16[128,1024]{1,0:T(8,128)(2,1)S(1)}, bf16[128,1024]{1,0:T(8,128)(2,1)S(1)}, u32[]{:S(2)}, u32[]{:S(2)}) collective-permute-start(bf16[128,1024]{1,0:T(8,128)(2,1)S(1)} %fusion.1), channel_id=1, source_target_pairs={{0,2},{1,5},{2,6},{3,1},{6,10},{7,3},{10,14},{11,7},{14,12},{15,11... | collective-permute-start | bytes 786440 | tf_op jit(solution)/shard_map/ppermute | solution.py:49
  101.2 1.8 %collective-permute-done.27 = bf16[64,1024]{1,0:T(8,128)(2,1)S(1)} collective-permute-done((bf16[64,1024]{1,0:T(8,128)(2,1)S(1)}, bf16[64,1024]{1,0:T(8,128)(2,1)S(1)}, u32[]{:S(2)}, u32[]{:S(2)}) %collective-permute-start.27) | collective-permute-done | bytes 131104 | tf_op jit(solution)/shard_map/ppermute | solution.py:49
  103.1 1.4 %collective-permute-start.28 = (bf16[128,1024]{1,0:T(8,128)(2,1)S(1)}, bf16[128,1024]{1,0:T(8,128)(2,1)S(1)}, u32[]{:S(2)}, u32[]{:S(2)}) collective-permute-start(bf16[128,1024]{1,0:T(8,128)(2,1)S(1)} %fusion), channel_id=1, source_target_pairs={{0,2},{1,5},{2,6},{3,1},{6,10},{7,3},{10,14},{11,7},{14,12},{15,11... | collective-permute-start | bytes 786440 | tf_op jit(solution)/shard_map/ppermute | solution.py:49
  105.1 0.9 collective-permute-done.36
  106.1 1.6 %collective-permute-start.37 = (bf16[128,1024]{1,0:T(8,128)(2,1)S(1)}, bf16[128,1024]{1,0:T(8,128)(2,1)S(1)}, u32[]{:S(2)}, u32[]{:S(2)}) collective-permute-start(bf16[128,1024]{1,0:T(8,128)(2,1)S(1)} %add_convert_fusion.2), channel_id=1, source_target_pairs={{0,2},{1,5},{2,6},{3,1},{6,10},{7,3},{10,14},{11,7},{14,12},{15,11... | collective-permute-start | bytes 786440 | tf_op jit(solution)/shard_map/ppermute | solution.py:49
  107.7 1.9 %collective-permute-done.28 = bf16[128,1024]{1,0:T(8,128)(2,1)S(1)} collective-permute-done((bf16[128,1024]{1,0:T(8,128)(2,1)S(1)}, bf16[128,1024]{1,0:T(8,128)(2,1)S(1)}, u32[]{:S(2)}, u32[]{:S(2)}) %collective-permute-start.28) | collective-permute-done | bytes 262176 | tf_op jit(solution)/shard_map/ppermute | solution.py:49
  109.7 1.4 %collective-permute-start.29 = (bf16[128,1024]{1,0:T(8,128)(2,1)S(1)}, bf16[128,1024]{1,0:T(8,128)(2,1)S(1)}, u32[]{:S(2)}, u32[]{:S(2)}) collective-permute-start(bf16[128,1024]{1,0:T(8,128)(2,1)S(1)} %add_convert_fusion.4), channel_id=1, source_target_pairs={{0,2},{1,5},{2,6},{3,1},{6,10},{7,3},{10,14},{11,7},{14,12},{15,11... | collective-permute-start | bytes 786440 | tf_op jit(solution)/shard_map/ppermute | solution.py:49
  111.1 1.4 %collective-permute-done.37 = bf16[128,1024]{1,0:T(8,128)(2,1)S(1)} collective-permute-done((bf16[128,1024]{1,0:T(8,128)(2,1)S(1)}, bf16[128,1024]{1,0:T(8,128)(2,1)S(1)}, u32[]{:S(2)}, u32[]{:S(2)}) %collective-permute-start.37) | collective-permute-done | bytes 262176 | tf_op jit(solution)/shard_map/ppermute | solution.py:49
  113.0 3.1 %collective-permute-done.29 = bf16[128,1024]{1,0:T(8,128)(2,1)S(1)} collective-permute-done((bf16[128,1024]{1,0:T(8,128)(2,1)S(1)}, bf16[128,1024]{1,0:T(8,128)(2,1)S(1)}, u32[]{:S(2)}, u32[]{:S(2)}) %collective-permute-start.29) | collective-permute-done | bytes 262176 | tf_op jit(solution)/shard_map/ppermute | solution.py:49
  116.3 1.4 %collective-permute-start.30 = (bf16[128,1024]{1,0:T(8,128)(2,1)S(1)}, bf16[128,1024]{1,0:T(8,128)(2,1)S(1)}, u32[]{:S(2)}, u32[]{:S(2)}) collective-permute-start(bf16[128,1024]{1,0:T(8,128)(2,1)S(1)} %add_convert_fusion.3), channel_id=1, source_target_pairs={{0,2},{1,5},{2,6},{3,1},{6,10},{7,3},{10,14},{11,7},{14,12},{15,11... | collective-permute-start | bytes 786440 | tf_op jit(solution)/shard_map/ppermute | solution.py:49
  117.7 0.8 collective-permute-done.38
  118.5 4.2 %collective-permute-done.30 = bf16[128,1024]{1,0:T(8,128)(2,1)S(1)} collective-permute-done((bf16[128,1024]{1,0:T(8,128)(2,1)S(1)}, bf16[128,1024]{1,0:T(8,128)(2,1)S(1)}, u32[]{:S(2)}, u32[]{:S(2)}) %collective-permute-start.30) | collective-permute-done | bytes 262176 | tf_op jit(solution)/shard_map/ppermute | solution.py:49
  122.7 0.9 add_convert_fusion
  (56 shorter events, 6.9 us)
Async XLA Ops:
  1.1 6.4 %collective-permute-start = (bf16[128,640]{1,0:T(8,128)(2,1)S(1)}, bf16[128,640]{1,0:T(8,128)(2,1)S(1)}, u32[]{:S(2)}, u32[]{:S(2)}) collective-permute-start(bf16[128,640]{1,0:T(8,128)(2,1)S(1)} %pack.1.refs_0_), channel_id=1, source_target_pairs={{0,2},{1,5},{2,6},{3,1},{6,10},{7,3},{10,14},{11,7},{14,12},{15,11... | collective-permute-start | bytes 491528 | tf_op jit(solution)/shard_map/ppermute | solution.py:49
  7.5 2.7 %collective-permute-start.2 = (bf16[128,640]{1,0:T(8,128)(2,1)S(1)}, bf16[128,640]{1,0:T(8,128)(2,1)S(1)}, u32[]{:S(2)}, u32[]{:S(2)}) collective-permute-start(bf16[128,640]{1,0:T(8,128)(2,1)S(1)} %collective-permute-done.refs_1_), channel_id=1, source_target_pairs={{0,1},{1,0},{2,3},{3,2},{4,5},{5,4},{6,7},{7,6},{8,9},{9,8},{10,11... | collective-permute-start | bytes 491528 | tf_op jit(solution)/shard_map/ppermute | solution.py:40
  7.5 5.3 %collective-permute-start.1 = (bf16[128,640]{1,0:T(8,128)(2,1)S(1)}, bf16[128,640]{1,0:T(8,128)(2,1)S(1)}, u32[]{:S(2)}, u32[]{:S(2)}) collective-permute-start(bf16[128,640]{1,0:T(8,128)(2,1)S(1)} %collective-permute-done.refs_1_), channel_id=1, source_target_pairs={{0,2},{1,5},{2,6},{3,1},{6,10},{7,3},{10,14},{11,7},{14,12},{15,11... | collective-permute-start | bytes 491528 | tf_op jit(solution)/shard_map/ppermute | solution.py:49
  12.9 2.0 %collective-permute-start.4 = (bf16[128,640]{1,0:T(8,128)(2,1)S(1)}, bf16[128,640]{1,0:T(8,128)(2,1)S(1)}, u32[]{:S(2)}, u32[]{:S(2)}) collective-permute-start(bf16[128,640]{1,0:T(8,128)(2,1)S(1)} %collective-permute-done.1.refs_2_), channel_id=1, source_target_pairs={{0,1},{1,0},{2,3},{3,2},{4,5},{5,4},{6,7},{7,6},{8,9},{9,8},{10,11... | collective-permute-start | bytes 491528 | tf_op jit(solution)/shard_map/ppermute | solution.py:40
  12.9 5.3 %collective-permute-start.3 = (bf16[128,640]{1,0:T(8,128)(2,1)S(1)}, bf16[128,640]{1,0:T(8,128)(2,1)S(1)}, u32[]{:S(2)}, u32[]{:S(2)}) collective-permute-start(bf16[128,640]{1,0:T(8,128)(2,1)S(1)} %collective-permute-done.1.refs_2_), channel_id=1, source_target_pairs={{0,2},{1,5},{2,6},{3,1},{6,10},{7,3},{10,14},{11,7},{14,12},{15,11... | collective-permute-start | bytes 491528 | tf_op jit(solution)/shard_map/ppermute | solution.py:49
  18.2 2.0 %collective-permute-start.6 = (bf16[128,640]{1,0:T(8,128)(2,1)S(1)}, bf16[128,640]{1,0:T(8,128)(2,1)S(1)}, u32[]{:S(2)}, u32[]{:S(2)}) collective-permute-start(bf16[128,640]{1,0:T(8,128)(2,1)S(1)} %collective-permute-done.3.refs_3_), channel_id=1, source_target_pairs={{0,1},{1,0},{2,3},{3,2},{4,5},{5,4},{6,7},{7,6},{8,9},{9,8},{10,11... | collective-permute-start | bytes 491528 | tf_op jit(solution)/shard_map/ppermute | solution.py:40
  18.2 5.3 %collective-permute-start.5 = (bf16[128,640]{1,0:T(8,128)(2,1)S(1)}, bf16[128,640]{1,0:T(8,128)(2,1)S(1)}, u32[]{:S(2)}, u32[]{:S(2)}) collective-permute-start(bf16[128,640]{1,0:T(8,128)(2,1)S(1)} %collective-permute-done.3.refs_3_), channel_id=1, source_target_pairs={{0,2},{1,5},{2,6},{3,1},{6,10},{7,3},{10,14},{11,7},{14,12},{15,11... | collective-permute-start | bytes 491528 | tf_op jit(solution)/shard_map/ppermute | solution.py:49
  29.4 2.0 %collective-permute-start.7 = (bf16[128,2048]{1,0:T(8,128)(2,1)S(1)}, bf16[128,2048]{1,0:T(8,128)(2,1)S(1)}, u32[]{:S(2)}, u32[]{:S(2)}) collective-permute-start(bf16[128,2048]{1,0:T(8,128)(2,1)S(1)} %get-tuple-element.74), channel_id=1, source_target_pairs={{0,1},{1,0},{2,3},{3,2},{4,5},{5,4},{6,7},{7,6},{8,9},{9,8},{10,11... | collective-permute-start | bytes 1572872 | tf_op jit(solution)/shard_map/ppermute | solution.py:40
  32.2 6.4 %collective-permute-start.9 = (bf16[128,1024]{1,0:T(8,128)(2,1)S(1)}, bf16[128,1024]{1,0:T(8,128)(2,1)S(1)}, u32[]{:S(2)}, u32[]{:S(2)}) collective-permute-start(bf16[128,1024]{1,0:T(8,128)(2,1)S(1)} %get-tuple-element.78.refs_1_), channel_id=1, source_target_pairs={{0,2},{1,5},{2,6},{3,1},{6,10},{7,3},{10,14},{11,7},{14,12},{15,11... | collective-permute-start | bytes 786440 | tf_op jit(solution)/shard_map/ppermute | solution.py:49
  34.2 8.2 %collective-permute-start.8 = (bf16[128,1024]{1,0:T(8,128)(2,1)S(1)}, bf16[128,1024]{1,0:T(8,128)(2,1)S(1)}, u32[]{:S(2)}, u32[]{:S(2)}) collective-permute-start(bf16[128,1024]{1,0:T(8,128)(2,1)S(1)} %get-tuple-element.77.refs_0_), channel_id=1, source_target_pairs={{0,2},{1,5},{2,6},{3,1},{6,10},{7,3},{10,14},{11,7},{14,12},{15,11... | collective-permute-start | bytes 786440 | tf_op jit(solution)/shard_map/ppermute | solution.py:49
  38.6 5.5 %collective-permute-start.13 = (bf16[128,1024]{1,0:T(8,128)(2,1)S(1)}, bf16[128,1024]{1,0:T(8,128)(2,1)S(1)}, u32[]{:S(2)}, u32[]{:S(2)}) collective-permute-start(bf16[128,1024]{1,0:T(8,128)(2,1)S(1)} %collective-permute-done.9.refs_3_), channel_id=1, source_target_pairs={{0,1},{1,0},{2,3},{3,2},{4,5},{5,4},{6,7},{7,6},{8,9},{9,8},{10,11... | collective-permute-start | bytes 786440 | tf_op jit(solution)/shard_map/ppermute | solution.py:40
  38.6 6.4 %collective-permute-start.12 = (bf16[128,1024]{1,0:T(8,128)(2,1)S(1)}, bf16[128,1024]{1,0:T(8,128)(2,1)S(1)}, u32[]{:S(2)}, u32[]{:S(2)}) collective-permute-start(bf16[128,1024]{1,0:T(8,128)(2,1)S(1)} %collective-permute-done.9.refs_3_), channel_id=1, source_target_pairs={{0,2},{1,5},{2,6},{3,1},{6,10},{7,3},{10,14},{11,7},{14,12},{15,11... | collective-permute-start | bytes 786440 | tf_op jit(solution)/shard_map/ppermute | solution.py:49
  42.5 4.5 %collective-permute-start.11 = (bf16[128,1024]{1,0:T(8,128)(2,1)S(1)}, bf16[128,1024]{1,0:T(8,128)(2,1)S(1)}, u32[]{:S(2)}, u32[]{:S(2)}) collective-permute-start(bf16[128,1024]{1,0:T(8,128)(2,1)S(1)} %collective-permute-done.8.refs_2_), channel_id=1, source_target_pairs={{0,1},{1,0},{2,3},{3,2},{4,5},{5,4},{6,7},{7,6},{8,9},{9,8},{10,11... | collective-permute-start | bytes 786440 | tf_op jit(solution)/shard_map/ppermute | solution.py:40
  42.8 6.4 %collective-permute-start.10 = (bf16[128,1024]{1,0:T(8,128)(2,1)S(1)}, bf16[128,1024]{1,0:T(8,128)(2,1)S(1)}, u32[]{:S(2)}, u32[]{:S(2)}) collective-permute-start(bf16[128,1024]{1,0:T(8,128)(2,1)S(1)} %collective-permute-done.8.refs_2_), channel_id=1, source_target_pairs={{0,2},{1,5},{2,6},{3,1},{6,10},{7,3},{10,14},{11,7},{14,12},{15,11... | collective-permute-start | bytes 786440 | tf_op jit(solution)/shard_map/ppermute | solution.py:49
  45.0 5.5 %collective-permute-start.17 = (bf16[128,1024]{1,0:T(8,128)(2,1)S(1)}, bf16[128,1024]{1,0:T(8,128)(2,1)S(1)}, u32[]{:S(2)}, u32[]{:S(2)}) collective-permute-start(bf16[128,1024]{1,0:T(8,128)(2,1)S(1)} %collective-permute-done.12.refs_5_), channel_id=1, source_target_pairs={{0,1},{1,0},{2,3},{3,2},{4,5},{5,4},{6,7},{7,6},{8,9},{9,8},{10,11... | collective-permute-start | bytes 786440 | tf_op jit(solution)/shard_map/ppermute | solution.py:40
  45.0 7.0 %collective-permute-start.16 = (bf16[128,1024]{1,0:T(8,128)(2,1)S(1)}, bf16[128,1024]{1,0:T(8,128)(2,1)S(1)}, u32[]{:S(2)}, u32[]{:S(2)}) collective-permute-start(bf16[128,1024]{1,0:T(8,128)(2,1)S(1)} %collective-permute-done.12.refs_5_), channel_id=1, source_target_pairs={{0,2},{1,5},{2,6},{3,1},{6,10},{7,3},{10,14},{11,7},{14,12},{15,11... | collective-permute-start | bytes 786440 | tf_op jit(solution)/shard_map/ppermute | solution.py:49
  49.2 4.2 %collective-permute-start.15 = (bf16[128,1024]{1,0:T(8,128)(2,1)S(1)}, bf16[128,1024]{1,0:T(8,128)(2,1)S(1)}, u32[]{:S(2)}, u32[]{:S(2)}) collective-permute-start(bf16[128,1024]{1,0:T(8,128)(2,1)S(1)} %collective-permute-done.10.refs_4_), channel_id=1, source_target_pairs={{0,1},{1,0},{2,3},{3,2},{4,5},{5,4},{6,7},{7,6},{8,9},{9,8},{10,11... | collective-permute-start | bytes 786440 | tf_op jit(solution)/shard_map/ppermute | solution.py:40
  49.2 6.4 %collective-permute-start.14 = (bf16[128,1024]{1,0:T(8,128)(2,1)S(1)}, bf16[128,1024]{1,0:T(8,128)(2,1)S(1)}, u32[]{:S(2)}, u32[]{:S(2)}) collective-permute-start(bf16[128,1024]{1,0:T(8,128)(2,1)S(1)} %collective-permute-done.10.refs_4_), channel_id=1, source_target_pairs={{0,2},{1,5},{2,6},{3,1},{6,10},{7,3},{10,14},{11,7},{14,12},{15,11... | collective-permute-start | bytes 786440 | tf_op jit(solution)/shard_map/ppermute | solution.py:49
  52.0 4.9 %collective-permute-start.21 = (bf16[128,1024]{1,0:T(8,128)(2,1)S(1)}, bf16[128,1024]{1,0:T(8,128)(2,1)S(1)}, u32[]{:S(2)}, u32[]{:S(2)}) collective-permute-start(bf16[128,1024]{1,0:T(8,128)(2,1)S(1)} %collective-permute-done.16.refs_7_), channel_id=1, source_target_pairs={{0,1},{1,0},{2,3},{3,2},{4,5},{5,4},{6,7},{7,6},{8,9},{9,8},{10,11... | collective-permute-start | bytes 786440 | tf_op jit(solution)/shard_map/ppermute | solution.py:40
  52.0 6.4 %collective-permute-start.20 = (bf16[128,1024]{1,0:T(8,128)(2,1)S(1)}, bf16[128,1024]{1,0:T(8,128)(2,1)S(1)}, u32[]{:S(2)}, u32[]{:S(2)}) collective-permute-start(bf16[128,1024]{1,0:T(8,128)(2,1)S(1)} %collective-permute-done.16.refs_7_), channel_id=1, source_target_pairs={{0,2},{1,5},{2,6},{3,1},{6,10},{7,3},{10,14},{11,7},{14,12},{15,11... | collective-permute-start | bytes 786440 | tf_op jit(solution)/shard_map/ppermute | solution.py:49
  55.6 2.8 %collective-permute-start.19 = (bf16[128,1024]{1,0:T(8,128)(2,1)S(1)}, bf16[128,1024]{1,0:T(8,128)(2,1)S(1)}, u32[]{:S(2)}, u32[]{:S(2)}) collective-permute-start(bf16[128,1024]{1,0:T(8,128)(2,1)S(1)} %collective-permute-done.14.refs_6_), channel_id=1, source_target_pairs={{0,1},{1,0},{2,3},{3,2},{4,5},{5,4},{6,7},{7,6},{8,9},{9,8},{10,11... | collective-permute-start | bytes 786440 | tf_op jit(solution)/shard_map/ppermute | solution.py:40
  55.6 6.4 %collective-permute-start.18 = (bf16[128,1024]{1,0:T(8,128)(2,1)S(1)}, bf16[128,1024]{1,0:T(8,128)(2,1)S(1)}, u32[]{:S(2)}, u32[]{:S(2)}) collective-permute-start(bf16[128,1024]{1,0:T(8,128)(2,1)S(1)} %collective-permute-done.14.refs_6_), channel_id=1, source_target_pairs={{0,2},{1,5},{2,6},{3,1},{6,10},{7,3},{10,14},{11,7},{14,12},{15,11... | collective-permute-start | bytes 786440 | tf_op jit(solution)/shard_map/ppermute | solution.py:49
  87.9 0.7 copy-start
  88.6 0.7 copy-start.1
  89.4 0.7 copy-start.2
  90.1 1.8 %collective-permute-start.34 = (bf16[64,1024]{1,0:T(8,128)(2,1)}, bf16[64,1024]{1,0:T(8,128)(2,1)}, u32[]{:S(2)}, u32[]{:S(2)}) collective-permute-start(bf16[64,1024]{1,0:T(8,128)(2,1)} %get-tuple-element.118), channel_id=1, source_target_pairs={{0,1},{1,0},{2,3},{3,2},{4,5},{5,4},{6,7},{7,6},{8,9},{9,8},{10,11... | collective-permute-start | bytes 393224 | tf_op jit(solution)/shard_map/ppermute | solution.py:40
  90.1 2.9 %collective-permute-start.26 = (bf16[64,1024]{1,0:T(8,128)(2,1)S(1)}, bf16[64,1024]{1,0:T(8,128)(2,1)S(1)}, u32[]{:S(2)}, u32[]{:S(2)}) collective-permute-start(bf16[64,1024]{1,0:T(8,128)(2,1)S(1)} %get-tuple-element.110), channel_id=1, source_target_pairs={{0,1},{1,0},{2,3},{3,2},{4,5},{5,4},{6,7},{7,6},{8,9},{9,8},{10,11... | collective-permute-start | bytes 393224 | tf_op jit(solution)/shard_map/ppermute | solution.py:40
  90.6 17.1 %collective-permute-start.24 = (bf16[128,1024]{1,0:T(8,128)(2,1)S(1)}, bf16[128,1024]{1,0:T(8,128)(2,1)S(1)}, u32[]{:S(2)}, u32[]{:S(2)}) collective-permute-start(bf16[128,1024]{1,0:T(8,128)(2,1)S(1)} %get-tuple-element.106), channel_id=1, source_target_pairs={{0,1},{1,0},{2,3},{3,2},{4,5},{5,4},{6,7},{7,6},{8,9},{9,8},{10,11... | collective-permute-start | bytes 786440 | tf_op jit(solution)/shard_map/ppermute | solution.py:40
  90.6 12.5 %collective-permute-start.25 = (bf16[128,1024]{1,0:T(8,128)(2,1)}, bf16[128,1024]{1,0:T(8,128)(2,1)S(1)}, u32[]{:S(2)}, u32[]{:S(2)}) collective-permute-start(bf16[128,1024]{1,0:T(8,128)(2,1)} %copy-done.1), channel_id=1, source_target_pairs={{0,1},{1,0},{2,3},{3,2},{4,5},{5,4},{6,7},{7,6},{8,9},{9,8},{10,11... | collective-permute-start | bytes 786440 | tf_op jit(solution)/shard_map/ppermute | solution.py:40
  91.1 13.5 %collective-permute-start.32 = (bf16[128,1024]{1,0:T(8,128)(2,1)}, bf16[128,1024]{1,0:T(8,128)(2,1)S(1)}, u32[]{:S(2)}, u32[]{:S(2)}) collective-permute-start(bf16[128,1024]{1,0:T(8,128)(2,1)} %copy-done), channel_id=1, source_target_pairs={{0,1},{1,0},{2,3},{3,2},{4,5},{5,4},{6,7},{7,6},{8,9},{9,8},{10,11... | collective-permute-start | bytes 786440 | tf_op jit(solution)/shard_map/ppermute | solution.py:40
  91.9 7.5 %collective-permute-start.33 = (bf16[128,1024]{1,0:T(8,128)(2,1)}, bf16[128,1024]{1,0:T(8,128)(2,1)S(1)}, u32[]{:S(2)}, u32[]{:S(2)}) collective-permute-start(bf16[128,1024]{1,0:T(8,128)(2,1)} %copy-done.2), channel_id=1, source_target_pairs={{0,1},{1,0},{2,3},{3,2},{4,5},{5,4},{6,7},{7,6},{8,9},{9,8},{10,11... | collective-permute-start | bytes 786440 | tf_op jit(solution)/shard_map/ppermute | solution.py:40
  93.0 5.0 %collective-permute-start.35 = (bf16[64,1024]{1,0:T(8,128)(2,1)S(1)}, bf16[64,1024]{1,0:T(8,128)(2,1)S(1)}, u32[]{:S(2)}, u32[]{:S(2)}) collective-permute-start(bf16[64,1024]{1,0:T(8,128)(2,1)S(1)} %add_convert_fusion.5), channel_id=1, source_target_pairs={{0,2},{1,5},{2,6},{3,1},{6,10},{7,3},{10,14},{11,7},{14,12},{15,11... | collective-permute-start | bytes 393224 | tf_op jit(solution)/shard_map/ppermute | solution.py:49
  98.0 5.0 %collective-permute-start.27 = (bf16[64,1024]{1,0:T(8,128)(2,1)S(1)}, bf16[64,1024]{1,0:T(8,128)(2,1)S(1)}, u32[]{:S(2)}, u32[]{:S(2)}) collective-permute-start(bf16[64,1024]{1,0:T(8,128)(2,1)S(1)} %add_convert_fusion.6), channel_id=1, source_target_pairs={{0,2},{1,5},{2,6},{3,1},{6,10},{7,3},{10,14},{11,7},{14,12},{15,11... | collective-permute-start | bytes 393224 | tf_op jit(solution)/shard_map/ppermute | solution.py:49
  99.5 6.4 %collective-permute-start.36 = (bf16[128,1024]{1,0:T(8,128)(2,1)S(1)}, bf16[128,1024]{1,0:T(8,128)(2,1)S(1)}, u32[]{:S(2)}, u32[]{:S(2)}) collective-permute-start(bf16[128,1024]{1,0:T(8,128)(2,1)S(1)} %fusion.1), channel_id=1, source_target_pairs={{0,2},{1,5},{2,6},{3,1},{6,10},{7,3},{10,14},{11,7},{14,12},{15,11... | collective-permute-start | bytes 786440 | tf_op jit(solution)/shard_map/ppermute | solution.py:49
  103.1 6.4 %collective-permute-start.28 = (bf16[128,1024]{1,0:T(8,128)(2,1)S(1)}, bf16[128,1024]{1,0:T(8,128)(2,1)S(1)}, u32[]{:S(2)}, u32[]{:S(2)}) collective-permute-start(bf16[128,1024]{1,0:T(8,128)(2,1)S(1)} %fusion), channel_id=1, source_target_pairs={{0,2},{1,5},{2,6},{3,1},{6,10},{7,3},{10,14},{11,7},{14,12},{15,11... | collective-permute-start | bytes 786440 | tf_op jit(solution)/shard_map/ppermute | solution.py:49
  104.6 8.4 %collective-permute-start.23 = (bf16[128,1024]{1,0:T(8,128)(2,1)S(1)}, bf16[128,1024]{1,0:T(8,128)(2,1)S(1)}, u32[]{:S(2)}, u32[]{:S(2)}) collective-permute-start(bf16[128,1024]{1,0:T(8,128)(2,1)S(1)} %get-tuple-element.104), channel_id=1, source_target_pairs={{0,1},{1,0},{2,3},{3,2},{4,5},{5,4},{6,7},{7,6},{8,9},{9,8},{10,11... | collective-permute-start | bytes 786440 | tf_op jit(solution)/shard_map/ppermute | solution.py:40
  104.6 6.6 %collective-permute-start.31 = (bf16[128,1024]{1,0:T(8,128)(2,1)S(1)}, bf16[128,1024]{1,0:T(8,128)(2,1)S(1)}, u32[]{:S(2)}, u32[]{:S(2)}) collective-permute-start(bf16[128,1024]{1,0:T(8,128)(2,1)S(1)} %get-tuple-element.112), channel_id=1, source_target_pairs={{0,1},{1,0},{2,3},{3,2},{4,5},{5,4},{6,7},{7,6},{8,9},{9,8},{10,11... | collective-permute-start | bytes 786440 | tf_op jit(solution)/shard_map/ppermute | solution.py:40
  106.1 6.4 %collective-permute-start.37 = (bf16[128,1024]{1,0:T(8,128)(2,1)S(1)}, bf16[128,1024]{1,0:T(8,128)(2,1)S(1)}, u32[]{:S(2)}, u32[]{:S(2)}) collective-permute-start(bf16[128,1024]{1,0:T(8,128)(2,1)S(1)} %add_convert_fusion.2), channel_id=1, source_target_pairs={{0,2},{1,5},{2,6},{3,1},{6,10},{7,3},{10,14},{11,7},{14,12},{15,11... | collective-permute-start | bytes 786440 | tf_op jit(solution)/shard_map/ppermute | solution.py:49
  109.7 6.4 %collective-permute-start.29 = (bf16[128,1024]{1,0:T(8,128)(2,1)S(1)}, bf16[128,1024]{1,0:T(8,128)(2,1)S(1)}, u32[]{:S(2)}, u32[]{:S(2)}) collective-permute-start(bf16[128,1024]{1,0:T(8,128)(2,1)S(1)} %add_convert_fusion.4), channel_id=1, source_target_pairs={{0,2},{1,5},{2,6},{3,1},{6,10},{7,3},{10,14},{11,7},{14,12},{15,11... | collective-permute-start | bytes 786440 | tf_op jit(solution)/shard_map/ppermute | solution.py:49
  111.1 6.6 %collective-permute-start.22 = (bf16[128,1024]{1,0:T(8,128)(2,1)S(1)}, bf16[128,1024]{1,0:T(8,128)(2,1)S(1)}, u32[]{:S(2)}, u32[]{:S(2)}) collective-permute-start(bf16[128,1024]{1,0:T(8,128)(2,1)S(1)} %get-tuple-element.102), channel_id=1, source_target_pairs={{0,1},{1,0},{2,3},{3,2},{4,5},{5,4},{6,7},{7,6},{8,9},{9,8},{10,11... | collective-permute-start | bytes 786440 | tf_op jit(solution)/shard_map/ppermute | solution.py:40
  112.6 5.9 %collective-permute-start.38 = (bf16[128,1024]{1,0:T(8,128)(2,1)S(1)}, bf16[128,1024]{1,0:T(8,128)(2,1)S(1)}, u32[]{:S(2)}, u32[]{:S(2)}) collective-permute-start(bf16[128,1024]{1,0:T(8,128)(2,1)S(1)} %add_convert_fusion.1), channel_id=1, source_target_pairs={{0,3},{1,4},{2,7},{3,0},{6,11},{7,2},{10,15},{11,6},{14,13},{15,10... | collective-permute-start | bytes 786440 | tf_op jit(solution)/shard_map/ppermute | solution.py:49
  116.3 6.4 %collective-permute-start.30 = (bf16[128,1024]{1,0:T(8,128)(2,1)S(1)}, bf16[128,1024]{1,0:T(8,128)(2,1)S(1)}, u32[]{:S(2)}, u32[]{:S(2)}) collective-permute-start(bf16[128,1024]{1,0:T(8,128)(2,1)S(1)} %add_convert_fusion.3), channel_id=1, source_target_pairs={{0,2},{1,5},{2,6},{3,1},{6,10},{7,3},{10,14},{11,7},{14,12},{15,11... | collective-permute-start | bytes 786440 | tf_op jit(solution)/shard_map/ppermute | solution.py:49

commit v12 on v11

--- a/solution.py
+++ b/solution.py
@@ -19,7 +19,7 @@
 WIDE = 640
 MIB = 1024 * 1024
 VMEM_LIMIT = 50 * MIB
-DEPTH = 3
+HELD = 7
 PIECES = 2
 SWAP = [(0, 1), (1, 0)]
 PARTS = 2
@@ -90,22 +90,27 @@
 def reduce(parts, side, count):
     middle = count // 2
     near, far = 0, 1
-    sums = [None, None]
-    given = {}
-    for d in range(middle, 0, -1):
+    sums = [swap(parts[1 - stream][middle][1]) for stream in (near, far)]
+    given = [swap(parts[1 - stream][middle - 1]) for stream in (near, far)]
+    for stream in (near, far):
+        first = summed([parts[stream][middle][0], sums[stream]]).astype(jnp.bfloat16)
+        sums[stream] = turn(first, count)
+    for d in range(middle - 1, 0, -1):
         for stream in (near, far):
-            mine = parts[1 - stream][d]
-            given[stream, d] = swap(mine[1] if d == middle else mine)
-    for stream in (near, far):
-        first = summed([parts[stream][middle][0], given[stream, middle]]).astype(jnp.bfloat16)
-        first = turn(first, count).astype(jnp.float32)
-        nothing = jnp.zeros_like(first)
-        running = jnp.concatenate([jnp.where(side == 0, first, nothing), jnp.where(side == 0, nothing, first)], axis=0)
-        for d in range(middle - 1, 0, -1):
-            total = (summed([parts[stream][middle + d], given[stream, d]]) + running).astype(jnp.bfloat16)
-            running = turn(total, count, cross=d == 1 and stream == far).astype(jnp.float32)
-        sums[stream] = running
-    return summed([parts[near][0], swap(parts[far][0])]) + sums[near] + sums[far]
+            arrived = sums[stream]
+            later = parts[1 - stream][d - 1] if d > 1 or stream == near else ()
+            arrived, later = lax.optimization_barrier((arrived, later))
+            running = arrived.astype(jnp.float32)
+            if d == middle - 1:
+                nothing = jnp.zeros_like(running)
+                running = jnp.concatenate(
+                    [jnp.where(side == 0, running, nothing), jnp.where(side == 0, nothing, running)], axis=0
+                )
+            total = (summed([parts[stream][middle + d], given[stream]]) + running).astype(jnp.bfloat16)
+            sums[stream] = turn(total, count, cross=d == 1 and stream == far)
+            if d > 1 or stream == near:
+                given[stream] = swap(later)
+    return summed([parts[near][0], given[near], sums[near], sums[far]])
 
 
 def attend_kernel(count, blocks, heads, info, *refs):
@@ -312,17 +317,20 @@
     )(*(pltpu.with_memory_space_constraint(x, pltpu.HBM) for x in arrays))
 
 
-def expert_rows(rows, gate_ref, up_ref, down_ref):
+def expert_hidden(rows, gate, up):
     by_columns = (((1,), (1,)), ((), ()))
-    gate = lax.dot_general(gate_ref[...], rows, by_columns, preferred_element_type=jnp.float32)
-    upper = lax.dot_general(up_ref[...], rows, by_columns, preferred_element_type=jnp.float32)
-    hidden = (gate / (1.0 + jnp.exp(-gate)) * upper).astype(jnp.bfloat16)
+    gate = lax.dot_general(gate, rows, by_columns, preferred_element_type=jnp.float32)
+    upper = lax.dot_general(up, rows, by_columns, preferred_element_type=jnp.float32)
+    return (gate / (1.0 + jnp.exp(-gate)) * upper).astype(jnp.bfloat16)
+
+
+def expert_down(hidden, down):
     by_rows = (((0,), (0,)), ((), ()))
-    return lax.dot_general(hidden, down_ref[...], by_rows, preferred_element_type=jnp.float32).astype(jnp.bfloat16)
+    return lax.dot_general(hidden, down, by_rows, preferred_element_type=jnp.float32).astype(jnp.bfloat16)
 
 
 def plain_kernel(where, rows_ref, gate_ref, up_ref, down_ref, out_ref):
-    out_ref[0] = expert_rows(rows_ref[0], gate_ref.at[0], up_ref.at[0], down_ref.at[0])
+    out_ref[0] = expert_down(expert_hidden(rows_ref[0], gate_ref[0], up_ref[0]), down_ref[0])
 
 
 def fused_kernel(count, where, *refs):
@@ -330,23 +338,31 @@
     blocks, combine_ref, weights = refs[:at], refs[at], refs[at + 1 : at + 4]
     near, far = refs[at + 4 : at + 5 + count], refs[at + 5 + count : at + 6 + 2 * count]
     at += 6 + 2 * count
-    picked, buffers, sems = refs[at], refs[at + 1 : at + 4], refs[at + 4]
+    picked, buffer, sems = refs[at : at + 3]
     here = picked.shape[0]
-    depth, units, width = buffers[0].shape
+    slots, units, width = buffer.shape
     side = where[1]
     piece = units // PIECES
     middle = count // 2
     by_rows = (((0,), (0,)), ((), ()))
 
-    def copies(expert, slot):
-        for w in range(3):
-            for i in range(PIECES):
-                rows = pl.ds(i * piece, piece)
-                yield pltpu.make_async_copy(weights[w].at[expert, rows], buffers[w].at[slot, rows], sems.at[slot, w, i])
-
-    for e in range(depth):
-        for copy in copies(e, e):
+    def copies(expert, w):
+        slot = lax.rem(3 * expert + w, slots)
+        for i in range(PIECES):
+            rows = pl.ds(i * piece, piece)
+            yield pltpu.make_async_copy(weights[w].at[expert, rows], buffer.at[slot, rows], sems.at[slot, i])
+
+    def start(expert, w):
+        for copy in copies(expert, w):
             copy.start()
+
+    def arrived(expert, w):
+        for copy in copies(expert, w):
+            copy.wait()
+        return buffer[lax.rem(3 * expert + w, slots)]
+
+    for i in range(slots):
+        start(i // 3, i % 3)
 
     for c in range(count):
         pick = (combine_ref[c].astype(jnp.float32) > 0).astype(jnp.float32).astype(jnp.bfloat16)
@@ -358,15 +374,18 @@
                 picked[e, c * SLOTS : (c + 1) * SLOTS, columns] = rows[e * SLOTS : (e + 1) * SLOTS]
 
     def work(expert, _):
-        slot = lax.rem(expert, depth)
-        for copy in copies(expert, slot):
-            copy.wait()
-        picked[expert] = expert_rows(picked[expert], *(buffer.at[slot] for buffer in buffers))
-
-        @pl.when(expert + depth < here)
+        hidden = expert_hidden(picked[expert], arrived(expert, 0), arrived(expert, 1))
+
+        @pl.when(expert + slots // 3 < here)
         def _():
-            for copy in copies(expert + depth, slot):
-                copy.start()
+            start(expert + slots // 3, 1)
+            start(expert + slots // 3, 2)
+
+        picked[expert] = expert_down(hidden, arrived(expert, 2))
+
+        @pl.when(expert + slots // 3 + 1 < here)
+        def _():
+            start(expert + slots // 3 + 1, 0)
 
         return 0
 
@@ -412,7 +431,6 @@
     count, local = len(found), found[0][0].shape[0]
     here, units, width = w_gate.shape
     rows = count * SLOTS
-    depth = min(DEPTH, here)
     middle = count // 2
     sizes = [local // 2 if c in (middle, count) else local for c in range(count + 1)]
     whole = pl.BlockSpec(memory_space=pltpu.VMEM)
@@ -423,10 +441,9 @@
         + [pl.BlockSpec(memory_space=pltpu.HBM)] * 3,
         out_specs=[whole] * (2 * count + 2),
         scratch_shapes=[pltpu.VMEM((here, rows, width), jnp.bfloat16)]
-        + [pltpu.VMEM((depth, units, width), jnp.bfloat16)] * 3
-        + [pltpu.SemaphoreType.DMA((depth, 3, PIECES))],
+        + [pltpu.VMEM((HELD, units, width), jnp.bfloat16), pltpu.SemaphoreType.DMA((HELD, PIECES))],
         out_shape=[pltpu.VMEM((size, width // 2), jnp.bfloat16) for size in sizes] * 2,
-        compiler_params=pltpu.CompilerParams(vmem_limit_bytes=36 * MIB),
+        compiler_params=pltpu.CompilerParams(vmem_limit_bytes=29 * MIB),
         name="experts",
     )(where, *(x for block in found for x in block), combine,
       *(pltpu.with_memory_space_constraint(w, pltpu.HBM) for w in (w_gate, w_up, w_down)))
@@ -464,8 +481,6 @@
     beside = [(scalars, (span_order, seg_lengths)), (lambda gain: gain.reshape(1, width), (norm_gain,))]
     found, (info, gain) = gather(packed, count, beside)
     partial, summand = attend(info, found, queries, kv_up, out_proj, residual, count)
-    middle, *normed = norm(where, summand, swap(partial), gain)
-
     def place_rows(*blocks):
         if few:
             return route(where, blocks, here)
@@ -481,9 +496,12 @@
         combine = jnp.where(rank[:, :, :, None] == slot, share[:, :, :, None], 0.0)
         return combine.astype(jnp.bfloat16).reshape(count, local_rows, here * SLOTS)
 
-    streams = [gather(x, count, [(place_rows, tuple(found))] if h == 0 else ()) for h, x in enumerate(normed)]
-    combine = streams[0][1][0]
-    got = list(zip(*(blocks for blocks, _ in streams)))
+    there = swap(partial)
+    blocks, _ = lax.optimization_barrier((tuple(found), partial))
+    combine, there = lax.optimization_barrier((place_rows(*blocks), there))
+    middle, *normed = norm(where, summand, there, gain)
+    streams = [gather(x, count)[0] for x in normed]
+    got = list(zip(*streams))
     if few:
         mixture = reduce(experts_fused(where, got, combine, w_gate, w_up, w_down), side, count)
     else:

time: 124 us -> 121 us (0.976)
  waiting for transfers between devices: 46.1 us -> 40 us
  starting transfers between devices: 34.6 us -> 38.1 us
  other arithmetic: 2.74 us -> 5.26 us
  local copies, waits for them, and re-layouts: 4.26 us -> 2.13 us
    ppermute x20, starting transfers between devices: 32.5 us -> 36.9 us  [turn(): return lax.ppermute(value, ('ctx', 'exp'), pairs)]
    ppermute x20, waiting for transfers between devices: 43.4 us -> 39.1 us  [turn(): return lax.ppermute(value, ('ctx', 'exp'), pairs)]
    unnamed x6 -> x2, local copies, waits for them, and re-layouts: 2.13 us -> 0.01 us
    select_n x2, other arithmetic: 0.09 us -> 1.9 us  [reduce(): jnp.where(side == 0, running, nothing)]
    ppermute x19, waiting for transfers between devices: 2.68 us -> 0.88 us  [swap(): return lax.ppermute(value, 'exp', SWAP)]
  transfers between devices with their start and end apart: 39 -> 39, of which waited for: 21 -> 21; matrix products, arithmetic and copies ran while one was open for 3% -> 5% of each run, Pallas kernels for 1% -> 2%
where the time goes in v12:
time: 121 us
  waiting for transfers between devices  40 us (33%)
  starting transfers between devices  38.1 us (31%)
  Pallas kernels  35 us (29%)
  other arithmetic  5.26 us (4%)
  local copies, waits for them, and re-layouts  2.13 us (2%)
    ppermute x20, waiting for transfers between devices, turn(): return lax.ppermute(value, ('ctx', 'exp'), pairs)  39.1 us
    ppermute x20, starting transfers between devices, turn(): return lax.ppermute(value, ('ctx', 'exp'), pairs)  36.9 us
    pallas_call x1, Pallas kernels, experts_fused(): pl.pallas_call(functools.partial(fused_kernel, count), in_specs=[pl.Block...  25.3 us
    pallas_call x1, Pallas kernels, attend(): pl.pallas_call(functools.partial(attend_kernel, count, blocks, heads), gr...  5.86 us
  transfers between devices with their start and end apart: 39, of which 21 were waited for; matrix products, arithmetic and copies ran while one was open for 5% of the time, Pallas kernels for 2%

profile of v12, /device:TPU:0, one launch (start us, length us, event | category | flops | bytes accessed | tf_op | source)
XLA Modules:
  0.0 120.7 jit_solution(16712730094636584805)
XLA Ops:
  0.0 1.1 pack.1.refs_0_
  1.1 3.0 %collective-permute-start = (bf16[128,640]{1,0:T(8,128)(2,1)S(1)}, bf16[128,640]{1,0:T(8,128)(2,1)S(1)}, u32[]{:S(2)}, u32[]{:S(2)}) collective-permute-start(bf16[128,640]{1,0:T(8,128)(2,1)S(1)} %pack.1.refs_0_), channel_id=1, source_target_pairs={{0,2},{1,5},{2,6},{3,1},{6,10},{7,3},{10,14},{11,7},{14,12},{15,11... | collective-permute-start | bytes 491528 | tf_op jit(solution)/shard_map/ppermute | solution.py:49
  5.6 1.9 %collective-permute-done.refs_1_ = bf16[128,640]{1,0:T(8,128)(2,1)S(1)} collective-permute-done((bf16[128,640]{1,0:T(8,128)(2,1)S(1)}, bf16[128,640]{1,0:T(8,128)(2,1)S(1)}, u32[]{:S(2)}, u32[]{:S(2)}) %collective-permute-start) | collective-permute-done | bytes 163872 | tf_op jit(solution)/shard_map/ppermute | solution.py:49
  7.5 2.0 %collective-permute-start.1 = (bf16[128,640]{1,0:T(8,128)(2,1)S(1)}, bf16[128,640]{1,0:T(8,128)(2,1)S(1)}, u32[]{:S(2)}, u32[]{:S(2)}) collective-permute-start(bf16[128,640]{1,0:T(8,128)(2,1)S(1)} %collective-permute-done.refs_1_), channel_id=1, source_target_pairs={{0,2},{1,5},{2,6},{3,1},{6,10},{7,3},{10,14},{11,7},{14,12},{15,11... | collective-permute-start | bytes 491528 | tf_op jit(solution)/shard_map/ppermute | solution.py:49
  10.2 2.7 %collective-permute-done.1.refs_2_ = bf16[128,640]{1,0:T(8,128)(2,1)S(1)} collective-permute-done((bf16[128,640]{1,0:T(8,128)(2,1)S(1)}, bf16[128,640]{1,0:T(8,128)(2,1)S(1)}, u32[]{:S(2)}, u32[]{:S(2)}) %collective-permute-start.1) | collective-permute-done | bytes 163872 | tf_op jit(solution)/shard_map/ppermute | solution.py:49
  12.9 2.0 %collective-permute-start.3 = (bf16[128,640]{1,0:T(8,128)(2,1)S(1)}, bf16[128,640]{1,0:T(8,128)(2,1)S(1)}, u32[]{:S(2)}, u32[]{:S(2)}) collective-permute-start(bf16[128,640]{1,0:T(8,128)(2,1)S(1)} %collective-permute-done.1.refs_2_), channel_id=1, source_target_pairs={{0,2},{1,5},{2,6},{3,1},{6,10},{7,3},{10,14},{11,7},{14,12},{15,11... | collective-permute-start | bytes 491528 | tf_op jit(solution)/shard_map/ppermute | solution.py:49
  14.8 3.4 %collective-permute-done.3.refs_3_ = bf16[128,640]{1,0:T(8,128)(2,1)S(1)} collective-permute-done((bf16[128,640]{1,0:T(8,128)(2,1)S(1)}, bf16[128,640]{1,0:T(8,128)(2,1)S(1)}, u32[]{:S(2)}, u32[]{:S(2)}) %collective-permute-start.3) | collective-permute-done | bytes 163872 | tf_op jit(solution)/shard_map/ppermute | solution.py:49
  18.2 2.0 %collective-permute-start.5 = (bf16[128,640]{1,0:T(8,128)(2,1)S(1)}, bf16[128,640]{1,0:T(8,128)(2,1)S(1)}, u32[]{:S(2)}, u32[]{:S(2)}) collective-permute-start(bf16[128,640]{1,0:T(8,128)(2,1)S(1)} %collective-permute-done.3.refs_3_), channel_id=1, source_target_pairs={{0,2},{1,5},{2,6},{3,1},{6,10},{7,3},{10,14},{11,7},{14,12},{15,11... | collective-permute-start | bytes 491528 | tf_op jit(solution)/shard_map/ppermute | solution.py:49
  20.1 3.4 %collective-permute-done.5.refs_4_ = bf16[128,640]{1,0:T(8,128)(2,1)S(1)} collective-permute-done((bf16[128,640]{1,0:T(8,128)(2,1)S(1)}, bf16[128,640]{1,0:T(8,128)(2,1)S(1)}, u32[]{:S(2)}, u32[]{:S(2)}) %collective-permute-start.5) | collective-permute-done | bytes 163872 | tf_op jit(solution)/shard_map/ppermute | solution.py:49
  23.5 5.9 %attend.1 = (bf16[128,2048]{1,0:T(8,128)(2,1)S(1)}, f32[128,2048]{1,0:T(8,128)S(1)}) custom-call(s32[42]{0:T(128)S(1)} %concatenate.10.info, bf16[128,640]{1,0:T(8,128)(2,1)S(1)} %pack.1.refs_0_, bf16[128,640]{1,0:T(8,128)(2,1)S(1)} %collective-permute-done.refs_1_, bf16[128,640]{1,0:T(8,128)(2,1)S(1)} %collective-permute-done.1.refs_2_, ...), custom_call_target="tpu_custom_call" | custom-call | tf_op jit(solution)/shard_map/attend/pallas_call | solution.py:207
  29.5 1.8 %route.1.refs_16_ = bf16[8,128,128]{2,1,0:T(8,128)(2,1)S(1)} custom-call(s32[2]{0:T(128)S(1)} %pad_add_fusion.where, bf16[128,640]{1,0:T(8,128)(2,1)S(1)} %pack.1.refs_0_, bf16[128,640]{1,0:T(8,128)(2,1)S(1)} %collective-permute-done.refs_1_, bf16[128,640]{1,0:T(8,128)(2,1)S(1)} %collective-permute-done.1.refs_2_, ...), custom_call_target="tpu_custom_call" | custom-call | tf_op jit(solution)/shard_map/route/pallas_call | solution.py:251
  31.4 0.9 norm.1
  32.3 2.0 %collective-permute-start.8 = (bf16[128,1024]{1,0:T(8,128)(2,1)S(1)}, bf16[128,1024]{1,0:T(8,128)(2,1)S(1)}, u32[]{:S(2)}, u32[]{:S(2)}) collective-permute-start(bf16[128,1024]{1,0:T(8,128)(2,1)S(1)} %get-tuple-element.96.refs_0_), channel_id=1, source_target_pairs={{0,2},{1,5},{2,6},{3,1},{6,10},{7,3},{10,14},{11,7},{14,12},{15,11... | collective-permute-start | bytes 786440 | tf_op jit(solution)/shard_map/ppermute | solution.py:49
  34.3 1.6 %collective-permute-start.9 = (bf16[128,1024]{1,0:T(8,128)(2,1)S(1)}, bf16[128,1024]{1,0:T(8,128)(2,1)S(1)}, u32[]{:S(2)}, u32[]{:S(2)}) collective-permute-start(bf16[128,1024]{1,0:T(8,128)(2,1)S(1)} %get-tuple-element.97.refs_1_), channel_id=1, source_target_pairs={{0,2},{1,5},{2,6},{3,1},{6,10},{7,3},{10,14},{11,7},{14,12},{15,11... | collective-permute-start | bytes 786440 | tf_op jit(solution)/shard_map/ppermute | solution.py:49
  35.9 2.8 %collective-permute-done.8.refs_2_ = bf16[128,1024]{1,0:T(8,128)(2,1)S(1)} collective-permute-done((bf16[128,1024]{1,0:T(8,128)(2,1)S(1)}, bf16[128,1024]{1,0:T(8,128)(2,1)S(1)}, u32[]{:S(2)}, u32[]{:S(2)}) %collective-permute-start.8) | collective-permute-done | bytes 262176 | tf_op jit(solution)/shard_map/ppermute | solution.py:49
  38.7 2.0 %collective-permute-start.10 = (bf16[128,1024]{1,0:T(8,128)(2,1)S(1)}, bf16[128,1024]{1,0:T(8,128)(2,1)S(1)}, u32[]{:S(2)}, u32[]{:S(2)}) collective-permute-start(bf16[128,1024]{1,0:T(8,128)(2,1)S(1)} %collective-permute-done.8.refs_2_), channel_id=1, source_target_pairs={{0,2},{1,5},{2,6},{3,1},{6,10},{7,3},{10,14},{11,7},{14,12},{15,11... | collective-permute-start | bytes 786440 | tf_op jit(solution)/shard_map/ppermute | solution.py:49
  40.7 0.8 collective-permute-done.9.refs_3_
  41.5 2.0 %collective-permute-start.12 = (bf16[128,1024]{1,0:T(8,128)(2,1)S(1)}, bf16[128,1024]{1,0:T(8,128)(2,1)S(1)}, u32[]{:S(2)}, u32[]{:S(2)}) collective-permute-start(bf16[128,1024]{1,0:T(8,128)(2,1)S(1)} %collective-permute-done.9.refs_3_), channel_id=1, source_target_pairs={{0,2},{1,5},{2,6},{3,1},{6,10},{7,3},{10,14},{11,7},{14,12},{15,11... | collective-permute-start | bytes 786440 | tf_op jit(solution)/shard_map/ppermute | solution.py:49
  43.5 1.6 %collective-permute-done.10.refs_4_ = bf16[128,1024]{1,0:T(8,128)(2,1)S(1)} collective-permute-done((bf16[128,1024]{1,0:T(8,128)(2,1)S(1)}, bf16[128,1024]{1,0:T(8,128)(2,1)S(1)}, u32[]{:S(2)}, u32[]{:S(2)}) %collective-permute-start.10) | collective-permute-done | bytes 262176 | tf_op jit(solution)/shard_map/ppermute | solution.py:49
  45.1 2.0 %collective-permute-start.14 = (bf16[128,1024]{1,0:T(8,128)(2,1)S(1)}, bf16[128,1024]{1,0:T(8,128)(2,1)S(1)}, u32[]{:S(2)}, u32[]{:S(2)}) collective-permute-start(bf16[128,1024]{1,0:T(8,128)(2,1)S(1)} %collective-permute-done.10.refs_4_), channel_id=1, source_target_pairs={{0,2},{1,5},{2,6},{3,1},{6,10},{7,3},{10,14},{11,7},{14,12},{15,11... | collective-permute-start | bytes 786440 | tf_op jit(solution)/shard_map/ppermute | solution.py:49
  47.0 0.8 collective-permute-done.12.refs_5_
  47.9 2.0 %collective-permute-start.16 = (bf16[128,1024]{1,0:T(8,128)(2,1)S(1)}, bf16[128,1024]{1,0:T(8,128)(2,1)S(1)}, u32[]{:S(2)}, u32[]{:S(2)}) collective-permute-start(bf16[128,1024]{1,0:T(8,128)(2,1)S(1)} %collective-permute-done.12.refs_5_), channel_id=1, source_target_pairs={{0,2},{1,5},{2,6},{3,1},{6,10},{7,3},{10,14},{11,7},{14,12},{15,11... | collective-permute-start | bytes 786440 | tf_op jit(solution)/shard_map/ppermute | solution.py:49
  49.8 1.6 %collective-permute-done.14.refs_6_ = bf16[128,1024]{1,0:T(8,128)(2,1)S(1)} collective-permute-done((bf16[128,1024]{1,0:T(8,128)(2,1)S(1)}, bf16[128,1024]{1,0:T(8,128)(2,1)S(1)}, u32[]{:S(2)}, u32[]{:S(2)}) %collective-permute-start.14) | collective-permute-done | bytes 262176 | tf_op jit(solution)/shard_map/ppermute | solution.py:49
  51.5 2.0 %collective-permute-start.18 = (bf16[128,1024]{1,0:T(8,128)(2,1)S(1)}, bf16[128,1024]{1,0:T(8,128)(2,1)S(1)}, u32[]{:S(2)}, u32[]{:S(2)}) collective-permute-start(bf16[128,1024]{1,0:T(8,128)(2,1)S(1)} %collective-permute-done.14.refs_6_), channel_id=1, source_target_pairs={{0,2},{1,5},{2,6},{3,1},{6,10},{7,3},{10,14},{11,7},{14,12},{15,11... | collective-permute-start | bytes 786440 | tf_op jit(solution)/shard_map/ppermute | solution.py:49
  53.4 0.8 collective-permute-done.16.refs_7_
  54.3 2.0 %collective-permute-start.20 = (bf16[128,1024]{1,0:T(8,128)(2,1)S(1)}, bf16[128,1024]{1,0:T(8,128)(2,1)S(1)}, u32[]{:S(2)}, u32[]{:S(2)}) collective-permute-start(bf16[128,1024]{1,0:T(8,128)(2,1)S(1)} %collective-permute-done.16.refs_7_), channel_id=1, source_target_pairs={{0,2},{1,5},{2,6},{3,1},{6,10},{7,3},{10,14},{11,7},{14,12},{15,11... | collective-permute-start | bytes 786440 | tf_op jit(solution)/shard_map/ppermute | solution.py:49
  56.2 1.6 %collective-permute-done.18.refs_8_ = bf16[128,1024]{1,0:T(8,128)(2,1)S(1)} collective-permute-done((bf16[128,1024]{1,0:T(8,128)(2,1)S(1)}, bf16[128,1024]{1,0:T(8,128)(2,1)S(1)}, u32[]{:S(2)}, u32[]{:S(2)}) %collective-permute-start.18) | collective-permute-done | bytes 262176 | tf_op jit(solution)/shard_map/ppermute | solution.py:49
  57.8 2.8 %collective-permute-done.20.refs_9_ = bf16[128,1024]{1,0:T(8,128)(2,1)S(1)} collective-permute-done((bf16[128,1024]{1,0:T(8,128)(2,1)S(1)}, bf16[128,1024]{1,0:T(8,128)(2,1)S(1)}, u32[]{:S(2)}, u32[]{:S(2)}) %collective-permute-start.20) | collective-permute-done | bytes 262176 | tf_op jit(solution)/shard_map/ppermute | solution.py:49
  60.6 25.3 %experts.1 = (bf16[128,1024]{1,0:T(8,128)(2,1)S(1)}, bf16[128,1024]{1,0:T(8,128)(2,1)S(1)}, bf16[128,1024]{1,0:T(8,128)(2,1)S(1)}, bf16[128,1024]{1,0:T(8,128)(2...) custom-call(s32[2]{0:T(128)S(1)} %pad_add_fusion.where, ...), custom_call_target="tpu_custom_call" | custom-call | tf_op jit(solution)/shard_map/experts/pallas_call | solution.py:437
  87.4 2.0 %collective-permute-start.23 = (bf16[64,1024]{1,0:T(8,128)(2,1)S(1)}, bf16[64,1024]{1,0:T(8,128)(2,1)}, u32[]{:S(2)}, u32[]{:S(2)}) collective-permute-start(bf16[64,1024]{1,0:T(8,128)(2,1)S(1)} %add_convert_fusion.6), channel_id=1, source_target_pairs={{0,2},{1,5},{2,6},{3,1},{6,10},{7,3},{10,14},{11,7},{14,12},{15,11... | collective-permute-start | bytes 393224 | tf_op jit(solution)/shard_map/ppermute | solution.py:49
  90.1 1.6 %collective-permute-start.33 = (bf16[64,1024]{1,0:T(8,128)(2,1)}, bf16[64,1024]{1,0:T(8,128)(2,1)}, u32[]{:S(2)}, u32[]{:S(2)}) collective-permute-start(bf16[64,1024]{1,0:T(8,128)(2,1)} %add_convert_fusion.5), channel_id=1, source_target_pairs={{0,2},{1,5},{2,6},{3,1},{6,10},{7,3},{10,14},{11,7},{14,12},{15,11... | collective-permute-start | bytes 393224 | tf_op jit(solution)/shard_map/ppermute | solution.py:49
  92.5 2.9 %collective-permute-done.33 = bf16[64,1024]{1,0:T(8,128)(2,1)} collective-permute-done((bf16[64,1024]{1,0:T(8,128)(2,1)}, bf16[64,1024]{1,0:T(8,128)(2,1)}, u32[]{:S(2)}, u32[]{:S(2)}) %collective-permute-start.33) | collective-permute-done | bytes 131104 | tf_op jit(solution)/shard_map/ppermute | solution.py:49
  95.4 0.9 convert_select_fusion.1
  96.4 1.0 fusion.1
  97.4 1.6 %collective-permute-start.34 = (bf16[128,1024]{1,0:T(8,128)(2,1)S(1)}, bf16[128,1024]{1,0:T(8,128)(2,1)S(1)}, u32[]{:S(2)}, u32[]{:S(2)}) collective-permute-start(bf16[128,1024]{1,0:T(8,128)(2,1)S(1)} %fusion.1), channel_id=1, source_target_pairs={{0,2},{1,5},{2,6},{3,1},{6,10},{7,3},{10,14},{11,7},{14,12},{15,11... | collective-permute-start | bytes 786440 | tf_op jit(solution)/shard_map/ppermute | solution.py:49
  99.1 0.9 convert_select_fusion.3
  100.1 1.6 %collective-permute-start.26 = (bf16[128,1024]{1,0:T(8,128)(2,1)S(1)}, bf16[128,1024]{1,0:T(8,128)(2,1)S(1)}, u32[]{:S(2)}, u32[]{:S(2)}) collective-permute-start(bf16[128,1024]{1,0:T(8,128)(2,1)S(1)} %fusion), channel_id=1, source_target_pairs={{0,2},{1,5},{2,6},{3,1},{6,10},{7,3},{10,14},{11,7},{14,12},{15,11... | collective-permute-start | bytes 786440 | tf_op jit(solution)/shard_map/ppermute | solution.py:49
  101.8 2.1 %collective-permute-done.34 = bf16[128,1024]{1,0:T(8,128)(2,1)S(1)} collective-permute-done((bf16[128,1024]{1,0:T(8,128)(2,1)S(1)}, bf16[128,1024]{1,0:T(8,128)(2,1)S(1)}, u32[]{:S(2)}, u32[]{:S(2)}) %collective-permute-start.34) | collective-permute-done | bytes 262176 | tf_op jit(solution)/shard_map/ppermute | solution.py:49
  104.0 1.6 %collective-permute-start.37 = (bf16[128,1024]{1,0:T(8,128)(2,1)S(1)}, bf16[128,1024]{1,0:T(8,128)(2,1)S(1)}, u32[]{:S(2)}, u32[]{:S(2)}) collective-permute-start(bf16[128,1024]{1,0:T(8,128)(2,1)S(1)} %add_convert_fusion.2), channel_id=1, source_target_pairs={{0,2},{1,5},{2,6},{3,1},{6,10},{7,3},{10,14},{11,7},{14,12},{15,11... | collective-permute-start | bytes 786440 | tf_op jit(solution)/shard_map/ppermute | solution.py:49
  105.6 1.0 collective-permute-done.26
  106.8 1.6 %collective-permute-start.27 = (bf16[128,1024]{1,0:T(8,128)(2,1)S(1)}, bf16[128,1024]{1,0:T(8,128)(2,1)S(1)}, u32[]{:S(2)}, u32[]{:S(2)}) collective-permute-start(bf16[128,1024]{1,0:T(8,128)(2,1)S(1)} %add_convert_fusion.4), channel_id=1, source_target_pairs={{0,2},{1,5},{2,6},{3,1},{6,10},{7,3},{10,14},{11,7},{14,12},{15,11... | collective-permute-start | bytes 786440 | tf_op jit(solution)/shard_map/ppermute | solution.py:49
  108.4 2.0 %collective-permute-done.37 = bf16[128,1024]{1,0:T(8,128)(2,1)S(1)} collective-permute-done((bf16[128,1024]{1,0:T(8,128)(2,1)S(1)}, bf16[128,1024]{1,0:T(8,128)(2,1)S(1)}, u32[]{:S(2)}, u32[]{:S(2)}) %collective-permute-start.37) | collective-permute-done | bytes 262176 | tf_op jit(solution)/shard_map/ppermute | solution.py:49
  110.6 0.9 collective-permute-start.38
  111.5 1.8 %collective-permute-done.27 = bf16[128,1024]{1,0:T(8,128)(2,1)S(1)} collective-permute-done((bf16[128,1024]{1,0:T(8,128)(2,1)S(1)}, bf16[128,1024]{1,0:T(8,128)(2,1)S(1)}, u32[]{:S(2)}, u32[]{:S(2)}) %collective-permute-start.27) | collective-permute-done | bytes 262176 | tf_op jit(solution)/shard_map/ppermute | solution.py:49
  113.4 1.6 %collective-permute-start.30 = (bf16[128,1024]{1,0:T(8,128)(2,1)S(1)}, bf16[128,1024]{1,0:T(8,128)(2,1)S(1)}, u32[]{:S(2)}, u32[]{:S(2)}) collective-permute-start(bf16[128,1024]{1,0:T(8,128)(2,1)S(1)} %add_convert_fusion.3), channel_id=1, source_target_pairs={{0,2},{1,5},{2,6},{3,1},{6,10},{7,3},{10,14},{11,7},{14,12},{15,11... | collective-permute-start | bytes 786440 | tf_op jit(solution)/shard_map/ppermute | solution.py:49
  115.0 1.4 %collective-permute-done.38 = bf16[128,1024]{1,0:T(8,128)(2,1)S(1)} collective-permute-done((bf16[128,1024]{1,0:T(8,128)(2,1)S(1)}, bf16[128,1024]{1,0:T(8,128)(2,1)S(1)}, u32[]{:S(2)}, u32[]{:S(2)}) %collective-permute-start.38) | collective-permute-done | bytes 262176 | tf_op jit(solution)/shard_map/ppermute | solution.py:49
  116.4 3.4 %collective-permute-done.30 = bf16[128,1024]{1,0:T(8,128)(2,1)S(1)} collective-permute-done((bf16[128,1024]{1,0:T(8,128)(2,1)S(1)}, bf16[128,1024]{1,0:T(8,128)(2,1)S(1)}, u32[]{:S(2)}, u32[]{:S(2)}) %collective-permute-start.30) | collective-permute-done | bytes 262176 | tf_op jit(solution)/shard_map/ppermute | solution.py:49
  119.8 0.9 add_convert_fusion
  (52 shorter events, 5.9 us)
Async XLA Ops:
  1.1 6.4 %collective-permute-start = (bf16[128,640]{1,0:T(8,128)(2,1)S(1)}, bf16[128,640]{1,0:T(8,128)(2,1)S(1)}, u32[]{:S(2)}, u32[]{:S(2)}) collective-permute-start(bf16[128,640]{1,0:T(8,128)(2,1)S(1)} %pack.1.refs_0_), channel_id=1, source_target_pairs={{0,2},{1,5},{2,6},{3,1},{6,10},{7,3},{10,14},{11,7},{14,12},{15,11... | collective-permute-start | bytes 491528 | tf_op jit(solution)/shard_map/ppermute | solution.py:49
  7.5 2.7 %collective-permute-start.2 = (bf16[128,640]{1,0:T(8,128)(2,1)S(1)}, bf16[128,640]{1,0:T(8,128)(2,1)S(1)}, u32[]{:S(2)}, u32[]{:S(2)}) collective-permute-start(bf16[128,640]{1,0:T(8,128)(2,1)S(1)} %collective-permute-done.refs_1_), channel_id=1, source_target_pairs={{0,1},{1,0},{2,3},{3,2},{4,5},{5,4},{6,7},{7,6},{8,9},{9,8},{10,11... | collective-permute-start | bytes 491528 | tf_op jit(solution)/shard_map/ppermute | solution.py:40
  7.5 5.3 %collective-permute-start.1 = (bf16[128,640]{1,0:T(8,128)(2,1)S(1)}, bf16[128,640]{1,0:T(8,128)(2,1)S(1)}, u32[]{:S(2)}, u32[]{:S(2)}) collective-permute-start(bf16[128,640]{1,0:T(8,128)(2,1)S(1)} %collective-permute-done.refs_1_), channel_id=1, source_target_pairs={{0,2},{1,5},{2,6},{3,1},{6,10},{7,3},{10,14},{11,7},{14,12},{15,11... | collective-permute-start | bytes 491528 | tf_op jit(solution)/shard_map/ppermute | solution.py:49
  12.9 2.0 %collective-permute-start.4 = (bf16[128,640]{1,0:T(8,128)(2,1)S(1)}, bf16[128,640]{1,0:T(8,128)(2,1)S(1)}, u32[]{:S(2)}, u32[]{:S(2)}) collective-permute-start(bf16[128,640]{1,0:T(8,128)(2,1)S(1)} %collective-permute-done.1.refs_2_), channel_id=1, source_target_pairs={{0,1},{1,0},{2,3},{3,2},{4,5},{5,4},{6,7},{7,6},{8,9},{9,8},{10,11... | collective-permute-start | bytes 491528 | tf_op jit(solution)/shard_map/ppermute | solution.py:40
  12.9 5.3 %collective-permute-start.3 = (bf16[128,640]{1,0:T(8,128)(2,1)S(1)}, bf16[128,640]{1,0:T(8,128)(2,1)S(1)}, u32[]{:S(2)}, u32[]{:S(2)}) collective-permute-start(bf16[128,640]{1,0:T(8,128)(2,1)S(1)} %collective-permute-done.1.refs_2_), channel_id=1, source_target_pairs={{0,2},{1,5},{2,6},{3,1},{6,10},{7,3},{10,14},{11,7},{14,12},{15,11... | collective-permute-start | bytes 491528 | tf_op jit(solution)/shard_map/ppermute | solution.py:49
  18.2 2.0 %collective-permute-start.6 = (bf16[128,640]{1,0:T(8,128)(2,1)S(1)}, bf16[128,640]{1,0:T(8,128)(2,1)S(1)}, u32[]{:S(2)}, u32[]{:S(2)}) collective-permute-start(bf16[128,640]{1,0:T(8,128)(2,1)S(1)} %collective-permute-done.3.refs_3_), channel_id=1, source_target_pairs={{0,1},{1,0},{2,3},{3,2},{4,5},{5,4},{6,7},{7,6},{8,9},{9,8},{10,11... | collective-permute-start | bytes 491528 | tf_op jit(solution)/shard_map/ppermute | solution.py:40
  18.2 5.3 %collective-permute-start.5 = (bf16[128,640]{1,0:T(8,128)(2,1)S(1)}, bf16[128,640]{1,0:T(8,128)(2,1)S(1)}, u32[]{:S(2)}, u32[]{:S(2)}) collective-permute-start(bf16[128,640]{1,0:T(8,128)(2,1)S(1)} %collective-permute-done.3.refs_3_), channel_id=1, source_target_pairs={{0,2},{1,5},{2,6},{3,1},{6,10},{7,3},{10,14},{11,7},{14,12},{15,11... | collective-permute-start | bytes 491528 | tf_op jit(solution)/shard_map/ppermute | solution.py:49
  29.4 2.0 %collective-permute-start.7 = (bf16[128,2048]{1,0:T(8,128)(2,1)S(1)}, bf16[128,2048]{1,0:T(8,128)(2,1)S(1)}, u32[]{:S(2)}, u32[]{:S(2)}) collective-permute-start(bf16[128,2048]{1,0:T(8,128)(2,1)S(1)} %get-tuple-element.84), channel_id=1, source_target_pairs={{0,1},{1,0},{2,3},{3,2},{4,5},{5,4},{6,7},{7,6},{8,9},{9,8},{10,11... | collective-permute-start | bytes 1572872 | tf_op jit(solution)/shard_map/ppermute | solution.py:40
  32.3 6.4 %collective-permute-start.8 = (bf16[128,1024]{1,0:T(8,128)(2,1)S(1)}, bf16[128,1024]{1,0:T(8,128)(2,1)S(1)}, u32[]{:S(2)}, u32[]{:S(2)}) collective-permute-start(bf16[128,1024]{1,0:T(8,128)(2,1)S(1)} %get-tuple-element.96.refs_0_), channel_id=1, source_target_pairs={{0,2},{1,5},{2,6},{3,1},{6,10},{7,3},{10,14},{11,7},{14,12},{15,11... | collective-permute-start | bytes 786440 | tf_op jit(solution)/shard_map/ppermute | solution.py:49
  34.3 7.2 %collective-permute-start.9 = (bf16[128,1024]{1,0:T(8,128)(2,1)S(1)}, bf16[128,1024]{1,0:T(8,128)(2,1)S(1)}, u32[]{:S(2)}, u32[]{:S(2)}) collective-permute-start(bf16[128,1024]{1,0:T(8,128)(2,1)S(1)} %get-tuple-element.97.refs_1_), channel_id=1, source_target_pairs={{0,2},{1,5},{2,6},{3,1},{6,10},{7,3},{10,14},{11,7},{14,12},{15,11... | collective-permute-start | bytes 786440 | tf_op jit(solution)/shard_map/ppermute | solution.py:49
  38.7 4.8 %collective-permute-start.11 = (bf16[128,1024]{1,0:T(8,128)(2,1)S(1)}, bf16[128,1024]{1,0:T(8,128)(2,1)S(1)}, u32[]{:S(2)}, u32[]{:S(2)}) collective-permute-start(bf16[128,1024]{1,0:T(8,128)(2,1)S(1)} %collective-permute-done.8.refs_2_), channel_id=1, source_target_pairs={{0,1},{1,0},{2,3},{3,2},{4,5},{5,4},{6,7},{7,6},{8,9},{9,8},{10,11... | collective-permute-start | bytes 786440 | tf_op jit(solution)/shard_map/ppermute | solution.py:40
  38.7 6.4 %collective-permute-start.10 = (bf16[128,1024]{1,0:T(8,128)(2,1)S(1)}, bf16[128,1024]{1,0:T(8,128)(2,1)S(1)}, u32[]{:S(2)}, u32[]{:S(2)}) collective-permute-start(bf16[128,1024]{1,0:T(8,128)(2,1)S(1)} %collective-permute-done.8.refs_2_), channel_id=1, source_target_pairs={{0,2},{1,5},{2,6},{3,1},{6,10},{7,3},{10,14},{11,7},{14,12},{15,11... | collective-permute-start | bytes 786440 | tf_op jit(solution)/shard_map/ppermute | solution.py:49
  41.5 5.5 %collective-permute-start.13 = (bf16[128,1024]{1,0:T(8,128)(2,1)S(1)}, bf16[128,1024]{1,0:T(8,128)(2,1)S(1)}, u32[]{:S(2)}, u32[]{:S(2)}) collective-permute-start(bf16[128,1024]{1,0:T(8,128)(2,1)S(1)} %collective-permute-done.9.refs_3_), channel_id=1, source_target_pairs={{0,1},{1,0},{2,3},{3,2},{4,5},{5,4},{6,7},{7,6},{8,9},{9,8},{10,11... | collective-permute-start | bytes 786440 | tf_op jit(solution)/shard_map/ppermute | solution.py:40
  41.5 6.4 %collective-permute-start.12 = (bf16[128,1024]{1,0:T(8,128)(2,1)S(1)}, bf16[128,1024]{1,0:T(8,128)(2,1)S(1)}, u32[]{:S(2)}, u32[]{:S(2)}) collective-permute-start(bf16[128,1024]{1,0:T(8,128)(2,1)S(1)} %collective-permute-done.9.refs_3_), channel_id=1, source_target_pairs={{0,2},{1,5},{2,6},{3,1},{6,10},{7,3},{10,14},{11,7},{14,12},{15,11... | collective-permute-start | bytes 786440 | tf_op jit(solution)/shard_map/ppermute | solution.py:49
  45.1 4.8 %collective-permute-start.15 = (bf16[128,1024]{1,0:T(8,128)(2,1)S(1)}, bf16[128,1024]{1,0:T(8,128)(2,1)S(1)}, u32[]{:S(2)}, u32[]{:S(2)}) collective-permute-start(bf16[128,1024]{1,0:T(8,128)(2,1)S(1)} %collective-permute-done.10.refs_4_), channel_id=1, source_target_pairs={{0,1},{1,0},{2,3},{3,2},{4,5},{5,4},{6,7},{7,6},{8,9},{9,8},{10,11... | collective-permute-start | bytes 786440 | tf_op jit(solution)/shard_map/ppermute | solution.py:40
  45.1 6.4 %collective-permute-start.14 = (bf16[128,1024]{1,0:T(8,128)(2,1)S(1)}, bf16[128,1024]{1,0:T(8,128)(2,1)S(1)}, u32[]{:S(2)}, u32[]{:S(2)}) collective-permute-start(bf16[128,1024]{1,0:T(8,128)(2,1)S(1)} %collective-permute-done.10.refs_4_), channel_id=1, source_target_pairs={{0,2},{1,5},{2,6},{3,1},{6,10},{7,3},{10,14},{11,7},{14,12},{15,11... | collective-permute-start | bytes 786440 | tf_op jit(solution)/shard_map/ppermute | solution.py:49
  47.9 5.5 %collective-permute-start.17 = (bf16[128,1024]{1,0:T(8,128)(2,1)S(1)}, bf16[128,1024]{1,0:T(8,128)(2,1)S(1)}, u32[]{:S(2)}, u32[]{:S(2)}) collective-permute-start(bf16[128,1024]{1,0:T(8,128)(2,1)S(1)} %collective-permute-done.12.refs_5_), channel_id=1, source_target_pairs={{0,1},{1,0},{2,3},{3,2},{4,5},{5,4},{6,7},{7,6},{8,9},{9,8},{10,11... | collective-permute-start | bytes 786440 | tf_op jit(solution)/shard_map/ppermute | solution.py:40
  47.9 6.4 %collective-permute-start.16 = (bf16[128,1024]{1,0:T(8,128)(2,1)S(1)}, bf16[128,1024]{1,0:T(8,128)(2,1)S(1)}, u32[]{:S(2)}, u32[]{:S(2)}) collective-permute-start(bf16[128,1024]{1,0:T(8,128)(2,1)S(1)} %collective-permute-done.12.refs_5_), channel_id=1, source_target_pairs={{0,2},{1,5},{2,6},{3,1},{6,10},{7,3},{10,14},{11,7},{14,12},{15,11... | collective-permute-start | bytes 786440 | tf_op jit(solution)/shard_map/ppermute | solution.py:49
  51.5 4.8 %collective-permute-start.19 = (bf16[128,1024]{1,0:T(8,128)(2,1)S(1)}, bf16[128,1024]{1,0:T(8,128)(2,1)S(1)}, u32[]{:S(2)}, u32[]{:S(2)}) collective-permute-start(bf16[128,1024]{1,0:T(8,128)(2,1)S(1)} %collective-permute-done.14.refs_6_), channel_id=1, source_target_pairs={{0,1},{1,0},{2,3},{3,2},{4,5},{5,4},{6,7},{7,6},{8,9},{9,8},{10,11... | collective-permute-start | bytes 786440 | tf_op jit(solution)/shard_map/ppermute | solution.py:40
  51.5 6.4 %collective-permute-start.18 = (bf16[128,1024]{1,0:T(8,128)(2,1)S(1)}, bf16[128,1024]{1,0:T(8,128)(2,1)S(1)}, u32[]{:S(2)}, u32[]{:S(2)}) collective-permute-start(bf16[128,1024]{1,0:T(8,128)(2,1)S(1)} %collective-permute-done.14.refs_6_), channel_id=1, source_target_pairs={{0,2},{1,5},{2,6},{3,1},{6,10},{7,3},{10,14},{11,7},{14,12},{15,11... | collective-permute-start | bytes 786440 | tf_op jit(solution)/shard_map/ppermute | solution.py:49
  54.3 3.6 %collective-permute-start.21 = (bf16[128,1024]{1,0:T(8,128)(2,1)S(1)}, bf16[128,1024]{1,0:T(8,128)(2,1)S(1)}, u32[]{:S(2)}, u32[]{:S(2)}) collective-permute-start(bf16[128,1024]{1,0:T(8,128)(2,1)S(1)} %collective-permute-done.16.refs_7_), channel_id=1, source_target_pairs={{0,1},{1,0},{2,3},{3,2},{4,5},{5,4},{6,7},{7,6},{8,9},{9,8},{10,11... | collective-permute-start | bytes 786440 | tf_op jit(solution)/shard_map/ppermute | solution.py:40
  54.3 6.4 %collective-permute-start.20 = (bf16[128,1024]{1,0:T(8,128)(2,1)S(1)}, bf16[128,1024]{1,0:T(8,128)(2,1)S(1)}, u32[]{:S(2)}, u32[]{:S(2)}) collective-permute-start(bf16[128,1024]{1,0:T(8,128)(2,1)S(1)} %collective-permute-done.16.refs_7_), channel_id=1, source_target_pairs={{0,2},{1,5},{2,6},{3,1},{6,10},{7,3},{10,14},{11,7},{14,12},{15,11... | collective-permute-start | bytes 786440 | tf_op jit(solution)/shard_map/ppermute | solution.py:49
  86.0 4.2 %copy-start = (bf16[128,1024]{1,0:T(8,128)(2,1)}, bf16[128,1024]{1,0:T(8,128)(2,1)S(1)}, u32[]{:S(2)}) copy-start(bf16[128,1024]{1,0:T(8,128)(2,1)S(1)} %get-tuple-element.118) | copy-start | bytes 786436
  86.0 1.4 %collective-permute-start.22 = (bf16[64,1024]{1,0:T(8,128)(2,1)S(1)}, bf16[64,1024]{1,0:T(8,128)(2,1)S(1)}, u32[]{:S(2)}, u32[]{:S(2)}) collective-permute-start(bf16[64,1024]{1,0:T(8,128)(2,1)S(1)} %get-tuple-element.114), channel_id=1, source_target_pairs={{0,1},{1,0},{2,3},{3,2},{4,5},{5,4},{6,7},{7,6},{8,9},{9,8},{10,11... | collective-permute-start | bytes 393224 | tf_op jit(solution)/shard_map/ppermute | solution.py:40
  86.0 3.4 %collective-permute-start.32 = (bf16[64,1024]{1,0:T(8,128)(2,1)S(1)}, bf16[64,1024]{1,0:T(8,128)(2,1)S(1)}, u32[]{:S(2)}, u32[]{:S(2)}) collective-permute-start(bf16[64,1024]{1,0:T(8,128)(2,1)S(1)} %get-tuple-element.131), channel_id=1, source_target_pairs={{0,1},{1,0},{2,3},{3,2},{4,5},{5,4},{6,7},{7,6},{8,9},{9,8},{10,11... | collective-permute-start | bytes 393224 | tf_op jit(solution)/shard_map/ppermute | solution.py:40
  87.4 5.1 %collective-permute-start.23 = (bf16[64,1024]{1,0:T(8,128)(2,1)S(1)}, bf16[64,1024]{1,0:T(8,128)(2,1)}, u32[]{:S(2)}, u32[]{:S(2)}) collective-permute-start(bf16[64,1024]{1,0:T(8,128)(2,1)S(1)} %add_convert_fusion.6), channel_id=1, source_target_pairs={{0,2},{1,5},{2,6},{3,1},{6,10},{7,3},{10,14},{11,7},{14,12},{15,11... | collective-permute-start | bytes 393224 | tf_op jit(solution)/shard_map/ppermute | solution.py:49
  90.1 5.3 %collective-permute-start.33 = (bf16[64,1024]{1,0:T(8,128)(2,1)}, bf16[64,1024]{1,0:T(8,128)(2,1)}, u32[]{:S(2)}, u32[]{:S(2)}) collective-permute-start(bf16[64,1024]{1,0:T(8,128)(2,1)} %add_convert_fusion.5), channel_id=1, source_target_pairs={{0,2},{1,5},{2,6},{3,1},{6,10},{7,3},{10,14},{11,7},{14,12},{15,11... | collective-permute-start | bytes 393224 | tf_op jit(solution)/shard_map/ppermute | solution.py:49
  91.7 4.7 %collective-permute-start.31 = (bf16[128,1024]{1,0:T(8,128)(2,1)}, bf16[128,1024]{1,0:T(8,128)(2,1)}, u32[]{:S(2)}, u32[]{:S(2)}) collective-permute-start(bf16[128,1024]{1,0:T(8,128)(2,1)} %get-tuple-element.129), channel_id=1, source_target_pairs={{0,1},{1,0},{2,3},{3,2},{4,5},{5,4},{6,7},{7,6},{8,9},{9,8},{10,11... | collective-permute-start | bytes 786440 | tf_op jit(solution)/shard_map/ppermute | solution.py:40
  91.7 8.3 %collective-permute-start.25 = (bf16[128,1024]{1,0:T(8,128)(2,1)}, bf16[128,1024]{1,0:T(8,128)(2,1)S(1)}, u32[]{:S(2)}, u32[]{:S(2)}) collective-permute-start(bf16[128,1024]{1,0:T(8,128)(2,1)} %copy-done), channel_id=1, source_target_pairs={{0,1},{1,0},{2,3},{3,2},{4,5},{5,4},{6,7},{7,6},{8,9},{9,8},{10,11... | collective-permute-start | bytes 786440 | tf_op jit(solution)/shard_map/ppermute | solution.py:40
  95.4 8.5 %collective-permute-start.36 = (bf16[128,1024]{1,0:T(8,128)(2,1)S(1)}, bf16[128,1024]{1,0:T(8,128)(2,1)S(1)}, u32[]{:S(2)}, u32[]{:S(2)}) collective-permute-start(bf16[128,1024]{1,0:T(8,128)(2,1)S(1)} %get-tuple-element.137), channel_id=1, source_target_pairs={{0,1},{1,0},{2,3},{3,2},{4,5},{5,4},{6,7},{7,6},{8,9},{9,8},{10,11... | collective-permute-start | bytes 786440 | tf_op jit(solution)/shard_map/ppermute | solution.py:40
  97.4 6.4 %collective-permute-start.34 = (bf16[128,1024]{1,0:T(8,128)(2,1)S(1)}, bf16[128,1024]{1,0:T(8,128)(2,1)S(1)}, u32[]{:S(2)}, u32[]{:S(2)}) collective-permute-start(bf16[128,1024]{1,0:T(8,128)(2,1)S(1)} %fusion.1), channel_id=1, source_target_pairs={{0,2},{1,5},{2,6},{3,1},{6,10},{7,3},{10,14},{11,7},{14,12},{15,11... | collective-permute-start | bytes 786440 | tf_op jit(solution)/shard_map/ppermute | solution.py:49
  100.1 6.5 %collective-permute-start.26 = (bf16[128,1024]{1,0:T(8,128)(2,1)S(1)}, bf16[128,1024]{1,0:T(8,128)(2,1)S(1)}, u32[]{:S(2)}, u32[]{:S(2)}) collective-permute-start(bf16[128,1024]{1,0:T(8,128)(2,1)S(1)} %fusion), channel_id=1, source_target_pairs={{0,2},{1,5},{2,6},{3,1},{6,10},{7,3},{10,14},{11,7},{14,12},{15,11... | collective-permute-start | bytes 786440 | tf_op jit(solution)/shard_map/ppermute | solution.py:49
  101.8 4.9 %collective-permute-start.24 = (bf16[128,1024]{1,0:T(8,128)(2,1)S(1)}, bf16[128,1024]{1,0:T(8,128)(2,1)S(1)}, u32[]{:S(2)}, u32[]{:S(2)}) collective-permute-start(bf16[128,1024]{1,0:T(8,128)(2,1)S(1)} %get-tuple-element.116), channel_id=1, source_target_pairs={{0,1},{1,0},{2,3},{3,2},{4,5},{5,4},{6,7},{7,6},{8,9},{9,8},{10,11... | collective-permute-start | bytes 786440 | tf_op jit(solution)/shard_map/ppermute | solution.py:40
  103.9 6.6 %collective-permute-start.35 = (bf16[128,1024]{1,0:T(8,128)(2,1)S(1)}, bf16[128,1024]{1,0:T(8,128)(2,1)S(1)}, u32[]{:S(2)}, u32[]{:S(2)}) collective-permute-start(bf16[128,1024]{1,0:T(8,128)(2,1)S(1)} %get-tuple-element.135), channel_id=1, source_target_pairs={{0,1},{1,0},{2,3},{3,2},{4,5},{5,4},{6,7},{7,6},{8,9},{9,8},{10,11... | collective-permute-start | bytes 786440 | tf_op jit(solution)/shard_map/ppermute | solution.py:40
  104.0 6.4 %collective-permute-start.37 = (bf16[128,1024]{1,0:T(8,128)(2,1)S(1)}, bf16[128,1024]{1,0:T(8,128)(2,1)S(1)}, u32[]{:S(2)}, u32[]{:S(2)}) collective-permute-start(bf16[128,1024]{1,0:T(8,128)(2,1)S(1)} %add_convert_fusion.2), channel_id=1, source_target_pairs={{0,2},{1,5},{2,6},{3,1},{6,10},{7,3},{10,14},{11,7},{14,12},{15,11... | collective-permute-start | bytes 786440 | tf_op jit(solution)/shard_map/ppermute | solution.py:49
  106.8 6.4 %collective-permute-start.27 = (bf16[128,1024]{1,0:T(8,128)(2,1)S(1)}, bf16[128,1024]{1,0:T(8,128)(2,1)S(1)}, u32[]{:S(2)}, u32[]{:S(2)}) collective-permute-start(bf16[128,1024]{1,0:T(8,128)(2,1)S(1)} %add_convert_fusion.4), channel_id=1, source_target_pairs={{0,2},{1,5},{2,6},{3,1},{6,10},{7,3},{10,14},{11,7},{14,12},{15,11... | collective-permute-start | bytes 786440 | tf_op jit(solution)/shard_map/ppermute | solution.py:49
  108.4 4.8 %collective-permute-start.29 = (bf16[128,1024]{1,0:T(8,128)(2,1)S(1)}, bf16[128,1024]{1,0:T(8,128)(2,1)S(1)}, u32[]{:S(2)}, u32[]{:S(2)}) collective-permute-start(bf16[128,1024]{1,0:T(8,128)(2,1)S(1)} %get-tuple-element.125), channel_id=1, source_target_pairs={{0,1},{1,0},{2,3},{3,2},{4,5},{5,4},{6,7},{7,6},{8,9},{9,8},{10,11... | collective-permute-start | bytes 786440 | tf_op jit(solution)/shard_map/ppermute | solution.py:40
  110.6 5.9 %collective-permute-start.38 = (bf16[128,1024]{1,0:T(8,128)(2,1)S(1)}, bf16[128,1024]{1,0:T(8,128)(2,1)S(1)}, u32[]{:S(2)}, u32[]{:S(2)}) collective-permute-start(bf16[128,1024]{1,0:T(8,128)(2,1)S(1)} %add_convert_fusion.1), channel_id=1, source_target_pairs={{0,3},{1,4},{2,7},{3,0},{6,11},{7,2},{10,15},{11,6},{14,13},{15,10... | collective-permute-start | bytes 786440 | tf_op jit(solution)/shard_map/ppermute | solution.py:49
  113.2 3.2 %collective-permute-start.28 = (bf16[128,1024]{1,0:T(8,128)(2,1)S(1)}, bf16[128,1024]{1,0:T(8,128)(2,1)S(1)}, u32[]{:S(2)}, u32[]{:S(2)}) collective-permute-start(bf16[128,1024]{1,0:T(8,128)(2,1)S(1)} %get-tuple-element.123), channel_id=1, source_target_pairs={{0,1},{1,0},{2,3},{3,2},{4,5},{5,4},{6,7},{7,6},{8,9},{9,8},{10,11... | collective-permute-start | bytes 786440 | tf_op jit(solution)/shard_map/ppermute | solution.py:40
  113.4 6.4 %collective-permute-start.30 = (bf16[128,1024]{1,0:T(8,128)(2,1)S(1)}, bf16[128,1024]{1,0:T(8,128)(2,1)S(1)}, u32[]{:S(2)}, u32[]{:S(2)}) collective-permute-start(bf16[128,1024]{1,0:T(8,128)(2,1)S(1)} %add_convert_fusion.3), channel_id=1, source_target_pairs={{0,2},{1,5},{2,6},{3,1},{6,10},{7,3},{10,14},{11,7},{14,12},{15,11... | collective-permute-start | bytes 786440 | tf_op jit(solution)/shard_map/ppermute | solution.py:49

commit v13 on v12

--- a/solution.py
+++ b/solution.py
@@ -22,7 +22,6 @@
 HELD = 7
 PIECES = 2
 SWAP = [(0, 1), (1, 0)]
-PARTS = 2
 FEW = 8
 
 
@@ -87,30 +86,38 @@
     return found + other[1:], made[: len(beside)]
 
 
-def reduce(parts, side, count):
+def gather_columns(near, far, count):
+    if count > FEW:
+        return list(zip(lax.all_gather(near, "ctx"), lax.all_gather(far, "ctx")))
     middle = count // 2
-    near, far = 0, 1
-    sums = [swap(parts[1 - stream][middle][1]) for stream in (near, far)]
-    given = [swap(parts[1 - stream][middle - 1]) for stream in (near, far)]
-    for stream in (near, far):
-        first = summed([parts[stream][middle][0], sums[stream]]).astype(jnp.bfloat16)
-        sums[stream] = turn(first, count)
-    for d in range(middle - 1, 0, -1):
-        for stream in (near, far):
-            arrived = sums[stream]
-            later = parts[1 - stream][d - 1] if d > 1 or stream == near else ()
-            arrived, later = lax.optimization_barrier((arrived, later))
-            running = arrived.astype(jnp.float32)
-            if d == middle - 1:
-                nothing = jnp.zeros_like(running)
-                running = jnp.concatenate(
-                    [jnp.where(side == 0, running, nothing), jnp.where(side == 0, nothing, running)], axis=0
-                )
-            total = (summed([parts[stream][middle + d], given[stream]]) + running).astype(jnp.bfloat16)
-            sums[stream] = turn(total, count, cross=d == 1 and stream == far)
-            if d > 1 or stream == near:
+    found, other = {0: [near], 1: [far]}, {0: [()], 1: [()]}
+    for d in range(1, middle + 1):
+        for stream in (0, 1) if d < middle else (0,):
+            arrived = turn(found[stream][-1], count)
+            arrived, other[stream][-1] = lax.optimization_barrier((arrived, other[stream][-1]))
+            found[stream].append(arrived)
+            other[stream].append(swap(arrived))
+    here = [(found[0][d], found[1][d]) for d in range(middle)]
+    there = [(other[1][d], other[0][d]) for d in range(1, middle)]
+    return here + [(found[0][middle], other[0][middle])] + there
+
+
+def reduce(parts, count):
+    middle = count // 2
+    given = [swap(parts[1][middle]), swap(parts[0][middle - 1])]
+    running = [None, None]
+    for d in range(middle, 0, -1):
+        for stream in (0, 1) if d < middle else (0,):
+            place = middle + d if d < middle else middle
+            later = parts[1 - stream][d - 1] if d > 1 or stream == 0 else ()
+            pieces = [parts[stream][place], given[stream]]
+            if running[stream] is not None:
+                running[stream], later = lax.optimization_barrier((running[stream], later))
+                pieces.append(running[stream])
+            running[stream] = turn(summed(pieces).astype(jnp.bfloat16), count, cross=d == 1 and stream == 1)
+            if d > 1 or stream == 0:
                 given[stream] = swap(later)
-    return summed([parts[near][0], given[near], sums[near], sums[far]])
+    return summed([parts[0][0], given[0], *running])
 
 
 def attend_kernel(count, blocks, heads, info, *refs):
@@ -258,27 +265,26 @@
     )(where, *found)
 
 
-def norm_kernel(where, base_ref, there_ref, gain_ref, middle_ref, *normed_refs):
+def norm_kernel(where, base_ref, there_ref, gain_ref, middle_ref, near_ref, far_ref):
     half = middle_ref.shape[1]
     middle = (base_ref[...] + there_ref[...].astype(jnp.float32)).astype(jnp.bfloat16)
     wide = middle.astype(jnp.float32)
     inverse = lax.rsqrt(jnp.mean(wide * wide, axis=1, keepdims=True) + 1e-06)
-    normed = (wide * inverse * gain_ref[...].astype(jnp.float32)).astype(jnp.bfloat16)
-    part = normed_refs[0].shape[1]
-    for h, ref in enumerate(normed_refs):
-        ref[...] = normed[:, h * part : (h + 1) * part]
-    middle_ref[...] = jnp.where(where[1] == 0, wide[:, :half], wide[:, half:]).astype(jnp.bfloat16)
+    normed = wide * inverse * gain_ref[...].astype(jnp.float32)
+    first = where[1] == 0
+    near_ref[...] = jnp.where(first, normed[:, :half], normed[:, half:]).astype(jnp.bfloat16)
+    far_ref[...] = jnp.where(first, normed[:, half:], normed[:, :half]).astype(jnp.bfloat16)
+    middle_ref[...] = jnp.where(first, wide[:, :half], wide[:, half:]).astype(jnp.bfloat16)
 
 
 def norm(where, base, there, gain):
     rows, width = base.shape
     whole = pl.BlockSpec(memory_space=pltpu.VMEM)
-    shapes = [(rows, width // 2)] + [(rows, width // PARTS)] * PARTS
     return pl.pallas_call(
         norm_kernel,
         in_specs=[pl.BlockSpec(memory_space=pltpu.SMEM)] + [whole] * 3,
-        out_specs=[whole] * len(shapes),
-        out_shape=[pltpu.VMEM(shape, jnp.bfloat16) for shape in shapes],
+        out_specs=[whole] * 3,
+        out_shape=[pltpu.VMEM((rows, width // 2), jnp.bfloat16)] * 3,
         compiler_params=pltpu.CompilerParams(vmem_limit_bytes=12 * MIB),
         name="norm",
     )(where, base, there, gain)
@@ -334,14 +340,16 @@
 
 
 def fused_kernel(count, where, *refs):
-    at = PARTS * count
+    at = 2 * count
     blocks, combine_ref, weights = refs[:at], refs[at], refs[at + 1 : at + 4]
-    near, far = refs[at + 4 : at + 5 + count], refs[at + 5 + count : at + 6 + 2 * count]
-    at += 6 + 2 * count
+    near, far = refs[at + 4 : at + 4 + count], refs[at + 4 + count : at + 4 + 2 * count]
+    at += 4 + 2 * count
     picked, buffer, sems = refs[at : at + 3]
     here = picked.shape[0]
     slots, units, width = buffer.shape
+    half = width // 2
     side = where[1]
+    columns = [pl.ds(pl.multiple_of(turned * half, half), half) for turned in (side, 1 - side)]
     piece = units // PIECES
     middle = count // 2
     by_rows = (((0,), (0,)), ((), ()))
@@ -366,12 +374,11 @@
 
     for c in range(count):
         pick = (combine_ref[c].astype(jnp.float32) > 0).astype(jnp.float32).astype(jnp.bfloat16)
-        for h in range(PARTS):
-            block = blocks[PARTS * c + h][...]
+        for h in range(2):
+            block = blocks[2 * c + h][...]
             rows = lax.dot_general(pick, block, by_rows, preferred_element_type=jnp.float32).astype(jnp.bfloat16)
-            columns = pl.ds(h * block.shape[1], block.shape[1])
             for e in range(here):
-                picked[e, c * SLOTS : (c + 1) * SLOTS, columns] = rows[e * SLOTS : (e + 1) * SLOTS]
+                picked[e, c * SLOTS : (c + 1) * SLOTS, columns[h]] = rows[e * SLOTS : (e + 1) * SLOTS]
 
     def work(expert, _):
         hidden = expert_hidden(picked[expert], arrived(expert, 0), arrived(expert, 1))
@@ -391,18 +398,10 @@
 
     lax.fori_loop(0, here, work, 0)
 
-    half = width // 2
     for c in [middle] + list(range(middle)) + list(range(middle + 1, count)):
-        for turned, outs in ((1 - side, far), (side, near)):
-            columns = pl.ds(pl.multiple_of(turned * half, half), half)
-            rows = jnp.concatenate([picked[e, c * SLOTS : (c + 1) * SLOTS, columns] for e in range(here)], axis=0)
-            total = jnp.dot(combine_ref[c], rows, preferred_element_type=jnp.float32).astype(jnp.bfloat16)
-            if c == middle:
-                upper, lower = total[: total.shape[0] // 2], total[total.shape[0] // 2 :]
-                outs[c][...] = jnp.where(side == 0, upper, lower)
-                outs[count][...] = jnp.where(side == 0, lower, upper)
-            else:
-                outs[c][...] = total
+        for h, outs in ((1, far), (0, near)):
+            rows = jnp.concatenate([picked[e, c * SLOTS : (c + 1) * SLOTS, columns[h]] for e in range(here)], axis=0)
+            outs[c][...] = jnp.dot(combine_ref[c], rows, preferred_element_type=jnp.float32).astype(jnp.bfloat16)
 
 
 def expert_specs(w_gate):
@@ -431,24 +430,21 @@
     count, local = len(found), found[0][0].shape[0]
     here, units, width = w_gate.shape
     rows = count * SLOTS
-    middle = count // 2
-    sizes = [local // 2 if c in (middle, count) else local for c in range(count + 1)]
     whole = pl.BlockSpec(memory_space=pltpu.VMEM)
     outs = pl.pallas_call(
         functools.partial(fused_kernel, count),
         in_specs=[pl.BlockSpec(memory_space=pltpu.SMEM)]
-        + [whole] * (PARTS * count + 1)
+        + [whole] * (2 * count + 1)
         + [pl.BlockSpec(memory_space=pltpu.HBM)] * 3,
-        out_specs=[whole] * (2 * count + 2),
+        out_specs=[whole] * (2 * count),
         scratch_shapes=[pltpu.VMEM((here, rows, width), jnp.bfloat16)]
         + [pltpu.VMEM((HELD, units, width), jnp.bfloat16), pltpu.SemaphoreType.DMA((HELD, PIECES))],
-        out_shape=[pltpu.VMEM((size, width // 2), jnp.bfloat16) for size in sizes] * 2,
+        out_shape=[pltpu.VMEM((local, width // 2), jnp.bfloat16)] * (2 * count),
         compiler_params=pltpu.CompilerParams(vmem_limit_bytes=29 * MIB),
         name="experts",
     )(where, *(x for block in found for x in block), combine,
       *(pltpu.with_memory_space_constraint(w, pltpu.HBM) for w in (w_gate, w_up, w_down)))
-    parts = [list(outs[: count + 1]), list(outs[count + 1 :])]
-    return [x[:middle] + [(x[middle], x[count])] + x[middle + 1 : count] for x in parts]
+    return outs[:count], outs[count:]
 
 
 def body(
@@ -500,13 +496,13 @@
     blocks, _ = lax.optimization_barrier((tuple(found), partial))
     combine, there = lax.optimization_barrier((place_rows(*blocks), there))
     middle, *normed = norm(where, summand, there, gain)
-    streams = [gather(x, count)[0] for x in normed]
-    got = list(zip(*streams))
+    got = gather_columns(*normed, count)
     if few:
-        mixture = reduce(experts_fused(where, got, combine, w_gate, w_up, w_down), side, count)
+        mixture = reduce(experts_fused(where, got, combine, w_gate, w_up, w_down), count)
     else:
         pick = (combine > 0).astype(jnp.bfloat16)
-        rows = jnp.stack([jnp.concatenate(block, axis=1) for block in got])
+        near, far = (jnp.stack(x) for x in zip(*got))
+        rows = jnp.concatenate([jnp.where(side == 0, near, far), jnp.where(side == 0, far, near)], axis=2)
         picked = jnp.einsum("cts,ctd->csd", pick, rows, preferred_element_type=jnp.float32).astype(jnp.bfloat16)
         picked = picked.reshape(count, here, SLOTS, width).transpose(1, 0, 2, 3).reshape(here, count * SLOTS, width)
         result = experts_plain(where, picked, w_gate, w_up, w_down)

time: 121 us -> 113 us (0.934)
  other arithmetic: 5.26 us -> 1.75 us
  starting transfers between devices: 38.1 us -> 36 us
  waiting for transfers between devices: 40 us -> 38.3 us
    ppermute x20 -> x18, waiting for transfers between devices: 39.1 us -> 35.7 us  [turn(): return lax.ppermute(value, ('ctx', 'exp'), pairs)]
    select_n x2 -> x0, other arithmetic: 1.9 us -> none  [reduce(): jnp.where(side == 0, running, nothing)]
    ppermute x19, waiting for transfers between devices: 0.88 us -> 2.6 us  [swap(): return lax.ppermute(value, 'exp', SWAP)]
    ppermute x20 -> x18, starting transfers between devices: 36.9 us -> 35.3 us  [turn(): return lax.ppermute(value, ('ctx', 'exp'), pairs)]
    convert_element_type x8 -> x7, other arithmetic: 2.36 us -> 0.75 us  [reduce(): summed(pieces).astype(jnp.bfloat16)]
  transfers between devices with their start and end apart: 39 -> 37, of which waited for: 21 -> 20; matrix products, arithmetic and copies ran while one was open for 5% -> 3% of each run, Pallas kernels for 2% -> 2%
where the time goes in v13:
time: 113 us
  waiting for transfers between devices  38.3 us (34%)
  starting transfers between devices  36 us (32%)
  Pallas kernels  34.9 us (31%)
  local copies, waits for them, and re-layouts  2.13 us (2%)
  other arithmetic  1.75 us (2%)
    ppermute x18, waiting for transfers between devices, turn(): return lax.ppermute(value, ('ctx', 'exp'), pairs)  35.7 us
    ppermute x18, starting transfers between devices, turn(): return lax.ppermute(value, ('ctx', 'exp'), pairs)  35.3 us
    pallas_call x1, Pallas kernels, experts_fused(): pl.pallas_call(functools.partial(fused_kernel, count), in_specs=[pl.Block...  25.1 us
    pallas_call x1, Pallas kernels, attend(): pl.pallas_call(functools.partial(attend_kernel, count, blocks, heads), gr...  5.86 us
    ppermute x19, waiting for transfers between devices, swap(): return lax.ppermute(value, 'exp', SWAP)  2.6 us
  transfers between devices with their start and end apart: 37, of which 20 were waited for; matrix products, arithmetic and copies ran while one was open for 3% of the time, Pallas kernels for 2%

profile of v13, /device:TPU:0, one launch (start us, length us, event | category | flops | bytes accessed | tf_op | source)
XLA Modules:
  0.0 113.2 jit_solution(1779587509393818672)
XLA Ops:
  0.0 1.1 %pack.1.refs_0_ = bf16[128,640]{1,0:T(8,128)(2,1)S(1)} custom-call(bf16[576,128]{1,0:T(8,128)(2,1)} %bitcast.11, s32[6,128]{1,0:T(8,128)} %bitcast.12, f32[6,128]{1,0:T(8,128)} %bitcast.13), custom_call_target="tpu_custom_call" | custom-call | tf_op jit(solution)/shard_map/pack/pallas_call | solution.py:314
  1.1 3.0 %collective-permute-start = (bf16[128,640]{1,0:T(8,128)(2,1)S(1)}, bf16[128,640]{1,0:T(8,128)(2,1)S(1)}, u32[]{:S(2)}, u32[]{:S(2)}) collective-permute-start(bf16[128,640]{1,0:T(8,128)(2,1)S(1)} %pack.1.refs_0_), channel_id=1, source_target_pairs={{0,2},{1,5},{2,6},{3,1},{6,10},{7,3},{10,14},{11,7},{14,12},{15,11... | collective-permute-start | bytes 491528 | tf_op jit(solution)/shard_map/ppermute | solution.py:48
  4.2 0.7 dynamic-slice_bitcast_fusion
  4.9 0.7 concatenate.4.info
  5.6 1.9 %collective-permute-done.refs_1_ = bf16[128,640]{1,0:T(8,128)(2,1)S(1)} collective-permute-done((bf16[128,640]{1,0:T(8,128)(2,1)S(1)}, bf16[128,640]{1,0:T(8,128)(2,1)S(1)}, u32[]{:S(2)}, u32[]{:S(2)}) %collective-permute-start) | collective-permute-done | bytes 163872 | tf_op jit(solution)/shard_map/ppermute | solution.py:48
  7.5 2.0 %collective-permute-start.1 = (bf16[128,640]{1,0:T(8,128)(2,1)S(1)}, bf16[128,640]{1,0:T(8,128)(2,1)S(1)}, u32[]{:S(2)}, u32[]{:S(2)}) collective-permute-start(bf16[128,640]{1,0:T(8,128)(2,1)S(1)} %collective-permute-done.refs_1_), channel_id=1, source_target_pairs={{0,2},{1,5},{2,6},{3,1},{6,10},{7,3},{10,14},{11,7},{14,12},{15,11... | collective-permute-start | bytes 491528 | tf_op jit(solution)/shard_map/ppermute | solution.py:48
  9.5 0.7 reshape.3.gain_ref
  10.2 2.7 %collective-permute-done.1.refs_2_ = bf16[128,640]{1,0:T(8,128)(2,1)S(1)} collective-permute-done((bf16[128,640]{1,0:T(8,128)(2,1)S(1)}, bf16[128,640]{1,0:T(8,128)(2,1)S(1)}, u32[]{:S(2)}, u32[]{:S(2)}) %collective-permute-start.1) | collective-permute-done | bytes 163872 | tf_op jit(solution)/shard_map/ppermute | solution.py:48
  12.9 2.0 %collective-permute-start.3 = (bf16[128,640]{1,0:T(8,128)(2,1)S(1)}, bf16[128,640]{1,0:T(8,128)(2,1)S(1)}, u32[]{:S(2)}, u32[]{:S(2)}) collective-permute-start(bf16[128,640]{1,0:T(8,128)(2,1)S(1)} %collective-permute-done.1.refs_2_), channel_id=1, source_target_pairs={{0,2},{1,5},{2,6},{3,1},{6,10},{7,3},{10,14},{11,7},{14,12},{15,11... | collective-permute-start | bytes 491528 | tf_op jit(solution)/shard_map/ppermute | solution.py:48
  14.8 3.4 %collective-permute-done.3.refs_3_ = bf16[128,640]{1,0:T(8,128)(2,1)S(1)} collective-permute-done((bf16[128,640]{1,0:T(8,128)(2,1)S(1)}, bf16[128,640]{1,0:T(8,128)(2,1)S(1)}, u32[]{:S(2)}, u32[]{:S(2)}) %collective-permute-start.3) | collective-permute-done | bytes 163872 | tf_op jit(solution)/shard_map/ppermute | solution.py:48
  18.2 2.0 %collective-permute-start.5 = (bf16[128,640]{1,0:T(8,128)(2,1)S(1)}, bf16[128,640]{1,0:T(8,128)(2,1)S(1)}, u32[]{:S(2)}, u32[]{:S(2)}) collective-permute-start(bf16[128,640]{1,0:T(8,128)(2,1)S(1)} %collective-permute-done.3.refs_3_), channel_id=1, source_target_pairs={{0,2},{1,5},{2,6},{3,1},{6,10},{7,3},{10,14},{11,7},{14,12},{15,11... | collective-permute-start | bytes 491528 | tf_op jit(solution)/shard_map/ppermute | solution.py:48
  20.1 3.4 %collective-permute-done.5.refs_4_ = bf16[128,640]{1,0:T(8,128)(2,1)S(1)} collective-permute-done((bf16[128,640]{1,0:T(8,128)(2,1)S(1)}, bf16[128,640]{1,0:T(8,128)(2,1)S(1)}, u32[]{:S(2)}, u32[]{:S(2)}) %collective-permute-start.5) | collective-permute-done | bytes 163872 | tf_op jit(solution)/shard_map/ppermute | solution.py:48
  23.5 5.9 %attend.1 = (bf16[128,2048]{1,0:T(8,128)(2,1)S(1)}, f32[128,2048]{1,0:T(8,128)S(1)}) custom-call(s32[42]{0:T(128)S(1)} %concatenate.4.info, bf16[128,640]{1,0:T(8,128)(2,1)S(1)} %pack.1.refs_0_, bf16[128,640]{1,0:T(8,128)(2,1)S(1)} %collective-permute-done.refs_1_, bf16[128,640]{1,0:T(8,128)(2,1)S(1)} %collective-permute-done.1.refs_2_, ...), custom_call_target="tpu_custom_call" | custom-call | tf_op jit(solution)/shard_map/attend/pallas_call | solution.py:214
  29.5 1.8 %route.1.refs_16_ = bf16[8,128,128]{2,1,0:T(8,128)(2,1)S(1)} custom-call(s32[2]{0:T(128)S(1)} %pad_add_fusion.where, bf16[128,640]{1,0:T(8,128)(2,1)S(1)} %pack.1.refs_0_, bf16[128,640]{1,0:T(8,128)(2,1)S(1)} %collective-permute-done.refs_1_, bf16[128,640]{1,0:T(8,128)(2,1)S(1)} %collective-permute-done.1.refs_2_, ...), custom_call_target="tpu_custom_call" | custom-call | tf_op jit(solution)/shard_map/route/pallas_call | solution.py:258
  31.4 0.9 norm.1
  32.3 2.0 %collective-permute-start.8 = (bf16[128,1024]{1,0:T(8,128)(2,1)S(1)}, bf16[128,1024]{1,0:T(8,128)(2,1)S(1)}, u32[]{:S(2)}, u32[]{:S(2)}) collective-permute-start(bf16[128,1024]{1,0:T(8,128)(2,1)S(1)} %get-tuple-element.90.refs_0_), channel_id=1, source_target_pairs={{0,2},{1,5},{2,6},{3,1},{6,10},{7,3},{10,14},{11,7},{14,12},{15,11... | collective-permute-start | bytes 786440 | tf_op jit(solution)/shard_map/ppermute | solution.py:48
  34.3 1.6 %collective-permute-start.9 = (bf16[128,1024]{1,0:T(8,128)(2,1)S(1)}, bf16[128,1024]{1,0:T(8,128)(2,1)S(1)}, u32[]{:S(2)}, u32[]{:S(2)}) collective-permute-start(bf16[128,1024]{1,0:T(8,128)(2,1)S(1)} %get-tuple-element.91.refs_1_), channel_id=1, source_target_pairs={{0,2},{1,5},{2,6},{3,1},{6,10},{7,3},{10,14},{11,7},{14,12},{15,11... | collective-permute-start | bytes 786440 | tf_op jit(solution)/shard_map/ppermute | solution.py:48
  35.9 2.8 %collective-permute-done.8.refs_2_ = bf16[128,1024]{1,0:T(8,128)(2,1)S(1)} collective-permute-done((bf16[128,1024]{1,0:T(8,128)(2,1)S(1)}, bf16[128,1024]{1,0:T(8,128)(2,1)S(1)}, u32[]{:S(2)}, u32[]{:S(2)}) %collective-permute-start.8) | collective-permute-done | bytes 262176 | tf_op jit(solution)/shard_map/ppermute | solution.py:48
  38.7 2.0 %collective-permute-start.10 = (bf16[128,1024]{1,0:T(8,128)(2,1)S(1)}, bf16[128,1024]{1,0:T(8,128)(2,1)S(1)}, u32[]{:S(2)}, u32[]{:S(2)}) collective-permute-start(bf16[128,1024]{1,0:T(8,128)(2,1)S(1)} %collective-permute-done.8.refs_2_), channel_id=1, source_target_pairs={{0,2},{1,5},{2,6},{3,1},{6,10},{7,3},{10,14},{11,7},{14,12},{15,11... | collective-permute-start | bytes 786440 | tf_op jit(solution)/shard_map/ppermute | solution.py:48
  40.7 0.8 collective-permute-done.9.refs_3_
  41.5 2.0 %collective-permute-start.12 = (bf16[128,1024]{1,0:T(8,128)(2,1)S(1)}, bf16[128,1024]{1,0:T(8,128)(2,1)S(1)}, u32[]{:S(2)}, u32[]{:S(2)}) collective-permute-start(bf16[128,1024]{1,0:T(8,128)(2,1)S(1)} %collective-permute-done.9.refs_3_), channel_id=1, source_target_pairs={{0,2},{1,5},{2,6},{3,1},{6,10},{7,3},{10,14},{11,7},{14,12},{15,11... | collective-permute-start | bytes 786440 | tf_op jit(solution)/shard_map/ppermute | solution.py:48
  43.5 1.6 %collective-permute-done.10.refs_4_ = bf16[128,1024]{1,0:T(8,128)(2,1)S(1)} collective-permute-done((bf16[128,1024]{1,0:T(8,128)(2,1)S(1)}, bf16[128,1024]{1,0:T(8,128)(2,1)S(1)}, u32[]{:S(2)}, u32[]{:S(2)}) %collective-permute-start.10) | collective-permute-done | bytes 262176 | tf_op jit(solution)/shard_map/ppermute | solution.py:48
  45.1 2.0 %collective-permute-start.14 = (bf16[128,1024]{1,0:T(8,128)(2,1)S(1)}, bf16[128,1024]{1,0:T(8,128)(2,1)S(1)}, u32[]{:S(2)}, u32[]{:S(2)}) collective-permute-start(bf16[128,1024]{1,0:T(8,128)(2,1)S(1)} %collective-permute-done.10.refs_4_), channel_id=1, source_target_pairs={{0,2},{1,5},{2,6},{3,1},{6,10},{7,3},{10,14},{11,7},{14,12},{15,11... | collective-permute-start | bytes 786440 | tf_op jit(solution)/shard_map/ppermute | solution.py:48
  47.1 0.8 collective-permute-done.12.refs_5_
  47.9 2.0 %collective-permute-start.16 = (bf16[128,1024]{1,0:T(8,128)(2,1)S(1)}, bf16[128,1024]{1,0:T(8,128)(2,1)S(1)}, u32[]{:S(2)}, u32[]{:S(2)}) collective-permute-start(bf16[128,1024]{1,0:T(8,128)(2,1)S(1)} %collective-permute-done.12.refs_5_), channel_id=1, source_target_pairs={{0,2},{1,5},{2,6},{3,1},{6,10},{7,3},{10,14},{11,7},{14,12},{15,11... | collective-permute-start | bytes 786440 | tf_op jit(solution)/shard_map/ppermute | solution.py:48
  49.9 1.6 %collective-permute-done.14.refs_6_ = bf16[128,1024]{1,0:T(8,128)(2,1)S(1)} collective-permute-done((bf16[128,1024]{1,0:T(8,128)(2,1)S(1)}, bf16[128,1024]{1,0:T(8,128)(2,1)S(1)}, u32[]{:S(2)}, u32[]{:S(2)}) %collective-permute-start.14) | collective-permute-done | bytes 262176 | tf_op jit(solution)/shard_map/ppermute | solution.py:48
  51.5 2.0 %collective-permute-start.18 = (bf16[128,1024]{1,0:T(8,128)(2,1)S(1)}, bf16[128,1024]{1,0:T(8,128)(2,1)S(1)}, u32[]{:S(2)}, u32[]{:S(2)}) collective-permute-start(bf16[128,1024]{1,0:T(8,128)(2,1)S(1)} %collective-permute-done.14.refs_6_), channel_id=1, source_target_pairs={{0,2},{1,5},{2,6},{3,1},{6,10},{7,3},{10,14},{11,7},{14,12},{15,11... | collective-permute-start | bytes 786440 | tf_op jit(solution)/shard_map/ppermute | solution.py:48
  53.4 0.8 collective-permute-done.16.refs_7_
  54.3 3.6 %collective-permute-done.18.refs_8_ = bf16[128,1024]{1,0:T(8,128)(2,1)S(1)} collective-permute-done((bf16[128,1024]{1,0:T(8,128)(2,1)S(1)}, bf16[128,1024]{1,0:T(8,128)(2,1)S(1)}, u32[]{:S(2)}, u32[]{:S(2)}) %collective-permute-start.18) | collective-permute-done | bytes 262176 | tf_op jit(solution)/shard_map/ppermute | solution.py:48
  57.9 1.5 %collective-permute-done.20.refs_9_ = bf16[128,1024]{1,0:T(8,128)(2,1)S(1)} collective-permute-done((bf16[128,1024]{1,0:T(8,128)(2,1)S(1)}, bf16[128,1024]{1,0:T(8,128)(2,1)S(1)}, u32[]{:S(2)}, u32[]{:S(2)}) %collective-permute-start.20) | collective-permute-done | bytes 262176 | tf_op jit(solution)/shard_map/ppermute | solution.py:39
  59.4 25.1 %experts.1 = (bf16[128,1024]{1,0:T(8,128)(2,1)S(1)}, bf16[128,1024]{1,0:T(8,128)(2,1)S(1)}, bf16[128,1024]{1,0:T(8,128)(2,1)S(1)}, bf16[128,1024]{1,0:T(8,128)(2...) custom-call(s32[2]{0:T(128)S(1)} %pad_add_fusion.where, ...), custom_call_target="tpu_custom_call" | custom-call | tf_op jit(solution)/shard_map/experts/pallas_call | solution.py:434
  84.5 0.2 collective-permute-start.22
  84.7 0.4 collective-permute-start.31
  85.1 1.0 collective-permute-done.22
  86.2 2.0 %collective-permute-start.23 = (bf16[128,1024]{1,0:T(8,128)(2,1)S(1)}, bf16[128,1024]{1,0:T(8,128)(2,1)S(1)}, u32[]{:S(2)}, u32[]{:S(2)}) collective-permute-start(bf16[128,1024]{1,0:T(8,128)(2,1)S(1)} %add_convert_fusion.7), channel_id=1, source_target_pairs={{0,2},{1,5},{2,6},{3,1},{6,10},{7,3},{10,14},{11,7},{14,12},{15,11... | collective-permute-start | bytes 786440 | tf_op jit(solution)/shard_map/ppermute | solution.py:48
  88.3 1.6 %collective-permute-start.32 = (bf16[128,1024]{1,0:T(8,128)(2,1)S(1)}, bf16[128,1024]{1,0:T(8,128)(2,1)S(1)}, u32[]{:S(2)}, u32[]{:S(2)}) collective-permute-start(bf16[128,1024]{1,0:T(8,128)(2,1)S(1)} %add_convert_fusion.3), channel_id=1, source_target_pairs={{0,2},{1,5},{2,6},{3,1},{6,10},{7,3},{10,14},{11,7},{14,12},{15,11... | collective-permute-start | bytes 786440 | tf_op jit(solution)/shard_map/ppermute | solution.py:48
  89.9 2.7 %collective-permute-done.23 = bf16[128,1024]{1,0:T(8,128)(2,1)S(1)} collective-permute-done((bf16[128,1024]{1,0:T(8,128)(2,1)S(1)}, bf16[128,1024]{1,0:T(8,128)(2,1)S(1)}, u32[]{:S(2)}, u32[]{:S(2)}) %collective-permute-start.23) | collective-permute-done | bytes 262176 | tf_op jit(solution)/shard_map/ppermute | solution.py:48
  92.8 2.0 %collective-permute-start.26 = (bf16[128,1024]{1,0:T(8,128)(2,1)S(1)}, bf16[128,1024]{1,0:T(8,128)(2,1)S(1)}, u32[]{:S(2)}, u32[]{:S(2)}) collective-permute-start(bf16[128,1024]{1,0:T(8,128)(2,1)S(1)} %add_convert_fusion.6), channel_id=1, source_target_pairs={{0,2},{1,5},{2,6},{3,1},{6,10},{7,3},{10,14},{11,7},{14,12},{15,11... | collective-permute-start | bytes 786440 | tf_op jit(solution)/shard_map/ppermute | solution.py:48
  94.8 0.7 collective-permute-done.32
  95.6 2.0 %collective-permute-start.35 = (bf16[128,1024]{1,0:T(8,128)(2,1)S(1)}, bf16[128,1024]{1,0:T(8,128)(2,1)S(1)}, u32[]{:S(2)}, u32[]{:S(2)}) collective-permute-start(bf16[128,1024]{1,0:T(8,128)(2,1)S(1)} %add_convert_fusion.2), channel_id=1, source_target_pairs={{0,2},{1,5},{2,6},{3,1},{6,10},{7,3},{10,14},{11,7},{14,12},{15,11... | collective-permute-start | bytes 786440 | tf_op jit(solution)/shard_map/ppermute | solution.py:48
  97.6 1.6 %collective-permute-done.26 = bf16[128,1024]{1,0:T(8,128)(2,1)S(1)} collective-permute-done((bf16[128,1024]{1,0:T(8,128)(2,1)S(1)}, bf16[128,1024]{1,0:T(8,128)(2,1)S(1)}, u32[]{:S(2)}, u32[]{:S(2)}) %collective-permute-start.26) | collective-permute-done | bytes 262176 | tf_op jit(solution)/shard_map/ppermute | solution.py:48
  99.3 2.0 %collective-permute-start.27 = (bf16[128,1024]{1,0:T(8,128)(2,1)S(1)}, bf16[128,1024]{1,0:T(8,128)(2,1)S(1)}, u32[]{:S(2)}, u32[]{:S(2)}) collective-permute-start(bf16[128,1024]{1,0:T(8,128)(2,1)S(1)} %add_convert_fusion.5), channel_id=1, source_target_pairs={{0,2},{1,5},{2,6},{3,1},{6,10},{7,3},{10,14},{11,7},{14,12},{15,11... | collective-permute-start | bytes 786440 | tf_op jit(solution)/shard_map/ppermute | solution.py:48
  101.3 0.7 collective-permute-done.35
  102.1 1.3 %collective-permute-start.36 = (bf16[128,1024]{1,0:T(8,128)(2,1)S(1)}, bf16[128,1024]{1,0:T(8,128)(2,1)S(1)}, u32[]{:S(2)}, u32[]{:S(2)}) collective-permute-start(bf16[128,1024]{1,0:T(8,128)(2,1)S(1)} %add_convert_fusion.1), channel_id=1, source_target_pairs={{0,3},{1,4},{2,7},{3,0},{6,11},{7,2},{10,15},{11,6},{14,13},{15,10... | collective-permute-start | bytes 786440 | tf_op jit(solution)/shard_map/ppermute | solution.py:48
  103.4 2.3 %collective-permute-done.27 = bf16[128,1024]{1,0:T(8,128)(2,1)S(1)} collective-permute-done((bf16[128,1024]{1,0:T(8,128)(2,1)S(1)}, bf16[128,1024]{1,0:T(8,128)(2,1)S(1)}, u32[]{:S(2)}, u32[]{:S(2)}) %collective-permute-start.27) | collective-permute-done | bytes 262176 | tf_op jit(solution)/shard_map/ppermute | solution.py:48
  105.9 2.0 %collective-permute-start.30 = (bf16[128,1024]{1,0:T(8,128)(2,1)S(1)}, bf16[128,1024]{1,0:T(8,128)(2,1)S(1)}, u32[]{:S(2)}, u32[]{:S(2)}) collective-permute-start(bf16[128,1024]{1,0:T(8,128)(2,1)S(1)} %add_convert_fusion.4), channel_id=1, source_target_pairs={{0,2},{1,5},{2,6},{3,1},{6,10},{7,3},{10,14},{11,7},{14,12},{15,11... | collective-permute-start | bytes 786440 | tf_op jit(solution)/shard_map/ppermute | solution.py:48
  108.0 4.3 %collective-permute-done.30 = bf16[128,1024]{1,0:T(8,128)(2,1)S(1)} collective-permute-done((bf16[128,1024]{1,0:T(8,128)(2,1)S(1)}, bf16[128,1024]{1,0:T(8,128)(2,1)S(1)}, u32[]{:S(2)}, u32[]{:S(2)}) %collective-permute-start.30) | collective-permute-done | bytes 262176 | tf_op jit(solution)/shard_map/ppermute | solution.py:48
  112.3 0.9 add_convert_fusion
  (43 shorter events, 1.1 us)
Async XLA Ops:
  1.1 6.4 %collective-permute-start = (bf16[128,640]{1,0:T(8,128)(2,1)S(1)}, bf16[128,640]{1,0:T(8,128)(2,1)S(1)}, u32[]{:S(2)}, u32[]{:S(2)}) collective-permute-start(bf16[128,640]{1,0:T(8,128)(2,1)S(1)} %pack.1.refs_0_), channel_id=1, source_target_pairs={{0,2},{1,5},{2,6},{3,1},{6,10},{7,3},{10,14},{11,7},{14,12},{15,11... | collective-permute-start | bytes 491528 | tf_op jit(solution)/shard_map/ppermute | solution.py:48
  7.5 2.7 %collective-permute-start.2 = (bf16[128,640]{1,0:T(8,128)(2,1)S(1)}, bf16[128,640]{1,0:T(8,128)(2,1)S(1)}, u32[]{:S(2)}, u32[]{:S(2)}) collective-permute-start(bf16[128,640]{1,0:T(8,128)(2,1)S(1)} %collective-permute-done.refs_1_), channel_id=1, source_target_pairs={{0,1},{1,0},{2,3},{3,2},{4,5},{5,4},{6,7},{7,6},{8,9},{9,8},{10,11... | collective-permute-start | bytes 491528 | tf_op jit(solution)/shard_map/ppermute | solution.py:39
  7.5 5.3 %collective-permute-start.1 = (bf16[128,640]{1,0:T(8,128)(2,1)S(1)}, bf16[128,640]{1,0:T(8,128)(2,1)S(1)}, u32[]{:S(2)}, u32[]{:S(2)}) collective-permute-start(bf16[128,640]{1,0:T(8,128)(2,1)S(1)} %collective-permute-done.refs_1_), channel_id=1, source_target_pairs={{0,2},{1,5},{2,6},{3,1},{6,10},{7,3},{10,14},{11,7},{14,12},{15,11... | collective-permute-start | bytes 491528 | tf_op jit(solution)/shard_map/ppermute | solution.py:48
  12.9 2.0 %collective-permute-start.4 = (bf16[128,640]{1,0:T(8,128)(2,1)S(1)}, bf16[128,640]{1,0:T(8,128)(2,1)S(1)}, u32[]{:S(2)}, u32[]{:S(2)}) collective-permute-start(bf16[128,640]{1,0:T(8,128)(2,1)S(1)} %collective-permute-done.1.refs_2_), channel_id=1, source_target_pairs={{0,1},{1,0},{2,3},{3,2},{4,5},{5,4},{6,7},{7,6},{8,9},{9,8},{10,11... | collective-permute-start | bytes 491528 | tf_op jit(solution)/shard_map/ppermute | solution.py:39
  12.9 5.3 %collective-permute-start.3 = (bf16[128,640]{1,0:T(8,128)(2,1)S(1)}, bf16[128,640]{1,0:T(8,128)(2,1)S(1)}, u32[]{:S(2)}, u32[]{:S(2)}) collective-permute-start(bf16[128,640]{1,0:T(8,128)(2,1)S(1)} %collective-permute-done.1.refs_2_), channel_id=1, source_target_pairs={{0,2},{1,5},{2,6},{3,1},{6,10},{7,3},{10,14},{11,7},{14,12},{15,11... | collective-permute-start | bytes 491528 | tf_op jit(solution)/shard_map/ppermute | solution.py:48
  18.2 2.0 %collective-permute-start.6 = (bf16[128,640]{1,0:T(8,128)(2,1)S(1)}, bf16[128,640]{1,0:T(8,128)(2,1)S(1)}, u32[]{:S(2)}, u32[]{:S(2)}) collective-permute-start(bf16[128,640]{1,0:T(8,128)(2,1)S(1)} %collective-permute-done.3.refs_3_), channel_id=1, source_target_pairs={{0,1},{1,0},{2,3},{3,2},{4,5},{5,4},{6,7},{7,6},{8,9},{9,8},{10,11... | collective-permute-start | bytes 491528 | tf_op jit(solution)/shard_map/ppermute | solution.py:39
  18.2 5.3 %collective-permute-start.5 = (bf16[128,640]{1,0:T(8,128)(2,1)S(1)}, bf16[128,640]{1,0:T(8,128)(2,1)S(1)}, u32[]{:S(2)}, u32[]{:S(2)}) collective-permute-start(bf16[128,640]{1,0:T(8,128)(2,1)S(1)} %collective-permute-done.3.refs_3_), channel_id=1, source_target_pairs={{0,2},{1,5},{2,6},{3,1},{6,10},{7,3},{10,14},{11,7},{14,12},{15,11... | collective-permute-start | bytes 491528 | tf_op jit(solution)/shard_map/ppermute | solution.py:48
  29.4 2.0 %collective-permute-start.7 = (bf16[128,2048]{1,0:T(8,128)(2,1)S(1)}, bf16[128,2048]{1,0:T(8,128)(2,1)S(1)}, u32[]{:S(2)}, u32[]{:S(2)}) collective-permute-start(bf16[128,2048]{1,0:T(8,128)(2,1)S(1)} %get-tuple-element.78), channel_id=1, source_target_pairs={{0,1},{1,0},{2,3},{3,2},{4,5},{5,4},{6,7},{7,6},{8,9},{9,8},{10,11... | collective-permute-start | bytes 1572872 | tf_op jit(solution)/shard_map/ppermute | solution.py:39
  32.3 6.4 %collective-permute-start.8 = (bf16[128,1024]{1,0:T(8,128)(2,1)S(1)}, bf16[128,1024]{1,0:T(8,128)(2,1)S(1)}, u32[]{:S(2)}, u32[]{:S(2)}) collective-permute-start(bf16[128,1024]{1,0:T(8,128)(2,1)S(1)} %get-tuple-element.90.refs_0_), channel_id=1, source_target_pairs={{0,2},{1,5},{2,6},{3,1},{6,10},{7,3},{10,14},{11,7},{14,12},{15,11... | collective-permute-start | bytes 786440 | tf_op jit(solution)/shard_map/ppermute | solution.py:48
  34.3 7.2 %collective-permute-start.9 = (bf16[128,1024]{1,0:T(8,128)(2,1)S(1)}, bf16[128,1024]{1,0:T(8,128)(2,1)S(1)}, u32[]{:S(2)}, u32[]{:S(2)}) collective-permute-start(bf16[128,1024]{1,0:T(8,128)(2,1)S(1)} %get-tuple-element.91.refs_1_), channel_id=1, source_target_pairs={{0,2},{1,5},{2,6},{3,1},{6,10},{7,3},{10,14},{11,7},{14,12},{15,11... | collective-permute-start | bytes 786440 | tf_op jit(solution)/shard_map/ppermute | solution.py:48
  38.7 4.8 %collective-permute-start.11 = (bf16[128,1024]{1,0:T(8,128)(2,1)S(1)}, bf16[128,1024]{1,0:T(8,128)(2,1)S(1)}, u32[]{:S(2)}, u32[]{:S(2)}) collective-permute-start(bf16[128,1024]{1,0:T(8,128)(2,1)S(1)} %collective-permute-done.8.refs_2_), channel_id=1, source_target_pairs={{0,1},{1,0},{2,3},{3,2},{4,5},{5,4},{6,7},{7,6},{8,9},{9,8},{10,11... | collective-permute-start | bytes 786440 | tf_op jit(solution)/shard_map/ppermute | solution.py:39
  38.7 6.4 %collective-permute-start.10 = (bf16[128,1024]{1,0:T(8,128)(2,1)S(1)}, bf16[128,1024]{1,0:T(8,128)(2,1)S(1)}, u32[]{:S(2)}, u32[]{:S(2)}) collective-permute-start(bf16[128,1024]{1,0:T(8,128)(2,1)S(1)} %collective-permute-done.8.refs_2_), channel_id=1, source_target_pairs={{0,2},{1,5},{2,6},{3,1},{6,10},{7,3},{10,14},{11,7},{14,12},{15,11... | collective-permute-start | bytes 786440 | tf_op jit(solution)/shard_map/ppermute | solution.py:48
  41.5 5.5 %collective-permute-start.13 = (bf16[128,1024]{1,0:T(8,128)(2,1)S(1)}, bf16[128,1024]{1,0:T(8,128)(2,1)S(1)}, u32[]{:S(2)}, u32[]{:S(2)}) collective-permute-start(bf16[128,1024]{1,0:T(8,128)(2,1)S(1)} %collective-permute-done.9.refs_3_), channel_id=1, source_target_pairs={{0,1},{1,0},{2,3},{3,2},{4,5},{5,4},{6,7},{7,6},{8,9},{9,8},{10,11... | collective-permute-start | bytes 786440 | tf_op jit(solution)/shard_map/ppermute | solution.py:39
  41.5 6.4 %collective-permute-start.12 = (bf16[128,1024]{1,0:T(8,128)(2,1)S(1)}, bf16[128,1024]{1,0:T(8,128)(2,1)S(1)}, u32[]{:S(2)}, u32[]{:S(2)}) collective-permute-start(bf16[128,1024]{1,0:T(8,128)(2,1)S(1)} %collective-permute-done.9.refs_3_), channel_id=1, source_target_pairs={{0,2},{1,5},{2,6},{3,1},{6,10},{7,3},{10,14},{11,7},{14,12},{15,11... | collective-permute-start | bytes 786440 | tf_op jit(solution)/shard_map/ppermute | solution.py:48
  45.1 4.8 %collective-permute-start.15 = (bf16[128,1024]{1,0:T(8,128)(2,1)S(1)}, bf16[128,1024]{1,0:T(8,128)(2,1)S(1)}, u32[]{:S(2)}, u32[]{:S(2)}) collective-permute-start(bf16[128,1024]{1,0:T(8,128)(2,1)S(1)} %collective-permute-done.10.refs_4_), channel_id=1, source_target_pairs={{0,1},{1,0},{2,3},{3,2},{4,5},{5,4},{6,7},{7,6},{8,9},{9,8},{10,11... | collective-permute-start | bytes 786440 | tf_op jit(solution)/shard_map/ppermute | solution.py:39
  45.1 6.4 %collective-permute-start.14 = (bf16[128,1024]{1,0:T(8,128)(2,1)S(1)}, bf16[128,1024]{1,0:T(8,128)(2,1)S(1)}, u32[]{:S(2)}, u32[]{:S(2)}) collective-permute-start(bf16[128,1024]{1,0:T(8,128)(2,1)S(1)} %collective-permute-done.10.refs_4_), channel_id=1, source_target_pairs={{0,2},{1,5},{2,6},{3,1},{6,10},{7,3},{10,14},{11,7},{14,12},{15,11... | collective-permute-start | bytes 786440 | tf_op jit(solution)/shard_map/ppermute | solution.py:48
  47.9 5.5 %collective-permute-start.17 = (bf16[128,1024]{1,0:T(8,128)(2,1)S(1)}, bf16[128,1024]{1,0:T(8,128)(2,1)S(1)}, u32[]{:S(2)}, u32[]{:S(2)}) collective-permute-start(bf16[128,1024]{1,0:T(8,128)(2,1)S(1)} %collective-permute-done.12.refs_5_), channel_id=1, source_target_pairs={{0,1},{1,0},{2,3},{3,2},{4,5},{5,4},{6,7},{7,6},{8,9},{9,8},{10,11... | collective-permute-start | bytes 786440 | tf_op jit(solution)/shard_map/ppermute | solution.py:39
  47.9 6.4 %collective-permute-start.16 = (bf16[128,1024]{1,0:T(8,128)(2,1)S(1)}, bf16[128,1024]{1,0:T(8,128)(2,1)S(1)}, u32[]{:S(2)}, u32[]{:S(2)}) collective-permute-start(bf16[128,1024]{1,0:T(8,128)(2,1)S(1)} %collective-permute-done.12.refs_5_), channel_id=1, source_target_pairs={{0,2},{1,5},{2,6},{3,1},{6,10},{7,3},{10,14},{11,7},{14,12},{15,11... | collective-permute-start | bytes 786440 | tf_op jit(solution)/shard_map/ppermute | solution.py:48
  51.5 2.8 %collective-permute-start.19 = (bf16[128,1024]{1,0:T(8,128)(2,1)S(1)}, bf16[128,1024]{1,0:T(8,128)(2,1)S(1)}, u32[]{:S(2)}, u32[]{:S(2)}) collective-permute-start(bf16[128,1024]{1,0:T(8,128)(2,1)S(1)} %collective-permute-done.14.refs_6_), channel_id=1, source_target_pairs={{0,1},{1,0},{2,3},{3,2},{4,5},{5,4},{6,7},{7,6},{8,9},{9,8},{10,11... | collective-permute-start | bytes 786440 | tf_op jit(solution)/shard_map/ppermute | solution.py:39
  51.5 6.4 %collective-permute-start.18 = (bf16[128,1024]{1,0:T(8,128)(2,1)S(1)}, bf16[128,1024]{1,0:T(8,128)(2,1)S(1)}, u32[]{:S(2)}, u32[]{:S(2)}) collective-permute-start(bf16[128,1024]{1,0:T(8,128)(2,1)S(1)} %collective-permute-done.14.refs_6_), channel_id=1, source_target_pairs={{0,2},{1,5},{2,6},{3,1},{6,10},{7,3},{10,14},{11,7},{14,12},{15,11... | collective-permute-start | bytes 786440 | tf_op jit(solution)/shard_map/ppermute | solution.py:48
  54.3 3.6 %collective-permute-start.21 = (bf16[128,1024]{1,0:T(8,128)(2,1)S(1)}, bf16[128,1024]{1,0:T(8,128)(2,1)S(1)}, u32[]{:S(2)}, u32[]{:S(2)}) collective-permute-start(bf16[128,1024]{1,0:T(8,128)(2,1)S(1)} %collective-permute-done.16.refs_7_), channel_id=1, source_target_pairs={{0,1},{1,0},{2,3},{3,2},{4,5},{5,4},{6,7},{7,6},{8,9},{9,8},{10,11... | collective-permute-start | bytes 786440 | tf_op jit(solution)/shard_map/ppermute | solution.py:39
  57.9 1.5 %collective-permute-start.20 = (bf16[128,1024]{1,0:T(8,128)(2,1)S(1)}, bf16[128,1024]{1,0:T(8,128)(2,1)S(1)}, u32[]{:S(2)}, u32[]{:S(2)}) collective-permute-start(bf16[128,1024]{1,0:T(8,128)(2,1)S(1)} %collective-permute-done.18.refs_8_), channel_id=1, source_target_pairs={{0,1},{1,0},{2,3},{3,2},{4,5},{5,4},{6,7},{7,6},{8,9},{9,8},{10,11... | collective-permute-start | bytes 786440 | tf_op jit(solution)/shard_map/ppermute | solution.py:39
  84.5 1.6 %collective-permute-start.22 = (bf16[128,1024]{1,0:T(8,128)(2,1)S(1)}, bf16[128,1024]{1,0:T(8,128)(2,1)S(1)}, u32[]{:S(2)}, u32[]{:S(2)}) collective-permute-start(bf16[128,1024]{1,0:T(8,128)(2,1)S(1)} %get-tuple-element.106), channel_id=1, source_target_pairs={{0,1},{1,0},{2,3},{3,2},{4,5},{5,4},{6,7},{7,6},{8,9},{9,8},{10,11... | collective-permute-start | bytes 786440 | tf_op jit(solution)/shard_map/ppermute | solution.py:39
  84.7 3.5 %collective-permute-start.31 = (bf16[128,1024]{1,0:T(8,128)(2,1)S(1)}, bf16[128,1024]{1,0:T(8,128)(2,1)S(1)}, u32[]{:S(2)}, u32[]{:S(2)}) collective-permute-start(bf16[128,1024]{1,0:T(8,128)(2,1)S(1)} %get-tuple-element.121), channel_id=1, source_target_pairs={{0,1},{1,0},{2,3},{3,2},{4,5},{5,4},{6,7},{7,6},{8,9},{9,8},{10,11... | collective-permute-start | bytes 786440 | tf_op jit(solution)/shard_map/ppermute | solution.py:39
  86.2 6.4 %collective-permute-start.23 = (bf16[128,1024]{1,0:T(8,128)(2,1)S(1)}, bf16[128,1024]{1,0:T(8,128)(2,1)S(1)}, u32[]{:S(2)}, u32[]{:S(2)}) collective-permute-start(bf16[128,1024]{1,0:T(8,128)(2,1)S(1)} %add_convert_fusion.7), channel_id=1, source_target_pairs={{0,2},{1,5},{2,6},{3,1},{6,10},{7,3},{10,14},{11,7},{14,12},{15,11... | collective-permute-start | bytes 786440 | tf_op jit(solution)/shard_map/ppermute | solution.py:48
  88.2 4.4 %collective-permute-start.25 = (bf16[128,1024]{1,0:T(8,128)(2,1)S(1)}, bf16[128,1024]{1,0:T(8,128)(2,1)S(1)}, u32[]{:S(2)}, u32[]{:S(2)}) collective-permute-start(bf16[128,1024]{1,0:T(8,128)(2,1)S(1)} %get-tuple-element.110), channel_id=1, source_target_pairs={{0,1},{1,0},{2,3},{3,2},{4,5},{5,4},{6,7},{7,6},{8,9},{9,8},{10,11... | collective-permute-start | bytes 786440 | tf_op jit(solution)/shard_map/ppermute | solution.py:39
  88.3 7.1 %collective-permute-start.32 = (bf16[128,1024]{1,0:T(8,128)(2,1)S(1)}, bf16[128,1024]{1,0:T(8,128)(2,1)S(1)}, u32[]{:S(2)}, u32[]{:S(2)}) collective-permute-start(bf16[128,1024]{1,0:T(8,128)(2,1)S(1)} %add_convert_fusion.3), channel_id=1, source_target_pairs={{0,2},{1,5},{2,6},{3,1},{6,10},{7,3},{10,14},{11,7},{14,12},{15,11... | collective-permute-start | bytes 786440 | tf_op jit(solution)/shard_map/ppermute | solution.py:48
  89.9 5.5 %collective-permute-start.34 = (bf16[128,1024]{1,0:T(8,128)(2,1)S(1)}, bf16[128,1024]{1,0:T(8,128)(2,1)S(1)}, u32[]{:S(2)}, u32[]{:S(2)}) collective-permute-start(bf16[128,1024]{1,0:T(8,128)(2,1)S(1)} %get-tuple-element.125), channel_id=1, source_target_pairs={{0,1},{1,0},{2,3},{3,2},{4,5},{5,4},{6,7},{7,6},{8,9},{9,8},{10,11... | collective-permute-start | bytes 786440 | tf_op jit(solution)/shard_map/ppermute | solution.py:39
  92.8 6.4 %collective-permute-start.26 = (bf16[128,1024]{1,0:T(8,128)(2,1)S(1)}, bf16[128,1024]{1,0:T(8,128)(2,1)S(1)}, u32[]{:S(2)}, u32[]{:S(2)}) collective-permute-start(bf16[128,1024]{1,0:T(8,128)(2,1)S(1)} %add_convert_fusion.6), channel_id=1, source_target_pairs={{0,2},{1,5},{2,6},{3,1},{6,10},{7,3},{10,14},{11,7},{14,12},{15,11... | collective-permute-start | bytes 786440 | tf_op jit(solution)/shard_map/ppermute | solution.py:48
  94.8 4.4 %collective-permute-start.24 = (bf16[128,1024]{1,0:T(8,128)(2,1)S(1)}, bf16[128,1024]{1,0:T(8,128)(2,1)S(1)}, u32[]{:S(2)}, u32[]{:S(2)}) collective-permute-start(bf16[128,1024]{1,0:T(8,128)(2,1)S(1)} %get-tuple-element.108), channel_id=1, source_target_pairs={{0,1},{1,0},{2,3},{3,2},{4,5},{5,4},{6,7},{7,6},{8,9},{9,8},{10,11... | collective-permute-start | bytes 786440 | tf_op jit(solution)/shard_map/ppermute | solution.py:39
  95.4 6.6 %collective-permute-start.33 = (bf16[128,1024]{1,0:T(8,128)(2,1)S(1)}, bf16[128,1024]{1,0:T(8,128)(2,1)S(1)}, u32[]{:S(2)}, u32[]{:S(2)}) collective-permute-start(bf16[128,1024]{1,0:T(8,128)(2,1)S(1)} %get-tuple-element.123), channel_id=1, source_target_pairs={{0,1},{1,0},{2,3},{3,2},{4,5},{5,4},{6,7},{7,6},{8,9},{9,8},{10,11... | collective-permute-start | bytes 786440 | tf_op jit(solution)/shard_map/ppermute | solution.py:39
  95.6 6.4 %collective-permute-start.35 = (bf16[128,1024]{1,0:T(8,128)(2,1)S(1)}, bf16[128,1024]{1,0:T(8,128)(2,1)S(1)}, u32[]{:S(2)}, u32[]{:S(2)}) collective-permute-start(bf16[128,1024]{1,0:T(8,128)(2,1)S(1)} %add_convert_fusion.2), channel_id=1, source_target_pairs={{0,2},{1,5},{2,6},{3,1},{6,10},{7,3},{10,14},{11,7},{14,12},{15,11... | collective-permute-start | bytes 786440 | tf_op jit(solution)/shard_map/ppermute | solution.py:48
  99.3 6.4 %collective-permute-start.27 = (bf16[128,1024]{1,0:T(8,128)(2,1)S(1)}, bf16[128,1024]{1,0:T(8,128)(2,1)S(1)}, u32[]{:S(2)}, u32[]{:S(2)}) collective-permute-start(bf16[128,1024]{1,0:T(8,128)(2,1)S(1)} %add_convert_fusion.5), channel_id=1, source_target_pairs={{0,2},{1,5},{2,6},{3,1},{6,10},{7,3},{10,14},{11,7},{14,12},{15,11... | collective-permute-start | bytes 786440 | tf_op jit(solution)/shard_map/ppermute | solution.py:48
  101.3 4.4 %collective-permute-start.29 = (bf16[128,1024]{1,0:T(8,128)(2,1)S(1)}, bf16[128,1024]{1,0:T(8,128)(2,1)S(1)}, u32[]{:S(2)}, u32[]{:S(2)}) collective-permute-start(bf16[128,1024]{1,0:T(8,128)(2,1)S(1)} %get-tuple-element.117), channel_id=1, source_target_pairs={{0,1},{1,0},{2,3},{3,2},{4,5},{5,4},{6,7},{7,6},{8,9},{9,8},{10,11... | collective-permute-start | bytes 786440 | tf_op jit(solution)/shard_map/ppermute | solution.py:39
  102.1 5.9 %collective-permute-start.36 = (bf16[128,1024]{1,0:T(8,128)(2,1)S(1)}, bf16[128,1024]{1,0:T(8,128)(2,1)S(1)}, u32[]{:S(2)}, u32[]{:S(2)}) collective-permute-start(bf16[128,1024]{1,0:T(8,128)(2,1)S(1)} %add_convert_fusion.1), channel_id=1, source_target_pairs={{0,3},{1,4},{2,7},{3,0},{6,11},{7,2},{10,15},{11,6},{14,13},{15,10... | collective-permute-start | bytes 786440 | tf_op jit(solution)/shard_map/ppermute | solution.py:48
  105.7 2.3 %collective-permute-start.28 = (bf16[128,1024]{1,0:T(8,128)(2,1)S(1)}, bf16[128,1024]{1,0:T(8,128)(2,1)S(1)}, u32[]{:S(2)}, u32[]{:S(2)}) collective-permute-start(bf16[128,1024]{1,0:T(8,128)(2,1)S(1)} %get-tuple-element.115), channel_id=1, source_target_pairs={{0,1},{1,0},{2,3},{3,2},{4,5},{5,4},{6,7},{7,6},{8,9},{9,8},{10,11... | collective-permute-start | bytes 786440 | tf_op jit(solution)/shard_map/ppermute | solution.py:39
  105.9 6.4 %collective-permute-start.30 = (bf16[128,1024]{1,0:T(8,128)(2,1)S(1)}, bf16[128,1024]{1,0:T(8,128)(2,1)S(1)}, u32[]{:S(2)}, u32[]{:S(2)}) collective-permute-start(bf16[128,1024]{1,0:T(8,128)(2,1)S(1)} %add_convert_fusion.4), channel_id=1, source_target_pairs={{0,2},{1,5},{2,6},{3,1},{6,10},{7,3},{10,14},{11,7},{14,12},{15,11... | collective-permute-start | bytes 786440 | tf_op jit(solution)/shard_map/ppermute | solution.py:48

commit v14 on v13

--- a/solution.py
+++ b/solution.py
@@ -72,18 +72,21 @@
     if count > FEW:
         return list(lax.all_gather(block, "ctx")), [run(*arguments) for run, arguments in beside]
     middle = count // 2
+    cycle = cycle_of(count)
     found, other, made = [block], [()], []
-    for d in range(1, middle + 1):
+    opposite = lax.ppermute(block, "ctx", [(cycle[p], cycle[(p + middle) % count]) for p in range(count)])
+    for d in range(1, middle):
         arrived, extra = turn(found[-1], count), ()
         if len(beside) >= d:
             run, arguments = beside[d - 1]
             extra = run(*lax.optimization_barrier((found[-1], arguments))[1])
+        if d == 2:
+            arrived, opposite = lax.optimization_barrier((arrived, opposite))
         arrived, other[-1], extra = lax.optimization_barrier((arrived, other[-1], extra))
         made.append(extra)
         found.append(arrived)
-        if d < middle:
-            other.append(swap(arrived))
-    return found + other[1:], made[: len(beside)]
+        other.append(swap(arrived))
+    return found + [opposite] + other[1:], made[: len(beside)]
 
 
 def gather_columns(near, far, count):
@@ -121,11 +124,11 @@
 
 
 def attend_kernel(count, blocks, heads, info, *refs):
-    latents, refs = refs[: len(refs) - 14], refs[len(refs) - 14 :]
-    wanted, (out_ref, base_ref) = refs[:4], refs[4:6]
-    held, sems, (m_ref, l_ref, acc_ref) = refs[6:10], refs[10], refs[11:14]
-    q_ref, up_ref, proj_ref, residual_ref = held
-    copies = [pltpu.make_async_copy(wanted[i], held[i], sems.at[i]) for i in range(4)]
+    latents, up_ref, refs = refs[: len(refs) - 13], refs[len(refs) - 13], refs[len(refs) - 12 :]
+    wanted, (out_ref, base_ref) = refs[:3], refs[3:5]
+    held, sems, (m_ref, l_ref, acc_ref) = refs[5:8], refs[8], refs[9:12]
+    q_ref, proj_ref, residual_ref = held
+    copies = [pltpu.make_async_copy(wanted[i], held[i], sems.at[i]) for i in range(3)]
     chunk = pl.program_id(0)
     sources = lambda c: info[2 + c]
     order = lambda j: info[2 + count + j]
@@ -169,7 +172,6 @@
     @pl.when(chunk == 0)
     def _():
         copies[0].wait()
-        copies[1].wait()
 
     keyval = jnp.dot(lat[:, :LAT], up_ref[...], preferred_element_type=jnp.float32).astype(jnp.bfloat16)
     rope = lat[:, LAT : LAT + ROPE]
@@ -193,8 +195,8 @@
     @pl.when(chunk == pl.num_programs(0) - 1)
     def _():
         attended = [(acc_ref[h] / l_ref[h]).astype(jnp.bfloat16) for h in range(heads)]
+        copies[1].wait()
         copies[2].wait()
-        copies[3].wait()
         out = jnp.dot(jnp.concatenate(attended, axis=1), proj_ref[...], preferred_element_type=jnp.float32)
         out = out.astype(jnp.bfloat16)
         out_ref[...] = out
@@ -210,17 +212,17 @@
         latents, lat_spec = found, whole
     else:
         latents, lat_spec = [jnp.stack(found)], pl.BlockSpec((blocks, rows, WIDE), lambda i, *_: (i, 0, 0))
-    wanted = (queries, kv_up, out_proj, residual)
+    wanted = (queries, out_proj, residual)
     return pl.pallas_call(
         functools.partial(attend_kernel, count, blocks, heads),
         grid_spec=pltpu.PrefetchScalarGridSpec(
             num_scalar_prefetch=1,
             grid=(count // blocks,),
-            in_specs=[lat_spec] * len(latents) + [pl.BlockSpec(memory_space=pltpu.HBM)] * 4,
+            in_specs=[lat_spec] * len(latents) + [whole] + [pl.BlockSpec(memory_space=pltpu.HBM)] * 3,
             out_specs=[whole, whole],
             scratch_shapes=[pltpu.VMEM(x.shape, x.dtype) for x in wanted]
             + [
-                pltpu.SemaphoreType.DMA((4,)),
+                pltpu.SemaphoreType.DMA((3,)),
                 pltpu.VMEM((heads, rows, 1), jnp.float32),
                 pltpu.VMEM((heads, rows, 1), jnp.float32),
                 pltpu.VMEM((heads, rows, VHEAD), jnp.float32),
@@ -229,7 +231,25 @@
         out_shape=[pltpu.VMEM((rows, width), jnp.bfloat16), pltpu.VMEM((rows, width), jnp.float32)],
         compiler_params=pltpu.CompilerParams(vmem_limit_bytes=28 * MIB),
         name="attend",
-    )(info, *latents, *(pltpu.with_memory_space_constraint(x, pltpu.HBM) for x in wanted))
+    )(info, *latents, kv_up, *(pltpu.with_memory_space_constraint(x, pltpu.HBM) for x in wanted))
+
+
+def stage_kernel(source, out, sem):
+    copy = pltpu.make_async_copy(source, out, sem)
+    copy.start()
+    copy.wait()
+
+
+def stage(x):
+    return pl.pallas_call(
+        stage_kernel,
+        in_specs=[pl.BlockSpec(memory_space=pltpu.HBM)],
+        out_specs=pl.BlockSpec(memory_space=pltpu.VMEM),
+        scratch_shapes=[pltpu.SemaphoreType.DMA],
+        out_shape=pltpu.VMEM(x.shape, x.dtype),
+        compiler_params=pltpu.CompilerParams(vmem_limit_bytes=2 * MIB),
+        name="stage",
+    )(pltpu.with_memory_space_constraint(x, pltpu.HBM))
 
 
 def route_kernel(count, where, *refs):
@@ -474,8 +494,12 @@
     packed = pack(latent, expert_ids, route_weights)
     few = count <= FEW
     scalars = lambda *arrays: jnp.concatenate([where, sources_of(me, side, count), *arrays])
-    beside = [(scalars, (span_order, seg_lengths)), (lambda gain: gain.reshape(1, width), (norm_gain,))]
-    found, (info, gain) = gather(packed, count, beside)
+    beside = [
+        (scalars, (span_order, seg_lengths)),
+        (lambda gain: gain.reshape(1, width), (norm_gain,)),
+        (stage if few else lambda x: x, (kv_up,)),
+    ]
+    found, (info, gain, kv_up) = gather(packed, count, beside)
     partial, summand = attend(info, found, queries, kv_up, out_proj, residual, count)
     def place_rows(*blocks):
         if few:

time: 113 us -> 115 us (1.018)
  waiting for transfers between devices: 38.3 us -> 55.2 us
  starting transfers between devices: 36 us -> 19.4 us
    ppermute x18 -> x17, starting transfers between devices: 35.3 us -> 13.5 us  [turn(): return lax.ppermute(value, ('ctx', 'exp'), pairs)]
    ppermute x18 -> x17, waiting for transfers between devices: 35.7 us -> 47.4 us  [turn(): return lax.ppermute(value, ('ctx', 'exp'), pairs)]
    ppermute x0 -> x1, waiting for transfers between devices: none -> 3.73 us  [gather(): lax.ppermute(block, 'ctx', [(cycle[p], cycle[(p + middle) % count]) for p...]
    ppermute x0 -> x1, starting transfers between devices: none -> 3.55 us  [gather(): lax.ppermute(block, 'ctx', [(cycle[p], cycle[(p + middle) % count]) for p...]
    ppermute x19, starting transfers between devices: 0.69 us -> 2.35 us  [swap(): return lax.ppermute(value, 'exp', SWAP)]
    ppermute x19, waiting for transfers between devices: 2.6 us -> 4.09 us  [swap(): return lax.ppermute(value, 'exp', SWAP)]
    pallas_call x0 -> x1, Pallas kernels: none -> 1.23 us  [stage(): pl.pallas_call(stage_kernel, in_specs=[pl.BlockSpec(memory_space=pltpu.HB...]
  transfers between devices with their start and end apart: 37 -> 37, of which waited for: 20 -> 21; matrix products, arithmetic and copies ran while one was open for 3% -> 3% of each run, Pallas kernels for 2% -> 3%
where the time goes in v14:
time: 115 us; the launch traced here: 114 us
  waiting for transfers between devices  55.2 us (48%)
  Pallas kernels  35.7 us (31%)
  starting transfers between devices  19.4 us (17%)
  local copies, waits for them, and re-layouts  2.13 us (2%)
  other arithmetic  1.75 us (2%)
    ppermute x17, waiting for transfers between devices, turn(): return lax.ppermute(value, ('ctx', 'exp'), pairs)  47.4 us
    pallas_call x1, Pallas kernels, experts_fused(): pl.pallas_call(functools.partial(fused_kernel, count), in_specs=[pl.Block...  25.1 us
    ppermute x17, starting transfers between devices, turn(): return lax.ppermute(value, ('ctx', 'exp'), pairs)  13.5 us
    pallas_call x1, Pallas kernels, attend(): pl.pallas_call(functools.partial(attend_kernel, count, blocks, heads), gr...  5.43 us
    ppermute x19, waiting for transfers between devices, swap(): return lax.ppermute(value, 'exp', SWAP)  4.09 us
    ppermute x1, waiting for transfers between devices, gather(): lax.ppermute(block, 'ctx', [(cycle[p], cycle[(p + middle) % count]) for p...  3.73 us
    ppermute x1, starting transfers between devices, gather(): lax.ppermute(block, 'ctx', [(cycle[p], cycle[(p + middle) % count]) for p...  3.55 us
    ppermute x19, starting transfers between devices, swap(): return lax.ppermute(value, 'exp', SWAP)  2.35 us
  transfers between devices with their start and end apart: 37, of which 21 were waited for; matrix products, arithmetic and copies ran while one was open for 3% of the time, Pallas kernels for 3%

profile of v14, /device:TPU:0, one launch (start us, length us, event | category | flops | bytes accessed | tf_op | source)
XLA Modules:
  0.0 114.3 jit_solution(14830557721238569210)
XLA Ops:
  0.0 1.1 pack.1.refs_0_
  1.1 3.0 %collective-permute-start = (bf16[128,640]{1,0:T(8,128)(2,1)S(1)}, bf16[128,640]{1,0:T(8,128)(2,1)S(1)}, u32[]{:S(2)}, u32[]{:S(2)}) collective-permute-start(bf16[128,640]{1,0:T(8,128)(2,1)S(1)} %pack.1.refs_0_), channel_id=1, source_target_pairs={{0,2},{1,5},{2,6},{3,1},{6,10},{7,3},{10,14},{11,7},{14,12},{15,11... | collective-permute-start | bytes 491528 | tf_op jit(solution)/shard_map/ppermute | solution.py:48
  4.2 3.5 %collective-permute-start.2 = (bf16[128,640]{1,0:T(8,128)(2,1)S(1)}, bf16[128,640]{1,0:T(8,128)(2,1)S(1)}, u32[]{:S(2)}, u32[]{:S(2)}) collective-permute-start(bf16[128,640]{1,0:T(8,128)(2,1)S(1)} %pack.1.refs_0_), channel_id=1, source_target_pairs={{0,14},{2,12},{6,8},{10,4},{14,0},{12,2},{8,6},{4,10},{1,15},{3,13... | collective-permute-start | bytes 491528 | tf_op jit(solution)/shard_map/ppermute | solution.py:77
  7.7 0.7 dynamic-slice_bitcast_fusion
  8.4 0.7 concatenate.4.info
  9.2 0.5 collective-permute-start.1
  9.6 0.7 reshape.3.gain_ref
  10.3 3.7 %collective-permute-done.2.refs_4_ = bf16[128,640]{1,0:T(8,128)(2,1)S(1)} collective-permute-done((bf16[128,640]{1,0:T(8,128)(2,1)S(1)}, bf16[128,640]{1,0:T(8,128)(2,1)S(1)}, u32[]{:S(2)}, u32[]{:S(2)}) %collective-permute-start.2) | collective-permute-done | bytes 163872 | tf_op jit(solution)/shard_map/ppermute | solution.py:77
  14.1 4.1 %collective-permute-done.1.refs_2_ = bf16[128,640]{1,0:T(8,128)(2,1)S(1)} collective-permute-done((bf16[128,640]{1,0:T(8,128)(2,1)S(1)}, bf16[128,640]{1,0:T(8,128)(2,1)S(1)}, u32[]{:S(2)}, u32[]{:S(2)}) %collective-permute-start.1) | collective-permute-done | bytes 163872 | tf_op jit(solution)/shard_map/ppermute | solution.py:48
  18.2 1.2 %stage.1.refs_8_ = bf16[512,1024]{1,0:T(8,128)(2,1)S(1)} custom-call(bf16[512,1024]{1,0:T(8,128)(2,1)} %source), custom_call_target="tpu_custom_call" | custom-call | tf_op jit(solution)/shard_map/stage/pallas_call | solution.py:244
  19.5 3.9 %collective-permute-done.4.refs_3_ = bf16[128,640]{1,0:T(8,128)(2,1)S(1)} collective-permute-done((bf16[128,640]{1,0:T(8,128)(2,1)S(1)}, bf16[128,640]{1,0:T(8,128)(2,1)S(1)}, u32[]{:S(2)}, u32[]{:S(2)}) %collective-permute-start.4) | collective-permute-done | bytes 163872 | tf_op jit(solution)/shard_map/ppermute | solution.py:48
  23.4 1.4 %collective-permute-done.6.refs_7_ = bf16[128,640]{1,0:T(8,128)(2,1)S(1)} collective-permute-done((bf16[128,640]{1,0:T(8,128)(2,1)S(1)}, bf16[128,640]{1,0:T(8,128)(2,1)S(1)}, u32[]{:S(2)}, u32[]{:S(2)}) %collective-permute-start.6) | collective-permute-done | bytes 163872 | tf_op jit(solution)/shard_map/ppermute | solution.py:39
  24.8 5.4 %attend.1 = (bf16[128,2048]{1,0:T(8,128)(2,1)S(1)}, f32[128,2048]{1,0:T(8,128)S(1)}) custom-call(s32[42]{0:T(128)S(1)} %concatenate.4.info, bf16[128,640]{1,0:T(8,128)(2,1)S(1)} %pack.1.refs_0_, bf16[128,640]{1,0:T(8,128)(2,1)S(1)} %collective-permute-done.refs_1_, bf16[128,640]{1,0:T(8,128)(2,1)S(1)} %collective-permute-done.1.refs_2_, ...), custom_call_target="tpu_custom_call" | custom-call | tf_op jit(solution)/shard_map/attend/pallas_call | solution.py:216
  30.6 1.8 %route.1.refs_16_ = bf16[8,128,128]{2,1,0:T(8,128)(2,1)S(1)} custom-call(s32[2]{0:T(128)S(1)} %pad_add_fusion.where, bf16[128,640]{1,0:T(8,128)(2,1)S(1)} %pack.1.refs_0_, bf16[128,640]{1,0:T(8,128)(2,1)S(1)} %collective-permute-done.refs_1_, bf16[128,640]{1,0:T(8,128)(2,1)S(1)} %collective-permute-done.1.refs_2_, ...), custom_call_target="tpu_custom_call" | custom-call | tf_op jit(solution)/shard_map/route/pallas_call | solution.py:278
  32.4 0.9 norm.1
  33.4 2.5 %collective-permute-start.9 = (bf16[128,1024]{1,0:T(8,128)(2,1)S(1)}, bf16[128,1024]{1,0:T(8,128)(2,1)S(1)}, u32[]{:S(2)}, u32[]{:S(2)}) collective-permute-start(bf16[128,1024]{1,0:T(8,128)(2,1)S(1)} %get-tuple-element.95.refs_1_), channel_id=1, source_target_pairs={{0,2},{1,5},{2,6},{3,1},{6,10},{7,3},{10,14},{11,7},{14,12},{15,11... | collective-permute-start | bytes 786440 | tf_op jit(solution)/shard_map/ppermute | solution.py:48
  35.9 3.8 %collective-permute-done.8.refs_2_ = bf16[128,1024]{1,0:T(8,128)(2,1)S(1)} collective-permute-done((bf16[128,1024]{1,0:T(8,128)(2,1)S(1)}, bf16[128,1024]{1,0:T(8,128)(2,1)S(1)}, u32[]{:S(2)}, u32[]{:S(2)}) %collective-permute-start.8) | collective-permute-done | bytes 262176 | tf_op jit(solution)/shard_map/ppermute | solution.py:48
  39.8 0.3 collective-permute-start.10
  40.1 2.5 %collective-permute-done.9.refs_3_ = bf16[128,1024]{1,0:T(8,128)(2,1)S(1)} collective-permute-done((bf16[128,1024]{1,0:T(8,128)(2,1)S(1)}, bf16[128,1024]{1,0:T(8,128)(2,1)S(1)}, u32[]{:S(2)}, u32[]{:S(2)}) %collective-permute-start.9) | collective-permute-done | bytes 262176 | tf_op jit(solution)/shard_map/ppermute | solution.py:48
  42.7 3.4 %collective-permute-done.10.refs_4_ = bf16[128,1024]{1,0:T(8,128)(2,1)S(1)} collective-permute-done((bf16[128,1024]{1,0:T(8,128)(2,1)S(1)}, bf16[128,1024]{1,0:T(8,128)(2,1)S(1)}, u32[]{:S(2)}, u32[]{:S(2)}) %collective-permute-start.10) | collective-permute-done | bytes 262176 | tf_op jit(solution)/shard_map/ppermute | solution.py:48
  46.1 0.4 collective-permute-start.14
  46.6 2.4 %collective-permute-done.12.refs_5_ = bf16[128,1024]{1,0:T(8,128)(2,1)S(1)} collective-permute-done((bf16[128,1024]{1,0:T(8,128)(2,1)S(1)}, bf16[128,1024]{1,0:T(8,128)(2,1)S(1)}, u32[]{:S(2)}, u32[]{:S(2)}) %collective-permute-start.12) | collective-permute-done | bytes 262176 | tf_op jit(solution)/shard_map/ppermute | solution.py:48
  48.9 0.4 collective-permute-start.16
  49.4 3.1 %collective-permute-done.14.refs_6_ = bf16[128,1024]{1,0:T(8,128)(2,1)S(1)} collective-permute-done((bf16[128,1024]{1,0:T(8,128)(2,1)S(1)}, bf16[128,1024]{1,0:T(8,128)(2,1)S(1)}, u32[]{:S(2)}, u32[]{:S(2)}) %collective-permute-start.14) | collective-permute-done | bytes 262176 | tf_op jit(solution)/shard_map/ppermute | solution.py:48
  52.5 0.7 collective-permute-start.18
  53.2 2.1 %collective-permute-done.16.refs_7_ = bf16[128,1024]{1,0:T(8,128)(2,1)S(1)} collective-permute-done((bf16[128,1024]{1,0:T(8,128)(2,1)S(1)}, bf16[128,1024]{1,0:T(8,128)(2,1)S(1)}, u32[]{:S(2)}, u32[]{:S(2)}) %collective-permute-start.16) | collective-permute-done | bytes 262176 | tf_op jit(solution)/shard_map/ppermute | solution.py:48
  55.3 3.6 %collective-permute-done.18.refs_8_ = bf16[128,1024]{1,0:T(8,128)(2,1)S(1)} collective-permute-done((bf16[128,1024]{1,0:T(8,128)(2,1)S(1)}, bf16[128,1024]{1,0:T(8,128)(2,1)S(1)}, u32[]{:S(2)}, u32[]{:S(2)}) %collective-permute-start.18) | collective-permute-done | bytes 262176 | tf_op jit(solution)/shard_map/ppermute | solution.py:48
  58.9 1.5 %collective-permute-done.20.refs_9_ = bf16[128,1024]{1,0:T(8,128)(2,1)S(1)} collective-permute-done((bf16[128,1024]{1,0:T(8,128)(2,1)S(1)}, bf16[128,1024]{1,0:T(8,128)(2,1)S(1)}, u32[]{:S(2)}, u32[]{:S(2)}) %collective-permute-start.20) | collective-permute-done | bytes 262176 | tf_op jit(solution)/shard_map/ppermute | solution.py:39
  60.4 25.1 %experts.1 = (bf16[128,1024]{1,0:T(8,128)(2,1)S(1)}, bf16[128,1024]{1,0:T(8,128)(2,1)S(1)}, bf16[128,1024]{1,0:T(8,128)(2,1)S(1)}, bf16[128,1024]{1,0:T(8,128)(2...) custom-call(s32[2]{0:T(128)S(1)} %pad_add_fusion.where, ...), custom_call_target="tpu_custom_call" | custom-call | tf_op jit(solution)/shard_map/experts/pallas_call | solution.py:454
  85.8 0.4 collective-permute-start.31
  86.1 1.0 collective-permute-done.22
  87.2 0.7 collective-permute-start.23
  88.0 1.2 %collective-permute-start.25 = (bf16[128,1024]{1,0:T(8,128)(2,1)S(1)}, bf16[128,1024]{1,0:T(8,128)(2,1)S(1)}, u32[]{:S(2)}, u32[]{:S(2)}) collective-permute-start(bf16[128,1024]{1,0:T(8,128)(2,1)S(1)} %get-tuple-element.114), channel_id=1, source_target_pairs={{0,1},{1,0},{2,3},{3,2},{4,5},{5,4},{6,7},{7,6},{8,9},{9,8},{10,11... | collective-permute-start | bytes 786440 | tf_op jit(solution)/shard_map/ppermute | solution.py:39
  89.2 1.1 collective-permute-start.32
  90.3 3.3 %collective-permute-done.23 = bf16[128,1024]{1,0:T(8,128)(2,1)S(1)} collective-permute-done((bf16[128,1024]{1,0:T(8,128)(2,1)S(1)}, bf16[128,1024]{1,0:T(8,128)(2,1)S(1)}, u32[]{:S(2)}, u32[]{:S(2)}) %collective-permute-start.23) | collective-permute-done | bytes 262176 | tf_op jit(solution)/shard_map/ppermute | solution.py:48
  93.8 0.7 collective-permute-start.26
  94.5 0.3 collective-permute-start.24
  94.9 1.6 %collective-permute-done.32 = bf16[128,1024]{1,0:T(8,128)(2,1)S(1)} collective-permute-done((bf16[128,1024]{1,0:T(8,128)(2,1)S(1)}, bf16[128,1024]{1,0:T(8,128)(2,1)S(1)}, u32[]{:S(2)}, u32[]{:S(2)}) %collective-permute-start.32) | collective-permute-done | bytes 262176 | tf_op jit(solution)/shard_map/ppermute | solution.py:48
  96.6 0.8 collective-permute-start.35
  97.4 2.8 %collective-permute-done.26 = bf16[128,1024]{1,0:T(8,128)(2,1)S(1)} collective-permute-done((bf16[128,1024]{1,0:T(8,128)(2,1)S(1)}, bf16[128,1024]{1,0:T(8,128)(2,1)S(1)}, u32[]{:S(2)}, u32[]{:S(2)}) %collective-permute-start.26) | collective-permute-done | bytes 262176 | tf_op jit(solution)/shard_map/ppermute | solution.py:48
  100.4 0.7 collective-permute-start.27
  101.1 1.9 %collective-permute-done.35 = bf16[128,1024]{1,0:T(8,128)(2,1)S(1)} collective-permute-done((bf16[128,1024]{1,0:T(8,128)(2,1)S(1)}, bf16[128,1024]{1,0:T(8,128)(2,1)S(1)}, u32[]{:S(2)}, u32[]{:S(2)}) %collective-permute-start.35) | collective-permute-done | bytes 262176 | tf_op jit(solution)/shard_map/ppermute | solution.py:48
  103.2 0.5 collective-permute-start.36
  103.6 3.1 %collective-permute-done.27 = bf16[128,1024]{1,0:T(8,128)(2,1)S(1)} collective-permute-done((bf16[128,1024]{1,0:T(8,128)(2,1)S(1)}, bf16[128,1024]{1,0:T(8,128)(2,1)S(1)}, u32[]{:S(2)}, u32[]{:S(2)}) %collective-permute-start.27) | collective-permute-done | bytes 262176 | tf_op jit(solution)/shard_map/ppermute | solution.py:48
  106.9 0.7 collective-permute-start.30
  107.6 1.4 %collective-permute-done.36 = bf16[128,1024]{1,0:T(8,128)(2,1)S(1)} collective-permute-done((bf16[128,1024]{1,0:T(8,128)(2,1)S(1)}, bf16[128,1024]{1,0:T(8,128)(2,1)S(1)}, u32[]{:S(2)}, u32[]{:S(2)}) %collective-permute-start.36) | collective-permute-done | bytes 262176 | tf_op jit(solution)/shard_map/ppermute | solution.py:48
  109.0 4.3 %collective-permute-done.30 = bf16[128,1024]{1,0:T(8,128)(2,1)S(1)} collective-permute-done((bf16[128,1024]{1,0:T(8,128)(2,1)S(1)}, bf16[128,1024]{1,0:T(8,128)(2,1)S(1)}, u32[]{:S(2)}, u32[]{:S(2)}) %collective-permute-start.30) | collective-permute-done | bytes 262176 | tf_op jit(solution)/shard_map/ppermute | solution.py:48
  113.3 0.9 add_convert_fusion
  (44 shorter events, 1.7 us)
Async XLA Ops:
  1.1 8.0 %collective-permute-start = (bf16[128,640]{1,0:T(8,128)(2,1)S(1)}, bf16[128,640]{1,0:T(8,128)(2,1)S(1)}, u32[]{:S(2)}, u32[]{:S(2)}) collective-permute-start(bf16[128,640]{1,0:T(8,128)(2,1)S(1)} %pack.1.refs_0_), channel_id=1, source_target_pairs={{0,2},{1,5},{2,6},{3,1},{6,10},{7,3},{10,14},{11,7},{14,12},{15,11... | collective-permute-start | bytes 491528 | tf_op jit(solution)/shard_map/ppermute | solution.py:48
  4.2 9.9 %collective-permute-start.2 = (bf16[128,640]{1,0:T(8,128)(2,1)S(1)}, bf16[128,640]{1,0:T(8,128)(2,1)S(1)}, u32[]{:S(2)}, u32[]{:S(2)}) collective-permute-start(bf16[128,640]{1,0:T(8,128)(2,1)S(1)} %pack.1.refs_0_), channel_id=1, source_target_pairs={{0,14},{2,12},{6,8},{10,4},{14,0},{12,2},{8,6},{4,10},{1,15},{3,13... | collective-permute-start | bytes 491528 | tf_op jit(solution)/shard_map/ppermute | solution.py:77
  9.2 8.9 %collective-permute-start.1 = (bf16[128,640]{1,0:T(8,128)(2,1)S(1)}, bf16[128,640]{1,0:T(8,128)(2,1)S(1)}, u32[]{:S(2)}, u32[]{:S(2)}) collective-permute-start(bf16[128,640]{1,0:T(8,128)(2,1)S(1)} %collective-permute-done.refs_1_), channel_id=1, source_target_pairs={{0,2},{1,5},{2,6},{3,1},{6,10},{7,3},{10,14},{11,7},{14,12},{15,11... | collective-permute-start | bytes 491528 | tf_op jit(solution)/shard_map/ppermute | solution.py:48
  9.6 8.5 %collective-permute-start.3 = (bf16[128,640]{1,0:T(8,128)(2,1)S(1)}, bf16[128,640]{1,0:T(8,128)(2,1)S(1)}, u32[]{:S(2)}, u32[]{:S(2)}) collective-permute-start(bf16[128,640]{1,0:T(8,128)(2,1)S(1)} %collective-permute-done.refs_1_), channel_id=1, source_target_pairs={{0,1},{1,0},{2,3},{3,2},{4,5},{5,4},{6,7},{7,6},{8,9},{9,8},{10,11... | collective-permute-start | bytes 491528 | tf_op jit(solution)/shard_map/ppermute | solution.py:39
  18.1 1.4 %collective-permute-start.5 = (bf16[128,640]{1,0:T(8,128)(2,1)S(1)}, bf16[128,640]{1,0:T(8,128)(2,1)S(1)}, u32[]{:S(2)}, u32[]{:S(2)}) collective-permute-start(bf16[128,640]{1,0:T(8,128)(2,1)S(1)} %collective-permute-done.1.refs_2_), channel_id=1, source_target_pairs={{0,1},{1,0},{2,3},{3,2},{4,5},{5,4},{6,7},{7,6},{8,9},{9,8},{10,11... | collective-permute-start | bytes 491528 | tf_op jit(solution)/shard_map/ppermute | solution.py:39
  18.1 5.3 %collective-permute-start.4 = (bf16[128,640]{1,0:T(8,128)(2,1)S(1)}, bf16[128,640]{1,0:T(8,128)(2,1)S(1)}, u32[]{:S(2)}, u32[]{:S(2)}) collective-permute-start(bf16[128,640]{1,0:T(8,128)(2,1)S(1)} %collective-permute-done.1.refs_2_), channel_id=1, source_target_pairs={{0,2},{1,5},{2,6},{3,1},{6,10},{7,3},{10,14},{11,7},{14,12},{15,11... | collective-permute-start | bytes 491528 | tf_op jit(solution)/shard_map/ppermute | solution.py:48
  23.4 1.4 %collective-permute-start.6 = (bf16[128,640]{1,0:T(8,128)(2,1)S(1)}, bf16[128,640]{1,0:T(8,128)(2,1)S(1)}, u32[]{:S(2)}, u32[]{:S(2)}) collective-permute-start(bf16[128,640]{1,0:T(8,128)(2,1)S(1)} %collective-permute-done.4.refs_3_), channel_id=1, source_target_pairs={{0,1},{1,0},{2,3},{3,2},{4,5},{5,4},{6,7},{7,6},{8,9},{9,8},{10,11... | collective-permute-start | bytes 491528 | tf_op jit(solution)/shard_map/ppermute | solution.py:39
  30.3 2.1 %collective-permute-start.7 = (bf16[128,2048]{1,0:T(8,128)(2,1)S(1)}, bf16[128,2048]{1,0:T(8,128)(2,1)S(1)}, u32[]{:S(2)}, u32[]{:S(2)}) collective-permute-start(bf16[128,2048]{1,0:T(8,128)(2,1)S(1)} %get-tuple-element.82), channel_id=1, source_target_pairs={{0,1},{1,0},{2,3},{3,2},{4,5},{5,4},{6,7},{7,6},{8,9},{9,8},{10,11... | collective-permute-start | bytes 1572872 | tf_op jit(solution)/shard_map/ppermute | solution.py:39
  33.3 6.4 %collective-permute-start.8 = (bf16[128,1024]{1,0:T(8,128)(2,1)S(1)}, bf16[128,1024]{1,0:T(8,128)(2,1)S(1)}, u32[]{:S(2)}, u32[]{:S(2)}) collective-permute-start(bf16[128,1024]{1,0:T(8,128)(2,1)S(1)} %get-tuple-element.94.refs_0_), channel_id=1, source_target_pairs={{0,2},{1,5},{2,6},{3,1},{6,10},{7,3},{10,14},{11,7},{14,12},{15,11... | collective-permute-start | bytes 786440 | tf_op jit(solution)/shard_map/ppermute | solution.py:48
  33.4 9.1 %collective-permute-start.9 = (bf16[128,1024]{1,0:T(8,128)(2,1)S(1)}, bf16[128,1024]{1,0:T(8,128)(2,1)S(1)}, u32[]{:S(2)}, u32[]{:S(2)}) collective-permute-start(bf16[128,1024]{1,0:T(8,128)(2,1)S(1)} %get-tuple-element.95.refs_1_), channel_id=1, source_target_pairs={{0,2},{1,5},{2,6},{3,1},{6,10},{7,3},{10,14},{11,7},{14,12},{15,11... | collective-permute-start | bytes 786440 | tf_op jit(solution)/shard_map/ppermute | solution.py:48
  39.8 3.0 %collective-permute-start.11 = (bf16[128,1024]{1,0:T(8,128)(2,1)S(1)}, bf16[128,1024]{1,0:T(8,128)(2,1)S(1)}, u32[]{:S(2)}, u32[]{:S(2)}) collective-permute-start(bf16[128,1024]{1,0:T(8,128)(2,1)S(1)} %collective-permute-done.8.refs_2_), channel_id=1, source_target_pairs={{0,1},{1,0},{2,3},{3,2},{4,5},{5,4},{6,7},{7,6},{8,9},{9,8},{10,11... | collective-permute-start | bytes 786440 | tf_op jit(solution)/shard_map/ppermute | solution.py:39
  39.8 6.4 %collective-permute-start.10 = (bf16[128,1024]{1,0:T(8,128)(2,1)S(1)}, bf16[128,1024]{1,0:T(8,128)(2,1)S(1)}, u32[]{:S(2)}, u32[]{:S(2)}) collective-permute-start(bf16[128,1024]{1,0:T(8,128)(2,1)S(1)} %collective-permute-done.8.refs_2_), channel_id=1, source_target_pairs={{0,2},{1,5},{2,6},{3,1},{6,10},{7,3},{10,14},{11,7},{14,12},{15,11... | collective-permute-start | bytes 786440 | tf_op jit(solution)/shard_map/ppermute | solution.py:48
  42.6 4.0 %collective-permute-start.13 = (bf16[128,1024]{1,0:T(8,128)(2,1)S(1)}, bf16[128,1024]{1,0:T(8,128)(2,1)S(1)}, u32[]{:S(2)}, u32[]{:S(2)}) collective-permute-start(bf16[128,1024]{1,0:T(8,128)(2,1)S(1)} %collective-permute-done.9.refs_3_), channel_id=1, source_target_pairs={{0,1},{1,0},{2,3},{3,2},{4,5},{5,4},{6,7},{7,6},{8,9},{9,8},{10,11... | collective-permute-start | bytes 786440 | tf_op jit(solution)/shard_map/ppermute | solution.py:39
  42.6 6.4 %collective-permute-start.12 = (bf16[128,1024]{1,0:T(8,128)(2,1)S(1)}, bf16[128,1024]{1,0:T(8,128)(2,1)S(1)}, u32[]{:S(2)}, u32[]{:S(2)}) collective-permute-start(bf16[128,1024]{1,0:T(8,128)(2,1)S(1)} %collective-permute-done.9.refs_3_), channel_id=1, source_target_pairs={{0,2},{1,5},{2,6},{3,1},{6,10},{7,3},{10,14},{11,7},{14,12},{15,11... | collective-permute-start | bytes 786440 | tf_op jit(solution)/shard_map/ppermute | solution.py:48
  46.1 3.2 %collective-permute-start.15 = (bf16[128,1024]{1,0:T(8,128)(2,1)S(1)}, bf16[128,1024]{1,0:T(8,128)(2,1)S(1)}, u32[]{:S(2)}, u32[]{:S(2)}) collective-permute-start(bf16[128,1024]{1,0:T(8,128)(2,1)S(1)} %collective-permute-done.10.refs_4_), channel_id=1, source_target_pairs={{0,1},{1,0},{2,3},{3,2},{4,5},{5,4},{6,7},{7,6},{8,9},{9,8},{10,11... | collective-permute-start | bytes 786440 | tf_op jit(solution)/shard_map/ppermute | solution.py:39
  46.1 6.4 %collective-permute-start.14 = (bf16[128,1024]{1,0:T(8,128)(2,1)S(1)}, bf16[128,1024]{1,0:T(8,128)(2,1)S(1)}, u32[]{:S(2)}, u32[]{:S(2)}) collective-permute-start(bf16[128,1024]{1,0:T(8,128)(2,1)S(1)} %collective-permute-done.10.refs_4_), channel_id=1, source_target_pairs={{0,2},{1,5},{2,6},{3,1},{6,10},{7,3},{10,14},{11,7},{14,12},{15,11... | collective-permute-start | bytes 786440 | tf_op jit(solution)/shard_map/ppermute | solution.py:48
  48.9 4.3 %collective-permute-start.17 = (bf16[128,1024]{1,0:T(8,128)(2,1)S(1)}, bf16[128,1024]{1,0:T(8,128)(2,1)S(1)}, u32[]{:S(2)}, u32[]{:S(2)}) collective-permute-start(bf16[128,1024]{1,0:T(8,128)(2,1)S(1)} %collective-permute-done.12.refs_5_), channel_id=1, source_target_pairs={{0,1},{1,0},{2,3},{3,2},{4,5},{5,4},{6,7},{7,6},{8,9},{9,8},{10,11... | collective-permute-start | bytes 786440 | tf_op jit(solution)/shard_map/ppermute | solution.py:39
  48.9 6.4 %collective-permute-start.16 = (bf16[128,1024]{1,0:T(8,128)(2,1)S(1)}, bf16[128,1024]{1,0:T(8,128)(2,1)S(1)}, u32[]{:S(2)}, u32[]{:S(2)}) collective-permute-start(bf16[128,1024]{1,0:T(8,128)(2,1)S(1)} %collective-permute-done.12.refs_5_), channel_id=1, source_target_pairs={{0,2},{1,5},{2,6},{3,1},{6,10},{7,3},{10,14},{11,7},{14,12},{15,11... | collective-permute-start | bytes 786440 | tf_op jit(solution)/shard_map/ppermute | solution.py:48
  52.5 2.8 %collective-permute-start.19 = (bf16[128,1024]{1,0:T(8,128)(2,1)S(1)}, bf16[128,1024]{1,0:T(8,128)(2,1)S(1)}, u32[]{:S(2)}, u32[]{:S(2)}) collective-permute-start(bf16[128,1024]{1,0:T(8,128)(2,1)S(1)} %collective-permute-done.14.refs_6_), channel_id=1, source_target_pairs={{0,1},{1,0},{2,3},{3,2},{4,5},{5,4},{6,7},{7,6},{8,9},{9,8},{10,11... | collective-permute-start | bytes 786440 | tf_op jit(solution)/shard_map/ppermute | solution.py:39
  52.5 6.4 %collective-permute-start.18 = (bf16[128,1024]{1,0:T(8,128)(2,1)S(1)}, bf16[128,1024]{1,0:T(8,128)(2,1)S(1)}, u32[]{:S(2)}, u32[]{:S(2)}) collective-permute-start(bf16[128,1024]{1,0:T(8,128)(2,1)S(1)} %collective-permute-done.14.refs_6_), channel_id=1, source_target_pairs={{0,2},{1,5},{2,6},{3,1},{6,10},{7,3},{10,14},{11,7},{14,12},{15,11... | collective-permute-start | bytes 786440 | tf_op jit(solution)/shard_map/ppermute | solution.py:48
  55.3 3.6 %collective-permute-start.21 = (bf16[128,1024]{1,0:T(8,128)(2,1)S(1)}, bf16[128,1024]{1,0:T(8,128)(2,1)S(1)}, u32[]{:S(2)}, u32[]{:S(2)}) collective-permute-start(bf16[128,1024]{1,0:T(8,128)(2,1)S(1)} %collective-permute-done.16.refs_7_), channel_id=1, source_target_pairs={{0,1},{1,0},{2,3},{3,2},{4,5},{5,4},{6,7},{7,6},{8,9},{9,8},{10,11... | collective-permute-start | bytes 786440 | tf_op jit(solution)/shard_map/ppermute | solution.py:39
  58.9 1.5 %collective-permute-start.20 = (bf16[128,1024]{1,0:T(8,128)(2,1)S(1)}, bf16[128,1024]{1,0:T(8,128)(2,1)S(1)}, u32[]{:S(2)}, u32[]{:S(2)}) collective-permute-start(bf16[128,1024]{1,0:T(8,128)(2,1)S(1)} %collective-permute-done.18.refs_8_), channel_id=1, source_target_pairs={{0,1},{1,0},{2,3},{3,2},{4,5},{5,4},{6,7},{7,6},{8,9},{9,8},{10,11... | collective-permute-start | bytes 786440 | tf_op jit(solution)/shard_map/ppermute | solution.py:39
  85.6 1.6 %collective-permute-start.22 = (bf16[128,1024]{1,0:T(8,128)(2,1)S(1)}, bf16[128,1024]{1,0:T(8,128)(2,1)S(1)}, u32[]{:S(2)}, u32[]{:S(2)}) collective-permute-start(bf16[128,1024]{1,0:T(8,128)(2,1)S(1)} %get-tuple-element.110), channel_id=1, source_target_pairs={{0,1},{1,0},{2,3},{3,2},{4,5},{5,4},{6,7},{7,6},{8,9},{9,8},{10,11... | collective-permute-start | bytes 786440 | tf_op jit(solution)/shard_map/ppermute | solution.py:39
  85.8 3.4 %collective-permute-start.31 = (bf16[128,1024]{1,0:T(8,128)(2,1)S(1)}, bf16[128,1024]{1,0:T(8,128)(2,1)S(1)}, u32[]{:S(2)}, u32[]{:S(2)}) collective-permute-start(bf16[128,1024]{1,0:T(8,128)(2,1)S(1)} %get-tuple-element.125), channel_id=1, source_target_pairs={{0,1},{1,0},{2,3},{3,2},{4,5},{5,4},{6,7},{7,6},{8,9},{9,8},{10,11... | collective-permute-start | bytes 786440 | tf_op jit(solution)/shard_map/ppermute | solution.py:39
  87.2 6.4 %collective-permute-start.23 = (bf16[128,1024]{1,0:T(8,128)(2,1)S(1)}, bf16[128,1024]{1,0:T(8,128)(2,1)S(1)}, u32[]{:S(2)}, u32[]{:S(2)}) collective-permute-start(bf16[128,1024]{1,0:T(8,128)(2,1)S(1)} %add_convert_fusion.7), channel_id=1, source_target_pairs={{0,2},{1,5},{2,6},{3,1},{6,10},{7,3},{10,14},{11,7},{14,12},{15,11... | collective-permute-start | bytes 786440 | tf_op jit(solution)/shard_map/ppermute | solution.py:48
  88.0 5.7 %collective-permute-start.25 = (bf16[128,1024]{1,0:T(8,128)(2,1)S(1)}, bf16[128,1024]{1,0:T(8,128)(2,1)S(1)}, u32[]{:S(2)}, u32[]{:S(2)}) collective-permute-start(bf16[128,1024]{1,0:T(8,128)(2,1)S(1)} %get-tuple-element.114), channel_id=1, source_target_pairs={{0,1},{1,0},{2,3},{3,2},{4,5},{5,4},{6,7},{7,6},{8,9},{9,8},{10,11... | collective-permute-start | bytes 786440 | tf_op jit(solution)/shard_map/ppermute | solution.py:39
  89.2 7.2 %collective-permute-start.32 = (bf16[128,1024]{1,0:T(8,128)(2,1)S(1)}, bf16[128,1024]{1,0:T(8,128)(2,1)S(1)}, u32[]{:S(2)}, u32[]{:S(2)}) collective-permute-start(bf16[128,1024]{1,0:T(8,128)(2,1)S(1)} %add_convert_fusion.3), channel_id=1, source_target_pairs={{0,2},{1,5},{2,6},{3,1},{6,10},{7,3},{10,14},{11,7},{14,12},{15,11... | collective-permute-start | bytes 786440 | tf_op jit(solution)/shard_map/ppermute | solution.py:48
  90.3 6.2 %collective-permute-start.34 = (bf16[128,1024]{1,0:T(8,128)(2,1)S(1)}, bf16[128,1024]{1,0:T(8,128)(2,1)S(1)}, u32[]{:S(2)}, u32[]{:S(2)}) collective-permute-start(bf16[128,1024]{1,0:T(8,128)(2,1)S(1)} %get-tuple-element.129), channel_id=1, source_target_pairs={{0,1},{1,0},{2,3},{3,2},{4,5},{5,4},{6,7},{7,6},{8,9},{9,8},{10,11... | collective-permute-start | bytes 786440 | tf_op jit(solution)/shard_map/ppermute | solution.py:39
  93.8 6.4 %collective-permute-start.26 = (bf16[128,1024]{1,0:T(8,128)(2,1)S(1)}, bf16[128,1024]{1,0:T(8,128)(2,1)S(1)}, u32[]{:S(2)}, u32[]{:S(2)}) collective-permute-start(bf16[128,1024]{1,0:T(8,128)(2,1)S(1)} %add_convert_fusion.6), channel_id=1, source_target_pairs={{0,2},{1,5},{2,6},{3,1},{6,10},{7,3},{10,14},{11,7},{14,12},{15,11... | collective-permute-start | bytes 786440 | tf_op jit(solution)/shard_map/ppermute | solution.py:48
  94.5 5.7 %collective-permute-start.24 = (bf16[128,1024]{1,0:T(8,128)(2,1)S(1)}, bf16[128,1024]{1,0:T(8,128)(2,1)S(1)}, u32[]{:S(2)}, u32[]{:S(2)}) collective-permute-start(bf16[128,1024]{1,0:T(8,128)(2,1)S(1)} %get-tuple-element.112), channel_id=1, source_target_pairs={{0,1},{1,0},{2,3},{3,2},{4,5},{5,4},{6,7},{7,6},{8,9},{9,8},{10,11... | collective-permute-start | bytes 786440 | tf_op jit(solution)/shard_map/ppermute | solution.py:39
  96.5 6.6 %collective-permute-start.33 = (bf16[128,1024]{1,0:T(8,128)(2,1)S(1)}, bf16[128,1024]{1,0:T(8,128)(2,1)S(1)}, u32[]{:S(2)}, u32[]{:S(2)}) collective-permute-start(bf16[128,1024]{1,0:T(8,128)(2,1)S(1)} %get-tuple-element.127), channel_id=1, source_target_pairs={{0,1},{1,0},{2,3},{3,2},{4,5},{5,4},{6,7},{7,6},{8,9},{9,8},{10,11... | collective-permute-start | bytes 786440 | tf_op jit(solution)/shard_map/ppermute | solution.py:39
  96.6 6.4 %collective-permute-start.35 = (bf16[128,1024]{1,0:T(8,128)(2,1)S(1)}, bf16[128,1024]{1,0:T(8,128)(2,1)S(1)}, u32[]{:S(2)}, u32[]{:S(2)}) collective-permute-start(bf16[128,1024]{1,0:T(8,128)(2,1)S(1)} %add_convert_fusion.2), channel_id=1, source_target_pairs={{0,2},{1,5},{2,6},{3,1},{6,10},{7,3},{10,14},{11,7},{14,12},{15,11... | collective-permute-start | bytes 786440 | tf_op jit(solution)/shard_map/ppermute | solution.py:48
  100.4 6.4 %collective-permute-start.27 = (bf16[128,1024]{1,0:T(8,128)(2,1)S(1)}, bf16[128,1024]{1,0:T(8,128)(2,1)S(1)}, u32[]{:S(2)}, u32[]{:S(2)}) collective-permute-start(bf16[128,1024]{1,0:T(8,128)(2,1)S(1)} %add_convert_fusion.5), channel_id=1, source_target_pairs={{0,2},{1,5},{2,6},{3,1},{6,10},{7,3},{10,14},{11,7},{14,12},{15,11... | collective-permute-start | bytes 786440 | tf_op jit(solution)/shard_map/ppermute | solution.py:48
  101.1 5.7 %collective-permute-start.29 = (bf16[128,1024]{1,0:T(8,128)(2,1)S(1)}, bf16[128,1024]{1,0:T(8,128)(2,1)S(1)}, u32[]{:S(2)}, u32[]{:S(2)}) collective-permute-start(bf16[128,1024]{1,0:T(8,128)(2,1)S(1)} %get-tuple-element.121), channel_id=1, source_target_pairs={{0,1},{1,0},{2,3},{3,2},{4,5},{5,4},{6,7},{7,6},{8,9},{9,8},{10,11... | collective-permute-start | bytes 786440 | tf_op jit(solution)/shard_map/ppermute | solution.py:39
  103.2 5.9 %collective-permute-start.36 = (bf16[128,1024]{1,0:T(8,128)(2,1)S(1)}, bf16[128,1024]{1,0:T(8,128)(2,1)S(1)}, u32[]{:S(2)}, u32[]{:S(2)}) collective-permute-start(bf16[128,1024]{1,0:T(8,128)(2,1)S(1)} %add_convert_fusion.1), channel_id=1, source_target_pairs={{0,3},{1,4},{2,7},{3,0},{6,11},{7,2},{10,15},{11,6},{14,13},{15,10... | collective-permute-start | bytes 786440 | tf_op jit(solution)/shard_map/ppermute | solution.py:48
  106.8 2.3 %collective-permute-start.28 = (bf16[128,1024]{1,0:T(8,128)(2,1)S(1)}, bf16[128,1024]{1,0:T(8,128)(2,1)S(1)}, u32[]{:S(2)}, u32[]{:S(2)}) collective-permute-start(bf16[128,1024]{1,0:T(8,128)(2,1)S(1)} %get-tuple-element.119), channel_id=1, source_target_pairs={{0,1},{1,0},{2,3},{3,2},{4,5},{5,4},{6,7},{7,6},{8,9},{9,8},{10,11... | collective-permute-start | bytes 786440 | tf_op jit(solution)/shard_map/ppermute | solution.py:39
  106.9 6.4 %collective-permute-start.30 = (bf16[128,1024]{1,0:T(8,128)(2,1)S(1)}, bf16[128,1024]{1,0:T(8,128)(2,1)S(1)}, u32[]{:S(2)}, u32[]{:S(2)}) collective-permute-start(bf16[128,1024]{1,0:T(8,128)(2,1)S(1)} %add_convert_fusion.4), channel_id=1, source_target_pairs={{0,2},{1,5},{2,6},{3,1},{6,10},{7,3},{10,14},{11,7},{14,12},{15,11... | collective-permute-start | bytes 786440 | tf_op jit(solution)/shard_map/ppermute | solution.py:48

commit v15 on v14

--- a/solution.py
+++ b/solution.py
@@ -72,21 +72,18 @@
     if count > FEW:
         return list(lax.all_gather(block, "ctx")), [run(*arguments) for run, arguments in beside]
     middle = count // 2
-    cycle = cycle_of(count)
     found, other, made = [block], [()], []
-    opposite = lax.ppermute(block, "ctx", [(cycle[p], cycle[(p + middle) % count]) for p in range(count)])
-    for d in range(1, middle):
+    for d in range(1, middle + 1):
         arrived, extra = turn(found[-1], count), ()
         if len(beside) >= d:
             run, arguments = beside[d - 1]
             extra = run(*lax.optimization_barrier((found[-1], arguments))[1])
-        if d == 2:
-            arrived, opposite = lax.optimization_barrier((arrived, opposite))
         arrived, other[-1], extra = lax.optimization_barrier((arrived, other[-1], extra))
         made.append(extra)
         found.append(arrived)
-        other.append(swap(arrived))
-    return found + [opposite] + other[1:], made[: len(beside)]
+        if d < middle:
+            other.append(swap(arrived))
+    return found + other[1:], made[: len(beside)]
 
 
 def gather_columns(near, far, count):
@@ -209,8 +206,9 @@
     blocks = math.gcd(count, 8)
     whole = pl.BlockSpec(memory_space=pltpu.VMEM)
     if blocks == count:
-        latents, lat_spec = found, whole
+        latents, lat_spec = [half for block in found for half in block], whole
     else:
+        found = [jnp.concatenate(block, axis=0) for block in found]
         latents, lat_spec = [jnp.stack(found)], pl.BlockSpec((blocks, rows, WIDE), lambda i, *_: (i, 0, 0))
     wanted = (queries, out_proj, residual)
     return pl.pallas_call(
@@ -253,7 +251,7 @@
 
 
 def route_kernel(count, where, *refs):
-    blocks, out_ref = refs[:count], refs[count]
+    blocks, out_ref = refs[: 2 * count], refs[2 * count]
     _, rows, width = out_ref.shape
     here = width // SLOTS
     lane = lax.broadcasted_iota(jnp.int32, (rows, width), 1)
@@ -262,7 +260,7 @@
     first = lax.broadcasted_iota(jnp.int32, (rows, rows), 0)
     before = (first > lax.broadcasted_iota(jnp.int32, (rows, rows), 1)).astype(jnp.float32).astype(jnp.bfloat16)
     for c in range(count):
-        facts = blocks[c][:, LAT:].astype(jnp.float32)
+        facts = jnp.concatenate([blocks[2 * c + i][:, LAT:].astype(jnp.float32) for i in range(2)], axis=0)
         hot, share = jnp.zeros((rows, width), jnp.float32), jnp.zeros((rows, width), jnp.float32)
         for k in range(TOP):
             hit = facts[:, ROPE + k : ROPE + k + 1] == own
@@ -273,16 +271,16 @@
 
 
 def route(where, found, here):
-    count, (rows, _) = len(found), found[0].shape
+    count, (span, _) = len(found), found[0][0].shape
     whole = pl.BlockSpec(memory_space=pltpu.VMEM)
     return pl.pallas_call(
         functools.partial(route_kernel, count),
-        in_specs=[pl.BlockSpec(memory_space=pltpu.SMEM)] + [whole] * count,
+        in_specs=[pl.BlockSpec(memory_space=pltpu.SMEM)] + [whole] * (2 * count),
         out_specs=whole,
-        out_shape=pltpu.VMEM((count, rows, here * SLOTS), jnp.bfloat16),
+        out_shape=pltpu.VMEM((count, 2 * span, here * SLOTS), jnp.bfloat16),
         compiler_params=pltpu.CompilerParams(vmem_limit_bytes=8 * MIB),
         name="route",
-    )(where, *found)
+    )(where, *(half for block in found for half in block))
 
 
 def norm_kernel(where, base_ref, there_ref, gain_ref, middle_ref, near_ref, far_ref):
@@ -311,13 +309,14 @@
 
 
 def pack_kernel(*refs):
-    copies = [pltpu.make_async_copy(refs[i], refs[4 + i], refs[8].at[i]) for i in range(3)]
+    copies = [pltpu.make_async_copy(refs[i], refs[5 + i], refs[9].at[i]) for i in range(3)]
     for copy in copies:
         copy.start()
     for copy in copies:
         copy.wait()
-    out_ref, (latent_ref, ids_ref, weights_ref, rows) = refs[3], refs[4:8]
-    tokens = out_ref.shape[0]
+    top_ref, bottom_ref, latent_ref, ids_ref, weights_ref, rows = refs[3:9]
+    span = top_ref.shape[0]
+    tokens = 2 * span
     rows[...] = jnp.zeros_like(rows)
     rows[0:TOP] = ids_ref[...].astype(jnp.float32)
     rows[TOP : 2 * TOP] = weights_ref[...]
@@ -325,7 +324,8 @@
     same = (row == lax.broadcasted_iota(jnp.int32, (tokens, tokens), 1)).astype(jnp.float32).astype(jnp.bfloat16)
     every = jnp.concatenate([latent_ref[...], rows[...].astype(jnp.bfloat16)], axis=0)
     turned = lax.dot_general(same, every, (((1,), (1,)), ((), ())), preferred_element_type=jnp.float32)
-    out_ref[...] = turned.astype(jnp.bfloat16)
+    top_ref[...] = turned[:span].astype(jnp.bfloat16)
+    bottom_ref[...] = turned[span:].astype(jnp.bfloat16)
 
 
 def pack(latent, expert_ids, route_weights):
@@ -334,10 +334,10 @@
     return pl.pallas_call(
         pack_kernel,
         in_specs=[pl.BlockSpec(memory_space=pltpu.HBM)] * 3,
-        out_specs=pl.BlockSpec(memory_space=pltpu.VMEM),
+        out_specs=[pl.BlockSpec(memory_space=pltpu.VMEM)] * 2,
         scratch_shapes=[pltpu.VMEM(x.shape, x.dtype) for x in arrays]
         + [pltpu.VMEM((WIDE - base, local_rows), jnp.float32), pltpu.SemaphoreType.DMA((3,))],
-        out_shape=pltpu.VMEM((local_rows, WIDE), jnp.bfloat16),
+        out_shape=[pltpu.VMEM((local_rows // 2, WIDE), jnp.bfloat16)] * 2,
         compiler_params=pltpu.CompilerParams(vmem_limit_bytes=4 * MIB),
         name="pack",
     )(*(pltpu.with_memory_space_constraint(x, pltpu.HBM) for x in arrays))
@@ -499,12 +499,15 @@
         (lambda gain: gain.reshape(1, width), (norm_gain,)),
         (stage if few else lambda x: x, (kv_up,)),
     ]
-    found, (info, gain, kv_up) = gather(packed, count, beside)
+    streams = [gather(x, count, beside if h == 0 else ()) for h, x in enumerate(packed)]
+    info, gain, kv_up = streams[0][1]
+    found = list(zip(*(blocks for blocks, _ in streams)))
     partial, summand = attend(info, found, queries, kv_up, out_proj, residual, count)
     def place_rows(*blocks):
         if few:
             return route(where, blocks, here)
-        facts = jnp.stack(blocks)[:, :, base : base + 2 * TOP].astype(jnp.float32)
+        facts = jnp.stack([jnp.concatenate(block, axis=0) for block in blocks])
+        facts = facts[:, :, base : base + 2 * TOP].astype(jnp.float32)
         own = (me * here + jnp.arange(here, dtype=jnp.int32)).astype(jnp.float32)
         hit = facts[:, :, :TOP, None] == own
         hot = jnp.any(hit, axis=2)

time: 115 us -> 113 us (0.983)
  waiting for transfers between devices: 55.2 us -> 37.2 us
  starting transfers between devices: 19.4 us -> 35.4 us
    ppermute x17 -> x22, starting transfers between devices: 13.5 us -> 33.8 us  [turn(): return lax.ppermute(value, ('ctx', 'exp'), pairs)]
    ppermute x17 -> x22, waiting for transfers between devices: 47.4 us -> 34.6 us  [turn(): return lax.ppermute(value, ('ctx', 'exp'), pairs)]
    ppermute x1 -> x0, waiting for transfers between devices: 3.73 us -> none  [gather(): lax.ppermute(block, 'ctx', [(cycle[p], cycle[(p + middle) % count]) for p...]
    ppermute x1 -> x0, starting transfers between devices: 3.55 us -> none  [gather(): lax.ppermute(block, 'ctx', [(cycle[p], cycle[(p + middle) % count]) for p...]
    ppermute x19 -> x22, waiting for transfers between devices: 4.09 us -> 2.61 us  [swap(): return lax.ppermute(value, 'exp', SWAP)]
    ppermute x19 -> x22, starting transfers between devices: 2.35 us -> 1.65 us  [swap(): return lax.ppermute(value, 'exp', SWAP)]
  transfers between devices with their start and end apart: 37 -> 44, of which waited for: 21 -> 21; matrix products, arithmetic and copies ran while one was open for 3% -> 3% of each run, Pallas kernels for 3% -> 3%
where the time goes in v15:
time: 113 us; the launch traced here: 112 us
  waiting for transfers between devices  37.2 us (33%)
  Pallas kernels  35.7 us (32%)
  starting transfers between devices  35.4 us (31%)
  local copies, waits for them, and re-layouts  2.13 us (2%)
  other arithmetic  1.75 us (2%)
    ppermute x22, waiting for transfers between devices, turn(): return lax.ppermute(value, ('ctx', 'exp'), pairs)  34.6 us
    ppermute x22, starting transfers between devices, turn(): return lax.ppermute(value, ('ctx', 'exp'), pairs)  33.8 us
    pallas_call x1, Pallas kernels, experts_fused(): pl.pallas_call(functools.partial(fused_kernel, count), in_specs=[pl.Block...  25.1 us
    pallas_call x1, Pallas kernels, attend(): pl.pallas_call(functools.partial(attend_kernel, count, blocks, heads), gr...  5.43 us
    ppermute x22, waiting for transfers between devices, swap(): return lax.ppermute(value, 'exp', SWAP)  2.61 us
  transfers between devices with their start and end apart: 44, of which 21 were waited for; matrix products, arithmetic and copies ran while one was open for 3% of the time, Pallas kernels for 3%

profile of v15, /device:TPU:0, one launch (start us, length us, event | category | flops | bytes accessed | tf_op | source)
XLA Modules:
  0.0 112.4 jit_solution(7656126930835474633)
XLA Ops:
  0.0 1.1 %pack.1 = (bf16[64,640]{1,0:T(8,128)(2,1)S(1)}, bf16[64,640]{1,0:T(8,128)(2,1)S(1)}) custom-call(bf16[576,128]{1,0:T(8,128)(2,1)} %bitcast.11, s32[6,128]{1,0:T(8,128)} %bitcast.12, f32[6,128]{1,0:T(8,128)} %bitcast.13), custom_call_target="tpu_custom_call" | custom-call | tf_op jit(solution)/shard_map/pack/pallas_call | solution.py:334
  1.1 3.0 %collective-permute-start.1 = (bf16[64,640]{1,0:T(8,128)(2,1)S(1)}, bf16[64,640]{1,0:T(8,128)(2,1)S(1)}, u32[]{:S(2)}, u32[]{:S(2)}) collective-permute-start(bf16[64,640]{1,0:T(8,128)(2,1)S(1)} %get-tuple-element.108.refs_1_), channel_id=1, source_target_pairs={{0,2},{1,5},{2,6},{3,1},{6,10},{7,3},{10,14},{11,7},{14,12},{15,11... | collective-permute-start | bytes 245768 | tf_op jit(solution)/shard_map/ppermute | solution.py:48
  4.2 1.6 %collective-permute-start = (bf16[64,640]{1,0:T(8,128)(2,1)S(1)}, bf16[64,640]{1,0:T(8,128)(2,1)S(1)}, u32[]{:S(2)}, u32[]{:S(2)}) collective-permute-start(bf16[64,640]{1,0:T(8,128)(2,1)S(1)} %get-tuple-element.107.refs_0_), channel_id=1, source_target_pairs={{0,2},{1,5},{2,6},{3,1},{6,10},{7,3},{10,14},{11,7},{14,12},{15,11... | collective-permute-start | bytes 245768 | tf_op jit(solution)/shard_map/ppermute | solution.py:48
  6.7 2.0 %collective-permute-start.4 = (bf16[64,640]{1,0:T(8,128)(2,1)S(1)}, bf16[64,640]{1,0:T(8,128)(2,1)S(1)}, u32[]{:S(2)}, u32[]{:S(2)}) collective-permute-start(bf16[64,640]{1,0:T(8,128)(2,1)S(1)} %collective-permute-done.1.refs_3_), channel_id=1, source_target_pairs={{0,2},{1,5},{2,6},{3,1},{6,10},{7,3},{10,14},{11,7},{14,12},{15,11... | collective-permute-start | bytes 245768 | tf_op jit(solution)/shard_map/ppermute | solution.py:48
  8.6 0.7 concatenate.4.info
  9.7 1.4 %collective-permute-start.2 = (bf16[64,640]{1,0:T(8,128)(2,1)S(1)}, bf16[64,640]{1,0:T(8,128)(2,1)S(1)}, u32[]{:S(2)}, u32[]{:S(2)}) collective-permute-start(bf16[64,640]{1,0:T(8,128)(2,1)S(1)} %collective-permute-done.refs_2_), channel_id=1, source_target_pairs={{0,2},{1,5},{2,6},{3,1},{6,10},{7,3},{10,14},{11,7},{14,12},{15,11... | collective-permute-start | bytes 245768 | tf_op jit(solution)/shard_map/ppermute | solution.py:48
  11.0 0.7 reshape.3.gain_ref
  11.8 1.6 %collective-permute-start.8 = (bf16[64,640]{1,0:T(8,128)(2,1)S(1)}, bf16[64,640]{1,0:T(8,128)(2,1)S(1)}, u32[]{:S(2)}, u32[]{:S(2)}) collective-permute-start(bf16[64,640]{1,0:T(8,128)(2,1)S(1)} %collective-permute-done.4.refs_5_), channel_id=1, source_target_pairs={{0,2},{1,5},{2,6},{3,1},{6,10},{7,3},{10,14},{11,7},{14,12},{15,11... | collective-permute-start | bytes 245768 | tf_op jit(solution)/shard_map/ppermute | solution.py:48
  14.1 1.4 %collective-permute-start.6 = (bf16[64,640]{1,0:T(8,128)(2,1)S(1)}, bf16[64,640]{1,0:T(8,128)(2,1)S(1)}, u32[]{:S(2)}, u32[]{:S(2)}) collective-permute-start(bf16[64,640]{1,0:T(8,128)(2,1)S(1)} %collective-permute-done.2.refs_4_), channel_id=1, source_target_pairs={{0,2},{1,5},{2,6},{3,1},{6,10},{7,3},{10,14},{11,7},{14,12},{15,11... | collective-permute-start | bytes 245768 | tf_op jit(solution)/shard_map/ppermute | solution.py:48
  15.5 1.2 %stage.1.refs_16_ = bf16[512,1024]{1,0:T(8,128)(2,1)S(1)} custom-call(bf16[512,1024]{1,0:T(8,128)(2,1)} %source), custom_call_target="tpu_custom_call" | custom-call | tf_op jit(solution)/shard_map/stage/pallas_call | solution.py:242
  17.3 1.2 %collective-permute-start.12 = (bf16[64,640]{1,0:T(8,128)(2,1)S(1)}, bf16[64,640]{1,0:T(8,128)(2,1)S(1)}, u32[]{:S(2)}, u32[]{:S(2)}) collective-permute-start(bf16[64,640]{1,0:T(8,128)(2,1)S(1)} %collective-permute-done.8.refs_7_), channel_id=1, source_target_pairs={{0,2},{1,5},{2,6},{3,1},{6,10},{7,3},{10,14},{11,7},{14,12},{15,11... | collective-permute-start | bytes 245768 | tf_op jit(solution)/shard_map/ppermute | solution.py:48
  18.6 1.5 %collective-permute-start.10 = (bf16[64,640]{1,0:T(8,128)(2,1)S(1)}, bf16[64,640]{1,0:T(8,128)(2,1)S(1)}, u32[]{:S(2)}, u32[]{:S(2)}) collective-permute-start(bf16[64,640]{1,0:T(8,128)(2,1)S(1)} %collective-permute-done.6.refs_6_), channel_id=1, source_target_pairs={{0,2},{1,5},{2,6},{3,1},{6,10},{7,3},{10,14},{11,7},{14,12},{15,11... | collective-permute-start | bytes 245768 | tf_op jit(solution)/shard_map/ppermute | solution.py:48
  20.1 1.6 %collective-permute-done.12.refs_9_ = bf16[64,640]{1,0:T(8,128)(2,1)S(1)} collective-permute-done((bf16[64,640]{1,0:T(8,128)(2,1)S(1)}, bf16[64,640]{1,0:T(8,128)(2,1)S(1)}, u32[]{:S(2)}, u32[]{:S(2)}) %collective-permute-start.12) | collective-permute-done | bytes 81952 | tf_op jit(solution)/shard_map/ppermute | solution.py:48
  21.7 1.4 %collective-permute-done.10.refs_8_ = bf16[64,640]{1,0:T(8,128)(2,1)S(1)} collective-permute-done((bf16[64,640]{1,0:T(8,128)(2,1)S(1)}, bf16[64,640]{1,0:T(8,128)(2,1)S(1)}, u32[]{:S(2)}, u32[]{:S(2)}) %collective-permute-start.10) | collective-permute-done | bytes 81952 | tf_op jit(solution)/shard_map/ppermute | solution.py:48
  23.1 5.4 %attend.1 = (bf16[128,2048]{1,0:T(8,128)(2,1)S(1)}, f32[128,2048]{1,0:T(8,128)S(1)}) custom-call(s32[42]{0:T(128)S(1)} %concatenate.4.info, bf16[64,640]{1,0:T(8,128)(2,1)S(1)} %get-tuple-element.107.refs_0_, bf16[64,640]{1,0:T(8,128)(2,1)S(1)} %get-tuple-element.108.refs_1_, bf16[64,640]{1,0:T(8,128)(2,1)S(1)} %collective-permute-done.refs_2_, ...), custom_call_target="tpu_custom_call" | custom-call | tf_op jit(solution)/shard_map/attend/pallas_call | solution.py:214
  28.7 1.8 %route.1.refs_16_ = bf16[8,128,128]{2,1,0:T(8,128)(2,1)S(1)} custom-call(s32[2]{0:T(128)S(1)} %pad_add_fusion.where, bf16[64,640]{1,0:T(8,128)(2,1)S(1)} %get-tuple-element.107.refs_0_, bf16[64,640]{1,0:T(8,128)(2,1)S(1)} %get-tuple-element.108.refs_1_, bf16[64,640]{1,0:T(8,128)(2,1)S(1)} %collective-permute-done.refs_2_, ...), custom_call_target="tpu_custom_call" | custom-call | tf_op jit(solution)/shard_map/route/pallas_call | solution.py:276
  30.5 0.9 norm.1
  31.5 1.5 %collective-permute-start.15 = (bf16[128,1024]{1,0:T(8,128)(2,1)S(1)}, bf16[128,1024]{1,0:T(8,128)(2,1)S(1)}, u32[]{:S(2)}, u32[]{:S(2)}) collective-permute-start(bf16[128,1024]{1,0:T(8,128)(2,1)S(1)} %get-tuple-element.126.refs_0_), channel_id=1, source_target_pairs={{0,2},{1,5},{2,6},{3,1},{6,10},{7,3},{10,14},{11,7},{14,12},{15,11... | collective-permute-start | bytes 786440 | tf_op jit(solution)/shard_map/ppermute | solution.py:48
  33.0 1.4 %collective-permute-start.16 = (bf16[128,1024]{1,0:T(8,128)(2,1)S(1)}, bf16[128,1024]{1,0:T(8,128)(2,1)S(1)}, u32[]{:S(2)}, u32[]{:S(2)}) collective-permute-start(bf16[128,1024]{1,0:T(8,128)(2,1)S(1)} %get-tuple-element.127.refs_1_), channel_id=1, source_target_pairs={{0,2},{1,5},{2,6},{3,1},{6,10},{7,3},{10,14},{11,7},{14,12},{15,11... | collective-permute-start | bytes 786440 | tf_op jit(solution)/shard_map/ppermute | solution.py:48
  34.4 3.5 %collective-permute-done.15.refs_2_ = bf16[128,1024]{1,0:T(8,128)(2,1)S(1)} collective-permute-done((bf16[128,1024]{1,0:T(8,128)(2,1)S(1)}, bf16[128,1024]{1,0:T(8,128)(2,1)S(1)}, u32[]{:S(2)}, u32[]{:S(2)}) %collective-permute-start.15) | collective-permute-done | bytes 262176 | tf_op jit(solution)/shard_map/ppermute | solution.py:48
  37.9 1.5 %collective-permute-start.17 = (bf16[128,1024]{1,0:T(8,128)(2,1)S(1)}, bf16[128,1024]{1,0:T(8,128)(2,1)S(1)}, u32[]{:S(2)}, u32[]{:S(2)}) collective-permute-start(bf16[128,1024]{1,0:T(8,128)(2,1)S(1)} %collective-permute-done.15.refs_2_), channel_id=1, source_target_pairs={{0,2},{1,5},{2,6},{3,1},{6,10},{7,3},{10,14},{11,7},{14,12},{15,11... | collective-permute-start | bytes 786440 | tf_op jit(solution)/shard_map/ppermute | solution.py:48
  39.4 1.3 %collective-permute-done.16.refs_3_ = bf16[128,1024]{1,0:T(8,128)(2,1)S(1)} collective-permute-done((bf16[128,1024]{1,0:T(8,128)(2,1)S(1)}, bf16[128,1024]{1,0:T(8,128)(2,1)S(1)}, u32[]{:S(2)}, u32[]{:S(2)}) %collective-permute-start.16) | collective-permute-done | bytes 262176 | tf_op jit(solution)/shard_map/ppermute | solution.py:48
  40.7 1.5 %collective-permute-start.19 = (bf16[128,1024]{1,0:T(8,128)(2,1)S(1)}, bf16[128,1024]{1,0:T(8,128)(2,1)S(1)}, u32[]{:S(2)}, u32[]{:S(2)}) collective-permute-start(bf16[128,1024]{1,0:T(8,128)(2,1)S(1)} %collective-permute-done.16.refs_3_), channel_id=1, source_target_pairs={{0,2},{1,5},{2,6},{3,1},{6,10},{7,3},{10,14},{11,7},{14,12},{15,11... | collective-permute-start | bytes 786440 | tf_op jit(solution)/shard_map/ppermute | solution.py:48
  42.2 2.1 %collective-permute-done.17.refs_4_ = bf16[128,1024]{1,0:T(8,128)(2,1)S(1)} collective-permute-done((bf16[128,1024]{1,0:T(8,128)(2,1)S(1)}, bf16[128,1024]{1,0:T(8,128)(2,1)S(1)}, u32[]{:S(2)}, u32[]{:S(2)}) %collective-permute-start.17) | collective-permute-done | bytes 262176 | tf_op jit(solution)/shard_map/ppermute | solution.py:48
  44.3 1.5 %collective-permute-start.21 = (bf16[128,1024]{1,0:T(8,128)(2,1)S(1)}, bf16[128,1024]{1,0:T(8,128)(2,1)S(1)}, u32[]{:S(2)}, u32[]{:S(2)}) collective-permute-start(bf16[128,1024]{1,0:T(8,128)(2,1)S(1)} %collective-permute-done.17.refs_4_), channel_id=1, source_target_pairs={{0,2},{1,5},{2,6},{3,1},{6,10},{7,3},{10,14},{11,7},{14,12},{15,11... | collective-permute-start | bytes 786440 | tf_op jit(solution)/shard_map/ppermute | solution.py:48
  45.7 1.3 %collective-permute-done.19.refs_5_ = bf16[128,1024]{1,0:T(8,128)(2,1)S(1)} collective-permute-done((bf16[128,1024]{1,0:T(8,128)(2,1)S(1)}, bf16[128,1024]{1,0:T(8,128)(2,1)S(1)}, u32[]{:S(2)}, u32[]{:S(2)}) %collective-permute-start.19) | collective-permute-done | bytes 262176 | tf_op jit(solution)/shard_map/ppermute | solution.py:48
  47.1 1.5 %collective-permute-start.23 = (bf16[128,1024]{1,0:T(8,128)(2,1)S(1)}, bf16[128,1024]{1,0:T(8,128)(2,1)S(1)}, u32[]{:S(2)}, u32[]{:S(2)}) collective-permute-start(bf16[128,1024]{1,0:T(8,128)(2,1)S(1)} %collective-permute-done.19.refs_5_), channel_id=1, source_target_pairs={{0,2},{1,5},{2,6},{3,1},{6,10},{7,3},{10,14},{11,7},{14,12},{15,11... | collective-permute-start | bytes 786440 | tf_op jit(solution)/shard_map/ppermute | solution.py:48
  48.5 2.1 %collective-permute-done.21.refs_6_ = bf16[128,1024]{1,0:T(8,128)(2,1)S(1)} collective-permute-done((bf16[128,1024]{1,0:T(8,128)(2,1)S(1)}, bf16[128,1024]{1,0:T(8,128)(2,1)S(1)}, u32[]{:S(2)}, u32[]{:S(2)}) %collective-permute-start.21) | collective-permute-done | bytes 262176 | tf_op jit(solution)/shard_map/ppermute | solution.py:48
  50.6 1.5 %collective-permute-start.25 = (bf16[128,1024]{1,0:T(8,128)(2,1)S(1)}, bf16[128,1024]{1,0:T(8,128)(2,1)S(1)}, u32[]{:S(2)}, u32[]{:S(2)}) collective-permute-start(bf16[128,1024]{1,0:T(8,128)(2,1)S(1)} %collective-permute-done.21.refs_6_), channel_id=1, source_target_pairs={{0,2},{1,5},{2,6},{3,1},{6,10},{7,3},{10,14},{11,7},{14,12},{15,11... | collective-permute-start | bytes 786440 | tf_op jit(solution)/shard_map/ppermute | solution.py:48
  52.1 1.3 %collective-permute-done.23.refs_7_ = bf16[128,1024]{1,0:T(8,128)(2,1)S(1)} collective-permute-done((bf16[128,1024]{1,0:T(8,128)(2,1)S(1)}, bf16[128,1024]{1,0:T(8,128)(2,1)S(1)}, u32[]{:S(2)}, u32[]{:S(2)}) %collective-permute-start.23) | collective-permute-done | bytes 262176 | tf_op jit(solution)/shard_map/ppermute | solution.py:48
  53.4 3.6 %collective-permute-done.25.refs_8_ = bf16[128,1024]{1,0:T(8,128)(2,1)S(1)} collective-permute-done((bf16[128,1024]{1,0:T(8,128)(2,1)S(1)}, bf16[128,1024]{1,0:T(8,128)(2,1)S(1)}, u32[]{:S(2)}, u32[]{:S(2)}) %collective-permute-start.25) | collective-permute-done | bytes 262176 | tf_op jit(solution)/shard_map/ppermute | solution.py:48
  57.0 1.5 %collective-permute-done.27.refs_9_ = bf16[128,1024]{1,0:T(8,128)(2,1)S(1)} collective-permute-done((bf16[128,1024]{1,0:T(8,128)(2,1)S(1)}, bf16[128,1024]{1,0:T(8,128)(2,1)S(1)}, u32[]{:S(2)}, u32[]{:S(2)}) %collective-permute-start.27) | collective-permute-done | bytes 262176 | tf_op jit(solution)/shard_map/ppermute | solution.py:39
  58.5 25.1 %experts.1 = (bf16[128,1024]{1,0:T(8,128)(2,1)S(1)}, bf16[128,1024]{1,0:T(8,128)(2,1)S(1)}, bf16[128,1024]{1,0:T(8,128)(2,1)S(1)}, bf16[128,1024]{1,0:T(8,128)(2...) custom-call(s32[2]{0:T(128)S(1)} %pad_add_fusion.where, ...), custom_call_target="tpu_custom_call" | custom-call | tf_op jit(solution)/shard_map/experts/pallas_call | solution.py:454
  84.3 1.0 collective-permute-done.29
  85.3 1.5 %collective-permute-start.30 = (bf16[128,1024]{1,0:T(8,128)(2,1)S(1)}, bf16[128,1024]{1,0:T(8,128)(2,1)S(1)}, u32[]{:S(2)}, u32[]{:S(2)}) collective-permute-start(bf16[128,1024]{1,0:T(8,128)(2,1)S(1)} %add_convert_fusion.7), channel_id=1, source_target_pairs={{0,2},{1,5},{2,6},{3,1},{6,10},{7,3},{10,14},{11,7},{14,12},{15,11... | collective-permute-start | bytes 786440 | tf_op jit(solution)/shard_map/ppermute | solution.py:48
  87.0 1.5 %collective-permute-start.39 = (bf16[128,1024]{1,0:T(8,128)(2,1)S(1)}, bf16[128,1024]{1,0:T(8,128)(2,1)S(1)}, u32[]{:S(2)}, u32[]{:S(2)}) collective-permute-start(bf16[128,1024]{1,0:T(8,128)(2,1)S(1)} %add_convert_fusion.3), channel_id=1, source_target_pairs={{0,2},{1,5},{2,6},{3,1},{6,10},{7,3},{10,14},{11,7},{14,12},{15,11... | collective-permute-start | bytes 786440 | tf_op jit(solution)/shard_map/ppermute | solution.py:48
  88.4 3.4 %collective-permute-done.30 = bf16[128,1024]{1,0:T(8,128)(2,1)S(1)} collective-permute-done((bf16[128,1024]{1,0:T(8,128)(2,1)S(1)}, bf16[128,1024]{1,0:T(8,128)(2,1)S(1)}, u32[]{:S(2)}, u32[]{:S(2)}) %collective-permute-start.30) | collective-permute-done | bytes 262176 | tf_op jit(solution)/shard_map/ppermute | solution.py:48
  91.9 1.5 %collective-permute-start.33 = (bf16[128,1024]{1,0:T(8,128)(2,1)S(1)}, bf16[128,1024]{1,0:T(8,128)(2,1)S(1)}, u32[]{:S(2)}, u32[]{:S(2)}) collective-permute-start(bf16[128,1024]{1,0:T(8,128)(2,1)S(1)} %add_convert_fusion.6), channel_id=1, source_target_pairs={{0,2},{1,5},{2,6},{3,1},{6,10},{7,3},{10,14},{11,7},{14,12},{15,11... | collective-permute-start | bytes 786440 | tf_op jit(solution)/shard_map/ppermute | solution.py:48
  93.4 1.1 %collective-permute-done.39 = bf16[128,1024]{1,0:T(8,128)(2,1)S(1)} collective-permute-done((bf16[128,1024]{1,0:T(8,128)(2,1)S(1)}, bf16[128,1024]{1,0:T(8,128)(2,1)S(1)}, u32[]{:S(2)}, u32[]{:S(2)}) %collective-permute-start.39) | collective-permute-done | bytes 262176 | tf_op jit(solution)/shard_map/ppermute | solution.py:48
  94.7 1.5 %collective-permute-start.42 = (bf16[128,1024]{1,0:T(8,128)(2,1)S(1)}, bf16[128,1024]{1,0:T(8,128)(2,1)S(1)}, u32[]{:S(2)}, u32[]{:S(2)}) collective-permute-start(bf16[128,1024]{1,0:T(8,128)(2,1)S(1)} %add_convert_fusion.2), channel_id=1, source_target_pairs={{0,2},{1,5},{2,6},{3,1},{6,10},{7,3},{10,14},{11,7},{14,12},{15,11... | collective-permute-start | bytes 786440 | tf_op jit(solution)/shard_map/ppermute | solution.py:48
  96.2 2.1 %collective-permute-done.33 = bf16[128,1024]{1,0:T(8,128)(2,1)S(1)} collective-permute-done((bf16[128,1024]{1,0:T(8,128)(2,1)S(1)}, bf16[128,1024]{1,0:T(8,128)(2,1)S(1)}, u32[]{:S(2)}, u32[]{:S(2)}) %collective-permute-start.33) | collective-permute-done | bytes 262176 | tf_op jit(solution)/shard_map/ppermute | solution.py:48
  98.5 1.5 %collective-permute-start.34 = (bf16[128,1024]{1,0:T(8,128)(2,1)S(1)}, bf16[128,1024]{1,0:T(8,128)(2,1)S(1)}, u32[]{:S(2)}, u32[]{:S(2)}) collective-permute-start(bf16[128,1024]{1,0:T(8,128)(2,1)S(1)} %add_convert_fusion.5), channel_id=1, source_target_pairs={{0,2},{1,5},{2,6},{3,1},{6,10},{7,3},{10,14},{11,7},{14,12},{15,11... | collective-permute-start | bytes 786440 | tf_op jit(solution)/shard_map/ppermute | solution.py:48
  100.0 1.1 %collective-permute-done.42 = bf16[128,1024]{1,0:T(8,128)(2,1)S(1)} collective-permute-done((bf16[128,1024]{1,0:T(8,128)(2,1)S(1)}, bf16[128,1024]{1,0:T(8,128)(2,1)S(1)}, u32[]{:S(2)}, u32[]{:S(2)}) %collective-permute-start.42) | collective-permute-done | bytes 262176 | tf_op jit(solution)/shard_map/ppermute | solution.py:48
  101.3 0.8 collective-permute-start.43
  102.1 2.8 %collective-permute-done.34 = bf16[128,1024]{1,0:T(8,128)(2,1)S(1)} collective-permute-done((bf16[128,1024]{1,0:T(8,128)(2,1)S(1)}, bf16[128,1024]{1,0:T(8,128)(2,1)S(1)}, u32[]{:S(2)}, u32[]{:S(2)}) %collective-permute-start.34) | collective-permute-done | bytes 262176 | tf_op jit(solution)/shard_map/ppermute | solution.py:48
  105.0 1.5 %collective-permute-start.37 = (bf16[128,1024]{1,0:T(8,128)(2,1)S(1)}, bf16[128,1024]{1,0:T(8,128)(2,1)S(1)}, u32[]{:S(2)}, u32[]{:S(2)}) collective-permute-start(bf16[128,1024]{1,0:T(8,128)(2,1)S(1)} %add_convert_fusion.4), channel_id=1, source_target_pairs={{0,2},{1,5},{2,6},{3,1},{6,10},{7,3},{10,14},{11,7},{14,12},{15,11... | collective-permute-start | bytes 786440 | tf_op jit(solution)/shard_map/ppermute | solution.py:48
  107.1 4.3 %collective-permute-done.37 = bf16[128,1024]{1,0:T(8,128)(2,1)S(1)} collective-permute-done((bf16[128,1024]{1,0:T(8,128)(2,1)S(1)}, bf16[128,1024]{1,0:T(8,128)(2,1)S(1)}, u32[]{:S(2)}, u32[]{:S(2)}) %collective-permute-start.37) | collective-permute-done | bytes 262176 | tf_op jit(solution)/shard_map/ppermute | solution.py:48
  111.5 0.9 add_convert_fusion
  (58 shorter events, 4.8 us)
Async XLA Ops:
  1.1 5.5 %collective-permute-start.1 = (bf16[64,640]{1,0:T(8,128)(2,1)S(1)}, bf16[64,640]{1,0:T(8,128)(2,1)S(1)}, u32[]{:S(2)}, u32[]{:S(2)}) collective-permute-start(bf16[64,640]{1,0:T(8,128)(2,1)S(1)} %get-tuple-element.108.refs_1_), channel_id=1, source_target_pairs={{0,2},{1,5},{2,6},{3,1},{6,10},{7,3},{10,14},{11,7},{14,12},{15,11... | collective-permute-start | bytes 245768 | tf_op jit(solution)/shard_map/ppermute | solution.py:48
  4.2 5.2 %collective-permute-start = (bf16[64,640]{1,0:T(8,128)(2,1)S(1)}, bf16[64,640]{1,0:T(8,128)(2,1)S(1)}, u32[]{:S(2)}, u32[]{:S(2)}) collective-permute-start(bf16[64,640]{1,0:T(8,128)(2,1)S(1)} %get-tuple-element.107.refs_0_), channel_id=1, source_target_pairs={{0,2},{1,5},{2,6},{3,1},{6,10},{7,3},{10,14},{11,7},{14,12},{15,11... | collective-permute-start | bytes 245768 | tf_op jit(solution)/shard_map/ppermute | solution.py:48
  6.7 5.1 %collective-permute-start.5 = (bf16[64,640]{1,0:T(8,128)(2,1)S(1)}, bf16[64,640]{1,0:T(8,128)(2,1)S(1)}, u32[]{:S(2)}, u32[]{:S(2)}) collective-permute-start(bf16[64,640]{1,0:T(8,128)(2,1)S(1)} %collective-permute-done.1.refs_3_), channel_id=1, source_target_pairs={{0,1},{1,0},{2,3},{3,2},{4,5},{5,4},{6,7},{7,6},{8,9},{9,8},{10,11... | collective-permute-start | bytes 245768 | tf_op jit(solution)/shard_map/ppermute | solution.py:39
  6.7 5.1 %collective-permute-start.4 = (bf16[64,640]{1,0:T(8,128)(2,1)S(1)}, bf16[64,640]{1,0:T(8,128)(2,1)S(1)}, u32[]{:S(2)}, u32[]{:S(2)}) collective-permute-start(bf16[64,640]{1,0:T(8,128)(2,1)S(1)} %collective-permute-done.1.refs_3_), channel_id=1, source_target_pairs={{0,2},{1,5},{2,6},{3,1},{6,10},{7,3},{10,14},{11,7},{14,12},{15,11... | collective-permute-start | bytes 245768 | tf_op jit(solution)/shard_map/ppermute | solution.py:48
  9.4 4.1 %collective-permute-start.3 = (bf16[64,640]{1,0:T(8,128)(2,1)S(1)}, bf16[64,640]{1,0:T(8,128)(2,1)S(1)}, u32[]{:S(2)}, u32[]{:S(2)}) collective-permute-start(bf16[64,640]{1,0:T(8,128)(2,1)S(1)} %collective-permute-done.refs_2_), channel_id=1, source_target_pairs={{0,1},{1,0},{2,3},{3,2},{4,5},{5,4},{6,7},{7,6},{8,9},{9,8},{10,11... | collective-permute-start | bytes 245768 | tf_op jit(solution)/shard_map/ppermute | solution.py:39
  9.7 4.4 %collective-permute-start.2 = (bf16[64,640]{1,0:T(8,128)(2,1)S(1)}, bf16[64,640]{1,0:T(8,128)(2,1)S(1)}, u32[]{:S(2)}, u32[]{:S(2)}) collective-permute-start(bf16[64,640]{1,0:T(8,128)(2,1)S(1)} %collective-permute-done.refs_2_), channel_id=1, source_target_pairs={{0,2},{1,5},{2,6},{3,1},{6,10},{7,3},{10,14},{11,7},{14,12},{15,11... | collective-permute-start | bytes 245768 | tf_op jit(solution)/shard_map/ppermute | solution.py:48
  11.7 5.0 %collective-permute-start.9 = (bf16[64,640]{1,0:T(8,128)(2,1)S(1)}, bf16[64,640]{1,0:T(8,128)(2,1)S(1)}, u32[]{:S(2)}, u32[]{:S(2)}) collective-permute-start(bf16[64,640]{1,0:T(8,128)(2,1)S(1)} %collective-permute-done.4.refs_5_), channel_id=1, source_target_pairs={{0,1},{1,0},{2,3},{3,2},{4,5},{5,4},{6,7},{7,6},{8,9},{9,8},{10,11... | collective-permute-start | bytes 245768 | tf_op jit(solution)/shard_map/ppermute | solution.py:39
  11.8 4.9 %collective-permute-start.8 = (bf16[64,640]{1,0:T(8,128)(2,1)S(1)}, bf16[64,640]{1,0:T(8,128)(2,1)S(1)}, u32[]{:S(2)}, u32[]{:S(2)}) collective-permute-start(bf16[64,640]{1,0:T(8,128)(2,1)S(1)} %collective-permute-done.4.refs_5_), channel_id=1, source_target_pairs={{0,2},{1,5},{2,6},{3,1},{6,10},{7,3},{10,14},{11,7},{14,12},{15,11... | collective-permute-start | bytes 245768 | tf_op jit(solution)/shard_map/ppermute | solution.py:48
  14.1 4.3 %collective-permute-start.7 = (bf16[64,640]{1,0:T(8,128)(2,1)S(1)}, bf16[64,640]{1,0:T(8,128)(2,1)S(1)}, u32[]{:S(2)}, u32[]{:S(2)}) collective-permute-start(bf16[64,640]{1,0:T(8,128)(2,1)S(1)} %collective-permute-done.2.refs_4_), channel_id=1, source_target_pairs={{0,1},{1,0},{2,3},{3,2},{4,5},{5,4},{6,7},{7,6},{8,9},{9,8},{10,11... | collective-permute-start | bytes 245768 | tf_op jit(solution)/shard_map/ppermute | solution.py:39
  14.1 4.4 %collective-permute-start.6 = (bf16[64,640]{1,0:T(8,128)(2,1)S(1)}, bf16[64,640]{1,0:T(8,128)(2,1)S(1)}, u32[]{:S(2)}, u32[]{:S(2)}) collective-permute-start(bf16[64,640]{1,0:T(8,128)(2,1)S(1)} %collective-permute-done.2.refs_4_), channel_id=1, source_target_pairs={{0,2},{1,5},{2,6},{3,1},{6,10},{7,3},{10,14},{11,7},{14,12},{15,11... | collective-permute-start | bytes 245768 | tf_op jit(solution)/shard_map/ppermute | solution.py:48
  16.7 3.4 %collective-permute-start.13 = (bf16[64,640]{1,0:T(8,128)(2,1)S(1)}, bf16[64,640]{1,0:T(8,128)(2,1)S(1)}, u32[]{:S(2)}, u32[]{:S(2)}) collective-permute-start(bf16[64,640]{1,0:T(8,128)(2,1)S(1)} %collective-permute-done.8.refs_7_), channel_id=1, source_target_pairs={{0,1},{1,0},{2,3},{3,2},{4,5},{5,4},{6,7},{7,6},{8,9},{9,8},{10,11... | collective-permute-start | bytes 245768 | tf_op jit(solution)/shard_map/ppermute | solution.py:39
  17.3 4.4 %collective-permute-start.12 = (bf16[64,640]{1,0:T(8,128)(2,1)S(1)}, bf16[64,640]{1,0:T(8,128)(2,1)S(1)}, u32[]{:S(2)}, u32[]{:S(2)}) collective-permute-start(bf16[64,640]{1,0:T(8,128)(2,1)S(1)} %collective-permute-done.8.refs_7_), channel_id=1, source_target_pairs={{0,2},{1,5},{2,6},{3,1},{6,10},{7,3},{10,14},{11,7},{14,12},{15,11... | collective-permute-start | bytes 245768 | tf_op jit(solution)/shard_map/ppermute | solution.py:48
  18.6 3.1 %collective-permute-start.11 = (bf16[64,640]{1,0:T(8,128)(2,1)S(1)}, bf16[64,640]{1,0:T(8,128)(2,1)S(1)}, u32[]{:S(2)}, u32[]{:S(2)}) collective-permute-start(bf16[64,640]{1,0:T(8,128)(2,1)S(1)} %collective-permute-done.6.refs_6_), channel_id=1, source_target_pairs={{0,1},{1,0},{2,3},{3,2},{4,5},{5,4},{6,7},{7,6},{8,9},{9,8},{10,11... | collective-permute-start | bytes 245768 | tf_op jit(solution)/shard_map/ppermute | solution.py:39
  18.6 4.4 %collective-permute-start.10 = (bf16[64,640]{1,0:T(8,128)(2,1)S(1)}, bf16[64,640]{1,0:T(8,128)(2,1)S(1)}, u32[]{:S(2)}, u32[]{:S(2)}) collective-permute-start(bf16[64,640]{1,0:T(8,128)(2,1)S(1)} %collective-permute-done.6.refs_6_), channel_id=1, source_target_pairs={{0,2},{1,5},{2,6},{3,1},{6,10},{7,3},{10,14},{11,7},{14,12},{15,11... | collective-permute-start | bytes 245768 | tf_op jit(solution)/shard_map/ppermute | solution.py:48
  28.5 2.0 %collective-permute-start.14 = (bf16[128,2048]{1,0:T(8,128)(2,1)S(1)}, bf16[128,2048]{1,0:T(8,128)(2,1)S(1)}, u32[]{:S(2)}, u32[]{:S(2)}) collective-permute-start(bf16[128,2048]{1,0:T(8,128)(2,1)S(1)} %get-tuple-element.106), channel_id=1, source_target_pairs={{0,1},{1,0},{2,3},{3,2},{4,5},{5,4},{6,7},{7,6},{8,9},{9,8},{10,11... | collective-permute-start | bytes 1572872 | tf_op jit(solution)/shard_map/ppermute | solution.py:39
  31.5 6.4 %collective-permute-start.15 = (bf16[128,1024]{1,0:T(8,128)(2,1)S(1)}, bf16[128,1024]{1,0:T(8,128)(2,1)S(1)}, u32[]{:S(2)}, u32[]{:S(2)}) collective-permute-start(bf16[128,1024]{1,0:T(8,128)(2,1)S(1)} %get-tuple-element.126.refs_0_), channel_id=1, source_target_pairs={{0,2},{1,5},{2,6},{3,1},{6,10},{7,3},{10,14},{11,7},{14,12},{15,11... | collective-permute-start | bytes 786440 | tf_op jit(solution)/shard_map/ppermute | solution.py:48
  33.0 7.7 %collective-permute-start.16 = (bf16[128,1024]{1,0:T(8,128)(2,1)S(1)}, bf16[128,1024]{1,0:T(8,128)(2,1)S(1)}, u32[]{:S(2)}, u32[]{:S(2)}) collective-permute-start(bf16[128,1024]{1,0:T(8,128)(2,1)S(1)} %get-tuple-element.127.refs_1_), channel_id=1, source_target_pairs={{0,2},{1,5},{2,6},{3,1},{6,10},{7,3},{10,14},{11,7},{14,12},{15,11... | collective-permute-start | bytes 786440 | tf_op jit(solution)/shard_map/ppermute | solution.py:48
  37.9 4.3 %collective-permute-start.18 = (bf16[128,1024]{1,0:T(8,128)(2,1)S(1)}, bf16[128,1024]{1,0:T(8,128)(2,1)S(1)}, u32[]{:S(2)}, u32[]{:S(2)}) collective-permute-start(bf16[128,1024]{1,0:T(8,128)(2,1)S(1)} %collective-permute-done.15.refs_2_), channel_id=1, source_target_pairs={{0,1},{1,0},{2,3},{3,2},{4,5},{5,4},{6,7},{7,6},{8,9},{9,8},{10,11... | collective-permute-start | bytes 786440 | tf_op jit(solution)/shard_map/ppermute | solution.py:39
  37.9 6.4 %collective-permute-start.17 = (bf16[128,1024]{1,0:T(8,128)(2,1)S(1)}, bf16[128,1024]{1,0:T(8,128)(2,1)S(1)}, u32[]{:S(2)}, u32[]{:S(2)}) collective-permute-start(bf16[128,1024]{1,0:T(8,128)(2,1)S(1)} %collective-permute-done.15.refs_2_), channel_id=1, source_target_pairs={{0,2},{1,5},{2,6},{3,1},{6,10},{7,3},{10,14},{11,7},{14,12},{15,11... | collective-permute-start | bytes 786440 | tf_op jit(solution)/shard_map/ppermute | solution.py:48
  40.7 5.1 %collective-permute-start.20 = (bf16[128,1024]{1,0:T(8,128)(2,1)S(1)}, bf16[128,1024]{1,0:T(8,128)(2,1)S(1)}, u32[]{:S(2)}, u32[]{:S(2)}) collective-permute-start(bf16[128,1024]{1,0:T(8,128)(2,1)S(1)} %collective-permute-done.16.refs_3_), channel_id=1, source_target_pairs={{0,1},{1,0},{2,3},{3,2},{4,5},{5,4},{6,7},{7,6},{8,9},{9,8},{10,11... | collective-permute-start | bytes 786440 | tf_op jit(solution)/shard_map/ppermute | solution.py:39
  40.7 6.4 %collective-permute-start.19 = (bf16[128,1024]{1,0:T(8,128)(2,1)S(1)}, bf16[128,1024]{1,0:T(8,128)(2,1)S(1)}, u32[]{:S(2)}, u32[]{:S(2)}) collective-permute-start(bf16[128,1024]{1,0:T(8,128)(2,1)S(1)} %collective-permute-done.16.refs_3_), channel_id=1, source_target_pairs={{0,2},{1,5},{2,6},{3,1},{6,10},{7,3},{10,14},{11,7},{14,12},{15,11... | collective-permute-start | bytes 786440 | tf_op jit(solution)/shard_map/ppermute | solution.py:48
  44.3 4.3 %collective-permute-start.22 = (bf16[128,1024]{1,0:T(8,128)(2,1)S(1)}, bf16[128,1024]{1,0:T(8,128)(2,1)S(1)}, u32[]{:S(2)}, u32[]{:S(2)}) collective-permute-start(bf16[128,1024]{1,0:T(8,128)(2,1)S(1)} %collective-permute-done.17.refs_4_), channel_id=1, source_target_pairs={{0,1},{1,0},{2,3},{3,2},{4,5},{5,4},{6,7},{7,6},{8,9},{9,8},{10,11... | collective-permute-start | bytes 786440 | tf_op jit(solution)/shard_map/ppermute | solution.py:39
  44.3 6.4 %collective-permute-start.21 = (bf16[128,1024]{1,0:T(8,128)(2,1)S(1)}, bf16[128,1024]{1,0:T(8,128)(2,1)S(1)}, u32[]{:S(2)}, u32[]{:S(2)}) collective-permute-start(bf16[128,1024]{1,0:T(8,128)(2,1)S(1)} %collective-permute-done.17.refs_4_), channel_id=1, source_target_pairs={{0,2},{1,5},{2,6},{3,1},{6,10},{7,3},{10,14},{11,7},{14,12},{15,11... | collective-permute-start | bytes 786440 | tf_op jit(solution)/shard_map/ppermute | solution.py:48
  47.1 5.1 %collective-permute-start.24 = (bf16[128,1024]{1,0:T(8,128)(2,1)S(1)}, bf16[128,1024]{1,0:T(8,128)(2,1)S(1)}, u32[]{:S(2)}, u32[]{:S(2)}) collective-permute-start(bf16[128,1024]{1,0:T(8,128)(2,1)S(1)} %collective-permute-done.19.refs_5_), channel_id=1, source_target_pairs={{0,1},{1,0},{2,3},{3,2},{4,5},{5,4},{6,7},{7,6},{8,9},{9,8},{10,11... | collective-permute-start | bytes 786440 | tf_op jit(solution)/shard_map/ppermute | solution.py:39
  47.1 6.4 %collective-permute-start.23 = (bf16[128,1024]{1,0:T(8,128)(2,1)S(1)}, bf16[128,1024]{1,0:T(8,128)(2,1)S(1)}, u32[]{:S(2)}, u32[]{:S(2)}) collective-permute-start(bf16[128,1024]{1,0:T(8,128)(2,1)S(1)} %collective-permute-done.19.refs_5_), channel_id=1, source_target_pairs={{0,2},{1,5},{2,6},{3,1},{6,10},{7,3},{10,14},{11,7},{14,12},{15,11... | collective-permute-start | bytes 786440 | tf_op jit(solution)/shard_map/ppermute | solution.py:48
  50.6 2.8 %collective-permute-start.26 = (bf16[128,1024]{1,0:T(8,128)(2,1)S(1)}, bf16[128,1024]{1,0:T(8,128)(2,1)S(1)}, u32[]{:S(2)}, u32[]{:S(2)}) collective-permute-start(bf16[128,1024]{1,0:T(8,128)(2,1)S(1)} %collective-permute-done.21.refs_6_), channel_id=1, source_target_pairs={{0,1},{1,0},{2,3},{3,2},{4,5},{5,4},{6,7},{7,6},{8,9},{9,8},{10,11... | collective-permute-start | bytes 786440 | tf_op jit(solution)/shard_map/ppermute | solution.py:39
  50.6 6.4 %collective-permute-start.25 = (bf16[128,1024]{1,0:T(8,128)(2,1)S(1)}, bf16[128,1024]{1,0:T(8,128)(2,1)S(1)}, u32[]{:S(2)}, u32[]{:S(2)}) collective-permute-start(bf16[128,1024]{1,0:T(8,128)(2,1)S(1)} %collective-permute-done.21.refs_6_), channel_id=1, source_target_pairs={{0,2},{1,5},{2,6},{3,1},{6,10},{7,3},{10,14},{11,7},{14,12},{15,11... | collective-permute-start | bytes 786440 | tf_op jit(solution)/shard_map/ppermute | solution.py:48
  53.4 3.6 %collective-permute-start.28 = (bf16[128,1024]{1,0:T(8,128)(2,1)S(1)}, bf16[128,1024]{1,0:T(8,128)(2,1)S(1)}, u32[]{:S(2)}, u32[]{:S(2)}) collective-permute-start(bf16[128,1024]{1,0:T(8,128)(2,1)S(1)} %collective-permute-done.23.refs_7_), channel_id=1, source_target_pairs={{0,1},{1,0},{2,3},{3,2},{4,5},{5,4},{6,7},{7,6},{8,9},{9,8},{10,11... | collective-permute-start | bytes 786440 | tf_op jit(solution)/shard_map/ppermute | solution.py:39
  57.0 1.5 %collective-permute-start.27 = (bf16[128,1024]{1,0:T(8,128)(2,1)S(1)}, bf16[128,1024]{1,0:T(8,128)(2,1)S(1)}, u32[]{:S(2)}, u32[]{:S(2)}) collective-permute-start(bf16[128,1024]{1,0:T(8,128)(2,1)S(1)} %collective-permute-done.25.refs_8_), channel_id=1, source_target_pairs={{0,1},{1,0},{2,3},{3,2},{4,5},{5,4},{6,7},{7,6},{8,9},{9,8},{10,11... | collective-permute-start | bytes 786440 | tf_op jit(solution)/shard_map/ppermute | solution.py:39
  83.7 1.6 %collective-permute-start.29 = (bf16[128,1024]{1,0:T(8,128)(2,1)S(1)}, bf16[128,1024]{1,0:T(8,128)(2,1)S(1)}, u32[]{:S(2)}, u32[]{:S(2)}) collective-permute-start(bf16[128,1024]{1,0:T(8,128)(2,1)S(1)} %get-tuple-element.142), channel_id=1, source_target_pairs={{0,1},{1,0},{2,3},{3,2},{4,5},{5,4},{6,7},{7,6},{8,9},{9,8},{10,11... | collective-permute-start | bytes 786440 | tf_op jit(solution)/shard_map/ppermute | solution.py:39
  83.9 3.0 %collective-permute-start.38 = (bf16[128,1024]{1,0:T(8,128)(2,1)S(1)}, bf16[128,1024]{1,0:T(8,128)(2,1)S(1)}, u32[]{:S(2)}, u32[]{:S(2)}) collective-permute-start(bf16[128,1024]{1,0:T(8,128)(2,1)S(1)} %get-tuple-element.157), channel_id=1, source_target_pairs={{0,1},{1,0},{2,3},{3,2},{4,5},{5,4},{6,7},{7,6},{8,9},{9,8},{10,11... | collective-permute-start | bytes 786440 | tf_op jit(solution)/shard_map/ppermute | solution.py:39
  85.3 6.4 %collective-permute-start.30 = (bf16[128,1024]{1,0:T(8,128)(2,1)S(1)}, bf16[128,1024]{1,0:T(8,128)(2,1)S(1)}, u32[]{:S(2)}, u32[]{:S(2)}) collective-permute-start(bf16[128,1024]{1,0:T(8,128)(2,1)S(1)} %add_convert_fusion.7), channel_id=1, source_target_pairs={{0,2},{1,5},{2,6},{3,1},{6,10},{7,3},{10,14},{11,7},{14,12},{15,11... | collective-permute-start | bytes 786440 | tf_op jit(solution)/shard_map/ppermute | solution.py:48
  86.9 4.9 %collective-permute-start.32 = (bf16[128,1024]{1,0:T(8,128)(2,1)S(1)}, bf16[128,1024]{1,0:T(8,128)(2,1)S(1)}, u32[]{:S(2)}, u32[]{:S(2)}) collective-permute-start(bf16[128,1024]{1,0:T(8,128)(2,1)S(1)} %get-tuple-element.146), channel_id=1, source_target_pairs={{0,1},{1,0},{2,3},{3,2},{4,5},{5,4},{6,7},{7,6},{8,9},{9,8},{10,11... | collective-permute-start | bytes 786440 | tf_op jit(solution)/shard_map/ppermute | solution.py:39
  87.0 7.6 %collective-permute-start.39 = (bf16[128,1024]{1,0:T(8,128)(2,1)S(1)}, bf16[128,1024]{1,0:T(8,128)(2,1)S(1)}, u32[]{:S(2)}, u32[]{:S(2)}) collective-permute-start(bf16[128,1024]{1,0:T(8,128)(2,1)S(1)} %add_convert_fusion.3), channel_id=1, source_target_pairs={{0,2},{1,5},{2,6},{3,1},{6,10},{7,3},{10,14},{11,7},{14,12},{15,11... | collective-permute-start | bytes 786440 | tf_op jit(solution)/shard_map/ppermute | solution.py:48
  88.4 6.2 %collective-permute-start.41 = (bf16[128,1024]{1,0:T(8,128)(2,1)S(1)}, bf16[128,1024]{1,0:T(8,128)(2,1)S(1)}, u32[]{:S(2)}, u32[]{:S(2)}) collective-permute-start(bf16[128,1024]{1,0:T(8,128)(2,1)S(1)} %get-tuple-element.161), channel_id=1, source_target_pairs={{0,1},{1,0},{2,3},{3,2},{4,5},{5,4},{6,7},{7,6},{8,9},{9,8},{10,11... | collective-permute-start | bytes 786440 | tf_op jit(solution)/shard_map/ppermute | solution.py:39
  91.9 6.4 %collective-permute-start.33 = (bf16[128,1024]{1,0:T(8,128)(2,1)S(1)}, bf16[128,1024]{1,0:T(8,128)(2,1)S(1)}, u32[]{:S(2)}, u32[]{:S(2)}) collective-permute-start(bf16[128,1024]{1,0:T(8,128)(2,1)S(1)} %add_convert_fusion.6), channel_id=1, source_target_pairs={{0,2},{1,5},{2,6},{3,1},{6,10},{7,3},{10,14},{11,7},{14,12},{15,11... | collective-permute-start | bytes 786440 | tf_op jit(solution)/shard_map/ppermute | solution.py:48
  93.4 4.9 %collective-permute-start.31 = (bf16[128,1024]{1,0:T(8,128)(2,1)S(1)}, bf16[128,1024]{1,0:T(8,128)(2,1)S(1)}, u32[]{:S(2)}, u32[]{:S(2)}) collective-permute-start(bf16[128,1024]{1,0:T(8,128)(2,1)S(1)} %get-tuple-element.144), channel_id=1, source_target_pairs={{0,1},{1,0},{2,3},{3,2},{4,5},{5,4},{6,7},{7,6},{8,9},{9,8},{10,11... | collective-permute-start | bytes 786440 | tf_op jit(solution)/shard_map/ppermute | solution.py:39
  94.6 6.6 %collective-permute-start.40 = (bf16[128,1024]{1,0:T(8,128)(2,1)S(1)}, bf16[128,1024]{1,0:T(8,128)(2,1)S(1)}, u32[]{:S(2)}, u32[]{:S(2)}) collective-permute-start(bf16[128,1024]{1,0:T(8,128)(2,1)S(1)} %get-tuple-element.159), channel_id=1, source_target_pairs={{0,1},{1,0},{2,3},{3,2},{4,5},{5,4},{6,7},{7,6},{8,9},{9,8},{10,11... | collective-permute-start | bytes 786440 | tf_op jit(solution)/shard_map/ppermute | solution.py:39
  94.7 6.4 %collective-permute-start.42 = (bf16[128,1024]{1,0:T(8,128)(2,1)S(1)}, bf16[128,1024]{1,0:T(8,128)(2,1)S(1)}, u32[]{:S(2)}, u32[]{:S(2)}) collective-permute-start(bf16[128,1024]{1,0:T(8,128)(2,1)S(1)} %add_convert_fusion.2), channel_id=1, source_target_pairs={{0,2},{1,5},{2,6},{3,1},{6,10},{7,3},{10,14},{11,7},{14,12},{15,11... | collective-permute-start | bytes 786440 | tf_op jit(solution)/shard_map/ppermute | solution.py:48
  98.5 6.4 %collective-permute-start.34 = (bf16[128,1024]{1,0:T(8,128)(2,1)S(1)}, bf16[128,1024]{1,0:T(8,128)(2,1)S(1)}, u32[]{:S(2)}, u32[]{:S(2)}) collective-permute-start(bf16[128,1024]{1,0:T(8,128)(2,1)S(1)} %add_convert_fusion.5), channel_id=1, source_target_pairs={{0,2},{1,5},{2,6},{3,1},{6,10},{7,3},{10,14},{11,7},{14,12},{15,11... | collective-permute-start | bytes 786440 | tf_op jit(solution)/shard_map/ppermute | solution.py:48
  100.0 4.9 %collective-permute-start.36 = (bf16[128,1024]{1,0:T(8,128)(2,1)S(1)}, bf16[128,1024]{1,0:T(8,128)(2,1)S(1)}, u32[]{:S(2)}, u32[]{:S(2)}) collective-permute-start(bf16[128,1024]{1,0:T(8,128)(2,1)S(1)} %get-tuple-element.153), channel_id=1, source_target_pairs={{0,1},{1,0},{2,3},{3,2},{4,5},{5,4},{6,7},{7,6},{8,9},{9,8},{10,11... | collective-permute-start | bytes 786440 | tf_op jit(solution)/shard_map/ppermute | solution.py:39
  101.3 5.9 %collective-permute-start.43 = (bf16[128,1024]{1,0:T(8,128)(2,1)S(1)}, bf16[128,1024]{1,0:T(8,128)(2,1)S(1)}, u32[]{:S(2)}, u32[]{:S(2)}) collective-permute-start(bf16[128,1024]{1,0:T(8,128)(2,1)S(1)} %add_convert_fusion.1), channel_id=1, source_target_pairs={{0,3},{1,4},{2,7},{3,0},{6,11},{7,2},{10,15},{11,6},{14,13},{15,10... | collective-permute-start | bytes 786440 | tf_op jit(solution)/shard_map/ppermute | solution.py:48
  104.9 2.3 %collective-permute-start.35 = (bf16[128,1024]{1,0:T(8,128)(2,1)S(1)}, bf16[128,1024]{1,0:T(8,128)(2,1)S(1)}, u32[]{:S(2)}, u32[]{:S(2)}) collective-permute-start(bf16[128,1024]{1,0:T(8,128)(2,1)S(1)} %get-tuple-element.151), channel_id=1, source_target_pairs={{0,1},{1,0},{2,3},{3,2},{4,5},{5,4},{6,7},{7,6},{8,9},{9,8},{10,11... | collective-permute-start | bytes 786440 | tf_op jit(solution)/shard_map/ppermute | solution.py:39
  105.0 6.4 %collective-permute-start.37 = (bf16[128,1024]{1,0:T(8,128)(2,1)S(1)}, bf16[128,1024]{1,0:T(8,128)(2,1)S(1)}, u32[]{:S(2)}, u32[]{:S(2)}) collective-permute-start(bf16[128,1024]{1,0:T(8,128)(2,1)S(1)} %add_convert_fusion.4), channel_id=1, source_target_pairs={{0,2},{1,5},{2,6},{3,1},{6,10},{7,3},{10,14},{11,7},{14,12},{15,11... | collective-permute-start | bytes 786440 | tf_op jit(solution)/shard_map/ppermute | solution.py:48

commit v16 on v15

--- a/solution.py
+++ b/solution.py
@@ -55,9 +55,9 @@
     return total
 
 
-def sources_of(me, side, count):
+def sources_table(count):
     if count > FEW:
-        return jnp.arange(count, dtype=jnp.int32)
+        return jnp.tile(jnp.arange(count, dtype=jnp.int32), 2 * count)
     cycle = cycle_of(count)
     middle = count // 2
     table = np.zeros((2 * count, count), np.int32)
@@ -65,7 +65,7 @@
         for core, sign in ((0, 1), (1, -1)):
             ways = [sign * d for d in range(middle + 1)] + [-sign * d for d in range(1, middle)]
             table[cycle[p] * 2 + core] = [cycle[(p - way) % count] for way in ways]
-    return lax.dynamic_index_in_dim(jnp.asarray(table), me * 2 + side, keepdims=False)
+    return jnp.asarray(table.reshape(-1))
 
 
 def gather(block, count, beside=()):
@@ -120,16 +120,16 @@
     return summed([parts[0][0], given[0], *running])
 
 
-def attend_kernel(count, blocks, heads, info, *refs):
-    latents, up_ref, refs = refs[: len(refs) - 13], refs[len(refs) - 13], refs[len(refs) - 12 :]
-    wanted, (out_ref, base_ref) = refs[:3], refs[3:5]
-    held, sems, (m_ref, l_ref, acc_ref) = refs[5:8], refs[8], refs[9:12]
-    q_ref, proj_ref, residual_ref = held
-    copies = [pltpu.make_async_copy(wanted[i], held[i], sems.at[i]) for i in range(3)]
+def attend_kernel(count, blocks, heads, where, *refs):
+    latents, refs = refs[: len(refs) - 20], refs[len(refs) - 20 :]
+    wanted, (out_ref, base_ref), held = refs[:7], refs[7:9], refs[9:16]
+    sems, (m_ref, l_ref, acc_ref) = refs[16], refs[17:20]
+    q_ref, up_ref, proj_ref, residual_ref, table, spans, lengths = held
+    copies = [pltpu.make_async_copy(wanted[i], held[i], sems.at[i]) for i in range(7)]
     chunk = pl.program_id(0)
-    sources = lambda c: info[2 + c]
-    order = lambda j: info[2 + count + j]
-    segs = info.shape[0] - 2 - 3 * count
+    sources = lambda c: table[(where[0] * 2 + where[1]) * count + c]
+    order = lambda j: spans[j]
+    segs = lengths.shape[0]
     rows = q_ref.shape[0]
     span = rows // 2
     depth = q_ref.shape[1] // heads
@@ -145,15 +145,23 @@
         l_ref[...] = jnp.zeros_like(l_ref)
         acc_ref[...] = jnp.zeros_like(acc_ref)
 
+    lat = jnp.concatenate([ref[...].reshape(-1, WIDE) for ref in latents], axis=0)
+
+    @pl.when(chunk == 0)
+    def _():
+        for i in (0, 1, 4, 5, 6):
+            copies[i].wait()
+
+    keyval = jnp.dot(lat[:, :LAT], up_ref[...], preferred_element_type=jnp.float32).astype(jnp.bfloat16)
     row = lax.broadcasted_iota(jnp.int32, (rows, 1), 0)
-    first = order(2 * info[0]) * span
-    second = order(2 * info[0] + 1) * span
+    first = order(2 * where[0]) * span
+    second = order(2 * where[0] + 1) * span
     qpos = jnp.where(row < span, first + row, second + row - span)
     low = jnp.zeros((rows, 1), jnp.int32)
     start = jnp.int32(0)
     for m in range(segs):
         low = jnp.where(qpos >= start, start, low)
-        start = start + info[2 + 3 * count + m]
+        start = start + lengths[m]
     keys = blocks * rows
     lane = lax.broadcasted_iota(jnp.int32, (1, keys), 1)
     which = lane // span
@@ -164,13 +172,6 @@
             kpos = jnp.where(which == 2 * j + i, order(2 * source + i) * span + lane % span, kpos)
     visible = (kpos >= low) & (kpos <= qpos)
 
-    lat = jnp.concatenate([ref[...].reshape(-1, WIDE) for ref in latents], axis=0)
-
-    @pl.when(chunk == 0)
-    def _():
-        copies[0].wait()
-
-    keyval = jnp.dot(lat[:, :LAT], up_ref[...], preferred_element_type=jnp.float32).astype(jnp.bfloat16)
     rope = lat[:, LAT : LAT + ROPE]
     scale = 1.0 / math.sqrt(NOPE + ROPE)
     for h in range(heads):
@@ -192,15 +193,15 @@
     @pl.when(chunk == pl.num_programs(0) - 1)
     def _():
         attended = [(acc_ref[h] / l_ref[h]).astype(jnp.bfloat16) for h in range(heads)]
-        copies[1].wait()
         copies[2].wait()
+        copies[3].wait()
         out = jnp.dot(jnp.concatenate(attended, axis=1), proj_ref[...], preferred_element_type=jnp.float32)
         out = out.astype(jnp.bfloat16)
         out_ref[...] = out
         base_ref[...] = residual_ref[...].astype(jnp.float32) + out.astype(jnp.float32)
 
 
-def attend(info, found, queries, kv_up, out_proj, residual, count):
+def attend(where, scalars, found, queries, kv_up, out_proj, residual, count):
     rows, width = residual.shape
     heads = kv_up.shape[1] // (NOPE + VHEAD)
     blocks = math.gcd(count, 8)
@@ -210,17 +211,18 @@
     else:
         found = [jnp.concatenate(block, axis=0) for block in found]
         latents, lat_spec = [jnp.stack(found)], pl.BlockSpec((blocks, rows, WIDE), lambda i, *_: (i, 0, 0))
-    wanted = (queries, out_proj, residual)
+    wanted = (queries, kv_up, out_proj, residual, *scalars)
     return pl.pallas_call(
         functools.partial(attend_kernel, count, blocks, heads),
         grid_spec=pltpu.PrefetchScalarGridSpec(
             num_scalar_prefetch=1,
             grid=(count // blocks,),
-            in_specs=[lat_spec] * len(latents) + [whole] + [pl.BlockSpec(memory_space=pltpu.HBM)] * 3,
+            in_specs=[lat_spec] * len(latents) + [pl.BlockSpec(memory_space=pltpu.HBM)] * 7,
             out_specs=[whole, whole],
-            scratch_shapes=[pltpu.VMEM(x.shape, x.dtype) for x in wanted]
+            scratch_shapes=[pltpu.VMEM(x.shape, x.dtype) for x in wanted[:4]]
+            + [pltpu.SMEM(x.shape, x.dtype) for x in scalars]
             + [
-                pltpu.SemaphoreType.DMA((3,)),
+                pltpu.SemaphoreType.DMA((7,)),
                 pltpu.VMEM((heads, rows, 1), jnp.float32),
                 pltpu.VMEM((heads, rows, 1), jnp.float32),
                 pltpu.VMEM((heads, rows, VHEAD), jnp.float32),
@@ -229,25 +231,7 @@
         out_shape=[pltpu.VMEM((rows, width), jnp.bfloat16), pltpu.VMEM((rows, width), jnp.float32)],
         compiler_params=pltpu.CompilerParams(vmem_limit_bytes=28 * MIB),
         name="attend",
-    )(info, *latents, kv_up, *(pltpu.with_memory_space_constraint(x, pltpu.HBM) for x in wanted))
-
-
-def stage_kernel(source, out, sem):
-    copy = pltpu.make_async_copy(source, out, sem)
-    copy.start()
-    copy.wait()
-
-
-def stage(x):
-    return pl.pallas_call(
-        stage_kernel,
-        in_specs=[pl.BlockSpec(memory_space=pltpu.HBM)],
-        out_specs=pl.BlockSpec(memory_space=pltpu.VMEM),
-        scratch_shapes=[pltpu.SemaphoreType.DMA],
-        out_shape=pltpu.VMEM(x.shape, x.dtype),
-        compiler_params=pltpu.CompilerParams(vmem_limit_bytes=2 * MIB),
-        name="stage",
-    )(pltpu.with_memory_space_constraint(x, pltpu.HBM))
+    )(where, *latents, *(pltpu.with_memory_space_constraint(x, pltpu.HBM) for x in wanted))
 
 
 def route_kernel(count, where, *refs):
@@ -493,16 +477,12 @@
     w_gate, w_up = w_gate.transpose(0, 2, 1), w_up.transpose(0, 2, 1)
     packed = pack(latent, expert_ids, route_weights)
     few = count <= FEW
-    scalars = lambda *arrays: jnp.concatenate([where, sources_of(me, side, count), *arrays])
-    beside = [
-        (scalars, (span_order, seg_lengths)),
-        (lambda gain: gain.reshape(1, width), (norm_gain,)),
-        (stage if few else lambda x: x, (kv_up,)),
-    ]
+    scalars = (sources_table(count), span_order, seg_lengths)
+    beside = [(lambda gain: gain.reshape(1, width), (norm_gain,))]
     streams = [gather(x, count, beside if h == 0 else ()) for h, x in enumerate(packed)]
-    info, gain, kv_up = streams[0][1]
+    gain = streams[0][1][0]
     found = list(zip(*(blocks for blocks, _ in streams)))
-    partial, summand = attend(info, found, queries, kv_up, out_proj, residual, count)
+    partial, summand = attend(where, scalars, found, queries, kv_up, out_proj, residual, count)
     def place_rows(*blocks):
         if few:
             return route(where, blocks, here)

time: 113 us -> 113 us (level)
  waiting for transfers between devices: 37.2 us -> 40.5 us
  local copies, waits for them, and re-layouts: 2.13 us -> 0.69 us
    ppermute x22, waiting for transfers between devices: 34.6 us -> 37.8 us  [turn(): return lax.ppermute(value, ('ctx', 'exp'), pairs)]
    pallas_call x1 -> x0, Pallas kernels: 1.23 us -> none  [stage(): pl.pallas_call(stage_kernel, in_specs=[pl.BlockSpec(memory_space=pltpu.HB...]
  transfers between devices with their start and end apart: 44 -> 44, of which waited for: 21 -> 23; matrix products, arithmetic and copies ran while one was open for 3% -> 1% of each run, Pallas kernels for 3% -> 2%
where the time goes in v16:
time: 113 us
  waiting for transfers between devices  40.5 us (36%)
  Pallas kernels  35 us (31%)
  starting transfers between devices  34.8 us (31%)
  other arithmetic  1.75 us (2%)
    ppermute x22, waiting for transfers between devices, turn(): return lax.ppermute(value, ('ctx', 'exp'), pairs)  37.8 us
    ppermute x22, starting transfers between devices, turn(): return lax.ppermute(value, ('ctx', 'exp'), pairs)  33.3 us
    pallas_call x1, Pallas kernels, experts_fused(): pl.pallas_call(functools.partial(fused_kernel, count), in_specs=[pl.Block...  25.1 us
    pallas_call x1, Pallas kernels, attend(): pl.pallas_call(functools.partial(attend_kernel, count, blocks, heads), gr...  6 us
    ppermute x22, waiting for transfers between devices, swap(): return lax.ppermute(value, 'exp', SWAP)  2.64 us
  transfers between devices with their start and end apart: 44, of which 23 were waited for; matrix products, arithmetic and copies ran while one was open for 1% of the time, Pallas kernels for 2%

profile of v16, /device:TPU:0, one launch (start us, length us, event | category | flops | bytes accessed | tf_op | source)
XLA Modules:
  0.0 112.8 jit_solution(9530167170853452379)
XLA Ops:
  0.0 1.1 %pack.1 = (bf16[64,640]{1,0:T(8,128)(2,1)S(1)}, bf16[64,640]{1,0:T(8,128)(2,1)S(1)}) custom-call(bf16[576,128]{1,0:T(8,128)(2,1)} %bitcast.9, s32[6,128]{1,0:T(8,128)} %bitcast.10, f32[6,128]{1,0:T(8,128)} %bitcast.11), custom_call_target="tpu_custom_call" | custom-call | tf_op jit(solution)/shard_map/pack/pallas_call | solution.py:318
  1.1 3.0 %collective-permute-start.1 = (bf16[64,640]{1,0:T(8,128)(2,1)S(1)}, bf16[64,640]{1,0:T(8,128)(2,1)S(1)}, u32[]{:S(2)}, u32[]{:S(2)}) collective-permute-start(bf16[64,640]{1,0:T(8,128)(2,1)S(1)} %get-tuple-element.98.refs_1_), channel_id=1, source_target_pairs={{0,2},{1,5},{2,6},{3,1},{6,10},{7,3},{10,14},{11,7},{14,12},{15,11... | collective-permute-start | bytes 245768 | tf_op jit(solution)/shard_map/ppermute | solution.py:48
  4.2 1.6 %collective-permute-start = (bf16[64,640]{1,0:T(8,128)(2,1)S(1)}, bf16[64,640]{1,0:T(8,128)(2,1)S(1)}, u32[]{:S(2)}, u32[]{:S(2)}) collective-permute-start(bf16[64,640]{1,0:T(8,128)(2,1)S(1)} %get-tuple-element.97.refs_0_), channel_id=1, source_target_pairs={{0,2},{1,5},{2,6},{3,1},{6,10},{7,3},{10,14},{11,7},{14,12},{15,11... | collective-permute-start | bytes 245768 | tf_op jit(solution)/shard_map/ppermute | solution.py:48
  5.7 0.9 collective-permute-done.1.refs_3_
  6.7 2.0 %collective-permute-start.4 = (bf16[64,640]{1,0:T(8,128)(2,1)S(1)}, bf16[64,640]{1,0:T(8,128)(2,1)S(1)}, u32[]{:S(2)}, u32[]{:S(2)}) collective-permute-start(bf16[64,640]{1,0:T(8,128)(2,1)S(1)} %collective-permute-done.1.refs_3_), channel_id=1, source_target_pairs={{0,2},{1,5},{2,6},{3,1},{6,10},{7,3},{10,14},{11,7},{14,12},{15,11... | collective-permute-start | bytes 245768 | tf_op jit(solution)/shard_map/ppermute | solution.py:48
  8.6 0.7 reshape.3.gain_ref
  9.7 1.4 %collective-permute-start.2 = (bf16[64,640]{1,0:T(8,128)(2,1)S(1)}, bf16[64,640]{1,0:T(8,128)(2,1)S(1)}, u32[]{:S(2)}, u32[]{:S(2)}) collective-permute-start(bf16[64,640]{1,0:T(8,128)(2,1)S(1)} %collective-permute-done.refs_2_), channel_id=1, source_target_pairs={{0,2},{1,5},{2,6},{3,1},{6,10},{7,3},{10,14},{11,7},{14,12},{15,11... | collective-permute-start | bytes 245768 | tf_op jit(solution)/shard_map/ppermute | solution.py:48
  11.1 2.0 %collective-permute-start.8 = (bf16[64,640]{1,0:T(8,128)(2,1)S(1)}, bf16[64,640]{1,0:T(8,128)(2,1)S(1)}, u32[]{:S(2)}, u32[]{:S(2)}) collective-permute-start(bf16[64,640]{1,0:T(8,128)(2,1)S(1)} %collective-permute-done.4.refs_5_), channel_id=1, source_target_pairs={{0,2},{1,5},{2,6},{3,1},{6,10},{7,3},{10,14},{11,7},{14,12},{15,11... | collective-permute-start | bytes 245768 | tf_op jit(solution)/shard_map/ppermute | solution.py:48
  13.1 1.0 collective-permute-done.2.refs_4_
  14.1 1.4 %collective-permute-start.6 = (bf16[64,640]{1,0:T(8,128)(2,1)S(1)}, bf16[64,640]{1,0:T(8,128)(2,1)S(1)}, u32[]{:S(2)}, u32[]{:S(2)}) collective-permute-start(bf16[64,640]{1,0:T(8,128)(2,1)S(1)} %collective-permute-done.2.refs_4_), channel_id=1, source_target_pairs={{0,2},{1,5},{2,6},{3,1},{6,10},{7,3},{10,14},{11,7},{14,12},{15,11... | collective-permute-start | bytes 245768 | tf_op jit(solution)/shard_map/ppermute | solution.py:48
  15.9 1.6 %collective-permute-start.12 = (bf16[64,640]{1,0:T(8,128)(2,1)S(1)}, bf16[64,640]{1,0:T(8,128)(2,1)S(1)}, u32[]{:S(2)}, u32[]{:S(2)}) collective-permute-start(bf16[64,640]{1,0:T(8,128)(2,1)S(1)} %collective-permute-done.8.refs_7_), channel_id=1, source_target_pairs={{0,2},{1,5},{2,6},{3,1},{6,10},{7,3},{10,14},{11,7},{14,12},{15,11... | collective-permute-start | bytes 245768 | tf_op jit(solution)/shard_map/ppermute | solution.py:48
  17.5 1.0 collective-permute-done.6.refs_6_
  18.6 1.4 %collective-permute-start.10 = (bf16[64,640]{1,0:T(8,128)(2,1)S(1)}, bf16[64,640]{1,0:T(8,128)(2,1)S(1)}, u32[]{:S(2)}, u32[]{:S(2)}) collective-permute-start(bf16[64,640]{1,0:T(8,128)(2,1)S(1)} %collective-permute-done.6.refs_6_), channel_id=1, source_target_pairs={{0,2},{1,5},{2,6},{3,1},{6,10},{7,3},{10,14},{11,7},{14,12},{15,11... | collective-permute-start | bytes 245768 | tf_op jit(solution)/shard_map/ppermute | solution.py:48
  20.4 2.6 %collective-permute-done.10.refs_8_ = bf16[64,640]{1,0:T(8,128)(2,1)S(1)} collective-permute-done((bf16[64,640]{1,0:T(8,128)(2,1)S(1)}, bf16[64,640]{1,0:T(8,128)(2,1)S(1)}, u32[]{:S(2)}, u32[]{:S(2)}) %collective-permute-start.10) | collective-permute-done | bytes 81952 | tf_op jit(solution)/shard_map/ppermute | solution.py:48
  23.0 6.0 %attend.1 = (bf16[128,2048]{1,0:T(8,128)(2,1)S(1)}, f32[128,2048]{1,0:T(8,128)S(1)}) custom-call(s32[2]{0:T(128)S(1)} %pad_add_fusion.where, bf16[64,640]{1,0:T(8,128)(2,1)S(1)} %get-tuple-element.97.refs_0_, bf16[64,640]{1,0:T(8,128)(2,1)S(1)} %get-tuple-element.98.refs_1_, bf16[64,640]{1,0:T(8,128)(2,1)S(1)} %collective-permute-done.refs_2_, ...), custom_call_target="tpu_custom_call" | custom-call | tf_op jit(solution)/shard_map/attend/pallas_call | solution.py:215
  29.1 1.9 %route.1.refs_16_ = bf16[8,128,128]{2,1,0:T(8,128)(2,1)S(1)} custom-call(s32[2]{0:T(128)S(1)} %pad_add_fusion.where, bf16[64,640]{1,0:T(8,128)(2,1)S(1)} %get-tuple-element.97.refs_0_, bf16[64,640]{1,0:T(8,128)(2,1)S(1)} %get-tuple-element.98.refs_1_, bf16[64,640]{1,0:T(8,128)(2,1)S(1)} %collective-permute-done.refs_2_, ...), custom_call_target="tpu_custom_call" | custom-call | tf_op jit(solution)/shard_map/route/pallas_call | solution.py:260
  31.0 0.9 norm.1
  31.9 1.4 %collective-permute-start.15 = (bf16[128,1024]{1,0:T(8,128)(2,1)S(1)}, bf16[128,1024]{1,0:T(8,128)(2,1)S(1)}, u32[]{:S(2)}, u32[]{:S(2)}) collective-permute-start(bf16[128,1024]{1,0:T(8,128)(2,1)S(1)} %get-tuple-element.116.refs_0_), channel_id=1, source_target_pairs={{0,2},{1,5},{2,6},{3,1},{6,10},{7,3},{10,14},{11,7},{14,12},{15,11... | collective-permute-start | bytes 786440 | tf_op jit(solution)/shard_map/ppermute | solution.py:48
  33.3 1.6 %collective-permute-start.16 = (bf16[128,1024]{1,0:T(8,128)(2,1)S(1)}, bf16[128,1024]{1,0:T(8,128)(2,1)S(1)}, u32[]{:S(2)}, u32[]{:S(2)}) collective-permute-start(bf16[128,1024]{1,0:T(8,128)(2,1)S(1)} %get-tuple-element.117.refs_1_), channel_id=1, source_target_pairs={{0,2},{1,5},{2,6},{3,1},{6,10},{7,3},{10,14},{11,7},{14,12},{15,11... | collective-permute-start | bytes 786440 | tf_op jit(solution)/shard_map/ppermute | solution.py:48
  34.9 3.4 %collective-permute-done.15.refs_2_ = bf16[128,1024]{1,0:T(8,128)(2,1)S(1)} collective-permute-done((bf16[128,1024]{1,0:T(8,128)(2,1)S(1)}, bf16[128,1024]{1,0:T(8,128)(2,1)S(1)}, u32[]{:S(2)}, u32[]{:S(2)}) %collective-permute-start.15) | collective-permute-done | bytes 262176 | tf_op jit(solution)/shard_map/ppermute | solution.py:48
  38.3 1.4 %collective-permute-start.17 = (bf16[128,1024]{1,0:T(8,128)(2,1)S(1)}, bf16[128,1024]{1,0:T(8,128)(2,1)S(1)}, u32[]{:S(2)}, u32[]{:S(2)}) collective-permute-start(bf16[128,1024]{1,0:T(8,128)(2,1)S(1)} %collective-permute-done.15.refs_2_), channel_id=1, source_target_pairs={{0,2},{1,5},{2,6},{3,1},{6,10},{7,3},{10,14},{11,7},{14,12},{15,11... | collective-permute-start | bytes 786440 | tf_op jit(solution)/shard_map/ppermute | solution.py:48
  39.7 1.4 %collective-permute-done.16.refs_3_ = bf16[128,1024]{1,0:T(8,128)(2,1)S(1)} collective-permute-done((bf16[128,1024]{1,0:T(8,128)(2,1)S(1)}, bf16[128,1024]{1,0:T(8,128)(2,1)S(1)}, u32[]{:S(2)}, u32[]{:S(2)}) %collective-permute-start.16) | collective-permute-done | bytes 262176 | tf_op jit(solution)/shard_map/ppermute | solution.py:48
  41.1 1.4 %collective-permute-start.19 = (bf16[128,1024]{1,0:T(8,128)(2,1)S(1)}, bf16[128,1024]{1,0:T(8,128)(2,1)S(1)}, u32[]{:S(2)}, u32[]{:S(2)}) collective-permute-start(bf16[128,1024]{1,0:T(8,128)(2,1)S(1)} %collective-permute-done.16.refs_3_), channel_id=1, source_target_pairs={{0,2},{1,5},{2,6},{3,1},{6,10},{7,3},{10,14},{11,7},{14,12},{15,11... | collective-permute-start | bytes 786440 | tf_op jit(solution)/shard_map/ppermute | solution.py:48
  42.5 2.2 %collective-permute-done.17.refs_4_ = bf16[128,1024]{1,0:T(8,128)(2,1)S(1)} collective-permute-done((bf16[128,1024]{1,0:T(8,128)(2,1)S(1)}, bf16[128,1024]{1,0:T(8,128)(2,1)S(1)}, u32[]{:S(2)}, u32[]{:S(2)}) %collective-permute-start.17) | collective-permute-done | bytes 262176 | tf_op jit(solution)/shard_map/ppermute | solution.py:48
  44.7 1.4 %collective-permute-start.21 = (bf16[128,1024]{1,0:T(8,128)(2,1)S(1)}, bf16[128,1024]{1,0:T(8,128)(2,1)S(1)}, u32[]{:S(2)}, u32[]{:S(2)}) collective-permute-start(bf16[128,1024]{1,0:T(8,128)(2,1)S(1)} %collective-permute-done.17.refs_4_), channel_id=1, source_target_pairs={{0,2},{1,5},{2,6},{3,1},{6,10},{7,3},{10,14},{11,7},{14,12},{15,11... | collective-permute-start | bytes 786440 | tf_op jit(solution)/shard_map/ppermute | solution.py:48
  46.1 1.4 %collective-permute-done.19.refs_5_ = bf16[128,1024]{1,0:T(8,128)(2,1)S(1)} collective-permute-done((bf16[128,1024]{1,0:T(8,128)(2,1)S(1)}, bf16[128,1024]{1,0:T(8,128)(2,1)S(1)}, u32[]{:S(2)}, u32[]{:S(2)}) %collective-permute-start.19) | collective-permute-done | bytes 262176 | tf_op jit(solution)/shard_map/ppermute | solution.py:48
  47.5 1.4 %collective-permute-start.23 = (bf16[128,1024]{1,0:T(8,128)(2,1)S(1)}, bf16[128,1024]{1,0:T(8,128)(2,1)S(1)}, u32[]{:S(2)}, u32[]{:S(2)}) collective-permute-start(bf16[128,1024]{1,0:T(8,128)(2,1)S(1)} %collective-permute-done.19.refs_5_), channel_id=1, source_target_pairs={{0,2},{1,5},{2,6},{3,1},{6,10},{7,3},{10,14},{11,7},{14,12},{15,11... | collective-permute-start | bytes 786440 | tf_op jit(solution)/shard_map/ppermute | solution.py:48
  48.9 2.2 %collective-permute-done.21.refs_6_ = bf16[128,1024]{1,0:T(8,128)(2,1)S(1)} collective-permute-done((bf16[128,1024]{1,0:T(8,128)(2,1)S(1)}, bf16[128,1024]{1,0:T(8,128)(2,1)S(1)}, u32[]{:S(2)}, u32[]{:S(2)}) %collective-permute-start.21) | collective-permute-done | bytes 262176 | tf_op jit(solution)/shard_map/ppermute | solution.py:48
  51.1 1.4 %collective-permute-start.25 = (bf16[128,1024]{1,0:T(8,128)(2,1)S(1)}, bf16[128,1024]{1,0:T(8,128)(2,1)S(1)}, u32[]{:S(2)}, u32[]{:S(2)}) collective-permute-start(bf16[128,1024]{1,0:T(8,128)(2,1)S(1)} %collective-permute-done.21.refs_6_), channel_id=1, source_target_pairs={{0,2},{1,5},{2,6},{3,1},{6,10},{7,3},{10,14},{11,7},{14,12},{15,11... | collective-permute-start | bytes 786440 | tf_op jit(solution)/shard_map/ppermute | solution.py:48
  52.4 1.4 %collective-permute-done.23.refs_7_ = bf16[128,1024]{1,0:T(8,128)(2,1)S(1)} collective-permute-done((bf16[128,1024]{1,0:T(8,128)(2,1)S(1)}, bf16[128,1024]{1,0:T(8,128)(2,1)S(1)}, u32[]{:S(2)}, u32[]{:S(2)}) %collective-permute-start.23) | collective-permute-done | bytes 262176 | tf_op jit(solution)/shard_map/ppermute | solution.py:48
  53.9 3.6 %collective-permute-done.25.refs_8_ = bf16[128,1024]{1,0:T(8,128)(2,1)S(1)} collective-permute-done((bf16[128,1024]{1,0:T(8,128)(2,1)S(1)}, bf16[128,1024]{1,0:T(8,128)(2,1)S(1)}, u32[]{:S(2)}, u32[]{:S(2)}) %collective-permute-start.25) | collective-permute-done | bytes 262176 | tf_op jit(solution)/shard_map/ppermute | solution.py:48
  57.5 1.5 %collective-permute-done.27.refs_9_ = bf16[128,1024]{1,0:T(8,128)(2,1)S(1)} collective-permute-done((bf16[128,1024]{1,0:T(8,128)(2,1)S(1)}, bf16[128,1024]{1,0:T(8,128)(2,1)S(1)}, u32[]{:S(2)}, u32[]{:S(2)}) %collective-permute-start.27) | collective-permute-done | bytes 262176 | tf_op jit(solution)/shard_map/ppermute | solution.py:39
  59.0 25.1 %experts.1 = (bf16[128,1024]{1,0:T(8,128)(2,1)S(1)}, bf16[128,1024]{1,0:T(8,128)(2,1)S(1)}, bf16[128,1024]{1,0:T(8,128)(2,1)S(1)}, bf16[128,1024]{1,0:T(8,128)(2...) custom-call(s32[2]{0:T(128)S(1)} %pad_add_fusion.where, ...), custom_call_target="tpu_custom_call" | custom-call | tf_op jit(solution)/shard_map/experts/pallas_call | solution.py:438
  84.7 1.0 collective-permute-done.29
  85.8 1.4 %collective-permute-start.30 = (bf16[128,1024]{1,0:T(8,128)(2,1)S(1)}, bf16[128,1024]{1,0:T(8,128)(2,1)S(1)}, u32[]{:S(2)}, u32[]{:S(2)}) collective-permute-start(bf16[128,1024]{1,0:T(8,128)(2,1)S(1)} %add_convert_fusion.7), channel_id=1, source_target_pairs={{0,2},{1,5},{2,6},{3,1},{6,10},{7,3},{10,14},{11,7},{14,12},{15,11... | collective-permute-start | bytes 786440 | tf_op jit(solution)/shard_map/ppermute | solution.py:48
  87.3 1.6 %collective-permute-start.39 = (bf16[128,1024]{1,0:T(8,128)(2,1)S(1)}, bf16[128,1024]{1,0:T(8,128)(2,1)S(1)}, u32[]{:S(2)}, u32[]{:S(2)}) collective-permute-start(bf16[128,1024]{1,0:T(8,128)(2,1)S(1)} %add_convert_fusion.3), channel_id=1, source_target_pairs={{0,2},{1,5},{2,6},{3,1},{6,10},{7,3},{10,14},{11,7},{14,12},{15,11... | collective-permute-start | bytes 786440 | tf_op jit(solution)/shard_map/ppermute | solution.py:48
  88.9 3.3 %collective-permute-done.30 = bf16[128,1024]{1,0:T(8,128)(2,1)S(1)} collective-permute-done((bf16[128,1024]{1,0:T(8,128)(2,1)S(1)}, bf16[128,1024]{1,0:T(8,128)(2,1)S(1)}, u32[]{:S(2)}, u32[]{:S(2)}) %collective-permute-start.30) | collective-permute-done | bytes 262176 | tf_op jit(solution)/shard_map/ppermute | solution.py:48
  92.3 1.4 %collective-permute-start.33 = (bf16[128,1024]{1,0:T(8,128)(2,1)S(1)}, bf16[128,1024]{1,0:T(8,128)(2,1)S(1)}, u32[]{:S(2)}, u32[]{:S(2)}) collective-permute-start(bf16[128,1024]{1,0:T(8,128)(2,1)S(1)} %add_convert_fusion.6), channel_id=1, source_target_pairs={{0,2},{1,5},{2,6},{3,1},{6,10},{7,3},{10,14},{11,7},{14,12},{15,11... | collective-permute-start | bytes 786440 | tf_op jit(solution)/shard_map/ppermute | solution.py:48
  93.8 1.3 %collective-permute-done.39 = bf16[128,1024]{1,0:T(8,128)(2,1)S(1)} collective-permute-done((bf16[128,1024]{1,0:T(8,128)(2,1)S(1)}, bf16[128,1024]{1,0:T(8,128)(2,1)S(1)}, u32[]{:S(2)}, u32[]{:S(2)}) %collective-permute-start.39) | collective-permute-done | bytes 262176 | tf_op jit(solution)/shard_map/ppermute | solution.py:48
  95.2 1.4 %collective-permute-start.42 = (bf16[128,1024]{1,0:T(8,128)(2,1)S(1)}, bf16[128,1024]{1,0:T(8,128)(2,1)S(1)}, u32[]{:S(2)}, u32[]{:S(2)}) collective-permute-start(bf16[128,1024]{1,0:T(8,128)(2,1)S(1)} %add_convert_fusion.2), channel_id=1, source_target_pairs={{0,2},{1,5},{2,6},{3,1},{6,10},{7,3},{10,14},{11,7},{14,12},{15,11... | collective-permute-start | bytes 786440 | tf_op jit(solution)/shard_map/ppermute | solution.py:48
  96.6 2.2 %collective-permute-done.33 = bf16[128,1024]{1,0:T(8,128)(2,1)S(1)} collective-permute-done((bf16[128,1024]{1,0:T(8,128)(2,1)S(1)}, bf16[128,1024]{1,0:T(8,128)(2,1)S(1)}, u32[]{:S(2)}, u32[]{:S(2)}) %collective-permute-start.33) | collective-permute-done | bytes 262176 | tf_op jit(solution)/shard_map/ppermute | solution.py:48
  98.9 1.4 %collective-permute-start.34 = (bf16[128,1024]{1,0:T(8,128)(2,1)S(1)}, bf16[128,1024]{1,0:T(8,128)(2,1)S(1)}, u32[]{:S(2)}, u32[]{:S(2)}) collective-permute-start(bf16[128,1024]{1,0:T(8,128)(2,1)S(1)} %add_convert_fusion.5), channel_id=1, source_target_pairs={{0,2},{1,5},{2,6},{3,1},{6,10},{7,3},{10,14},{11,7},{14,12},{15,11... | collective-permute-start | bytes 786440 | tf_op jit(solution)/shard_map/ppermute | solution.py:48
  100.3 1.3 %collective-permute-done.42 = bf16[128,1024]{1,0:T(8,128)(2,1)S(1)} collective-permute-done((bf16[128,1024]{1,0:T(8,128)(2,1)S(1)}, bf16[128,1024]{1,0:T(8,128)(2,1)S(1)}, u32[]{:S(2)}, u32[]{:S(2)}) %collective-permute-start.42) | collective-permute-done | bytes 262176 | tf_op jit(solution)/shard_map/ppermute | solution.py:48
  102.4 2.9 %collective-permute-done.34 = bf16[128,1024]{1,0:T(8,128)(2,1)S(1)} collective-permute-done((bf16[128,1024]{1,0:T(8,128)(2,1)S(1)}, bf16[128,1024]{1,0:T(8,128)(2,1)S(1)}, u32[]{:S(2)}, u32[]{:S(2)}) %collective-permute-start.34) | collective-permute-done | bytes 262176 | tf_op jit(solution)/shard_map/ppermute | solution.py:48
  105.5 1.4 %collective-permute-start.37 = (bf16[128,1024]{1,0:T(8,128)(2,1)S(1)}, bf16[128,1024]{1,0:T(8,128)(2,1)S(1)}, u32[]{:S(2)}, u32[]{:S(2)}) collective-permute-start(bf16[128,1024]{1,0:T(8,128)(2,1)S(1)} %add_convert_fusion.4), channel_id=1, source_target_pairs={{0,2},{1,5},{2,6},{3,1},{6,10},{7,3},{10,14},{11,7},{14,12},{15,11... | collective-permute-start | bytes 786440 | tf_op jit(solution)/shard_map/ppermute | solution.py:48
  106.9 0.7 collective-permute-done.43
  107.6 4.3 %collective-permute-done.37 = bf16[128,1024]{1,0:T(8,128)(2,1)S(1)} collective-permute-done((bf16[128,1024]{1,0:T(8,128)(2,1)S(1)}, bf16[128,1024]{1,0:T(8,128)(2,1)S(1)}, u32[]{:S(2)}, u32[]{:S(2)}) %collective-permute-start.37) | collective-permute-done | bytes 262176 | tf_op jit(solution)/shard_map/ppermute | solution.py:48
  111.9 0.9 add_convert_fusion
  (55 shorter events, 3.6 us)
Async XLA Ops:
  1.1 5.5 %collective-permute-start.1 = (bf16[64,640]{1,0:T(8,128)(2,1)S(1)}, bf16[64,640]{1,0:T(8,128)(2,1)S(1)}, u32[]{:S(2)}, u32[]{:S(2)}) collective-permute-start(bf16[64,640]{1,0:T(8,128)(2,1)S(1)} %get-tuple-element.98.refs_1_), channel_id=1, source_target_pairs={{0,2},{1,5},{2,6},{3,1},{6,10},{7,3},{10,14},{11,7},{14,12},{15,11... | collective-permute-start | bytes 245768 | tf_op jit(solution)/shard_map/ppermute | solution.py:48
  4.2 5.1 %collective-permute-start = (bf16[64,640]{1,0:T(8,128)(2,1)S(1)}, bf16[64,640]{1,0:T(8,128)(2,1)S(1)}, u32[]{:S(2)}, u32[]{:S(2)}) collective-permute-start(bf16[64,640]{1,0:T(8,128)(2,1)S(1)} %get-tuple-element.97.refs_0_), channel_id=1, source_target_pairs={{0,2},{1,5},{2,6},{3,1},{6,10},{7,3},{10,14},{11,7},{14,12},{15,11... | collective-permute-start | bytes 245768 | tf_op jit(solution)/shard_map/ppermute | solution.py:48
  6.7 4.4 %collective-permute-start.5 = (bf16[64,640]{1,0:T(8,128)(2,1)S(1)}, bf16[64,640]{1,0:T(8,128)(2,1)S(1)}, u32[]{:S(2)}, u32[]{:S(2)}) collective-permute-start(bf16[64,640]{1,0:T(8,128)(2,1)S(1)} %collective-permute-done.1.refs_3_), channel_id=1, source_target_pairs={{0,1},{1,0},{2,3},{3,2},{4,5},{5,4},{6,7},{7,6},{8,9},{9,8},{10,11... | collective-permute-start | bytes 245768 | tf_op jit(solution)/shard_map/ppermute | solution.py:39
  6.7 4.4 %collective-permute-start.4 = (bf16[64,640]{1,0:T(8,128)(2,1)S(1)}, bf16[64,640]{1,0:T(8,128)(2,1)S(1)}, u32[]{:S(2)}, u32[]{:S(2)}) collective-permute-start(bf16[64,640]{1,0:T(8,128)(2,1)S(1)} %collective-permute-done.1.refs_3_), channel_id=1, source_target_pairs={{0,2},{1,5},{2,6},{3,1},{6,10},{7,3},{10,14},{11,7},{14,12},{15,11... | collective-permute-start | bytes 245768 | tf_op jit(solution)/shard_map/ppermute | solution.py:48
  9.3 3.7 %collective-permute-start.3 = (bf16[64,640]{1,0:T(8,128)(2,1)S(1)}, bf16[64,640]{1,0:T(8,128)(2,1)S(1)}, u32[]{:S(2)}, u32[]{:S(2)}) collective-permute-start(bf16[64,640]{1,0:T(8,128)(2,1)S(1)} %collective-permute-done.refs_2_), channel_id=1, source_target_pairs={{0,1},{1,0},{2,3},{3,2},{4,5},{5,4},{6,7},{7,6},{8,9},{9,8},{10,11... | collective-permute-start | bytes 245768 | tf_op jit(solution)/shard_map/ppermute | solution.py:39
  9.7 4.4 %collective-permute-start.2 = (bf16[64,640]{1,0:T(8,128)(2,1)S(1)}, bf16[64,640]{1,0:T(8,128)(2,1)S(1)}, u32[]{:S(2)}, u32[]{:S(2)}) collective-permute-start(bf16[64,640]{1,0:T(8,128)(2,1)S(1)} %collective-permute-done.refs_2_), channel_id=1, source_target_pairs={{0,2},{1,5},{2,6},{3,1},{6,10},{7,3},{10,14},{11,7},{14,12},{15,11... | collective-permute-start | bytes 245768 | tf_op jit(solution)/shard_map/ppermute | solution.py:48
  11.1 4.4 %collective-permute-start.9 = (bf16[64,640]{1,0:T(8,128)(2,1)S(1)}, bf16[64,640]{1,0:T(8,128)(2,1)S(1)}, u32[]{:S(2)}, u32[]{:S(2)}) collective-permute-start(bf16[64,640]{1,0:T(8,128)(2,1)S(1)} %collective-permute-done.4.refs_5_), channel_id=1, source_target_pairs={{0,1},{1,0},{2,3},{3,2},{4,5},{5,4},{6,7},{7,6},{8,9},{9,8},{10,11... | collective-permute-start | bytes 245768 | tf_op jit(solution)/shard_map/ppermute | solution.py:39
  11.1 4.4 %collective-permute-start.8 = (bf16[64,640]{1,0:T(8,128)(2,1)S(1)}, bf16[64,640]{1,0:T(8,128)(2,1)S(1)}, u32[]{:S(2)}, u32[]{:S(2)}) collective-permute-start(bf16[64,640]{1,0:T(8,128)(2,1)S(1)} %collective-permute-done.4.refs_5_), channel_id=1, source_target_pairs={{0,2},{1,5},{2,6},{3,1},{6,10},{7,3},{10,14},{11,7},{14,12},{15,11... | collective-permute-start | bytes 245768 | tf_op jit(solution)/shard_map/ppermute | solution.py:48
  14.1 3.4 %collective-permute-start.7 = (bf16[64,640]{1,0:T(8,128)(2,1)S(1)}, bf16[64,640]{1,0:T(8,128)(2,1)S(1)}, u32[]{:S(2)}, u32[]{:S(2)}) collective-permute-start(bf16[64,640]{1,0:T(8,128)(2,1)S(1)} %collective-permute-done.2.refs_4_), channel_id=1, source_target_pairs={{0,1},{1,0},{2,3},{3,2},{4,5},{5,4},{6,7},{7,6},{8,9},{9,8},{10,11... | collective-permute-start | bytes 245768 | tf_op jit(solution)/shard_map/ppermute | solution.py:39
  14.1 4.4 %collective-permute-start.6 = (bf16[64,640]{1,0:T(8,128)(2,1)S(1)}, bf16[64,640]{1,0:T(8,128)(2,1)S(1)}, u32[]{:S(2)}, u32[]{:S(2)}) collective-permute-start(bf16[64,640]{1,0:T(8,128)(2,1)S(1)} %collective-permute-done.2.refs_4_), channel_id=1, source_target_pairs={{0,2},{1,5},{2,6},{3,1},{6,10},{7,3},{10,14},{11,7},{14,12},{15,11... | collective-permute-start | bytes 245768 | tf_op jit(solution)/shard_map/ppermute | solution.py:48
  15.5 4.5 %collective-permute-start.13 = (bf16[64,640]{1,0:T(8,128)(2,1)S(1)}, bf16[64,640]{1,0:T(8,128)(2,1)S(1)}, u32[]{:S(2)}, u32[]{:S(2)}) collective-permute-start(bf16[64,640]{1,0:T(8,128)(2,1)S(1)} %collective-permute-done.8.refs_7_), channel_id=1, source_target_pairs={{0,1},{1,0},{2,3},{3,2},{4,5},{5,4},{6,7},{7,6},{8,9},{9,8},{10,11... | collective-permute-start | bytes 245768 | tf_op jit(solution)/shard_map/ppermute | solution.py:39
  15.9 4.4 %collective-permute-start.12 = (bf16[64,640]{1,0:T(8,128)(2,1)S(1)}, bf16[64,640]{1,0:T(8,128)(2,1)S(1)}, u32[]{:S(2)}, u32[]{:S(2)}) collective-permute-start(bf16[64,640]{1,0:T(8,128)(2,1)S(1)} %collective-permute-done.8.refs_7_), channel_id=1, source_target_pairs={{0,2},{1,5},{2,6},{3,1},{6,10},{7,3},{10,14},{11,7},{14,12},{15,11... | collective-permute-start | bytes 245768 | tf_op jit(solution)/shard_map/ppermute | solution.py:48
  18.6 1.8 %collective-permute-start.11 = (bf16[64,640]{1,0:T(8,128)(2,1)S(1)}, bf16[64,640]{1,0:T(8,128)(2,1)S(1)}, u32[]{:S(2)}, u32[]{:S(2)}) collective-permute-start(bf16[64,640]{1,0:T(8,128)(2,1)S(1)} %collective-permute-done.6.refs_6_), channel_id=1, source_target_pairs={{0,1},{1,0},{2,3},{3,2},{4,5},{5,4},{6,7},{7,6},{8,9},{9,8},{10,11... | collective-permute-start | bytes 245768 | tf_op jit(solution)/shard_map/ppermute | solution.py:39
  18.6 4.4 %collective-permute-start.10 = (bf16[64,640]{1,0:T(8,128)(2,1)S(1)}, bf16[64,640]{1,0:T(8,128)(2,1)S(1)}, u32[]{:S(2)}, u32[]{:S(2)}) collective-permute-start(bf16[64,640]{1,0:T(8,128)(2,1)S(1)} %collective-permute-done.6.refs_6_), channel_id=1, source_target_pairs={{0,2},{1,5},{2,6},{3,1},{6,10},{7,3},{10,14},{11,7},{14,12},{15,11... | collective-permute-start | bytes 245768 | tf_op jit(solution)/shard_map/ppermute | solution.py:48
  29.0 2.0 %collective-permute-start.14 = (bf16[128,2048]{1,0:T(8,128)(2,1)S(1)}, bf16[128,2048]{1,0:T(8,128)(2,1)S(1)}, u32[]{:S(2)}, u32[]{:S(2)}) collective-permute-start(bf16[128,2048]{1,0:T(8,128)(2,1)S(1)} %get-tuple-element.96), channel_id=1, source_target_pairs={{0,1},{1,0},{2,3},{3,2},{4,5},{5,4},{6,7},{7,6},{8,9},{9,8},{10,11... | collective-permute-start | bytes 1572872 | tf_op jit(solution)/shard_map/ppermute | solution.py:39
  31.9 6.4 %collective-permute-start.15 = (bf16[128,1024]{1,0:T(8,128)(2,1)S(1)}, bf16[128,1024]{1,0:T(8,128)(2,1)S(1)}, u32[]{:S(2)}, u32[]{:S(2)}) collective-permute-start(bf16[128,1024]{1,0:T(8,128)(2,1)S(1)} %get-tuple-element.116.refs_0_), channel_id=1, source_target_pairs={{0,2},{1,5},{2,6},{3,1},{6,10},{7,3},{10,14},{11,7},{14,12},{15,11... | collective-permute-start | bytes 786440 | tf_op jit(solution)/shard_map/ppermute | solution.py:48
  33.3 7.8 %collective-permute-start.16 = (bf16[128,1024]{1,0:T(8,128)(2,1)S(1)}, bf16[128,1024]{1,0:T(8,128)(2,1)S(1)}, u32[]{:S(2)}, u32[]{:S(2)}) collective-permute-start(bf16[128,1024]{1,0:T(8,128)(2,1)S(1)} %get-tuple-element.117.refs_1_), channel_id=1, source_target_pairs={{0,2},{1,5},{2,6},{3,1},{6,10},{7,3},{10,14},{11,7},{14,12},{15,11... | collective-permute-start | bytes 786440 | tf_op jit(solution)/shard_map/ppermute | solution.py:48
  38.3 4.2 %collective-permute-start.18 = (bf16[128,1024]{1,0:T(8,128)(2,1)S(1)}, bf16[128,1024]{1,0:T(8,128)(2,1)S(1)}, u32[]{:S(2)}, u32[]{:S(2)}) collective-permute-start(bf16[128,1024]{1,0:T(8,128)(2,1)S(1)} %collective-permute-done.15.refs_2_), channel_id=1, source_target_pairs={{0,1},{1,0},{2,3},{3,2},{4,5},{5,4},{6,7},{7,6},{8,9},{9,8},{10,11... | collective-permute-start | bytes 786440 | tf_op jit(solution)/shard_map/ppermute | solution.py:39
  38.3 6.4 %collective-permute-start.17 = (bf16[128,1024]{1,0:T(8,128)(2,1)S(1)}, bf16[128,1024]{1,0:T(8,128)(2,1)S(1)}, u32[]{:S(2)}, u32[]{:S(2)}) collective-permute-start(bf16[128,1024]{1,0:T(8,128)(2,1)S(1)} %collective-permute-done.15.refs_2_), channel_id=1, source_target_pairs={{0,2},{1,5},{2,6},{3,1},{6,10},{7,3},{10,14},{11,7},{14,12},{15,11... | collective-permute-start | bytes 786440 | tf_op jit(solution)/shard_map/ppermute | solution.py:48
  41.1 4.9 %collective-permute-start.20 = (bf16[128,1024]{1,0:T(8,128)(2,1)S(1)}, bf16[128,1024]{1,0:T(8,128)(2,1)S(1)}, u32[]{:S(2)}, u32[]{:S(2)}) collective-permute-start(bf16[128,1024]{1,0:T(8,128)(2,1)S(1)} %collective-permute-done.16.refs_3_), channel_id=1, source_target_pairs={{0,1},{1,0},{2,3},{3,2},{4,5},{5,4},{6,7},{7,6},{8,9},{9,8},{10,11... | collective-permute-start | bytes 786440 | tf_op jit(solution)/shard_map/ppermute | solution.py:39
  41.1 6.4 %collective-permute-start.19 = (bf16[128,1024]{1,0:T(8,128)(2,1)S(1)}, bf16[128,1024]{1,0:T(8,128)(2,1)S(1)}, u32[]{:S(2)}, u32[]{:S(2)}) collective-permute-start(bf16[128,1024]{1,0:T(8,128)(2,1)S(1)} %collective-permute-done.16.refs_3_), channel_id=1, source_target_pairs={{0,2},{1,5},{2,6},{3,1},{6,10},{7,3},{10,14},{11,7},{14,12},{15,11... | collective-permute-start | bytes 786440 | tf_op jit(solution)/shard_map/ppermute | solution.py:48
  44.7 4.2 %collective-permute-start.22 = (bf16[128,1024]{1,0:T(8,128)(2,1)S(1)}, bf16[128,1024]{1,0:T(8,128)(2,1)S(1)}, u32[]{:S(2)}, u32[]{:S(2)}) collective-permute-start(bf16[128,1024]{1,0:T(8,128)(2,1)S(1)} %collective-permute-done.17.refs_4_), channel_id=1, source_target_pairs={{0,1},{1,0},{2,3},{3,2},{4,5},{5,4},{6,7},{7,6},{8,9},{9,8},{10,11... | collective-permute-start | bytes 786440 | tf_op jit(solution)/shard_map/ppermute | solution.py:39
  44.7 6.4 %collective-permute-start.21 = (bf16[128,1024]{1,0:T(8,128)(2,1)S(1)}, bf16[128,1024]{1,0:T(8,128)(2,1)S(1)}, u32[]{:S(2)}, u32[]{:S(2)}) collective-permute-start(bf16[128,1024]{1,0:T(8,128)(2,1)S(1)} %collective-permute-done.17.refs_4_), channel_id=1, source_target_pairs={{0,2},{1,5},{2,6},{3,1},{6,10},{7,3},{10,14},{11,7},{14,12},{15,11... | collective-permute-start | bytes 786440 | tf_op jit(solution)/shard_map/ppermute | solution.py:48
  47.5 4.9 %collective-permute-start.24 = (bf16[128,1024]{1,0:T(8,128)(2,1)S(1)}, bf16[128,1024]{1,0:T(8,128)(2,1)S(1)}, u32[]{:S(2)}, u32[]{:S(2)}) collective-permute-start(bf16[128,1024]{1,0:T(8,128)(2,1)S(1)} %collective-permute-done.19.refs_5_), channel_id=1, source_target_pairs={{0,1},{1,0},{2,3},{3,2},{4,5},{5,4},{6,7},{7,6},{8,9},{9,8},{10,11... | collective-permute-start | bytes 786440 | tf_op jit(solution)/shard_map/ppermute | solution.py:39
  47.5 6.4 %collective-permute-start.23 = (bf16[128,1024]{1,0:T(8,128)(2,1)S(1)}, bf16[128,1024]{1,0:T(8,128)(2,1)S(1)}, u32[]{:S(2)}, u32[]{:S(2)}) collective-permute-start(bf16[128,1024]{1,0:T(8,128)(2,1)S(1)} %collective-permute-done.19.refs_5_), channel_id=1, source_target_pairs={{0,2},{1,5},{2,6},{3,1},{6,10},{7,3},{10,14},{11,7},{14,12},{15,11... | collective-permute-start | bytes 786440 | tf_op jit(solution)/shard_map/ppermute | solution.py:48
  51.1 2.8 %collective-permute-start.26 = (bf16[128,1024]{1,0:T(8,128)(2,1)S(1)}, bf16[128,1024]{1,0:T(8,128)(2,1)S(1)}, u32[]{:S(2)}, u32[]{:S(2)}) collective-permute-start(bf16[128,1024]{1,0:T(8,128)(2,1)S(1)} %collective-permute-done.21.refs_6_), channel_id=1, source_target_pairs={{0,1},{1,0},{2,3},{3,2},{4,5},{5,4},{6,7},{7,6},{8,9},{9,8},{10,11... | collective-permute-start | bytes 786440 | tf_op jit(solution)/shard_map/ppermute | solution.py:39
  51.1 6.4 %collective-permute-start.25 = (bf16[128,1024]{1,0:T(8,128)(2,1)S(1)}, bf16[128,1024]{1,0:T(8,128)(2,1)S(1)}, u32[]{:S(2)}, u32[]{:S(2)}) collective-permute-start(bf16[128,1024]{1,0:T(8,128)(2,1)S(1)} %collective-permute-done.21.refs_6_), channel_id=1, source_target_pairs={{0,2},{1,5},{2,6},{3,1},{6,10},{7,3},{10,14},{11,7},{14,12},{15,11... | collective-permute-start | bytes 786440 | tf_op jit(solution)/shard_map/ppermute | solution.py:48
  53.9 3.6 %collective-permute-start.28 = (bf16[128,1024]{1,0:T(8,128)(2,1)S(1)}, bf16[128,1024]{1,0:T(8,128)(2,1)S(1)}, u32[]{:S(2)}, u32[]{:S(2)}) collective-permute-start(bf16[128,1024]{1,0:T(8,128)(2,1)S(1)} %collective-permute-done.23.refs_7_), channel_id=1, source_target_pairs={{0,1},{1,0},{2,3},{3,2},{4,5},{5,4},{6,7},{7,6},{8,9},{9,8},{10,11... | collective-permute-start | bytes 786440 | tf_op jit(solution)/shard_map/ppermute | solution.py:39
  57.4 1.5 %collective-permute-start.27 = (bf16[128,1024]{1,0:T(8,128)(2,1)S(1)}, bf16[128,1024]{1,0:T(8,128)(2,1)S(1)}, u32[]{:S(2)}, u32[]{:S(2)}) collective-permute-start(bf16[128,1024]{1,0:T(8,128)(2,1)S(1)} %collective-permute-done.25.refs_8_), channel_id=1, source_target_pairs={{0,1},{1,0},{2,3},{3,2},{4,5},{5,4},{6,7},{7,6},{8,9},{9,8},{10,11... | collective-permute-start | bytes 786440 | tf_op jit(solution)/shard_map/ppermute | solution.py:39
  84.1 1.6 %collective-permute-start.29 = (bf16[128,1024]{1,0:T(8,128)(2,1)S(1)}, bf16[128,1024]{1,0:T(8,128)(2,1)S(1)}, u32[]{:S(2)}, u32[]{:S(2)}) collective-permute-start(bf16[128,1024]{1,0:T(8,128)(2,1)S(1)} %get-tuple-element.132), channel_id=1, source_target_pairs={{0,1},{1,0},{2,3},{3,2},{4,5},{5,4},{6,7},{7,6},{8,9},{9,8},{10,11... | collective-permute-start | bytes 786440 | tf_op jit(solution)/shard_map/ppermute | solution.py:39
  84.3 3.0 %collective-permute-start.38 = (bf16[128,1024]{1,0:T(8,128)(2,1)S(1)}, bf16[128,1024]{1,0:T(8,128)(2,1)S(1)}, u32[]{:S(2)}, u32[]{:S(2)}) collective-permute-start(bf16[128,1024]{1,0:T(8,128)(2,1)S(1)} %get-tuple-element.147), channel_id=1, source_target_pairs={{0,1},{1,0},{2,3},{3,2},{4,5},{5,4},{6,7},{7,6},{8,9},{9,8},{10,11... | collective-permute-start | bytes 786440 | tf_op jit(solution)/shard_map/ppermute | solution.py:39
  85.8 6.4 %collective-permute-start.30 = (bf16[128,1024]{1,0:T(8,128)(2,1)S(1)}, bf16[128,1024]{1,0:T(8,128)(2,1)S(1)}, u32[]{:S(2)}, u32[]{:S(2)}) collective-permute-start(bf16[128,1024]{1,0:T(8,128)(2,1)S(1)} %add_convert_fusion.7), channel_id=1, source_target_pairs={{0,2},{1,5},{2,6},{3,1},{6,10},{7,3},{10,14},{11,7},{14,12},{15,11... | collective-permute-start | bytes 786440 | tf_op jit(solution)/shard_map/ppermute | solution.py:48
  87.2 5.0 %collective-permute-start.32 = (bf16[128,1024]{1,0:T(8,128)(2,1)S(1)}, bf16[128,1024]{1,0:T(8,128)(2,1)S(1)}, u32[]{:S(2)}, u32[]{:S(2)}) collective-permute-start(bf16[128,1024]{1,0:T(8,128)(2,1)S(1)} %get-tuple-element.136), channel_id=1, source_target_pairs={{0,1},{1,0},{2,3},{3,2},{4,5},{5,4},{6,7},{7,6},{8,9},{9,8},{10,11... | collective-permute-start | bytes 786440 | tf_op jit(solution)/shard_map/ppermute | solution.py:39
  87.3 7.7 %collective-permute-start.39 = (bf16[128,1024]{1,0:T(8,128)(2,1)S(1)}, bf16[128,1024]{1,0:T(8,128)(2,1)S(1)}, u32[]{:S(2)}, u32[]{:S(2)}) collective-permute-start(bf16[128,1024]{1,0:T(8,128)(2,1)S(1)} %add_convert_fusion.3), channel_id=1, source_target_pairs={{0,2},{1,5},{2,6},{3,1},{6,10},{7,3},{10,14},{11,7},{14,12},{15,11... | collective-permute-start | bytes 786440 | tf_op jit(solution)/shard_map/ppermute | solution.py:48
  88.9 6.1 %collective-permute-start.41 = (bf16[128,1024]{1,0:T(8,128)(2,1)S(1)}, bf16[128,1024]{1,0:T(8,128)(2,1)S(1)}, u32[]{:S(2)}, u32[]{:S(2)}) collective-permute-start(bf16[128,1024]{1,0:T(8,128)(2,1)S(1)} %get-tuple-element.151), channel_id=1, source_target_pairs={{0,1},{1,0},{2,3},{3,2},{4,5},{5,4},{6,7},{7,6},{8,9},{9,8},{10,11... | collective-permute-start | bytes 786440 | tf_op jit(solution)/shard_map/ppermute | solution.py:39
  92.3 6.4 %collective-permute-start.33 = (bf16[128,1024]{1,0:T(8,128)(2,1)S(1)}, bf16[128,1024]{1,0:T(8,128)(2,1)S(1)}, u32[]{:S(2)}, u32[]{:S(2)}) collective-permute-start(bf16[128,1024]{1,0:T(8,128)(2,1)S(1)} %add_convert_fusion.6), channel_id=1, source_target_pairs={{0,2},{1,5},{2,6},{3,1},{6,10},{7,3},{10,14},{11,7},{14,12},{15,11... | collective-permute-start | bytes 786440 | tf_op jit(solution)/shard_map/ppermute | solution.py:48
  93.8 5.0 %collective-permute-start.31 = (bf16[128,1024]{1,0:T(8,128)(2,1)S(1)}, bf16[128,1024]{1,0:T(8,128)(2,1)S(1)}, u32[]{:S(2)}, u32[]{:S(2)}) collective-permute-start(bf16[128,1024]{1,0:T(8,128)(2,1)S(1)} %get-tuple-element.134), channel_id=1, source_target_pairs={{0,1},{1,0},{2,3},{3,2},{4,5},{5,4},{6,7},{7,6},{8,9},{9,8},{10,11... | collective-permute-start | bytes 786440 | tf_op jit(solution)/shard_map/ppermute | solution.py:39
  95.0 6.6 %collective-permute-start.40 = (bf16[128,1024]{1,0:T(8,128)(2,1)S(1)}, bf16[128,1024]{1,0:T(8,128)(2,1)S(1)}, u32[]{:S(2)}, u32[]{:S(2)}) collective-permute-start(bf16[128,1024]{1,0:T(8,128)(2,1)S(1)} %get-tuple-element.149), channel_id=1, source_target_pairs={{0,1},{1,0},{2,3},{3,2},{4,5},{5,4},{6,7},{7,6},{8,9},{9,8},{10,11... | collective-permute-start | bytes 786440 | tf_op jit(solution)/shard_map/ppermute | solution.py:39
  95.2 6.4 %collective-permute-start.42 = (bf16[128,1024]{1,0:T(8,128)(2,1)S(1)}, bf16[128,1024]{1,0:T(8,128)(2,1)S(1)}, u32[]{:S(2)}, u32[]{:S(2)}) collective-permute-start(bf16[128,1024]{1,0:T(8,128)(2,1)S(1)} %add_convert_fusion.2), channel_id=1, source_target_pairs={{0,2},{1,5},{2,6},{3,1},{6,10},{7,3},{10,14},{11,7},{14,12},{15,11... | collective-permute-start | bytes 786440 | tf_op jit(solution)/shard_map/ppermute | solution.py:48
  98.9 6.4 %collective-permute-start.34 = (bf16[128,1024]{1,0:T(8,128)(2,1)S(1)}, bf16[128,1024]{1,0:T(8,128)(2,1)S(1)}, u32[]{:S(2)}, u32[]{:S(2)}) collective-permute-start(bf16[128,1024]{1,0:T(8,128)(2,1)S(1)} %add_convert_fusion.5), channel_id=1, source_target_pairs={{0,2},{1,5},{2,6},{3,1},{6,10},{7,3},{10,14},{11,7},{14,12},{15,11... | collective-permute-start | bytes 786440 | tf_op jit(solution)/shard_map/ppermute | solution.py:48
  100.3 5.0 %collective-permute-start.36 = (bf16[128,1024]{1,0:T(8,128)(2,1)S(1)}, bf16[128,1024]{1,0:T(8,128)(2,1)S(1)}, u32[]{:S(2)}, u32[]{:S(2)}) collective-permute-start(bf16[128,1024]{1,0:T(8,128)(2,1)S(1)} %get-tuple-element.143), channel_id=1, source_target_pairs={{0,1},{1,0},{2,3},{3,2},{4,5},{5,4},{6,7},{7,6},{8,9},{9,8},{10,11... | collective-permute-start | bytes 786440 | tf_op jit(solution)/shard_map/ppermute | solution.py:39
  101.7 5.9 %collective-permute-start.43 = (bf16[128,1024]{1,0:T(8,128)(2,1)S(1)}, bf16[128,1024]{1,0:T(8,128)(2,1)S(1)}, u32[]{:S(2)}, u32[]{:S(2)}) collective-permute-start(bf16[128,1024]{1,0:T(8,128)(2,1)S(1)} %add_convert_fusion.1), channel_id=1, source_target_pairs={{0,3},{1,4},{2,7},{3,0},{6,11},{7,2},{10,15},{11,6},{14,13},{15,10... | collective-permute-start | bytes 786440 | tf_op jit(solution)/shard_map/ppermute | solution.py:48
  105.3 2.3 %collective-permute-start.35 = (bf16[128,1024]{1,0:T(8,128)(2,1)S(1)}, bf16[128,1024]{1,0:T(8,128)(2,1)S(1)}, u32[]{:S(2)}, u32[]{:S(2)}) collective-permute-start(bf16[128,1024]{1,0:T(8,128)(2,1)S(1)} %get-tuple-element.141), channel_id=1, source_target_pairs={{0,1},{1,0},{2,3},{3,2},{4,5},{5,4},{6,7},{7,6},{8,9},{9,8},{10,11... | collective-permute-start | bytes 786440 | tf_op jit(solution)/shard_map/ppermute | solution.py:39
  105.5 6.4 %collective-permute-start.37 = (bf16[128,1024]{1,0:T(8,128)(2,1)S(1)}, bf16[128,1024]{1,0:T(8,128)(2,1)S(1)}, u32[]{:S(2)}, u32[]{:S(2)}) collective-permute-start(bf16[128,1024]{1,0:T(8,128)(2,1)S(1)} %add_convert_fusion.4), channel_id=1, source_target_pairs={{0,2},{1,5},{2,6},{3,1},{6,10},{7,3},{10,14},{11,7},{14,12},{15,11... | collective-permute-start | bytes 786440 | tf_op jit(solution)/shard_map/ppermute | solution.py:48

commit v17 on v15

--- a/solution.py
+++ b/solution.py
@@ -20,7 +20,7 @@
 MIB = 1024 * 1024
 VMEM_LIMIT = 50 * MIB
 HELD = 7
-PIECES = 2
+PIECES = 4
 SWAP = [(0, 1), (1, 0)]
 FEW = 8
 
@@ -178,20 +178,25 @@
         key = jnp.concatenate([keyval[:, base : base + NOPE], rope], axis=1)
         scores = lax.dot_general(q_ref[:, h * depth : (h + 1) * depth], key, (((1,), (1,)), ((), ())), preferred_element_type=jnp.float32)
         scores = jnp.where(visible, scores * scale, -1e30)
+        values = keyval[:, base + NOPE : base + NOPE + VHEAD]
+        if blocks == count:
+            weights = jnp.where(visible, jnp.exp(scores - jnp.max(scores, axis=1, keepdims=True)), 0.0)
+            mixed = jnp.dot(weights.astype(jnp.bfloat16), values, preferred_element_type=jnp.float32)
+            acc_ref[h] = mixed / jnp.sum(weights, axis=1, keepdims=True)
+            continue
         best = m_ref[h]
         fresh = jnp.maximum(best, jnp.max(scores, axis=1, keepdims=True))
         weights = jnp.where(visible, jnp.exp(scores - fresh), 0.0)
         shrink = jnp.exp(best - fresh)
         m_ref[h] = fresh
         l_ref[h] = l_ref[h] * shrink + jnp.sum(weights, axis=1, keepdims=True)
-        mixed = jnp.dot(
-            weights.astype(jnp.bfloat16), keyval[:, base + NOPE : base + NOPE + VHEAD], preferred_element_type=jnp.float32
-        )
+        mixed = jnp.dot(weights.astype(jnp.bfloat16), values, preferred_element_type=jnp.float32)
         acc_ref[h] = acc_ref[h] * shrink + mixed
 
     @pl.when(chunk == pl.num_programs(0) - 1)
     def _():
-        attended = [(acc_ref[h] / l_ref[h]).astype(jnp.bfloat16) for h in range(heads)]
+        totals = [1.0 if blocks == count else l_ref[h] for h in range(heads)]
+        attended = [(acc_ref[h] / totals[h]).astype(jnp.bfloat16) for h in range(heads)]
         copies[1].wait()
         copies[2].wait()
         out = jnp.dot(jnp.concatenate(attended, axis=1), proj_ref[...], preferred_element_type=jnp.float32)

time: 113 us -> 112 us (level)
  no operation moved by 1% of the time
where the time goes in v17:
time: 112 us
  waiting for transfers between devices  37.3 us (33%)
  Pallas kernels  35.5 us (32%)
  starting transfers between devices  35.3 us (32%)
  local copies, waits for them, and re-layouts  2.13 us (2%)
  other arithmetic  1.75 us (2%)
    ppermute x22, waiting for transfers between devices, turn(): return lax.ppermute(value, ('ctx', 'exp'), pairs)  34.7 us
    ppermute x22, starting transfers between devices, turn(): return lax.ppermute(value, ('ctx', 'exp'), pairs)  33.7 us
    pallas_call x1, Pallas kernels, experts_fused(): pl.pallas_call(functools.partial(fused_kernel, count), in_specs=[pl.Block...  25.3 us
    pallas_call x1, Pallas kernels, attend(): pl.pallas_call(functools.partial(attend_kernel, count, blocks, heads), gr...  5.06 us
    ppermute x22, waiting for transfers between devices, swap(): return lax.ppermute(value, 'exp', SWAP)  2.61 us
  transfers between devices with their start and end apart: 44, of which 21 were waited for; matrix products, arithmetic and copies ran while one was open for 3% of the time, Pallas kernels for 3%

profile of v17, /device:TPU:0, one launch (start us, length us, event | category | flops | bytes accessed | tf_op | source)
XLA Modules:
  0.0 112.1 jit_solution(10809861401480834428)
XLA Ops:
  0.0 1.1 %pack.1 = (bf16[64,640]{1,0:T(8,128)(2,1)S(1)}, bf16[64,640]{1,0:T(8,128)(2,1)S(1)}) custom-call(bf16[576,128]{1,0:T(8,128)(2,1)} %bitcast.11, s32[6,128]{1,0:T(8,128)} %bitcast.12, f32[6,128]{1,0:T(8,128)} %bitcast.13), custom_call_target="tpu_custom_call" | custom-call | tf_op jit(solution)/shard_map/pack/pallas_call | solution.py:339
  1.1 3.0 %collective-permute-start.1 = (bf16[64,640]{1,0:T(8,128)(2,1)S(1)}, bf16[64,640]{1,0:T(8,128)(2,1)S(1)}, u32[]{:S(2)}, u32[]{:S(2)}) collective-permute-start(bf16[64,640]{1,0:T(8,128)(2,1)S(1)} %get-tuple-element.108.refs_1_), channel_id=1, source_target_pairs={{0,2},{1,5},{2,6},{3,1},{6,10},{7,3},{10,14},{11,7},{14,12},{15,11... | collective-permute-start | bytes 245768 | tf_op jit(solution)/shard_map/ppermute | solution.py:48
  4.2 1.6 %collective-permute-start = (bf16[64,640]{1,0:T(8,128)(2,1)S(1)}, bf16[64,640]{1,0:T(8,128)(2,1)S(1)}, u32[]{:S(2)}, u32[]{:S(2)}) collective-permute-start(bf16[64,640]{1,0:T(8,128)(2,1)S(1)} %get-tuple-element.107.refs_0_), channel_id=1, source_target_pairs={{0,2},{1,5},{2,6},{3,1},{6,10},{7,3},{10,14},{11,7},{14,12},{15,11... | collective-permute-start | bytes 245768 | tf_op jit(solution)/shard_map/ppermute | solution.py:48
  6.7 2.0 %collective-permute-start.4 = (bf16[64,640]{1,0:T(8,128)(2,1)S(1)}, bf16[64,640]{1,0:T(8,128)(2,1)S(1)}, u32[]{:S(2)}, u32[]{:S(2)}) collective-permute-start(bf16[64,640]{1,0:T(8,128)(2,1)S(1)} %collective-permute-done.1.refs_3_), channel_id=1, source_target_pairs={{0,2},{1,5},{2,6},{3,1},{6,10},{7,3},{10,14},{11,7},{14,12},{15,11... | collective-permute-start | bytes 245768 | tf_op jit(solution)/shard_map/ppermute | solution.py:48
  8.6 0.7 concatenate.4.info
  9.7 1.4 %collective-permute-start.2 = (bf16[64,640]{1,0:T(8,128)(2,1)S(1)}, bf16[64,640]{1,0:T(8,128)(2,1)S(1)}, u32[]{:S(2)}, u32[]{:S(2)}) collective-permute-start(bf16[64,640]{1,0:T(8,128)(2,1)S(1)} %collective-permute-done.refs_2_), channel_id=1, source_target_pairs={{0,2},{1,5},{2,6},{3,1},{6,10},{7,3},{10,14},{11,7},{14,12},{15,11... | collective-permute-start | bytes 245768 | tf_op jit(solution)/shard_map/ppermute | solution.py:48
  11.0 0.7 reshape.3.gain_ref
  11.8 1.6 %collective-permute-start.8 = (bf16[64,640]{1,0:T(8,128)(2,1)S(1)}, bf16[64,640]{1,0:T(8,128)(2,1)S(1)}, u32[]{:S(2)}, u32[]{:S(2)}) collective-permute-start(bf16[64,640]{1,0:T(8,128)(2,1)S(1)} %collective-permute-done.4.refs_5_), channel_id=1, source_target_pairs={{0,2},{1,5},{2,6},{3,1},{6,10},{7,3},{10,14},{11,7},{14,12},{15,11... | collective-permute-start | bytes 245768 | tf_op jit(solution)/shard_map/ppermute | solution.py:48
  14.1 1.4 %collective-permute-start.6 = (bf16[64,640]{1,0:T(8,128)(2,1)S(1)}, bf16[64,640]{1,0:T(8,128)(2,1)S(1)}, u32[]{:S(2)}, u32[]{:S(2)}) collective-permute-start(bf16[64,640]{1,0:T(8,128)(2,1)S(1)} %collective-permute-done.2.refs_4_), channel_id=1, source_target_pairs={{0,2},{1,5},{2,6},{3,1},{6,10},{7,3},{10,14},{11,7},{14,12},{15,11... | collective-permute-start | bytes 245768 | tf_op jit(solution)/shard_map/ppermute | solution.py:48
  15.5 1.2 %stage.1.refs_16_ = bf16[512,1024]{1,0:T(8,128)(2,1)S(1)} custom-call(bf16[512,1024]{1,0:T(8,128)(2,1)} %source), custom_call_target="tpu_custom_call" | custom-call | tf_op jit(solution)/shard_map/stage/pallas_call | solution.py:247
  17.3 1.2 %collective-permute-start.12 = (bf16[64,640]{1,0:T(8,128)(2,1)S(1)}, bf16[64,640]{1,0:T(8,128)(2,1)S(1)}, u32[]{:S(2)}, u32[]{:S(2)}) collective-permute-start(bf16[64,640]{1,0:T(8,128)(2,1)S(1)} %collective-permute-done.8.refs_7_), channel_id=1, source_target_pairs={{0,2},{1,5},{2,6},{3,1},{6,10},{7,3},{10,14},{11,7},{14,12},{15,11... | collective-permute-start | bytes 245768 | tf_op jit(solution)/shard_map/ppermute | solution.py:48
  18.6 1.5 %collective-permute-start.10 = (bf16[64,640]{1,0:T(8,128)(2,1)S(1)}, bf16[64,640]{1,0:T(8,128)(2,1)S(1)}, u32[]{:S(2)}, u32[]{:S(2)}) collective-permute-start(bf16[64,640]{1,0:T(8,128)(2,1)S(1)} %collective-permute-done.6.refs_6_), channel_id=1, source_target_pairs={{0,2},{1,5},{2,6},{3,1},{6,10},{7,3},{10,14},{11,7},{14,12},{15,11... | collective-permute-start | bytes 245768 | tf_op jit(solution)/shard_map/ppermute | solution.py:48
  20.1 1.6 %collective-permute-done.12.refs_9_ = bf16[64,640]{1,0:T(8,128)(2,1)S(1)} collective-permute-done((bf16[64,640]{1,0:T(8,128)(2,1)S(1)}, bf16[64,640]{1,0:T(8,128)(2,1)S(1)}, u32[]{:S(2)}, u32[]{:S(2)}) %collective-permute-start.12) | collective-permute-done | bytes 81952 | tf_op jit(solution)/shard_map/ppermute | solution.py:48
  21.7 1.4 %collective-permute-done.10.refs_8_ = bf16[64,640]{1,0:T(8,128)(2,1)S(1)} collective-permute-done((bf16[64,640]{1,0:T(8,128)(2,1)S(1)}, bf16[64,640]{1,0:T(8,128)(2,1)S(1)}, u32[]{:S(2)}, u32[]{:S(2)}) %collective-permute-start.10) | collective-permute-done | bytes 81952 | tf_op jit(solution)/shard_map/ppermute | solution.py:48
  23.1 5.1 %attend.1 = (bf16[128,2048]{1,0:T(8,128)(2,1)S(1)}, f32[128,2048]{1,0:T(8,128)S(1)}) custom-call(s32[42]{0:T(128)S(1)} %concatenate.4.info, bf16[64,640]{1,0:T(8,128)(2,1)S(1)} %get-tuple-element.107.refs_0_, bf16[64,640]{1,0:T(8,128)(2,1)S(1)} %get-tuple-element.108.refs_1_, bf16[64,640]{1,0:T(8,128)(2,1)S(1)} %collective-permute-done.refs_2_, ...), custom_call_target="tpu_custom_call" | custom-call | tf_op jit(solution)/shard_map/attend/pallas_call | solution.py:219
  28.3 1.8 %route.1.refs_16_ = bf16[8,128,128]{2,1,0:T(8,128)(2,1)S(1)} custom-call(s32[2]{0:T(128)S(1)} %pad_add_fusion.where, bf16[64,640]{1,0:T(8,128)(2,1)S(1)} %get-tuple-element.107.refs_0_, bf16[64,640]{1,0:T(8,128)(2,1)S(1)} %get-tuple-element.108.refs_1_, bf16[64,640]{1,0:T(8,128)(2,1)S(1)} %collective-permute-done.refs_2_, ...), custom_call_target="tpu_custom_call" | custom-call | tf_op jit(solution)/shard_map/route/pallas_call | solution.py:281
  30.2 0.9 norm.1
  31.1 1.5 %collective-permute-start.15 = (bf16[128,1024]{1,0:T(8,128)(2,1)S(1)}, bf16[128,1024]{1,0:T(8,128)(2,1)S(1)}, u32[]{:S(2)}, u32[]{:S(2)}) collective-permute-start(bf16[128,1024]{1,0:T(8,128)(2,1)S(1)} %get-tuple-element.126.refs_0_), channel_id=1, source_target_pairs={{0,2},{1,5},{2,6},{3,1},{6,10},{7,3},{10,14},{11,7},{14,12},{15,11... | collective-permute-start | bytes 786440 | tf_op jit(solution)/shard_map/ppermute | solution.py:48
  32.6 1.4 %collective-permute-start.16 = (bf16[128,1024]{1,0:T(8,128)(2,1)S(1)}, bf16[128,1024]{1,0:T(8,128)(2,1)S(1)}, u32[]{:S(2)}, u32[]{:S(2)}) collective-permute-start(bf16[128,1024]{1,0:T(8,128)(2,1)S(1)} %get-tuple-element.127.refs_1_), channel_id=1, source_target_pairs={{0,2},{1,5},{2,6},{3,1},{6,10},{7,3},{10,14},{11,7},{14,12},{15,11... | collective-permute-start | bytes 786440 | tf_op jit(solution)/shard_map/ppermute | solution.py:48
  34.0 3.5 %collective-permute-done.15.refs_2_ = bf16[128,1024]{1,0:T(8,128)(2,1)S(1)} collective-permute-done((bf16[128,1024]{1,0:T(8,128)(2,1)S(1)}, bf16[128,1024]{1,0:T(8,128)(2,1)S(1)}, u32[]{:S(2)}, u32[]{:S(2)}) %collective-permute-start.15) | collective-permute-done | bytes 262176 | tf_op jit(solution)/shard_map/ppermute | solution.py:48
  37.5 1.5 %collective-permute-start.17 = (bf16[128,1024]{1,0:T(8,128)(2,1)S(1)}, bf16[128,1024]{1,0:T(8,128)(2,1)S(1)}, u32[]{:S(2)}, u32[]{:S(2)}) collective-permute-start(bf16[128,1024]{1,0:T(8,128)(2,1)S(1)} %collective-permute-done.15.refs_2_), channel_id=1, source_target_pairs={{0,2},{1,5},{2,6},{3,1},{6,10},{7,3},{10,14},{11,7},{14,12},{15,11... | collective-permute-start | bytes 786440 | tf_op jit(solution)/shard_map/ppermute | solution.py:48
  39.0 1.3 %collective-permute-done.16.refs_3_ = bf16[128,1024]{1,0:T(8,128)(2,1)S(1)} collective-permute-done((bf16[128,1024]{1,0:T(8,128)(2,1)S(1)}, bf16[128,1024]{1,0:T(8,128)(2,1)S(1)}, u32[]{:S(2)}, u32[]{:S(2)}) %collective-permute-start.16) | collective-permute-done | bytes 262176 | tf_op jit(solution)/shard_map/ppermute | solution.py:48
  40.3 1.5 %collective-permute-start.19 = (bf16[128,1024]{1,0:T(8,128)(2,1)S(1)}, bf16[128,1024]{1,0:T(8,128)(2,1)S(1)}, u32[]{:S(2)}, u32[]{:S(2)}) collective-permute-start(bf16[128,1024]{1,0:T(8,128)(2,1)S(1)} %collective-permute-done.16.refs_3_), channel_id=1, source_target_pairs={{0,2},{1,5},{2,6},{3,1},{6,10},{7,3},{10,14},{11,7},{14,12},{15,11... | collective-permute-start | bytes 786440 | tf_op jit(solution)/shard_map/ppermute | solution.py:48
  41.8 2.1 %collective-permute-done.17.refs_4_ = bf16[128,1024]{1,0:T(8,128)(2,1)S(1)} collective-permute-done((bf16[128,1024]{1,0:T(8,128)(2,1)S(1)}, bf16[128,1024]{1,0:T(8,128)(2,1)S(1)}, u32[]{:S(2)}, u32[]{:S(2)}) %collective-permute-start.17) | collective-permute-done | bytes 262176 | tf_op jit(solution)/shard_map/ppermute | solution.py:48
  43.9 1.5 %collective-permute-start.21 = (bf16[128,1024]{1,0:T(8,128)(2,1)S(1)}, bf16[128,1024]{1,0:T(8,128)(2,1)S(1)}, u32[]{:S(2)}, u32[]{:S(2)}) collective-permute-start(bf16[128,1024]{1,0:T(8,128)(2,1)S(1)} %collective-permute-done.17.refs_4_), channel_id=1, source_target_pairs={{0,2},{1,5},{2,6},{3,1},{6,10},{7,3},{10,14},{11,7},{14,12},{15,11... | collective-permute-start | bytes 786440 | tf_op jit(solution)/shard_map/ppermute | solution.py:48
  45.4 1.3 %collective-permute-done.19.refs_5_ = bf16[128,1024]{1,0:T(8,128)(2,1)S(1)} collective-permute-done((bf16[128,1024]{1,0:T(8,128)(2,1)S(1)}, bf16[128,1024]{1,0:T(8,128)(2,1)S(1)}, u32[]{:S(2)}, u32[]{:S(2)}) %collective-permute-start.19) | collective-permute-done | bytes 262176 | tf_op jit(solution)/shard_map/ppermute | solution.py:48
  46.7 1.5 %collective-permute-start.23 = (bf16[128,1024]{1,0:T(8,128)(2,1)S(1)}, bf16[128,1024]{1,0:T(8,128)(2,1)S(1)}, u32[]{:S(2)}, u32[]{:S(2)}) collective-permute-start(bf16[128,1024]{1,0:T(8,128)(2,1)S(1)} %collective-permute-done.19.refs_5_), channel_id=1, source_target_pairs={{0,2},{1,5},{2,6},{3,1},{6,10},{7,3},{10,14},{11,7},{14,12},{15,11... | collective-permute-start | bytes 786440 | tf_op jit(solution)/shard_map/ppermute | solution.py:48
  48.2 2.1 %collective-permute-done.21.refs_6_ = bf16[128,1024]{1,0:T(8,128)(2,1)S(1)} collective-permute-done((bf16[128,1024]{1,0:T(8,128)(2,1)S(1)}, bf16[128,1024]{1,0:T(8,128)(2,1)S(1)}, u32[]{:S(2)}, u32[]{:S(2)}) %collective-permute-start.21) | collective-permute-done | bytes 262176 | tf_op jit(solution)/shard_map/ppermute | solution.py:48
  50.3 1.5 %collective-permute-start.25 = (bf16[128,1024]{1,0:T(8,128)(2,1)S(1)}, bf16[128,1024]{1,0:T(8,128)(2,1)S(1)}, u32[]{:S(2)}, u32[]{:S(2)}) collective-permute-start(bf16[128,1024]{1,0:T(8,128)(2,1)S(1)} %collective-permute-done.21.refs_6_), channel_id=1, source_target_pairs={{0,2},{1,5},{2,6},{3,1},{6,10},{7,3},{10,14},{11,7},{14,12},{15,11... | collective-permute-start | bytes 786440 | tf_op jit(solution)/shard_map/ppermute | solution.py:48
  51.7 1.3 %collective-permute-done.23.refs_7_ = bf16[128,1024]{1,0:T(8,128)(2,1)S(1)} collective-permute-done((bf16[128,1024]{1,0:T(8,128)(2,1)S(1)}, bf16[128,1024]{1,0:T(8,128)(2,1)S(1)}, u32[]{:S(2)}, u32[]{:S(2)}) %collective-permute-start.23) | collective-permute-done | bytes 262176 | tf_op jit(solution)/shard_map/ppermute | solution.py:48
  53.1 3.6 %collective-permute-done.25.refs_8_ = bf16[128,1024]{1,0:T(8,128)(2,1)S(1)} collective-permute-done((bf16[128,1024]{1,0:T(8,128)(2,1)S(1)}, bf16[128,1024]{1,0:T(8,128)(2,1)S(1)}, u32[]{:S(2)}, u32[]{:S(2)}) %collective-permute-start.25) | collective-permute-done | bytes 262176 | tf_op jit(solution)/shard_map/ppermute | solution.py:48
  56.6 1.5 %collective-permute-done.27.refs_9_ = bf16[128,1024]{1,0:T(8,128)(2,1)S(1)} collective-permute-done((bf16[128,1024]{1,0:T(8,128)(2,1)S(1)}, bf16[128,1024]{1,0:T(8,128)(2,1)S(1)}, u32[]{:S(2)}, u32[]{:S(2)}) %collective-permute-start.27) | collective-permute-done | bytes 262176 | tf_op jit(solution)/shard_map/ppermute | solution.py:39
  58.2 25.3 %experts.1 = (bf16[128,1024]{1,0:T(8,128)(2,1)S(1)}, bf16[128,1024]{1,0:T(8,128)(2,1)S(1)}, bf16[128,1024]{1,0:T(8,128)(2,1)S(1)}, bf16[128,1024]{1,0:T(8,128)(2...) custom-call(s32[2]{0:T(128)S(1)} %pad_add_fusion.where, ...), custom_call_target="tpu_custom_call" | custom-call | tf_op jit(solution)/shard_map/experts/pallas_call | solution.py:459
  84.0 1.0 collective-permute-done.29
  85.1 1.5 %collective-permute-start.30 = (bf16[128,1024]{1,0:T(8,128)(2,1)S(1)}, bf16[128,1024]{1,0:T(8,128)(2,1)S(1)}, u32[]{:S(2)}, u32[]{:S(2)}) collective-permute-start(bf16[128,1024]{1,0:T(8,128)(2,1)S(1)} %add_convert_fusion.7), channel_id=1, source_target_pairs={{0,2},{1,5},{2,6},{3,1},{6,10},{7,3},{10,14},{11,7},{14,12},{15,11... | collective-permute-start | bytes 786440 | tf_op jit(solution)/shard_map/ppermute | solution.py:48
  86.7 1.5 %collective-permute-start.39 = (bf16[128,1024]{1,0:T(8,128)(2,1)S(1)}, bf16[128,1024]{1,0:T(8,128)(2,1)S(1)}, u32[]{:S(2)}, u32[]{:S(2)}) collective-permute-start(bf16[128,1024]{1,0:T(8,128)(2,1)S(1)} %add_convert_fusion.3), channel_id=1, source_target_pairs={{0,2},{1,5},{2,6},{3,1},{6,10},{7,3},{10,14},{11,7},{14,12},{15,11... | collective-permute-start | bytes 786440 | tf_op jit(solution)/shard_map/ppermute | solution.py:48
  88.2 3.4 %collective-permute-done.30 = bf16[128,1024]{1,0:T(8,128)(2,1)S(1)} collective-permute-done((bf16[128,1024]{1,0:T(8,128)(2,1)S(1)}, bf16[128,1024]{1,0:T(8,128)(2,1)S(1)}, u32[]{:S(2)}, u32[]{:S(2)}) %collective-permute-start.30) | collective-permute-done | bytes 262176 | tf_op jit(solution)/shard_map/ppermute | solution.py:48
  91.7 1.5 %collective-permute-start.33 = (bf16[128,1024]{1,0:T(8,128)(2,1)S(1)}, bf16[128,1024]{1,0:T(8,128)(2,1)S(1)}, u32[]{:S(2)}, u32[]{:S(2)}) collective-permute-start(bf16[128,1024]{1,0:T(8,128)(2,1)S(1)} %add_convert_fusion.6), channel_id=1, source_target_pairs={{0,2},{1,5},{2,6},{3,1},{6,10},{7,3},{10,14},{11,7},{14,12},{15,11... | collective-permute-start | bytes 786440 | tf_op jit(solution)/shard_map/ppermute | solution.py:48
  93.2 1.2 %collective-permute-done.39 = bf16[128,1024]{1,0:T(8,128)(2,1)S(1)} collective-permute-done((bf16[128,1024]{1,0:T(8,128)(2,1)S(1)}, bf16[128,1024]{1,0:T(8,128)(2,1)S(1)}, u32[]{:S(2)}, u32[]{:S(2)}) %collective-permute-start.39) | collective-permute-done | bytes 262176 | tf_op jit(solution)/shard_map/ppermute | solution.py:48
  94.5 1.5 %collective-permute-start.42 = (bf16[128,1024]{1,0:T(8,128)(2,1)S(1)}, bf16[128,1024]{1,0:T(8,128)(2,1)S(1)}, u32[]{:S(2)}, u32[]{:S(2)}) collective-permute-start(bf16[128,1024]{1,0:T(8,128)(2,1)S(1)} %add_convert_fusion.2), channel_id=1, source_target_pairs={{0,2},{1,5},{2,6},{3,1},{6,10},{7,3},{10,14},{11,7},{14,12},{15,11... | collective-permute-start | bytes 786440 | tf_op jit(solution)/shard_map/ppermute | solution.py:48
  96.0 2.1 %collective-permute-done.33 = bf16[128,1024]{1,0:T(8,128)(2,1)S(1)} collective-permute-done((bf16[128,1024]{1,0:T(8,128)(2,1)S(1)}, bf16[128,1024]{1,0:T(8,128)(2,1)S(1)}, u32[]{:S(2)}, u32[]{:S(2)}) %collective-permute-start.33) | collective-permute-done | bytes 262176 | tf_op jit(solution)/shard_map/ppermute | solution.py:48
  98.2 1.5 %collective-permute-start.34 = (bf16[128,1024]{1,0:T(8,128)(2,1)S(1)}, bf16[128,1024]{1,0:T(8,128)(2,1)S(1)}, u32[]{:S(2)}, u32[]{:S(2)}) collective-permute-start(bf16[128,1024]{1,0:T(8,128)(2,1)S(1)} %add_convert_fusion.5), channel_id=1, source_target_pairs={{0,2},{1,5},{2,6},{3,1},{6,10},{7,3},{10,14},{11,7},{14,12},{15,11... | collective-permute-start | bytes 786440 | tf_op jit(solution)/shard_map/ppermute | solution.py:48
  99.8 1.2 %collective-permute-done.42 = bf16[128,1024]{1,0:T(8,128)(2,1)S(1)} collective-permute-done((bf16[128,1024]{1,0:T(8,128)(2,1)S(1)}, bf16[128,1024]{1,0:T(8,128)(2,1)S(1)}, u32[]{:S(2)}, u32[]{:S(2)}) %collective-permute-start.42) | collective-permute-done | bytes 262176 | tf_op jit(solution)/shard_map/ppermute | solution.py:48
  101.0 0.8 collective-permute-start.43
  101.8 2.8 %collective-permute-done.34 = bf16[128,1024]{1,0:T(8,128)(2,1)S(1)} collective-permute-done((bf16[128,1024]{1,0:T(8,128)(2,1)S(1)}, bf16[128,1024]{1,0:T(8,128)(2,1)S(1)}, u32[]{:S(2)}, u32[]{:S(2)}) %collective-permute-start.34) | collective-permute-done | bytes 262176 | tf_op jit(solution)/shard_map/ppermute | solution.py:48
  104.8 1.5 %collective-permute-start.37 = (bf16[128,1024]{1,0:T(8,128)(2,1)S(1)}, bf16[128,1024]{1,0:T(8,128)(2,1)S(1)}, u32[]{:S(2)}, u32[]{:S(2)}) collective-permute-start(bf16[128,1024]{1,0:T(8,128)(2,1)S(1)} %add_convert_fusion.4), channel_id=1, source_target_pairs={{0,2},{1,5},{2,6},{3,1},{6,10},{7,3},{10,14},{11,7},{14,12},{15,11... | collective-permute-start | bytes 786440 | tf_op jit(solution)/shard_map/ppermute | solution.py:48
  106.9 4.3 %collective-permute-done.37 = bf16[128,1024]{1,0:T(8,128)(2,1)S(1)} collective-permute-done((bf16[128,1024]{1,0:T(8,128)(2,1)S(1)}, bf16[128,1024]{1,0:T(8,128)(2,1)S(1)}, u32[]{:S(2)}, u32[]{:S(2)}) %collective-permute-start.37) | collective-permute-done | bytes 262176 | tf_op jit(solution)/shard_map/ppermute | solution.py:48
  111.2 0.9 add_convert_fusion
  (58 shorter events, 4.8 us)
Async XLA Ops:
  1.1 5.5 %collective-permute-start.1 = (bf16[64,640]{1,0:T(8,128)(2,1)S(1)}, bf16[64,640]{1,0:T(8,128)(2,1)S(1)}, u32[]{:S(2)}, u32[]{:S(2)}) collective-permute-start(bf16[64,640]{1,0:T(8,128)(2,1)S(1)} %get-tuple-element.108.refs_1_), channel_id=1, source_target_pairs={{0,2},{1,5},{2,6},{3,1},{6,10},{7,3},{10,14},{11,7},{14,12},{15,11... | collective-permute-start | bytes 245768 | tf_op jit(solution)/shard_map/ppermute | solution.py:48
  4.2 5.2 %collective-permute-start = (bf16[64,640]{1,0:T(8,128)(2,1)S(1)}, bf16[64,640]{1,0:T(8,128)(2,1)S(1)}, u32[]{:S(2)}, u32[]{:S(2)}) collective-permute-start(bf16[64,640]{1,0:T(8,128)(2,1)S(1)} %get-tuple-element.107.refs_0_), channel_id=1, source_target_pairs={{0,2},{1,5},{2,6},{3,1},{6,10},{7,3},{10,14},{11,7},{14,12},{15,11... | collective-permute-start | bytes 245768 | tf_op jit(solution)/shard_map/ppermute | solution.py:48
  6.7 5.1 %collective-permute-start.5 = (bf16[64,640]{1,0:T(8,128)(2,1)S(1)}, bf16[64,640]{1,0:T(8,128)(2,1)S(1)}, u32[]{:S(2)}, u32[]{:S(2)}) collective-permute-start(bf16[64,640]{1,0:T(8,128)(2,1)S(1)} %collective-permute-done.1.refs_3_), channel_id=1, source_target_pairs={{0,1},{1,0},{2,3},{3,2},{4,5},{5,4},{6,7},{7,6},{8,9},{9,8},{10,11... | collective-permute-start | bytes 245768 | tf_op jit(solution)/shard_map/ppermute | solution.py:39
  6.7 5.1 %collective-permute-start.4 = (bf16[64,640]{1,0:T(8,128)(2,1)S(1)}, bf16[64,640]{1,0:T(8,128)(2,1)S(1)}, u32[]{:S(2)}, u32[]{:S(2)}) collective-permute-start(bf16[64,640]{1,0:T(8,128)(2,1)S(1)} %collective-permute-done.1.refs_3_), channel_id=1, source_target_pairs={{0,2},{1,5},{2,6},{3,1},{6,10},{7,3},{10,14},{11,7},{14,12},{15,11... | collective-permute-start | bytes 245768 | tf_op jit(solution)/shard_map/ppermute | solution.py:48
  9.4 4.1 %collective-permute-start.3 = (bf16[64,640]{1,0:T(8,128)(2,1)S(1)}, bf16[64,640]{1,0:T(8,128)(2,1)S(1)}, u32[]{:S(2)}, u32[]{:S(2)}) collective-permute-start(bf16[64,640]{1,0:T(8,128)(2,1)S(1)} %collective-permute-done.refs_2_), channel_id=1, source_target_pairs={{0,1},{1,0},{2,3},{3,2},{4,5},{5,4},{6,7},{7,6},{8,9},{9,8},{10,11... | collective-permute-start | bytes 245768 | tf_op jit(solution)/shard_map/ppermute | solution.py:39
  9.7 4.4 %collective-permute-start.2 = (bf16[64,640]{1,0:T(8,128)(2,1)S(1)}, bf16[64,640]{1,0:T(8,128)(2,1)S(1)}, u32[]{:S(2)}, u32[]{:S(2)}) collective-permute-start(bf16[64,640]{1,0:T(8,128)(2,1)S(1)} %collective-permute-done.refs_2_), channel_id=1, source_target_pairs={{0,2},{1,5},{2,6},{3,1},{6,10},{7,3},{10,14},{11,7},{14,12},{15,11... | collective-permute-start | bytes 245768 | tf_op jit(solution)/shard_map/ppermute | solution.py:48
  11.7 5.0 %collective-permute-start.9 = (bf16[64,640]{1,0:T(8,128)(2,1)S(1)}, bf16[64,640]{1,0:T(8,128)(2,1)S(1)}, u32[]{:S(2)}, u32[]{:S(2)}) collective-permute-start(bf16[64,640]{1,0:T(8,128)(2,1)S(1)} %collective-permute-done.4.refs_5_), channel_id=1, source_target_pairs={{0,1},{1,0},{2,3},{3,2},{4,5},{5,4},{6,7},{7,6},{8,9},{9,8},{10,11... | collective-permute-start | bytes 245768 | tf_op jit(solution)/shard_map/ppermute | solution.py:39
  11.8 4.9 %collective-permute-start.8 = (bf16[64,640]{1,0:T(8,128)(2,1)S(1)}, bf16[64,640]{1,0:T(8,128)(2,1)S(1)}, u32[]{:S(2)}, u32[]{:S(2)}) collective-permute-start(bf16[64,640]{1,0:T(8,128)(2,1)S(1)} %collective-permute-done.4.refs_5_), channel_id=1, source_target_pairs={{0,2},{1,5},{2,6},{3,1},{6,10},{7,3},{10,14},{11,7},{14,12},{15,11... | collective-permute-start | bytes 245768 | tf_op jit(solution)/shard_map/ppermute | solution.py:48
  14.1 4.3 %collective-permute-start.7 = (bf16[64,640]{1,0:T(8,128)(2,1)S(1)}, bf16[64,640]{1,0:T(8,128)(2,1)S(1)}, u32[]{:S(2)}, u32[]{:S(2)}) collective-permute-start(bf16[64,640]{1,0:T(8,128)(2,1)S(1)} %collective-permute-done.2.refs_4_), channel_id=1, source_target_pairs={{0,1},{1,0},{2,3},{3,2},{4,5},{5,4},{6,7},{7,6},{8,9},{9,8},{10,11... | collective-permute-start | bytes 245768 | tf_op jit(solution)/shard_map/ppermute | solution.py:39
  14.1 4.4 %collective-permute-start.6 = (bf16[64,640]{1,0:T(8,128)(2,1)S(1)}, bf16[64,640]{1,0:T(8,128)(2,1)S(1)}, u32[]{:S(2)}, u32[]{:S(2)}) collective-permute-start(bf16[64,640]{1,0:T(8,128)(2,1)S(1)} %collective-permute-done.2.refs_4_), channel_id=1, source_target_pairs={{0,2},{1,5},{2,6},{3,1},{6,10},{7,3},{10,14},{11,7},{14,12},{15,11... | collective-permute-start | bytes 245768 | tf_op jit(solution)/shard_map/ppermute | solution.py:48
  16.7 3.4 %collective-permute-start.13 = (bf16[64,640]{1,0:T(8,128)(2,1)S(1)}, bf16[64,640]{1,0:T(8,128)(2,1)S(1)}, u32[]{:S(2)}, u32[]{:S(2)}) collective-permute-start(bf16[64,640]{1,0:T(8,128)(2,1)S(1)} %collective-permute-done.8.refs_7_), channel_id=1, source_target_pairs={{0,1},{1,0},{2,3},{3,2},{4,5},{5,4},{6,7},{7,6},{8,9},{9,8},{10,11... | collective-permute-start | bytes 245768 | tf_op jit(solution)/shard_map/ppermute | solution.py:39
  17.3 4.4 %collective-permute-start.12 = (bf16[64,640]{1,0:T(8,128)(2,1)S(1)}, bf16[64,640]{1,0:T(8,128)(2,1)S(1)}, u32[]{:S(2)}, u32[]{:S(2)}) collective-permute-start(bf16[64,640]{1,0:T(8,128)(2,1)S(1)} %collective-permute-done.8.refs_7_), channel_id=1, source_target_pairs={{0,2},{1,5},{2,6},{3,1},{6,10},{7,3},{10,14},{11,7},{14,12},{15,11... | collective-permute-start | bytes 245768 | tf_op jit(solution)/shard_map/ppermute | solution.py:48
  18.6 3.1 %collective-permute-start.11 = (bf16[64,640]{1,0:T(8,128)(2,1)S(1)}, bf16[64,640]{1,0:T(8,128)(2,1)S(1)}, u32[]{:S(2)}, u32[]{:S(2)}) collective-permute-start(bf16[64,640]{1,0:T(8,128)(2,1)S(1)} %collective-permute-done.6.refs_6_), channel_id=1, source_target_pairs={{0,1},{1,0},{2,3},{3,2},{4,5},{5,4},{6,7},{7,6},{8,9},{9,8},{10,11... | collective-permute-start | bytes 245768 | tf_op jit(solution)/shard_map/ppermute | solution.py:39
  18.6 4.4 %collective-permute-start.10 = (bf16[64,640]{1,0:T(8,128)(2,1)S(1)}, bf16[64,640]{1,0:T(8,128)(2,1)S(1)}, u32[]{:S(2)}, u32[]{:S(2)}) collective-permute-start(bf16[64,640]{1,0:T(8,128)(2,1)S(1)} %collective-permute-done.6.refs_6_), channel_id=1, source_target_pairs={{0,2},{1,5},{2,6},{3,1},{6,10},{7,3},{10,14},{11,7},{14,12},{15,11... | collective-permute-start | bytes 245768 | tf_op jit(solution)/shard_map/ppermute | solution.py:48
  28.1 2.0 %collective-permute-start.14 = (bf16[128,2048]{1,0:T(8,128)(2,1)S(1)}, bf16[128,2048]{1,0:T(8,128)(2,1)S(1)}, u32[]{:S(2)}, u32[]{:S(2)}) collective-permute-start(bf16[128,2048]{1,0:T(8,128)(2,1)S(1)} %get-tuple-element.106), channel_id=1, source_target_pairs={{0,1},{1,0},{2,3},{3,2},{4,5},{5,4},{6,7},{7,6},{8,9},{9,8},{10,11... | collective-permute-start | bytes 1572872 | tf_op jit(solution)/shard_map/ppermute | solution.py:39
  31.1 6.4 %collective-permute-start.15 = (bf16[128,1024]{1,0:T(8,128)(2,1)S(1)}, bf16[128,1024]{1,0:T(8,128)(2,1)S(1)}, u32[]{:S(2)}, u32[]{:S(2)}) collective-permute-start(bf16[128,1024]{1,0:T(8,128)(2,1)S(1)} %get-tuple-element.126.refs_0_), channel_id=1, source_target_pairs={{0,2},{1,5},{2,6},{3,1},{6,10},{7,3},{10,14},{11,7},{14,12},{15,11... | collective-permute-start | bytes 786440 | tf_op jit(solution)/shard_map/ppermute | solution.py:48
  32.6 7.7 %collective-permute-start.16 = (bf16[128,1024]{1,0:T(8,128)(2,1)S(1)}, bf16[128,1024]{1,0:T(8,128)(2,1)S(1)}, u32[]{:S(2)}, u32[]{:S(2)}) collective-permute-start(bf16[128,1024]{1,0:T(8,128)(2,1)S(1)} %get-tuple-element.127.refs_1_), channel_id=1, source_target_pairs={{0,2},{1,5},{2,6},{3,1},{6,10},{7,3},{10,14},{11,7},{14,12},{15,11... | collective-permute-start | bytes 786440 | tf_op jit(solution)/shard_map/ppermute | solution.py:48
  37.5 4.3 %collective-permute-start.18 = (bf16[128,1024]{1,0:T(8,128)(2,1)S(1)}, bf16[128,1024]{1,0:T(8,128)(2,1)S(1)}, u32[]{:S(2)}, u32[]{:S(2)}) collective-permute-start(bf16[128,1024]{1,0:T(8,128)(2,1)S(1)} %collective-permute-done.15.refs_2_), channel_id=1, source_target_pairs={{0,1},{1,0},{2,3},{3,2},{4,5},{5,4},{6,7},{7,6},{8,9},{9,8},{10,11... | collective-permute-start | bytes 786440 | tf_op jit(solution)/shard_map/ppermute | solution.py:39
  37.5 6.4 %collective-permute-start.17 = (bf16[128,1024]{1,0:T(8,128)(2,1)S(1)}, bf16[128,1024]{1,0:T(8,128)(2,1)S(1)}, u32[]{:S(2)}, u32[]{:S(2)}) collective-permute-start(bf16[128,1024]{1,0:T(8,128)(2,1)S(1)} %collective-permute-done.15.refs_2_), channel_id=1, source_target_pairs={{0,2},{1,5},{2,6},{3,1},{6,10},{7,3},{10,14},{11,7},{14,12},{15,11... | collective-permute-start | bytes 786440 | tf_op jit(solution)/shard_map/ppermute | solution.py:48
  40.3 5.0 %collective-permute-start.20 = (bf16[128,1024]{1,0:T(8,128)(2,1)S(1)}, bf16[128,1024]{1,0:T(8,128)(2,1)S(1)}, u32[]{:S(2)}, u32[]{:S(2)}) collective-permute-start(bf16[128,1024]{1,0:T(8,128)(2,1)S(1)} %collective-permute-done.16.refs_3_), channel_id=1, source_target_pairs={{0,1},{1,0},{2,3},{3,2},{4,5},{5,4},{6,7},{7,6},{8,9},{9,8},{10,11... | collective-permute-start | bytes 786440 | tf_op jit(solution)/shard_map/ppermute | solution.py:39
  40.3 6.4 %collective-permute-start.19 = (bf16[128,1024]{1,0:T(8,128)(2,1)S(1)}, bf16[128,1024]{1,0:T(8,128)(2,1)S(1)}, u32[]{:S(2)}, u32[]{:S(2)}) collective-permute-start(bf16[128,1024]{1,0:T(8,128)(2,1)S(1)} %collective-permute-done.16.refs_3_), channel_id=1, source_target_pairs={{0,2},{1,5},{2,6},{3,1},{6,10},{7,3},{10,14},{11,7},{14,12},{15,11... | collective-permute-start | bytes 786440 | tf_op jit(solution)/shard_map/ppermute | solution.py:48
  43.9 4.3 %collective-permute-start.22 = (bf16[128,1024]{1,0:T(8,128)(2,1)S(1)}, bf16[128,1024]{1,0:T(8,128)(2,1)S(1)}, u32[]{:S(2)}, u32[]{:S(2)}) collective-permute-start(bf16[128,1024]{1,0:T(8,128)(2,1)S(1)} %collective-permute-done.17.refs_4_), channel_id=1, source_target_pairs={{0,1},{1,0},{2,3},{3,2},{4,5},{5,4},{6,7},{7,6},{8,9},{9,8},{10,11... | collective-permute-start | bytes 786440 | tf_op jit(solution)/shard_map/ppermute | solution.py:39
  43.9 6.4 %collective-permute-start.21 = (bf16[128,1024]{1,0:T(8,128)(2,1)S(1)}, bf16[128,1024]{1,0:T(8,128)(2,1)S(1)}, u32[]{:S(2)}, u32[]{:S(2)}) collective-permute-start(bf16[128,1024]{1,0:T(8,128)(2,1)S(1)} %collective-permute-done.17.refs_4_), channel_id=1, source_target_pairs={{0,2},{1,5},{2,6},{3,1},{6,10},{7,3},{10,14},{11,7},{14,12},{15,11... | collective-permute-start | bytes 786440 | tf_op jit(solution)/shard_map/ppermute | solution.py:48
  46.7 5.0 %collective-permute-start.24 = (bf16[128,1024]{1,0:T(8,128)(2,1)S(1)}, bf16[128,1024]{1,0:T(8,128)(2,1)S(1)}, u32[]{:S(2)}, u32[]{:S(2)}) collective-permute-start(bf16[128,1024]{1,0:T(8,128)(2,1)S(1)} %collective-permute-done.19.refs_5_), channel_id=1, source_target_pairs={{0,1},{1,0},{2,3},{3,2},{4,5},{5,4},{6,7},{7,6},{8,9},{9,8},{10,11... | collective-permute-start | bytes 786440 | tf_op jit(solution)/shard_map/ppermute | solution.py:39
  46.7 6.4 %collective-permute-start.23 = (bf16[128,1024]{1,0:T(8,128)(2,1)S(1)}, bf16[128,1024]{1,0:T(8,128)(2,1)S(1)}, u32[]{:S(2)}, u32[]{:S(2)}) collective-permute-start(bf16[128,1024]{1,0:T(8,128)(2,1)S(1)} %collective-permute-done.19.refs_5_), channel_id=1, source_target_pairs={{0,2},{1,5},{2,6},{3,1},{6,10},{7,3},{10,14},{11,7},{14,12},{15,11... | collective-permute-start | bytes 786440 | tf_op jit(solution)/shard_map/ppermute | solution.py:48
  50.3 2.8 %collective-permute-start.26 = (bf16[128,1024]{1,0:T(8,128)(2,1)S(1)}, bf16[128,1024]{1,0:T(8,128)(2,1)S(1)}, u32[]{:S(2)}, u32[]{:S(2)}) collective-permute-start(bf16[128,1024]{1,0:T(8,128)(2,1)S(1)} %collective-permute-done.21.refs_6_), channel_id=1, source_target_pairs={{0,1},{1,0},{2,3},{3,2},{4,5},{5,4},{6,7},{7,6},{8,9},{9,8},{10,11... | collective-permute-start | bytes 786440 | tf_op jit(solution)/shard_map/ppermute | solution.py:39
  50.3 6.4 %collective-permute-start.25 = (bf16[128,1024]{1,0:T(8,128)(2,1)S(1)}, bf16[128,1024]{1,0:T(8,128)(2,1)S(1)}, u32[]{:S(2)}, u32[]{:S(2)}) collective-permute-start(bf16[128,1024]{1,0:T(8,128)(2,1)S(1)} %collective-permute-done.21.refs_6_), channel_id=1, source_target_pairs={{0,2},{1,5},{2,6},{3,1},{6,10},{7,3},{10,14},{11,7},{14,12},{15,11... | collective-permute-start | bytes 786440 | tf_op jit(solution)/shard_map/ppermute | solution.py:48
  53.1 3.6 %collective-permute-start.28 = (bf16[128,1024]{1,0:T(8,128)(2,1)S(1)}, bf16[128,1024]{1,0:T(8,128)(2,1)S(1)}, u32[]{:S(2)}, u32[]{:S(2)}) collective-permute-start(bf16[128,1024]{1,0:T(8,128)(2,1)S(1)} %collective-permute-done.23.refs_7_), channel_id=1, source_target_pairs={{0,1},{1,0},{2,3},{3,2},{4,5},{5,4},{6,7},{7,6},{8,9},{9,8},{10,11... | collective-permute-start | bytes 786440 | tf_op jit(solution)/shard_map/ppermute | solution.py:39
  56.6 1.5 %collective-permute-start.27 = (bf16[128,1024]{1,0:T(8,128)(2,1)S(1)}, bf16[128,1024]{1,0:T(8,128)(2,1)S(1)}, u32[]{:S(2)}, u32[]{:S(2)}) collective-permute-start(bf16[128,1024]{1,0:T(8,128)(2,1)S(1)} %collective-permute-done.25.refs_8_), channel_id=1, source_target_pairs={{0,1},{1,0},{2,3},{3,2},{4,5},{5,4},{6,7},{7,6},{8,9},{9,8},{10,11... | collective-permute-start | bytes 786440 | tf_op jit(solution)/shard_map/ppermute | solution.py:39
  83.4 1.6 %collective-permute-start.29 = (bf16[128,1024]{1,0:T(8,128)(2,1)S(1)}, bf16[128,1024]{1,0:T(8,128)(2,1)S(1)}, u32[]{:S(2)}, u32[]{:S(2)}) collective-permute-start(bf16[128,1024]{1,0:T(8,128)(2,1)S(1)} %get-tuple-element.142), channel_id=1, source_target_pairs={{0,1},{1,0},{2,3},{3,2},{4,5},{5,4},{6,7},{7,6},{8,9},{9,8},{10,11... | collective-permute-start | bytes 786440 | tf_op jit(solution)/shard_map/ppermute | solution.py:39
  83.6 3.0 %collective-permute-start.38 = (bf16[128,1024]{1,0:T(8,128)(2,1)S(1)}, bf16[128,1024]{1,0:T(8,128)(2,1)S(1)}, u32[]{:S(2)}, u32[]{:S(2)}) collective-permute-start(bf16[128,1024]{1,0:T(8,128)(2,1)S(1)} %get-tuple-element.157), channel_id=1, source_target_pairs={{0,1},{1,0},{2,3},{3,2},{4,5},{5,4},{6,7},{7,6},{8,9},{9,8},{10,11... | collective-permute-start | bytes 786440 | tf_op jit(solution)/shard_map/ppermute | solution.py:39
  85.1 6.4 %collective-permute-start.30 = (bf16[128,1024]{1,0:T(8,128)(2,1)S(1)}, bf16[128,1024]{1,0:T(8,128)(2,1)S(1)}, u32[]{:S(2)}, u32[]{:S(2)}) collective-permute-start(bf16[128,1024]{1,0:T(8,128)(2,1)S(1)} %add_convert_fusion.7), channel_id=1, source_target_pairs={{0,2},{1,5},{2,6},{3,1},{6,10},{7,3},{10,14},{11,7},{14,12},{15,11... | collective-permute-start | bytes 786440 | tf_op jit(solution)/shard_map/ppermute | solution.py:48
  86.6 4.9 %collective-permute-start.32 = (bf16[128,1024]{1,0:T(8,128)(2,1)S(1)}, bf16[128,1024]{1,0:T(8,128)(2,1)S(1)}, u32[]{:S(2)}, u32[]{:S(2)}) collective-permute-start(bf16[128,1024]{1,0:T(8,128)(2,1)S(1)} %get-tuple-element.146), channel_id=1, source_target_pairs={{0,1},{1,0},{2,3},{3,2},{4,5},{5,4},{6,7},{7,6},{8,9},{9,8},{10,11... | collective-permute-start | bytes 786440 | tf_op jit(solution)/shard_map/ppermute | solution.py:39
  86.7 7.6 %collective-permute-start.39 = (bf16[128,1024]{1,0:T(8,128)(2,1)S(1)}, bf16[128,1024]{1,0:T(8,128)(2,1)S(1)}, u32[]{:S(2)}, u32[]{:S(2)}) collective-permute-start(bf16[128,1024]{1,0:T(8,128)(2,1)S(1)} %add_convert_fusion.3), channel_id=1, source_target_pairs={{0,2},{1,5},{2,6},{3,1},{6,10},{7,3},{10,14},{11,7},{14,12},{15,11... | collective-permute-start | bytes 786440 | tf_op jit(solution)/shard_map/ppermute | solution.py:48
  88.2 6.2 %collective-permute-start.41 = (bf16[128,1024]{1,0:T(8,128)(2,1)S(1)}, bf16[128,1024]{1,0:T(8,128)(2,1)S(1)}, u32[]{:S(2)}, u32[]{:S(2)}) collective-permute-start(bf16[128,1024]{1,0:T(8,128)(2,1)S(1)} %get-tuple-element.161), channel_id=1, source_target_pairs={{0,1},{1,0},{2,3},{3,2},{4,5},{5,4},{6,7},{7,6},{8,9},{9,8},{10,11... | collective-permute-start | bytes 786440 | tf_op jit(solution)/shard_map/ppermute | solution.py:39
  91.7 6.4 %collective-permute-start.33 = (bf16[128,1024]{1,0:T(8,128)(2,1)S(1)}, bf16[128,1024]{1,0:T(8,128)(2,1)S(1)}, u32[]{:S(2)}, u32[]{:S(2)}) collective-permute-start(bf16[128,1024]{1,0:T(8,128)(2,1)S(1)} %add_convert_fusion.6), channel_id=1, source_target_pairs={{0,2},{1,5},{2,6},{3,1},{6,10},{7,3},{10,14},{11,7},{14,12},{15,11... | collective-permute-start | bytes 786440 | tf_op jit(solution)/shard_map/ppermute | solution.py:48
  93.2 4.9 %collective-permute-start.31 = (bf16[128,1024]{1,0:T(8,128)(2,1)S(1)}, bf16[128,1024]{1,0:T(8,128)(2,1)S(1)}, u32[]{:S(2)}, u32[]{:S(2)}) collective-permute-start(bf16[128,1024]{1,0:T(8,128)(2,1)S(1)} %get-tuple-element.144), channel_id=1, source_target_pairs={{0,1},{1,0},{2,3},{3,2},{4,5},{5,4},{6,7},{7,6},{8,9},{9,8},{10,11... | collective-permute-start | bytes 786440 | tf_op jit(solution)/shard_map/ppermute | solution.py:39
  94.4 6.6 %collective-permute-start.40 = (bf16[128,1024]{1,0:T(8,128)(2,1)S(1)}, bf16[128,1024]{1,0:T(8,128)(2,1)S(1)}, u32[]{:S(2)}, u32[]{:S(2)}) collective-permute-start(bf16[128,1024]{1,0:T(8,128)(2,1)S(1)} %get-tuple-element.159), channel_id=1, source_target_pairs={{0,1},{1,0},{2,3},{3,2},{4,5},{5,4},{6,7},{7,6},{8,9},{9,8},{10,11... | collective-permute-start | bytes 786440 | tf_op jit(solution)/shard_map/ppermute | solution.py:39
  94.5 6.4 %collective-permute-start.42 = (bf16[128,1024]{1,0:T(8,128)(2,1)S(1)}, bf16[128,1024]{1,0:T(8,128)(2,1)S(1)}, u32[]{:S(2)}, u32[]{:S(2)}) collective-permute-start(bf16[128,1024]{1,0:T(8,128)(2,1)S(1)} %add_convert_fusion.2), channel_id=1, source_target_pairs={{0,2},{1,5},{2,6},{3,1},{6,10},{7,3},{10,14},{11,7},{14,12},{15,11... | collective-permute-start | bytes 786440 | tf_op jit(solution)/shard_map/ppermute | solution.py:48
  98.2 6.4 %collective-permute-start.34 = (bf16[128,1024]{1,0:T(8,128)(2,1)S(1)}, bf16[128,1024]{1,0:T(8,128)(2,1)S(1)}, u32[]{:S(2)}, u32[]{:S(2)}) collective-permute-start(bf16[128,1024]{1,0:T(8,128)(2,1)S(1)} %add_convert_fusion.5), channel_id=1, source_target_pairs={{0,2},{1,5},{2,6},{3,1},{6,10},{7,3},{10,14},{11,7},{14,12},{15,11... | collective-permute-start | bytes 786440 | tf_op jit(solution)/shard_map/ppermute | solution.py:48
  99.8 4.9 %collective-permute-start.36 = (bf16[128,1024]{1,0:T(8,128)(2,1)S(1)}, bf16[128,1024]{1,0:T(8,128)(2,1)S(1)}, u32[]{:S(2)}, u32[]{:S(2)}) collective-permute-start(bf16[128,1024]{1,0:T(8,128)(2,1)S(1)} %get-tuple-element.153), channel_id=1, source_target_pairs={{0,1},{1,0},{2,3},{3,2},{4,5},{5,4},{6,7},{7,6},{8,9},{9,8},{10,11... | collective-permute-start | bytes 786440 | tf_op jit(solution)/shard_map/ppermute | solution.py:39
  101.0 5.9 %collective-permute-start.43 = (bf16[128,1024]{1,0:T(8,128)(2,1)S(1)}, bf16[128,1024]{1,0:T(8,128)(2,1)S(1)}, u32[]{:S(2)}, u32[]{:S(2)}) collective-permute-start(bf16[128,1024]{1,0:T(8,128)(2,1)S(1)} %add_convert_fusion.1), channel_id=1, source_target_pairs={{0,3},{1,4},{2,7},{3,0},{6,11},{7,2},{10,15},{11,6},{14,13},{15,10... | collective-permute-start | bytes 786440 | tf_op jit(solution)/shard_map/ppermute | solution.py:48
  104.7 2.3 %collective-permute-start.35 = (bf16[128,1024]{1,0:T(8,128)(2,1)S(1)}, bf16[128,1024]{1,0:T(8,128)(2,1)S(1)}, u32[]{:S(2)}, u32[]{:S(2)}) collective-permute-start(bf16[128,1024]{1,0:T(8,128)(2,1)S(1)} %get-tuple-element.151), channel_id=1, source_target_pairs={{0,1},{1,0},{2,3},{3,2},{4,5},{5,4},{6,7},{7,6},{8,9},{9,8},{10,11... | collective-permute-start | bytes 786440 | tf_op jit(solution)/shard_map/ppermute | solution.py:39
  104.8 6.4 %collective-permute-start.37 = (bf16[128,1024]{1,0:T(8,128)(2,1)S(1)}, bf16[128,1024]{1,0:T(8,128)(2,1)S(1)}, u32[]{:S(2)}, u32[]{:S(2)}) collective-permute-start(bf16[128,1024]{1,0:T(8,128)(2,1)S(1)} %add_convert_fusion.4), channel_id=1, source_target_pairs={{0,2},{1,5},{2,6},{3,1},{6,10},{7,3},{10,14},{11,7},{14,12},{15,11... | collective-permute-start | bytes 786440 | tf_op jit(solution)/shard_map/ppermute | solution.py:48

commit v18 on v17

--- a/solution.py
+++ b/solution.py
@@ -20,7 +20,7 @@
 MIB = 1024 * 1024
 VMEM_LIMIT = 50 * MIB
 HELD = 7
-PIECES = 4
+PIECES = 2
 SWAP = [(0, 1), (1, 0)]
 FEW = 8
 

time: 112 us -> 112 us (level)
  no operation moved by 1% of the time
where the time goes in v18:
time: 112 us
  waiting for transfers between devices  37.3 us (33%)
  Pallas kernels  35.3 us (32%)
  starting transfers between devices  35.3 us (32%)
  local copies, waits for them, and re-layouts  2.13 us (2%)
  other arithmetic  1.75 us (2%)
    ppermute x22, waiting for transfers between devices, turn(): return lax.ppermute(value, ('ctx', 'exp'), pairs)  34.7 us
    ppermute x22, starting transfers between devices, turn(): return lax.ppermute(value, ('ctx', 'exp'), pairs)  33.7 us
    pallas_call x1, Pallas kernels, experts_fused(): pl.pallas_call(functools.partial(fused_kernel, count), in_specs=[pl.Block...  25.1 us
    pallas_call x1, Pallas kernels, attend(): pl.pallas_call(functools.partial(attend_kernel, count, blocks, heads), gr...  5.06 us
    ppermute x22, waiting for transfers between devices, swap(): return lax.ppermute(value, 'exp', SWAP)  2.61 us
  transfers between devices with their start and end apart: 44, of which 21 were waited for; matrix products, arithmetic and copies ran while one was open for 3% of the time, Pallas kernels for 3%

profile of v18, /device:TPU:0, one launch (start us, length us, event | category | flops | bytes accessed | tf_op | source)
XLA Modules:
  0.0 112.0 jit_solution(16919669570652333856)
XLA Ops:
  0.0 1.1 %pack.1 = (bf16[64,640]{1,0:T(8,128)(2,1)S(1)}, bf16[64,640]{1,0:T(8,128)(2,1)S(1)}) custom-call(bf16[576,128]{1,0:T(8,128)(2,1)} %bitcast.11, s32[6,128]{1,0:T(8,128)} %bitcast.12, f32[6,128]{1,0:T(8,128)} %bitcast.13), custom_call_target="tpu_custom_call" | custom-call | tf_op jit(solution)/shard_map/pack/pallas_call | solution.py:339
  1.1 3.0 %collective-permute-start.1 = (bf16[64,640]{1,0:T(8,128)(2,1)S(1)}, bf16[64,640]{1,0:T(8,128)(2,1)S(1)}, u32[]{:S(2)}, u32[]{:S(2)}) collective-permute-start(bf16[64,640]{1,0:T(8,128)(2,1)S(1)} %get-tuple-element.108.refs_1_), channel_id=1, source_target_pairs={{0,2},{1,5},{2,6},{3,1},{6,10},{7,3},{10,14},{11,7},{14,12},{15,11... | collective-permute-start | bytes 245768 | tf_op jit(solution)/shard_map/ppermute | solution.py:48
  4.2 1.6 %collective-permute-start = (bf16[64,640]{1,0:T(8,128)(2,1)S(1)}, bf16[64,640]{1,0:T(8,128)(2,1)S(1)}, u32[]{:S(2)}, u32[]{:S(2)}) collective-permute-start(bf16[64,640]{1,0:T(8,128)(2,1)S(1)} %get-tuple-element.107.refs_0_), channel_id=1, source_target_pairs={{0,2},{1,5},{2,6},{3,1},{6,10},{7,3},{10,14},{11,7},{14,12},{15,11... | collective-permute-start | bytes 245768 | tf_op jit(solution)/shard_map/ppermute | solution.py:48
  6.7 2.0 %collective-permute-start.4 = (bf16[64,640]{1,0:T(8,128)(2,1)S(1)}, bf16[64,640]{1,0:T(8,128)(2,1)S(1)}, u32[]{:S(2)}, u32[]{:S(2)}) collective-permute-start(bf16[64,640]{1,0:T(8,128)(2,1)S(1)} %collective-permute-done.1.refs_3_), channel_id=1, source_target_pairs={{0,2},{1,5},{2,6},{3,1},{6,10},{7,3},{10,14},{11,7},{14,12},{15,11... | collective-permute-start | bytes 245768 | tf_op jit(solution)/shard_map/ppermute | solution.py:48
  8.6 0.7 concatenate.4.info
  9.7 1.4 %collective-permute-start.2 = (bf16[64,640]{1,0:T(8,128)(2,1)S(1)}, bf16[64,640]{1,0:T(8,128)(2,1)S(1)}, u32[]{:S(2)}, u32[]{:S(2)}) collective-permute-start(bf16[64,640]{1,0:T(8,128)(2,1)S(1)} %collective-permute-done.refs_2_), channel_id=1, source_target_pairs={{0,2},{1,5},{2,6},{3,1},{6,10},{7,3},{10,14},{11,7},{14,12},{15,11... | collective-permute-start | bytes 245768 | tf_op jit(solution)/shard_map/ppermute | solution.py:48
  11.0 0.7 reshape.3.gain_ref
  11.8 1.6 %collective-permute-start.8 = (bf16[64,640]{1,0:T(8,128)(2,1)S(1)}, bf16[64,640]{1,0:T(8,128)(2,1)S(1)}, u32[]{:S(2)}, u32[]{:S(2)}) collective-permute-start(bf16[64,640]{1,0:T(8,128)(2,1)S(1)} %collective-permute-done.4.refs_5_), channel_id=1, source_target_pairs={{0,2},{1,5},{2,6},{3,1},{6,10},{7,3},{10,14},{11,7},{14,12},{15,11... | collective-permute-start | bytes 245768 | tf_op jit(solution)/shard_map/ppermute | solution.py:48
  14.1 1.4 %collective-permute-start.6 = (bf16[64,640]{1,0:T(8,128)(2,1)S(1)}, bf16[64,640]{1,0:T(8,128)(2,1)S(1)}, u32[]{:S(2)}, u32[]{:S(2)}) collective-permute-start(bf16[64,640]{1,0:T(8,128)(2,1)S(1)} %collective-permute-done.2.refs_4_), channel_id=1, source_target_pairs={{0,2},{1,5},{2,6},{3,1},{6,10},{7,3},{10,14},{11,7},{14,12},{15,11... | collective-permute-start | bytes 245768 | tf_op jit(solution)/shard_map/ppermute | solution.py:48
  15.5 1.2 %stage.1.refs_16_ = bf16[512,1024]{1,0:T(8,128)(2,1)S(1)} custom-call(bf16[512,1024]{1,0:T(8,128)(2,1)} %source), custom_call_target="tpu_custom_call" | custom-call | tf_op jit(solution)/shard_map/stage/pallas_call | solution.py:247
  17.3 1.2 %collective-permute-start.12 = (bf16[64,640]{1,0:T(8,128)(2,1)S(1)}, bf16[64,640]{1,0:T(8,128)(2,1)S(1)}, u32[]{:S(2)}, u32[]{:S(2)}) collective-permute-start(bf16[64,640]{1,0:T(8,128)(2,1)S(1)} %collective-permute-done.8.refs_7_), channel_id=1, source_target_pairs={{0,2},{1,5},{2,6},{3,1},{6,10},{7,3},{10,14},{11,7},{14,12},{15,11... | collective-permute-start | bytes 245768 | tf_op jit(solution)/shard_map/ppermute | solution.py:48
  18.6 1.5 %collective-permute-start.10 = (bf16[64,640]{1,0:T(8,128)(2,1)S(1)}, bf16[64,640]{1,0:T(8,128)(2,1)S(1)}, u32[]{:S(2)}, u32[]{:S(2)}) collective-permute-start(bf16[64,640]{1,0:T(8,128)(2,1)S(1)} %collective-permute-done.6.refs_6_), channel_id=1, source_target_pairs={{0,2},{1,5},{2,6},{3,1},{6,10},{7,3},{10,14},{11,7},{14,12},{15,11... | collective-permute-start | bytes 245768 | tf_op jit(solution)/shard_map/ppermute | solution.py:48
  20.1 1.6 %collective-permute-done.12.refs_9_ = bf16[64,640]{1,0:T(8,128)(2,1)S(1)} collective-permute-done((bf16[64,640]{1,0:T(8,128)(2,1)S(1)}, bf16[64,640]{1,0:T(8,128)(2,1)S(1)}, u32[]{:S(2)}, u32[]{:S(2)}) %collective-permute-start.12) | collective-permute-done | bytes 81952 | tf_op jit(solution)/shard_map/ppermute | solution.py:48
  21.7 1.4 %collective-permute-done.10.refs_8_ = bf16[64,640]{1,0:T(8,128)(2,1)S(1)} collective-permute-done((bf16[64,640]{1,0:T(8,128)(2,1)S(1)}, bf16[64,640]{1,0:T(8,128)(2,1)S(1)}, u32[]{:S(2)}, u32[]{:S(2)}) %collective-permute-start.10) | collective-permute-done | bytes 81952 | tf_op jit(solution)/shard_map/ppermute | solution.py:48
  23.1 5.1 %attend.1 = (bf16[128,2048]{1,0:T(8,128)(2,1)S(1)}, f32[128,2048]{1,0:T(8,128)S(1)}) custom-call(s32[42]{0:T(128)S(1)} %concatenate.4.info, bf16[64,640]{1,0:T(8,128)(2,1)S(1)} %get-tuple-element.107.refs_0_, bf16[64,640]{1,0:T(8,128)(2,1)S(1)} %get-tuple-element.108.refs_1_, bf16[64,640]{1,0:T(8,128)(2,1)S(1)} %collective-permute-done.refs_2_, ...), custom_call_target="tpu_custom_call" | custom-call | tf_op jit(solution)/shard_map/attend/pallas_call | solution.py:219
  28.3 1.8 %route.1.refs_16_ = bf16[8,128,128]{2,1,0:T(8,128)(2,1)S(1)} custom-call(s32[2]{0:T(128)S(1)} %pad_add_fusion.where, bf16[64,640]{1,0:T(8,128)(2,1)S(1)} %get-tuple-element.107.refs_0_, bf16[64,640]{1,0:T(8,128)(2,1)S(1)} %get-tuple-element.108.refs_1_, bf16[64,640]{1,0:T(8,128)(2,1)S(1)} %collective-permute-done.refs_2_, ...), custom_call_target="tpu_custom_call" | custom-call | tf_op jit(solution)/shard_map/route/pallas_call | solution.py:281
  30.2 0.9 norm.1
  31.1 1.5 %collective-permute-start.15 = (bf16[128,1024]{1,0:T(8,128)(2,1)S(1)}, bf16[128,1024]{1,0:T(8,128)(2,1)S(1)}, u32[]{:S(2)}, u32[]{:S(2)}) collective-permute-start(bf16[128,1024]{1,0:T(8,128)(2,1)S(1)} %get-tuple-element.126.refs_0_), channel_id=1, source_target_pairs={{0,2},{1,5},{2,6},{3,1},{6,10},{7,3},{10,14},{11,7},{14,12},{15,11... | collective-permute-start | bytes 786440 | tf_op jit(solution)/shard_map/ppermute | solution.py:48
  32.6 1.4 %collective-permute-start.16 = (bf16[128,1024]{1,0:T(8,128)(2,1)S(1)}, bf16[128,1024]{1,0:T(8,128)(2,1)S(1)}, u32[]{:S(2)}, u32[]{:S(2)}) collective-permute-start(bf16[128,1024]{1,0:T(8,128)(2,1)S(1)} %get-tuple-element.127.refs_1_), channel_id=1, source_target_pairs={{0,2},{1,5},{2,6},{3,1},{6,10},{7,3},{10,14},{11,7},{14,12},{15,11... | collective-permute-start | bytes 786440 | tf_op jit(solution)/shard_map/ppermute | solution.py:48
  34.0 3.5 %collective-permute-done.15.refs_2_ = bf16[128,1024]{1,0:T(8,128)(2,1)S(1)} collective-permute-done((bf16[128,1024]{1,0:T(8,128)(2,1)S(1)}, bf16[128,1024]{1,0:T(8,128)(2,1)S(1)}, u32[]{:S(2)}, u32[]{:S(2)}) %collective-permute-start.15) | collective-permute-done | bytes 262176 | tf_op jit(solution)/shard_map/ppermute | solution.py:48
  37.5 1.5 %collective-permute-start.17 = (bf16[128,1024]{1,0:T(8,128)(2,1)S(1)}, bf16[128,1024]{1,0:T(8,128)(2,1)S(1)}, u32[]{:S(2)}, u32[]{:S(2)}) collective-permute-start(bf16[128,1024]{1,0:T(8,128)(2,1)S(1)} %collective-permute-done.15.refs_2_), channel_id=1, source_target_pairs={{0,2},{1,5},{2,6},{3,1},{6,10},{7,3},{10,14},{11,7},{14,12},{15,11... | collective-permute-start | bytes 786440 | tf_op jit(solution)/shard_map/ppermute | solution.py:48
  39.0 1.3 %collective-permute-done.16.refs_3_ = bf16[128,1024]{1,0:T(8,128)(2,1)S(1)} collective-permute-done((bf16[128,1024]{1,0:T(8,128)(2,1)S(1)}, bf16[128,1024]{1,0:T(8,128)(2,1)S(1)}, u32[]{:S(2)}, u32[]{:S(2)}) %collective-permute-start.16) | collective-permute-done | bytes 262176 | tf_op jit(solution)/shard_map/ppermute | solution.py:48
  40.3 1.5 %collective-permute-start.19 = (bf16[128,1024]{1,0:T(8,128)(2,1)S(1)}, bf16[128,1024]{1,0:T(8,128)(2,1)S(1)}, u32[]{:S(2)}, u32[]{:S(2)}) collective-permute-start(bf16[128,1024]{1,0:T(8,128)(2,1)S(1)} %collective-permute-done.16.refs_3_), channel_id=1, source_target_pairs={{0,2},{1,5},{2,6},{3,1},{6,10},{7,3},{10,14},{11,7},{14,12},{15,11... | collective-permute-start | bytes 786440 | tf_op jit(solution)/shard_map/ppermute | solution.py:48
  41.8 2.1 %collective-permute-done.17.refs_4_ = bf16[128,1024]{1,0:T(8,128)(2,1)S(1)} collective-permute-done((bf16[128,1024]{1,0:T(8,128)(2,1)S(1)}, bf16[128,1024]{1,0:T(8,128)(2,1)S(1)}, u32[]{:S(2)}, u32[]{:S(2)}) %collective-permute-start.17) | collective-permute-done | bytes 262176 | tf_op jit(solution)/shard_map/ppermute | solution.py:48
  43.9 1.5 %collective-permute-start.21 = (bf16[128,1024]{1,0:T(8,128)(2,1)S(1)}, bf16[128,1024]{1,0:T(8,128)(2,1)S(1)}, u32[]{:S(2)}, u32[]{:S(2)}) collective-permute-start(bf16[128,1024]{1,0:T(8,128)(2,1)S(1)} %collective-permute-done.17.refs_4_), channel_id=1, source_target_pairs={{0,2},{1,5},{2,6},{3,1},{6,10},{7,3},{10,14},{11,7},{14,12},{15,11... | collective-permute-start | bytes 786440 | tf_op jit(solution)/shard_map/ppermute | solution.py:48
  45.4 1.3 %collective-permute-done.19.refs_5_ = bf16[128,1024]{1,0:T(8,128)(2,1)S(1)} collective-permute-done((bf16[128,1024]{1,0:T(8,128)(2,1)S(1)}, bf16[128,1024]{1,0:T(8,128)(2,1)S(1)}, u32[]{:S(2)}, u32[]{:S(2)}) %collective-permute-start.19) | collective-permute-done | bytes 262176 | tf_op jit(solution)/shard_map/ppermute | solution.py:48
  46.7 1.5 %collective-permute-start.23 = (bf16[128,1024]{1,0:T(8,128)(2,1)S(1)}, bf16[128,1024]{1,0:T(8,128)(2,1)S(1)}, u32[]{:S(2)}, u32[]{:S(2)}) collective-permute-start(bf16[128,1024]{1,0:T(8,128)(2,1)S(1)} %collective-permute-done.19.refs_5_), channel_id=1, source_target_pairs={{0,2},{1,5},{2,6},{3,1},{6,10},{7,3},{10,14},{11,7},{14,12},{15,11... | collective-permute-start | bytes 786440 | tf_op jit(solution)/shard_map/ppermute | solution.py:48
  48.2 2.1 %collective-permute-done.21.refs_6_ = bf16[128,1024]{1,0:T(8,128)(2,1)S(1)} collective-permute-done((bf16[128,1024]{1,0:T(8,128)(2,1)S(1)}, bf16[128,1024]{1,0:T(8,128)(2,1)S(1)}, u32[]{:S(2)}, u32[]{:S(2)}) %collective-permute-start.21) | collective-permute-done | bytes 262176 | tf_op jit(solution)/shard_map/ppermute | solution.py:48
  50.3 1.5 %collective-permute-start.25 = (bf16[128,1024]{1,0:T(8,128)(2,1)S(1)}, bf16[128,1024]{1,0:T(8,128)(2,1)S(1)}, u32[]{:S(2)}, u32[]{:S(2)}) collective-permute-start(bf16[128,1024]{1,0:T(8,128)(2,1)S(1)} %collective-permute-done.21.refs_6_), channel_id=1, source_target_pairs={{0,2},{1,5},{2,6},{3,1},{6,10},{7,3},{10,14},{11,7},{14,12},{15,11... | collective-permute-start | bytes 786440 | tf_op jit(solution)/shard_map/ppermute | solution.py:48
  51.7 1.3 %collective-permute-done.23.refs_7_ = bf16[128,1024]{1,0:T(8,128)(2,1)S(1)} collective-permute-done((bf16[128,1024]{1,0:T(8,128)(2,1)S(1)}, bf16[128,1024]{1,0:T(8,128)(2,1)S(1)}, u32[]{:S(2)}, u32[]{:S(2)}) %collective-permute-start.23) | collective-permute-done | bytes 262176 | tf_op jit(solution)/shard_map/ppermute | solution.py:48
  53.1 3.6 %collective-permute-done.25.refs_8_ = bf16[128,1024]{1,0:T(8,128)(2,1)S(1)} collective-permute-done((bf16[128,1024]{1,0:T(8,128)(2,1)S(1)}, bf16[128,1024]{1,0:T(8,128)(2,1)S(1)}, u32[]{:S(2)}, u32[]{:S(2)}) %collective-permute-start.25) | collective-permute-done | bytes 262176 | tf_op jit(solution)/shard_map/ppermute | solution.py:48
  56.6 1.5 %collective-permute-done.27.refs_9_ = bf16[128,1024]{1,0:T(8,128)(2,1)S(1)} collective-permute-done((bf16[128,1024]{1,0:T(8,128)(2,1)S(1)}, bf16[128,1024]{1,0:T(8,128)(2,1)S(1)}, u32[]{:S(2)}, u32[]{:S(2)}) %collective-permute-start.27) | collective-permute-done | bytes 262176 | tf_op jit(solution)/shard_map/ppermute | solution.py:39
  58.2 25.1 %experts.1 = (bf16[128,1024]{1,0:T(8,128)(2,1)S(1)}, bf16[128,1024]{1,0:T(8,128)(2,1)S(1)}, bf16[128,1024]{1,0:T(8,128)(2,1)S(1)}, bf16[128,1024]{1,0:T(8,128)(2...) custom-call(s32[2]{0:T(128)S(1)} %pad_add_fusion.where, ...), custom_call_target="tpu_custom_call" | custom-call | tf_op jit(solution)/shard_map/experts/pallas_call | solution.py:459
  83.9 1.0 collective-permute-done.29
  85.0 1.5 %collective-permute-start.30 = (bf16[128,1024]{1,0:T(8,128)(2,1)S(1)}, bf16[128,1024]{1,0:T(8,128)(2,1)S(1)}, u32[]{:S(2)}, u32[]{:S(2)}) collective-permute-start(bf16[128,1024]{1,0:T(8,128)(2,1)S(1)} %add_convert_fusion.7), channel_id=1, source_target_pairs={{0,2},{1,5},{2,6},{3,1},{6,10},{7,3},{10,14},{11,7},{14,12},{15,11... | collective-permute-start | bytes 786440 | tf_op jit(solution)/shard_map/ppermute | solution.py:48
  86.6 1.5 %collective-permute-start.39 = (bf16[128,1024]{1,0:T(8,128)(2,1)S(1)}, bf16[128,1024]{1,0:T(8,128)(2,1)S(1)}, u32[]{:S(2)}, u32[]{:S(2)}) collective-permute-start(bf16[128,1024]{1,0:T(8,128)(2,1)S(1)} %add_convert_fusion.3), channel_id=1, source_target_pairs={{0,2},{1,5},{2,6},{3,1},{6,10},{7,3},{10,14},{11,7},{14,12},{15,11... | collective-permute-start | bytes 786440 | tf_op jit(solution)/shard_map/ppermute | solution.py:48
  88.0 3.4 %collective-permute-done.30 = bf16[128,1024]{1,0:T(8,128)(2,1)S(1)} collective-permute-done((bf16[128,1024]{1,0:T(8,128)(2,1)S(1)}, bf16[128,1024]{1,0:T(8,128)(2,1)S(1)}, u32[]{:S(2)}, u32[]{:S(2)}) %collective-permute-start.30) | collective-permute-done | bytes 262176 | tf_op jit(solution)/shard_map/ppermute | solution.py:48
  91.5 1.5 %collective-permute-start.33 = (bf16[128,1024]{1,0:T(8,128)(2,1)S(1)}, bf16[128,1024]{1,0:T(8,128)(2,1)S(1)}, u32[]{:S(2)}, u32[]{:S(2)}) collective-permute-start(bf16[128,1024]{1,0:T(8,128)(2,1)S(1)} %add_convert_fusion.6), channel_id=1, source_target_pairs={{0,2},{1,5},{2,6},{3,1},{6,10},{7,3},{10,14},{11,7},{14,12},{15,11... | collective-permute-start | bytes 786440 | tf_op jit(solution)/shard_map/ppermute | solution.py:48
  93.1 1.2 %collective-permute-done.39 = bf16[128,1024]{1,0:T(8,128)(2,1)S(1)} collective-permute-done((bf16[128,1024]{1,0:T(8,128)(2,1)S(1)}, bf16[128,1024]{1,0:T(8,128)(2,1)S(1)}, u32[]{:S(2)}, u32[]{:S(2)}) %collective-permute-start.39) | collective-permute-done | bytes 262176 | tf_op jit(solution)/shard_map/ppermute | solution.py:48
  94.3 1.5 %collective-permute-start.42 = (bf16[128,1024]{1,0:T(8,128)(2,1)S(1)}, bf16[128,1024]{1,0:T(8,128)(2,1)S(1)}, u32[]{:S(2)}, u32[]{:S(2)}) collective-permute-start(bf16[128,1024]{1,0:T(8,128)(2,1)S(1)} %add_convert_fusion.2), channel_id=1, source_target_pairs={{0,2},{1,5},{2,6},{3,1},{6,10},{7,3},{10,14},{11,7},{14,12},{15,11... | collective-permute-start | bytes 786440 | tf_op jit(solution)/shard_map/ppermute | solution.py:48
  95.9 2.1 %collective-permute-done.33 = bf16[128,1024]{1,0:T(8,128)(2,1)S(1)} collective-permute-done((bf16[128,1024]{1,0:T(8,128)(2,1)S(1)}, bf16[128,1024]{1,0:T(8,128)(2,1)S(1)}, u32[]{:S(2)}, u32[]{:S(2)}) %collective-permute-start.33) | collective-permute-done | bytes 262176 | tf_op jit(solution)/shard_map/ppermute | solution.py:48
  98.1 1.5 %collective-permute-start.34 = (bf16[128,1024]{1,0:T(8,128)(2,1)S(1)}, bf16[128,1024]{1,0:T(8,128)(2,1)S(1)}, u32[]{:S(2)}, u32[]{:S(2)}) collective-permute-start(bf16[128,1024]{1,0:T(8,128)(2,1)S(1)} %add_convert_fusion.5), channel_id=1, source_target_pairs={{0,2},{1,5},{2,6},{3,1},{6,10},{7,3},{10,14},{11,7},{14,12},{15,11... | collective-permute-start | bytes 786440 | tf_op jit(solution)/shard_map/ppermute | solution.py:48
  99.6 1.2 %collective-permute-done.42 = bf16[128,1024]{1,0:T(8,128)(2,1)S(1)} collective-permute-done((bf16[128,1024]{1,0:T(8,128)(2,1)S(1)}, bf16[128,1024]{1,0:T(8,128)(2,1)S(1)}, u32[]{:S(2)}, u32[]{:S(2)}) %collective-permute-start.42) | collective-permute-done | bytes 262176 | tf_op jit(solution)/shard_map/ppermute | solution.py:48
  100.9 0.8 collective-permute-start.43
  101.7 2.8 %collective-permute-done.34 = bf16[128,1024]{1,0:T(8,128)(2,1)S(1)} collective-permute-done((bf16[128,1024]{1,0:T(8,128)(2,1)S(1)}, bf16[128,1024]{1,0:T(8,128)(2,1)S(1)}, u32[]{:S(2)}, u32[]{:S(2)}) %collective-permute-start.34) | collective-permute-done | bytes 262176 | tf_op jit(solution)/shard_map/ppermute | solution.py:48
  104.7 1.5 %collective-permute-start.37 = (bf16[128,1024]{1,0:T(8,128)(2,1)S(1)}, bf16[128,1024]{1,0:T(8,128)(2,1)S(1)}, u32[]{:S(2)}, u32[]{:S(2)}) collective-permute-start(bf16[128,1024]{1,0:T(8,128)(2,1)S(1)} %add_convert_fusion.4), channel_id=1, source_target_pairs={{0,2},{1,5},{2,6},{3,1},{6,10},{7,3},{10,14},{11,7},{14,12},{15,11... | collective-permute-start | bytes 786440 | tf_op jit(solution)/shard_map/ppermute | solution.py:48
  106.8 4.3 %collective-permute-done.37 = bf16[128,1024]{1,0:T(8,128)(2,1)S(1)} collective-permute-done((bf16[128,1024]{1,0:T(8,128)(2,1)S(1)}, bf16[128,1024]{1,0:T(8,128)(2,1)S(1)}, u32[]{:S(2)}, u32[]{:S(2)}) %collective-permute-start.37) | collective-permute-done | bytes 262176 | tf_op jit(solution)/shard_map/ppermute | solution.py:48
  111.1 0.9 add_convert_fusion
  (58 shorter events, 4.8 us)
Async XLA Ops:
  1.1 5.5 %collective-permute-start.1 = (bf16[64,640]{1,0:T(8,128)(2,1)S(1)}, bf16[64,640]{1,0:T(8,128)(2,1)S(1)}, u32[]{:S(2)}, u32[]{:S(2)}) collective-permute-start(bf16[64,640]{1,0:T(8,128)(2,1)S(1)} %get-tuple-element.108.refs_1_), channel_id=1, source_target_pairs={{0,2},{1,5},{2,6},{3,1},{6,10},{7,3},{10,14},{11,7},{14,12},{15,11... | collective-permute-start | bytes 245768 | tf_op jit(solution)/shard_map/ppermute | solution.py:48
  4.2 5.2 %collective-permute-start = (bf16[64,640]{1,0:T(8,128)(2,1)S(1)}, bf16[64,640]{1,0:T(8,128)(2,1)S(1)}, u32[]{:S(2)}, u32[]{:S(2)}) collective-permute-start(bf16[64,640]{1,0:T(8,128)(2,1)S(1)} %get-tuple-element.107.refs_0_), channel_id=1, source_target_pairs={{0,2},{1,5},{2,6},{3,1},{6,10},{7,3},{10,14},{11,7},{14,12},{15,11... | collective-permute-start | bytes 245768 | tf_op jit(solution)/shard_map/ppermute | solution.py:48
  6.7 5.1 %collective-permute-start.5 = (bf16[64,640]{1,0:T(8,128)(2,1)S(1)}, bf16[64,640]{1,0:T(8,128)(2,1)S(1)}, u32[]{:S(2)}, u32[]{:S(2)}) collective-permute-start(bf16[64,640]{1,0:T(8,128)(2,1)S(1)} %collective-permute-done.1.refs_3_), channel_id=1, source_target_pairs={{0,1},{1,0},{2,3},{3,2},{4,5},{5,4},{6,7},{7,6},{8,9},{9,8},{10,11... | collective-permute-start | bytes 245768 | tf_op jit(solution)/shard_map/ppermute | solution.py:39
  6.7 5.1 %collective-permute-start.4 = (bf16[64,640]{1,0:T(8,128)(2,1)S(1)}, bf16[64,640]{1,0:T(8,128)(2,1)S(1)}, u32[]{:S(2)}, u32[]{:S(2)}) collective-permute-start(bf16[64,640]{1,0:T(8,128)(2,1)S(1)} %collective-permute-done.1.refs_3_), channel_id=1, source_target_pairs={{0,2},{1,5},{2,6},{3,1},{6,10},{7,3},{10,14},{11,7},{14,12},{15,11... | collective-permute-start | bytes 245768 | tf_op jit(solution)/shard_map/ppermute | solution.py:48
  9.4 4.1 %collective-permute-start.3 = (bf16[64,640]{1,0:T(8,128)(2,1)S(1)}, bf16[64,640]{1,0:T(8,128)(2,1)S(1)}, u32[]{:S(2)}, u32[]{:S(2)}) collective-permute-start(bf16[64,640]{1,0:T(8,128)(2,1)S(1)} %collective-permute-done.refs_2_), channel_id=1, source_target_pairs={{0,1},{1,0},{2,3},{3,2},{4,5},{5,4},{6,7},{7,6},{8,9},{9,8},{10,11... | collective-permute-start | bytes 245768 | tf_op jit(solution)/shard_map/ppermute | solution.py:39
  9.7 4.4 %collective-permute-start.2 = (bf16[64,640]{1,0:T(8,128)(2,1)S(1)}, bf16[64,640]{1,0:T(8,128)(2,1)S(1)}, u32[]{:S(2)}, u32[]{:S(2)}) collective-permute-start(bf16[64,640]{1,0:T(8,128)(2,1)S(1)} %collective-permute-done.refs_2_), channel_id=1, source_target_pairs={{0,2},{1,5},{2,6},{3,1},{6,10},{7,3},{10,14},{11,7},{14,12},{15,11... | collective-permute-start | bytes 245768 | tf_op jit(solution)/shard_map/ppermute | solution.py:48
  11.7 5.0 %collective-permute-start.9 = (bf16[64,640]{1,0:T(8,128)(2,1)S(1)}, bf16[64,640]{1,0:T(8,128)(2,1)S(1)}, u32[]{:S(2)}, u32[]{:S(2)}) collective-permute-start(bf16[64,640]{1,0:T(8,128)(2,1)S(1)} %collective-permute-done.4.refs_5_), channel_id=1, source_target_pairs={{0,1},{1,0},{2,3},{3,2},{4,5},{5,4},{6,7},{7,6},{8,9},{9,8},{10,11... | collective-permute-start | bytes 245768 | tf_op jit(solution)/shard_map/ppermute | solution.py:39
  11.8 4.9 %collective-permute-start.8 = (bf16[64,640]{1,0:T(8,128)(2,1)S(1)}, bf16[64,640]{1,0:T(8,128)(2,1)S(1)}, u32[]{:S(2)}, u32[]{:S(2)}) collective-permute-start(bf16[64,640]{1,0:T(8,128)(2,1)S(1)} %collective-permute-done.4.refs_5_), channel_id=1, source_target_pairs={{0,2},{1,5},{2,6},{3,1},{6,10},{7,3},{10,14},{11,7},{14,12},{15,11... | collective-permute-start | bytes 245768 | tf_op jit(solution)/shard_map/ppermute | solution.py:48
  14.1 4.3 %collective-permute-start.7 = (bf16[64,640]{1,0:T(8,128)(2,1)S(1)}, bf16[64,640]{1,0:T(8,128)(2,1)S(1)}, u32[]{:S(2)}, u32[]{:S(2)}) collective-permute-start(bf16[64,640]{1,0:T(8,128)(2,1)S(1)} %collective-permute-done.2.refs_4_), channel_id=1, source_target_pairs={{0,1},{1,0},{2,3},{3,2},{4,5},{5,4},{6,7},{7,6},{8,9},{9,8},{10,11... | collective-permute-start | bytes 245768 | tf_op jit(solution)/shard_map/ppermute | solution.py:39
  14.1 4.4 %collective-permute-start.6 = (bf16[64,640]{1,0:T(8,128)(2,1)S(1)}, bf16[64,640]{1,0:T(8,128)(2,1)S(1)}, u32[]{:S(2)}, u32[]{:S(2)}) collective-permute-start(bf16[64,640]{1,0:T(8,128)(2,1)S(1)} %collective-permute-done.2.refs_4_), channel_id=1, source_target_pairs={{0,2},{1,5},{2,6},{3,1},{6,10},{7,3},{10,14},{11,7},{14,12},{15,11... | collective-permute-start | bytes 245768 | tf_op jit(solution)/shard_map/ppermute | solution.py:48
  16.7 3.4 %collective-permute-start.13 = (bf16[64,640]{1,0:T(8,128)(2,1)S(1)}, bf16[64,640]{1,0:T(8,128)(2,1)S(1)}, u32[]{:S(2)}, u32[]{:S(2)}) collective-permute-start(bf16[64,640]{1,0:T(8,128)(2,1)S(1)} %collective-permute-done.8.refs_7_), channel_id=1, source_target_pairs={{0,1},{1,0},{2,3},{3,2},{4,5},{5,4},{6,7},{7,6},{8,9},{9,8},{10,11... | collective-permute-start | bytes 245768 | tf_op jit(solution)/shard_map/ppermute | solution.py:39
  17.3 4.4 %collective-permute-start.12 = (bf16[64,640]{1,0:T(8,128)(2,1)S(1)}, bf16[64,640]{1,0:T(8,128)(2,1)S(1)}, u32[]{:S(2)}, u32[]{:S(2)}) collective-permute-start(bf16[64,640]{1,0:T(8,128)(2,1)S(1)} %collective-permute-done.8.refs_7_), channel_id=1, source_target_pairs={{0,2},{1,5},{2,6},{3,1},{6,10},{7,3},{10,14},{11,7},{14,12},{15,11... | collective-permute-start | bytes 245768 | tf_op jit(solution)/shard_map/ppermute | solution.py:48
  18.6 3.1 %collective-permute-start.11 = (bf16[64,640]{1,0:T(8,128)(2,1)S(1)}, bf16[64,640]{1,0:T(8,128)(2,1)S(1)}, u32[]{:S(2)}, u32[]{:S(2)}) collective-permute-start(bf16[64,640]{1,0:T(8,128)(2,1)S(1)} %collective-permute-done.6.refs_6_), channel_id=1, source_target_pairs={{0,1},{1,0},{2,3},{3,2},{4,5},{5,4},{6,7},{7,6},{8,9},{9,8},{10,11... | collective-permute-start | bytes 245768 | tf_op jit(solution)/shard_map/ppermute | solution.py:39
  18.6 4.4 %collective-permute-start.10 = (bf16[64,640]{1,0:T(8,128)(2,1)S(1)}, bf16[64,640]{1,0:T(8,128)(2,1)S(1)}, u32[]{:S(2)}, u32[]{:S(2)}) collective-permute-start(bf16[64,640]{1,0:T(8,128)(2,1)S(1)} %collective-permute-done.6.refs_6_), channel_id=1, source_target_pairs={{0,2},{1,5},{2,6},{3,1},{6,10},{7,3},{10,14},{11,7},{14,12},{15,11... | collective-permute-start | bytes 245768 | tf_op jit(solution)/shard_map/ppermute | solution.py:48
  28.1 2.0 %collective-permute-start.14 = (bf16[128,2048]{1,0:T(8,128)(2,1)S(1)}, bf16[128,2048]{1,0:T(8,128)(2,1)S(1)}, u32[]{:S(2)}, u32[]{:S(2)}) collective-permute-start(bf16[128,2048]{1,0:T(8,128)(2,1)S(1)} %get-tuple-element.106), channel_id=1, source_target_pairs={{0,1},{1,0},{2,3},{3,2},{4,5},{5,4},{6,7},{7,6},{8,9},{9,8},{10,11... | collective-permute-start | bytes 1572872 | tf_op jit(solution)/shard_map/ppermute | solution.py:39
  31.1 6.4 %collective-permute-start.15 = (bf16[128,1024]{1,0:T(8,128)(2,1)S(1)}, bf16[128,1024]{1,0:T(8,128)(2,1)S(1)}, u32[]{:S(2)}, u32[]{:S(2)}) collective-permute-start(bf16[128,1024]{1,0:T(8,128)(2,1)S(1)} %get-tuple-element.126.refs_0_), channel_id=1, source_target_pairs={{0,2},{1,5},{2,6},{3,1},{6,10},{7,3},{10,14},{11,7},{14,12},{15,11... | collective-permute-start | bytes 786440 | tf_op jit(solution)/shard_map/ppermute | solution.py:48
  32.6 7.7 %collective-permute-start.16 = (bf16[128,1024]{1,0:T(8,128)(2,1)S(1)}, bf16[128,1024]{1,0:T(8,128)(2,1)S(1)}, u32[]{:S(2)}, u32[]{:S(2)}) collective-permute-start(bf16[128,1024]{1,0:T(8,128)(2,1)S(1)} %get-tuple-element.127.refs_1_), channel_id=1, source_target_pairs={{0,2},{1,5},{2,6},{3,1},{6,10},{7,3},{10,14},{11,7},{14,12},{15,11... | collective-permute-start | bytes 786440 | tf_op jit(solution)/shard_map/ppermute | solution.py:48
  37.5 4.3 %collective-permute-start.18 = (bf16[128,1024]{1,0:T(8,128)(2,1)S(1)}, bf16[128,1024]{1,0:T(8,128)(2,1)S(1)}, u32[]{:S(2)}, u32[]{:S(2)}) collective-permute-start(bf16[128,1024]{1,0:T(8,128)(2,1)S(1)} %collective-permute-done.15.refs_2_), channel_id=1, source_target_pairs={{0,1},{1,0},{2,3},{3,2},{4,5},{5,4},{6,7},{7,6},{8,9},{9,8},{10,11... | collective-permute-start | bytes 786440 | tf_op jit(solution)/shard_map/ppermute | solution.py:39
  37.5 6.4 %collective-permute-start.17 = (bf16[128,1024]{1,0:T(8,128)(2,1)S(1)}, bf16[128,1024]{1,0:T(8,128)(2,1)S(1)}, u32[]{:S(2)}, u32[]{:S(2)}) collective-permute-start(bf16[128,1024]{1,0:T(8,128)(2,1)S(1)} %collective-permute-done.15.refs_2_), channel_id=1, source_target_pairs={{0,2},{1,5},{2,6},{3,1},{6,10},{7,3},{10,14},{11,7},{14,12},{15,11... | collective-permute-start | bytes 786440 | tf_op jit(solution)/shard_map/ppermute | solution.py:48
  40.3 5.0 %collective-permute-start.20 = (bf16[128,1024]{1,0:T(8,128)(2,1)S(1)}, bf16[128,1024]{1,0:T(8,128)(2,1)S(1)}, u32[]{:S(2)}, u32[]{:S(2)}) collective-permute-start(bf16[128,1024]{1,0:T(8,128)(2,1)S(1)} %collective-permute-done.16.refs_3_), channel_id=1, source_target_pairs={{0,1},{1,0},{2,3},{3,2},{4,5},{5,4},{6,7},{7,6},{8,9},{9,8},{10,11... | collective-permute-start | bytes 786440 | tf_op jit(solution)/shard_map/ppermute | solution.py:39
  40.3 6.4 %collective-permute-start.19 = (bf16[128,1024]{1,0:T(8,128)(2,1)S(1)}, bf16[128,1024]{1,0:T(8,128)(2,1)S(1)}, u32[]{:S(2)}, u32[]{:S(2)}) collective-permute-start(bf16[128,1024]{1,0:T(8,128)(2,1)S(1)} %collective-permute-done.16.refs_3_), channel_id=1, source_target_pairs={{0,2},{1,5},{2,6},{3,1},{6,10},{7,3},{10,14},{11,7},{14,12},{15,11... | collective-permute-start | bytes 786440 | tf_op jit(solution)/shard_map/ppermute | solution.py:48
  43.9 4.3 %collective-permute-start.22 = (bf16[128,1024]{1,0:T(8,128)(2,1)S(1)}, bf16[128,1024]{1,0:T(8,128)(2,1)S(1)}, u32[]{:S(2)}, u32[]{:S(2)}) collective-permute-start(bf16[128,1024]{1,0:T(8,128)(2,1)S(1)} %collective-permute-done.17.refs_4_), channel_id=1, source_target_pairs={{0,1},{1,0},{2,3},{3,2},{4,5},{5,4},{6,7},{7,6},{8,9},{9,8},{10,11... | collective-permute-start | bytes 786440 | tf_op jit(solution)/shard_map/ppermute | solution.py:39
  43.9 6.4 %collective-permute-start.21 = (bf16[128,1024]{1,0:T(8,128)(2,1)S(1)}, bf16[128,1024]{1,0:T(8,128)(2,1)S(1)}, u32[]{:S(2)}, u32[]{:S(2)}) collective-permute-start(bf16[128,1024]{1,0:T(8,128)(2,1)S(1)} %collective-permute-done.17.refs_4_), channel_id=1, source_target_pairs={{0,2},{1,5},{2,6},{3,1},{6,10},{7,3},{10,14},{11,7},{14,12},{15,11... | collective-permute-start | bytes 786440 | tf_op jit(solution)/shard_map/ppermute | solution.py:48
  46.7 5.0 %collective-permute-start.24 = (bf16[128,1024]{1,0:T(8,128)(2,1)S(1)}, bf16[128,1024]{1,0:T(8,128)(2,1)S(1)}, u32[]{:S(2)}, u32[]{:S(2)}) collective-permute-start(bf16[128,1024]{1,0:T(8,128)(2,1)S(1)} %collective-permute-done.19.refs_5_), channel_id=1, source_target_pairs={{0,1},{1,0},{2,3},{3,2},{4,5},{5,4},{6,7},{7,6},{8,9},{9,8},{10,11... | collective-permute-start | bytes 786440 | tf_op jit(solution)/shard_map/ppermute | solution.py:39
  46.7 6.4 %collective-permute-start.23 = (bf16[128,1024]{1,0:T(8,128)(2,1)S(1)}, bf16[128,1024]{1,0:T(8,128)(2,1)S(1)}, u32[]{:S(2)}, u32[]{:S(2)}) collective-permute-start(bf16[128,1024]{1,0:T(8,128)(2,1)S(1)} %collective-permute-done.19.refs_5_), channel_id=1, source_target_pairs={{0,2},{1,5},{2,6},{3,1},{6,10},{7,3},{10,14},{11,7},{14,12},{15,11... | collective-permute-start | bytes 786440 | tf_op jit(solution)/shard_map/ppermute | solution.py:48
  50.3 2.8 %collective-permute-start.26 = (bf16[128,1024]{1,0:T(8,128)(2,1)S(1)}, bf16[128,1024]{1,0:T(8,128)(2,1)S(1)}, u32[]{:S(2)}, u32[]{:S(2)}) collective-permute-start(bf16[128,1024]{1,0:T(8,128)(2,1)S(1)} %collective-permute-done.21.refs_6_), channel_id=1, source_target_pairs={{0,1},{1,0},{2,3},{3,2},{4,5},{5,4},{6,7},{7,6},{8,9},{9,8},{10,11... | collective-permute-start | bytes 786440 | tf_op jit(solution)/shard_map/ppermute | solution.py:39
  50.3 6.4 %collective-permute-start.25 = (bf16[128,1024]{1,0:T(8,128)(2,1)S(1)}, bf16[128,1024]{1,0:T(8,128)(2,1)S(1)}, u32[]{:S(2)}, u32[]{:S(2)}) collective-permute-start(bf16[128,1024]{1,0:T(8,128)(2,1)S(1)} %collective-permute-done.21.refs_6_), channel_id=1, source_target_pairs={{0,2},{1,5},{2,6},{3,1},{6,10},{7,3},{10,14},{11,7},{14,12},{15,11... | collective-permute-start | bytes 786440 | tf_op jit(solution)/shard_map/ppermute | solution.py:48
  53.1 3.6 %collective-permute-start.28 = (bf16[128,1024]{1,0:T(8,128)(2,1)S(1)}, bf16[128,1024]{1,0:T(8,128)(2,1)S(1)}, u32[]{:S(2)}, u32[]{:S(2)}) collective-permute-start(bf16[128,1024]{1,0:T(8,128)(2,1)S(1)} %collective-permute-done.23.refs_7_), channel_id=1, source_target_pairs={{0,1},{1,0},{2,3},{3,2},{4,5},{5,4},{6,7},{7,6},{8,9},{9,8},{10,11... | collective-permute-start | bytes 786440 | tf_op jit(solution)/shard_map/ppermute | solution.py:39
  56.6 1.5 %collective-permute-start.27 = (bf16[128,1024]{1,0:T(8,128)(2,1)S(1)}, bf16[128,1024]{1,0:T(8,128)(2,1)S(1)}, u32[]{:S(2)}, u32[]{:S(2)}) collective-permute-start(bf16[128,1024]{1,0:T(8,128)(2,1)S(1)} %collective-permute-done.25.refs_8_), channel_id=1, source_target_pairs={{0,1},{1,0},{2,3},{3,2},{4,5},{5,4},{6,7},{7,6},{8,9},{9,8},{10,11... | collective-permute-start | bytes 786440 | tf_op jit(solution)/shard_map/ppermute | solution.py:39
  83.3 1.6 %collective-permute-start.29 = (bf16[128,1024]{1,0:T(8,128)(2,1)S(1)}, bf16[128,1024]{1,0:T(8,128)(2,1)S(1)}, u32[]{:S(2)}, u32[]{:S(2)}) collective-permute-start(bf16[128,1024]{1,0:T(8,128)(2,1)S(1)} %get-tuple-element.142), channel_id=1, source_target_pairs={{0,1},{1,0},{2,3},{3,2},{4,5},{5,4},{6,7},{7,6},{8,9},{9,8},{10,11... | collective-permute-start | bytes 786440 | tf_op jit(solution)/shard_map/ppermute | solution.py:39
  83.5 3.0 %collective-permute-start.38 = (bf16[128,1024]{1,0:T(8,128)(2,1)S(1)}, bf16[128,1024]{1,0:T(8,128)(2,1)S(1)}, u32[]{:S(2)}, u32[]{:S(2)}) collective-permute-start(bf16[128,1024]{1,0:T(8,128)(2,1)S(1)} %get-tuple-element.157), channel_id=1, source_target_pairs={{0,1},{1,0},{2,3},{3,2},{4,5},{5,4},{6,7},{7,6},{8,9},{9,8},{10,11... | collective-permute-start | bytes 786440 | tf_op jit(solution)/shard_map/ppermute | solution.py:39
  85.0 6.4 %collective-permute-start.30 = (bf16[128,1024]{1,0:T(8,128)(2,1)S(1)}, bf16[128,1024]{1,0:T(8,128)(2,1)S(1)}, u32[]{:S(2)}, u32[]{:S(2)}) collective-permute-start(bf16[128,1024]{1,0:T(8,128)(2,1)S(1)} %add_convert_fusion.7), channel_id=1, source_target_pairs={{0,2},{1,5},{2,6},{3,1},{6,10},{7,3},{10,14},{11,7},{14,12},{15,11... | collective-permute-start | bytes 786440 | tf_op jit(solution)/shard_map/ppermute | solution.py:48
  86.5 4.9 %collective-permute-start.32 = (bf16[128,1024]{1,0:T(8,128)(2,1)S(1)}, bf16[128,1024]{1,0:T(8,128)(2,1)S(1)}, u32[]{:S(2)}, u32[]{:S(2)}) collective-permute-start(bf16[128,1024]{1,0:T(8,128)(2,1)S(1)} %get-tuple-element.146), channel_id=1, source_target_pairs={{0,1},{1,0},{2,3},{3,2},{4,5},{5,4},{6,7},{7,6},{8,9},{9,8},{10,11... | collective-permute-start | bytes 786440 | tf_op jit(solution)/shard_map/ppermute | solution.py:39
  86.6 7.6 %collective-permute-start.39 = (bf16[128,1024]{1,0:T(8,128)(2,1)S(1)}, bf16[128,1024]{1,0:T(8,128)(2,1)S(1)}, u32[]{:S(2)}, u32[]{:S(2)}) collective-permute-start(bf16[128,1024]{1,0:T(8,128)(2,1)S(1)} %add_convert_fusion.3), channel_id=1, source_target_pairs={{0,2},{1,5},{2,6},{3,1},{6,10},{7,3},{10,14},{11,7},{14,12},{15,11... | collective-permute-start | bytes 786440 | tf_op jit(solution)/shard_map/ppermute | solution.py:48
  88.0 6.2 %collective-permute-start.41 = (bf16[128,1024]{1,0:T(8,128)(2,1)S(1)}, bf16[128,1024]{1,0:T(8,128)(2,1)S(1)}, u32[]{:S(2)}, u32[]{:S(2)}) collective-permute-start(bf16[128,1024]{1,0:T(8,128)(2,1)S(1)} %get-tuple-element.161), channel_id=1, source_target_pairs={{0,1},{1,0},{2,3},{3,2},{4,5},{5,4},{6,7},{7,6},{8,9},{9,8},{10,11... | collective-permute-start | bytes 786440 | tf_op jit(solution)/shard_map/ppermute | solution.py:39
  91.5 6.4 %collective-permute-start.33 = (bf16[128,1024]{1,0:T(8,128)(2,1)S(1)}, bf16[128,1024]{1,0:T(8,128)(2,1)S(1)}, u32[]{:S(2)}, u32[]{:S(2)}) collective-permute-start(bf16[128,1024]{1,0:T(8,128)(2,1)S(1)} %add_convert_fusion.6), channel_id=1, source_target_pairs={{0,2},{1,5},{2,6},{3,1},{6,10},{7,3},{10,14},{11,7},{14,12},{15,11... | collective-permute-start | bytes 786440 | tf_op jit(solution)/shard_map/ppermute | solution.py:48
  93.1 4.9 %collective-permute-start.31 = (bf16[128,1024]{1,0:T(8,128)(2,1)S(1)}, bf16[128,1024]{1,0:T(8,128)(2,1)S(1)}, u32[]{:S(2)}, u32[]{:S(2)}) collective-permute-start(bf16[128,1024]{1,0:T(8,128)(2,1)S(1)} %get-tuple-element.144), channel_id=1, source_target_pairs={{0,1},{1,0},{2,3},{3,2},{4,5},{5,4},{6,7},{7,6},{8,9},{9,8},{10,11... | collective-permute-start | bytes 786440 | tf_op jit(solution)/shard_map/ppermute | solution.py:39
  94.2 6.6 %collective-permute-start.40 = (bf16[128,1024]{1,0:T(8,128)(2,1)S(1)}, bf16[128,1024]{1,0:T(8,128)(2,1)S(1)}, u32[]{:S(2)}, u32[]{:S(2)}) collective-permute-start(bf16[128,1024]{1,0:T(8,128)(2,1)S(1)} %get-tuple-element.159), channel_id=1, source_target_pairs={{0,1},{1,0},{2,3},{3,2},{4,5},{5,4},{6,7},{7,6},{8,9},{9,8},{10,11... | collective-permute-start | bytes 786440 | tf_op jit(solution)/shard_map/ppermute | solution.py:39
  94.3 6.4 %collective-permute-start.42 = (bf16[128,1024]{1,0:T(8,128)(2,1)S(1)}, bf16[128,1024]{1,0:T(8,128)(2,1)S(1)}, u32[]{:S(2)}, u32[]{:S(2)}) collective-permute-start(bf16[128,1024]{1,0:T(8,128)(2,1)S(1)} %add_convert_fusion.2), channel_id=1, source_target_pairs={{0,2},{1,5},{2,6},{3,1},{6,10},{7,3},{10,14},{11,7},{14,12},{15,11... | collective-permute-start | bytes 786440 | tf_op jit(solution)/shard_map/ppermute | solution.py:48
  98.1 6.4 %collective-permute-start.34 = (bf16[128,1024]{1,0:T(8,128)(2,1)S(1)}, bf16[128,1024]{1,0:T(8,128)(2,1)S(1)}, u32[]{:S(2)}, u32[]{:S(2)}) collective-permute-start(bf16[128,1024]{1,0:T(8,128)(2,1)S(1)} %add_convert_fusion.5), channel_id=1, source_target_pairs={{0,2},{1,5},{2,6},{3,1},{6,10},{7,3},{10,14},{11,7},{14,12},{15,11... | collective-permute-start | bytes 786440 | tf_op jit(solution)/shard_map/ppermute | solution.py:48
  99.6 4.9 %collective-permute-start.36 = (bf16[128,1024]{1,0:T(8,128)(2,1)S(1)}, bf16[128,1024]{1,0:T(8,128)(2,1)S(1)}, u32[]{:S(2)}, u32[]{:S(2)}) collective-permute-start(bf16[128,1024]{1,0:T(8,128)(2,1)S(1)} %get-tuple-element.153), channel_id=1, source_target_pairs={{0,1},{1,0},{2,3},{3,2},{4,5},{5,4},{6,7},{7,6},{8,9},{9,8},{10,11... | collective-permute-start | bytes 786440 | tf_op jit(solution)/shard_map/ppermute | solution.py:39
  100.9 5.9 %collective-permute-start.43 = (bf16[128,1024]{1,0:T(8,128)(2,1)S(1)}, bf16[128,1024]{1,0:T(8,128)(2,1)S(1)}, u32[]{:S(2)}, u32[]{:S(2)}) collective-permute-start(bf16[128,1024]{1,0:T(8,128)(2,1)S(1)} %add_convert_fusion.1), channel_id=1, source_target_pairs={{0,3},{1,4},{2,7},{3,0},{6,11},{7,2},{10,15},{11,6},{14,13},{15,10... | collective-permute-start | bytes 786440 | tf_op jit(solution)/shard_map/ppermute | solution.py:48
  104.5 2.3 %collective-permute-start.35 = (bf16[128,1024]{1,0:T(8,128)(2,1)S(1)}, bf16[128,1024]{1,0:T(8,128)(2,1)S(1)}, u32[]{:S(2)}, u32[]{:S(2)}) collective-permute-start(bf16[128,1024]{1,0:T(8,128)(2,1)S(1)} %get-tuple-element.151), channel_id=1, source_target_pairs={{0,1},{1,0},{2,3},{3,2},{4,5},{5,4},{6,7},{7,6},{8,9},{9,8},{10,11... | collective-permute-start | bytes 786440 | tf_op jit(solution)/shard_map/ppermute | solution.py:39
  104.7 6.4 %collective-permute-start.37 = (bf16[128,1024]{1,0:T(8,128)(2,1)S(1)}, bf16[128,1024]{1,0:T(8,128)(2,1)S(1)}, u32[]{:S(2)}, u32[]{:S(2)}) collective-permute-start(bf16[128,1024]{1,0:T(8,128)(2,1)S(1)} %add_convert_fusion.4), channel_id=1, source_target_pairs={{0,2},{1,5},{2,6},{3,1},{6,10},{7,3},{10,14},{11,7},{14,12},{15,11... | collective-permute-start | bytes 786440 | tf_op jit(solution)/shard_map/ppermute | solution.py:48
